TPU v7x, 32 devices: a whole 2x2x4 slice. The times are simulated.
32 devices in a mesh: seq: 8 (over y, x, core), chan: 4 (over z).
Axes of the slice: x: 2, y: 2, z: 4, core: 2. Of those that a mesh axis runs over, the one named last changes fastest.
Arguments:
- values_in: bfloat16 [1024, 4096], P('seq', 'chan'), may hold values from -6 to 6
- gate_values: bfloat16 [1024, 4096], P('seq', 'chan'), may hold values from -6 to 6
- filter_spectrum: float32 [2, 16, 128, 4096], P(None, 'seq', None, 'chan'), may hold values from -6 to 6
- skip_gain: float32 [4096], P('chan'), may hold values from -4 to 4
- out_weight: bfloat16 [4096, 4096], P('chan', 'seq'), may hold values from -0.09375 to 0.09375
Outputs:
- mixed: bfloat16 [1024, 4096], P('seq', 'chan')
All inputs are finite; a program needn't handle non-finite values.
Results may differ from a plain program's by a relative error of at most 0.009.
Values may be sent and summed in bfloat16 or wider, within the bound.
No kernel may reach another device: no remote copies, remote signals or barrier semaphores. Data moves between devices by JAX's collectives and lax.ppermute only.
A program may use at most 64 MiB of HBM per device.

v0:
```python
import math

import jax
import jax.numpy as jnp
from jax import lax
from jax.sharding import PartitionSpec as P

precise = lax.Precision.HIGHEST


def swapped(value, axis, bit):
    mask = 2**bit
    pairs = [(source, source ^ mask) for source in range(lax.axis_size(axis))]
    return lax.ppermute(value, axis, pairs)


def reversed_bits(number, width_bits):
    flipped = number * 0
    for bit_place in range(width_bits):
        flipped = flipped + (number >> bit_place & 1) * (1 << width_bits - 1 - bit_place)
    return flipped


def angle_table(left_index, right_index, modulus, direction):
    product = left_index[:, None] * right_index[None, :] % modulus
    phases = direction * 2.0 * math.pi * product.astype(jnp.float32) / modulus
    return (jnp.cos(phases), jnp.sin(phases))


def rotate(real_part, imag_part, cos_table, sin_table):
    return (
        real_part * cos_table - imag_part * sin_table,
        real_part * sin_table + imag_part * cos_table,
    )


def apply_table(cos_table, sin_table, real_part, imag_part, pattern):

    def contract(table, data):
        return jnp.einsum(pattern, table, data, precision=precise)

    return (
        contract(cos_table, real_part) - contract(sin_table, imag_part),
        contract(cos_table, imag_part) + contract(sin_table, real_part),
    )


def forward_section(spectra, device, bit_place):
    half_span = 1 << bit_place
    partner = swapped(spectra, "seq", bit_place)
    is_upper = device >> bit_place & 1
    signed = (1 - 2 * is_upper).astype(jnp.float32)
    summed = partner + signed * spectra
    phases = (
        -math.pi
        * (device % half_span).astype(jnp.float32)
        / half_span
        * is_upper.astype(jnp.float32)
    )
    real_part, imag_part = rotate(summed[0], summed[1], jnp.cos(phases), jnp.sin(phases))
    return jnp.stack([real_part, imag_part])


def inverse_section(spectra, device, bit_place):
    half_span = 1 << bit_place
    partner = swapped(spectra, "seq", bit_place)
    is_upper = device >> bit_place & 1 == 1
    lower_value = jnp.where(is_upper, partner, spectra)
    upper_value = jnp.where(is_upper, spectra, partner)
    phases = math.pi * (device % half_span).astype(jnp.float32) / half_span
    real_part, imag_part = rotate(upper_value[0], upper_value[1], jnp.cos(phases), jnp.sin(phases))
    signed = jnp.where(is_upper, -1.0, 1.0).astype(jnp.float32)
    return jnp.stack(
        [(lower_value[0] + signed * real_part) * 0.5, (lower_value[1] + signed * imag_part) * 0.5]
    )


def shards(values_in, gate_values, filter_spectrum, skip_gain, out_weight):
    seq_parts = lax.axis_size("seq")
    width_bits = seq_parts.bit_length() - 1
    seq_rows = values_in.shape[0]
    total_len = 2 * seq_parts * seq_rows
    device = lax.axis_index("seq")
    signal = values_in.astype(jnp.float32)
    positions = jnp.arange(seq_rows, dtype=jnp.int32)
    forward_cos, forward_sin = angle_table(positions, positions, seq_rows, -1.0)
    inverse_cos, inverse_sin = angle_table(positions, positions, seq_rows, 1.0)
    half_phase = math.pi * device.astype(jnp.float32) / seq_parts
    half_cos = jnp.cos(half_phase)
    half_sin = jnp.sin(half_phase)
    nothing = jnp.zeros_like(signal)
    spectra = jnp.stack(
        [jnp.stack([signal, signal * half_cos]), jnp.stack([nothing, -signal * half_sin])]
    )
    for bit_place in range(width_bits - 1, -1, -1):
        spectra = forward_section(spectra, device, bit_place)
    frequency = 2 * reversed_bits(device, width_bits) + jnp.arange(2, dtype=jnp.int32)
    twiddle_cos, twiddle_sin = angle_table(frequency, positions, total_len, -1.0)
    real_part, imag_part = rotate(
        spectra[0], spectra[1], twiddle_cos[:, :, None], twiddle_sin[:, :, None]
    )
    spec_real, spec_imag = apply_table(
        forward_cos, forward_sin, real_part, imag_part, "cj,ejh->ech"
    )
    prod_real = spec_real * filter_spectrum[0] - spec_imag * filter_spectrum[1]
    prod_imag = spec_real * filter_spectrum[1] + spec_imag * filter_spectrum[0]
    back_real, back_imag = apply_table(
        inverse_cos, inverse_sin, prod_real, prod_imag, "jc,ech->ejh"
    )
    back_real, back_imag = rotate(
        back_real / seq_rows,
        back_imag / seq_rows,
        twiddle_cos[:, :, None],
        -twiddle_sin[:, :, None],
    )
    spectra = jnp.stack([back_real, back_imag])
    for bit_place in range(width_bits):
        spectra = inverse_section(spectra, device, bit_place)
    convolved = (spectra[0, 0] + half_cos * spectra[0, 1] - half_sin * spectra[1, 1]) * 0.5
    gated_values = (gate_values.astype(jnp.float32) * (convolved + skip_gain * signal)).astype(
        jnp.bfloat16
    )
    partials = jnp.dot(
        gated_values,
        lax.all_gather(out_weight, "seq", axis=1, tiled=True),
        preferred_element_type=jnp.float32,
    )
    return lax.psum_scatter(partials.astype(jnp.bfloat16), "chan", scatter_dimension=1, tiled=True)


def solution(mesh):
    in_specs = (
        P("seq", "chan"),
        P("seq", "chan"),
        P(None, "seq", None, "chan"),
        P("chan"),
        P("chan", "seq"),
    )
    out_specs = P("seq", "chan")
    return jax.shard_map(shards, mesh=mesh, in_specs=in_specs, out_specs=out_specs, check_vma=False)
```

profile of v0, /device:TPU:0, one launch (start us, length us, event | category | flops | bytes accessed | tf_op | source)
XLA Modules:
  0.0 316.9 jit_solution(8046803529232145685)
XLA Ops:
  9.6 3.0 collective-permute-start
  12.7 45.8 %collective-permute-done = f32[2,2,128,1024]{2,3,1,0:T(8,128)} collective-permute-done((f32[2,2,128,1024]{2,3,1,0:T(8,128)}, f32[2,2,128,1024]{2,3,1,0:T(8,128)}, u32[]{:S(2)}, u32[]{:S(2)}) %collective-permute-start) | collective-permute-done | bytes 2097184 | tf_op jit(solution)/shard_map/ppermute | solution.py:14
  58.5 1.8 multiply_add_fusion.2
  60.5 1.5 pad_maximum_fusion.1
  62.0 1.7 collective-permute-start.1
  64.0 73.7 %collective-permute-done.1 = f32[2,2,128,1024]{2,3,1,0:T(8,128)} collective-permute-done((f32[2,2,128,1024]{2,3,1,0:T(8,128)}, f32[2,2,128,1024]{2,3,1,0:T(8,128)}, u32[]{:S(2)}, u32[]{:S(2)}) %collective-permute-start.1) | collective-permute-done | bytes 2097184 | tf_op jit(solution)/shard_map/ppermute | solution.py:14
  137.7 1.8 multiply_add_fusion.1
  139.8 1.5 pad_maximum_fusion.2
  141.5 3.1 fusion.108
  144.6 1.5 copy.10
  146.1 2.6 copy.11
  148.9 1.8 multiply_add_fusion
  159.9 1.6 subtract_bitcast_fusion
  161.4 1.5 pad_maximum_fusion.3
  163.5 4.1 %collective-permute-done.3 = f32[2,2,128,1024]{2,3,1,0:T(8,128)} collective-permute-done((f32[2,2,128,1024]{2,3,1,0:T(8,128)}, f32[2,2,128,1024]{2,3,1,0:T(8,128)}, u32[]{:S(2)}, u32[]{:S(2)}) %collective-permute-start.3) | collective-permute-done | bytes 2097184 | tf_op jit(solution)/shard_map/ppermute | solution.py:14
  167.6 1.9 broadcast_select_fusion
  169.8 1.5 pad_maximum_fusion.4
  171.3 2.6 collective-permute-start.4
  174.1 46.3 %collective-permute-done.4 = f32[2,2,128,1024]{2,3,1,0:T(8,128)} collective-permute-done((f32[2,2,128,1024]{2,3,1,0:T(8,128)}, f32[2,2,128,1024]{2,3,1,0:T(8,128)}, u32[]{:S(2)}, u32[]{:S(2)}) %collective-permute-start.4) | collective-permute-done | bytes 2097184 | tf_op jit(solution)/shard_map/ppermute | solution.py:14
  220.4 1.9 broadcast_select_fusion.2
  226.5 45.3 %collective-permute-done.5 = f32[2,2,128,1024]{2,3,1,0:T(8,128)} collective-permute-done((f32[2,2,128,1024]{2,3,1,0:T(8,128)}, f32[2,2,128,1024]{2,3,1,0:T(8,128)}, u32[]{:S(2)}, u32[]{:S(2)}) %collective-permute-start.5) | collective-permute-done | bytes 2097184 | tf_op jit(solution)/shard_map/ppermute | solution.py:14
  271.9 1.9 broadcast_select_fusion.4
  275.1 6.3 %convolution_convert_fusion = bf16[128,4096]{1,0:T(8,128)(2,1)} fusion(bf16[1024,4096]{1,0:T(8,128)(2,1)} %all-gather.2.cloned.1.call-done, bf16[128,1024]{0,1:T(8,128)(2,1)S(1)} %copy.7, f32[1,2,128,1024]{2,3,1,0:T(8,128)} %get-tuple-element.22, f32[1,2,128,1024]{2,3,1,0:T(8,128)S(1)} %get-tuple-element.20, f32[1,2,128,1024]{2,3,1,0:T(8,128)S(1)} %get-tuple-element.21, ...), kind=kOutput, calls=%fused_computation | convolution fusion | flops 1076494336 | bytes 12587028 | tf_op jit(solution)/shard_map/dot_general | solution.py:123
  281.4 28.6 %reduce-scatter.2.cloned.1.call-done = bf16[128,1024]{1,0:T(8,128)(2,1)} async-done(((bf16[128,4096]{1,0:T(8,128)(2,1)}), bf16[128,1024]{1,0:T(8,128)(2,1)}) %reduce-scatter.2.cloned.1.call-update) | async-done | bytes 262160 | tf_op jit(solution)/shard_map/reduce_scatter | solution.py:128
  (37 shorter events, 18.9 us)
Async XLA Ops:
  6.5 268.6 %all-gather.2.cloned.1.call-start = ((), (), s32[]{:S(2)}) async-start(), calls=%async_computation.1 | async-start | bytes 9437184 | tf_op jit(solution)/shard_map/all_gather | solution.py:125
  9.6 48.9 %collective-permute-start = (f32[2,2,128,1024]{2,3,1,0:T(8,128)}, f32[2,2,128,1024]{2,3,1,0:T(8,128)}, u32[]{:S(2)}, u32[]{:S(2)}) collective-permute-start(f32[2,2,128,1024]{2,3,1,0:T(8,128)} %pad_maximum_fusion), channel_id=1, source_target_pairs={{0,16},{4,20},{8,24},{12,28},{16,0},{20,4},{24,8},{28,12},{1,17},{... | collective-permute-start | bytes 6291464 | tf_op jit(solution)/shard_map/ppermute | solution.py:14
  62.0 75.7 %collective-permute-start.1 = (f32[2,2,128,1024]{2,3,1,0:T(8,128)}, f32[2,2,128,1024]{2,3,1,0:T(8,128)}, u32[]{:S(2)}, u32[]{:S(2)}) collective-permute-start(f32[2,2,128,1024]{2,3,1,0:T(8,128)} %pad_maximum_fusion.1), channel_id=1, source_target_pairs={{0,8},{4,12},{8,0},{12,4},{16,24},{20,28},{24,16},{28,20},{1,9},{5... | collective-permute-start | bytes 6291464 | tf_op jit(solution)/shard_map/ppermute | solution.py:14
  63.8 246.3 %reduce-scatter.2.cloned.1.call-start = ((), (), s32[]{:S(2)}) async-start(), calls=%async_computation.2 | async-start | bytes 1310720 | tf_op jit(solution)/shard_map/reduce_scatter | solution.py:128
  141.3 7.6 %collective-permute-start.2 = (f32[2,2,128,1024]{2,3,1,0:T(8,128)}, f32[2,2,128,1024]{2,3,1,0:T(8,128)}, u32[]{:S(2)}, u32[]{:S(2)}) collective-permute-start(f32[2,2,128,1024]{2,3,1,0:T(8,128)} %pad_maximum_fusion.2), channel_id=1, source_target_pairs={{0,4},{4,0},{8,12},{12,8},{16,20},{20,16},{24,28},{28,24},{1,5},{5... | collective-permute-start | bytes 6291464 | tf_op jit(solution)/shard_map/ppermute | solution.py:14
  153.4 1.3 copy-start
  163.0 4.6 %collective-permute-start.3 = (f32[2,2,128,1024]{2,3,1,0:T(8,128)}, f32[2,2,128,1024]{2,3,1,0:T(8,128)}, u32[]{:S(2)}, u32[]{:S(2)}) collective-permute-start(f32[2,2,128,1024]{2,3,1,0:T(8,128)} %pad_maximum_fusion.3), channel_id=1, source_target_pairs={{0,4},{4,0},{8,12},{12,8},{16,20},{20,16},{24,28},{28,24},{1,5},{5... | collective-permute-start | bytes 6291464 | tf_op jit(solution)/shard_map/ppermute | solution.py:14
  171.3 49.1 %collective-permute-start.4 = (f32[2,2,128,1024]{2,3,1,0:T(8,128)}, f32[2,2,128,1024]{2,3,1,0:T(8,128)}, u32[]{:S(2)}, u32[]{:S(2)}) collective-permute-start(f32[2,2,128,1024]{2,3,1,0:T(8,128)} %pad_maximum_fusion.4), channel_id=1, source_target_pairs={{0,8},{4,12},{8,0},{12,4},{16,24},{20,28},{24,16},{28,20},{1,9},{5... | collective-permute-start | bytes 6291464 | tf_op jit(solution)/shard_map/ppermute | solution.py:14
  222.7 3.0 copy-start.1
  224.2 47.6 %collective-permute-start.5 = (f32[2,2,128,1024]{2,3,1,0:T(8,128)}, f32[2,2,128,1024]{2,3,1,0:T(8,128)}, u32[]{:S(2)}, u32[]{:S(2)}) collective-permute-start(f32[2,2,128,1024]{2,3,1,0:T(8,128)} %pad_maximum_fusion.5), channel_id=1, source_target_pairs={{0,16},{4,20},{8,24},{12,28},{16,0},{20,4},{24,8},{28,12},{1,17},{... | collective-permute-start | bytes 6291464 | tf_op jit(solution)/shard_map/ppermute | solution.py:14
  273.8 1.4 copy-start.2
Sparse Core Ops, SparseCore 0:
  63.9 82.3 all-gather.1
  281.6 28.4 reduce-scatter.1
where the time goes:
time: 317 us
  waiting for transfers between devices  244 us (77%)
  other arithmetic  23.2 us (7%)
  matrix products  16.7 us (5%)
  between operations  14.6 us (5%)
  local copies, waits for them, and re-layouts  9.23 us (3%)
  starting transfers between devices  9.13 us (3%)
    ppermute x6, waiting for transfers between devices, swapped(): return lax.ppermute(value, axis, pairs)  215 us
    reduce_scatter x1, waiting for transfers between devices, shards(): lax.psum_scatter(partials.astype(jnp.bfloat16), 'chan', scatter_dimension...  28.6 us
    dot_general x8, matrix products, contract(): return jnp.einsum(pattern, table, data, precision=precise)  10.5 us
    ppermute x6, starting transfers between devices, swapped(): return lax.ppermute(value, axis, pairs)  9.08 us
  transfers between devices with their start and end apart: 8, of which 6 were waited for; matrix products, arithmetic and copies ran while one was open for 12% of the time, Pallas kernels for 0%

commit v1 on v0

v1 whole, which is shorter than its diff:
```python
import functools

import jax
import jax.numpy as jnp
import numpy as np
from jax import lax
from jax.experimental import pallas as pl
from jax.experimental.pallas import tpu as pltpu
from jax.sharding import PartitionSpec as P

BF16 = jnp.bfloat16
F32 = jnp.float32


def bit_reversed(number, width_bits):
    flipped = 0
    for bit_place in range(width_bits):
        flipped |= (number >> bit_place & 1) << (width_bits - 1 - bit_place)
    return flipped


def filter_row(residue, width_bits):
    return 2 * bit_reversed(residue // 2, width_bits) + residue % 2


def dft_tables(parts, rows):
    total = 2 * parts * rows
    residue = np.arange(2 * parts)[:, None, None]
    column = np.arange(rows)[None, :, None]
    position = np.arange(rows)[None, None, :]
    phase = 2.0 * np.pi * (position * (residue + 2 * parts * column) % total) / total
    cos, sin = np.cos(phase), np.sin(phase)
    forward = np.concatenate(
        [np.concatenate([cos, sin], axis=2), np.concatenate([-sin, cos], axis=2)], axis=1
    )
    inverse = np.transpose(forward, (0, 2, 1)) / total
    return forward.astype(BF16), inverse.astype(BF16)


def convolve_kernel(parts, rows, moved_ref, skip_ref, forward_ref, inverse_ref, out_ref, waves_ref, back_ref):
    width_bits = parts.bit_length() - 1
    chunk = 16

    def cosine(residue, block):
        return float(np.cos(np.pi * residue * block / parts))

    def sine(residue, block):
        return float(np.sin(np.pi * residue * block / parts))

    def spread(index, carry):
        here = pl.ds(index * chunk, chunk)
        there = pl.ds(rows + index * chunk, chunk)
        blocks = [moved_ref[block, here, :].astype(F32) for block in range(parts)]
        for residue in range(parts + 1):
            real = blocks[0]
            imag = jnp.zeros_like(real)
            for block in range(1, parts):
                real = real + cosine(residue, block) * blocks[block]
                imag = imag - sine(residue, block) * blocks[block]
            waves_ref[residue, here, :] = real.astype(BF16)
            waves_ref[residue, there, :] = imag.astype(BF16)
            if 0 < residue < parts:
                waves_ref[2 * parts - residue, here, :] = real.astype(BF16)
                waves_ref[2 * parts - residue, there, :] = (-imag).astype(BF16)
        return carry

    lax.fori_loop(0, rows // chunk, spread, 0)

    def through(residue):
        wave = jnp.dot(forward_ref[residue], waves_ref[residue], preferred_element_type=F32)
        source, odd = divmod(filter_row(residue, width_bits), 2)
        filter_real = moved_ref[source, pl.ds((2 + odd) * rows, rows), :].astype(F32)
        filter_imag = moved_ref[source, pl.ds((4 + odd) * rows, rows), :].astype(F32)
        real, imag = wave[:rows], wave[rows:]
        product = jnp.concatenate(
            [real * filter_real - imag * filter_imag, real * filter_imag + imag * filter_real], axis=0
        )
        return jnp.dot(inverse_ref[residue], product.astype(BF16), preferred_element_type=F32)

    for residue in range(parts + 1):
        back = through(residue)
        if 0 < residue < parts:
            other = through(2 * parts - residue)
            back_ref[residue, pl.ds(0, rows), :] = back[:rows] + other[:rows]
            back_ref[residue, pl.ds(rows, rows), :] = back[rows:] - other[rows:]
        else:
            back_ref[residue] = back

    skip = skip_ref[...]

    def gather(index, carry):
        here = pl.ds(index * chunk, chunk)
        there = pl.ds(rows + index * chunk, chunk)
        reals = [back_ref[residue, here, :] for residue in range(parts + 1)]
        imags = [back_ref[residue, there, :] for residue in range(parts + 1)]
        for block in range(parts):
            total = reals[0]
            for residue in range(1, parts + 1):
                total = total + cosine(residue, block) * reals[residue]
                if residue < parts and block:
                    total = total - sine(residue, block) * imags[residue]
            signal = moved_ref[block, here, :].astype(F32)
            gate = moved_ref[block, pl.ds(rows + index * chunk, chunk), :].astype(F32)
            out_ref[block, here, :] = (gate * (total + skip * signal)).astype(BF16)
        return carry

    lax.fori_loop(0, rows // chunk, gather, 0)


def convolve(moved, skip):
    parts, stacked, width = moved.shape
    rows = stacked // 6
    forward, inverse = dft_tables(parts, rows)
    whole = pl.BlockSpec(memory_space=pltpu.VMEM)
    return pl.pallas_call(
        functools.partial(convolve_kernel, parts, rows),
        out_shape=jax.ShapeDtypeStruct((parts, rows, width), BF16),
        in_specs=[whole] * 4,
        out_specs=whole,
        scratch_shapes=[
            pltpu.VMEM((2 * parts, 2 * rows, width), BF16),
            pltpu.VMEM((parts + 1, 2 * rows, width), F32),
        ],
        compiler_params=pltpu.CompilerParams(vmem_limit_bytes=40 * 2**20),
    )(moved, skip[None, :], forward, inverse)


def shards(values_in, gate_values, filter_spectrum, skip_gain, out_weight):
    parts = lax.axis_size("seq")
    layers = lax.axis_size("chan")
    rows, width = values_in.shape
    lanes = width // parts
    device = lax.axis_index("seq")

    def by_channel(array):
        return jnp.transpose(array.reshape(array.shape[0], parts, lanes), (1, 0, 2))

    filters = filter_spectrum.astype(BF16).reshape(4 * rows, width)
    packed = jnp.concatenate([by_channel(values_in), by_channel(gate_values), by_channel(filters)], axis=1)
    moved = lax.all_to_all(packed, "seq", 0, 0)
    skip = lax.dynamic_slice_in_dim(skip_gain, device * lanes, lanes)
    gated = convolve(moved, skip)
    gathered = lax.all_gather(gated.reshape(parts * rows, lanes), "seq", axis=1, tiled=True)

    own_cols = out_weight.shape[1]
    share = own_cols * parts // layers // parts
    per_block = parts // layers
    pieces = own_cols // share
    group = device % per_block
    member = device // per_block
    weight = jnp.zeros_like(out_weight)
    for step in range(pieces):
        piece = (member + step) % pieces
        sent = lax.dynamic_slice_in_dim(out_weight, piece * share, share, 1)
        pairs = [
            (source, source % per_block * pieces + (source // per_block + step) % pieces) for source in range(parts)
        ]
        arrived = lax.ppermute(sent, "seq", pairs)
        block = (device % pieces - step) % pieces
        weight = lax.dynamic_update_slice_in_dim(weight, arrived, block * share, 1)
    partials = jnp.dot(gathered, weight, preferred_element_type=F32).astype(BF16)
    mixed = lax.psum_scatter(partials, "chan", scatter_dimension=1, tiled=True)
    return lax.all_to_all(mixed, "seq", 0, 1, tiled=True)


def solution(mesh):
    in_specs = (
        P("seq", "chan"),
        P("seq", "chan"),
        P(None, "seq", None, "chan"),
        P("chan"),
        P("chan", "seq"),
    )
    out_specs = P("seq", "chan")
    return jax.shard_map(shards, mesh=mesh, in_specs=in_specs, out_specs=out_specs, check_vma=False)
```

time: 317 us -> 126 us (0.40)
  waiting for transfers between devices: 244 us -> 68.9 us
  other arithmetic: 23.2 us -> 3.04 us
  matrix products: 16.7 us -> 2.86 us
  blocking collectives: 0 us -> 10.4 us
  starting transfers between devices: 9.13 us -> 14.5 us
  Pallas kernels: 0 us -> 3.29 us
    ppermute x6 -> x4, waiting for transfers between devices: 215 us -> 9.7 us  [shards(): arrived = lax.ppermute(sent, 'seq', pairs)]
    reduce_scatter x1 -> x0, waiting for transfers between devices: 28.6 us -> none  [shards(): lax.psum_scatter(partials.astype(jnp.bfloat16), 'chan', scatter_dimension...]
    unnamed x2 -> x3, waiting for transfers between devices: 0.03 us -> 27.3 us
    all_to_all x0 -> x1, waiting for transfers between devices: none -> 20.9 us  [shards(): moved = lax.all_to_all(packed, 'seq', 0, 0)]
    dot_general x9 -> x1, matrix products: 16.7 us -> 2.86 us  [shards(): jnp.dot(gathered, weight, preferred_element_type=F32).astype(BF16)]
    all_gather x1, waiting for transfers between devices: 0.01 us -> 11 us  [shards(): lax.all_gather(gated.reshape(parts * rows, lanes), 'seq', axis=1, tiled=T...]
    all_to_all x0 -> x1, blocking collectives: none -> 10.4 us  [shards(): return lax.all_to_all(mixed, 'seq', 0, 1, tiled=True)]
    another operation x9 -> x0, other arithmetic: 9.36 us -> none  [the longest x2 3.06 us: inverse_section(): jnp.stack([(lower_value[0] + signed * real_part) * 0.5, (lower_value[1] +...]
  transfers between devices with their start and end apart: 8 -> 7, of which waited for: 6 -> 6; matrix products, arithmetic and copies ran while one was open for 12% -> 0% of each run, Pallas kernels for 0% -> 0%
where the time goes in v1:
time: 126 us; the launch traced here: 125 us
  waiting for transfers between devices  68.9 us (55%)
  starting transfers between devices  14.5 us (12%)
  between operations  13.8 us (11%)
  blocking collectives  10.4 us (8%)
  local copies, waits for them, and re-layouts  8.6 us (7%)
  Pallas kernels  3.29 us (3%)
  other arithmetic  3.04 us (2%)
  matrix products  2.86 us (2%)
    unnamed x3, waiting for transfers between devices  27.3 us
    all_to_all x1, waiting for transfers between devices, shards(): moved = lax.all_to_all(packed, 'seq', 0, 0)  20.9 us
    all_gather x1, waiting for transfers between devices, shards(): lax.all_gather(gated.reshape(parts * rows, lanes), 'seq', axis=1, tiled=T...  11 us
    all_to_all x1, blocking collectives, shards(): return lax.all_to_all(mixed, 'seq', 0, 1, tiled=True)  10.4 us
    ppermute x4, waiting for transfers between devices, shards(): arrived = lax.ppermute(sent, 'seq', pairs)  9.7 us
    ppermute x4, starting transfers between devices, shards(): arrived = lax.ppermute(sent, 'seq', pairs)  9.21 us
    unnamed x17, local copies, waits for them, and re-layouts  6.75 us
    all_to_all x1, starting transfers between devices, shards(): moved = lax.all_to_all(packed, 'seq', 0, 0)  5.17 us
  transfers between devices with their start and end apart: 7, of which 6 were waited for; matrix products, arithmetic and copies ran while one was open for 0% of the time, Pallas kernels for 0%

profile of v1, /device:TPU:0, one launch (start us, length us, event | category | flops | bytes accessed | tf_op | source)
XLA Modules:
  0.0 125.3 jit_solution(16680294028819980558)
XLA Ops:
  6.5 1.8 %convert_element_type.6 = bf16[2,2,128,1024]{3,2,1,0:T(8,128)(2,1)S(1)} convert(f32[2,2,128,1024]{3,2,1,0:T(8,128)} %param.9) | non-fusion elementwise | flops 524288 | bytes 3145728 | tf_op jit(solution)/shard_map/convert_element_type | solution.py:138
  8.3 0.3 copy.24
  8.7 0.5 copy-done.4
  9.4 0.2 copy.16
  10.0 1.3 %pad_maximum_fusion = bf16[8,768,128]{2,1,0:T(8,128)(2,1)} fusion(bf16[8,512,128]{2,1,0:T(8,128)(2,1)S(1)} %bitcast.25, bf16[8,128,128]{2,1,0:T(8,128)(2,1)S(1)} %bitcast.30, bf16[8,128,128]{2,1,0:T(8,128)(2,1)S(1)} %bitcast.29), kind=kLoop, calls=%fused_computation | loop fusion | flops 4718592 | bytes 3145728 | tf_op jit(solution)/shard_map/concatenate | solution.py:139
  11.3 5.2 %all-to-all-start = ((bf16[8,768,128]{2,1,0:T(8,128)(2,1)}), bf16[8,768,128]{2,1,0:T(8,128)(2,1)S(1)}, u32[]{:S(2)}, u32[]{:S(2)}) async-start(bf16[8,768,128]{2,1,0:T(8,128)(2,1)} %pad_maximum_fusion), calls=%async_computation | async-start | bytes 3145728 | tf_op jit(solution)/shard_map/all_to_all | solution.py:140
  16.6 20.9 %all-to-all-done.moved_ref = bf16[8,768,128]{2,1,0:T(8,128)(2,1)S(1)} async-done(((bf16[8,768,128]{2,1,0:T(8,128)(2,1)}), bf16[8,768,128]{2,1,0:T(8,128)(2,1)S(1)}, u32[]{:S(2)}, u32[]{:S(2)}) %all-to-all-start) | async-done | bytes 1572896 | tf_op jit(solution)/shard_map/all_to_all | solution.py:140
  37.5 1.6 %copy-done.1 = bf16[16,256,256]{2,1,0:T(8,128)(2,1)S(1)} copy-done((bf16[16,256,256]{2,1,0:T(8,128)(2,1)S(1)}, bf16[16,256,256]{2,1,0:T(8,128)(2,1)}, u32[]{:S(2)}) %copy-start.1) | copy-done | bytes 2097176
  39.1 1.6 %copy-done.2 = bf16[16,256,256]{2,1,0:T(8,128)(2,1)S(1)} copy-done((bf16[16,256,256]{2,1,0:T(8,128)(2,1)S(1)}, bf16[16,256,256]{2,1,0:T(8,128)(2,1)}, u32[]{:S(2)}) %copy-start.2) | copy-done | bytes 2097176
  40.7 3.3 %shard_map.73 = bf16[8,128,128]{2,1,0:T(8,128)(2,1)} custom-call(bf16[8,768,128]{2,1,0:T(8,128)(2,1)S(1)} %all-to-all-done.moved_ref, f32[1,128]{1,0:T(1,128)S(1)} %dynamic-slice_bitcast_fusion.skip_ref, bf16[16,256,256]{2,1,0:T(8,128)(2,1)S(1)} %copy-done.1, bf16[16,256,256]{2,1,0:T(8,128)(2,1)S(1)} %copy-done.2), custom_call_target="tpu_custom_call" | custom-call | tf_op jit(solution)/shard_map/pallas_call | solution.py:115
  44.1 0.2 constant_dynamic-slice_fusion
  44.3 0.7 collective-permute-start
  45.0 3.8 %collective-permute-start.1 = (bf16[1024,128]{1,0:T(8,128)(2,1)S(1)}, bf16[1024,128]{1,0:T(8,128)(2,1)S(1)}, u32[]{:S(2)}, u32[]{:S(2)}) collective-permute-start(bf16[1024,128]{1,0:T(8,128)(2,1)S(1)} %get-tuple-element.6), channel_id=1, source_target_pairs={{0,4},{4,20},{8,8},{12,24},{16,12},{20,28},{24,0},{28,16},{1,5},{5... | collective-permute-start | bytes 786440 | tf_op jit(solution)/shard_map/ppermute | solution.py:158
  48.9 4.7 %collective-permute-start.3 = (bf16[1024,128]{1,0:T(8,128)(2,1)S(1)}, bf16[1024,128]{1,0:T(8,128)(2,1)S(1)}, u32[]{:S(2)}, u32[]{:S(2)}) collective-permute-start(bf16[1024,128]{1,0:T(8,128)(2,1)S(1)} %get-tuple-element.5), channel_id=1, source_target_pairs={{0,12},{4,28},{8,0},{12,16},{16,4},{20,20},{24,8},{28,24},{1,13},{... | collective-permute-start | bytes 786440 | tf_op jit(solution)/shard_map/ppermute | solution.py:158
  53.8 3.1 %collective-permute-done.1 = bf16[1024,128]{1,0:T(8,128)(2,1)S(1)} collective-permute-done((bf16[1024,128]{1,0:T(8,128)(2,1)S(1)}, bf16[1024,128]{1,0:T(8,128)(2,1)S(1)}, u32[]{:S(2)}, u32[]{:S(2)}) %collective-permute-start.1) | collective-permute-done | bytes 262176 | tf_op jit(solution)/shard_map/ppermute | solution.py:158
  57.0 4.0 %collective-permute-done.2 = bf16[1024,128]{1,0:T(8,128)(2,1)S(1)} collective-permute-done((bf16[1024,128]{1,0:T(8,128)(2,1)S(1)}, bf16[1024,128]{1,0:T(8,128)(2,1)S(1)}, u32[]{:S(2)}, u32[]{:S(2)}) %collective-permute-start.2) | collective-permute-done | bytes 262176 | tf_op jit(solution)/shard_map/ppermute | solution.py:158
  61.1 2.6 %collective-permute-done.3 = bf16[1024,128]{1,0:T(8,128)(2,1)S(1)} collective-permute-done((bf16[1024,128]{1,0:T(8,128)(2,1)S(1)}, bf16[1024,128]{1,0:T(8,128)(2,1)S(1)}, u32[]{:S(2)}, u32[]{:S(2)}) %collective-permute-start.3) | collective-permute-done | bytes 262176 | tf_op jit(solution)/shard_map/ppermute | solution.py:158
  63.7 11.0 %all-gather.2.cloned.1.call-done = bf16[1024,1024]{1,0:T(8,128)(2,1)} async-done(((bf16[1024,128]{1,0:T(8,128)(2,1)}), bf16[1024,1024]{1,0:T(8,128)(2,1)}) %all-gather.2.cloned.1.call-update) | async-done | bytes 2097168 | tf_op jit(solution)/shard_map/all_gather | solution.py:143
  74.7 2.9 %convolution_convert_fusion = bf16[1024,512]{1,0:T(8,128)(2,1)S(1)} fusion(bf16[1024,1024]{1,0:T(8,128)(2,1)} %all-gather.2.cloned.1.call-done, bf16[1024,512]{1,0:T(8,128)(2,1)S(1)} %constant_dynamic-update-slice_fusion), kind=kOutput, calls=%fused_computation.1 | convolution fusion | flops 1074266112 | bytes 4194304 | tf_op jit(solution)/shard_map/dot_general | solution.py:161
  77.6 1.3 %copy.21 = bf16[1024,512]{0,1:T(8,128)(2,1)} copy(bf16[1024,512]{1,0:T(8,128)(2,1)S(1)} %convolution_convert_fusion) | data formatting | bytes 2097152
  78.9 27.3 %reduce-scatter.4.cloned.1.call-done = bf16[128,1024]{1,0:T(8,128)(2,1)} async-done(((bf16[512,1024]{1,0:T(8,128)(2,1)}), bf16[128,1024]{1,0:T(8,128)(2,1)}) %reduce-scatter.4.cloned.1.call-update) | async-done | bytes 262160
  106.2 1.1 copy.22
  107.3 10.4 %all_to_all.24 = bf16[8,128,128]{2,1,0:T(8,128)(2,1)S(1)} all-to-all(bf16[8,128,128]{2,1,0:T(8,128)(2,1)S(1)} %bitcast.31), channel_id=1, replica_groups=mesh['seq'=8,'chan'=4] {'seq'}, dimensions={0} | all-to-all | bytes 524288 | tf_op jit(solution)/shard_map/all_to_all | solution.py:163
  117.7 0.7 copy_bitcast_fusion.1
  (25 shorter events, 1.3 us)
Async XLA Ops:
  6.5 10.0 %copy-start = (f32[1024]{0:T(1024)S(1)}, f32[1024]{0:T(1024)}, u32[]{:S(2)}) copy-start(f32[1024]{0:T(1024)} %param.10) | copy-start | bytes 12292
  8.3 1.0 copy-start.4
  8.6 1.0 copy-start.5
  11.3 26.2 %all-to-all-start = ((bf16[8,768,128]{2,1,0:T(8,128)(2,1)}), bf16[8,768,128]{2,1,0:T(8,128)(2,1)S(1)}, u32[]{:S(2)}, u32[]{:S(2)}) async-start(bf16[8,768,128]{2,1,0:T(8,128)(2,1)} %pad_maximum_fusion), calls=%async_computation | async-start | bytes 3145728 | tf_op jit(solution)/shard_map/all_to_all | solution.py:140
  16.5 58.2 %all-gather.2.cloned.1.call-start = ((), (), s32[]{:S(2)}) async-start(), calls=%async_computation.3 | async-start | bytes 2359296 | tf_op jit(solution)/shard_map/all_gather | solution.py:143
  37.5 1.6 %copy-start.1 = (bf16[16,256,256]{2,1,0:T(8,128)(2,1)S(1)}, bf16[16,256,256]{2,1,0:T(8,128)(2,1)}, u32[]{:S(2)}) copy-start(bf16[16,256,256]{2,1,0:T(8,128)(2,1)} %constant.91.clone.forward_ref) | copy-start | bytes 6291460
  39.1 1.6 %copy-start.2 = (bf16[16,256,256]{2,1,0:T(8,128)(2,1)S(1)}, bf16[16,256,256]{2,1,0:T(8,128)(2,1)}, u32[]{:S(2)}) copy-start(bf16[16,256,256]{2,1,0:T(8,128)(2,1)} %constant.92.clone.inverse_ref) | copy-start | bytes 6291460
  40.7 3.5 %copy-start.3 = (bf16[1024,512]{1,0:T(8,128)(2,1)S(1)}, bf16[1024,512]{1,0:T(8,128)(2,1)}, u32[]{:S(2)}) copy-start(bf16[1024,512]{1,0:T(8,128)(2,1)} %param.11) | copy-start | bytes 3145732
  44.0 62.2 %reduce-scatter.4.cloned.1.call-start = ((), (), s32[]{:S(2)}) async-start(), calls=%async_computation.4 | async-start | bytes 1310720
  44.3 9.3 %collective-permute-start = (bf16[1024,128]{1,0:T(8,128)(2,1)S(1)}, bf16[1024,128]{1,0:T(8,128)(2,1)S(1)}, u32[]{:S(2)}, u32[]{:S(2)}) collective-permute-start(bf16[1024,128]{1,0:T(8,128)(2,1)S(1)} %get-tuple-element.7), channel_id=1, source_target_pairs={{0,0},{4,16},{8,4},{12,20},{16,8},{20,24},{24,12},{28,28},{1,1},{5... | collective-permute-start | bytes 786440 | tf_op jit(solution)/shard_map/ppermute | solution.py:158
  45.0 11.9 %collective-permute-start.1 = (bf16[1024,128]{1,0:T(8,128)(2,1)S(1)}, bf16[1024,128]{1,0:T(8,128)(2,1)S(1)}, u32[]{:S(2)}, u32[]{:S(2)}) collective-permute-start(bf16[1024,128]{1,0:T(8,128)(2,1)S(1)} %get-tuple-element.6), channel_id=1, source_target_pairs={{0,4},{4,20},{8,8},{12,24},{16,12},{20,28},{24,0},{28,16},{1,5},{5... | collective-permute-start | bytes 786440 | tf_op jit(solution)/shard_map/ppermute | solution.py:158
  48.8 12.2 %collective-permute-start.2 = (bf16[1024,128]{1,0:T(8,128)(2,1)S(1)}, bf16[1024,128]{1,0:T(8,128)(2,1)S(1)}, u32[]{:S(2)}, u32[]{:S(2)}) collective-permute-start(bf16[1024,128]{1,0:T(8,128)(2,1)S(1)} %get-tuple-element.8), channel_id=1, source_target_pairs={{0,8},{4,24},{8,12},{12,28},{16,0},{20,16},{24,4},{28,20},{1,9},{5... | collective-permute-start | bytes 786440 | tf_op jit(solution)/shard_map/ppermute | solution.py:158
  48.9 14.8 %collective-permute-start.3 = (bf16[1024,128]{1,0:T(8,128)(2,1)S(1)}, bf16[1024,128]{1,0:T(8,128)(2,1)S(1)}, u32[]{:S(2)}, u32[]{:S(2)}) collective-permute-start(bf16[1024,128]{1,0:T(8,128)(2,1)S(1)} %get-tuple-element.5), channel_id=1, source_target_pairs={{0,12},{4,28},{8,0},{12,16},{16,4},{20,20},{24,8},{28,24},{1,13},{... | collective-permute-start | bytes 786440 | tf_op jit(solution)/shard_map/ppermute | solution.py:158
Sparse Core Ops, SparseCore 0:
  44.1 30.5 all-gather.1
  79.0 27.1 reduce-scatter.3

commit v2 on v1

--- a/solution.py
+++ b/solution.py
@@ -125,7 +125,7 @@
     )(moved, skip[None, :], forward, inverse)
 
 
-def shards(values_in, gate_values, filter_spectrum, skip_gain, out_weight):
+def shards_general(values_in, gate_values, filter_spectrum, skip_gain, out_weight):
     parts = lax.axis_size("seq")
     layers = lax.axis_size("chan")
     rows, width = values_in.shape
@@ -163,6 +163,394 @@
     return lax.all_to_all(mixed, "seq", 0, 1, tiled=True)
 
 
+def small_tables(parts, rows):
+    total = 2 * parts * rows
+    index = np.arange(rows)
+    phase = 2.0 * np.pi * (index[:, None] * index[None, :] % rows) / rows
+    cos, sin = np.cos(phase), np.sin(phase)
+    forward = np.block([[cos, sin], [-sin, cos]])
+    turn = 2.0 * np.pi * (index[:, None] * np.arange(2 * parts)[None, :]) / total
+    return forward.astype(BF16), forward.T.astype(BF16), np.cos(turn).astype(F32), np.sin(turn).astype(F32)
+
+
+def cosine(parts, residue, block):
+    return float(np.cos(np.pi * residue * block / parts))
+
+
+def sine(parts, residue, block):
+    return float(np.sin(np.pi * residue * block / parts))
+
+
+def weighted(terms):
+    total = None
+    for factor, term in terms:
+        if abs(factor) < 1e-12:
+            continue
+        part = term if factor == 1.0 else factor * term
+        total = part if total is None else total + part
+    return total
+
+
+def plus(left, right):
+    return left if right is None else right if left is None else left + right
+
+
+def minus(left, right):
+    return left if right is None else -right if left is None else left - right
+
+
+def pack_filters_kernel(parts, lanes, device_ref, filter_ref, *out_refs):
+    for offset in range(parts):
+        start = pl.multiple_of((device_ref[0] ^ offset) * lanes, lanes)
+        out_refs[offset][0] = filter_ref[0, :, pl.ds(start, lanes)].astype(BF16)
+
+
+def pack_filters(device, filters):
+    planes, rows, width = filters.shape
+    parts = lax.axis_size("seq")
+    lanes = width // parts
+    return pl.pallas_call(
+        functools.partial(pack_filters_kernel, parts, lanes),
+        grid=(planes,),
+        in_specs=[
+            pl.BlockSpec(memory_space=pltpu.SMEM),
+            pl.BlockSpec((1, rows, width), lambda plane: (plane, 0, 0)),
+        ],
+        out_specs=[pl.BlockSpec((1, rows, lanes), lambda plane: (plane, 0, 0))] * parts,
+        out_shape=[jax.ShapeDtypeStruct((planes, rows, lanes), BF16)] * parts,
+        name="pack_filters",
+    )(device, filters)
+
+
+def pack_signals_kernel(parts, lanes, device_ref, values_ref, gate_ref, *out_refs):
+    for offset in range(parts):
+        start = pl.multiple_of((device_ref[0] ^ offset) * lanes, lanes)
+        out_refs[offset][0] = values_ref[:, pl.ds(start, lanes)]
+        out_refs[offset][1] = gate_ref[:, pl.ds(start, lanes)]
+
+
+def pack_signals(device, values_in, gate_values):
+    rows, width = values_in.shape
+    parts = lax.axis_size("seq")
+    lanes = width // parts
+    return pl.pallas_call(
+        functools.partial(pack_signals_kernel, parts, lanes),
+        in_specs=[pl.BlockSpec(memory_space=pltpu.SMEM)] + [pl.BlockSpec(memory_space=pltpu.VMEM)] * 2,
+        out_specs=[pl.BlockSpec(memory_space=pltpu.VMEM)] * parts,
+        out_shape=[jax.ShapeDtypeStruct((2, rows, lanes), BF16)] * parts,
+        name="pack_signals",
+    )(device, values_in, gate_values)
+
+
+def forward_kernel(parts, rows, lanes, device_ref, cos_ref, sin_ref, table_ref, *refs):
+    signal_refs, out_ref, signal_ref, waves_ref = refs[:parts], refs[parts], refs[parts + 1], refs[parts + 2]
+    chunk = 16
+    for offset in range(parts):
+        signal_ref[device_ref[0] ^ offset] = signal_refs[offset][0]
+
+    def spread(index, carry):
+        here = pl.ds(pl.multiple_of(index * chunk, chunk), chunk)
+        there = pl.ds(pl.multiple_of(rows + index * chunk, chunk), chunk)
+        cos_all, sin_all = cos_ref[here, :], sin_ref[here, :]
+        blocks = [signal_ref[block, here, :].astype(F32) for block in range(parts)]
+
+        def store(residue, real, imag):
+            if residue:
+                cos, sin = cos_all[:, residue : residue + 1], sin_all[:, residue : residue + 1]
+                if imag is None:
+                    real, imag = real * cos, -(real * sin)
+                else:
+                    real, imag = real * cos + imag * sin, imag * cos - real * sin
+            if imag is None:
+                imag = jnp.zeros_like(real)
+            columns = pl.ds(residue * lanes, lanes)
+            waves_ref[here, columns] = real.astype(BF16)
+            waves_ref[there, columns] = imag.astype(BF16)
+
+        def store_both(residue, real, imag):
+            store(residue, real, imag)
+            if 0 < residue < parts:
+                store(2 * parts - residue, real, None if imag is None else -imag)
+
+        for residue in range(parts // 2 + 1):
+            even = range(0, parts, 2)
+            odd = range(1, parts, 2)
+            cos_even = weighted([(cosine(parts, residue, block), blocks[block]) for block in even])
+            cos_odd = weighted([(cosine(parts, residue, block), blocks[block]) for block in odd])
+            sin_even = weighted([(sine(parts, residue, block), blocks[block]) for block in even])
+            sin_odd = weighted([(sine(parts, residue, block), blocks[block]) for block in odd])
+            sin_sum = plus(sin_even, sin_odd)
+            store_both(residue, plus(cos_even, cos_odd), None if sin_sum is None else -sin_sum)
+            if 2 * residue != parts:
+                store_both(parts - residue, minus(cos_even, cos_odd), minus(sin_even, sin_odd))
+        return carry
+
+    lax.fori_loop(0, rows // chunk, spread, 0)
+    for pair in range(parts):
+        columns = pl.ds(2 * pair * lanes, 2 * lanes)
+        out_ref[:, columns] = jnp.dot(table_ref[...], waves_ref[:, columns], preferred_element_type=F32)
+
+
+def forward(device, signals, tables):
+    parts = len(signals)
+    rows, lanes = signals[0].shape[1:]
+    forward_table, _, cos, sin = tables
+    whole = pl.BlockSpec(memory_space=pltpu.VMEM)
+    return pl.pallas_call(
+        functools.partial(forward_kernel, parts, rows, lanes),
+        in_specs=[pl.BlockSpec(memory_space=pltpu.SMEM)] + [whole] * (3 + parts),
+        out_specs=whole,
+        out_shape=jax.ShapeDtypeStruct((2 * rows, 2 * parts * lanes), F32),
+        scratch_shapes=[
+            pltpu.VMEM((parts, rows, lanes), BF16),
+            pltpu.VMEM((2 * rows, 2 * parts * lanes), BF16),
+        ],
+        compiler_params=pltpu.CompilerParams(vmem_limit_bytes=32 * 2**20),
+        name="forward",
+    )(device, cos, sin, forward_table, *signals)
+
+
+def backward_kernel(parts, rows, lanes, device_ref, cos_ref, sin_ref, table_ref, spectrum_ref, skip_ref, *refs):
+    signal_refs, filter_refs = refs[:parts], refs[parts : 2 * parts]
+    mine_ref, other_ref, signal_ref, filter_ref, product_ref, back_ref, gated_ref = refs[2 * parts :]
+    width_bits = parts.bit_length() - 1
+    chunk = 16
+    device = device_ref[0]
+    for offset in range(parts):
+        signal_ref[device ^ offset] = signal_refs[offset][...]
+        filter_ref[device ^ offset] = filter_refs[offset][...]
+
+    for residue in range(2 * parts):
+        source, odd = divmod(filter_row(residue, width_bits), 2)
+        columns = pl.ds(residue * lanes, lanes)
+        filter_real = filter_ref[source, odd].astype(F32)
+        filter_imag = filter_ref[source, 2 + odd].astype(F32)
+        real = spectrum_ref[pl.ds(0, rows), columns]
+        imag = spectrum_ref[pl.ds(rows, rows), columns]
+        product_ref[pl.ds(0, rows), columns] = (real * filter_real - imag * filter_imag).astype(BF16)
+        product_ref[pl.ds(rows, rows), columns] = (real * filter_imag + imag * filter_real).astype(BF16)
+        if residue % 2:
+            columns = pl.ds((residue - 1) * lanes, 2 * lanes)
+            back_ref[:, columns] = jnp.dot(table_ref[...], product_ref[:, columns], preferred_element_type=F32)
+
+    skip = skip_ref[...]
+    scale = 1.0 / (2 * parts * rows)
+
+    def gather(index, carry):
+        here = pl.ds(pl.multiple_of(index * chunk, chunk), chunk)
+        there = pl.ds(pl.multiple_of(rows + index * chunk, chunk), chunk)
+        cos_all, sin_all = cos_ref[here, :] * scale, sin_ref[here, :] * scale
+
+        def turned(residue):
+            columns = pl.ds(residue * lanes, lanes)
+            real, imag = back_ref[here, columns], back_ref[there, columns]
+            if not residue:
+                return real * scale, None
+            cos, sin = cos_all[:, residue : residue + 1], sin_all[:, residue : residue + 1]
+            return real * cos - imag * sin, real * sin + imag * cos
+
+        reals, imags = [], []
+        for residue in range(parts + 1):
+            real, imag = turned(residue)
+            if 0 < residue < parts:
+                other_real, other_imag = turned(2 * parts - residue)
+                real, imag = real + other_real, imag - other_imag
+            reals.append(real)
+            imags.append(imag)
+
+        def store(block, total):
+            signal = signal_ref[block, 0, here, :].astype(F32)
+            gate = signal_ref[block, 1, here, :].astype(F32)
+            gated_ref[block, here, :] = (gate * (total + skip * signal)).astype(BF16)
+
+        for block in range(parts // 2 + 1):
+            even = range(0, parts + 1, 2)
+            odd = range(1, parts + 1, 2)
+            cos_even = weighted([(cosine(parts, residue, block), reals[residue]) for residue in even])
+            cos_odd = weighted([(cosine(parts, residue, block), reals[residue]) for residue in odd])
+            sin_even = weighted([(sine(parts, residue, block), imags[residue]) for residue in even])
+            sin_odd = weighted([(sine(parts, residue, block), imags[residue]) for residue in odd])
+            store(block, minus(plus(cos_even, cos_odd), plus(sin_even, sin_odd)))
+            if 0 < block and 2 * block != parts:
+                store(parts - block, plus(minus(cos_even, cos_odd), minus(sin_even, sin_odd)))
+        return carry
+
+    lax.fori_loop(0, rows // chunk, gather, 0)
+    for chip in range(parts // 2):
+        mine_ref[chip] = gated_ref[2 * chip + device % 2]
+        other_ref[chip] = gated_ref[2 * chip + 1 - device % 2]
+
+
+def backward(device, spectrum, skip, signals, filters, tables):
+    parts = len(signals)
+    rows, lanes = signals[0].shape[1:]
+    _, inverse_table, cos, sin = tables
+    whole = pl.BlockSpec(memory_space=pltpu.VMEM)
+    return pl.pallas_call(
+        functools.partial(backward_kernel, parts, rows, lanes),
+        in_specs=[pl.BlockSpec(memory_space=pltpu.SMEM)] + [whole] * (5 + 2 * parts),
+        out_specs=[whole] * 2,
+        out_shape=[jax.ShapeDtypeStruct((parts // 2, rows, lanes), BF16)] * 2,
+        scratch_shapes=[
+            pltpu.VMEM((parts, 2, rows, lanes), BF16),
+            pltpu.VMEM((parts, 4, rows, lanes), BF16),
+            pltpu.VMEM((2 * rows, 2 * parts * lanes), BF16),
+            pltpu.VMEM((2 * rows, 2 * parts * lanes), F32),
+            pltpu.VMEM((parts, rows, lanes), BF16),
+        ],
+        compiler_params=pltpu.CompilerParams(vmem_limit_bytes=40 * 2**20),
+        name="backward",
+    )(device, cos, sin, inverse_table, spectrum, skip, *signals, *filters)
+
+
+def arrange_kernel(layers, share, place_ref, *refs):
+    own_refs, other_refs, out_ref = refs[:layers], refs[layers : 2 * layers], refs[2 * layers]
+    device, layer = place_ref[0], place_ref[1]
+    own_start = pl.multiple_of(device % 2 * share, share)
+    other_start = pl.multiple_of((1 - device % 2) * share, share)
+    for step in range(layers):
+        target = device % layers ^ layer ^ step
+        out_ref[target, :, pl.ds(own_start, share)] = own_refs[step][...]
+        out_ref[target, :, pl.ds(other_start, share)] = other_refs[step ^ 1][...]
+
+
+def arrange(place, own, other):
+    layers = len(own)
+    rows, share = own[0].shape
+    whole = pl.BlockSpec(memory_space=pltpu.VMEM)
+    return pl.pallas_call(
+        functools.partial(arrange_kernel, layers, share),
+        in_specs=[pl.BlockSpec(memory_space=pltpu.SMEM)] + [whole] * (2 * layers),
+        out_specs=whole,
+        out_shape=jax.ShapeDtypeStruct((layers, rows, 2 * share), BF16),
+        compiler_params=pltpu.CompilerParams(vmem_limit_bytes=32 * 2**20),
+        name="arrange_weights",
+    )(place, *own, *other)
+
+
+def project_kernel(parts, layers, place_ref, weight_ref, *refs):
+    gated_refs, out_refs, joined_ref = refs[:parts], refs[parts : parts + layers], refs[parts + layers]
+    lanes = gated_refs[0].shape[1]
+    for offset in range(parts):
+        start = pl.multiple_of((place_ref[0] ^ offset) * lanes, lanes)
+        joined_ref[:, pl.ds(start, lanes)] = gated_refs[offset][...]
+    for target in reversed(range(layers)):
+        out_refs[target][...] = jnp.dot(joined_ref[...], weight_ref[target], preferred_element_type=F32).astype(BF16)
+
+
+def project(place, weight, gated):
+    parts = len(gated)
+    layers, depth, columns = weight.shape
+    rows = gated[0].shape[0]
+    whole = pl.BlockSpec(memory_space=pltpu.VMEM)
+    return pl.pallas_call(
+        functools.partial(project_kernel, parts, layers),
+        in_specs=[pl.BlockSpec(memory_space=pltpu.SMEM)] + [whole] * (1 + parts),
+        out_specs=[whole] * layers,
+        out_shape=[jax.ShapeDtypeStruct((rows, columns), BF16)] * layers,
+        scratch_shapes=[pltpu.VMEM((rows, depth), BF16)],
+        compiler_params=pltpu.CompilerParams(vmem_limit_bytes=32 * 2**20),
+        name="project",
+    )(place, weight, *gated)
+
+
+def add_kernel(chips, place_ref, *refs):
+    in_refs, out_refs = refs[:-chips], refs[-chips:]
+    rows = out_refs[0].shape[0]
+    for offset in range(chips):
+        start = pl.multiple_of((place_ref[0] // 2 ^ offset) * rows, rows)
+        here = pl.ds(start, rows)
+        total = in_refs[0][here, :].astype(F32)
+        for in_ref in in_refs[1:]:
+            total = total + in_ref[here, :].astype(F32)
+        out_refs[offset][...] = total.astype(BF16)
+
+
+def add_partials(place, partials, chips):
+    rows, columns = partials[0].shape
+    whole = pl.BlockSpec(memory_space=pltpu.VMEM)
+    return pl.pallas_call(
+        functools.partial(add_kernel, chips),
+        in_specs=[pl.BlockSpec(memory_space=pltpu.SMEM)] + [whole] * len(partials),
+        out_specs=[whole] * chips,
+        out_shape=[jax.ShapeDtypeStruct((rows // chips, columns), BF16)] * chips,
+        name="add_partials",
+    )(place, *partials)
+
+
+def join_kernel(chips, place_ref, *refs):
+    in_refs, out_ref = refs[:chips], refs[chips]
+    columns = in_refs[0].shape[1]
+    for offset in range(chips):
+        start = pl.multiple_of((place_ref[0] // 2 ^ offset) * columns, columns)
+        out_ref[:, pl.ds(start, columns)] = in_refs[offset][...]
+
+
+def join(place, blocks):
+    chips = len(blocks)
+    rows, columns = blocks[0].shape
+    whole = pl.BlockSpec(memory_space=pltpu.VMEM)
+    return pl.pallas_call(
+        functools.partial(join_kernel, chips),
+        in_specs=[pl.BlockSpec(memory_space=pltpu.SMEM)] + [whole] * chips,
+        out_specs=whole,
+        out_shape=jax.ShapeDtypeStruct((rows, chips * columns), BF16),
+        name="join",
+    )(place, *blocks)
+
+
+def swapped(value, axis, offset):
+    if not offset:
+        return value
+    return lax.ppermute(value, axis, [(source, source ^ offset) for source in range(lax.axis_size(axis))])
+
+
+def shards_direct(values_in, gate_values, filter_spectrum, skip_gain, out_weight):
+    parts = lax.axis_size("seq")
+    layers = lax.axis_size("chan")
+    chips = parts // 2
+    rows, width = values_in.shape
+    lanes = width // parts
+    device = lax.axis_index("seq")
+    place = jnp.stack([device, lax.axis_index("chan")])
+    tables = small_tables(parts, rows)
+    offsets = range(parts)
+
+    signals = [swapped(block, "seq", offset) for offset, block in enumerate(pack_signals(place, values_in, gate_values))]
+    filters = pack_filters(place, filter_spectrum.reshape(4, rows, width))
+    filters = [swapped(block, "seq", offset) for offset, block in enumerate(filters)]
+
+    share = out_weight.shape[1] // layers
+    own_weight = []
+    for step in range(layers):
+        sent = lax.dynamic_slice_in_dim(out_weight, (device // 2 ^ step) * share, share, 1)
+        pairs = [(source, source % 2 * layers + (source // 2 ^ step)) for source in range(parts)]
+        own_weight.append(lax.ppermute(sent, "seq", pairs))
+    other_weight = [swapped(block, "seq", 1) for block in own_weight]
+    weight = arrange(place, own_weight, other_weight)
+
+    skip = lax.dynamic_slice_in_dim(skip_gain, device * lanes, lanes)[None, :]
+    spectrum = forward(place, signals, tables)
+    mine, other = backward(place, spectrum, skip, signals, filters, tables)
+    gated = [swapped(other if offset % 2 else mine, "seq", offset) for offset in offsets]
+    gated = [block.reshape(chips * rows, lanes) for block in gated]
+    partials = project(place, weight, gated)
+    partials = [swapped(block, "chan", offset) for offset, block in enumerate(partials)]
+    blocks = add_partials(place, partials, chips)
+    blocks = [swapped(block, "seq", 2 * offset) for offset, block in enumerate(blocks)]
+    return join(place, blocks)
+
+
+def shards(values_in, gate_values, filter_spectrum, skip_gain, out_weight):
+    parts = lax.axis_size("seq")
+    layers = lax.axis_size("chan")
+    lanes = values_in.shape[1] // parts
+    share = out_weight.shape[1] // layers
+    aligned = lanes % 128 == 0 and share % 128 == 0 and values_in.shape[0] % 16 == 0
+    run = shards_direct if aligned and parts == 2 * layers else shards_general
+    return run(values_in, gate_values, filter_spectrum, skip_gain, out_weight)
+
+
 def solution(mesh):
     in_specs = (
         P("seq", "chan"),

time: 126 us -> 112 us (0.89)
  the two profiles are of different devices: /device:TPU:0 before, /device:TPU:8 now
where the time goes in v2:
time: 112 us
  waiting for transfers between devices  56.2 us (50%)
  starting transfers between devices  33.9 us (30%)
  Pallas kernels  17.6 us (16%)
  local copies, waits for them, and re-layouts  3.13 us (3%)
    ppermute x31, waiting for transfers between devices, swapped(): lax.ppermute(value, axis, [(source, source ^ offset) for source in range(...  56.2 us
    ppermute x31, starting transfers between devices, swapped(): lax.ppermute(value, axis, [(source, source ^ offset) for source in range(...  26.9 us
    ppermute x4, starting transfers between devices, shards_direct(): own_weight.append(lax.ppermute(sent, 'seq', pairs))  7.02 us
    pallas_call x1, Pallas kernels, pack_filters(): pl.pallas_call(functools.partial(pack_filters_kernel, parts, lanes), grid...  3.77 us
    pallas_call x1, Pallas kernels, backward(): pl.pallas_call(functools.partial(backward_kernel, parts, rows, lanes), in...  2.94 us
    pallas_call x1, Pallas kernels, forward(): pl.pallas_call(functools.partial(forward_kernel, parts, rows, lanes), in_...  2.25 us
  transfers between devices with their start and end apart: 35, of which 16 were waited for; matrix products, arithmetic and copies ran while one was open for 1% of the time, Pallas kernels for 9%

profile of v2, /device:TPU:8, one launch (start us, length us, event | category | flops | bytes accessed | tf_op | source)
XLA Modules:
  0.0 111.6 jit_solution(14137581711550490943)
XLA Ops:
  0.6 2.0 %pack_signals.1 = (bf16[2,128,128]{2,1,0:T(8,128)(2,1)}, bf16[2,128,128]{2,1,0:T(8,128)(2,1)}, bf16[2,128,128]{2,1,0:T(8,128)(2,1)}, bf16[2,128,128]{2,1,0:T(8,1...) custom-call(s32[2]{0:T(128)} %pad_add_fusion.place_ref.device_ref, ...), custom_call_target="tpu_custom_call" | custom-call | tf_op jit(solution)/shard_map/pack_signals/pallas_call | solution.py:236
  5.7 3.8 %pack_filters.1 = (bf16[4,128,128]{2,1,0:T(8,128)(2,1)}, bf16[4,128,128]{2,1,0:T(8,128)(2,1)}, bf16[4,128,128]{2,1,0:T(8,128)(2,1)}, bf16[4,128,128]{2,1,0:T(8,1...) custom-call(s32[2]{0:T(128)} %pad_add_fusion.place_ref.device_ref, ...), custom_call_target="tpu_custom_call" | custom-call | tf_op jit(solution)/shard_map/pack_filters/pallas_call | solution.py:212
  13.3 1.6 %collective-permute-done.13.refs_6_ = bf16[2,128,128]{2,1,0:T(8,128)(2,1)S(1)} collective-permute-done((bf16[2,128,128]{2,1,0:T(8,128)(2,1)S(1)}, bf16[2,128,128]{2,1,0:T(8,128)(2,1)S(1)}, u32[]{:S(2)}, u32[]{:S(2)}) %collective-permute-start.13) | collective-permute-done | bytes 65568 | tf_op jit(solution)/shard_map/ppermute | solution.py:505
  23.1 2.3 %collective-permute-start.1 = (bf16[1024,128]{1,0:T(8,128)(2,1)}, bf16[1024,128]{1,0:T(8,128)(2,1)S(1)}, u32[]{:S(2)}, u32[]{:S(2)}) collective-permute-start(bf16[1024,128]{1,0:T(8,128)(2,1)} %get-tuple-element.58), channel_id=1, source_target_pairs={{0,4},{4,20},{8,0},{12,16},{16,12},{20,28},{24,8},{28,24},{1,5},{5... | collective-permute-start | bytes 786440 | tf_op jit(solution)/shard_map/ppermute | solution.py:528
  26.6 3.8 %collective-permute-done.19.refs_13_ = bf16[4,128,128]{2,1,0:T(8,128)(2,1)S(1)} collective-permute-done((bf16[4,128,128]{2,1,0:T(8,128)(2,1)}, bf16[4,128,128]{2,1,0:T(8,128)(2,1)S(1)}, u32[]{:S(2)}, u32[]{:S(2)}) %collective-permute-start.19) | collective-permute-done | bytes 131104 | tf_op jit(solution)/shard_map/ppermute | solution.py:505
  30.4 1.9 %collective-permute-start.3 = (bf16[1024,128]{1,0:T(8,128)(2,1)S(1)}, bf16[1024,128]{1,0:T(8,128)(2,1)S(1)}, u32[]{:S(2)}, u32[]{:S(2)}) collective-permute-start(bf16[1024,128]{1,0:T(8,128)(2,1)S(1)} %get-tuple-element.57), channel_id=1, source_target_pairs={{0,12},{4,28},{8,8},{12,24},{16,4},{20,20},{24,0},{28,16},{1,13},{... | collective-permute-start | bytes 786440 | tf_op jit(solution)/shard_map/ppermute | solution.py:528
  32.3 3.9 %collective-permute-start.21 = (bf16[4,128,128]{2,1,0:T(8,128)(2,1)}, bf16[4,128,128]{2,1,0:T(8,128)(2,1)S(1)}, u32[]{:S(2)}, u32[]{:S(2)}) collective-permute-start(bf16[4,128,128]{2,1,0:T(8,128)(2,1)} %get-tuple-element.46), channel_id=1, source_target_pairs={{0,28},{4,24},{8,20},{12,16},{16,12},{20,8},{24,4},{28,0},{1,29},{... | collective-permute-start | bytes 393224 | tf_op jit(solution)/shard_map/ppermute | solution.py:505
  36.3 2.3 %forward.1.spectrum_ref = f32[256,2048]{1,0:T(8,128)S(1)} custom-call(s32[2]{0:T(128)S(1)} %copy-done.8, f32[128,16]{1,0:T(8,128)S(1)} %copy-done.1, f32[128,16]{1,0:T(8,128)S(1)} %copy-done.2, bf16[256,256]{1,0:T(8,128)(2,1)S(1)} %copy-done.6, bf16[2,128,128]{2,1,0:T(8,128)(2,1)S(1)} %copy-done.3, bf16[2,128,128]{2,1,0:T(8,128)(2,1)S(1)} %collective-permute-done.8.refs_1_, ...), custom_call_target="tpu_custom_call" | custom-call | tf_op jit(solution)/shard_map/forward/pallas_call | solution.py:299
  38.6 6.6 %collective-permute-done.21.refs_15_ = bf16[4,128,128]{2,1,0:T(8,128)(2,1)S(1)} collective-permute-done((bf16[4,128,128]{2,1,0:T(8,128)(2,1)}, bf16[4,128,128]{2,1,0:T(8,128)(2,1)S(1)}, u32[]{:S(2)}, u32[]{:S(2)}) %collective-permute-start.21) | collective-permute-done | bytes 131104 | tf_op jit(solution)/shard_map/ppermute | solution.py:505
  45.2 2.9 %backward.1 = (bf16[4,128,128]{2,1,0:T(8,128)(2,1)S(1)}, bf16[4,128,128]{2,1,0:T(8,128)(2,1)S(1)}) custom-call(s32[2]{0:T(128)S(1)} %copy-done.8, f32[128,16]{1,0:T(8,128)S(1)} %copy-done.1, f32[128,16]{1,0:T(8,128)S(1)} %copy-done.2, bf16[256,256]{1,0:T(8,128)(2,1)S(1)} %copy-done.5, f32[256,2048]{1,0:T(8,128)S(1)} %forward.1.spectrum_ref, ...), custom_call_target="tpu_custom_call" | custom-call | tf_op jit(solution)/shard_map/backward/pallas_call | solution.py:389
  49.3 4.7 %collective-permute-done.27 = bf16[4,128,128]{2,1,0:T(8,128)(2,1)S(1)} collective-permute-done((bf16[4,128,128]{2,1,0:T(8,128)(2,1)S(1)}, bf16[4,128,128]{2,1,0:T(8,128)(2,1)S(1)}, u32[]{:S(2)}, u32[]{:S(2)}) %collective-permute-start.27) | collective-permute-done | bytes 131104 | tf_op jit(solution)/shard_map/ppermute | solution.py:505
  54.1 5.3 %collective-permute-done.28 = bf16[4,128,128]{2,1,0:T(8,128)(2,1)S(1)} collective-permute-done((bf16[4,128,128]{2,1,0:T(8,128)(2,1)S(1)}, bf16[4,128,128]{2,1,0:T(8,128)(2,1)S(1)}, u32[]{:S(2)}, u32[]{:S(2)}) %collective-permute-start.28) | collective-permute-done | bytes 131104 | tf_op jit(solution)/shard_map/ppermute | solution.py:505
  59.4 1.9 %collective-permute-start.24 = (bf16[4,128,128]{2,1,0:T(8,128)(2,1)S(1)}, bf16[4,128,128]{2,1,0:T(8,128)(2,1)S(1)}, u32[]{:S(2)}, u32[]{:S(2)}) collective-permute-start(bf16[4,128,128]{2,1,0:T(8,128)(2,1)S(1)} %get-tuple-element.48), channel_id=1, source_target_pairs={{0,12},{4,8},{8,4},{12,0},{16,28},{20,24},{24,20},{28,16},{1,13},{... | collective-permute-start | bytes 393224 | tf_op jit(solution)/shard_map/ppermute | solution.py:505
  63.8 1.9 %collective-permute-done.23 = bf16[4,128,128]{2,1,0:T(8,128)(2,1)S(1)} collective-permute-done((bf16[4,128,128]{2,1,0:T(8,128)(2,1)S(1)}, bf16[4,128,128]{2,1,0:T(8,128)(2,1)S(1)}, u32[]{:S(2)}, u32[]{:S(2)}) %collective-permute-start.23) | collective-permute-done | bytes 131104 | tf_op jit(solution)/shard_map/ppermute | solution.py:505
  65.7 2.1 %collective-permute-done.24 = bf16[4,128,128]{2,1,0:T(8,128)(2,1)S(1)} collective-permute-done((bf16[4,128,128]{2,1,0:T(8,128)(2,1)S(1)}, bf16[4,128,128]{2,1,0:T(8,128)(2,1)S(1)}, u32[]{:S(2)}, u32[]{:S(2)}) %collective-permute-start.24) | collective-permute-done | bytes 131104 | tf_op jit(solution)/shard_map/ppermute | solution.py:505
  69.1 2.1 %project.1 = (bf16[512,256]{1,0:T(8,128)(2,1)S(1)}, bf16[512,256]{1,0:T(8,128)(2,1)S(1)}, bf16[512,256]{1,0:T(8,128)(2,1)S(1)}, bf16[512,256]{1,0:T(8,128)(2,1)S(1)}) custom-call(s32[2]{0:T(128)S(1)} %copy-done.8, bf16[4,1024,256]{2,1,0:T(8,128)(2,1)S(1)} %arrange_weights.1.weight_ref, bf16[512,128]{1,0:T(8,128)(2,1)S(1)} %bitcast.13, ...), custom_call_target="tpu_custom_call" | custom-call | tf_op jit(solution)/shard_map/project/pallas_call | solution.py:446
  72.3 2.6 %collective-permute-start.30 = (bf16[512,256]{1,0:T(8,128)(2,1)S(1)}, bf16[512,256]{1,0:T(8,128)(2,1)S(1)}, u32[]{:S(2)}, u32[]{:S(2)}) collective-permute-start(bf16[512,256]{1,0:T(8,128)(2,1)S(1)} %get-tuple-element.51), channel_id=1, source_target_pairs={{0,2},{1,3},{2,0},{3,1},{4,6},{5,7},{6,4},{7,5},{8,10},{9,11},{10,... | collective-permute-start | bytes 786440 | tf_op jit(solution)/shard_map/ppermute | solution.py:505
  75.3 8.4 %collective-permute-done.29.refs_1_ = bf16[512,256]{1,0:T(8,128)(2,1)S(1)} collective-permute-done((bf16[512,256]{1,0:T(8,128)(2,1)S(1)}, bf16[512,256]{1,0:T(8,128)(2,1)S(1)}, u32[]{:S(2)}, u32[]{:S(2)}) %collective-permute-start.29) | collective-permute-done | bytes 262176 | tf_op jit(solution)/shard_map/ppermute | solution.py:505
  83.7 9.1 %collective-permute-done.30.refs_2_ = bf16[512,256]{1,0:T(8,128)(2,1)S(1)} collective-permute-done((bf16[512,256]{1,0:T(8,128)(2,1)S(1)}, bf16[512,256]{1,0:T(8,128)(2,1)S(1)}, u32[]{:S(2)}, u32[]{:S(2)}) %collective-permute-start.30) | collective-permute-done | bytes 262176 | tf_op jit(solution)/shard_map/ppermute | solution.py:505
  92.8 5.8 %collective-permute-done.31.refs_3_ = bf16[512,256]{1,0:T(8,128)(2,1)S(1)} collective-permute-done((bf16[512,256]{1,0:T(8,128)(2,1)S(1)}, bf16[512,256]{1,0:T(8,128)(2,1)S(1)}, u32[]{:S(2)}, u32[]{:S(2)}) %collective-permute-start.31) | collective-permute-done | bytes 262176 | tf_op jit(solution)/shard_map/ppermute | solution.py:505
  99.3 2.0 %add_partials.1 = (bf16[128,256]{1,0:T(8,128)(2,1)}, bf16[128,256]{1,0:T(8,128)(2,1)}, bf16[128,256]{1,0:T(8,128)(2,1)}, bf16[128,256]{1,0:T(8,128)(2,1)}) custom-call(s32[2]{0:T(128)} %pad_add_fusion.place_ref.device_ref, bf16[512,256]{1,0:T(8,128)(2,1)} %copy-done.4, bf16[512,256]{1,0:T(8,128)(2,1)} %copy-done.10, bf16[512,256]{1,0:T(8,128)(2,1)} %copy-done.11, ...), custom_call_target="tpu_custom_call" | custom-call | tf_op jit(solution)/shard_map/add_partials/pallas_call | solution.py:472
  102.2 1.7 %collective-permute-start.33 = (bf16[128,256]{1,0:T(8,128)(2,1)}, bf16[128,256]{1,0:T(8,128)(2,1)S(1)}, u32[]{:S(2)}, u32[]{:S(2)}) collective-permute-start(bf16[128,256]{1,0:T(8,128)(2,1)} %get-tuple-element.55), channel_id=1, source_target_pairs={{0,16},{4,20},{8,24},{12,28},{16,0},{20,4},{24,8},{28,12},{1,17},{... | collective-permute-start | bytes 196616 | tf_op jit(solution)/shard_map/ppermute | solution.py:505
  107.3 1.9 %collective-permute-done.34.refs_3_ = bf16[128,256]{1,0:T(8,128)(2,1)S(1)} collective-permute-done((bf16[128,256]{1,0:T(8,128)(2,1)}, bf16[128,256]{1,0:T(8,128)(2,1)S(1)}, u32[]{:S(2)}, u32[]{:S(2)}) %collective-permute-start.34) | collective-permute-done | bytes 65568 | tf_op jit(solution)/shard_map/ppermute | solution.py:505
  109.9 1.7 %join.1 = bf16[128,1024]{1,0:T(8,128)(2,1)} custom-call(s32[2]{0:T(128)} %pad_add_fusion.place_ref.device_ref, bf16[128,256]{1,0:T(8,128)(2,1)} %get-tuple-element.53.refs_0_, bf16[128,256]{1,0:T(8,128)(2,1)} %copy-done.13, bf16[128,256]{1,0:T(8,128)(2,1)} %copy-done.14, bf16[128,256]{1,0:T(8,128)(2,1)} %copy-done.15), custom_call_target="tpu_custom_call" | custom-call | tf_op jit(solution)/shard_map/join/pallas_call | solution.py:493
  (97 shorter events, 29.2 us)
Async XLA Ops:
  2.6 8.6 %collective-permute-start.10 = (bf16[2,128,128]{2,1,0:T(8,128)(2,1)}, bf16[2,128,128]{2,1,0:T(8,128)(2,1)S(1)}, u32[]{:S(2)}, u32[]{:S(2)}) collective-permute-start(bf16[2,128,128]{2,1,0:T(8,128)(2,1)} %get-tuple-element.34), channel_id=1, source_target_pairs={{0,12},{4,8},{8,4},{12,0},{16,28},{20,24},{24,20},{28,16},{1,13},{... | collective-permute-start | bytes 196616 | tf_op jit(solution)/shard_map/ppermute | solution.py:505
  3.6 8.7 %collective-permute-start.11 = (bf16[2,128,128]{2,1,0:T(8,128)(2,1)}, bf16[2,128,128]{2,1,0:T(8,128)(2,1)S(1)}, u32[]{:S(2)}, u32[]{:S(2)}) collective-permute-start(bf16[2,128,128]{2,1,0:T(8,128)(2,1)} %get-tuple-element.35), channel_id=1, source_target_pairs={{0,16},{4,20},{8,24},{12,28},{16,0},{20,4},{24,8},{28,12},{1,17},{... | collective-permute-start | bytes 196616 | tf_op jit(solution)/shard_map/ppermute | solution.py:505
  5.1 7.5 %collective-permute-start.12 = (bf16[2,128,128]{2,1,0:T(8,128)(2,1)}, bf16[2,128,128]{2,1,0:T(8,128)(2,1)S(1)}, u32[]{:S(2)}, u32[]{:S(2)}) collective-permute-start(bf16[2,128,128]{2,1,0:T(8,128)(2,1)} %get-tuple-element.36), channel_id=1, source_target_pairs={{0,20},{4,16},{8,28},{12,24},{16,4},{20,0},{24,12},{28,8},{1,21},{... | collective-permute-start | bytes 196616 | tf_op jit(solution)/shard_map/ppermute | solution.py:505
  9.4 9.6 %collective-permute-start.15 = (bf16[4,128,128]{2,1,0:T(8,128)(2,1)}, bf16[4,128,128]{2,1,0:T(8,128)(2,1)S(1)}, u32[]{:S(2)}, u32[]{:S(2)}) collective-permute-start(bf16[4,128,128]{2,1,0:T(8,128)(2,1)} %get-tuple-element.40), channel_id=1, source_target_pairs={{0,4},{4,0},{8,12},{12,8},{16,20},{20,16},{24,28},{28,24},{1,5},{5... | collective-permute-start | bytes 393224 | tf_op jit(solution)/shard_map/ppermute | solution.py:505
  14.9 6.6 %collective-permute-start.16 = (bf16[4,128,128]{2,1,0:T(8,128)(2,1)}, bf16[4,128,128]{2,1,0:T(8,128)(2,1)S(1)}, u32[]{:S(2)}, u32[]{:S(2)}) collective-permute-start(bf16[4,128,128]{2,1,0:T(8,128)(2,1)} %get-tuple-element.41), channel_id=1, source_target_pairs={{0,8},{4,12},{8,0},{12,4},{16,24},{20,28},{24,16},{28,20},{1,9},{5... | collective-permute-start | bytes 393224 | tf_op jit(solution)/shard_map/ppermute | solution.py:505
  16.3 6.9 %collective-permute-start.17 = (bf16[4,128,128]{2,1,0:T(8,128)(2,1)}, bf16[4,128,128]{2,1,0:T(8,128)(2,1)S(1)}, u32[]{:S(2)}, u32[]{:S(2)}) collective-permute-start(bf16[4,128,128]{2,1,0:T(8,128)(2,1)} %get-tuple-element.42), channel_id=1, source_target_pairs={{0,12},{4,8},{8,4},{12,0},{16,28},{20,24},{24,20},{28,16},{1,13},{... | collective-permute-start | bytes 393224 | tf_op jit(solution)/shard_map/ppermute | solution.py:505
  17.6 7.8 %collective-permute-start.18 = (bf16[4,128,128]{2,1,0:T(8,128)(2,1)}, bf16[4,128,128]{2,1,0:T(8,128)(2,1)S(1)}, u32[]{:S(2)}, u32[]{:S(2)}) collective-permute-start(bf16[4,128,128]{2,1,0:T(8,128)(2,1)} %get-tuple-element.43), channel_id=1, source_target_pairs={{0,16},{4,20},{8,24},{12,28},{16,0},{20,4},{24,8},{28,12},{1,17},{... | collective-permute-start | bytes 393224 | tf_op jit(solution)/shard_map/ppermute | solution.py:505
  18.1 12.3 %collective-permute-start.19 = (bf16[4,128,128]{2,1,0:T(8,128)(2,1)}, bf16[4,128,128]{2,1,0:T(8,128)(2,1)S(1)}, u32[]{:S(2)}, u32[]{:S(2)}) collective-permute-start(bf16[4,128,128]{2,1,0:T(8,128)(2,1)} %get-tuple-element.44), channel_id=1, source_target_pairs={{0,20},{4,16},{8,28},{12,24},{16,4},{20,0},{24,12},{28,8},{1,21},{... | collective-permute-start | bytes 393224 | tf_op jit(solution)/shard_map/ppermute | solution.py:505
  19.0 13.3 %collective-permute-start.20 = (bf16[4,128,128]{2,1,0:T(8,128)(2,1)}, bf16[4,128,128]{2,1,0:T(8,128)(2,1)S(1)}, u32[]{:S(2)}, u32[]{:S(2)}) collective-permute-start(bf16[4,128,128]{2,1,0:T(8,128)(2,1)} %get-tuple-element.45), channel_id=1, source_target_pairs={{0,24},{4,28},{8,16},{12,20},{16,8},{20,12},{24,0},{28,4},{1,25},{... | collective-permute-start | bytes 393224 | tf_op jit(solution)/shard_map/ppermute | solution.py:505
  21.5 26.7 %collective-permute-start = (bf16[1024,128]{1,0:T(8,128)(2,1)}, bf16[1024,128]{1,0:T(8,128)(2,1)S(1)}, u32[]{:S(2)}, u32[]{:S(2)}) collective-permute-start(bf16[1024,128]{1,0:T(8,128)(2,1)} %get-tuple-element.59), channel_id=1, source_target_pairs={{0,0},{4,16},{8,4},{12,20},{16,8},{20,24},{24,12},{28,28},{1,1},{5... | collective-permute-start | bytes 786440 | tf_op jit(solution)/shard_map/ppermute | solution.py:528
  23.1 25.2 %collective-permute-start.1 = (bf16[1024,128]{1,0:T(8,128)(2,1)}, bf16[1024,128]{1,0:T(8,128)(2,1)S(1)}, u32[]{:S(2)}, u32[]{:S(2)}) collective-permute-start(bf16[1024,128]{1,0:T(8,128)(2,1)} %get-tuple-element.58), channel_id=1, source_target_pairs={{0,4},{4,20},{8,0},{12,16},{16,12},{20,28},{24,8},{28,24},{1,5},{5... | collective-permute-start | bytes 786440 | tf_op jit(solution)/shard_map/ppermute | solution.py:528
  25.5 23.3 %collective-permute-start.2 = (bf16[1024,128]{1,0:T(8,128)(2,1)S(1)}, bf16[1024,128]{1,0:T(8,128)(2,1)S(1)}, u32[]{:S(2)}, u32[]{:S(2)}) collective-permute-start(bf16[1024,128]{1,0:T(8,128)(2,1)S(1)} %get-tuple-element.60), channel_id=1, source_target_pairs={{0,8},{4,24},{8,12},{12,28},{16,0},{20,16},{24,4},{28,20},{1,9},{5... | collective-permute-start | bytes 786440 | tf_op jit(solution)/shard_map/ppermute | solution.py:528
  30.4 18.5 %collective-permute-start.3 = (bf16[1024,128]{1,0:T(8,128)(2,1)S(1)}, bf16[1024,128]{1,0:T(8,128)(2,1)S(1)}, u32[]{:S(2)}, u32[]{:S(2)}) collective-permute-start(bf16[1024,128]{1,0:T(8,128)(2,1)S(1)} %get-tuple-element.57), channel_id=1, source_target_pairs={{0,12},{4,28},{8,8},{12,24},{16,4},{20,20},{24,0},{28,16},{1,13},{... | collective-permute-start | bytes 786440 | tf_op jit(solution)/shard_map/ppermute | solution.py:528
  32.3 12.8 %collective-permute-start.21 = (bf16[4,128,128]{2,1,0:T(8,128)(2,1)}, bf16[4,128,128]{2,1,0:T(8,128)(2,1)S(1)}, u32[]{:S(2)}, u32[]{:S(2)}) collective-permute-start(bf16[4,128,128]{2,1,0:T(8,128)(2,1)} %get-tuple-element.46), channel_id=1, source_target_pairs={{0,28},{4,24},{8,20},{12,16},{16,12},{20,8},{24,4},{28,0},{1,29},{... | collective-permute-start | bytes 393224 | tf_op jit(solution)/shard_map/ppermute | solution.py:505
  48.2 11.1 %collective-permute-start.4 = (bf16[1024,128]{1,0:T(8,128)(2,1)S(1)}, bf16[1024,128]{1,0:T(8,128)(2,1)S(1)}, u32[]{:S(2)}, u32[]{:S(2)}) collective-permute-start(bf16[1024,128]{1,0:T(8,128)(2,1)S(1)} %collective-permute-done.refs_0_), channel_id=1, source_target_pairs={{0,4},{4,0},{8,12},{12,8},{16,20},{20,16},{24,28},{28,24},{1,5},{5... | collective-permute-start | bytes 786440 | tf_op jit(solution)/shard_map/ppermute | solution.py:505
  48.3 11.1 %collective-permute-start.5 = (bf16[1024,128]{1,0:T(8,128)(2,1)S(1)}, bf16[1024,128]{1,0:T(8,128)(2,1)S(1)}, u32[]{:S(2)}, u32[]{:S(2)}) collective-permute-start(bf16[1024,128]{1,0:T(8,128)(2,1)S(1)} %collective-permute-done.1.refs_1_), channel_id=1, source_target_pairs={{0,4},{4,0},{8,12},{12,8},{16,20},{20,16},{24,28},{28,24},{1,5},{5... | collective-permute-start | bytes 786440 | tf_op jit(solution)/shard_map/ppermute | solution.py:505
  48.8 12.4 %collective-permute-start.6 = (bf16[1024,128]{1,0:T(8,128)(2,1)S(1)}, bf16[1024,128]{1,0:T(8,128)(2,1)S(1)}, u32[]{:S(2)}, u32[]{:S(2)}) collective-permute-start(bf16[1024,128]{1,0:T(8,128)(2,1)S(1)} %collective-permute-done.2.refs_2_), channel_id=1, source_target_pairs={{0,4},{4,0},{8,12},{12,8},{16,20},{20,16},{24,28},{28,24},{1,5},{5... | collective-permute-start | bytes 786440 | tf_op jit(solution)/shard_map/ppermute | solution.py:505
  48.9 13.1 %collective-permute-start.7 = (bf16[1024,128]{1,0:T(8,128)(2,1)S(1)}, bf16[1024,128]{1,0:T(8,128)(2,1)S(1)}, u32[]{:S(2)}, u32[]{:S(2)}) collective-permute-start(bf16[1024,128]{1,0:T(8,128)(2,1)S(1)} %collective-permute-done.3.refs_3_), channel_id=1, source_target_pairs={{0,4},{4,0},{8,12},{12,8},{16,20},{20,16},{24,28},{28,24},{1,5},{5... | collective-permute-start | bytes 786440 | tf_op jit(solution)/shard_map/ppermute | solution.py:505
  59.4 8.3 %collective-permute-start.24 = (bf16[4,128,128]{2,1,0:T(8,128)(2,1)S(1)}, bf16[4,128,128]{2,1,0:T(8,128)(2,1)S(1)}, u32[]{:S(2)}, u32[]{:S(2)}) collective-permute-start(bf16[4,128,128]{2,1,0:T(8,128)(2,1)S(1)} %get-tuple-element.48), channel_id=1, source_target_pairs={{0,12},{4,8},{8,4},{12,0},{16,28},{20,24},{24,20},{28,16},{1,13},{... | collective-permute-start | bytes 393224 | tf_op jit(solution)/shard_map/ppermute | solution.py:505
  61.2 6.5 %collective-permute-start.25 = (bf16[4,128,128]{2,1,0:T(8,128)(2,1)S(1)}, bf16[4,128,128]{2,1,0:T(8,128)(2,1)S(1)}, u32[]{:S(2)}, u32[]{:S(2)}) collective-permute-start(bf16[4,128,128]{2,1,0:T(8,128)(2,1)S(1)} %get-tuple-element.47), channel_id=1, source_target_pairs={{0,16},{4,20},{8,24},{12,28},{16,0},{20,4},{24,8},{28,12},{1,17},{... | collective-permute-start | bytes 393224 | tf_op jit(solution)/shard_map/ppermute | solution.py:505
  62.0 7.1 %collective-permute-start.26 = (bf16[4,128,128]{2,1,0:T(8,128)(2,1)S(1)}, bf16[4,128,128]{2,1,0:T(8,128)(2,1)S(1)}, u32[]{:S(2)}, u32[]{:S(2)}) collective-permute-start(bf16[4,128,128]{2,1,0:T(8,128)(2,1)S(1)} %get-tuple-element.48), channel_id=1, source_target_pairs={{0,20},{4,16},{8,28},{12,24},{16,4},{20,0},{24,12},{28,8},{1,21},{... | collective-permute-start | bytes 393224 | tf_op jit(solution)/shard_map/ppermute | solution.py:505
  71.9 11.8 %collective-permute-start.29 = (bf16[512,256]{1,0:T(8,128)(2,1)S(1)}, bf16[512,256]{1,0:T(8,128)(2,1)S(1)}, u32[]{:S(2)}, u32[]{:S(2)}) collective-permute-start(bf16[512,256]{1,0:T(8,128)(2,1)S(1)} %get-tuple-element.50), channel_id=1, source_target_pairs={{0,1},{1,0},{2,3},{3,2},{4,5},{5,4},{6,7},{7,6},{8,9},{9,8},{10,11... | collective-permute-start | bytes 786440 | tf_op jit(solution)/shard_map/ppermute | solution.py:505
  72.3 20.5 %collective-permute-start.30 = (bf16[512,256]{1,0:T(8,128)(2,1)S(1)}, bf16[512,256]{1,0:T(8,128)(2,1)S(1)}, u32[]{:S(2)}, u32[]{:S(2)}) collective-permute-start(bf16[512,256]{1,0:T(8,128)(2,1)S(1)} %get-tuple-element.51), channel_id=1, source_target_pairs={{0,2},{1,3},{2,0},{3,1},{4,6},{5,7},{6,4},{7,5},{8,10},{9,11},{10,... | collective-permute-start | bytes 786440 | tf_op jit(solution)/shard_map/ppermute | solution.py:505
  74.9 23.7 %collective-permute-start.31 = (bf16[512,256]{1,0:T(8,128)(2,1)S(1)}, bf16[512,256]{1,0:T(8,128)(2,1)S(1)}, u32[]{:S(2)}, u32[]{:S(2)}) collective-permute-start(bf16[512,256]{1,0:T(8,128)(2,1)S(1)} %get-tuple-element.52), channel_id=1, source_target_pairs={{0,3},{1,2},{2,1},{3,0},{4,7},{5,6},{6,5},{7,4},{8,11},{9,10},{10,... | collective-permute-start | bytes 786440 | tf_op jit(solution)/shard_map/ppermute | solution.py:505
  (31 other events, 383.9 us)

commit v3 on v1

--- a/solution.py
+++ b/solution.py
@@ -125,7 +125,7 @@
     )(moved, skip[None, :], forward, inverse)
 
 
-def shards(values_in, gate_values, filter_spectrum, skip_gain, out_weight):
+def shards_general(values_in, gate_values, filter_spectrum, skip_gain, out_weight):
     parts = lax.axis_size("seq")
     layers = lax.axis_size("chan")
     rows, width = values_in.shape
@@ -163,6 +163,424 @@
     return lax.all_to_all(mixed, "seq", 0, 1, tiled=True)
 
 
+WHOLE = pl.BlockSpec(memory_space=pltpu.VMEM)
+
+
+def small_tables(parts, rows):
+    total = 2 * parts * rows
+    index = np.arange(rows)
+    phase = 2.0 * np.pi * (index[:, None] * index[None, :] % rows) / rows
+    cos, sin = np.cos(phase), np.sin(phase)
+    forward = np.block([[cos, sin], [-sin, cos]])
+    residue = np.arange(2 * parts).reshape(2, 1, parts)
+    turn = 2.0 * np.pi * index[None, :, None] * residue / total
+    return forward.astype(BF16), forward.T.astype(BF16), np.cos(turn).astype(F32), np.sin(turn).astype(F32)
+
+
+def cosine(parts, residue, block):
+    return float(np.cos(np.pi * residue * block / parts))
+
+
+def sine(parts, residue, block):
+    return float(np.sin(np.pi * residue * block / parts))
+
+
+def weighted(terms):
+    total = None
+    for factor, term in terms:
+        if abs(factor) < 1e-12:
+            continue
+        part = term if factor == 1.0 else factor * term
+        total = part if total is None else total + part
+    return total
+
+
+def plus(left, right):
+    return left if right is None else right if left is None else left + right
+
+
+def minus(left, right):
+    return left if right is None else -right if left is None else left - right
+
+
+def own_place():
+    device = lax.axis_index("seq")
+    return device // 2, device % 2
+
+
+def block_at(index, size):
+    return pl.ds(pl.multiple_of(index * size, size), size)
+
+
+def pack_signals_kernel(chips, values_ref, gate_ref, *out_refs):
+    chip, _ = own_place()
+    lanes = out_refs[0].shape[2]
+    for offset in range(chips):
+        out_refs[offset][0] = values_ref[:, block_at(chip ^ offset, lanes)]
+        out_refs[offset][1] = gate_ref[:, block_at(chip ^ offset, lanes)]
+
+
+def pack_signals(values_in, gate_values, chips):
+    rows, width = values_in.shape
+    return pl.pallas_call(
+        functools.partial(pack_signals_kernel, chips),
+        in_specs=[WHOLE] * 2,
+        out_specs=[WHOLE] * chips,
+        out_shape=[jax.ShapeDtypeStruct((2, rows, width // chips), BF16)] * chips,
+        name="pack_signals",
+    )(values_in, gate_values)
+
+
+def pack_filter_kernel(offset, filter_ref, out_ref, plane_ref, arrived):
+    chip, _ = own_place()
+    planes, _, lanes = out_ref.shape
+    copies = [
+        pltpu.make_async_copy(
+            filter_ref.at[plane, :, block_at(chip ^ offset, lanes)], plane_ref.at[plane], arrived.at[plane]
+        )
+        for plane in range(planes)
+    ]
+    for copy in copies:
+        copy.start()
+    for plane, copy in enumerate(copies):
+        copy.wait()
+        out_ref[plane] = plane_ref[plane].astype(BF16)
+
+
+def pack_filter(filters, chips, offset):
+    planes, rows, width = filters.shape
+    shape = (planes, rows, width // chips)
+    return pl.pallas_call(
+        functools.partial(pack_filter_kernel, offset),
+        in_specs=[pl.BlockSpec(memory_space=pl.ANY)],
+        out_specs=WHOLE,
+        out_shape=jax.ShapeDtypeStruct(shape, BF16),
+        scratch_shapes=[pltpu.VMEM(shape, F32), pltpu.SemaphoreType.DMA((planes,))],
+        name="pack_filter",
+    )(filters)
+
+
+def forward_kernel(chips, cos_ref, sin_ref, table_ref, own_ref, other_ref, out_ref, signal_ref, waves_ref):
+    chip, core = own_place()
+    parts = 2 * chips
+    rows, lanes = own_ref.shape[1:]
+    chunk, width = 16, 128
+    for offset in range(chips):
+        signal_ref[2 * (chip ^ offset) + core] = own_ref[offset]
+        signal_ref[2 * (chip ^ offset) + 1 - core] = other_ref[offset]
+    sign = (1 - 2 * core).astype(F32)
+
+    def spread(index, carry):
+        here = block_at(index, chunk)
+        there = pl.ds(pl.multiple_of(rows + index * chunk, chunk), chunk)
+        cos_all, sin_all = cos_ref[core, here, :], sin_ref[core, here, :]
+        for start in range(0, lanes, width):
+            blocks = [signal_ref[block, here, pl.ds(start, width)].astype(F32) for block in range(parts)]
+            blocks = [block * sign if place % 2 else block for place, block in enumerate(blocks)]
+
+            def store(residue, real, imag):
+                cos, sin = cos_all[:, residue : residue + 1], sin_all[:, residue : residue + 1]
+                if imag is None:
+                    real, imag = real * cos, -(real * sin)
+                else:
+                    real, imag = real * cos + imag * sin, imag * cos - real * sin
+                columns = pl.ds(residue * lanes + start, width)
+                waves_ref[here, columns] = real.astype(BF16)
+                waves_ref[there, columns] = imag.astype(BF16)
+
+            for residue in range(parts // 2 + 1):
+                even, odd = range(0, parts, 2), range(1, parts, 2)
+                cos_even = weighted([(cosine(parts, residue, block), blocks[block]) for block in even])
+                cos_odd = weighted([(cosine(parts, residue, block), blocks[block]) for block in odd])
+                sin_even = weighted([(sine(parts, residue, block), blocks[block]) for block in even])
+                sin_odd = weighted([(sine(parts, residue, block), blocks[block]) for block in odd])
+                sin_sum = plus(sin_even, sin_odd)
+                store(residue, plus(cos_even, cos_odd), None if sin_sum is None else -sin_sum)
+                if 0 < residue and 2 * residue != parts:
+                    store(parts - residue, minus(cos_even, cos_odd), minus(sin_even, sin_odd))
+        return carry
+
+    lax.fori_loop(0, rows // chunk, spread, 0)
+    for residue in range(parts):
+        columns = pl.ds(residue * lanes, lanes)
+        out_ref[:, columns] = jnp.dot(table_ref[...], waves_ref[:, columns], preferred_element_type=F32)
+
+
+def forward(own, other, tables):
+    chips, rows, lanes = own.shape
+    table, _, cos, sin = tables
+    spectrum = (2 * rows, 2 * chips * lanes)
+    return pl.pallas_call(
+        functools.partial(forward_kernel, chips),
+        in_specs=[WHOLE] * 5,
+        out_specs=WHOLE,
+        out_shape=jax.ShapeDtypeStruct(spectrum, F32),
+        scratch_shapes=[pltpu.VMEM((2 * chips, rows, lanes), BF16), pltpu.VMEM(spectrum, BF16)],
+        compiler_params=pltpu.CompilerParams(vmem_limit_bytes=32 * 2**20),
+        name="forward",
+    )(cos, sin, table, own, other)
+
+
+def backward_kernel(chips, cos_ref, sin_ref, table_ref, spectrum_ref, *refs):
+    filter_refs, (keep_ref, send_ref, filter_ref, product_ref, back_ref) = refs[:chips], refs[chips:]
+    chip, core = own_place()
+    parts = 2 * chips
+    rows, lanes = keep_ref.shape[1:]
+    chip_bits = chips.bit_length() - 1
+    chunk, width = 16, 128
+    for offset in range(chips):
+        filter_ref[chip ^ offset] = filter_refs[offset][...]
+
+    for residue in range(parts):
+        source, odd = bit_reversed(residue // 2, chip_bits), residue % 2
+        columns = pl.ds(residue * lanes, lanes)
+        filter_real = filter_ref[source, odd].astype(F32)
+        filter_imag = filter_ref[source, 2 + odd].astype(F32)
+        real = spectrum_ref[pl.ds(0, rows), columns]
+        imag = spectrum_ref[pl.ds(rows, rows), columns]
+        product_ref[pl.ds(0, rows), columns] = (real * filter_real - imag * filter_imag).astype(BF16)
+        product_ref[pl.ds(rows, rows), columns] = (real * filter_imag + imag * filter_real).astype(BF16)
+        back_ref[:, columns] = jnp.dot(table_ref[...], product_ref[:, columns], preferred_element_type=F32)
+
+    scale = 1.0 / (2 * parts * rows)
+    sign = (1 - 2 * core).astype(F32)
+    upper = core == 1
+
+    def gather(index, carry):
+        here = block_at(index, chunk)
+        there = pl.ds(pl.multiple_of(rows + index * chunk, chunk), chunk)
+        cos_all, sin_all = cos_ref[core, here, :] * scale, sin_ref[core, here, :] * scale
+        for start in range(0, lanes, width):
+            reals, imags = [], []
+            for residue in range(parts):
+                columns = pl.ds(residue * lanes + start, width)
+                real, imag = back_ref[here, columns], back_ref[there, columns]
+                cos, sin = cos_all[:, residue : residue + 1], sin_all[:, residue : residue + 1]
+                reals.append(real * cos - imag * sin)
+                imags.append(real * sin + imag * cos)
+            totals = [None] * parts
+            for block in range(parts // 2 + 1):
+                even, odd = range(0, parts, 2), range(1, parts, 2)
+                cos_even = weighted([(cosine(parts, residue, block), reals[residue]) for residue in even])
+                cos_odd = weighted([(cosine(parts, residue, block), reals[residue]) for residue in odd])
+                sin_even = weighted([(sine(parts, residue, block), imags[residue]) for residue in even])
+                sin_odd = weighted([(sine(parts, residue, block), imags[residue]) for residue in odd])
+                totals[block] = minus(plus(cos_even, cos_odd), plus(sin_even, sin_odd))
+                if 0 < block and 2 * block != parts:
+                    totals[parts - block] = plus(minus(cos_even, cos_odd), minus(sin_even, sin_odd))
+            lane = pl.ds(start, width)
+            for pair in range(chips):
+                low, high = totals[2 * pair], totals[2 * pair + 1] * sign
+                keep_ref[pair, here, lane] = jnp.where(upper, high, low)
+                send_ref[pair, here, lane] = jnp.where(upper, low, high).astype(BF16)
+        return carry
+
+    lax.fori_loop(0, rows // chunk, gather, 0)
+
+
+def backward(spectrum, filters, tables):
+    chips = len(filters)
+    planes, rows, lanes = filters[0].shape
+    _, table, cos, sin = tables
+    kept = (chips, rows, lanes)
+    return pl.pallas_call(
+        functools.partial(backward_kernel, chips),
+        in_specs=[WHOLE] * (4 + chips),
+        out_specs=[WHOLE] * 2,
+        out_shape=[jax.ShapeDtypeStruct(kept, F32), jax.ShapeDtypeStruct(kept, BF16)],
+        scratch_shapes=[
+            pltpu.VMEM((chips, planes, rows, lanes), BF16),
+            pltpu.VMEM(spectrum.shape, BF16),
+            pltpu.VMEM(spectrum.shape, F32),
+        ],
+        compiler_params=pltpu.CompilerParams(vmem_limit_bytes=40 * 2**20),
+        name="backward",
+    )(cos, sin, table, spectrum, *filters)
+
+
+def gate_kernel(chips, skip_ref, keep_ref, arrived_ref, *refs):
+    signal_refs, out_refs = refs[:chips], refs[chips:]
+    chip, _ = own_place()
+    rows, lanes = keep_ref.shape[1:]
+    step = rows // len(out_refs)
+    skip = skip_ref[:, block_at(chip, lanes)]
+    for offset in range(chips):
+        block = chip ^ offset
+        for part, out_ref in enumerate(out_refs):
+            here = pl.ds(part * step, step)
+            convolved = keep_ref[block, here, :] + arrived_ref[block, here, :].astype(F32)
+            signal = signal_refs[offset][0, here, :].astype(F32)
+            gate = signal_refs[offset][1, here, :].astype(F32)
+            out_ref[block_at(block, step), :] = (gate * (convolved + skip * signal)).astype(BF16)
+
+
+def gate(skip, keep, arrived, signals, pieces):
+    chips, rows, lanes = keep.shape
+    return pl.pallas_call(
+        functools.partial(gate_kernel, chips),
+        in_specs=[WHOLE] * (3 + chips),
+        out_specs=[WHOLE] * pieces,
+        out_shape=[jax.ShapeDtypeStruct((chips * rows // pieces, lanes), BF16)] * pieces,
+        name="gate",
+    )(skip, keep, arrived, *signals)
+
+
+def arrange_kernel(layers, *refs):
+    own_refs, other_refs, out_ref = refs[:layers], refs[layers : 2 * layers], refs[2 * layers]
+    device, layer = lax.axis_index("seq"), lax.axis_index("chan")
+    share = own_refs[0].shape[1]
+    for step in range(layers):
+        target = device % layers ^ layer ^ step
+        out_ref[target, :, block_at(device % 2, share)] = own_refs[step][...]
+        out_ref[target, :, block_at(1 - device % 2, share)] = other_refs[step ^ 1][...]
+
+
+def arrange(own, other):
+    layers = len(own)
+    rows, share = own[0].shape
+    return pl.pallas_call(
+        functools.partial(arrange_kernel, layers),
+        in_specs=[WHOLE] * (2 * layers),
+        out_specs=WHOLE,
+        out_shape=jax.ShapeDtypeStruct((layers, rows, 2 * share), BF16),
+        compiler_params=pltpu.CompilerParams(vmem_limit_bytes=32 * 2**20),
+        name="arrange_weights",
+    )(*own, *other)
+
+
+def project_kernel(chips, weight_ref, *refs):
+    gated_refs, (keep_ref, pass_ref, send_ref, joined_ref) = refs[:chips], refs[chips:]
+    chip, _ = own_place()
+    lanes = gated_refs[0].shape[1]
+    for offset in range(chips):
+        joined_ref[:, block_at(chip ^ offset, lanes)] = gated_refs[offset][...]
+
+    def partial_of(target):
+        return jnp.dot(joined_ref[...], weight_ref[target], preferred_element_type=F32).astype(BF16)
+
+    send_ref[0] = partial_of(1)
+    send_ref[1] = partial_of(3)
+    pass_ref[...] = partial_of(2)
+    keep_ref[...] = partial_of(0)
+
+
+def project(weight, gated):
+    chips = len(gated)
+    _, depth, columns = weight.shape
+    rows = gated[0].shape[0]
+    block = jax.ShapeDtypeStruct((rows, columns), BF16)
+    return pl.pallas_call(
+        functools.partial(project_kernel, chips),
+        in_specs=[WHOLE] * (1 + chips),
+        out_specs=[WHOLE] * 3,
+        out_shape=[block, block, jax.ShapeDtypeStruct((2, rows, columns), BF16)],
+        scratch_shapes=[pltpu.VMEM((rows, depth), BF16)],
+        compiler_params=pltpu.CompilerParams(vmem_limit_bytes=32 * 2**20),
+        name="project",
+    )(weight, *gated)
+
+
+def finish_kernel(chips, pieces, *refs):
+    keep_refs, first_refs, second_refs = refs[:pieces], refs[pieces : 2 * pieces], refs[2 * pieces : 3 * pieces]
+    out_refs = refs[3 * pieces :]
+    chip, _ = own_place()
+    step = keep_refs[0].shape[0] // chips
+    for offset in range(chips):
+        here = block_at(chip ^ offset, step)
+        for part in range(pieces):
+            total = keep_refs[part][here, :].astype(F32) + first_refs[part][0, here, :].astype(F32)
+            total = total + second_refs[part][here, :].astype(F32)
+            out_refs[offset][pl.ds(part * step, step), :] = total.astype(BF16)
+
+
+def finish(keep, first, second, chips):
+    pieces = len(keep)
+    rows, columns = keep[0].shape
+    return pl.pallas_call(
+        functools.partial(finish_kernel, chips, pieces),
+        in_specs=[WHOLE] * (3 * pieces),
+        out_specs=[WHOLE] * chips,
+        out_shape=[jax.ShapeDtypeStruct((rows * pieces // chips, columns), BF16)] * chips,
+        name="finish",
+    )(*keep, *first, *second)
+
+
+def join_kernel(chips, *refs):
+    in_refs, out_ref = refs[:chips], refs[chips]
+    chip, _ = own_place()
+    columns = in_refs[0].shape[1]
+    for offset in range(chips):
+        out_ref[:, block_at(chip ^ offset, columns)] = in_refs[offset][...]
+
+
+def join(blocks):
+    chips = len(blocks)
+    rows, columns = blocks[0].shape
+    return pl.pallas_call(
+        functools.partial(join_kernel, chips),
+        in_specs=[WHOLE] * chips,
+        out_specs=WHOLE,
+        out_shape=jax.ShapeDtypeStruct((rows, chips * columns), BF16),
+        name="join",
+    )(*blocks)
+
+
+def swapped(value, axis, offset):
+    if not offset:
+        return value
+    return lax.ppermute(value, axis, [(source, source ^ offset) for source in range(lax.axis_size(axis))])
+
+
+def to_chips(blocks):
+    return [swapped(block, "seq", 2 * offset) for offset, block in enumerate(blocks)]
+
+
+def shards_direct(values_in, gate_values, filter_spectrum, skip_gain, out_weight):
+    parts = lax.axis_size("seq")
+    layers = lax.axis_size("chan")
+    chips = parts // 2
+    pieces = 2
+    rows, width = values_in.shape
+    device = lax.axis_index("seq")
+    tables = small_tables(parts, rows)
+
+    signals = to_chips(pack_signals(values_in, gate_values, chips))
+    flat_filters = filter_spectrum.reshape(4, rows, width)
+    filters = to_chips([pack_filter(flat_filters, chips, offset) for offset in range(chips)])
+
+    share = out_weight.shape[1] // layers
+    own_weight = []
+    for step in range(layers):
+        sent = lax.dynamic_slice_in_dim(out_weight, (device // 2 ^ step) * share, share, 1)
+        pairs = [(source, source % 2 * layers + (source // 2 ^ step)) for source in range(parts)]
+        own_weight.append(lax.ppermute(sent, "seq", pairs))
+    weight = arrange(own_weight, [swapped(block, "seq", 1) for block in own_weight])
+
+    own = jnp.stack([block[0] for block in signals])
+    spectrum = forward(own, swapped(own, "seq", 1), tables)
+    keep, send = backward(spectrum, filters, tables)
+    gated = gate(skip_gain[None, :], keep, swapped(send, "seq", 1), signals, pieces)
+
+    kept, firsts, seconds = [], [], []
+    for piece in gated:
+        keep, passed, send = project(weight, to_chips([piece] * chips))
+        first = swapped(send, "chan", 1)
+        passed = (passed.astype(F32) + first[1].astype(F32)).astype(BF16)
+        kept.append(keep)
+        firsts.append(first)
+        seconds.append(swapped(passed, "chan", 2))
+    return join(to_chips(finish(kept, firsts, seconds, chips)))
+
+
+def shards(values_in, gate_values, filter_spectrum, skip_gain, out_weight):
+    parts, layers = lax.axis_size("seq"), lax.axis_size("chan")
+    rows, width = values_in.shape
+    share = out_weight.shape[1] // layers
+    aligned = width // parts % 128 == 0 and share % 128 == 0 and rows % 32 == 0
+    run = shards_direct if aligned and layers == 4 and parts == 8 else shards_general
+    return run(values_in, gate_values, filter_spectrum, skip_gain, out_weight)
+
+
 def solution(mesh):
     in_specs = (
         P("seq", "chan"),

time: 126 us -> 95.6 us (0.76)
  waiting for transfers between devices: 68.9 us -> 35 us
  starting transfers between devices: 14.5 us -> 34.8 us
  Pallas kernels: 3.29 us -> 20.5 us
  between operations: 13.8 us -> 0.42 us
  blocking collectives: 10.4 us -> 0 us
  local copies, waits for them, and re-layouts: 8.6 us -> 4.5 us
  other arithmetic: 3.04 us -> 0.1 us
  matrix products: 2.86 us -> 0 us
    unnamed x3 -> x0, waiting for transfers between devices: 27.3 us -> none
    ppermute x4 -> x29, starting transfers between devices: 9.21 us -> 34.8 us  [the longest x25 28.2 us: swapped(): lax.ppermute(value, axis, [(source, source ^ offset) for source in range(...]
    ppermute x4 -> x29, waiting for transfers between devices: 9.7 us -> 35 us  [the longest x25 34.8 us: swapped(): lax.ppermute(value, axis, [(source, source ^ offset) for source in range(...]
    all_to_all x1 -> x0, waiting for transfers between devices: 20.9 us -> none  [shards(): moved = lax.all_to_all(packed, 'seq', 0, 0)]
    pallas_call x1 -> x13, Pallas kernels: 3.29 us -> 20.5 us  [the longest x4 7.41 us: pack_filter(): pl.pallas_call(functools.partial(pack_filter_kernel, offset), in_specs=[p...]
    all_gather x1 -> x0, waiting for transfers between devices: 11 us -> none  [shards(): lax.all_gather(gated.reshape(parts * rows, lanes), 'seq', axis=1, tiled=T...]
    all_to_all x1 -> x0, blocking collectives: 10.4 us -> none  [shards(): return lax.all_to_all(mixed, 'seq', 0, 1, tiled=True)]
    all_to_all x1 -> x0, starting transfers between devices: 5.17 us -> none  [shards(): moved = lax.all_to_all(packed, 'seq', 0, 0)]
  transfers between devices with their start and end apart: 7 -> 29, of which waited for: 6 -> 12; matrix products, arithmetic and copies ran while one was open for 0% -> 1% of each run, Pallas kernels for 0% -> 15%
where the time goes in v3:
time: 95.6 us; the launch traced here: 95.2 us
  waiting for transfers between devices  35 us (37%)
  starting transfers between devices  34.8 us (36%)
  Pallas kernels  20.5 us (21%)
  local copies, waits for them, and re-layouts  4.5 us (5%)
    ppermute x25, waiting for transfers between devices, swapped(): lax.ppermute(value, axis, [(source, source ^ offset) for source in range(...  34.8 us
    ppermute x25, starting transfers between devices, swapped(): lax.ppermute(value, axis, [(source, source ^ offset) for source in range(...  28.2 us
    pallas_call x4, Pallas kernels, pack_filter(): pl.pallas_call(functools.partial(pack_filter_kernel, offset), in_specs=[p...  7.41 us
    ppermute x4, starting transfers between devices, shards_direct(): own_weight.append(lax.ppermute(sent, 'seq', pairs))  6.57 us
    unnamed x46, local copies, waits for them, and re-layouts  3.47 us
    pallas_call x1, Pallas kernels, gate(): pl.pallas_call(functools.partial(gate_kernel, chips), in_specs=[WHOLE] *...  2.14 us
    pallas_call x1, Pallas kernels, backward(): pl.pallas_call(functools.partial(backward_kernel, chips), in_specs=[WHOLE...  2.02 us
    pallas_call x1, Pallas kernels, finish(): pl.pallas_call(functools.partial(finish_kernel, chips, pieces), in_specs=...  1.96 us
  transfers between devices with their start and end apart: 29, of which 12 were waited for; matrix products, arithmetic and copies ran while one was open for 1% of the time, Pallas kernels for 15%

profile of v3, /device:TPU:0, one launch (start us, length us, event | category | flops | bytes accessed | tf_op | source)
XLA Modules:
  0.0 95.2 jit_solution(7994406720598485417)
XLA Ops:
  0.0 1.9 %pack_signals.1 = (bf16[2,128,256]{2,1,0:T(8,128)(2,1)}, bf16[2,128,256]{2,1,0:T(8,128)(2,1)}, bf16[2,128,256]{2,1,0:T(8,128)(2,1)}, bf16[2,128,256]{2,1,0:T(8,128)(2,1)}) custom-call(bf16[128,1024]{1,0:T(8,128)(2,1)} %values_ref.1, bf16[128,1024]{1,0:T(8,128)(2,1)} %gate_ref.1), custom_call_target="tpu_custom_call" | custom-call | tf_op jit(solution)/shard_map/pack_signals/pallas_call | solution.py:225
  1.9 2.9 %collective-permute-start.8 = (bf16[2,128,256]{2,1,0:T(8,128)(2,1)}, bf16[2,128,256]{2,1,0:T(8,128)(2,1)S(1)}, u32[]{:S(2)}, u32[]{:S(2)}) collective-permute-start(bf16[2,128,256]{2,1,0:T(8,128)(2,1)} %get-tuple-element.24), channel_id=1, source_target_pairs={{0,8},{4,12},{8,0},{12,4},{16,24},{20,28},{24,16},{28,20},{1,9},{5... | collective-permute-start | bytes 393224 | tf_op jit(solution)/shard_map/ppermute | solution.py:531
  6.3 1.8 %pack_filter.5 = bf16[4,128,256]{2,1,0:T(8,128)(2,1)} custom-call(f32[4,128,1024]{2,1,0:T(8,128)} %bitcast.12), custom_call_target="tpu_custom_call" | custom-call | tf_op jit(solution)/shard_map/pack_filter/pallas_call | solution.py:253
  8.2 2.0 %collective-permute-start.12 = (bf16[4,128,256]{2,1,0:T(8,128)(2,1)}, bf16[4,128,256]{2,1,0:T(8,128)(2,1)S(1)}, u32[]{:S(2)}, u32[]{:S(2)}) collective-permute-start(bf16[4,128,256]{2,1,0:T(8,128)(2,1)} %pack_filter.5), channel_id=1, source_target_pairs={{0,8},{4,12},{8,0},{12,4},{16,24},{20,28},{24,16},{28,20},{1,9},{5... | collective-permute-start | bytes 786440 | tf_op jit(solution)/shard_map/ppermute | solution.py:531
  10.2 1.8 %pack_filter.6 = bf16[4,128,256]{2,1,0:T(8,128)(2,1)} custom-call(f32[4,128,1024]{2,1,0:T(8,128)} %bitcast.13), custom_call_target="tpu_custom_call" | custom-call | tf_op jit(solution)/shard_map/pack_filter/pallas_call | solution.py:253
  13.7 1.8 %pack_filter.7 = bf16[4,128,256]{2,1,0:T(8,128)(2,1)} custom-call(f32[4,128,1024]{2,1,0:T(8,128)} %bitcast.14), custom_call_target="tpu_custom_call" | custom-call | tf_op jit(solution)/shard_map/pack_filter/pallas_call | solution.py:253
  17.0 3.8 %collective-permute-start.3 = (bf16[1024,128]{1,0:T(8,128)(2,1)}, bf16[1024,128]{1,0:T(8,128)(2,1)S(1)}, u32[]{:S(2)}, u32[]{:S(2)}) collective-permute-start(bf16[1024,128]{1,0:T(8,128)(2,1)} %get-tuple-element.41), channel_id=1, source_target_pairs={{0,12},{4,28},{8,8},{12,24},{16,4},{20,20},{24,0},{28,16},{1,13},{... | collective-permute-start | bytes 786440 | tf_op jit(solution)/shard_map/ppermute | solution.py:556
  22.0 6.3 %collective-permute-done.13.refs_2_ = bf16[4,128,256]{2,1,0:T(8,128)(2,1)S(1)} collective-permute-done((bf16[4,128,256]{2,1,0:T(8,128)(2,1)}, bf16[4,128,256]{2,1,0:T(8,128)(2,1)S(1)}, u32[]{:S(2)}, u32[]{:S(2)}) %collective-permute-start.13) | collective-permute-done | bytes 262176 | tf_op jit(solution)/shard_map/ppermute | solution.py:531
  28.3 1.6 %collective-permute-start = (bf16[1024,128]{1,0:T(8,128)(2,1)}, bf16[1024,128]{1,0:T(8,128)(2,1)S(1)}, u32[]{:S(2)}, u32[]{:S(2)}) collective-permute-start(bf16[1024,128]{1,0:T(8,128)(2,1)} %get-tuple-element.43), channel_id=1, source_target_pairs={{0,0},{4,16},{8,4},{12,20},{16,8},{20,24},{24,12},{28,28},{1,1},{5... | collective-permute-start | bytes 786440 | tf_op jit(solution)/shard_map/ppermute | solution.py:556
  29.9 1.9 %pack_filter.4.refs_0_ = bf16[4,128,256]{2,1,0:T(8,128)(2,1)} custom-call(f32[4,128,1024]{2,1,0:T(8,128)} %bitcast.15), custom_call_target="tpu_custom_call" | custom-call | tf_op jit(solution)/shard_map/pack_filter/pallas_call | solution.py:253
  33.4 2.0 %backward.1 = (f32[4,128,256]{2,1,0:T(8,128)S(1)}, bf16[4,128,256]{2,1,0:T(8,128)(2,1)S(1)}) custom-call(f32[2,128,8]{2,1,0:T(8,128)S(1)} %copy-done.2, f32[2,128,8]{2,1,0:T(8,128)S(1)} %copy-done.1, bf16[256,256]{1,0:T(8,128)(2,1)S(1)} %copy-done.4, f32[256,2048]{1,0:T(8,128)S(1)} %forward.1.spectrum_ref, bf16[4,128,256]{2,1,0:T(8,128)(2,1)S(1)} %copy-done, ...), custom_call_target="tpu_custom_call" | custom-call | tf_op jit(solution)/shard_map/backward/pallas_call | solution.py:386
  36.2 3.3 %collective-permute-start.15 = (bf16[4,128,256]{2,1,0:T(8,128)(2,1)S(1)}, bf16[4,128,256]{2,1,0:T(8,128)(2,1)S(1)}, u32[]{:S(2)}, u32[]{:S(2)}) collective-permute-start(bf16[4,128,256]{2,1,0:T(8,128)(2,1)S(1)} %get-tuple-element.28), channel_id=1, source_target_pairs={{0,4},{4,0},{8,12},{12,8},{16,20},{20,16},{24,28},{28,24},{1,5},{5... | collective-permute-start | bytes 786440 | tf_op jit(solution)/shard_map/ppermute | solution.py:531
  41.4 2.1 %gate.1 = (bf16[256,256]{1,0:T(8,128)(2,1)}, bf16[256,256]{1,0:T(8,128)(2,1)}) custom-call(f32[1,1024]{1,0:T(1,128)} %bitcast.16, f32[4,128,256]{2,1,0:T(8,128)} %copy-done.3, bf16[4,128,256]{2,1,0:T(8,128)(2,1)} %copy-done.17, bf16[2,128,256]{2,1,0:T(8,128)(2,1)} %get-tuple-element.23.refs_0_, bf16[2,128,256]{2,1,0:T(8,128)(2,1)} %copy-done.14, ...), custom_call_target="tpu_custom_call" | custom-call | tf_op jit(solution)/shard_map/gate/pallas_call | solution.py:419
  43.6 2.9 %collective-permute-start.21 = (bf16[256,256]{1,0:T(8,128)(2,1)}, bf16[256,256]{1,0:T(8,128)(2,1)S(1)}, u32[]{:S(2)}, u32[]{:S(2)}) collective-permute-start(bf16[256,256]{1,0:T(8,128)(2,1)} %get-tuple-element.31.refs_0_), channel_id=1, source_target_pairs={{0,24},{4,28},{8,16},{12,20},{16,8},{20,12},{24,0},{28,4},{1,25},{... | collective-permute-start | bytes 393224 | tf_op jit(solution)/shard_map/ppermute | solution.py:531
  47.5 3.2 %collective-permute-done.21.refs_3_ = bf16[256,256]{1,0:T(8,128)(2,1)S(1)} collective-permute-done((bf16[256,256]{1,0:T(8,128)(2,1)}, bf16[256,256]{1,0:T(8,128)(2,1)S(1)}, u32[]{:S(2)}, u32[]{:S(2)}) %collective-permute-start.21) | collective-permute-done | bytes 131104 | tf_op jit(solution)/shard_map/ppermute | solution.py:531
  50.7 2.6 %collective-permute-done.20.refs_2_ = bf16[256,256]{1,0:T(8,128)(2,1)S(1)} collective-permute-done((bf16[256,256]{1,0:T(8,128)(2,1)}, bf16[256,256]{1,0:T(8,128)(2,1)S(1)}, u32[]{:S(2)}, u32[]{:S(2)}) %collective-permute-start.20) | collective-permute-done | bytes 131104 | tf_op jit(solution)/shard_map/ppermute | solution.py:531
  55.6 1.7 %collective-permute-start.18 = (bf16[256,256]{1,0:T(8,128)(2,1)S(1)}, bf16[256,256]{1,0:T(8,128)(2,1)S(1)}, u32[]{:S(2)}, u32[]{:S(2)}) collective-permute-start(bf16[256,256]{1,0:T(8,128)(2,1)S(1)} %copy-done.6), channel_id=1, source_target_pairs={{0,24},{4,28},{8,16},{12,20},{16,8},{20,12},{24,0},{28,4},{1,25},{... | collective-permute-start | bytes 393224 | tf_op jit(solution)/shard_map/ppermute | solution.py:531
  59.1 3.8 %collective-permute-done.18.refs_3_ = bf16[256,256]{1,0:T(8,128)(2,1)S(1)} collective-permute-done((bf16[256,256]{1,0:T(8,128)(2,1)S(1)}, bf16[256,256]{1,0:T(8,128)(2,1)S(1)}, u32[]{:S(2)}, u32[]{:S(2)}) %collective-permute-start.18) | collective-permute-done | bytes 131104 | tf_op jit(solution)/shard_map/ppermute | solution.py:531
  66.4 1.9 %collective-permute-start.25 = (bf16[256,256]{1,0:T(8,128)(2,1)S(1)}, bf16[256,256]{1,0:T(8,128)(2,1)S(1)}, u32[]{:S(2)}, u32[]{:S(2)}) collective-permute-start(bf16[256,256]{1,0:T(8,128)(2,1)S(1)} %fusion), channel_id=1, source_target_pairs={{0,2},{1,3},{2,0},{3,1},{4,6},{5,7},{6,4},{7,5},{8,10},{9,11},{10,... | collective-permute-start | bytes 393224 | tf_op jit(solution)/shard_map/ppermute | solution.py:531
  68.3 7.5 %collective-permute-done.22.refs_2_ = bf16[2,256,256]{2,1,0:T(8,128)(2,1)S(1)} collective-permute-done((bf16[2,256,256]{2,1,0:T(8,128)(2,1)S(1)}, bf16[2,256,256]{2,1,0:T(8,128)(2,1)S(1)}, u32[]{:S(2)}, u32[]{:S(2)}) %collective-permute-start.22) | collective-permute-done | bytes 262176 | tf_op jit(solution)/shard_map/ppermute | solution.py:531
  77.1 6.5 %collective-permute-done.24.refs_4_ = bf16[256,256]{1,0:T(8,128)(2,1)S(1)} collective-permute-done((bf16[256,256]{1,0:T(8,128)(2,1)S(1)}, bf16[256,256]{1,0:T(8,128)(2,1)S(1)}, u32[]{:S(2)}, u32[]{:S(2)}) %collective-permute-start.24) | collective-permute-done | bytes 131104 | tf_op jit(solution)/shard_map/ppermute | solution.py:531
  84.3 2.0 %finish.1 = (bf16[128,256]{1,0:T(8,128)(2,1)}, bf16[128,256]{1,0:T(8,128)(2,1)}, bf16[128,256]{1,0:T(8,128)(2,1)}, bf16[128,256]{1,0:T(8,128)(2,1)}) custom-call(bf16[256,256]{1,0:T(8,128)(2,1)} %copy-done.9, bf16[256,256]{1,0:T(8,128)(2,1)} %copy-done.8, bf16[2,256,256]{2,1,0:T(8,128)(2,1)} %copy-done.12, bf16[2,256,256]{2,1,0:T(8,128)(2,1)} %copy-done.11, ...), custom_call_target="tpu_custom_call" | custom-call | tf_op jit(solution)/shard_map/finish/pallas_call | solution.py:499
  87.5 2.2 %collective-permute-start.28 = (bf16[128,256]{1,0:T(8,128)(2,1)}, bf16[128,256]{1,0:T(8,128)(2,1)S(1)}, u32[]{:S(2)}, u32[]{:S(2)}) collective-permute-start(bf16[128,256]{1,0:T(8,128)(2,1)} %get-tuple-element.40), channel_id=1, source_target_pairs={{0,24},{4,28},{8,16},{12,20},{16,8},{20,12},{24,0},{28,4},{1,25},{... | collective-permute-start | bytes 196616 | tf_op jit(solution)/shard_map/ppermute | solution.py:531
  93.5 1.7 %join.1 = bf16[128,1024]{1,0:T(8,128)(2,1)} custom-call(bf16[128,256]{1,0:T(8,128)(2,1)} %get-tuple-element.37.refs_0_, bf16[128,256]{1,0:T(8,128)(2,1)} %copy-done.20, bf16[128,256]{1,0:T(8,128)(2,1)} %copy-done.21, bf16[128,256]{1,0:T(8,128)(2,1)} %copy-done.22), custom_call_target="tpu_custom_call" | custom-call | tf_op jit(solution)/shard_map/join/pallas_call | solution.py:519
  (101 shorter events, 25.2 us)
Async XLA Ops:
  1.9 13.7 %collective-permute-start.8 = (bf16[2,128,256]{2,1,0:T(8,128)(2,1)}, bf16[2,128,256]{2,1,0:T(8,128)(2,1)S(1)}, u32[]{:S(2)}, u32[]{:S(2)}) collective-permute-start(bf16[2,128,256]{2,1,0:T(8,128)(2,1)} %get-tuple-element.24), channel_id=1, source_target_pairs={{0,8},{4,12},{8,0},{12,4},{16,24},{20,28},{24,16},{28,20},{1,9},{5... | collective-permute-start | bytes 393224 | tf_op jit(solution)/shard_map/ppermute | solution.py:531
  4.8 11.0 %collective-permute-start.9 = (bf16[2,128,256]{2,1,0:T(8,128)(2,1)}, bf16[2,128,256]{2,1,0:T(8,128)(2,1)S(1)}, u32[]{:S(2)}, u32[]{:S(2)}) collective-permute-start(bf16[2,128,256]{2,1,0:T(8,128)(2,1)} %get-tuple-element.25), channel_id=1, source_target_pairs={{0,16},{4,20},{8,24},{12,28},{16,0},{20,4},{24,8},{28,12},{1,17},{... | collective-permute-start | bytes 393224 | tf_op jit(solution)/shard_map/ppermute | solution.py:531
  6.3 9.5 %collective-permute-start.10 = (bf16[2,128,256]{2,1,0:T(8,128)(2,1)}, bf16[2,128,256]{2,1,0:T(8,128)(2,1)S(1)}, u32[]{:S(2)}, u32[]{:S(2)}) collective-permute-start(bf16[2,128,256]{2,1,0:T(8,128)(2,1)} %get-tuple-element.26), channel_id=1, source_target_pairs={{0,24},{4,28},{8,16},{12,20},{16,8},{20,12},{24,0},{28,4},{1,25},{... | collective-permute-start | bytes 393224 | tf_op jit(solution)/shard_map/ppermute | solution.py:531
  8.2 12.7 %collective-permute-start.12 = (bf16[4,128,256]{2,1,0:T(8,128)(2,1)}, bf16[4,128,256]{2,1,0:T(8,128)(2,1)S(1)}, u32[]{:S(2)}, u32[]{:S(2)}) collective-permute-start(bf16[4,128,256]{2,1,0:T(8,128)(2,1)} %pack_filter.5), channel_id=1, source_target_pairs={{0,8},{4,12},{8,0},{12,4},{16,24},{20,28},{24,16},{28,20},{1,9},{5... | collective-permute-start | bytes 786440 | tf_op jit(solution)/shard_map/ppermute | solution.py:531
  12.1 16.2 %collective-permute-start.13 = (bf16[4,128,256]{2,1,0:T(8,128)(2,1)}, bf16[4,128,256]{2,1,0:T(8,128)(2,1)S(1)}, u32[]{:S(2)}, u32[]{:S(2)}) collective-permute-start(bf16[4,128,256]{2,1,0:T(8,128)(2,1)} %pack_filter.6), channel_id=1, source_target_pairs={{0,16},{4,20},{8,24},{12,28},{16,0},{20,4},{24,8},{28,12},{1,17},{... | collective-permute-start | bytes 786440 | tf_op jit(solution)/shard_map/ppermute | solution.py:531
  15.6 17.8 %collective-permute-start.14 = (bf16[4,128,256]{2,1,0:T(8,128)(2,1)}, bf16[4,128,256]{2,1,0:T(8,128)(2,1)S(1)}, u32[]{:S(2)}, u32[]{:S(2)}) collective-permute-start(bf16[4,128,256]{2,1,0:T(8,128)(2,1)} %pack_filter.7), channel_id=1, source_target_pairs={{0,24},{4,28},{8,16},{12,20},{16,8},{20,12},{24,0},{28,4},{1,25},{... | collective-permute-start | bytes 786440 | tf_op jit(solution)/shard_map/ppermute | solution.py:531
  15.9 14.0 %collective-permute-start.11 = (bf16[4,128,256]{2,1,0:T(8,128)(2,1)S(1)}, bf16[4,128,256]{2,1,0:T(8,128)(2,1)S(1)}, u32[]{:S(2)}, u32[]{:S(2)}) collective-permute-start(bf16[4,128,256]{2,1,0:T(8,128)(2,1)S(1)} %pad_maximum_fusion.own_ref), channel_id=1, source_target_pairs={{0,4},{4,0},{8,12},{12,8},{16,20},{20,16},{24,28},{28,24},{1,5},{5... | collective-permute-start | bytes 786440 | tf_op jit(solution)/shard_map/ppermute | solution.py:531
  17.0 22.6 %collective-permute-start.3 = (bf16[1024,128]{1,0:T(8,128)(2,1)}, bf16[1024,128]{1,0:T(8,128)(2,1)S(1)}, u32[]{:S(2)}, u32[]{:S(2)}) collective-permute-start(bf16[1024,128]{1,0:T(8,128)(2,1)} %get-tuple-element.41), channel_id=1, source_target_pairs={{0,12},{4,28},{8,8},{12,24},{16,4},{20,20},{24,0},{28,16},{1,13},{... | collective-permute-start | bytes 786440 | tf_op jit(solution)/shard_map/ppermute | solution.py:556
  20.9 18.7 %collective-permute-start.1 = (bf16[1024,128]{1,0:T(8,128)(2,1)}, bf16[1024,128]{1,0:T(8,128)(2,1)S(1)}, u32[]{:S(2)}, u32[]{:S(2)}) collective-permute-start(bf16[1024,128]{1,0:T(8,128)(2,1)} %get-tuple-element.42), channel_id=1, source_target_pairs={{0,4},{4,20},{8,0},{12,16},{16,12},{20,28},{24,8},{28,24},{1,5},{5... | collective-permute-start | bytes 786440 | tf_op jit(solution)/shard_map/ppermute | solution.py:556
  28.3 11.8 %collective-permute-start = (bf16[1024,128]{1,0:T(8,128)(2,1)}, bf16[1024,128]{1,0:T(8,128)(2,1)S(1)}, u32[]{:S(2)}, u32[]{:S(2)}) collective-permute-start(bf16[1024,128]{1,0:T(8,128)(2,1)} %get-tuple-element.43), channel_id=1, source_target_pairs={{0,0},{4,16},{8,4},{12,20},{16,8},{20,24},{24,12},{28,28},{1,1},{5... | collective-permute-start | bytes 786440 | tf_op jit(solution)/shard_map/ppermute | solution.py:556
  29.9 10.4 %collective-permute-start.2 = (bf16[1024,128]{1,0:T(8,128)(2,1)S(1)}, bf16[1024,128]{1,0:T(8,128)(2,1)S(1)}, u32[]{:S(2)}, u32[]{:S(2)}) collective-permute-start(bf16[1024,128]{1,0:T(8,128)(2,1)S(1)} %get-tuple-element.44), channel_id=1, source_target_pairs={{0,8},{4,24},{8,12},{12,28},{16,0},{20,16},{24,4},{28,20},{1,9},{5... | collective-permute-start | bytes 786440 | tf_op jit(solution)/shard_map/ppermute | solution.py:556
  39.6 6.9 %collective-permute-start.7 = (bf16[1024,128]{1,0:T(8,128)(2,1)S(1)}, bf16[1024,128]{1,0:T(8,128)(2,1)S(1)}, u32[]{:S(2)}, u32[]{:S(2)}) collective-permute-start(bf16[1024,128]{1,0:T(8,128)(2,1)S(1)} %collective-permute-done.3.refs_3_), channel_id=1, source_target_pairs={{0,4},{4,0},{8,12},{12,8},{16,20},{20,16},{24,28},{28,24},{1,5},{5... | collective-permute-start | bytes 786440 | tf_op jit(solution)/shard_map/ppermute | solution.py:531
  39.6 6.9 %collective-permute-start.5 = (bf16[1024,128]{1,0:T(8,128)(2,1)S(1)}, bf16[1024,128]{1,0:T(8,128)(2,1)S(1)}, u32[]{:S(2)}, u32[]{:S(2)}) collective-permute-start(bf16[1024,128]{1,0:T(8,128)(2,1)S(1)} %collective-permute-done.1.refs_1_), channel_id=1, source_target_pairs={{0,4},{4,0},{8,12},{12,8},{16,20},{20,16},{24,28},{28,24},{1,5},{5... | collective-permute-start | bytes 786440 | tf_op jit(solution)/shard_map/ppermute | solution.py:531
  40.1 7.0 %collective-permute-start.4 = (bf16[1024,128]{1,0:T(8,128)(2,1)S(1)}, bf16[1024,128]{1,0:T(8,128)(2,1)S(1)}, u32[]{:S(2)}, u32[]{:S(2)}) collective-permute-start(bf16[1024,128]{1,0:T(8,128)(2,1)S(1)} %collective-permute-done.refs_0_), channel_id=1, source_target_pairs={{0,4},{4,0},{8,12},{12,8},{16,20},{20,16},{24,28},{28,24},{1,5},{5... | collective-permute-start | bytes 786440 | tf_op jit(solution)/shard_map/ppermute | solution.py:531
  40.3 6.8 %collective-permute-start.6 = (bf16[1024,128]{1,0:T(8,128)(2,1)S(1)}, bf16[1024,128]{1,0:T(8,128)(2,1)S(1)}, u32[]{:S(2)}, u32[]{:S(2)}) collective-permute-start(bf16[1024,128]{1,0:T(8,128)(2,1)S(1)} %collective-permute-done.2.refs_2_), channel_id=1, source_target_pairs={{0,4},{4,0},{8,12},{12,8},{16,20},{20,16},{24,28},{28,24},{1,5},{5... | collective-permute-start | bytes 786440 | tf_op jit(solution)/shard_map/ppermute | solution.py:531
  43.6 7.1 %collective-permute-start.21 = (bf16[256,256]{1,0:T(8,128)(2,1)}, bf16[256,256]{1,0:T(8,128)(2,1)S(1)}, u32[]{:S(2)}, u32[]{:S(2)}) collective-permute-start(bf16[256,256]{1,0:T(8,128)(2,1)} %get-tuple-element.31.refs_0_), channel_id=1, source_target_pairs={{0,24},{4,28},{8,16},{12,20},{16,8},{20,12},{24,0},{28,4},{1,25},{... | collective-permute-start | bytes 393224 | tf_op jit(solution)/shard_map/ppermute | solution.py:531
  46.5 6.9 %collective-permute-start.20 = (bf16[256,256]{1,0:T(8,128)(2,1)}, bf16[256,256]{1,0:T(8,128)(2,1)S(1)}, u32[]{:S(2)}, u32[]{:S(2)}) collective-permute-start(bf16[256,256]{1,0:T(8,128)(2,1)} %get-tuple-element.31.refs_0_), channel_id=1, source_target_pairs={{0,16},{4,20},{8,24},{12,28},{16,0},{20,4},{24,8},{28,12},{1,17},{... | collective-permute-start | bytes 393224 | tf_op jit(solution)/shard_map/ppermute | solution.py:531
  46.5 6.9 %collective-permute-start.19 = (bf16[256,256]{1,0:T(8,128)(2,1)}, bf16[256,256]{1,0:T(8,128)(2,1)S(1)}, u32[]{:S(2)}, u32[]{:S(2)}) collective-permute-start(bf16[256,256]{1,0:T(8,128)(2,1)} %get-tuple-element.31.refs_0_), channel_id=1, source_target_pairs={{0,8},{4,12},{8,0},{12,4},{16,24},{20,28},{24,16},{28,20},{1,9},{5... | collective-permute-start | bytes 393224 | tf_op jit(solution)/shard_map/ppermute | solution.py:531
  54.8 11.6 %collective-permute-start.23 = (bf16[2,256,256]{2,1,0:T(8,128)(2,1)S(1)}, bf16[2,256,256]{2,1,0:T(8,128)(2,1)S(1)}, u32[]{:S(2)}, u32[]{:S(2)}) collective-permute-start(bf16[2,256,256]{2,1,0:T(8,128)(2,1)S(1)} %get-tuple-element.34), channel_id=1, source_target_pairs={{0,1},{1,0},{2,3},{3,2},{4,5},{5,4},{6,7},{7,6},{8,9},{9,8},{10,11... | collective-permute-start | bytes 786440 | tf_op jit(solution)/shard_map/ppermute | solution.py:531
  55.6 7.3 %collective-permute-start.18 = (bf16[256,256]{1,0:T(8,128)(2,1)S(1)}, bf16[256,256]{1,0:T(8,128)(2,1)S(1)}, u32[]{:S(2)}, u32[]{:S(2)}) collective-permute-start(bf16[256,256]{1,0:T(8,128)(2,1)S(1)} %copy-done.6), channel_id=1, source_target_pairs={{0,24},{4,28},{8,16},{12,20},{16,8},{20,12},{24,0},{28,4},{1,25},{... | collective-permute-start | bytes 393224 | tf_op jit(solution)/shard_map/ppermute | solution.py:531
  57.3 7.0 %collective-permute-start.17 = (bf16[256,256]{1,0:T(8,128)(2,1)S(1)}, bf16[256,256]{1,0:T(8,128)(2,1)S(1)}, u32[]{:S(2)}, u32[]{:S(2)}) collective-permute-start(bf16[256,256]{1,0:T(8,128)(2,1)S(1)} %copy-done.6), channel_id=1, source_target_pairs={{0,16},{4,20},{8,24},{12,28},{16,0},{20,4},{24,8},{28,12},{1,17},{... | collective-permute-start | bytes 393224 | tf_op jit(solution)/shard_map/ppermute | solution.py:531
  65.1 10.7 %collective-permute-start.22 = (bf16[2,256,256]{2,1,0:T(8,128)(2,1)S(1)}, bf16[2,256,256]{2,1,0:T(8,128)(2,1)S(1)}, u32[]{:S(2)}, u32[]{:S(2)}) collective-permute-start(bf16[2,256,256]{2,1,0:T(8,128)(2,1)S(1)} %get-tuple-element.33), channel_id=1, source_target_pairs={{0,1},{1,0},{2,3},{3,2},{4,5},{5,4},{6,7},{7,6},{8,9},{9,8},{10,11... | collective-permute-start | bytes 786440 | tf_op jit(solution)/shard_map/ppermute | solution.py:531
  66.4 10.7 %collective-permute-start.25 = (bf16[256,256]{1,0:T(8,128)(2,1)S(1)}, bf16[256,256]{1,0:T(8,128)(2,1)S(1)}, u32[]{:S(2)}, u32[]{:S(2)}) collective-permute-start(bf16[256,256]{1,0:T(8,128)(2,1)S(1)} %fusion), channel_id=1, source_target_pairs={{0,2},{1,3},{2,0},{3,1},{4,6},{5,7},{6,4},{7,5},{8,10},{9,11},{10,... | collective-permute-start | bytes 393224 | tf_op jit(solution)/shard_map/ppermute | solution.py:531
  75.9 7.8 %collective-permute-start.24 = (bf16[256,256]{1,0:T(8,128)(2,1)S(1)}, bf16[256,256]{1,0:T(8,128)(2,1)S(1)}, u32[]{:S(2)}, u32[]{:S(2)}) collective-permute-start(bf16[256,256]{1,0:T(8,128)(2,1)S(1)} %fusion.1), channel_id=1, source_target_pairs={{0,2},{1,3},{2,0},{3,1},{4,6},{5,7},{6,4},{7,5},{8,10},{9,11},{10,... | collective-permute-start | bytes 393224 | tf_op jit(solution)/shard_map/ppermute | solution.py:531
  (28 other events, 204.5 us)

commit v4 on v3

--- a/solution.py
+++ b/solution.py
@@ -227,6 +227,7 @@
         in_specs=[WHOLE] * 2,
         out_specs=[WHOLE] * chips,
         out_shape=[jax.ShapeDtypeStruct((2, rows, width // chips), BF16)] * chips,
+        compiler_params=pltpu.CompilerParams(vmem_limit_bytes=4 * 2**20),
         name="pack_signals",
     )(values_in, gate_values)
 
@@ -256,6 +257,7 @@
         out_specs=WHOLE,
         out_shape=jax.ShapeDtypeStruct(shape, BF16),
         scratch_shapes=[pltpu.VMEM(shape, F32), pltpu.SemaphoreType.DMA((planes,))],
+        compiler_params=pltpu.CompilerParams(vmem_limit_bytes=4 * 2**20),
         name="pack_filter",
     )(filters)
 
@@ -316,7 +318,7 @@
         out_specs=WHOLE,
         out_shape=jax.ShapeDtypeStruct(spectrum, F32),
         scratch_shapes=[pltpu.VMEM((2 * chips, rows, lanes), BF16), pltpu.VMEM(spectrum, BF16)],
-        compiler_params=pltpu.CompilerParams(vmem_limit_bytes=32 * 2**20),
+        compiler_params=pltpu.CompilerParams(vmem_limit_bytes=8 * 2**20),
         name="forward",
     )(cos, sin, table, own, other)
 
@@ -393,7 +395,7 @@
             pltpu.VMEM(spectrum.shape, BF16),
             pltpu.VMEM(spectrum.shape, F32),
         ],
-        compiler_params=pltpu.CompilerParams(vmem_limit_bytes=40 * 2**20),
+        compiler_params=pltpu.CompilerParams(vmem_limit_bytes=12 * 2**20),
         name="backward",
     )(cos, sin, table, spectrum, *filters)
 
@@ -421,6 +423,7 @@
         in_specs=[WHOLE] * (3 + chips),
         out_specs=[WHOLE] * pieces,
         out_shape=[jax.ShapeDtypeStruct((chips * rows // pieces, lanes), BF16)] * pieces,
+        compiler_params=pltpu.CompilerParams(vmem_limit_bytes=6 * 2**20),
         name="gate",
     )(skip, keep, arrived, *signals)
 
@@ -443,7 +446,7 @@
         in_specs=[WHOLE] * (2 * layers),
         out_specs=WHOLE,
         out_shape=jax.ShapeDtypeStruct((layers, rows, 2 * share), BF16),
-        compiler_params=pltpu.CompilerParams(vmem_limit_bytes=32 * 2**20),
+        compiler_params=pltpu.CompilerParams(vmem_limit_bytes=8 * 2**20),
         name="arrange_weights",
     )(*own, *other)
 
@@ -475,7 +478,7 @@
         out_specs=[WHOLE] * 3,
         out_shape=[block, block, jax.ShapeDtypeStruct((2, rows, columns), BF16)],
         scratch_shapes=[pltpu.VMEM((rows, depth), BF16)],
-        compiler_params=pltpu.CompilerParams(vmem_limit_bytes=32 * 2**20),
+        compiler_params=pltpu.CompilerParams(vmem_limit_bytes=8 * 2**20),
         name="project",
     )(weight, *gated)
 
@@ -501,6 +504,7 @@
         in_specs=[WHOLE] * (3 * pieces),
         out_specs=[WHOLE] * chips,
         out_shape=[jax.ShapeDtypeStruct((rows * pieces // chips, columns), BF16)] * chips,
+        compiler_params=pltpu.CompilerParams(vmem_limit_bytes=4 * 2**20),
         name="finish",
     )(*keep, *first, *second)
 
@@ -521,6 +525,7 @@
         in_specs=[WHOLE] * chips,
         out_specs=WHOLE,
         out_shape=jax.ShapeDtypeStruct((rows, chips * columns), BF16),
+        compiler_params=pltpu.CompilerParams(vmem_limit_bytes=2 * 2**20),
         name="join",
     )(*blocks)
 
@@ -540,6 +545,7 @@
     layers = lax.axis_size("chan")
     chips = parts // 2
     pieces = 2
+    early = layers // 2
     rows, width = values_in.shape
     device = lax.axis_index("seq")
     tables = small_tables(parts, rows)
@@ -549,16 +555,21 @@
     filters = to_chips([pack_filter(flat_filters, chips, offset) for offset in range(chips)])
 
     share = out_weight.shape[1] // layers
-    own_weight = []
-    for step in range(layers):
-        sent = lax.dynamic_slice_in_dim(out_weight, (device // 2 ^ step) * share, share, 1)
+    sent = [lax.dynamic_slice_in_dim(out_weight, (device // 2 ^ step) * share, share, 1) for step in range(layers)]
+
+    def weights_from(step, block):
         pairs = [(source, source % 2 * layers + (source // 2 ^ step)) for source in range(parts)]
-        own_weight.append(lax.ppermute(sent, "seq", pairs))
-    weight = arrange(own_weight, [swapped(block, "seq", 1) for block in own_weight])
+        return lax.ppermute(block, "seq", pairs)
+
+    own_weight = [weights_from(step, sent[step]) for step in range(early)]
 
     own = jnp.stack([block[0] for block in signals])
     spectrum = forward(own, swapped(own, "seq", 1), tables)
     keep, send = backward(spectrum, filters, tables)
+    late = lax.optimization_barrier((send, *sent[early:]))
+    send = late[0]
+    own_weight += [weights_from(early + step, block) for step, block in enumerate(late[1:])]
+    weight = arrange(own_weight, [swapped(block, "seq", 1) for block in own_weight])
     gated = gate(skip_gain[None, :], keep, swapped(send, "seq", 1), signals, pieces)
 
     kept, firsts, seconds = [], [], []

time: 95.6 us -> 94.9 us (level)
  Pallas kernels: 20.5 us -> 11.1 us
  waiting for transfers between devices: 35 us -> 42.8 us
    ppermute x4, waiting for transfers between devices: 0.18 us -> 10.1 us  [weights_from(): return lax.ppermute(block, 'seq', pairs)]
    pallas_call x4, Pallas kernels: 7.41 us -> 2.72 us  [pack_filter(): pl.pallas_call(functools.partial(pack_filter_kernel, offset), in_specs=[p...]
    ppermute x25, waiting for transfers between devices: 34.8 us -> 32.7 us  [swapped(): lax.ppermute(value, axis, [(source, source ^ offset) for source in range(...]
    pallas_call x1, Pallas kernels: 2.14 us -> 0.16 us  [gate(): pl.pallas_call(functools.partial(gate_kernel, chips), in_specs=[WHOLE] *...]
    pallas_call x1, Pallas kernels: 1.96 us -> 0.1 us  [finish(): pl.pallas_call(functools.partial(finish_kernel, chips, pieces), in_specs=...]
    pallas_call x1, Pallas kernels: 1.88 us -> 0.07 us  [pack_signals(): pl.pallas_call(functools.partial(pack_signals_kernel, chips), in_specs=[W...]
    ppermute x25, starting transfers between devices: 28.2 us -> 29.3 us  [swapped(): lax.ppermute(value, axis, [(source, source ^ offset) for source in range(...]
    pallas_call x1, Pallas kernels: 1.48 us -> 2.46 us  [forward(): pl.pallas_call(functools.partial(forward_kernel, chips), in_specs=[WHOLE]...]
  transfers between devices with their start and end apart: 29 -> 29, of which waited for: 12 -> 15; matrix products, arithmetic and copies ran while one was open for 1% -> 1% of each run, Pallas kernels for 15% -> 10%
where the time goes in v4:
time: 94.9 us; the launch traced here: 94.6 us
  waiting for transfers between devices  42.8 us (45%)
  starting transfers between devices  35.5 us (37%)
  Pallas kernels  11.1 us (12%)
  local copies, waits for them, and re-layouts  4.87 us (5%)
    ppermute x25, waiting for transfers between devices, swapped(): lax.ppermute(value, axis, [(source, source ^ offset) for source in range(...  32.7 us
    ppermute x25, starting transfers between devices, swapped(): lax.ppermute(value, axis, [(source, source ^ offset) for source in range(...  29.3 us
    ppermute x4, waiting for transfers between devices, weights_from(): return lax.ppermute(block, 'seq', pairs)  10.1 us
    ppermute x4, starting transfers between devices, weights_from(): return lax.ppermute(block, 'seq', pairs)  6.14 us
    unnamed x18, local copies, waits for them, and re-layouts  3.52 us
    pallas_call x1, Pallas kernels, backward(): pl.pallas_call(functools.partial(backward_kernel, chips), in_specs=[WHOLE...  2.96 us
    pallas_call x4, Pallas kernels, pack_filter(): pl.pallas_call(functools.partial(pack_filter_kernel, offset), in_specs=[p...  2.72 us
    pallas_call x1, Pallas kernels, forward(): pl.pallas_call(functools.partial(forward_kernel, chips), in_specs=[WHOLE]...  2.46 us
  transfers between devices with their start and end apart: 29, of which 15 were waited for; matrix products, arithmetic and copies ran while one was open for 1% of the time, Pallas kernels for 10%

profile of v4, /device:TPU:0, one launch (start us, length us, event | category | flops | bytes accessed | tf_op | source)
XLA Modules:
  0.0 94.6 jit_solution(9927396043925337345)
XLA Ops:
  2.0 3.0 %collective-permute-start.2 = (bf16[2,128,256]{2,1,0:T(8,128)(2,1)S(1)}, bf16[2,128,256]{2,1,0:T(8,128)(2,1)S(1)}, u32[]{:S(2)}, u32[]{:S(2)}) collective-permute-start(bf16[2,128,256]{2,1,0:T(8,128)(2,1)S(1)} %get-tuple-element.27), channel_id=1, source_target_pairs={{0,8},{4,12},{8,0},{12,4},{16,24},{20,28},{24,16},{28,20},{1,9},{5... | collective-permute-start | bytes 393224 | tf_op jit(solution)/shard_map/ppermute | solution.py:536
  6.5 2.4 %collective-permute-done.2.refs_1_ = bf16[2,128,256]{2,1,0:T(8,128)(2,1)S(1)} collective-permute-done((bf16[2,128,256]{2,1,0:T(8,128)(2,1)S(1)}, bf16[2,128,256]{2,1,0:T(8,128)(2,1)S(1)}, u32[]{:S(2)}, u32[]{:S(2)}) %collective-permute-start.2) | collective-permute-done | bytes 131104 | tf_op jit(solution)/shard_map/ppermute | solution.py:536
  8.9 3.9 %collective-permute-done.3.refs_2_ = bf16[2,128,256]{2,1,0:T(8,128)(2,1)S(1)} collective-permute-done((bf16[2,128,256]{2,1,0:T(8,128)(2,1)S(1)}, bf16[2,128,256]{2,1,0:T(8,128)(2,1)S(1)}, u32[]{:S(2)}, u32[]{:S(2)}) %collective-permute-start.3) | collective-permute-done | bytes 131104 | tf_op jit(solution)/shard_map/ppermute | solution.py:536
  22.8 2.9 %collective-permute-start.1 = (bf16[1024,128]{1,0:T(8,128)(2,1)S(1)}, bf16[1024,128]{1,0:T(8,128)(2,1)S(1)}, u32[]{:S(2)}, u32[]{:S(2)}) collective-permute-start(bf16[1024,128]{1,0:T(8,128)(2,1)S(1)} %get-tuple-element.48), channel_id=1, source_target_pairs={{0,4},{4,20},{8,0},{12,16},{16,12},{20,28},{24,8},{28,24},{1,5},{5... | collective-permute-start | bytes 786440 | tf_op jit(solution)/shard_map/ppermute | solution.py:562
  25.9 2.5 %forward.1.spectrum_ref = f32[256,2048]{1,0:T(8,128)S(1)} custom-call(f32[2,128,8]{2,1,0:T(8,128)S(1)} %copy-done.2, f32[2,128,8]{2,1,0:T(8,128)S(1)} %copy-done.3, bf16[256,256]{1,0:T(8,128)(2,1)S(1)} %copy-done.7, bf16[4,128,256]{2,1,0:T(8,128)(2,1)S(1)} %pad_maximum_fusion.own_ref, bf16[4,128,256]{2,1,0:T(8,128)(2,1)} %collective-permute-done.5.other_ref), custom_call_target="tpu_custom_call" | custom-call | tf_op jit(solution)/shard_map/forward/pallas_call | solution.py:315
  28.4 4.4 %collective-permute-done.7.refs_2_ = bf16[4,128,256]{2,1,0:T(8,128)(2,1)S(1)} collective-permute-done((bf16[4,128,256]{2,1,0:T(8,128)(2,1)}, bf16[4,128,256]{2,1,0:T(8,128)(2,1)S(1)}, u32[]{:S(2)}, u32[]{:S(2)}) %collective-permute-start.7) | collective-permute-done | bytes 262176 | tf_op jit(solution)/shard_map/ppermute | solution.py:536
  32.8 3.0 %backward.1 = (f32[4,128,256]{2,1,0:T(8,128)S(1)}, bf16[4,128,256]{2,1,0:T(8,128)(2,1)S(1)}) custom-call(f32[2,128,8]{2,1,0:T(8,128)S(1)} %copy-done.2, f32[2,128,8]{2,1,0:T(8,128)S(1)} %copy-done.3, bf16[256,256]{1,0:T(8,128)(2,1)S(1)} %copy-done.6, f32[256,2048]{1,0:T(8,128)S(1)} %forward.1.spectrum_ref, bf16[4,128,256]{2,1,0:T(8,128)(2,1)S(1)} %pack_filter.4.refs_0_, ...), custom_call_target="tpu_custom_call" | custom-call | tf_op jit(solution)/shard_map/backward/pallas_call | solution.py:388
  36.4 1.9 %collective-permute-start.10 = (bf16[1024,128]{1,0:T(8,128)(2,1)S(1)}, bf16[1024,128]{1,0:T(8,128)(2,1)S(1)}, u32[]{:S(2)}, u32[]{:S(2)}) collective-permute-start(bf16[1024,128]{1,0:T(8,128)(2,1)S(1)} %get-tuple-element.32), channel_id=1, source_target_pairs={{0,12},{4,28},{8,8},{12,24},{16,4},{20,20},{24,0},{28,16},{1,13},{... | collective-permute-start | bytes 786440 | tf_op jit(solution)/shard_map/ppermute | solution.py:562
  38.9 2.3 %collective-permute-done.1.refs_1_ = bf16[1024,128]{1,0:T(8,128)(2,1)S(1)} collective-permute-done((bf16[1024,128]{1,0:T(8,128)(2,1)S(1)}, bf16[1024,128]{1,0:T(8,128)(2,1)S(1)}, u32[]{:S(2)}, u32[]{:S(2)}) %collective-permute-start.1) | collective-permute-done | bytes 262176 | tf_op jit(solution)/shard_map/ppermute | solution.py:562
  41.5 4.4 %collective-permute-done.9.refs_2_ = bf16[1024,128]{1,0:T(8,128)(2,1)S(1)} collective-permute-done((bf16[1024,128]{1,0:T(8,128)(2,1)S(1)}, bf16[1024,128]{1,0:T(8,128)(2,1)S(1)}, u32[]{:S(2)}, u32[]{:S(2)}) %collective-permute-start.9) | collective-permute-done | bytes 262176 | tf_op jit(solution)/shard_map/ppermute | solution.py:562
  45.9 3.4 %collective-permute-done.10.refs_3_ = bf16[1024,128]{1,0:T(8,128)(2,1)S(1)} collective-permute-done((bf16[1024,128]{1,0:T(8,128)(2,1)S(1)}, bf16[1024,128]{1,0:T(8,128)(2,1)S(1)}, u32[]{:S(2)}, u32[]{:S(2)}) %collective-permute-start.10) | collective-permute-done | bytes 262176 | tf_op jit(solution)/shard_map/ppermute | solution.py:562
  52.1 2.0 %collective-permute-start.21 = (bf16[256,256]{1,0:T(8,128)(2,1)S(1)}, bf16[256,256]{1,0:T(8,128)(2,1)S(1)}, u32[]{:S(2)}, u32[]{:S(2)}) collective-permute-start(bf16[256,256]{1,0:T(8,128)(2,1)S(1)} %get-tuple-element.37.refs_0_), channel_id=1, source_target_pairs={{0,24},{4,28},{8,16},{12,20},{16,8},{20,12},{24,0},{28,4},{1,25},{... | collective-permute-start | bytes 393224 | tf_op jit(solution)/shard_map/ppermute | solution.py:536
  54.5 2.5 %collective-permute-done.19.refs_1_ = bf16[256,256]{1,0:T(8,128)(2,1)S(1)} collective-permute-done((bf16[256,256]{1,0:T(8,128)(2,1)S(1)}, bf16[256,256]{1,0:T(8,128)(2,1)S(1)}, u32[]{:S(2)}, u32[]{:S(2)}) %collective-permute-start.19) | collective-permute-done | bytes 131104 | tf_op jit(solution)/shard_map/ppermute | solution.py:536
  57.0 1.9 %collective-permute-done.20.refs_2_ = bf16[256,256]{1,0:T(8,128)(2,1)S(1)} collective-permute-done((bf16[256,256]{1,0:T(8,128)(2,1)S(1)}, bf16[256,256]{1,0:T(8,128)(2,1)S(1)}, u32[]{:S(2)}, u32[]{:S(2)}) %collective-permute-start.20) | collective-permute-done | bytes 131104 | tf_op jit(solution)/shard_map/ppermute | solution.py:536
  59.7 1.6 %collective-permute-start.23 = (bf16[2,256,256]{2,1,0:T(8,128)(2,1)S(1)}, bf16[2,256,256]{2,1,0:T(8,128)(2,1)S(1)}, u32[]{:S(2)}, u32[]{:S(2)}) collective-permute-start(bf16[2,256,256]{2,1,0:T(8,128)(2,1)S(1)} %get-tuple-element.40), channel_id=1, source_target_pairs={{0,1},{1,0},{2,3},{3,2},{4,5},{5,4},{6,7},{7,6},{8,9},{9,8},{10,11... | collective-permute-start | bytes 786440 | tf_op jit(solution)/shard_map/ppermute | solution.py:536
  61.3 1.7 %collective-permute-start.16 = (bf16[256,256]{1,0:T(8,128)(2,1)S(1)}, bf16[256,256]{1,0:T(8,128)(2,1)S(1)}, u32[]{:S(2)}, u32[]{:S(2)}) collective-permute-start(bf16[256,256]{1,0:T(8,128)(2,1)S(1)} %get-tuple-element.35.refs_0_), channel_id=1, source_target_pairs={{0,8},{4,12},{8,0},{12,4},{16,24},{20,28},{24,16},{28,20},{1,9},{5... | collective-permute-start | bytes 393224 | tf_op jit(solution)/shard_map/ppermute | solution.py:536
  64.8 2.5 %collective-permute-done.16.refs_1_ = bf16[256,256]{1,0:T(8,128)(2,1)S(1)} collective-permute-done((bf16[256,256]{1,0:T(8,128)(2,1)S(1)}, bf16[256,256]{1,0:T(8,128)(2,1)S(1)}, u32[]{:S(2)}, u32[]{:S(2)}) %collective-permute-start.16) | collective-permute-done | bytes 131104 | tf_op jit(solution)/shard_map/ppermute | solution.py:536
  67.3 2.3 %collective-permute-done.17.refs_2_ = bf16[256,256]{1,0:T(8,128)(2,1)S(1)} collective-permute-done((bf16[256,256]{1,0:T(8,128)(2,1)S(1)}, bf16[256,256]{1,0:T(8,128)(2,1)S(1)}, u32[]{:S(2)}, u32[]{:S(2)}) %collective-permute-start.17) | collective-permute-done | bytes 131104 | tf_op jit(solution)/shard_map/ppermute | solution.py:536
  70.9 2.7 %collective-permute-start.25 = (bf16[256,256]{1,0:T(8,128)(2,1)S(1)}, bf16[256,256]{1,0:T(8,128)(2,1)S(1)}, u32[]{:S(2)}, u32[]{:S(2)}) collective-permute-start(bf16[256,256]{1,0:T(8,128)(2,1)S(1)} %fusion), channel_id=1, source_target_pairs={{0,2},{1,3},{2,0},{3,1},{4,6},{5,7},{6,4},{7,5},{8,10},{9,11},{10,... | collective-permute-start | bytes 393224 | tf_op jit(solution)/shard_map/ppermute | solution.py:536
  73.6 5.2 %collective-permute-done.22.refs_2_ = bf16[2,256,256]{2,1,0:T(8,128)(2,1)S(1)} collective-permute-done((bf16[2,256,256]{2,1,0:T(8,128)(2,1)S(1)}, bf16[2,256,256]{2,1,0:T(8,128)(2,1)S(1)}, u32[]{:S(2)}, u32[]{:S(2)}) %collective-permute-start.22) | collective-permute-done | bytes 262176 | tf_op jit(solution)/shard_map/ppermute | solution.py:536
  78.8 2.6 %collective-permute-start.24 = (bf16[256,256]{1,0:T(8,128)(2,1)S(1)}, bf16[256,256]{1,0:T(8,128)(2,1)S(1)}, u32[]{:S(2)}, u32[]{:S(2)}) collective-permute-start(bf16[256,256]{1,0:T(8,128)(2,1)S(1)} %fusion.1), channel_id=1, source_target_pairs={{0,2},{1,3},{2,0},{3,1},{4,6},{5,7},{6,4},{7,5},{8,10},{9,11},{10,... | collective-permute-start | bytes 393224 | tf_op jit(solution)/shard_map/ppermute | solution.py:536
  81.4 4.0 %collective-permute-done.24.refs_4_ = bf16[256,256]{1,0:T(8,128)(2,1)S(1)} collective-permute-done((bf16[256,256]{1,0:T(8,128)(2,1)S(1)}, bf16[256,256]{1,0:T(8,128)(2,1)S(1)}, u32[]{:S(2)}, u32[]{:S(2)}) %collective-permute-start.24) | collective-permute-done | bytes 131104 | tf_op jit(solution)/shard_map/ppermute | solution.py:536
  85.5 3.1 %collective-permute-start.26 = (bf16[128,256]{1,0:T(8,128)(2,1)S(1)}, bf16[128,256]{1,0:T(8,128)(2,1)S(1)}, u32[]{:S(2)}, u32[]{:S(2)}) collective-permute-start(bf16[128,256]{1,0:T(8,128)(2,1)S(1)} %get-tuple-element.44), channel_id=1, source_target_pairs={{0,8},{4,12},{8,0},{12,4},{16,24},{20,28},{24,16},{28,20},{1,9},{5... | collective-permute-start | bytes 196616 | tf_op jit(solution)/shard_map/ppermute | solution.py:536
  90.9 2.0 %collective-permute-done.27.refs_2_ = bf16[128,256]{1,0:T(8,128)(2,1)S(1)} collective-permute-done((bf16[128,256]{1,0:T(8,128)(2,1)S(1)}, bf16[128,256]{1,0:T(8,128)(2,1)S(1)}, u32[]{:S(2)}, u32[]{:S(2)}) %collective-permute-start.27) | collective-permute-done | bytes 65568 | tf_op jit(solution)/shard_map/ppermute | solution.py:536
  (73 shorter events, 26.2 us)
Async XLA Ops:
  2.0 6.9 %collective-permute-start.2 = (bf16[2,128,256]{2,1,0:T(8,128)(2,1)S(1)}, bf16[2,128,256]{2,1,0:T(8,128)(2,1)S(1)}, u32[]{:S(2)}, u32[]{:S(2)}) collective-permute-start(bf16[2,128,256]{2,1,0:T(8,128)(2,1)S(1)} %get-tuple-element.27), channel_id=1, source_target_pairs={{0,8},{4,12},{8,0},{12,4},{16,24},{20,28},{24,16},{28,20},{1,9},{5... | collective-permute-start | bytes 393224 | tf_op jit(solution)/shard_map/ppermute | solution.py:536
  5.0 7.8 %collective-permute-start.3 = (bf16[2,128,256]{2,1,0:T(8,128)(2,1)S(1)}, bf16[2,128,256]{2,1,0:T(8,128)(2,1)S(1)}, u32[]{:S(2)}, u32[]{:S(2)}) collective-permute-start(bf16[2,128,256]{2,1,0:T(8,128)(2,1)S(1)} %get-tuple-element.28), channel_id=1, source_target_pairs={{0,16},{4,20},{8,24},{12,28},{16,0},{20,4},{24,8},{28,12},{1,17},{... | collective-permute-start | bytes 393224 | tf_op jit(solution)/shard_map/ppermute | solution.py:536
  6.5 6.3 %collective-permute-start.4 = (bf16[2,128,256]{2,1,0:T(8,128)(2,1)S(1)}, bf16[2,128,256]{2,1,0:T(8,128)(2,1)S(1)}, u32[]{:S(2)}, u32[]{:S(2)}) collective-permute-start(bf16[2,128,256]{2,1,0:T(8,128)(2,1)S(1)} %get-tuple-element.29), channel_id=1, source_target_pairs={{0,24},{4,28},{8,16},{12,20},{16,8},{20,12},{24,0},{28,4},{1,25},{... | collective-permute-start | bytes 393224 | tf_op jit(solution)/shard_map/ppermute | solution.py:536
  12.8 10.0 %collective-permute-start.5 = (bf16[4,128,256]{2,1,0:T(8,128)(2,1)S(1)}, bf16[4,128,256]{2,1,0:T(8,128)(2,1)}, u32[]{:S(2)}, u32[]{:S(2)}) collective-permute-start(bf16[4,128,256]{2,1,0:T(8,128)(2,1)S(1)} %pad_maximum_fusion.own_ref), channel_id=1, source_target_pairs={{0,4},{4,0},{8,12},{12,8},{16,20},{20,16},{24,28},{28,24},{1,5},{5... | collective-permute-start | bytes 786440 | tf_op jit(solution)/shard_map/ppermute | solution.py:536
  15.4 13.1 %collective-permute-start.6 = (bf16[4,128,256]{2,1,0:T(8,128)(2,1)}, bf16[4,128,256]{2,1,0:T(8,128)(2,1)S(1)}, u32[]{:S(2)}, u32[]{:S(2)}) collective-permute-start(bf16[4,128,256]{2,1,0:T(8,128)(2,1)} %pack_filter.5), channel_id=1, source_target_pairs={{0,8},{4,12},{8,0},{12,4},{16,24},{20,28},{24,16},{28,20},{1,9},{5... | collective-permute-start | bytes 786440 | tf_op jit(solution)/shard_map/ppermute | solution.py:536
  17.5 15.3 %collective-permute-start.7 = (bf16[4,128,256]{2,1,0:T(8,128)(2,1)}, bf16[4,128,256]{2,1,0:T(8,128)(2,1)S(1)}, u32[]{:S(2)}, u32[]{:S(2)}) collective-permute-start(bf16[4,128,256]{2,1,0:T(8,128)(2,1)} %pack_filter.6), channel_id=1, source_target_pairs={{0,16},{4,20},{8,24},{12,28},{16,0},{20,4},{24,8},{28,12},{1,17},{... | collective-permute-start | bytes 786440 | tf_op jit(solution)/shard_map/ppermute | solution.py:536
  19.3 13.5 %collective-permute-start.8 = (bf16[4,128,256]{2,1,0:T(8,128)(2,1)}, bf16[4,128,256]{2,1,0:T(8,128)(2,1)}, u32[]{:S(2)}, u32[]{:S(2)}) collective-permute-start(bf16[4,128,256]{2,1,0:T(8,128)(2,1)} %pack_filter.7), channel_id=1, source_target_pairs={{0,24},{4,28},{8,16},{12,20},{16,8},{20,12},{24,0},{28,4},{1,25},{... | collective-permute-start | bytes 786440 | tf_op jit(solution)/shard_map/ppermute | solution.py:536
  22.1 16.7 %collective-permute-start = (bf16[1024,128]{1,0:T(8,128)(2,1)S(1)}, bf16[1024,128]{1,0:T(8,128)(2,1)S(1)}, u32[]{:S(2)}, u32[]{:S(2)}) collective-permute-start(bf16[1024,128]{1,0:T(8,128)(2,1)S(1)} %get-tuple-element.49), channel_id=1, source_target_pairs={{0,0},{4,16},{8,4},{12,20},{16,8},{20,24},{24,12},{28,28},{1,1},{5... | collective-permute-start | bytes 786440 | tf_op jit(solution)/shard_map/ppermute | solution.py:562
  22.8 18.4 %collective-permute-start.1 = (bf16[1024,128]{1,0:T(8,128)(2,1)S(1)}, bf16[1024,128]{1,0:T(8,128)(2,1)S(1)}, u32[]{:S(2)}, u32[]{:S(2)}) collective-permute-start(bf16[1024,128]{1,0:T(8,128)(2,1)S(1)} %get-tuple-element.48), channel_id=1, source_target_pairs={{0,4},{4,20},{8,0},{12,16},{16,12},{20,28},{24,8},{28,24},{1,5},{5... | collective-permute-start | bytes 786440 | tf_op jit(solution)/shard_map/ppermute | solution.py:562
  35.8 10.1 %collective-permute-start.9 = (bf16[1024,128]{1,0:T(8,128)(2,1)S(1)}, bf16[1024,128]{1,0:T(8,128)(2,1)S(1)}, u32[]{:S(2)}, u32[]{:S(2)}) collective-permute-start(bf16[1024,128]{1,0:T(8,128)(2,1)S(1)} %get-tuple-element.31), channel_id=1, source_target_pairs={{0,8},{4,24},{8,12},{12,28},{16,0},{20,16},{24,4},{28,20},{1,9},{5... | collective-permute-start | bytes 786440 | tf_op jit(solution)/shard_map/ppermute | solution.py:562
  36.4 12.9 %collective-permute-start.10 = (bf16[1024,128]{1,0:T(8,128)(2,1)S(1)}, bf16[1024,128]{1,0:T(8,128)(2,1)S(1)}, u32[]{:S(2)}, u32[]{:S(2)}) collective-permute-start(bf16[1024,128]{1,0:T(8,128)(2,1)S(1)} %get-tuple-element.32), channel_id=1, source_target_pairs={{0,12},{4,28},{8,8},{12,24},{16,4},{20,20},{24,0},{28,16},{1,13},{... | collective-permute-start | bytes 786440 | tf_op jit(solution)/shard_map/ppermute | solution.py:562
  38.4 12.0 %collective-permute-start.15 = (bf16[4,128,256]{2,1,0:T(8,128)(2,1)S(1)}, bf16[4,128,256]{2,1,0:T(8,128)(2,1)S(1)}, u32[]{:S(2)}, u32[]{:S(2)}) collective-permute-start(bf16[4,128,256]{2,1,0:T(8,128)(2,1)S(1)} %get-tuple-element.34), channel_id=1, source_target_pairs={{0,4},{4,0},{8,12},{12,8},{16,20},{20,16},{24,28},{28,24},{1,5},{5... | collective-permute-start | bytes 786440 | tf_op jit(solution)/shard_map/ppermute | solution.py:536
  38.8 12.1 %collective-permute-start.11 = (bf16[1024,128]{1,0:T(8,128)(2,1)S(1)}, bf16[1024,128]{1,0:T(8,128)(2,1)S(1)}, u32[]{:S(2)}, u32[]{:S(2)}) collective-permute-start(bf16[1024,128]{1,0:T(8,128)(2,1)S(1)} %collective-permute-done.refs_0_), channel_id=1, source_target_pairs={{0,4},{4,0},{8,12},{12,8},{16,20},{20,16},{24,28},{28,24},{1,5},{5... | collective-permute-start | bytes 786440 | tf_op jit(solution)/shard_map/ppermute | solution.py:536
  41.2 10.8 %collective-permute-start.12 = (bf16[1024,128]{1,0:T(8,128)(2,1)S(1)}, bf16[1024,128]{1,0:T(8,128)(2,1)S(1)}, u32[]{:S(2)}, u32[]{:S(2)}) collective-permute-start(bf16[1024,128]{1,0:T(8,128)(2,1)S(1)} %collective-permute-done.1.refs_1_), channel_id=1, source_target_pairs={{0,4},{4,0},{8,12},{12,8},{16,20},{20,16},{24,28},{28,24},{1,5},{5... | collective-permute-start | bytes 786440 | tf_op jit(solution)/shard_map/ppermute | solution.py:536
  45.9 8.2 %collective-permute-start.13 = (bf16[1024,128]{1,0:T(8,128)(2,1)S(1)}, bf16[1024,128]{1,0:T(8,128)(2,1)S(1)}, u32[]{:S(2)}, u32[]{:S(2)}) collective-permute-start(bf16[1024,128]{1,0:T(8,128)(2,1)S(1)} %collective-permute-done.9.refs_2_), channel_id=1, source_target_pairs={{0,4},{4,0},{8,12},{12,8},{16,20},{20,16},{24,28},{28,24},{1,5},{5... | collective-permute-start | bytes 786440 | tf_op jit(solution)/shard_map/ppermute | solution.py:536
  50.5 6.4 %collective-permute-start.19 = (bf16[256,256]{1,0:T(8,128)(2,1)S(1)}, bf16[256,256]{1,0:T(8,128)(2,1)S(1)}, u32[]{:S(2)}, u32[]{:S(2)}) collective-permute-start(bf16[256,256]{1,0:T(8,128)(2,1)S(1)} %get-tuple-element.37.refs_0_), channel_id=1, source_target_pairs={{0,8},{4,12},{8,0},{12,4},{16,24},{20,28},{24,16},{28,20},{1,9},{5... | collective-permute-start | bytes 393224 | tf_op jit(solution)/shard_map/ppermute | solution.py:536
  50.9 8.0 %collective-permute-start.20 = (bf16[256,256]{1,0:T(8,128)(2,1)S(1)}, bf16[256,256]{1,0:T(8,128)(2,1)S(1)}, u32[]{:S(2)}, u32[]{:S(2)}) collective-permute-start(bf16[256,256]{1,0:T(8,128)(2,1)S(1)} %get-tuple-element.37.refs_0_), channel_id=1, source_target_pairs={{0,16},{4,20},{8,24},{12,28},{16,0},{20,4},{24,8},{28,12},{1,17},{... | collective-permute-start | bytes 393224 | tf_op jit(solution)/shard_map/ppermute | solution.py:536
  52.1 6.8 %collective-permute-start.21 = (bf16[256,256]{1,0:T(8,128)(2,1)S(1)}, bf16[256,256]{1,0:T(8,128)(2,1)S(1)}, u32[]{:S(2)}, u32[]{:S(2)}) collective-permute-start(bf16[256,256]{1,0:T(8,128)(2,1)S(1)} %get-tuple-element.37.refs_0_), channel_id=1, source_target_pairs={{0,24},{4,28},{8,16},{12,20},{16,8},{20,12},{24,0},{28,4},{1,25},{... | collective-permute-start | bytes 393224 | tf_op jit(solution)/shard_map/ppermute | solution.py:536
  59.7 11.2 %collective-permute-start.23 = (bf16[2,256,256]{2,1,0:T(8,128)(2,1)S(1)}, bf16[2,256,256]{2,1,0:T(8,128)(2,1)S(1)}, u32[]{:S(2)}, u32[]{:S(2)}) collective-permute-start(bf16[2,256,256]{2,1,0:T(8,128)(2,1)S(1)} %get-tuple-element.40), channel_id=1, source_target_pairs={{0,1},{1,0},{2,3},{3,2},{4,5},{5,4},{6,7},{7,6},{8,9},{9,8},{10,11... | collective-permute-start | bytes 786440 | tf_op jit(solution)/shard_map/ppermute | solution.py:536
  63.0 6.6 %collective-permute-start.17 = (bf16[256,256]{1,0:T(8,128)(2,1)S(1)}, bf16[256,256]{1,0:T(8,128)(2,1)S(1)}, u32[]{:S(2)}, u32[]{:S(2)}) collective-permute-start(bf16[256,256]{1,0:T(8,128)(2,1)S(1)} %get-tuple-element.35.refs_0_), channel_id=1, source_target_pairs={{0,16},{4,20},{8,24},{12,28},{16,0},{20,4},{24,8},{28,12},{1,17},{... | collective-permute-start | bytes 393224 | tf_op jit(solution)/shard_map/ppermute | solution.py:536
  63.3 6.3 %collective-permute-start.18 = (bf16[256,256]{1,0:T(8,128)(2,1)S(1)}, bf16[256,256]{1,0:T(8,128)(2,1)S(1)}, u32[]{:S(2)}, u32[]{:S(2)}) collective-permute-start(bf16[256,256]{1,0:T(8,128)(2,1)S(1)} %get-tuple-element.35.refs_0_), channel_id=1, source_target_pairs={{0,24},{4,28},{8,16},{12,20},{16,8},{20,12},{24,0},{28,4},{1,25},{... | collective-permute-start | bytes 393224 | tf_op jit(solution)/shard_map/ppermute | solution.py:536
  70.4 8.4 %collective-permute-start.22 = (bf16[2,256,256]{2,1,0:T(8,128)(2,1)S(1)}, bf16[2,256,256]{2,1,0:T(8,128)(2,1)S(1)}, u32[]{:S(2)}, u32[]{:S(2)}) collective-permute-start(bf16[2,256,256]{2,1,0:T(8,128)(2,1)S(1)} %get-tuple-element.39), channel_id=1, source_target_pairs={{0,1},{1,0},{2,3},{3,2},{4,5},{5,4},{6,7},{7,6},{8,9},{9,8},{10,11... | collective-permute-start | bytes 786440 | tf_op jit(solution)/shard_map/ppermute | solution.py:536
  70.9 10.5 %collective-permute-start.25 = (bf16[256,256]{1,0:T(8,128)(2,1)S(1)}, bf16[256,256]{1,0:T(8,128)(2,1)S(1)}, u32[]{:S(2)}, u32[]{:S(2)}) collective-permute-start(bf16[256,256]{1,0:T(8,128)(2,1)S(1)} %fusion), channel_id=1, source_target_pairs={{0,2},{1,3},{2,0},{3,1},{4,6},{5,7},{6,4},{7,5},{8,10},{9,11},{10,... | collective-permute-start | bytes 393224 | tf_op jit(solution)/shard_map/ppermute | solution.py:536
  78.8 6.6 %collective-permute-start.24 = (bf16[256,256]{1,0:T(8,128)(2,1)S(1)}, bf16[256,256]{1,0:T(8,128)(2,1)S(1)}, u32[]{:S(2)}, u32[]{:S(2)}) collective-permute-start(bf16[256,256]{1,0:T(8,128)(2,1)S(1)} %fusion.1), channel_id=1, source_target_pairs={{0,2},{1,3},{2,0},{3,1},{4,6},{5,7},{6,4},{7,5},{8,10},{9,11},{10,... | collective-permute-start | bytes 393224 | tf_op jit(solution)/shard_map/ppermute | solution.py:536
  (14 other events, 81.5 us)

commit v5 on v3

--- a/solution.py
+++ b/solution.py
@@ -212,51 +212,67 @@
     return pl.ds(pl.multiple_of(index * size, size), size)
 
 
-def pack_signals_kernel(chips, values_ref, gate_ref, *out_refs):
+def pack_signals_kernel(chips, values_ref, gate_ref, *refs):
+    out_refs, arrived = refs[:chips], refs[chips]
     chip, _ = own_place()
     lanes = out_refs[0].shape[2]
+    copies = []
     for offset in range(chips):
-        out_refs[offset][0] = values_ref[:, block_at(chip ^ offset, lanes)]
-        out_refs[offset][1] = gate_ref[:, block_at(chip ^ offset, lanes)]
+        here = block_at(chip ^ offset, lanes)
+        for plane, in_ref in enumerate((values_ref, gate_ref)):
+            copies.append(
+                pltpu.make_async_copy(in_ref.at[:, here], out_refs[offset].at[plane], arrived.at[offset, plane])
+            )
+    for copy in copies:
+        copy.start()
+    for copy in copies:
+        copy.wait()
 
 
 def pack_signals(values_in, gate_values, chips):
     rows, width = values_in.shape
     return pl.pallas_call(
         functools.partial(pack_signals_kernel, chips),
-        in_specs=[WHOLE] * 2,
+        in_specs=[pl.BlockSpec(memory_space=pltpu.HBM)] * 2,
         out_specs=[WHOLE] * chips,
         out_shape=[jax.ShapeDtypeStruct((2, rows, width // chips), BF16)] * chips,
+        scratch_shapes=[pltpu.SemaphoreType.DMA((chips, 2))],
+        compiler_params=pltpu.CompilerParams(vmem_limit_bytes=4 * 2**20),
         name="pack_signals",
     )(values_in, gate_values)
 
 
-def pack_filter_kernel(offset, filter_ref, out_ref, plane_ref, arrived):
+def pack_filters_kernel(chips, filter_ref, *refs):
+    out_refs, (plane_ref, arrived) = refs[:chips], refs[chips:]
     chip, _ = own_place()
-    planes, _, lanes = out_ref.shape
+    planes, _, lanes = out_refs[0].shape
+    order = [(offset, plane) for offset in reversed(range(chips)) for plane in range(planes)]
     copies = [
         pltpu.make_async_copy(
-            filter_ref.at[plane, :, block_at(chip ^ offset, lanes)], plane_ref.at[plane], arrived.at[plane]
+            filter_ref.at[plane, :, block_at(chip ^ offset, lanes)],
+            plane_ref.at[offset, plane],
+            arrived.at[offset, plane],
         )
-        for plane in range(planes)
+        for offset, plane in order
     ]
     for copy in copies:
         copy.start()
-    for plane, copy in enumerate(copies):
+    for (offset, plane), copy in zip(order, copies):
         copy.wait()
-        out_ref[plane] = plane_ref[plane].astype(BF16)
-
-
-def pack_filter(filters, chips, offset):
+        out_refs[offset][plane] = plane_ref[offset, plane].astype(BF16)
+
+
+def pack_filters(filters, chips):
     planes, rows, width = filters.shape
     shape = (planes, rows, width // chips)
     return pl.pallas_call(
-        functools.partial(pack_filter_kernel, offset),
-        in_specs=[pl.BlockSpec(memory_space=pl.ANY)],
-        out_specs=WHOLE,
-        out_shape=jax.ShapeDtypeStruct(shape, BF16),
-        scratch_shapes=[pltpu.VMEM(shape, F32), pltpu.SemaphoreType.DMA((planes,))],
-        name="pack_filter",
+        functools.partial(pack_filters_kernel, chips),
+        in_specs=[pl.BlockSpec(memory_space=pltpu.HBM)],
+        out_specs=[WHOLE] * chips,
+        out_shape=[jax.ShapeDtypeStruct(shape, BF16)] * chips,
+        scratch_shapes=[pltpu.VMEM((chips, *shape), F32), pltpu.SemaphoreType.DMA((chips, planes))],
+        compiler_params=pltpu.CompilerParams(vmem_limit_bytes=8 * 2**20),
+        name="pack_filters",
     )(filters)
 
 
@@ -393,25 +409,26 @@
             pltpu.VMEM(spectrum.shape, BF16),
             pltpu.VMEM(spectrum.shape, F32),
         ],
-        compiler_params=pltpu.CompilerParams(vmem_limit_bytes=40 * 2**20),
+        compiler_params=pltpu.CompilerParams(vmem_limit_bytes=32 * 2**20),
         name="backward",
     )(cos, sin, table, spectrum, *filters)
 
 
 def gate_kernel(chips, skip_ref, keep_ref, arrived_ref, *refs):
-    signal_refs, out_refs = refs[:chips], refs[chips:]
+    signal_refs, out_ref = refs[:chips], refs[chips]
     chip, _ = own_place()
     rows, lanes = keep_ref.shape[1:]
-    step = rows // len(out_refs)
+    pieces = out_ref.shape[0]
+    step = rows // pieces
     skip = skip_ref[:, block_at(chip, lanes)]
     for offset in range(chips):
         block = chip ^ offset
-        for part, out_ref in enumerate(out_refs):
-            here = pl.ds(part * step, step)
+        for piece in range(pieces):
+            here = pl.ds(piece * step, step)
             convolved = keep_ref[block, here, :] + arrived_ref[block, here, :].astype(F32)
             signal = signal_refs[offset][0, here, :].astype(F32)
             gate = signal_refs[offset][1, here, :].astype(F32)
-            out_ref[block_at(block, step), :] = (gate * (convolved + skip * signal)).astype(BF16)
+            out_ref[piece, block_at(block, step), :] = (gate * (convolved + skip * signal)).astype(BF16)
 
 
 def gate(skip, keep, arrived, signals, pieces):
@@ -419,8 +436,9 @@
     return pl.pallas_call(
         functools.partial(gate_kernel, chips),
         in_specs=[WHOLE] * (3 + chips),
-        out_specs=[WHOLE] * pieces,
-        out_shape=[jax.ShapeDtypeStruct((chips * rows // pieces, lanes), BF16)] * pieces,
+        out_specs=WHOLE,
+        out_shape=jax.ShapeDtypeStruct((pieces, chips * rows // pieces, lanes), BF16),
+        compiler_params=pltpu.CompilerParams(vmem_limit_bytes=6 * 2**20),
         name="gate",
     )(skip, keep, arrived, *signals)
 
@@ -443,17 +461,17 @@
         in_specs=[WHOLE] * (2 * layers),
         out_specs=WHOLE,
         out_shape=jax.ShapeDtypeStruct((layers, rows, 2 * share), BF16),
-        compiler_params=pltpu.CompilerParams(vmem_limit_bytes=32 * 2**20),
+        compiler_params=pltpu.CompilerParams(vmem_limit_bytes=8 * 2**20),
         name="arrange_weights",
     )(*own, *other)
 
 
-def project_kernel(chips, weight_ref, *refs):
+def project_kernel(chips, piece, weight_ref, *refs):
     gated_refs, (keep_ref, pass_ref, send_ref, joined_ref) = refs[:chips], refs[chips:]
     chip, _ = own_place()
-    lanes = gated_refs[0].shape[1]
+    lanes = gated_refs[0].shape[2]
     for offset in range(chips):
-        joined_ref[:, block_at(chip ^ offset, lanes)] = gated_refs[offset][...]
+        joined_ref[:, block_at(chip ^ offset, lanes)] = gated_refs[offset][piece]
 
     def partial_of(target):
         return jnp.dot(joined_ref[...], weight_ref[target], preferred_element_type=F32).astype(BF16)
@@ -464,18 +482,18 @@
     keep_ref[...] = partial_of(0)
 
 
-def project(weight, gated):
+def project(weight, gated, piece):
     chips = len(gated)
     _, depth, columns = weight.shape
-    rows = gated[0].shape[0]
+    rows = gated[0].shape[1]
     block = jax.ShapeDtypeStruct((rows, columns), BF16)
     return pl.pallas_call(
-        functools.partial(project_kernel, chips),
+        functools.partial(project_kernel, chips, piece),
         in_specs=[WHOLE] * (1 + chips),
         out_specs=[WHOLE] * 3,
         out_shape=[block, block, jax.ShapeDtypeStruct((2, rows, columns), BF16)],
         scratch_shapes=[pltpu.VMEM((rows, depth), BF16)],
-        compiler_params=pltpu.CompilerParams(vmem_limit_bytes=32 * 2**20),
+        compiler_params=pltpu.CompilerParams(vmem_limit_bytes=8 * 2**20),
         name="project",
     )(weight, *gated)
 
@@ -501,6 +519,7 @@
         in_specs=[WHOLE] * (3 * pieces),
         out_specs=[WHOLE] * chips,
         out_shape=[jax.ShapeDtypeStruct((rows * pieces // chips, columns), BF16)] * chips,
+        compiler_params=pltpu.CompilerParams(vmem_limit_bytes=4 * 2**20),
         name="finish",
     )(*keep, *first, *second)
 
@@ -521,6 +540,7 @@
         in_specs=[WHOLE] * chips,
         out_specs=WHOLE,
         out_shape=jax.ShapeDtypeStruct((rows, chips * columns), BF16),
+        compiler_params=pltpu.CompilerParams(vmem_limit_bytes=2 * 2**20),
         name="join",
     )(*blocks)
 
@@ -533,6 +553,10 @@
 
 def to_chips(blocks):
     return [swapped(block, "seq", 2 * offset) for offset, block in enumerate(blocks)]
+
+
+def after(value, *others):
+    return lax.optimization_barrier((value, *others))[0]
 
 
 def shards_direct(values_in, gate_values, filter_spectrum, skip_gain, out_weight):
@@ -544,26 +568,30 @@
     device = lax.axis_index("seq")
     tables = small_tables(parts, rows)
 
-    signals = to_chips(pack_signals(values_in, gate_values, chips))
-    flat_filters = filter_spectrum.reshape(4, rows, width)
-    filters = to_chips([pack_filter(flat_filters, chips, offset) for offset in range(chips)])
-
-    share = out_weight.shape[1] // layers
-    own_weight = []
-    for step in range(layers):
-        sent = lax.dynamic_slice_in_dim(out_weight, (device // 2 ^ step) * share, share, 1)
-        pairs = [(source, source % 2 * layers + (source // 2 ^ step)) for source in range(parts)]
-        own_weight.append(lax.ppermute(sent, "seq", pairs))
-    weight = arrange(own_weight, [swapped(block, "seq", 1) for block in own_weight])
-
-    own = jnp.stack([block[0] for block in signals])
+    signals = pack_signals(values_in, gate_values, chips)
+    filters = pack_filters(after(filter_spectrum.reshape(4, rows, width), signals[0]), chips)
+    signals = to_chips(signals)
+    own = jnp.stack([after(block, filters[0])[0] for block in signals])
+    filters = to_chips(filters)
     spectrum = forward(own, swapped(own, "seq", 1), tables)
     keep, send = backward(spectrum, filters, tables)
     gated = gate(skip_gain[None, :], keep, swapped(send, "seq", 1), signals, pieces)
 
+    share = out_weight.shape[1] // layers
+    sent = [
+        lax.dynamic_slice_in_dim(after(out_weight, own), (device // 2 ^ step) * share, share, 1)
+        for step in range(layers)
+    ]
+    own_weight = []
+    for step, earlier in enumerate((spectrum, send, send, gated)):
+        pairs = [(source, source % 2 * layers + (source // 2 ^ step)) for source in range(parts)]
+        own_weight.append(lax.ppermute(after(sent[step], earlier), "seq", pairs))
+    weight = arrange(own_weight, [swapped(after(block, gated), "seq", 1) for block in own_weight])
+
+    gathered = to_chips([gated] * chips)
     kept, firsts, seconds = [], [], []
-    for piece in gated:
-        keep, passed, send = project(weight, to_chips([piece] * chips))
+    for piece in range(pieces):
+        keep, passed, send = project(weight, gathered, piece)
         first = swapped(send, "chan", 1)
         passed = (passed.astype(F32) + first[1].astype(F32)).astype(BF16)
         kept.append(keep)

time: 95.6 us -> 94.2 us (0.985)
  Pallas kernels: 20.5 us -> 7.12 us
  waiting for transfers between devices: 35 us -> 46.2 us
  starting transfers between devices: 34.8 us -> 36.6 us
    ppermute x25 -> x22, waiting for transfers between devices: 34.8 us -> 43.9 us  [swapped(): lax.ppermute(value, axis, [(source, source ^ offset) for source in range(...]
    pallas_call x7 -> x4, Pallas kernels: 10.8 us -> 2.27 us  [the longest x2 1.51 us: project(): pl.pallas_call(functools.partial(project_kernel, chips, piece), in_specs=...]
    ppermute x4, waiting for transfers between devices: 0.18 us -> 2.35 us  [shards_direct(): own_weight.append(lax.ppermute(after(sent[step], earlier), 'seq', pairs))]
    pallas_call x1, Pallas kernels: 2.14 us -> 0.16 us  [gate(): pl.pallas_call(functools.partial(gate_kernel, chips), in_specs=[WHOLE] *...]
    pallas_call x1, Pallas kernels: 1.96 us -> 0.1 us  [finish(): pl.pallas_call(functools.partial(finish_kernel, chips, pieces), in_specs=...]
    ppermute x25 -> x22, starting transfers between devices: 28.2 us -> 29.2 us  [swapped(): lax.ppermute(value, axis, [(source, source ^ offset) for source in range(...]
    unnamed x46 -> x18, local copies, waits for them, and re-layouts: 3.47 us -> 3.56 us
  transfers between devices with their start and end apart: 29 -> 26, of which waited for: 12 -> 15; matrix products, arithmetic and copies ran while one was open for 1% -> 0% of each run, Pallas kernels for 15% -> 4%
where the time goes in v5:
time: 94.2 us; the launch traced here: 94 us
  waiting for transfers between devices  46.2 us (49%)
  starting transfers between devices  36.6 us (39%)
  Pallas kernels  7.12 us (8%)
  local copies, waits for them, and re-layouts  3.78 us (4%)
    ppermute x22, waiting for transfers between devices, swapped(): lax.ppermute(value, axis, [(source, source ^ offset) for source in range(...  43.9 us
    ppermute x22, starting transfers between devices, swapped(): lax.ppermute(value, axis, [(source, source ^ offset) for source in range(...  29.2 us
    ppermute x4, starting transfers between devices, shards_direct(): own_weight.append(lax.ppermute(after(sent[step], earlier), 'seq', pairs))  7.41 us
    unnamed x18, local copies, waits for them, and re-layouts  3.56 us
    ppermute x4, waiting for transfers between devices, shards_direct(): own_weight.append(lax.ppermute(after(sent[step], earlier), 'seq', pairs))  2.35 us
    pallas_call x1, Pallas kernels, backward(): pl.pallas_call(functools.partial(backward_kernel, chips), in_specs=[WHOLE...  2.02 us
  transfers between devices with their start and end apart: 26, of which 15 were waited for; matrix products, arithmetic and copies ran while one was open for 0% of the time, Pallas kernels for 4%

profile of v5, /device:TPU:0, one launch (start us, length us, event | category | flops | bytes accessed | tf_op | source)
XLA Modules:
  0.0 94.0 jit_solution(3611930017686635854)
XLA Ops:
  2.1 3.0 %collective-permute-start = (bf16[2,128,256]{2,1,0:T(8,128)(2,1)S(1)}, bf16[2,128,256]{2,1,0:T(8,128)(2,1)S(1)}, u32[]{:S(2)}, u32[]{:S(2)}) collective-permute-start(bf16[2,128,256]{2,1,0:T(8,128)(2,1)S(1)} %get-tuple-element.43), channel_id=1, source_target_pairs={{0,8},{4,12},{8,0},{12,4},{16,24},{20,28},{24,16},{28,20},{1,9},{5... | collective-permute-start | bytes 393224 | tf_op jit(solution)/shard_map/ppermute | solution.py:551
  5.1 1.5 %collective-permute-start.1 = (bf16[2,128,256]{2,1,0:T(8,128)(2,1)S(1)}, bf16[2,128,256]{2,1,0:T(8,128)(2,1)S(1)}, u32[]{:S(2)}, u32[]{:S(2)}) collective-permute-start(bf16[2,128,256]{2,1,0:T(8,128)(2,1)S(1)} %get-tuple-element.45), channel_id=1, source_target_pairs={{0,16},{4,20},{8,24},{12,28},{16,0},{20,4},{24,8},{28,12},{1,17},{... | collective-permute-start | bytes 393224 | tf_op jit(solution)/shard_map/ppermute | solution.py:551
  6.7 1.6 %copy-done = f32[2,2,128,1024]{3,2,1,0:T(8,128)S(1)} copy-done((f32[2,2,128,1024]{3,2,1,0:T(8,128)S(1)}, f32[2,2,128,1024]{3,2,1,0:T(8,128)}, u32[]{:S(2)}) %copy-start) | copy-done | bytes 2097176
  9.0 3.9 %collective-permute-done.1.refs_2_ = bf16[2,128,256]{2,1,0:T(8,128)(2,1)S(1)} collective-permute-done((bf16[2,128,256]{2,1,0:T(8,128)(2,1)S(1)}, bf16[2,128,256]{2,1,0:T(8,128)(2,1)S(1)}, u32[]{:S(2)}, u32[]{:S(2)}) %collective-permute-start.1) | collective-permute-done | bytes 131104 | tf_op jit(solution)/shard_map/ppermute | solution.py:551
  15.2 1.4 %collective-permute-start.7 = (bf16[4,128,256]{2,1,0:T(8,128)(2,1)S(1)}, bf16[4,128,256]{2,1,0:T(8,128)(2,1)S(1)}, u32[]{:S(2)}, u32[]{:S(2)}) collective-permute-start(bf16[4,128,256]{2,1,0:T(8,128)(2,1)S(1)} %get-tuple-element.53), channel_id=1, source_target_pairs={{0,24},{4,28},{8,16},{12,20},{16,8},{20,12},{24,0},{28,4},{1,25},{... | collective-permute-start | bytes 786440 | tf_op jit(solution)/shard_map/ppermute | solution.py:551
  16.6 1.5 %forward.1.spectrum_ref = f32[256,2048]{1,0:T(8,128)S(1)} custom-call(f32[2,128,8]{2,1,0:T(8,128)S(1)} %copy-done.1, f32[2,128,8]{2,1,0:T(8,128)S(1)} %copy-done.2, bf16[256,256]{1,0:T(8,128)(2,1)S(1)} %copy-done.6, bf16[4,128,256]{2,1,0:T(8,128)(2,1)S(1)} %pad_maximum_fusion.own_ref, bf16[4,128,256]{2,1,0:T(8,128)(2,1)S(1)} %collective-permute-done.3.other_ref), custom_call_target="tpu_custom_call" | custom-call | tf_op jit(solution)/shard_map/forward/pallas_call | solution.py:329
  18.1 4.1 %collective-permute-done.5.refs_1_ = bf16[4,128,256]{2,1,0:T(8,128)(2,1)S(1)} collective-permute-done((bf16[4,128,256]{2,1,0:T(8,128)(2,1)S(1)}, bf16[4,128,256]{2,1,0:T(8,128)(2,1)S(1)}, u32[]{:S(2)}, u32[]{:S(2)}) %collective-permute-start.5) | collective-permute-done | bytes 262176 | tf_op jit(solution)/shard_map/ppermute | solution.py:551
  22.2 4.5 %collective-permute-done.6.refs_2_ = bf16[4,128,256]{2,1,0:T(8,128)(2,1)S(1)} collective-permute-done((bf16[4,128,256]{2,1,0:T(8,128)(2,1)S(1)}, bf16[4,128,256]{2,1,0:T(8,128)(2,1)S(1)}, u32[]{:S(2)}, u32[]{:S(2)}) %collective-permute-start.6) | collective-permute-done | bytes 262176 | tf_op jit(solution)/shard_map/ppermute | solution.py:551
  26.7 1.6 %collective-permute-done.7.refs_3_ = bf16[4,128,256]{2,1,0:T(8,128)(2,1)S(1)} collective-permute-done((bf16[4,128,256]{2,1,0:T(8,128)(2,1)S(1)}, bf16[4,128,256]{2,1,0:T(8,128)(2,1)S(1)}, u32[]{:S(2)}, u32[]{:S(2)}) %collective-permute-start.7) | collective-permute-done | bytes 262176 | tf_op jit(solution)/shard_map/ppermute | solution.py:551
  28.3 2.0 %backward.1 = (f32[4,128,256]{2,1,0:T(8,128)S(1)}, bf16[4,128,256]{2,1,0:T(8,128)(2,1)S(1)}) custom-call(f32[2,128,8]{2,1,0:T(8,128)S(1)} %copy-done.1, f32[2,128,8]{2,1,0:T(8,128)S(1)} %copy-done.2, bf16[256,256]{1,0:T(8,128)(2,1)S(1)} %copy-done.5, f32[256,2048]{1,0:T(8,128)S(1)} %forward.1.spectrum_ref, ...), custom_call_target="tpu_custom_call" | custom-call | tf_op jit(solution)/shard_map/backward/pallas_call | solution.py:402
  33.4 4.8 %collective-permute-start.11 = (bf16[1024,128]{1,0:T(8,128)(2,1)S(1)}, bf16[1024,128]{1,0:T(8,128)(2,1)S(1)}, u32[]{:S(2)}, u32[]{:S(2)}) collective-permute-start(bf16[1024,128]{1,0:T(8,128)(2,1)S(1)} %get-tuple-element.58), channel_id=1, source_target_pairs={{0,12},{4,28},{8,8},{12,24},{16,4},{20,20},{24,0},{28,16},{1,13},{... | collective-permute-start | bytes 786440 | tf_op jit(solution)/shard_map/ppermute | solution.py:588
  38.3 1.6 %collective-permute-done.9.refs_2_ = bf16[1024,128]{1,0:T(8,128)(2,1)S(1)} collective-permute-done((bf16[1024,128]{1,0:T(8,128)(2,1)S(1)}, bf16[1024,128]{1,0:T(8,128)(2,1)S(1)}, u32[]{:S(2)}, u32[]{:S(2)}) %collective-permute-start.9) | collective-permute-done | bytes 262176 | tf_op jit(solution)/shard_map/ppermute | solution.py:588
  40.6 2.2 %collective-permute-start.16 = (bf16[2,256,256]{2,1,0:T(8,128)(2,1)S(1)}, bf16[2,256,256]{2,1,0:T(8,128)(2,1)S(1)}, u32[]{:S(2)}, u32[]{:S(2)}) collective-permute-start(bf16[2,256,256]{2,1,0:T(8,128)(2,1)S(1)} %gate.1.refs_0_), channel_id=1, source_target_pairs={{0,8},{4,12},{8,0},{12,4},{16,24},{20,28},{24,16},{28,20},{1,9},{5... | collective-permute-start | bytes 786440 | tf_op jit(solution)/shard_map/ppermute | solution.py:551
  42.8 3.4 %collective-permute-start.12 = (bf16[1024,128]{1,0:T(8,128)(2,1)S(1)}, bf16[1024,128]{1,0:T(8,128)(2,1)S(1)}, u32[]{:S(2)}, u32[]{:S(2)}) collective-permute-start(bf16[1024,128]{1,0:T(8,128)(2,1)S(1)} %collective-permute-done.4.refs_0_), channel_id=1, source_target_pairs={{0,4},{4,0},{8,12},{12,8},{16,20},{20,16},{24,28},{28,24},{1,5},{5... | collective-permute-start | bytes 786440 | tf_op jit(solution)/shard_map/ppermute | solution.py:551
  47.8 2.8 %collective-permute-start.18 = (bf16[2,256,256]{2,1,0:T(8,128)(2,1)S(1)}, bf16[2,256,256]{2,1,0:T(8,128)(2,1)S(1)}, u32[]{:S(2)}, u32[]{:S(2)}) collective-permute-start(bf16[2,256,256]{2,1,0:T(8,128)(2,1)S(1)} %gate.1.refs_0_), channel_id=1, source_target_pairs={{0,24},{4,28},{8,16},{12,20},{16,8},{20,12},{24,0},{28,4},{1,25},{... | collective-permute-start | bytes 786440 | tf_op jit(solution)/shard_map/ppermute | solution.py:551
  51.9 8.7 %collective-permute-done.17.refs_2_ = bf16[2,256,256]{2,1,0:T(8,128)(2,1)S(1)} collective-permute-done((bf16[2,256,256]{2,1,0:T(8,128)(2,1)S(1)}, bf16[2,256,256]{2,1,0:T(8,128)(2,1)S(1)}, u32[]{:S(2)}, u32[]{:S(2)}) %collective-permute-start.17) | collective-permute-done | bytes 262176 | tf_op jit(solution)/shard_map/ppermute | solution.py:551
  61.4 1.6 %collective-permute-start.20 = (bf16[2,256,256]{2,1,0:T(8,128)(2,1)S(1)}, bf16[2,256,256]{2,1,0:T(8,128)(2,1)S(1)}, u32[]{:S(2)}, u32[]{:S(2)}) collective-permute-start(bf16[2,256,256]{2,1,0:T(8,128)(2,1)S(1)} %get-tuple-element.66), channel_id=1, source_target_pairs={{0,1},{1,0},{2,3},{3,2},{4,5},{5,4},{6,7},{7,6},{8,9},{9,8},{10,11... | collective-permute-start | bytes 786440 | tf_op jit(solution)/shard_map/ppermute | solution.py:551
  64.3 6.4 %collective-permute-done.20.refs_3_ = bf16[2,256,256]{2,1,0:T(8,128)(2,1)S(1)} collective-permute-done((bf16[2,256,256]{2,1,0:T(8,128)(2,1)S(1)}, bf16[2,256,256]{2,1,0:T(8,128)(2,1)S(1)}, u32[]{:S(2)}, u32[]{:S(2)}) %collective-permute-start.20) | collective-permute-done | bytes 262176 | tf_op jit(solution)/shard_map/ppermute | solution.py:551
  70.7 2.6 %collective-permute-start.22 = (bf16[256,256]{1,0:T(8,128)(2,1)S(1)}, bf16[256,256]{1,0:T(8,128)(2,1)S(1)}, u32[]{:S(2)}, u32[]{:S(2)}) collective-permute-start(bf16[256,256]{1,0:T(8,128)(2,1)S(1)} %fusion), channel_id=1, source_target_pairs={{0,2},{1,3},{2,0},{3,1},{4,6},{5,7},{6,4},{7,5},{8,10},{9,11},{10,... | collective-permute-start | bytes 393224 | tf_op jit(solution)/shard_map/ppermute | solution.py:551
  73.4 3.0 %collective-permute-done.19.refs_2_ = bf16[2,256,256]{2,1,0:T(8,128)(2,1)S(1)} collective-permute-done((bf16[2,256,256]{2,1,0:T(8,128)(2,1)S(1)}, bf16[2,256,256]{2,1,0:T(8,128)(2,1)S(1)}, u32[]{:S(2)}, u32[]{:S(2)}) %collective-permute-start.19) | collective-permute-done | bytes 262176 | tf_op jit(solution)/shard_map/ppermute | solution.py:551
  76.4 2.1 %collective-permute-start.21 = (bf16[256,256]{1,0:T(8,128)(2,1)S(1)}, bf16[256,256]{1,0:T(8,128)(2,1)S(1)}, u32[]{:S(2)}, u32[]{:S(2)}) collective-permute-start(bf16[256,256]{1,0:T(8,128)(2,1)S(1)} %fusion.1), channel_id=1, source_target_pairs={{0,2},{1,3},{2,0},{3,1},{4,6},{5,7},{6,4},{7,5},{8,10},{9,11},{10,... | collective-permute-start | bytes 393224 | tf_op jit(solution)/shard_map/ppermute | solution.py:551
  78.5 6.2 %collective-permute-done.21.refs_4_ = bf16[256,256]{1,0:T(8,128)(2,1)S(1)} collective-permute-done((bf16[256,256]{1,0:T(8,128)(2,1)S(1)}, bf16[256,256]{1,0:T(8,128)(2,1)S(1)}, u32[]{:S(2)}, u32[]{:S(2)}) %collective-permute-start.21) | collective-permute-done | bytes 131104 | tf_op jit(solution)/shard_map/ppermute | solution.py:551
  84.8 2.6 %collective-permute-start.23 = (bf16[128,256]{1,0:T(8,128)(2,1)S(1)}, bf16[128,256]{1,0:T(8,128)(2,1)S(1)}, u32[]{:S(2)}, u32[]{:S(2)}) collective-permute-start(bf16[128,256]{1,0:T(8,128)(2,1)S(1)} %get-tuple-element.70), channel_id=1, source_target_pairs={{0,8},{4,12},{8,0},{12,4},{16,24},{20,28},{24,16},{28,20},{1,9},{5... | collective-permute-start | bytes 196616 | tf_op jit(solution)/shard_map/ppermute | solution.py:551
  89.7 2.3 %collective-permute-done.24.refs_2_ = bf16[128,256]{1,0:T(8,128)(2,1)S(1)} collective-permute-done((bf16[128,256]{1,0:T(8,128)(2,1)S(1)}, bf16[128,256]{1,0:T(8,128)(2,1)S(1)}, u32[]{:S(2)}, u32[]{:S(2)}) %collective-permute-start.24) | collective-permute-done | bytes 65568 | tf_op jit(solution)/shard_map/ppermute | solution.py:551
  (64 shorter events, 18.2 us)
Async XLA Ops:
  2.1 6.9 %collective-permute-start = (bf16[2,128,256]{2,1,0:T(8,128)(2,1)S(1)}, bf16[2,128,256]{2,1,0:T(8,128)(2,1)S(1)}, u32[]{:S(2)}, u32[]{:S(2)}) collective-permute-start(bf16[2,128,256]{2,1,0:T(8,128)(2,1)S(1)} %get-tuple-element.43), channel_id=1, source_target_pairs={{0,8},{4,12},{8,0},{12,4},{16,24},{20,28},{24,16},{28,20},{1,9},{5... | collective-permute-start | bytes 393224 | tf_op jit(solution)/shard_map/ppermute | solution.py:551
  5.1 7.8 %collective-permute-start.1 = (bf16[2,128,256]{2,1,0:T(8,128)(2,1)S(1)}, bf16[2,128,256]{2,1,0:T(8,128)(2,1)S(1)}, u32[]{:S(2)}, u32[]{:S(2)}) collective-permute-start(bf16[2,128,256]{2,1,0:T(8,128)(2,1)S(1)} %get-tuple-element.45), channel_id=1, source_target_pairs={{0,16},{4,20},{8,24},{12,28},{16,0},{20,4},{24,8},{28,12},{1,17},{... | collective-permute-start | bytes 393224 | tf_op jit(solution)/shard_map/ppermute | solution.py:551
  6.6 6.3 %collective-permute-start.2 = (bf16[2,128,256]{2,1,0:T(8,128)(2,1)S(1)}, bf16[2,128,256]{2,1,0:T(8,128)(2,1)S(1)}, u32[]{:S(2)}, u32[]{:S(2)}) collective-permute-start(bf16[2,128,256]{2,1,0:T(8,128)(2,1)S(1)} %get-tuple-element.47), channel_id=1, source_target_pairs={{0,24},{4,28},{8,16},{12,20},{16,8},{20,12},{24,0},{28,4},{1,25},{... | collective-permute-start | bytes 393224 | tf_op jit(solution)/shard_map/ppermute | solution.py:551
  13.1 9.2 %collective-permute-start.5 = (bf16[4,128,256]{2,1,0:T(8,128)(2,1)S(1)}, bf16[4,128,256]{2,1,0:T(8,128)(2,1)S(1)}, u32[]{:S(2)}, u32[]{:S(2)}) collective-permute-start(bf16[4,128,256]{2,1,0:T(8,128)(2,1)S(1)} %get-tuple-element.51), channel_id=1, source_target_pairs={{0,8},{4,12},{8,0},{12,4},{16,24},{20,28},{24,16},{28,20},{1,9},{5... | collective-permute-start | bytes 786440 | tf_op jit(solution)/shard_map/ppermute | solution.py:551
  14.3 12.4 %collective-permute-start.6 = (bf16[4,128,256]{2,1,0:T(8,128)(2,1)S(1)}, bf16[4,128,256]{2,1,0:T(8,128)(2,1)S(1)}, u32[]{:S(2)}, u32[]{:S(2)}) collective-permute-start(bf16[4,128,256]{2,1,0:T(8,128)(2,1)S(1)} %get-tuple-element.52), channel_id=1, source_target_pairs={{0,16},{4,20},{8,24},{12,28},{16,0},{20,4},{24,8},{28,12},{1,17},{... | collective-permute-start | bytes 786440 | tf_op jit(solution)/shard_map/ppermute | solution.py:551
  15.2 13.2 %collective-permute-start.7 = (bf16[4,128,256]{2,1,0:T(8,128)(2,1)S(1)}, bf16[4,128,256]{2,1,0:T(8,128)(2,1)S(1)}, u32[]{:S(2)}, u32[]{:S(2)}) collective-permute-start(bf16[4,128,256]{2,1,0:T(8,128)(2,1)S(1)} %get-tuple-element.53), channel_id=1, source_target_pairs={{0,24},{4,28},{8,16},{12,20},{16,8},{20,12},{24,0},{28,4},{1,25},{... | collective-permute-start | bytes 786440 | tf_op jit(solution)/shard_map/ppermute | solution.py:551
  30.7 9.2 %collective-permute-start.9 = (bf16[1024,128]{1,0:T(8,128)(2,1)S(1)}, bf16[1024,128]{1,0:T(8,128)(2,1)S(1)}, u32[]{:S(2)}, u32[]{:S(2)}) collective-permute-start(bf16[1024,128]{1,0:T(8,128)(2,1)S(1)} %get-tuple-element.56), channel_id=1, source_target_pairs={{0,8},{4,24},{8,12},{12,28},{16,0},{20,16},{24,4},{28,20},{1,9},{5... | collective-permute-start | bytes 786440 | tf_op jit(solution)/shard_map/ppermute | solution.py:588
  31.5 9.1 %collective-permute-start.8 = (bf16[1024,128]{1,0:T(8,128)(2,1)S(1)}, bf16[1024,128]{1,0:T(8,128)(2,1)S(1)}, u32[]{:S(2)}, u32[]{:S(2)}) collective-permute-start(bf16[1024,128]{1,0:T(8,128)(2,1)S(1)} %get-tuple-element.55), channel_id=1, source_target_pairs={{0,4},{4,20},{8,0},{12,16},{16,12},{20,28},{24,8},{28,24},{1,5},{5... | collective-permute-start | bytes 786440 | tf_op jit(solution)/shard_map/ppermute | solution.py:588
  32.6 10.2 %collective-permute-start.4 = (bf16[1024,128]{1,0:T(8,128)(2,1)S(1)}, bf16[1024,128]{1,0:T(8,128)(2,1)S(1)}, u32[]{:S(2)}, u32[]{:S(2)}) collective-permute-start(bf16[1024,128]{1,0:T(8,128)(2,1)S(1)} %get-tuple-element.50), channel_id=1, source_target_pairs={{0,0},{4,16},{8,4},{12,20},{16,8},{20,24},{24,12},{28,28},{1,1},{5... | collective-permute-start | bytes 786440 | tf_op jit(solution)/shard_map/ppermute | solution.py:588
  33.4 12.8 %collective-permute-start.11 = (bf16[1024,128]{1,0:T(8,128)(2,1)S(1)}, bf16[1024,128]{1,0:T(8,128)(2,1)S(1)}, u32[]{:S(2)}, u32[]{:S(2)}) collective-permute-start(bf16[1024,128]{1,0:T(8,128)(2,1)S(1)} %get-tuple-element.58), channel_id=1, source_target_pairs={{0,12},{4,28},{8,8},{12,24},{16,4},{20,20},{24,0},{28,16},{1,13},{... | collective-permute-start | bytes 786440 | tf_op jit(solution)/shard_map/ppermute | solution.py:588
  39.9 6.9 %collective-permute-start.14 = (bf16[1024,128]{1,0:T(8,128)(2,1)S(1)}, bf16[1024,128]{1,0:T(8,128)(2,1)S(1)}, u32[]{:S(2)}, u32[]{:S(2)}) collective-permute-start(bf16[1024,128]{1,0:T(8,128)(2,1)S(1)} %collective-permute-done.9.refs_2_), channel_id=1, source_target_pairs={{0,4},{4,0},{8,12},{12,8},{16,20},{20,16},{24,28},{28,24},{1,5},{5... | collective-permute-start | bytes 786440 | tf_op jit(solution)/shard_map/ppermute | solution.py:551
  40.6 7.1 %collective-permute-start.13 = (bf16[1024,128]{1,0:T(8,128)(2,1)S(1)}, bf16[1024,128]{1,0:T(8,128)(2,1)S(1)}, u32[]{:S(2)}, u32[]{:S(2)}) collective-permute-start(bf16[1024,128]{1,0:T(8,128)(2,1)S(1)} %collective-permute-done.8.refs_1_), channel_id=1, source_target_pairs={{0,4},{4,0},{8,12},{12,8},{16,20},{20,16},{24,28},{28,24},{1,5},{5... | collective-permute-start | bytes 786440 | tf_op jit(solution)/shard_map/ppermute | solution.py:551
  40.6 11.2 %collective-permute-start.16 = (bf16[2,256,256]{2,1,0:T(8,128)(2,1)S(1)}, bf16[2,256,256]{2,1,0:T(8,128)(2,1)S(1)}, u32[]{:S(2)}, u32[]{:S(2)}) collective-permute-start(bf16[2,256,256]{2,1,0:T(8,128)(2,1)S(1)} %gate.1.refs_0_), channel_id=1, source_target_pairs={{0,8},{4,12},{8,0},{12,4},{16,24},{20,28},{24,16},{28,20},{1,9},{5... | collective-permute-start | bytes 786440 | tf_op jit(solution)/shard_map/ppermute | solution.py:551
  42.8 7.8 %collective-permute-start.12 = (bf16[1024,128]{1,0:T(8,128)(2,1)S(1)}, bf16[1024,128]{1,0:T(8,128)(2,1)S(1)}, u32[]{:S(2)}, u32[]{:S(2)}) collective-permute-start(bf16[1024,128]{1,0:T(8,128)(2,1)S(1)} %collective-permute-done.4.refs_0_), channel_id=1, source_target_pairs={{0,4},{4,0},{8,12},{12,8},{16,20},{20,16},{24,28},{28,24},{1,5},{5... | collective-permute-start | bytes 786440 | tf_op jit(solution)/shard_map/ppermute | solution.py:551
  46.2 4.3 %collective-permute-start.15 = (bf16[1024,128]{1,0:T(8,128)(2,1)S(1)}, bf16[1024,128]{1,0:T(8,128)(2,1)S(1)}, u32[]{:S(2)}, u32[]{:S(2)}) collective-permute-start(bf16[1024,128]{1,0:T(8,128)(2,1)S(1)} %collective-permute-done.11.refs_3_), channel_id=1, source_target_pairs={{0,4},{4,0},{8,12},{12,8},{16,20},{20,16},{24,28},{28,24},{1,5},{5... | collective-permute-start | bytes 786440 | tf_op jit(solution)/shard_map/ppermute | solution.py:551
  46.8 13.8 %collective-permute-start.17 = (bf16[2,256,256]{2,1,0:T(8,128)(2,1)S(1)}, bf16[2,256,256]{2,1,0:T(8,128)(2,1)S(1)}, u32[]{:S(2)}, u32[]{:S(2)}) collective-permute-start(bf16[2,256,256]{2,1,0:T(8,128)(2,1)S(1)} %gate.1.refs_0_), channel_id=1, source_target_pairs={{0,16},{4,20},{8,24},{12,28},{16,0},{20,4},{24,8},{28,12},{1,17},{... | collective-permute-start | bytes 786440 | tf_op jit(solution)/shard_map/ppermute | solution.py:551
  47.8 12.8 %collective-permute-start.18 = (bf16[2,256,256]{2,1,0:T(8,128)(2,1)S(1)}, bf16[2,256,256]{2,1,0:T(8,128)(2,1)S(1)}, u32[]{:S(2)}, u32[]{:S(2)}) collective-permute-start(bf16[2,256,256]{2,1,0:T(8,128)(2,1)S(1)} %gate.1.refs_0_), channel_id=1, source_target_pairs={{0,24},{4,28},{8,16},{12,20},{16,8},{20,12},{24,0},{28,4},{1,25},{... | collective-permute-start | bytes 786440 | tf_op jit(solution)/shard_map/ppermute | solution.py:551
  61.4 9.3 %collective-permute-start.20 = (bf16[2,256,256]{2,1,0:T(8,128)(2,1)S(1)}, bf16[2,256,256]{2,1,0:T(8,128)(2,1)S(1)}, u32[]{:S(2)}, u32[]{:S(2)}) collective-permute-start(bf16[2,256,256]{2,1,0:T(8,128)(2,1)S(1)} %get-tuple-element.66), channel_id=1, source_target_pairs={{0,1},{1,0},{2,3},{3,2},{4,5},{5,4},{6,7},{7,6},{8,9},{9,8},{10,11... | collective-permute-start | bytes 786440 | tf_op jit(solution)/shard_map/ppermute | solution.py:551
  63.8 12.6 %collective-permute-start.19 = (bf16[2,256,256]{2,1,0:T(8,128)(2,1)S(1)}, bf16[2,256,256]{2,1,0:T(8,128)(2,1)S(1)}, u32[]{:S(2)}, u32[]{:S(2)}) collective-permute-start(bf16[2,256,256]{2,1,0:T(8,128)(2,1)S(1)} %get-tuple-element.65), channel_id=1, source_target_pairs={{0,1},{1,0},{2,3},{3,2},{4,5},{5,4},{6,7},{7,6},{8,9},{9,8},{10,11... | collective-permute-start | bytes 786440 | tf_op jit(solution)/shard_map/ppermute | solution.py:551
  70.7 7.8 %collective-permute-start.22 = (bf16[256,256]{1,0:T(8,128)(2,1)S(1)}, bf16[256,256]{1,0:T(8,128)(2,1)S(1)}, u32[]{:S(2)}, u32[]{:S(2)}) collective-permute-start(bf16[256,256]{1,0:T(8,128)(2,1)S(1)} %fusion), channel_id=1, source_target_pairs={{0,2},{1,3},{2,0},{3,1},{4,6},{5,7},{6,4},{7,5},{8,10},{9,11},{10,... | collective-permute-start | bytes 393224 | tf_op jit(solution)/shard_map/ppermute | solution.py:551
  76.4 8.3 %collective-permute-start.21 = (bf16[256,256]{1,0:T(8,128)(2,1)S(1)}, bf16[256,256]{1,0:T(8,128)(2,1)S(1)}, u32[]{:S(2)}, u32[]{:S(2)}) collective-permute-start(bf16[256,256]{1,0:T(8,128)(2,1)S(1)} %fusion.1), channel_id=1, source_target_pairs={{0,2},{1,3},{2,0},{3,1},{4,6},{5,7},{6,4},{7,5},{8,10},{9,11},{10,... | collective-permute-start | bytes 393224 | tf_op jit(solution)/shard_map/ppermute | solution.py:551
  84.8 4.9 %collective-permute-start.23 = (bf16[128,256]{1,0:T(8,128)(2,1)S(1)}, bf16[128,256]{1,0:T(8,128)(2,1)S(1)}, u32[]{:S(2)}, u32[]{:S(2)}) collective-permute-start(bf16[128,256]{1,0:T(8,128)(2,1)S(1)} %get-tuple-element.70), channel_id=1, source_target_pairs={{0,8},{4,12},{8,0},{12,4},{16,24},{20,28},{24,16},{28,20},{1,9},{5... | collective-permute-start | bytes 196616 | tf_op jit(solution)/shard_map/ppermute | solution.py:551
  87.4 4.6 %collective-permute-start.24 = (bf16[128,256]{1,0:T(8,128)(2,1)S(1)}, bf16[128,256]{1,0:T(8,128)(2,1)S(1)}, u32[]{:S(2)}, u32[]{:S(2)}) collective-permute-start(bf16[128,256]{1,0:T(8,128)(2,1)S(1)} %get-tuple-element.71), channel_id=1, source_target_pairs={{0,16},{4,20},{8,24},{12,28},{16,0},{20,4},{24,8},{28,12},{1,17},{... | collective-permute-start | bytes 196616 | tf_op jit(solution)/shard_map/ppermute | solution.py:551
  88.1 5.2 %collective-permute-start.25 = (bf16[128,256]{1,0:T(8,128)(2,1)S(1)}, bf16[128,256]{1,0:T(8,128)(2,1)S(1)}, u32[]{:S(2)}, u32[]{:S(2)}) collective-permute-start(bf16[128,256]{1,0:T(8,128)(2,1)S(1)} %get-tuple-element.72), channel_id=1, source_target_pairs={{0,24},{4,28},{8,16},{12,20},{16,8},{20,12},{24,0},{28,4},{1,25},{... | collective-permute-start | bytes 196616 | tf_op jit(solution)/shard_map/ppermute | solution.py:551
  (11 other events, 104.9 us)

commit v6 on v5

--- a/solution.py
+++ b/solution.py
@@ -164,6 +164,7 @@
 
 
 WHOLE = pl.BlockSpec(memory_space=pltpu.VMEM)
+CHEAP = pl.CostEstimate(flops=0, transcendentals=0, bytes_accessed=0)
 
 
 def small_tables(parts, rows):
@@ -212,68 +213,47 @@
     return pl.ds(pl.multiple_of(index * size, size), size)
 
 
-def pack_signals_kernel(chips, values_ref, gate_ref, *refs):
-    out_refs, arrived = refs[:chips], refs[chips]
+def pack_kernel(chips, planes, signal_ref, filter_ref, *refs):
+    out_refs, (plane_ref, arrived) = refs[:chips], refs[chips:]
     chip, _ = own_place()
     lanes = out_refs[0].shape[2]
     copies = []
-    for offset in range(chips):
+    for offset in reversed(range(chips)):
         here = block_at(chip ^ offset, lanes)
-        for plane, in_ref in enumerate((values_ref, gate_ref)):
+        for place, plane in enumerate(planes):
             copies.append(
-                pltpu.make_async_copy(in_ref.at[:, here], out_refs[offset].at[plane], arrived.at[offset, plane])
+                pltpu.make_async_copy(
+                    filter_ref.at[plane, :, here], plane_ref.at[offset, place], arrived.at[offset, 1 + place]
+                )
             )
+        copies.append(
+            pltpu.make_async_copy(signal_ref.at[:, here], out_refs[offset].at[0], arrived.at[offset, 0])
+        )
     for copy in copies:
         copy.start()
     for copy in copies:
         copy.wait()
-
-
-def pack_signals(values_in, gate_values, chips):
-    rows, width = values_in.shape
-    return pl.pallas_call(
-        functools.partial(pack_signals_kernel, chips),
+    for offset in range(chips):
+        for place in range(len(planes)):
+            out_refs[offset][1 + place] = plane_ref[offset, place].astype(BF16)
+
+
+def pack(signal, filters, chips, planes):
+    rows, width = signal.shape
+    lanes = width // chips
+    return pl.pallas_call(
+        functools.partial(pack_kernel, chips, planes),
         in_specs=[pl.BlockSpec(memory_space=pltpu.HBM)] * 2,
         out_specs=[WHOLE] * chips,
-        out_shape=[jax.ShapeDtypeStruct((2, rows, width // chips), BF16)] * chips,
-        scratch_shapes=[pltpu.SemaphoreType.DMA((chips, 2))],
-        compiler_params=pltpu.CompilerParams(vmem_limit_bytes=4 * 2**20),
-        name="pack_signals",
-    )(values_in, gate_values)
-
-
-def pack_filters_kernel(chips, filter_ref, *refs):
-    out_refs, (plane_ref, arrived) = refs[:chips], refs[chips:]
-    chip, _ = own_place()
-    planes, _, lanes = out_refs[0].shape
-    order = [(offset, plane) for offset in reversed(range(chips)) for plane in range(planes)]
-    copies = [
-        pltpu.make_async_copy(
-            filter_ref.at[plane, :, block_at(chip ^ offset, lanes)],
-            plane_ref.at[offset, plane],
-            arrived.at[offset, plane],
-        )
-        for offset, plane in order
-    ]
-    for copy in copies:
-        copy.start()
-    for (offset, plane), copy in zip(order, copies):
-        copy.wait()
-        out_refs[offset][plane] = plane_ref[offset, plane].astype(BF16)
-
-
-def pack_filters(filters, chips):
-    planes, rows, width = filters.shape
-    shape = (planes, rows, width // chips)
-    return pl.pallas_call(
-        functools.partial(pack_filters_kernel, chips),
-        in_specs=[pl.BlockSpec(memory_space=pltpu.HBM)],
-        out_specs=[WHOLE] * chips,
-        out_shape=[jax.ShapeDtypeStruct(shape, BF16)] * chips,
-        scratch_shapes=[pltpu.VMEM((chips, *shape), F32), pltpu.SemaphoreType.DMA((chips, planes))],
+        out_shape=[jax.ShapeDtypeStruct((1 + len(planes), rows, lanes), BF16)] * chips,
+        scratch_shapes=[
+            pltpu.VMEM((chips, len(planes), rows, lanes), F32),
+            pltpu.SemaphoreType.DMA((chips, 1 + len(planes))),
+        ],
+        cost_estimate=CHEAP,
         compiler_params=pltpu.CompilerParams(vmem_limit_bytes=8 * 2**20),
-        name="pack_filters",
-    )(filters)
+        name="pack",
+    )(pltpu.with_memory_space_constraint(signal, pltpu.HBM), pltpu.with_memory_space_constraint(filters, pltpu.HBM))
 
 
 def forward_kernel(chips, cos_ref, sin_ref, table_ref, own_ref, other_ref, out_ref, signal_ref, waves_ref):
@@ -332,26 +312,28 @@
         out_specs=WHOLE,
         out_shape=jax.ShapeDtypeStruct(spectrum, F32),
         scratch_shapes=[pltpu.VMEM((2 * chips, rows, lanes), BF16), pltpu.VMEM(spectrum, BF16)],
+        cost_estimate=CHEAP,
         compiler_params=pltpu.CompilerParams(vmem_limit_bytes=32 * 2**20),
         name="forward",
     )(cos, sin, table, own, other)
 
 
 def backward_kernel(chips, cos_ref, sin_ref, table_ref, spectrum_ref, *refs):
-    filter_refs, (keep_ref, send_ref, filter_ref, product_ref, back_ref) = refs[:chips], refs[chips:]
+    group_refs, (keep_ref, send_ref, filter_ref, product_ref, back_ref) = refs[: 2 * chips], refs[2 * chips :]
     chip, core = own_place()
     parts = 2 * chips
     rows, lanes = keep_ref.shape[1:]
     chip_bits = chips.bit_length() - 1
     chunk, width = 16, 128
-    for offset in range(chips):
-        filter_ref[chip ^ offset] = filter_refs[offset][...]
+    for odd in range(2):
+        for offset in range(chips):
+            filter_ref[chip ^ offset, odd] = group_refs[odd * chips + offset][pl.ds(1, 2)]
 
     for residue in range(parts):
         source, odd = bit_reversed(residue // 2, chip_bits), residue % 2
         columns = pl.ds(residue * lanes, lanes)
-        filter_real = filter_ref[source, odd].astype(F32)
-        filter_imag = filter_ref[source, 2 + odd].astype(F32)
+        filter_real = filter_ref[source, odd, 0].astype(F32)
+        filter_imag = filter_ref[source, odd, 1].astype(F32)
         real = spectrum_ref[pl.ds(0, rows), columns]
         imag = spectrum_ref[pl.ds(rows, rows), columns]
         product_ref[pl.ds(0, rows), columns] = (real * filter_real - imag * filter_imag).astype(BF16)
@@ -394,28 +376,29 @@
     lax.fori_loop(0, rows // chunk, gather, 0)
 
 
-def backward(spectrum, filters, tables):
-    chips = len(filters)
-    planes, rows, lanes = filters[0].shape
+def backward(spectrum, first, second, tables):
+    chips = len(first)
+    _, rows, lanes = first[0].shape
     _, table, cos, sin = tables
     kept = (chips, rows, lanes)
     return pl.pallas_call(
         functools.partial(backward_kernel, chips),
-        in_specs=[WHOLE] * (4 + chips),
+        in_specs=[WHOLE] * (4 + 2 * chips),
         out_specs=[WHOLE] * 2,
         out_shape=[jax.ShapeDtypeStruct(kept, F32), jax.ShapeDtypeStruct(kept, BF16)],
         scratch_shapes=[
-            pltpu.VMEM((chips, planes, rows, lanes), BF16),
+            pltpu.VMEM((chips, 2, 2, rows, lanes), BF16),
             pltpu.VMEM(spectrum.shape, BF16),
             pltpu.VMEM(spectrum.shape, F32),
         ],
+        cost_estimate=CHEAP,
         compiler_params=pltpu.CompilerParams(vmem_limit_bytes=32 * 2**20),
         name="backward",
-    )(cos, sin, table, spectrum, *filters)
+    )(cos, sin, table, spectrum, *first, *second)
 
 
 def gate_kernel(chips, skip_ref, keep_ref, arrived_ref, *refs):
-    signal_refs, out_ref = refs[:chips], refs[chips]
+    signal_refs, gate_refs, out_ref = refs[:chips], refs[chips : 2 * chips], refs[2 * chips]
     chip, _ = own_place()
     rows, lanes = keep_ref.shape[1:]
     pieces = out_ref.shape[0]
@@ -427,101 +410,129 @@
             here = pl.ds(piece * step, step)
             convolved = keep_ref[block, here, :] + arrived_ref[block, here, :].astype(F32)
             signal = signal_refs[offset][0, here, :].astype(F32)
-            gate = signal_refs[offset][1, here, :].astype(F32)
+            gate = gate_refs[offset][0, here, :].astype(F32)
             out_ref[piece, block_at(block, step), :] = (gate * (convolved + skip * signal)).astype(BF16)
 
 
-def gate(skip, keep, arrived, signals, pieces):
+def gate(skip, keep, arrived, first, second, pieces):
     chips, rows, lanes = keep.shape
     return pl.pallas_call(
         functools.partial(gate_kernel, chips),
-        in_specs=[WHOLE] * (3 + chips),
+        in_specs=[WHOLE] * (3 + 2 * chips),
         out_specs=WHOLE,
         out_shape=jax.ShapeDtypeStruct((pieces, chips * rows // pieces, lanes), BF16),
+        cost_estimate=CHEAP,
         compiler_params=pltpu.CompilerParams(vmem_limit_bytes=6 * 2**20),
         name="gate",
-    )(skip, keep, arrived, *signals)
-
-
-def arrange_kernel(layers, *refs):
-    own_refs, other_refs, out_ref = refs[:layers], refs[layers : 2 * layers], refs[2 * layers]
+    )(skip, keep, arrived, *first, *second)
+
+
+def collect_kernel(layers, *refs):
+    in_refs, out_ref = refs[:layers], refs[layers]
     device, layer = lax.axis_index("seq"), lax.axis_index("chan")
-    share = own_refs[0].shape[1]
     for step in range(layers):
-        target = device % layers ^ layer ^ step
-        out_ref[target, :, block_at(device % 2, share)] = own_refs[step][...]
-        out_ref[target, :, block_at(1 - device % 2, share)] = other_refs[step ^ 1][...]
+        out_ref[device % layers ^ layer ^ step] = in_refs[step][...]
+
+
+def collect(blocks):
+    layers = len(blocks)
+    return pl.pallas_call(
+        functools.partial(collect_kernel, layers),
+        in_specs=[WHOLE] * layers,
+        out_specs=WHOLE,
+        out_shape=jax.ShapeDtypeStruct((layers, *blocks[0].shape), BF16),
+        cost_estimate=CHEAP,
+        compiler_params=pltpu.CompilerParams(vmem_limit_bytes=4 * 2**20),
+        name="collect_weights",
+    )(*blocks)
+
+
+def arrange_kernel(own_ref, other_ref, out_ref):
+    _, core = own_place()
+    share = own_ref.shape[2]
+    out_ref[:, :, block_at(core, share)] = own_ref[...]
+    out_ref[:, :, block_at(1 - core, share)] = other_ref[...]
 
 
 def arrange(own, other):
-    layers = len(own)
-    rows, share = own[0].shape
-    return pl.pallas_call(
-        functools.partial(arrange_kernel, layers),
-        in_specs=[WHOLE] * (2 * layers),
+    layers, rows, share = own.shape
+    return pl.pallas_call(
+        arrange_kernel,
+        in_specs=[WHOLE] * 2,
         out_specs=WHOLE,
         out_shape=jax.ShapeDtypeStruct((layers, rows, 2 * share), BF16),
+        cost_estimate=CHEAP,
         compiler_params=pltpu.CompilerParams(vmem_limit_bytes=8 * 2**20),
         name="arrange_weights",
-    )(*own, *other)
+    )(own, other)
 
 
 def project_kernel(chips, piece, weight_ref, *refs):
-    gated_refs, (keep_ref, pass_ref, send_ref, joined_ref) = refs[:chips], refs[chips:]
+    gated_refs, out_refs, joined_ref = refs[:chips], refs[chips:-1], refs[-1]
     chip, _ = own_place()
     lanes = gated_refs[0].shape[2]
     for offset in range(chips):
         joined_ref[:, block_at(chip ^ offset, lanes)] = gated_refs[offset][piece]
-
-    def partial_of(target):
-        return jnp.dot(joined_ref[...], weight_ref[target], preferred_element_type=F32).astype(BF16)
-
-    send_ref[0] = partial_of(1)
-    send_ref[1] = partial_of(3)
-    pass_ref[...] = partial_of(2)
-    keep_ref[...] = partial_of(0)
-
-
-def project(weight, gated, piece):
+    order = (3, 2, 1, 0) if len(out_refs) == 4 else (1, 3, 2, 0)
+    for target in order:
+        partial = jnp.dot(joined_ref[...], weight_ref[target], preferred_element_type=F32).astype(BF16)
+        if len(out_refs) == 4:
+            out_refs[target][...] = partial
+        elif target % 2:
+            out_refs[2][target // 2] = partial
+        else:
+            out_refs[target // 2][...] = partial
+
+
+def project(weight, gated, piece, paired):
     chips = len(gated)
-    _, depth, columns = weight.shape
+    layers, depth, columns = weight.shape
     rows = gated[0].shape[1]
     block = jax.ShapeDtypeStruct((rows, columns), BF16)
+    pair = jax.ShapeDtypeStruct((2, rows, columns), BF16)
+    out_shape = [block, block, pair] if paired else [block] * layers
     return pl.pallas_call(
         functools.partial(project_kernel, chips, piece),
         in_specs=[WHOLE] * (1 + chips),
-        out_specs=[WHOLE] * 3,
-        out_shape=[block, block, jax.ShapeDtypeStruct((2, rows, columns), BF16)],
+        out_specs=[WHOLE] * len(out_shape),
+        out_shape=out_shape,
         scratch_shapes=[pltpu.VMEM((rows, depth), BF16)],
+        cost_estimate=CHEAP,
         compiler_params=pltpu.CompilerParams(vmem_limit_bytes=8 * 2**20),
         name="project",
     )(weight, *gated)
 
 
-def finish_kernel(chips, pieces, *refs):
-    keep_refs, first_refs, second_refs = refs[:pieces], refs[pieces : 2 * pieces], refs[2 * pieces : 3 * pieces]
-    out_refs = refs[3 * pieces :]
+def finish_kernel(chips, direct_refs, paired_refs, out_refs):
     chip, _ = own_place()
-    step = keep_refs[0].shape[0] // chips
+    step = direct_refs[0].shape[0] // chips
     for offset in range(chips):
         here = block_at(chip ^ offset, step)
-        for part in range(pieces):
-            total = keep_refs[part][here, :].astype(F32) + first_refs[part][0, here, :].astype(F32)
-            total = total + second_refs[part][here, :].astype(F32)
-            out_refs[offset][pl.ds(part * step, step), :] = total.astype(BF16)
-
-
-def finish(keep, first, second, chips):
-    pieces = len(keep)
-    rows, columns = keep[0].shape
-    return pl.pallas_call(
-        functools.partial(finish_kernel, chips, pieces),
-        in_specs=[WHOLE] * (3 * pieces),
+        total = direct_refs[0][here, :].astype(F32)
+        for part_ref in direct_refs[1:]:
+            total = total + part_ref[here, :].astype(F32)
+        out_refs[offset][pl.ds(0, step), :] = total.astype(BF16)
+        keep_ref, first_ref, second_ref = paired_refs
+        total = keep_ref[here, :].astype(F32) + first_ref[0, here, :].astype(F32) + second_ref[here, :].astype(F32)
+        out_refs[offset][pl.ds(step, step), :] = total.astype(BF16)
+
+
+def finish(direct, paired, chips):
+    rows, columns = direct[0].shape
+
+    def kernel(*refs):
+        ends = (len(direct), len(direct) + len(paired))
+        finish_kernel(chips, refs[: ends[0]], refs[ends[0] : ends[1]], refs[ends[1] :])
+
+    return pl.pallas_call(
+        kernel,
+        in_specs=[WHOLE] * (len(direct) + len(paired)),
         out_specs=[WHOLE] * chips,
-        out_shape=[jax.ShapeDtypeStruct((rows * pieces // chips, columns), BF16)] * chips,
+        out_shape=[jax.ShapeDtypeStruct((2 * rows // chips, columns), BF16)] * chips,
+        cost_estimate=CHEAP,
         compiler_params=pltpu.CompilerParams(vmem_limit_bytes=4 * 2**20),
         name="finish",
-    )(*keep, *first, *second)
+    )(*direct, *paired)
 
 
 def join_kernel(chips, *refs):
@@ -540,6 +551,7 @@
         in_specs=[WHOLE] * chips,
         out_specs=WHOLE,
         out_shape=jax.ShapeDtypeStruct((rows, chips * columns), BF16),
+        cost_estimate=CHEAP,
         compiler_params=pltpu.CompilerParams(vmem_limit_bytes=2 * 2**20),
         name="join",
     )(*blocks)
@@ -563,41 +575,36 @@
     parts = lax.axis_size("seq")
     layers = lax.axis_size("chan")
     chips = parts // 2
-    pieces = 2
     rows, width = values_in.shape
     device = lax.axis_index("seq")
     tables = small_tables(parts, rows)
 
-    signals = pack_signals(values_in, gate_values, chips)
-    filters = pack_filters(after(filter_spectrum.reshape(4, rows, width), signals[0]), chips)
-    signals = to_chips(signals)
-    own = jnp.stack([after(block, filters[0])[0] for block in signals])
-    filters = to_chips(filters)
+    flat_filters = filter_spectrum.reshape(4, rows, width)
+    first = pack(values_in, flat_filters, chips, (0, 2))
+    second = pack(after(gate_values, first[0]), flat_filters, chips, (1, 3))
+    first = to_chips(first)
+    own = jnp.stack([after(block, second[0])[0] for block in first])
+    second = to_chips(second)
     spectrum = forward(own, swapped(own, "seq", 1), tables)
-    keep, send = backward(spectrum, filters, tables)
-    gated = gate(skip_gain[None, :], keep, swapped(send, "seq", 1), signals, pieces)
+    keep, send = backward(spectrum, first, second, tables)
+    gated = gate(skip_gain[None, :], keep, swapped(send, "seq", 1), first, second, 2)
 
     share = out_weight.shape[1] // layers
-    sent = [
-        lax.dynamic_slice_in_dim(after(out_weight, own), (device // 2 ^ step) * share, share, 1)
-        for step in range(layers)
-    ]
     own_weight = []
-    for step, earlier in enumerate((spectrum, send, send, gated)):
+    for step, earlier in enumerate((spectrum, spectrum, send, send)):
+        sent = lax.dynamic_slice_in_dim(after(out_weight, second[0]), (device // 2 ^ step) * share, share, 1)
         pairs = [(source, source % 2 * layers + (source // 2 ^ step)) for source in range(parts)]
-        own_weight.append(lax.ppermute(after(sent[step], earlier), "seq", pairs))
-    weight = arrange(own_weight, [swapped(after(block, gated), "seq", 1) for block in own_weight])
+        own_weight.append(lax.ppermute(after(sent, earlier), "seq", pairs))
+    own_weight = collect([after(block, gated) for block in own_weight])
+    weight = arrange(own_weight, swapped(own_weight, "seq", 1))
 
     gathered = to_chips([gated] * chips)
-    kept, firsts, seconds = [], [], []
-    for piece in range(pieces):
-        keep, passed, send = project(weight, gathered, piece)
-        first = swapped(send, "chan", 1)
-        passed = (passed.astype(F32) + first[1].astype(F32)).astype(BF16)
-        kept.append(keep)
-        firsts.append(first)
-        seconds.append(swapped(passed, "chan", 2))
-    return join(to_chips(finish(kept, firsts, seconds, chips)))
+    partials = project(weight, gathered, 0, False)
+    direct = [swapped(block, "chan", offset) for offset, block in enumerate(partials)]
+    keep, passed, send = project(weight, gathered, 1, True)
+    arrived = swapped(send, "chan", 1)
+    passed = after((passed.astype(F32) + arrived[1].astype(F32)).astype(BF16), *direct)
+    return join(to_chips(finish(direct, (keep, arrived, swapped(passed, "chan", 2)), chips)))
 
 
 def shards(values_in, gate_values, filter_spectrum, skip_gain, out_weight):

time: 94.2 us -> 97.5 us (1.035)
  waiting for transfers between devices: 46.2 us -> 56.9 us
  starting transfers between devices: 36.6 us -> 28.8 us
  Pallas kernels: 7.12 us -> 9.84 us
  local copies, waits for them, and re-layouts: 3.78 us -> 1.37 us
    ppermute x4, waiting for transfers between devices: 2.35 us -> 10.9 us  [shards_direct(): own_weight.append(lax.ppermute(after(sent, earlier), 'seq', pairs))]
    ppermute x22 -> x20, starting transfers between devices: 29.2 us -> 23.2 us  [swapped(): lax.ppermute(value, axis, [(source, source ^ offset) for source in range(...]
    unnamed x18 -> x10, local copies, waits for them, and re-layouts: 3.56 us -> 0.03 us
    pallas_call x4 -> x5, Pallas kernels: 1.22 us -> 3.79 us  [the longest x2 3.04 us: pack(): pl.pallas_call(functools.partial(pack_kernel, chips, planes), in_specs=[p...]
    ppermute x22 -> x20, waiting for transfers between devices: 43.9 us -> 46 us  [swapped(): lax.ppermute(value, axis, [(source, source ^ offset) for source in range(...]
    ppermute x4, starting transfers between devices: 7.41 us -> 5.66 us  [shards_direct(): own_weight.append(lax.ppermute(after(sent, earlier), 'seq', pairs))]
    dynamic_slice x1, local copies, waits for them, and re-layouts: 0.19 us -> 1.32 us  [shards_direct(): lax.dynamic_slice_in_dim(after(out_weight, second[0]), (device // 2 ^ ste...]
  transfers between devices with their start and end apart: 26 -> 24, of which waited for: 15 -> 17; matrix products, arithmetic and copies ran while one was open for 0% -> 1% of each run, Pallas kernels for 4% -> 5%
where the time goes in v6:
time: 97.5 us; the launch traced here: 97.3 us
  waiting for transfers between devices  56.9 us (58%)
  starting transfers between devices  28.8 us (30%)
  Pallas kernels  9.84 us (10%)
  local copies, waits for them, and re-layouts  1.37 us (1%)
    ppermute x20, waiting for transfers between devices, swapped(): lax.ppermute(value, axis, [(source, source ^ offset) for source in range(...  46 us
    ppermute x20, starting transfers between devices, swapped(): lax.ppermute(value, axis, [(source, source ^ offset) for source in range(...  23.2 us
    ppermute x4, waiting for transfers between devices, shards_direct(): own_weight.append(lax.ppermute(after(sent, earlier), 'seq', pairs))  10.9 us
    ppermute x4, starting transfers between devices, shards_direct(): own_weight.append(lax.ppermute(after(sent, earlier), 'seq', pairs))  5.66 us
    pallas_call x2, Pallas kernels, pack(): pl.pallas_call(functools.partial(pack_kernel, chips, planes), in_specs=[p...  3.04 us
    pallas_call x1, Pallas kernels, backward(): pl.pallas_call(functools.partial(backward_kernel, chips), in_specs=[WHOLE...  2.1 us
  transfers between devices with their start and end apart: 24, of which 17 were waited for; matrix products, arithmetic and copies ran while one was open for 1% of the time, Pallas kernels for 5%

profile of v6, /device:TPU:0, one launch (start us, length us, event | category | flops | bytes accessed | tf_op | source)
XLA Modules:
  0.0 97.3 jit_solution(654400632761386352)
XLA Ops:
  0.0 1.5 %pack.2 = (bf16[3,128,256]{2,1,0:T(8,128)(2,1)S(1)}, bf16[3,128,256]{2,1,0:T(8,128)(2,1)S(1)}, bf16[3,128,256]{2,1,0:T(8,128)(2,1)S(1)}, bf16[3,128,256]{2,1,0:T(8,128)(2,1)S(1)}) custom-call(bf16[128,1024]{1,0:T(8,128)(2,1)} %signal_ref.1, f32[4,128,1024]{2,1,0:T(8,128)} %bitcast.8), custom_call_target="tpu_custom_call" | custom-call | tf_op jit(solution)/shard_map/pack/pallas_call | solution.py:244
  1.5 4.0 %collective-permute-start.2 = (bf16[3,128,256]{2,1,0:T(8,128)(2,1)S(1)}, bf16[3,128,256]{2,1,0:T(8,128)(2,1)S(1)}, u32[]{:S(2)}, u32[]{:S(2)}) collective-permute-start(bf16[3,128,256]{2,1,0:T(8,128)(2,1)S(1)} %get-tuple-element.50), channel_id=1, source_target_pairs={{0,24},{4,28},{8,16},{12,20},{16,8},{20,12},{24,0},{28,4},{1,25},{... | collective-permute-start | bytes 589832 | tf_op jit(solution)/shard_map/ppermute | solution.py:563
  6.1 1.5 %pack.3 = (bf16[3,128,256]{2,1,0:T(8,128)(2,1)S(1)}, bf16[3,128,256]{2,1,0:T(8,128)(2,1)S(1)}, bf16[3,128,256]{2,1,0:T(8,128)(2,1)S(1)}, bf16[3,128,256]{2,1,0:T(8,128)(2,1)S(1)}) custom-call(bf16[128,1024]{1,0:T(8,128)(2,1)} %signal_ref.2, f32[4,128,1024]{2,1,0:T(8,128)} %bitcast.9), custom_call_target="tpu_custom_call" | custom-call | tf_op jit(solution)/shard_map/pack/pallas_call | solution.py:244
  7.7 3.6 %collective-permute-done.2.refs_3_ = bf16[3,128,256]{2,1,0:T(8,128)(2,1)S(1)} collective-permute-done((bf16[3,128,256]{2,1,0:T(8,128)(2,1)S(1)}, bf16[3,128,256]{2,1,0:T(8,128)(2,1)S(1)}, u32[]{:S(2)}, u32[]{:S(2)}) %collective-permute-start.2) | collective-permute-done | bytes 196640 | tf_op jit(solution)/shard_map/ppermute | solution.py:563
  11.3 3.3 %collective-permute-done.1.refs_2_ = bf16[3,128,256]{2,1,0:T(8,128)(2,1)S(1)} collective-permute-done((bf16[3,128,256]{2,1,0:T(8,128)(2,1)S(1)}, bf16[3,128,256]{2,1,0:T(8,128)(2,1)S(1)}, u32[]{:S(2)}, u32[]{:S(2)}) %collective-permute-start.1) | collective-permute-done | bytes 196640 | tf_op jit(solution)/shard_map/ppermute | solution.py:563
  15.0 1.6 %collective-permute-start.5 = (bf16[3,128,256]{2,1,0:T(8,128)(2,1)S(1)}, bf16[3,128,256]{2,1,0:T(8,128)(2,1)S(1)}, u32[]{:S(2)}, u32[]{:S(2)}) collective-permute-start(bf16[3,128,256]{2,1,0:T(8,128)(2,1)S(1)} %get-tuple-element.53), channel_id=1, source_target_pairs={{0,8},{4,12},{8,0},{12,4},{16,24},{20,28},{24,16},{28,20},{1,9},{5... | collective-permute-start | bytes 589832 | tf_op jit(solution)/shard_map/ppermute | solution.py:563
  20.0 1.5 %forward.1.spectrum_ref = f32[256,2048]{1,0:T(8,128)S(1)} custom-call(f32[2,128,8]{2,1,0:T(8,128)S(1)} %copy-done.1, f32[2,128,8]{2,1,0:T(8,128)S(1)} %copy-done, bf16[256,256]{1,0:T(8,128)(2,1)S(1)} %copy-done.3, bf16[4,128,256]{2,1,0:T(8,128)(2,1)S(1)} %pad_maximum_fusion.own_ref, bf16[4,128,256]{2,1,0:T(8,128)(2,1)S(1)} %collective-permute-done.3.other_ref), custom_call_target="tpu_custom_call" | custom-call | tf_op jit(solution)/shard_map/forward/pallas_call | solution.py:309
  22.8 5.0 %collective-permute-done.6.refs_6_ = bf16[3,128,256]{2,1,0:T(8,128)(2,1)S(1)} collective-permute-done((bf16[3,128,256]{2,1,0:T(8,128)(2,1)S(1)}, bf16[3,128,256]{2,1,0:T(8,128)(2,1)S(1)}, u32[]{:S(2)}, u32[]{:S(2)}) %collective-permute-start.6) | collective-permute-done | bytes 196640 | tf_op jit(solution)/shard_map/ppermute | solution.py:563
  27.8 2.1 %backward.1 = (f32[4,128,256]{2,1,0:T(8,128)S(1)}, bf16[4,128,256]{2,1,0:T(8,128)(2,1)S(1)}) custom-call(f32[2,128,8]{2,1,0:T(8,128)S(1)} %copy-done.1, f32[2,128,8]{2,1,0:T(8,128)S(1)} %copy-done, bf16[256,256]{1,0:T(8,128)(2,1)S(1)} %copy-done.2, f32[256,2048]{1,0:T(8,128)S(1)} %forward.1.spectrum_ref, bf16[3,128,256]{2,1,0:T(8,128)(2,1)S(1)} %get-tuple-element.45.refs_0_, ...), custom_call_target="tpu_custom_call" | custom-call | tf_op jit(solution)/shard_map/backward/pallas_call | solution.py:384
  30.0 2.5 %collective-permute-start.11 = (bf16[1024,128]{1,0:T(8,128)(2,1)S(1)}, bf16[1024,128]{1,0:T(8,128)(2,1)S(1)}, u32[]{:S(2)}, u32[]{:S(2)}) collective-permute-start(bf16[1024,128]{1,0:T(8,128)(2,1)S(1)} %get-tuple-element.63), channel_id=1, source_target_pairs={{0,12},{4,28},{8,8},{12,24},{16,4},{20,20},{24,0},{28,16},{1,13},{... | collective-permute-start | bytes 786440 | tf_op jit(solution)/shard_map/ppermute | solution.py:597
  32.6 2.4 %collective-permute-start.9 = (bf16[1024,128]{1,0:T(8,128)(2,1)S(1)}, bf16[1024,128]{1,0:T(8,128)(2,1)S(1)}, u32[]{:S(2)}, u32[]{:S(2)}) collective-permute-start(bf16[1024,128]{1,0:T(8,128)(2,1)S(1)} %get-tuple-element.59), channel_id=1, source_target_pairs={{0,4},{4,20},{8,0},{12,16},{16,12},{20,28},{24,8},{28,24},{1,5},{5... | collective-permute-start | bytes 786440 | tf_op jit(solution)/shard_map/ppermute | solution.py:597
  35.9 6.1 %collective-permute-done.11.refs_3_ = bf16[1024,128]{1,0:T(8,128)(2,1)S(1)} collective-permute-done((bf16[1024,128]{1,0:T(8,128)(2,1)S(1)}, bf16[1024,128]{1,0:T(8,128)(2,1)S(1)}, u32[]{:S(2)}, u32[]{:S(2)}) %collective-permute-start.11) | collective-permute-done | bytes 262176 | tf_op jit(solution)/shard_map/ppermute | solution.py:597
  42.0 4.8 %collective-permute-done.10.refs_2_ = bf16[1024,128]{1,0:T(8,128)(2,1)S(1)} collective-permute-done((bf16[1024,128]{1,0:T(8,128)(2,1)S(1)}, bf16[1024,128]{1,0:T(8,128)(2,1)S(1)}, u32[]{:S(2)}, u32[]{:S(2)}) %collective-permute-start.10) | collective-permute-done | bytes 262176 | tf_op jit(solution)/shard_map/ppermute | solution.py:597
  46.9 1.7 %collective-permute-start.15 = (bf16[2,256,256]{2,1,0:T(8,128)(2,1)S(1)}, bf16[2,256,256]{2,1,0:T(8,128)(2,1)S(1)}, u32[]{:S(2)}, u32[]{:S(2)}) collective-permute-start(bf16[2,256,256]{2,1,0:T(8,128)(2,1)S(1)} %gate.1.refs_0_), channel_id=1, source_target_pairs={{0,24},{4,28},{8,16},{12,20},{16,8},{20,12},{24,0},{28,4},{1,25},{... | collective-permute-start | bytes 786440 | tf_op jit(solution)/shard_map/ppermute | solution.py:563
  48.7 2.2 %collective-permute-start.14 = (bf16[2,256,256]{2,1,0:T(8,128)(2,1)S(1)}, bf16[2,256,256]{2,1,0:T(8,128)(2,1)S(1)}, u32[]{:S(2)}, u32[]{:S(2)}) collective-permute-start(bf16[2,256,256]{2,1,0:T(8,128)(2,1)S(1)} %gate.1.refs_0_), channel_id=1, source_target_pairs={{0,16},{4,20},{8,24},{12,28},{16,0},{20,4},{24,8},{28,12},{1,17},{... | collective-permute-start | bytes 786440 | tf_op jit(solution)/shard_map/ppermute | solution.py:563
  51.4 5.6 %collective-permute-done.15.refs_3_ = bf16[2,256,256]{2,1,0:T(8,128)(2,1)S(1)} collective-permute-done((bf16[2,256,256]{2,1,0:T(8,128)(2,1)S(1)}, bf16[2,256,256]{2,1,0:T(8,128)(2,1)S(1)}, u32[]{:S(2)}, u32[]{:S(2)}) %collective-permute-start.15) | collective-permute-done | bytes 262176 | tf_op jit(solution)/shard_map/ppermute | solution.py:563
  57.1 5.1 %collective-permute-done.14.refs_2_ = bf16[2,256,256]{2,1,0:T(8,128)(2,1)S(1)} collective-permute-done((bf16[2,256,256]{2,1,0:T(8,128)(2,1)S(1)}, bf16[2,256,256]{2,1,0:T(8,128)(2,1)S(1)}, u32[]{:S(2)}, u32[]{:S(2)}) %collective-permute-start.14) | collective-permute-done | bytes 262176 | tf_op jit(solution)/shard_map/ppermute | solution.py:563
  63.9 1.6 %collective-permute-start.19 = (bf16[2,256,256]{2,1,0:T(8,128)(2,1)S(1)}, bf16[2,256,256]{2,1,0:T(8,128)(2,1)S(1)}, u32[]{:S(2)}, u32[]{:S(2)}) collective-permute-start(bf16[2,256,256]{2,1,0:T(8,128)(2,1)S(1)} %get-tuple-element.70), channel_id=1, source_target_pairs={{0,1},{1,0},{2,3},{3,2},{4,5},{5,4},{6,7},{7,6},{8,9},{9,8},{10,11... | collective-permute-start | bytes 786440 | tf_op jit(solution)/shard_map/ppermute | solution.py:563
  66.8 2.6 %collective-permute-start.17 = (bf16[256,256]{1,0:T(8,128)(2,1)S(1)}, bf16[256,256]{1,0:T(8,128)(2,1)S(1)}, u32[]{:S(2)}, u32[]{:S(2)}) collective-permute-start(bf16[256,256]{1,0:T(8,128)(2,1)S(1)} %get-tuple-element.67), channel_id=1, source_target_pairs={{0,2},{1,3},{2,0},{3,1},{4,6},{5,7},{6,4},{7,5},{8,10},{9,11},{10,... | collective-permute-start | bytes 393224 | tf_op jit(solution)/shard_map/ppermute | solution.py:563
  70.8 5.2 %collective-permute-done.19.refs_5_ = bf16[2,256,256]{2,1,0:T(8,128)(2,1)S(1)} collective-permute-done((bf16[2,256,256]{2,1,0:T(8,128)(2,1)S(1)}, bf16[2,256,256]{2,1,0:T(8,128)(2,1)S(1)}, u32[]{:S(2)}, u32[]{:S(2)}) %collective-permute-start.19) | collective-permute-done | bytes 262176 | tf_op jit(solution)/shard_map/ppermute | solution.py:563
  77.9 4.3 %collective-permute-done.18.refs_3_ = bf16[256,256]{1,0:T(8,128)(2,1)S(1)} collective-permute-done((bf16[256,256]{1,0:T(8,128)(2,1)S(1)}, bf16[256,256]{1,0:T(8,128)(2,1)S(1)}, u32[]{:S(2)}, u32[]{:S(2)}) %collective-permute-start.18) | collective-permute-done | bytes 131104 | tf_op jit(solution)/shard_map/ppermute | solution.py:563
  83.4 5.5 %collective-permute-done.20.refs_6_ = bf16[256,256]{1,0:T(8,128)(2,1)S(1)} collective-permute-done((bf16[256,256]{1,0:T(8,128)(2,1)S(1)}, bf16[256,256]{1,0:T(8,128)(2,1)S(1)}, u32[]{:S(2)}, u32[]{:S(2)}) %collective-permute-start.20) | collective-permute-done | bytes 131104 | tf_op jit(solution)/shard_map/ppermute | solution.py:563
  89.0 2.0 %collective-permute-start.21 = (bf16[128,256]{1,0:T(8,128)(2,1)S(1)}, bf16[128,256]{1,0:T(8,128)(2,1)S(1)}, u32[]{:S(2)}, u32[]{:S(2)}) collective-permute-start(bf16[128,256]{1,0:T(8,128)(2,1)S(1)} %get-tuple-element.74), channel_id=1, source_target_pairs={{0,8},{4,12},{8,0},{12,4},{16,24},{20,28},{24,16},{28,20},{1,9},{5... | collective-permute-start | bytes 196616 | tf_op jit(solution)/shard_map/ppermute | solution.py:563
  93.4 3.2 %collective-permute-done.22.refs_2_ = bf16[128,256]{1,0:T(8,128)(2,1)S(1)} collective-permute-done((bf16[128,256]{1,0:T(8,128)(2,1)S(1)}, bf16[128,256]{1,0:T(8,128)(2,1)S(1)}, u32[]{:S(2)}, u32[]{:S(2)}) %collective-permute-start.22) | collective-permute-done | bytes 65568 | tf_op jit(solution)/shard_map/ppermute | solution.py:563
  (52 shorter events, 18.1 us)
Async XLA Ops:
  1.5 9.7 %collective-permute-start.2 = (bf16[3,128,256]{2,1,0:T(8,128)(2,1)S(1)}, bf16[3,128,256]{2,1,0:T(8,128)(2,1)S(1)}, u32[]{:S(2)}, u32[]{:S(2)}) collective-permute-start(bf16[3,128,256]{2,1,0:T(8,128)(2,1)S(1)} %get-tuple-element.50), channel_id=1, source_target_pairs={{0,24},{4,28},{8,16},{12,20},{16,8},{20,12},{24,0},{28,4},{1,25},{... | collective-permute-start | bytes 589832 | tf_op jit(solution)/shard_map/ppermute | solution.py:563
  5.5 9.1 %collective-permute-start.1 = (bf16[3,128,256]{2,1,0:T(8,128)(2,1)S(1)}, bf16[3,128,256]{2,1,0:T(8,128)(2,1)S(1)}, u32[]{:S(2)}, u32[]{:S(2)}) collective-permute-start(bf16[3,128,256]{2,1,0:T(8,128)(2,1)S(1)} %get-tuple-element.48), channel_id=1, source_target_pairs={{0,16},{4,20},{8,24},{12,28},{16,0},{20,4},{24,8},{28,12},{1,17},{... | collective-permute-start | bytes 589832 | tf_op jit(solution)/shard_map/ppermute | solution.py:563
  6.0 8.9 %collective-permute-start = (bf16[3,128,256]{2,1,0:T(8,128)(2,1)S(1)}, bf16[3,128,256]{2,1,0:T(8,128)(2,1)S(1)}, u32[]{:S(2)}, u32[]{:S(2)}) collective-permute-start(bf16[3,128,256]{2,1,0:T(8,128)(2,1)S(1)} %get-tuple-element.46), channel_id=1, source_target_pairs={{0,8},{4,12},{8,0},{12,4},{16,24},{20,28},{24,16},{28,20},{1,9},{5... | collective-permute-start | bytes 589832 | tf_op jit(solution)/shard_map/ppermute | solution.py:563
  15.0 5.0 %collective-permute-start.3 = (bf16[4,128,256]{2,1,0:T(8,128)(2,1)S(1)}, bf16[4,128,256]{2,1,0:T(8,128)(2,1)S(1)}, u32[]{:S(2)}, u32[]{:S(2)}) collective-permute-start(bf16[4,128,256]{2,1,0:T(8,128)(2,1)S(1)} %pad_maximum_fusion.own_ref), channel_id=1, source_target_pairs={{0,4},{4,0},{8,12},{12,8},{16,20},{20,16},{24,28},{28,24},{1,5},{5... | collective-permute-start | bytes 786440 | tf_op jit(solution)/shard_map/ppermute | solution.py:563
  15.0 7.8 %collective-permute-start.5 = (bf16[3,128,256]{2,1,0:T(8,128)(2,1)S(1)}, bf16[3,128,256]{2,1,0:T(8,128)(2,1)S(1)}, u32[]{:S(2)}, u32[]{:S(2)}) collective-permute-start(bf16[3,128,256]{2,1,0:T(8,128)(2,1)S(1)} %get-tuple-element.53), channel_id=1, source_target_pairs={{0,8},{4,12},{8,0},{12,4},{16,24},{20,28},{24,16},{28,20},{1,9},{5... | collective-permute-start | bytes 589832 | tf_op jit(solution)/shard_map/ppermute | solution.py:563
  16.6 11.2 %collective-permute-start.6 = (bf16[3,128,256]{2,1,0:T(8,128)(2,1)S(1)}, bf16[3,128,256]{2,1,0:T(8,128)(2,1)S(1)}, u32[]{:S(2)}, u32[]{:S(2)}) collective-permute-start(bf16[3,128,256]{2,1,0:T(8,128)(2,1)S(1)} %get-tuple-element.54), channel_id=1, source_target_pairs={{0,16},{4,20},{8,24},{12,28},{16,0},{20,4},{24,8},{28,12},{1,17},{... | collective-permute-start | bytes 589832 | tf_op jit(solution)/shard_map/ppermute | solution.py:563
  17.2 10.6 %collective-permute-start.7 = (bf16[3,128,256]{2,1,0:T(8,128)(2,1)S(1)}, bf16[3,128,256]{2,1,0:T(8,128)(2,1)S(1)}, u32[]{:S(2)}, u32[]{:S(2)}) collective-permute-start(bf16[3,128,256]{2,1,0:T(8,128)(2,1)S(1)} %get-tuple-element.55), channel_id=1, source_target_pairs={{0,24},{4,28},{8,16},{12,20},{16,8},{20,12},{24,0},{28,4},{1,25},{... | collective-permute-start | bytes 589832 | tf_op jit(solution)/shard_map/ppermute | solution.py:563
  29.9 5.8 %collective-permute-start.8 = (bf16[4,128,256]{2,1,0:T(8,128)(2,1)S(1)}, bf16[4,128,256]{2,1,0:T(8,128)(2,1)S(1)}, u32[]{:S(2)}, u32[]{:S(2)}) collective-permute-start(bf16[4,128,256]{2,1,0:T(8,128)(2,1)S(1)} %get-tuple-element.57), channel_id=1, source_target_pairs={{0,4},{4,0},{8,12},{12,8},{16,20},{20,16},{24,28},{28,24},{1,5},{5... | collective-permute-start | bytes 786440 | tf_op jit(solution)/shard_map/ppermute | solution.py:563
  30.0 12.0 %collective-permute-start.11 = (bf16[1024,128]{1,0:T(8,128)(2,1)S(1)}, bf16[1024,128]{1,0:T(8,128)(2,1)S(1)}, u32[]{:S(2)}, u32[]{:S(2)}) collective-permute-start(bf16[1024,128]{1,0:T(8,128)(2,1)S(1)} %get-tuple-element.63), channel_id=1, source_target_pairs={{0,12},{4,28},{8,8},{12,24},{16,4},{20,20},{24,0},{28,16},{1,13},{... | collective-permute-start | bytes 786440 | tf_op jit(solution)/shard_map/ppermute | solution.py:597
  32.5 14.2 %collective-permute-start.10 = (bf16[1024,128]{1,0:T(8,128)(2,1)S(1)}, bf16[1024,128]{1,0:T(8,128)(2,1)S(1)}, u32[]{:S(2)}, u32[]{:S(2)}) collective-permute-start(bf16[1024,128]{1,0:T(8,128)(2,1)S(1)} %get-tuple-element.61), channel_id=1, source_target_pairs={{0,8},{4,24},{8,12},{12,28},{16,0},{20,16},{24,4},{28,20},{1,9},{5... | collective-permute-start | bytes 786440 | tf_op jit(solution)/shard_map/ppermute | solution.py:597
  32.6 14.2 %collective-permute-start.9 = (bf16[1024,128]{1,0:T(8,128)(2,1)S(1)}, bf16[1024,128]{1,0:T(8,128)(2,1)S(1)}, u32[]{:S(2)}, u32[]{:S(2)}) collective-permute-start(bf16[1024,128]{1,0:T(8,128)(2,1)S(1)} %get-tuple-element.59), channel_id=1, source_target_pairs={{0,4},{4,20},{8,0},{12,16},{16,12},{20,28},{24,8},{28,24},{1,5},{5... | collective-permute-start | bytes 786440 | tf_op jit(solution)/shard_map/ppermute | solution.py:597
  35.0 11.8 %collective-permute-start.4 = (bf16[1024,128]{1,0:T(8,128)(2,1)S(1)}, bf16[1024,128]{1,0:T(8,128)(2,1)S(1)}, u32[]{:S(2)}, u32[]{:S(2)}) collective-permute-start(bf16[1024,128]{1,0:T(8,128)(2,1)S(1)} %get-tuple-element.52), channel_id=1, source_target_pairs={{0,0},{4,16},{8,4},{12,20},{16,8},{20,24},{24,12},{28,28},{1,1},{5... | collective-permute-start | bytes 786440 | tf_op jit(solution)/shard_map/ppermute | solution.py:597
  46.9 4.0 %collective-permute-start.12 = (bf16[4,1024,128]{2,1,0:T(8,128)(2,1)S(1)}, bf16[4,1024,128]{2,1,0:T(8,128)(2,1)S(1)}, u32[]{:S(2)}, u32[]{:S(2)}) collective-permute-start(bf16[4,1024,128]{2,1,0:T(8,128)(2,1)S(1)} %collect_weights.1.own_ref), channel_id=1, source_target_pairs={{0,4},{4,0},{8,12},{12,8},{16,20},{20,16},{24,28},{28,24},{1,5},{5... | collective-permute-start | bytes 3145736 | tf_op jit(solution)/shard_map/ppermute | solution.py:563
  46.9 10.1 %collective-permute-start.15 = (bf16[2,256,256]{2,1,0:T(8,128)(2,1)S(1)}, bf16[2,256,256]{2,1,0:T(8,128)(2,1)S(1)}, u32[]{:S(2)}, u32[]{:S(2)}) collective-permute-start(bf16[2,256,256]{2,1,0:T(8,128)(2,1)S(1)} %gate.1.refs_0_), channel_id=1, source_target_pairs={{0,24},{4,28},{8,16},{12,20},{16,8},{20,12},{24,0},{28,4},{1,25},{... | collective-permute-start | bytes 786440 | tf_op jit(solution)/shard_map/ppermute | solution.py:563
  48.7 13.5 %collective-permute-start.14 = (bf16[2,256,256]{2,1,0:T(8,128)(2,1)S(1)}, bf16[2,256,256]{2,1,0:T(8,128)(2,1)S(1)}, u32[]{:S(2)}, u32[]{:S(2)}) collective-permute-start(bf16[2,256,256]{2,1,0:T(8,128)(2,1)S(1)} %gate.1.refs_0_), channel_id=1, source_target_pairs={{0,16},{4,20},{8,24},{12,28},{16,0},{20,4},{24,8},{28,12},{1,17},{... | collective-permute-start | bytes 786440 | tf_op jit(solution)/shard_map/ppermute | solution.py:563
  50.9 12.2 %collective-permute-start.13 = (bf16[2,256,256]{2,1,0:T(8,128)(2,1)S(1)}, bf16[2,256,256]{2,1,0:T(8,128)(2,1)S(1)}, u32[]{:S(2)}, u32[]{:S(2)}) collective-permute-start(bf16[2,256,256]{2,1,0:T(8,128)(2,1)S(1)} %gate.1.refs_0_), channel_id=1, source_target_pairs={{0,8},{4,12},{8,0},{12,4},{16,24},{20,28},{24,16},{28,20},{1,9},{5... | collective-permute-start | bytes 786440 | tf_op jit(solution)/shard_map/ppermute | solution.py:563
  63.9 12.1 %collective-permute-start.19 = (bf16[2,256,256]{2,1,0:T(8,128)(2,1)S(1)}, bf16[2,256,256]{2,1,0:T(8,128)(2,1)S(1)}, u32[]{:S(2)}, u32[]{:S(2)}) collective-permute-start(bf16[2,256,256]{2,1,0:T(8,128)(2,1)S(1)} %get-tuple-element.70), channel_id=1, source_target_pairs={{0,1},{1,0},{2,3},{3,2},{4,5},{5,4},{6,7},{7,6},{8,9},{9,8},{10,11... | collective-permute-start | bytes 786440 | tf_op jit(solution)/shard_map/ppermute | solution.py:563
  66.3 11.1 %collective-permute-start.16 = (bf16[256,256]{1,0:T(8,128)(2,1)S(1)}, bf16[256,256]{1,0:T(8,128)(2,1)S(1)}, u32[]{:S(2)}, u32[]{:S(2)}) collective-permute-start(bf16[256,256]{1,0:T(8,128)(2,1)S(1)} %get-tuple-element.66), channel_id=1, source_target_pairs={{0,1},{1,0},{2,3},{3,2},{4,5},{5,4},{6,7},{7,6},{8,9},{9,8},{10,11... | collective-permute-start | bytes 393224 | tf_op jit(solution)/shard_map/ppermute | solution.py:563
  66.8 11.1 %collective-permute-start.17 = (bf16[256,256]{1,0:T(8,128)(2,1)S(1)}, bf16[256,256]{1,0:T(8,128)(2,1)S(1)}, u32[]{:S(2)}, u32[]{:S(2)}) collective-permute-start(bf16[256,256]{1,0:T(8,128)(2,1)S(1)} %get-tuple-element.67), channel_id=1, source_target_pairs={{0,2},{1,3},{2,0},{3,1},{4,6},{5,7},{6,4},{7,5},{8,10},{9,11},{10,... | collective-permute-start | bytes 393224 | tf_op jit(solution)/shard_map/ppermute | solution.py:563
  69.4 12.9 %collective-permute-start.18 = (bf16[256,256]{1,0:T(8,128)(2,1)S(1)}, bf16[256,256]{1,0:T(8,128)(2,1)S(1)}, u32[]{:S(2)}, u32[]{:S(2)}) collective-permute-start(bf16[256,256]{1,0:T(8,128)(2,1)S(1)} %get-tuple-element.68), channel_id=1, source_target_pairs={{0,3},{1,2},{2,1},{3,0},{4,7},{5,6},{6,5},{7,4},{8,11},{9,10},{10,... | collective-permute-start | bytes 393224 | tf_op jit(solution)/shard_map/ppermute | solution.py:563
  82.3 6.6 %collective-permute-start.20 = (bf16[256,256]{1,0:T(8,128)(2,1)S(1)}, bf16[256,256]{1,0:T(8,128)(2,1)S(1)}, u32[]{:S(2)}, u32[]{:S(2)}) collective-permute-start(bf16[256,256]{1,0:T(8,128)(2,1)S(1)} %fusion), channel_id=1, source_target_pairs={{0,2},{1,3},{2,0},{3,1},{4,6},{5,7},{6,4},{7,5},{8,10},{9,11},{10,... | collective-permute-start | bytes 393224 | tf_op jit(solution)/shard_map/ppermute | solution.py:563
  89.0 4.3 %collective-permute-start.21 = (bf16[128,256]{1,0:T(8,128)(2,1)S(1)}, bf16[128,256]{1,0:T(8,128)(2,1)S(1)}, u32[]{:S(2)}, u32[]{:S(2)}) collective-permute-start(bf16[128,256]{1,0:T(8,128)(2,1)S(1)} %get-tuple-element.74), channel_id=1, source_target_pairs={{0,8},{4,12},{8,0},{12,4},{16,24},{20,28},{24,16},{28,20},{1,9},{5... | collective-permute-start | bytes 196616 | tf_op jit(solution)/shard_map/ppermute | solution.py:563
  91.0 5.5 %collective-permute-start.22 = (bf16[128,256]{1,0:T(8,128)(2,1)S(1)}, bf16[128,256]{1,0:T(8,128)(2,1)S(1)}, u32[]{:S(2)}, u32[]{:S(2)}) collective-permute-start(bf16[128,256]{1,0:T(8,128)(2,1)S(1)} %get-tuple-element.75), channel_id=1, source_target_pairs={{0,16},{4,20},{8,24},{12,28},{16,0},{20,4},{24,8},{28,12},{1,17},{... | collective-permute-start | bytes 196616 | tf_op jit(solution)/shard_map/ppermute | solution.py:563
  91.3 5.2 %collective-permute-start.23 = (bf16[128,256]{1,0:T(8,128)(2,1)S(1)}, bf16[128,256]{1,0:T(8,128)(2,1)S(1)}, u32[]{:S(2)}, u32[]{:S(2)}) collective-permute-start(bf16[128,256]{1,0:T(8,128)(2,1)S(1)} %get-tuple-element.76), channel_id=1, source_target_pairs={{0,24},{4,28},{8,16},{12,20},{16,8},{20,12},{24,0},{28,4},{1,25},{... | collective-permute-start | bytes 196616 | tf_op jit(solution)/shard_map/ppermute | solution.py:563
  (5 other events, 60.3 us)

commit v7 on v6

--- a/solution.py
+++ b/solution.py
@@ -213,47 +213,94 @@
     return pl.ds(pl.multiple_of(index * size, size), size)
 
 
-def pack_kernel(chips, planes, signal_ref, filter_ref, *refs):
+def pack_signals_kernel(chips, values_ref, filter_ref, *refs):
     out_refs, (plane_ref, arrived) = refs[:chips], refs[chips:]
     chip, _ = own_place()
+    planes, rows, _ = filter_ref.shape
     lanes = out_refs[0].shape[2]
     copies = []
     for offset in reversed(range(chips)):
         here = block_at(chip ^ offset, lanes)
-        for place, plane in enumerate(planes):
+        for plane in range(planes):
             copies.append(
-                pltpu.make_async_copy(
-                    filter_ref.at[plane, :, here], plane_ref.at[offset, place], arrived.at[offset, 1 + place]
-                )
+                pltpu.make_async_copy(filter_ref.at[plane, :, here], plane_ref.at[offset, plane], arrived.at[offset, plane])
             )
         copies.append(
-            pltpu.make_async_copy(signal_ref.at[:, here], out_refs[offset].at[0], arrived.at[offset, 0])
+            pltpu.make_async_copy(values_ref.at[:, here], out_refs[offset].at[planes], arrived.at[offset, planes])
         )
     for copy in copies:
         copy.start()
+    for place, copy in enumerate(copies):
+        copy.wait()
+        offset, plane = chips - 1 - place // (planes + 1), place % (planes + 1)
+        if plane < planes:
+            out_refs[offset][plane] = plane_ref[offset, plane].astype(BF16)
+
+
+def pack_signals(values_in, filters, chips):
+    planes, rows, width = filters.shape
+    lanes = width // chips
+    return pl.pallas_call(
+        functools.partial(pack_signals_kernel, chips),
+        in_specs=[pl.BlockSpec(memory_space=pltpu.HBM)] * 2,
+        out_specs=[WHOLE] * chips,
+        out_shape=[jax.ShapeDtypeStruct((planes + 1, rows, lanes), BF16)] * chips,
+        scratch_shapes=[
+            pltpu.VMEM((chips, planes, rows, lanes), F32),
+            pltpu.SemaphoreType.DMA((chips, planes + 1)),
+        ],
+        cost_estimate=CHEAP,
+        compiler_params=pltpu.CompilerParams(vmem_limit_bytes=8 * 2**20),
+        name="pack_signals",
+    )(
+        pltpu.with_memory_space_constraint(values_in, pltpu.HBM),
+        pltpu.with_memory_space_constraint(filters, pltpu.HBM),
+    )
+
+
+def pack_weights_kernel(chips, gate_ref, weight_ref, other_ref, *refs):
+    out_refs, (joined_ref, arrived) = refs[:chips], refs[chips:]
+    chip, core = own_place()
+    rows = gate_ref.shape[0]
+    half, held = other_ref.shape
+    lanes = out_refs[0].shape[1]
+    copies = [
+        pltpu.make_async_copy(
+            weight_ref.at[block_at(core, half), :], joined_ref.at[:, block_at(core, held)], arrived.at[chips]
+        )
+    ]
+    for offset in range(chips):
+        copies.append(
+            pltpu.make_async_copy(
+                gate_ref.at[:, block_at(chip ^ offset, lanes)], out_refs[offset].at[pl.ds(0, rows)], arrived.at[offset]
+            )
+        )
+    for copy in copies:
+        copy.start()
+    joined_ref[:, block_at(1 - core, held)] = other_ref[...]
     for copy in copies:
         copy.wait()
     for offset in range(chips):
-        for place in range(len(planes)):
-            out_refs[offset][1 + place] = plane_ref[offset, place].astype(BF16)
-
-
-def pack(signal, filters, chips, planes):
-    rows, width = signal.shape
-    lanes = width // chips
-    return pl.pallas_call(
-        functools.partial(pack_kernel, chips, planes),
-        in_specs=[pl.BlockSpec(memory_space=pltpu.HBM)] * 2,
+        out_refs[offset][pl.ds(rows, half), :] = joined_ref[:, block_at(chip ^ offset, lanes)]
+
+
+def pack_weights(gate_values, weight, other, chips):
+    rows, width = gate_values.shape
+    half, held = other.shape
+    return pl.pallas_call(
+        functools.partial(pack_weights_kernel, chips),
+        in_specs=[pl.BlockSpec(memory_space=pltpu.HBM)] * 2 + [WHOLE],
         out_specs=[WHOLE] * chips,
-        out_shape=[jax.ShapeDtypeStruct((1 + len(planes), rows, lanes), BF16)] * chips,
-        scratch_shapes=[
-            pltpu.VMEM((chips, len(planes), rows, lanes), F32),
-            pltpu.SemaphoreType.DMA((chips, 1 + len(planes))),
-        ],
+        out_shape=[jax.ShapeDtypeStruct((rows + half, width // chips), BF16)] * chips,
+        scratch_shapes=[pltpu.VMEM((half, 2 * held), BF16), pltpu.SemaphoreType.DMA((chips + 1,))],
         cost_estimate=CHEAP,
         compiler_params=pltpu.CompilerParams(vmem_limit_bytes=8 * 2**20),
-        name="pack",
-    )(pltpu.with_memory_space_constraint(signal, pltpu.HBM), pltpu.with_memory_space_constraint(filters, pltpu.HBM))
+        name="pack_weights",
+    )(
+        pltpu.with_memory_space_constraint(gate_values, pltpu.HBM),
+        pltpu.with_memory_space_constraint(weight, pltpu.HBM),
+        other,
+    )
 
 
 def forward_kernel(chips, cos_ref, sin_ref, table_ref, own_ref, other_ref, out_ref, signal_ref, waves_ref):
@@ -319,21 +366,20 @@
 
 
 def backward_kernel(chips, cos_ref, sin_ref, table_ref, spectrum_ref, *refs):
-    group_refs, (keep_ref, send_ref, filter_ref, product_ref, back_ref) = refs[: 2 * chips], refs[2 * chips :]
+    filter_refs, (keep_ref, send_ref, filter_ref, product_ref, back_ref) = refs[:chips], refs[chips:]
     chip, core = own_place()
     parts = 2 * chips
     rows, lanes = keep_ref.shape[1:]
     chip_bits = chips.bit_length() - 1
     chunk, width = 16, 128
-    for odd in range(2):
-        for offset in range(chips):
-            filter_ref[chip ^ offset, odd] = group_refs[odd * chips + offset][pl.ds(1, 2)]
+    for offset in range(chips):
+        filter_ref[chip ^ offset] = filter_refs[offset][pl.ds(0, 4)]
 
     for residue in range(parts):
         source, odd = bit_reversed(residue // 2, chip_bits), residue % 2
         columns = pl.ds(residue * lanes, lanes)
-        filter_real = filter_ref[source, odd, 0].astype(F32)
-        filter_imag = filter_ref[source, odd, 1].astype(F32)
+        filter_real = filter_ref[source, odd].astype(F32)
+        filter_imag = filter_ref[source, 2 + odd].astype(F32)
         real = spectrum_ref[pl.ds(0, rows), columns]
         imag = spectrum_ref[pl.ds(rows, rows), columns]
         product_ref[pl.ds(0, rows), columns] = (real * filter_real - imag * filter_imag).astype(BF16)
@@ -376,25 +422,25 @@
     lax.fori_loop(0, rows // chunk, gather, 0)
 
 
-def backward(spectrum, first, second, tables):
+def backward(spectrum, first, tables):
     chips = len(first)
     _, rows, lanes = first[0].shape
     _, table, cos, sin = tables
     kept = (chips, rows, lanes)
     return pl.pallas_call(
         functools.partial(backward_kernel, chips),
-        in_specs=[WHOLE] * (4 + 2 * chips),
+        in_specs=[WHOLE] * (4 + chips),
         out_specs=[WHOLE] * 2,
         out_shape=[jax.ShapeDtypeStruct(kept, F32), jax.ShapeDtypeStruct(kept, BF16)],
         scratch_shapes=[
-            pltpu.VMEM((chips, 2, 2, rows, lanes), BF16),
+            pltpu.VMEM((chips, 4, rows, lanes), BF16),
             pltpu.VMEM(spectrum.shape, BF16),
             pltpu.VMEM(spectrum.shape, F32),
         ],
         cost_estimate=CHEAP,
         compiler_params=pltpu.CompilerParams(vmem_limit_bytes=32 * 2**20),
         name="backward",
-    )(cos, sin, table, spectrum, *first, *second)
+    )(cos, sin, table, spectrum, *first)
 
 
 def gate_kernel(chips, skip_ref, keep_ref, arrived_ref, *refs):
@@ -409,8 +455,8 @@
         for piece in range(pieces):
             here = pl.ds(piece * step, step)
             convolved = keep_ref[block, here, :] + arrived_ref[block, here, :].astype(F32)
-            signal = signal_refs[offset][0, here, :].astype(F32)
-            gate = gate_refs[offset][0, here, :].astype(F32)
+            signal = signal_refs[offset][4, here, :].astype(F32)
+            gate = gate_refs[offset][here, :].astype(F32)
             out_ref[piece, block_at(block, step), :] = (gate * (convolved + skip * signal)).astype(BF16)
 
 
@@ -427,55 +473,41 @@
     )(skip, keep, arrived, *first, *second)
 
 
-def collect_kernel(layers, *refs):
-    in_refs, out_ref = refs[:layers], refs[layers]
-    device, layer = lax.axis_index("seq"), lax.axis_index("chan")
-    for step in range(layers):
-        out_ref[device % layers ^ layer ^ step] = in_refs[step][...]
-
-
-def collect(blocks):
-    layers = len(blocks)
-    return pl.pallas_call(
-        functools.partial(collect_kernel, layers),
-        in_specs=[WHOLE] * layers,
+def collect_kernel(chips, *refs):
+    in_refs, out_ref = refs[:chips], refs[chips]
+    chip, _ = own_place()
+    layer = lax.axis_index("chan")
+    half = out_ref.shape[1]
+    start = in_refs[0].shape[0] - half
+    for offset in range(chips):
+        out_ref[chip ^ layer ^ offset] = in_refs[offset][pl.ds(start, half), :]
+
+
+def collect(second, half):
+    chips = len(second)
+    return pl.pallas_call(
+        functools.partial(collect_kernel, chips),
+        in_specs=[WHOLE] * chips,
         out_specs=WHOLE,
-        out_shape=jax.ShapeDtypeStruct((layers, *blocks[0].shape), BF16),
+        out_shape=jax.ShapeDtypeStruct((chips, half, second[0].shape[1]), BF16),
         cost_estimate=CHEAP,
         compiler_params=pltpu.CompilerParams(vmem_limit_bytes=4 * 2**20),
         name="collect_weights",
-    )(*blocks)
-
-
-def arrange_kernel(own_ref, other_ref, out_ref):
-    _, core = own_place()
-    share = own_ref.shape[2]
-    out_ref[:, :, block_at(core, share)] = own_ref[...]
-    out_ref[:, :, block_at(1 - core, share)] = other_ref[...]
-
-
-def arrange(own, other):
-    layers, rows, share = own.shape
-    return pl.pallas_call(
-        arrange_kernel,
-        in_specs=[WHOLE] * 2,
-        out_specs=WHOLE,
-        out_shape=jax.ShapeDtypeStruct((layers, rows, 2 * share), BF16),
-        cost_estimate=CHEAP,
-        compiler_params=pltpu.CompilerParams(vmem_limit_bytes=8 * 2**20),
-        name="arrange_weights",
-    )(own, other)
-
-
-def project_kernel(chips, piece, weight_ref, *refs):
+    )(*second)
+
+
+def project_kernel(chips, piece, own_ref, other_ref, *refs):
     gated_refs, out_refs, joined_ref = refs[:chips], refs[chips:-1], refs[-1]
-    chip, _ = own_place()
+    chip, core = own_place()
+    half = own_ref.shape[1]
     lanes = gated_refs[0].shape[2]
     for offset in range(chips):
         joined_ref[:, block_at(chip ^ offset, lanes)] = gated_refs[offset][piece]
     order = (3, 2, 1, 0) if len(out_refs) == 4 else (1, 3, 2, 0)
     for target in order:
-        partial = jnp.dot(joined_ref[...], weight_ref[target], preferred_element_type=F32).astype(BF16)
+        partial = jnp.dot(joined_ref[:, block_at(core, half)], own_ref[target], preferred_element_type=F32)
+        partial += jnp.dot(joined_ref[:, block_at(1 - core, half)], other_ref[target], preferred_element_type=F32)
+        partial = partial.astype(BF16)
         if len(out_refs) == 4:
             out_refs[target][...] = partial
         elif target % 2:
@@ -484,23 +516,23 @@
             out_refs[target // 2][...] = partial
 
 
-def project(weight, gated, piece, paired):
+def project(own, other, gated, piece, paired):
     chips = len(gated)
-    layers, depth, columns = weight.shape
+    layers, half, columns = own.shape
     rows = gated[0].shape[1]
     block = jax.ShapeDtypeStruct((rows, columns), BF16)
     pair = jax.ShapeDtypeStruct((2, rows, columns), BF16)
     out_shape = [block, block, pair] if paired else [block] * layers
     return pl.pallas_call(
         functools.partial(project_kernel, chips, piece),
-        in_specs=[WHOLE] * (1 + chips),
+        in_specs=[WHOLE] * (2 + chips),
         out_specs=[WHOLE] * len(out_shape),
         out_shape=out_shape,
-        scratch_shapes=[pltpu.VMEM((rows, depth), BF16)],
+        scratch_shapes=[pltpu.VMEM((rows, 2 * half), BF16)],
         cost_estimate=CHEAP,
         compiler_params=pltpu.CompilerParams(vmem_limit_bytes=8 * 2**20),
         name="project",
-    )(weight, *gated)
+    )(own, other, *gated)
 
 
 def finish_kernel(chips, direct_refs, paired_refs, out_refs):
@@ -573,37 +605,30 @@
 
 def shards_direct(values_in, gate_values, filter_spectrum, skip_gain, out_weight):
     parts = lax.axis_size("seq")
-    layers = lax.axis_size("chan")
     chips = parts // 2
     rows, width = values_in.shape
     device = lax.axis_index("seq")
     tables = small_tables(parts, rows)
 
-    flat_filters = filter_spectrum.reshape(4, rows, width)
-    first = pack(values_in, flat_filters, chips, (0, 2))
-    second = pack(after(gate_values, first[0]), flat_filters, chips, (1, 3))
+    first = pack_signals(values_in, filter_spectrum.reshape(4, rows, width), chips)
+    half = out_weight.shape[0] // 2
+    others_half = lax.dynamic_slice_in_dim(after(out_weight, first[0]), (1 - device % 2) * half, half, 0)
+    second = pack_weights(gate_values, out_weight, swapped(others_half, "seq", 1), chips)
     first = to_chips(first)
-    own = jnp.stack([after(block, second[0])[0] for block in first])
+    own = jnp.stack([after(block, second[0])[4] for block in first])
     second = to_chips(second)
     spectrum = forward(own, swapped(own, "seq", 1), tables)
-    keep, send = backward(spectrum, first, second, tables)
+    keep, send = backward(spectrum, first, tables)
     gated = gate(skip_gain[None, :], keep, swapped(send, "seq", 1), first, second, 2)
-
-    share = out_weight.shape[1] // layers
-    own_weight = []
-    for step, earlier in enumerate((spectrum, spectrum, send, send)):
-        sent = lax.dynamic_slice_in_dim(after(out_weight, second[0]), (device // 2 ^ step) * share, share, 1)
-        pairs = [(source, source % 2 * layers + (source // 2 ^ step)) for source in range(parts)]
-        own_weight.append(lax.ppermute(after(sent, earlier), "seq", pairs))
-    own_weight = collect([after(block, gated) for block in own_weight])
-    weight = arrange(own_weight, swapped(own_weight, "seq", 1))
-
     gathered = to_chips([gated] * chips)
-    partials = project(weight, gathered, 0, False)
+    own_weight = collect([after(block, gated) for block in second], half)
+    weights = (own_weight, swapped(own_weight, "seq", 1))
+
+    partials = project(*weights, gathered, 0, False)
     direct = [swapped(block, "chan", offset) for offset, block in enumerate(partials)]
-    keep, passed, send = project(weight, gathered, 1, True)
+    keep, passed, send = project(*weights, gathered, 1, True)
     arrived = swapped(send, "chan", 1)
-    passed = after((passed.astype(F32) + arrived[1].astype(F32)).astype(BF16), *direct)
+    passed = (passed.astype(F32) + arrived[1].astype(F32)).astype(BF16)
     return join(to_chips(finish(direct, (keep, arrived, swapped(passed, "chan", 2)), chips)))
 
 

time: 97.5 us -> 89.2 us (0.915)
  starting transfers between devices: 28.8 us -> 23.4 us
  local copies, waits for them, and re-layouts: 1.37 us -> 0.15 us
  waiting for transfers between devices: 56.9 us -> 55.9 us
    ppermute x4 -> x0, waiting for transfers between devices: 10.9 us -> none  [shards_direct(): own_weight.append(lax.ppermute(after(sent, earlier), 'seq', pairs))]
    ppermute x20 -> x21, waiting for transfers between devices: 46 us -> 55.9 us  [swapped(): lax.ppermute(value, axis, [(source, source ^ offset) for source in range(...]
    ppermute x4 -> x0, starting transfers between devices: 5.66 us -> none  [shards_direct(): own_weight.append(lax.ppermute(after(sent, earlier), 'seq', pairs))]
    dynamic_slice x1, local copies, waits for them, and re-layouts: 1.32 us -> 0.03 us  [shards_direct(): lax.dynamic_slice_in_dim(after(out_weight, first[0]), (1 - device % 2) *...]
    pallas_call x4 -> x3, Pallas kernels: 3.67 us -> 3.28 us  [the longest x1 1.94 us: pack_signals(): pl.pallas_call(functools.partial(pack_signals_kernel, chips), in_specs=[p...]
    ppermute x20 -> x21, starting transfers between devices: 23.2 us -> 23.4 us  [swapped(): lax.ppermute(value, axis, [(source, source ^ offset) for source in range(...]
  transfers between devices with their start and end apart: 24 -> 21, of which waited for: 17 -> 14; matrix products, arithmetic and copies ran while one was open for 1% -> 0% of each run, Pallas kernels for 5% -> 6%
where the time goes in v7:
time: 89.2 us; the launch traced here: 89 us
  waiting for transfers between devices  55.9 us (63%)
  starting transfers between devices  23.4 us (26%)
  Pallas kernels  9.34 us (10%)
    ppermute x21, waiting for transfers between devices, swapped(): lax.ppermute(value, axis, [(source, source ^ offset) for source in range(...  55.9 us
    ppermute x21, starting transfers between devices, swapped(): lax.ppermute(value, axis, [(source, source ^ offset) for source in range(...  23.4 us
    pallas_call x1, Pallas kernels, backward(): pl.pallas_call(functools.partial(backward_kernel, chips), in_specs=[WHOLE...  2.02 us
    pallas_call x1, Pallas kernels, pack_signals(): pl.pallas_call(functools.partial(pack_signals_kernel, chips), in_specs=[p...  1.94 us
  transfers between devices with their start and end apart: 21, of which 14 were waited for; matrix products, arithmetic and copies ran while one was open for 0% of the time, Pallas kernels for 6%

profile of v7, /device:TPU:0, one launch (start us, length us, event | category | flops | bytes accessed | tf_op | source)
XLA Modules:
  0.0 89.0 jit_solution(14218916575226599748)
XLA Ops:
  0.0 1.9 %pack_signals.1 = (bf16[5,128,256]{2,1,0:T(8,128)(2,1)S(1)}, bf16[5,128,256]{2,1,0:T(8,128)(2,1)S(1)}, bf16[5,128,256]{2,1,0:T(8,128)(2,1)S(1)}, bf16[5,128,256]{2,1,0:T(8,128)(2,1)S(1)}) custom-call(bf16[128,1024]{1,0:T(8,128)(2,1)} %values_ref.1, f32[4,128,1024]{2,1,0:T(8,128)} %bitcast.8), custom_call_target="tpu_custom_call" | custom-call | tf_op jit(solution)/shard_map/pack_signals/pallas_call | solution.py:243
  2.6 3.5 %collective-permute-start.3 = (bf16[5,128,256]{2,1,0:T(8,128)(2,1)S(1)}, bf16[5,128,256]{2,1,0:T(8,128)(2,1)S(1)}, u32[]{:S(2)}, u32[]{:S(2)}) collective-permute-start(bf16[5,128,256]{2,1,0:T(8,128)(2,1)S(1)} %get-tuple-element.43), channel_id=1, source_target_pairs={{0,24},{4,28},{8,16},{12,20},{16,8},{20,12},{24,0},{28,4},{1,25},{... | collective-permute-start | bytes 983048 | tf_op jit(solution)/shard_map/ppermute | solution.py:595
  8.0 6.7 %collective-permute-done.3.refs_3_ = bf16[5,128,256]{2,1,0:T(8,128)(2,1)S(1)} collective-permute-done((bf16[5,128,256]{2,1,0:T(8,128)(2,1)S(1)}, bf16[5,128,256]{2,1,0:T(8,128)(2,1)S(1)}, u32[]{:S(2)}, u32[]{:S(2)}) %collective-permute-start.3) | collective-permute-done | bytes 327712 | tf_op jit(solution)/shard_map/ppermute | solution.py:595
  14.7 6.7 %collective-permute-done.2.refs_2_ = bf16[5,128,256]{2,1,0:T(8,128)(2,1)S(1)} collective-permute-done((bf16[5,128,256]{2,1,0:T(8,128)(2,1)S(1)}, bf16[5,128,256]{2,1,0:T(8,128)(2,1)S(1)}, u32[]{:S(2)}, u32[]{:S(2)}) %collective-permute-start.2) | collective-permute-done | bytes 327712 | tf_op jit(solution)/shard_map/ppermute | solution.py:595
  21.9 1.6 %collective-permute-start.6 = (bf16[640,256]{1,0:T(8,128)(2,1)S(1)}, bf16[640,256]{1,0:T(8,128)(2,1)S(1)}, u32[]{:S(2)}, u32[]{:S(2)}) collective-permute-start(bf16[640,256]{1,0:T(8,128)(2,1)S(1)} %get-tuple-element.47), channel_id=1, source_target_pairs={{0,8},{4,12},{8,0},{12,4},{16,24},{20,28},{24,16},{28,20},{1,9},{5... | collective-permute-start | bytes 983048 | tf_op jit(solution)/shard_map/ppermute | solution.py:595
  24.0 1.5 %collective-permute-start.8 = (bf16[640,256]{1,0:T(8,128)(2,1)S(1)}, bf16[640,256]{1,0:T(8,128)(2,1)S(1)}, u32[]{:S(2)}, u32[]{:S(2)}) collective-permute-start(bf16[640,256]{1,0:T(8,128)(2,1)S(1)} %get-tuple-element.49), channel_id=1, source_target_pairs={{0,24},{4,28},{8,16},{12,20},{16,8},{20,12},{24,0},{28,4},{1,25},{... | collective-permute-start | bytes 983048 | tf_op jit(solution)/shard_map/ppermute | solution.py:595
  25.5 1.5 %forward.1.spectrum_ref = f32[256,2048]{1,0:T(8,128)S(1)} custom-call(f32[2,128,8]{2,1,0:T(8,128)S(1)} %copy-done.1, f32[2,128,8]{2,1,0:T(8,128)S(1)} %copy-done, bf16[256,256]{1,0:T(8,128)(2,1)S(1)} %copy-done.2, bf16[4,128,256]{2,1,0:T(8,128)(2,1)S(1)} %pad_maximum_fusion.own_ref, bf16[4,128,256]{2,1,0:T(8,128)(2,1)S(1)} %collective-permute-done.4.other_ref), custom_call_target="tpu_custom_call" | custom-call | tf_op jit(solution)/shard_map/forward/pallas_call | solution.py:356
  27.0 2.0 %backward.1 = (f32[4,128,256]{2,1,0:T(8,128)S(1)}, bf16[4,128,256]{2,1,0:T(8,128)(2,1)S(1)}) custom-call(f32[2,128,8]{2,1,0:T(8,128)S(1)} %copy-done.1, f32[2,128,8]{2,1,0:T(8,128)S(1)} %copy-done, bf16[256,256]{1,0:T(8,128)(2,1)S(1)} %copy-done.3, f32[256,2048]{1,0:T(8,128)S(1)} %forward.1.spectrum_ref, bf16[5,128,256]{2,1,0:T(8,128)(2,1)S(1)} %get-tuple-element.38.refs_0_, ...), custom_call_target="tpu_custom_call" | custom-call | tf_op jit(solution)/shard_map/backward/pallas_call | solution.py:430
  29.1 3.4 %collective-permute-done.6.refs_5_.refs_1_ = bf16[640,256]{1,0:T(8,128)(2,1)S(1)} collective-permute-done((bf16[640,256]{1,0:T(8,128)(2,1)S(1)}, bf16[640,256]{1,0:T(8,128)(2,1)S(1)}, u32[]{:S(2)}, u32[]{:S(2)}) %collective-permute-start.6) | collective-permute-done | bytes 327712 | tf_op jit(solution)/shard_map/ppermute | solution.py:595
  32.5 7.8 %collective-permute-done.7.refs_6_.refs_2_ = bf16[640,256]{1,0:T(8,128)(2,1)S(1)} collective-permute-done((bf16[640,256]{1,0:T(8,128)(2,1)S(1)}, bf16[640,256]{1,0:T(8,128)(2,1)S(1)}, u32[]{:S(2)}, u32[]{:S(2)}) %collective-permute-start.7) | collective-permute-done | bytes 327712 | tf_op jit(solution)/shard_map/ppermute | solution.py:595
  40.6 1.5 %collective-permute-start.12 = (bf16[2,256,256]{2,1,0:T(8,128)(2,1)S(1)}, bf16[2,256,256]{2,1,0:T(8,128)(2,1)S(1)}, u32[]{:S(2)}, u32[]{:S(2)}) collective-permute-start(bf16[2,256,256]{2,1,0:T(8,128)(2,1)S(1)} %gate.1.refs_0_), channel_id=1, source_target_pairs={{0,24},{4,28},{8,16},{12,20},{16,8},{20,12},{24,0},{28,4},{1,25},{... | collective-permute-start | bytes 786440 | tf_op jit(solution)/shard_map/ppermute | solution.py:595
  42.7 1.5 %collective-permute-start.10 = (bf16[2,256,256]{2,1,0:T(8,128)(2,1)S(1)}, bf16[2,256,256]{2,1,0:T(8,128)(2,1)S(1)}, u32[]{:S(2)}, u32[]{:S(2)}) collective-permute-start(bf16[2,256,256]{2,1,0:T(8,128)(2,1)S(1)} %gate.1.refs_0_), channel_id=1, source_target_pairs={{0,8},{4,12},{8,0},{12,4},{16,24},{20,28},{24,16},{28,20},{1,9},{5... | collective-permute-start | bytes 786440 | tf_op jit(solution)/shard_map/ppermute | solution.py:595
  44.2 6.6 %collective-permute-done.12.refs_3_ = bf16[2,256,256]{2,1,0:T(8,128)(2,1)S(1)} collective-permute-done((bf16[2,256,256]{2,1,0:T(8,128)(2,1)S(1)}, bf16[2,256,256]{2,1,0:T(8,128)(2,1)S(1)}, u32[]{:S(2)}, u32[]{:S(2)}) %collective-permute-start.12) | collective-permute-done | bytes 262176 | tf_op jit(solution)/shard_map/ppermute | solution.py:595
  50.8 5.1 %collective-permute-done.11.refs_2_ = bf16[2,256,256]{2,1,0:T(8,128)(2,1)S(1)} collective-permute-done((bf16[2,256,256]{2,1,0:T(8,128)(2,1)S(1)}, bf16[2,256,256]{2,1,0:T(8,128)(2,1)S(1)}, u32[]{:S(2)}, u32[]{:S(2)}) %collective-permute-start.11) | collective-permute-done | bytes 262176 | tf_op jit(solution)/shard_map/ppermute | solution.py:595
  56.7 1.6 %collective-permute-start.16 = (bf16[2,256,256]{2,1,0:T(8,128)(2,1)S(1)}, bf16[2,256,256]{2,1,0:T(8,128)(2,1)S(1)}, u32[]{:S(2)}, u32[]{:S(2)}) collective-permute-start(bf16[2,256,256]{2,1,0:T(8,128)(2,1)S(1)} %get-tuple-element.59), channel_id=1, source_target_pairs={{0,1},{1,0},{2,3},{3,2},{4,5},{5,4},{6,7},{7,6},{8,9},{9,8},{10,11... | collective-permute-start | bytes 786440 | tf_op jit(solution)/shard_map/ppermute | solution.py:595
  59.6 2.6 %collective-permute-start.14 = (bf16[256,256]{1,0:T(8,128)(2,1)S(1)}, bf16[256,256]{1,0:T(8,128)(2,1)S(1)}, u32[]{:S(2)}, u32[]{:S(2)}) collective-permute-start(bf16[256,256]{1,0:T(8,128)(2,1)S(1)} %get-tuple-element.56), channel_id=1, source_target_pairs={{0,2},{1,3},{2,0},{3,1},{4,6},{5,7},{6,4},{7,5},{8,10},{9,11},{10,... | collective-permute-start | bytes 393224 | tf_op jit(solution)/shard_map/ppermute | solution.py:595
  62.2 1.3 %collective-permute-start.15 = (bf16[256,256]{1,0:T(8,128)(2,1)S(1)}, bf16[256,256]{1,0:T(8,128)(2,1)S(1)}, u32[]{:S(2)}, u32[]{:S(2)}) collective-permute-start(bf16[256,256]{1,0:T(8,128)(2,1)S(1)} %get-tuple-element.57), channel_id=1, source_target_pairs={{0,3},{1,2},{2,1},{3,0},{4,7},{5,6},{6,5},{7,4},{8,11},{9,10},{10,... | collective-permute-start | bytes 393224 | tf_op jit(solution)/shard_map/ppermute | solution.py:595
  63.6 5.2 %collective-permute-done.16.refs_5_ = bf16[2,256,256]{2,1,0:T(8,128)(2,1)S(1)} collective-permute-done((bf16[2,256,256]{2,1,0:T(8,128)(2,1)S(1)}, bf16[2,256,256]{2,1,0:T(8,128)(2,1)S(1)}, u32[]{:S(2)}, u32[]{:S(2)}) %collective-permute-start.16) | collective-permute-done | bytes 262176 | tf_op jit(solution)/shard_map/ppermute | solution.py:595
  68.8 1.8 %collective-permute-start.17 = (bf16[256,256]{1,0:T(8,128)(2,1)S(1)}, bf16[256,256]{1,0:T(8,128)(2,1)S(1)}, u32[]{:S(2)}, u32[]{:S(2)}) collective-permute-start(bf16[256,256]{1,0:T(8,128)(2,1)S(1)} %fusion), channel_id=1, source_target_pairs={{0,2},{1,3},{2,0},{3,1},{4,6},{5,7},{6,4},{7,5},{8,10},{9,11},{10,... | collective-permute-start | bytes 393224 | tf_op jit(solution)/shard_map/ppermute | solution.py:595
  70.7 5.8 %collective-permute-done.15.refs_3_ = bf16[256,256]{1,0:T(8,128)(2,1)S(1)} collective-permute-done((bf16[256,256]{1,0:T(8,128)(2,1)S(1)}, bf16[256,256]{1,0:T(8,128)(2,1)S(1)}, u32[]{:S(2)}, u32[]{:S(2)}) %collective-permute-start.15) | collective-permute-done | bytes 131104 | tf_op jit(solution)/shard_map/ppermute | solution.py:595
  76.5 4.5 %collective-permute-done.17.refs_6_ = bf16[256,256]{1,0:T(8,128)(2,1)S(1)} collective-permute-done((bf16[256,256]{1,0:T(8,128)(2,1)S(1)}, bf16[256,256]{1,0:T(8,128)(2,1)S(1)}, u32[]{:S(2)}, u32[]{:S(2)}) %collective-permute-start.17) | collective-permute-done | bytes 131104 | tf_op jit(solution)/shard_map/ppermute | solution.py:595
  81.7 1.4 %collective-permute-start.19 = (bf16[128,256]{1,0:T(8,128)(2,1)S(1)}, bf16[128,256]{1,0:T(8,128)(2,1)S(1)}, u32[]{:S(2)}, u32[]{:S(2)}) collective-permute-start(bf16[128,256]{1,0:T(8,128)(2,1)S(1)} %get-tuple-element.63), channel_id=1, source_target_pairs={{0,16},{4,20},{8,24},{12,28},{16,0},{20,4},{24,8},{28,12},{1,17},{... | collective-permute-start | bytes 196616 | tf_op jit(solution)/shard_map/ppermute | solution.py:595
  83.1 1.5 %collective-permute-start.20 = (bf16[128,256]{1,0:T(8,128)(2,1)S(1)}, bf16[128,256]{1,0:T(8,128)(2,1)S(1)}, u32[]{:S(2)}, u32[]{:S(2)}) collective-permute-start(bf16[128,256]{1,0:T(8,128)(2,1)S(1)} %get-tuple-element.64), channel_id=1, source_target_pairs={{0,24},{4,28},{8,16},{12,20},{16,8},{20,12},{24,0},{28,4},{1,25},{... | collective-permute-start | bytes 196616 | tf_op jit(solution)/shard_map/ppermute | solution.py:595
  85.9 2.3 %collective-permute-done.20.refs_3_ = bf16[128,256]{1,0:T(8,128)(2,1)S(1)} collective-permute-done((bf16[128,256]{1,0:T(8,128)(2,1)S(1)}, bf16[128,256]{1,0:T(8,128)(2,1)S(1)}, u32[]{:S(2)}, u32[]{:S(2)}) %collective-permute-start.20) | collective-permute-done | bytes 65568 | tf_op jit(solution)/shard_map/ppermute | solution.py:595
  (47 shorter events, 9.5 us)
Async XLA Ops:
  1.9 23.5 %copy-start = (f32[2,128,8]{2,1,0:T(8,128)S(1)}, f32[2,128,8]{2,1,0:T(8,128)}, u32[]{:S(2)}) copy-start(f32[2,128,8]{2,1,0:T(8,128)} %constant.34.clone.sin_ref) | copy-start | bytes 24580
  2.0 23.5 %copy-start.1 = (f32[2,128,8]{2,1,0:T(8,128)S(1)}, f32[2,128,8]{2,1,0:T(8,128)}, u32[]{:S(2)}) copy-start(f32[2,128,8]{2,1,0:T(8,128)} %constant.33.clone.cos_ref) | copy-start | bytes 24580
  2.0 23.5 %copy-start.2 = (bf16[256,256]{1,0:T(8,128)(2,1)S(1)}, bf16[256,256]{1,0:T(8,128)(2,1)}, u32[]{:S(2)}) copy-start(bf16[256,256]{1,0:T(8,128)(2,1)} %constant.35.clone.table_ref) | copy-start | bytes 393220
  2.1 4.7 %collective-permute-start = (bf16[512,512]{1,0:T(8,128)(2,1)S(1)}, bf16[512,512]{1,0:T(8,128)(2,1)S(1)}, u32[]{:S(2)}, u32[]{:S(2)}) collective-permute-start(bf16[512,512]{1,0:T(8,128)(2,1)S(1)} %constant_dynamic-slice_fusion), channel_id=1, source_target_pairs={{0,4},{4,0},{8,12},{12,8},{16,20},{20,16},{24,28},{28,24},{1,5},{5... | collective-permute-start | bytes 1572872 | tf_op jit(solution)/shard_map/ppermute | solution.py:595
  2.6 12.1 %collective-permute-start.3 = (bf16[5,128,256]{2,1,0:T(8,128)(2,1)S(1)}, bf16[5,128,256]{2,1,0:T(8,128)(2,1)S(1)}, u32[]{:S(2)}, u32[]{:S(2)}) collective-permute-start(bf16[5,128,256]{2,1,0:T(8,128)(2,1)S(1)} %get-tuple-element.43), channel_id=1, source_target_pairs={{0,24},{4,28},{8,16},{12,20},{16,8},{20,12},{24,0},{28,4},{1,25},{... | collective-permute-start | bytes 983048 | tf_op jit(solution)/shard_map/ppermute | solution.py:595
  6.1 15.3 %collective-permute-start.2 = (bf16[5,128,256]{2,1,0:T(8,128)(2,1)S(1)}, bf16[5,128,256]{2,1,0:T(8,128)(2,1)S(1)}, u32[]{:S(2)}, u32[]{:S(2)}) collective-permute-start(bf16[5,128,256]{2,1,0:T(8,128)(2,1)S(1)} %get-tuple-element.41), channel_id=1, source_target_pairs={{0,16},{4,20},{8,24},{12,28},{16,0},{20,4},{24,8},{28,12},{1,17},{... | collective-permute-start | bytes 983048 | tf_op jit(solution)/shard_map/ppermute | solution.py:595
  6.6 15.1 %collective-permute-start.1 = (bf16[5,128,256]{2,1,0:T(8,128)(2,1)S(1)}, bf16[5,128,256]{2,1,0:T(8,128)(2,1)S(1)}, u32[]{:S(2)}, u32[]{:S(2)}) collective-permute-start(bf16[5,128,256]{2,1,0:T(8,128)(2,1)S(1)} %get-tuple-element.39), channel_id=1, source_target_pairs={{0,8},{4,12},{8,0},{12,4},{16,24},{20,28},{24,16},{28,20},{1,9},{5... | collective-permute-start | bytes 983048 | tf_op jit(solution)/shard_map/ppermute | solution.py:595
  21.8 3.6 %collective-permute-start.4 = (bf16[4,128,256]{2,1,0:T(8,128)(2,1)S(1)}, bf16[4,128,256]{2,1,0:T(8,128)(2,1)S(1)}, u32[]{:S(2)}, u32[]{:S(2)}) collective-permute-start(bf16[4,128,256]{2,1,0:T(8,128)(2,1)S(1)} %pad_maximum_fusion.own_ref), channel_id=1, source_target_pairs={{0,4},{4,0},{8,12},{12,8},{16,20},{20,16},{24,28},{28,24},{1,5},{5... | collective-permute-start | bytes 786440 | tf_op jit(solution)/shard_map/ppermute | solution.py:595
  21.9 10.6 %collective-permute-start.6 = (bf16[640,256]{1,0:T(8,128)(2,1)S(1)}, bf16[640,256]{1,0:T(8,128)(2,1)S(1)}, u32[]{:S(2)}, u32[]{:S(2)}) collective-permute-start(bf16[640,256]{1,0:T(8,128)(2,1)S(1)} %get-tuple-element.47), channel_id=1, source_target_pairs={{0,8},{4,12},{8,0},{12,4},{16,24},{20,28},{24,16},{28,20},{1,9},{5... | collective-permute-start | bytes 983048 | tf_op jit(solution)/shard_map/ppermute | solution.py:595
  23.5 16.8 %collective-permute-start.7 = (bf16[640,256]{1,0:T(8,128)(2,1)S(1)}, bf16[640,256]{1,0:T(8,128)(2,1)S(1)}, u32[]{:S(2)}, u32[]{:S(2)}) collective-permute-start(bf16[640,256]{1,0:T(8,128)(2,1)S(1)} %get-tuple-element.48), channel_id=1, source_target_pairs={{0,16},{4,20},{8,24},{12,28},{16,0},{20,4},{24,8},{28,12},{1,17},{... | collective-permute-start | bytes 983048 | tf_op jit(solution)/shard_map/ppermute | solution.py:595
  24.0 16.3 %collective-permute-start.8 = (bf16[640,256]{1,0:T(8,128)(2,1)S(1)}, bf16[640,256]{1,0:T(8,128)(2,1)S(1)}, u32[]{:S(2)}, u32[]{:S(2)}) collective-permute-start(bf16[640,256]{1,0:T(8,128)(2,1)S(1)} %get-tuple-element.49), channel_id=1, source_target_pairs={{0,24},{4,28},{8,16},{12,20},{16,8},{20,12},{24,0},{28,4},{1,25},{... | collective-permute-start | bytes 983048 | tf_op jit(solution)/shard_map/ppermute | solution.py:595
  29.0 11.3 %collective-permute-start.5 = (bf16[4,128,256]{2,1,0:T(8,128)(2,1)S(1)}, bf16[4,128,256]{2,1,0:T(8,128)(2,1)S(1)}, u32[]{:S(2)}, u32[]{:S(2)}) collective-permute-start(bf16[4,128,256]{2,1,0:T(8,128)(2,1)S(1)} %get-tuple-element.46), channel_id=1, source_target_pairs={{0,4},{4,0},{8,12},{12,8},{16,20},{20,16},{24,28},{28,24},{1,5},{5... | collective-permute-start | bytes 786440 | tf_op jit(solution)/shard_map/ppermute | solution.py:595
  40.6 15.3 %collective-permute-start.9 = (bf16[4,512,256]{2,1,0:T(8,128)(2,1)S(1)}, bf16[4,512,256]{2,1,0:T(8,128)(2,1)S(1)}, u32[]{:S(2)}, u32[]{:S(2)}) collective-permute-start(bf16[4,512,256]{2,1,0:T(8,128)(2,1)S(1)} %collect_weights.1.own_ref), channel_id=1, source_target_pairs={{0,4},{4,0},{8,12},{12,8},{16,20},{20,16},{24,28},{28,24},{1,5},{5... | collective-permute-start | bytes 3145736 | tf_op jit(solution)/shard_map/ppermute | solution.py:595
  40.6 10.1 %collective-permute-start.12 = (bf16[2,256,256]{2,1,0:T(8,128)(2,1)S(1)}, bf16[2,256,256]{2,1,0:T(8,128)(2,1)S(1)}, u32[]{:S(2)}, u32[]{:S(2)}) collective-permute-start(bf16[2,256,256]{2,1,0:T(8,128)(2,1)S(1)} %gate.1.refs_0_), channel_id=1, source_target_pairs={{0,24},{4,28},{8,16},{12,20},{16,8},{20,12},{24,0},{28,4},{1,25},{... | collective-permute-start | bytes 786440 | tf_op jit(solution)/shard_map/ppermute | solution.py:595
  42.1 13.8 %collective-permute-start.11 = (bf16[2,256,256]{2,1,0:T(8,128)(2,1)S(1)}, bf16[2,256,256]{2,1,0:T(8,128)(2,1)S(1)}, u32[]{:S(2)}, u32[]{:S(2)}) collective-permute-start(bf16[2,256,256]{2,1,0:T(8,128)(2,1)S(1)} %gate.1.refs_0_), channel_id=1, source_target_pairs={{0,16},{4,20},{8,24},{12,28},{16,0},{20,4},{24,8},{28,12},{1,17},{... | collective-permute-start | bytes 786440 | tf_op jit(solution)/shard_map/ppermute | solution.py:595
  42.7 13.2 %collective-permute-start.10 = (bf16[2,256,256]{2,1,0:T(8,128)(2,1)S(1)}, bf16[2,256,256]{2,1,0:T(8,128)(2,1)S(1)}, u32[]{:S(2)}, u32[]{:S(2)}) collective-permute-start(bf16[2,256,256]{2,1,0:T(8,128)(2,1)S(1)} %gate.1.refs_0_), channel_id=1, source_target_pairs={{0,8},{4,12},{8,0},{12,4},{16,24},{20,28},{24,16},{28,20},{1,9},{5... | collective-permute-start | bytes 786440 | tf_op jit(solution)/shard_map/ppermute | solution.py:595
  56.7 12.0 %collective-permute-start.16 = (bf16[2,256,256]{2,1,0:T(8,128)(2,1)S(1)}, bf16[2,256,256]{2,1,0:T(8,128)(2,1)S(1)}, u32[]{:S(2)}, u32[]{:S(2)}) collective-permute-start(bf16[2,256,256]{2,1,0:T(8,128)(2,1)S(1)} %get-tuple-element.59), channel_id=1, source_target_pairs={{0,1},{1,0},{2,3},{3,2},{4,5},{5,4},{6,7},{7,6},{8,9},{9,8},{10,11... | collective-permute-start | bytes 786440 | tf_op jit(solution)/shard_map/ppermute | solution.py:595
  59.1 11.5 %collective-permute-start.13 = (bf16[256,256]{1,0:T(8,128)(2,1)S(1)}, bf16[256,256]{1,0:T(8,128)(2,1)S(1)}, u32[]{:S(2)}, u32[]{:S(2)}) collective-permute-start(bf16[256,256]{1,0:T(8,128)(2,1)S(1)} %get-tuple-element.55), channel_id=1, source_target_pairs={{0,1},{1,0},{2,3},{3,2},{4,5},{5,4},{6,7},{7,6},{8,9},{9,8},{10,11... | collective-permute-start | bytes 393224 | tf_op jit(solution)/shard_map/ppermute | solution.py:595
  59.6 11.0 %collective-permute-start.14 = (bf16[256,256]{1,0:T(8,128)(2,1)S(1)}, bf16[256,256]{1,0:T(8,128)(2,1)S(1)}, u32[]{:S(2)}, u32[]{:S(2)}) collective-permute-start(bf16[256,256]{1,0:T(8,128)(2,1)S(1)} %get-tuple-element.56), channel_id=1, source_target_pairs={{0,2},{1,3},{2,0},{3,1},{4,6},{5,7},{6,4},{7,5},{8,10},{9,11},{10,... | collective-permute-start | bytes 393224 | tf_op jit(solution)/shard_map/ppermute | solution.py:595
  62.2 14.3 %collective-permute-start.15 = (bf16[256,256]{1,0:T(8,128)(2,1)S(1)}, bf16[256,256]{1,0:T(8,128)(2,1)S(1)}, u32[]{:S(2)}, u32[]{:S(2)}) collective-permute-start(bf16[256,256]{1,0:T(8,128)(2,1)S(1)} %get-tuple-element.57), channel_id=1, source_target_pairs={{0,3},{1,2},{2,1},{3,0},{4,7},{5,6},{6,5},{7,4},{8,11},{9,10},{10,... | collective-permute-start | bytes 393224 | tf_op jit(solution)/shard_map/ppermute | solution.py:595
  68.8 12.2 %collective-permute-start.17 = (bf16[256,256]{1,0:T(8,128)(2,1)S(1)}, bf16[256,256]{1,0:T(8,128)(2,1)S(1)}, u32[]{:S(2)}, u32[]{:S(2)}) collective-permute-start(bf16[256,256]{1,0:T(8,128)(2,1)S(1)} %fusion), channel_id=1, source_target_pairs={{0,2},{1,3},{2,0},{3,1},{4,6},{5,7},{6,4},{7,5},{8,10},{9,11},{10,... | collective-permute-start | bytes 393224 | tf_op jit(solution)/shard_map/ppermute | solution.py:595
  81.1 4.7 %collective-permute-start.18 = (bf16[128,256]{1,0:T(8,128)(2,1)S(1)}, bf16[128,256]{1,0:T(8,128)(2,1)S(1)}, u32[]{:S(2)}, u32[]{:S(2)}) collective-permute-start(bf16[128,256]{1,0:T(8,128)(2,1)S(1)} %get-tuple-element.62), channel_id=1, source_target_pairs={{0,8},{4,12},{8,0},{12,4},{16,24},{20,28},{24,16},{28,20},{1,9},{5... | collective-permute-start | bytes 196616 | tf_op jit(solution)/shard_map/ppermute | solution.py:595
  81.7 4.3 %collective-permute-start.19 = (bf16[128,256]{1,0:T(8,128)(2,1)S(1)}, bf16[128,256]{1,0:T(8,128)(2,1)S(1)}, u32[]{:S(2)}, u32[]{:S(2)}) collective-permute-start(bf16[128,256]{1,0:T(8,128)(2,1)S(1)} %get-tuple-element.63), channel_id=1, source_target_pairs={{0,16},{4,20},{8,24},{12,28},{16,0},{20,4},{24,8},{28,12},{1,17},{... | collective-permute-start | bytes 196616 | tf_op jit(solution)/shard_map/ppermute | solution.py:595
  83.1 5.2 %collective-permute-start.20 = (bf16[128,256]{1,0:T(8,128)(2,1)S(1)}, bf16[128,256]{1,0:T(8,128)(2,1)S(1)}, u32[]{:S(2)}, u32[]{:S(2)}) collective-permute-start(bf16[128,256]{1,0:T(8,128)(2,1)S(1)} %get-tuple-element.64), channel_id=1, source_target_pairs={{0,24},{4,28},{8,16},{12,20},{16,8},{20,12},{24,0},{28,4},{1,25},{... | collective-permute-start | bytes 196616 | tf_op jit(solution)/shard_map/ppermute | solution.py:595
  (3 other events, 34.3 us)

commit v8 on v3

--- a/solution.py
+++ b/solution.py
@@ -164,6 +164,7 @@
 
 
 WHOLE = pl.BlockSpec(memory_space=pltpu.VMEM)
+CHEAP = pl.CostEstimate(flops=0, transcendentals=0, bytes_accessed=0)
 
 
 def small_tables(parts, rows):
@@ -212,52 +213,85 @@
     return pl.ds(pl.multiple_of(index * size, size), size)
 
 
-def pack_signals_kernel(chips, values_ref, gate_ref, *out_refs):
+def pack_signals_kernel(offsets, filter_ref, values_ref, *refs):
+    out_refs, (plane_ref, arrived) = refs[: len(offsets)], refs[len(offsets) :]
     chip, _ = own_place()
+    planes = filter_ref.shape[0]
     lanes = out_refs[0].shape[2]
-    for offset in range(chips):
-        out_refs[offset][0] = values_ref[:, block_at(chip ^ offset, lanes)]
-        out_refs[offset][1] = gate_ref[:, block_at(chip ^ offset, lanes)]
-
-
-def pack_signals(values_in, gate_values, chips):
-    rows, width = values_in.shape
-    return pl.pallas_call(
-        functools.partial(pack_signals_kernel, chips),
-        in_specs=[WHOLE] * 2,
-        out_specs=[WHOLE] * chips,
-        out_shape=[jax.ShapeDtypeStruct((2, rows, width // chips), BF16)] * chips,
-        name="pack_signals",
-    )(values_in, gate_values)
-
-
-def pack_filter_kernel(offset, filter_ref, out_ref, plane_ref, arrived):
-    chip, _ = own_place()
-    planes, _, lanes = out_ref.shape
-    copies = [
-        pltpu.make_async_copy(
-            filter_ref.at[plane, :, block_at(chip ^ offset, lanes)], plane_ref.at[plane], arrived.at[plane]
+    copies, work = [], []
+    for place, offset in enumerate(offsets):
+        here = block_at(chip ^ offset, lanes)
+        for plane in range(planes):
+            copies.append(
+                pltpu.make_async_copy(filter_ref.at[plane, :, here], plane_ref.at[place, plane], arrived.at[place, plane])
+            )
+            work.append((place, plane))
+        copies.append(
+            pltpu.make_async_copy(values_ref.at[:, here], out_refs[place].at[planes], arrived.at[place, planes])
         )
-        for plane in range(planes)
-    ]
+        work.append(None)
     for copy in copies:
         copy.start()
-    for plane, copy in enumerate(copies):
+    for copy, task in zip(copies, work):
         copy.wait()
-        out_ref[plane] = plane_ref[plane].astype(BF16)
-
-
-def pack_filter(filters, chips, offset):
+        if task:
+            place, plane = task
+            out_refs[place][plane] = plane_ref[place, plane].astype(BF16)
+
+
+def pack_signals(values_in, filters, chips, offsets):
     planes, rows, width = filters.shape
-    shape = (planes, rows, width // chips)
-    return pl.pallas_call(
-        functools.partial(pack_filter_kernel, offset),
-        in_specs=[pl.BlockSpec(memory_space=pl.ANY)],
-        out_specs=WHOLE,
-        out_shape=jax.ShapeDtypeStruct(shape, BF16),
-        scratch_shapes=[pltpu.VMEM(shape, F32), pltpu.SemaphoreType.DMA((planes,))],
-        name="pack_filter",
-    )(filters)
+    lanes = width // chips
+    return pl.pallas_call(
+        functools.partial(pack_signals_kernel, offsets),
+        in_specs=[pl.BlockSpec(memory_space=pltpu.HBM)] * 2,
+        out_specs=[WHOLE] * len(offsets),
+        out_shape=[jax.ShapeDtypeStruct((planes + 1, rows, lanes), BF16)] * len(offsets),
+        scratch_shapes=[
+            pltpu.VMEM((len(offsets), planes, rows, lanes), F32),
+            pltpu.SemaphoreType.DMA((len(offsets), planes + 1)),
+        ],
+        cost_estimate=CHEAP,
+        compiler_params=pltpu.CompilerParams(vmem_limit_bytes=8 * 2**20),
+        name="pack_signals",
+    )(*(pltpu.with_memory_space_constraint(array, pltpu.HBM) for array in (filters, values_in)))
+
+
+def pack_weights_kernel(chips, gate_ref, weight_ref, *refs):
+    out_refs, arrived = refs[:chips], refs[chips]
+    chip, _ = own_place()
+    rows = gate_ref.shape[0]
+    depth, held = weight_ref.shape
+    half, share = depth // 2, held // chips
+    copies = []
+    for offset in range(chips):
+        out_ref, target = out_refs[offset], chip ^ offset
+        gates = gate_ref.at[:, block_at(target, out_ref.shape[1])]
+        copies.append(pltpu.make_async_copy(gates, out_ref.at[pl.ds(0, rows)], arrived.at[offset, 2]))
+        for part in range(2):
+            source = weight_ref.at[pl.ds(part * half, half), block_at(target, share)]
+            sink = out_ref.at[pl.ds(rows, half), pl.ds(part * share, share)]
+            copies.append(pltpu.make_async_copy(source, sink, arrived.at[offset, part]))
+    for copy in copies:
+        copy.start()
+    for copy in copies:
+        copy.wait()
+
+
+def pack_weights(gate_values, weight, chips):
+    rows, width = gate_values.shape
+    depth, held = weight.shape
+    shape = (rows + depth // 2, 2 * held // chips)
+    return pl.pallas_call(
+        functools.partial(pack_weights_kernel, chips),
+        in_specs=[pl.BlockSpec(memory_space=pltpu.HBM)] * 2,
+        out_specs=[WHOLE] * chips,
+        out_shape=[jax.ShapeDtypeStruct(shape, BF16)] * chips,
+        scratch_shapes=[pltpu.SemaphoreType.DMA((chips, 3))],
+        cost_estimate=CHEAP,
+        compiler_params=pltpu.CompilerParams(vmem_limit_bytes=8 * 2**20),
+        name="pack_weights",
+    )(*(pltpu.with_memory_space_constraint(array, pltpu.HBM) for array in (gate_values, weight)))
 
 
 def forward_kernel(chips, cos_ref, sin_ref, table_ref, own_ref, other_ref, out_ref, signal_ref, waves_ref):
@@ -316,6 +350,7 @@
         out_specs=WHOLE,
         out_shape=jax.ShapeDtypeStruct(spectrum, F32),
         scratch_shapes=[pltpu.VMEM((2 * chips, rows, lanes), BF16), pltpu.VMEM(spectrum, BF16)],
+        cost_estimate=CHEAP,
         compiler_params=pltpu.CompilerParams(vmem_limit_bytes=32 * 2**20),
         name="forward",
     )(cos, sin, table, own, other)
@@ -329,7 +364,7 @@
     chip_bits = chips.bit_length() - 1
     chunk, width = 16, 128
     for offset in range(chips):
-        filter_ref[chip ^ offset] = filter_refs[offset][...]
+        filter_ref[chip ^ offset] = filter_refs[offset][pl.ds(0, 4)]
 
     for residue in range(parts):
         source, odd = bit_reversed(residue // 2, chip_bits), residue % 2
@@ -378,9 +413,9 @@
     lax.fori_loop(0, rows // chunk, gather, 0)
 
 
-def backward(spectrum, filters, tables):
-    chips = len(filters)
-    planes, rows, lanes = filters[0].shape
+def backward(spectrum, first, tables):
+    chips = len(first)
+    _, rows, lanes = first[0].shape
     _, table, cos, sin = tables
     kept = (chips, rows, lanes)
     return pl.pallas_call(
@@ -389,63 +424,89 @@
         out_specs=[WHOLE] * 2,
         out_shape=[jax.ShapeDtypeStruct(kept, F32), jax.ShapeDtypeStruct(kept, BF16)],
         scratch_shapes=[
-            pltpu.VMEM((chips, planes, rows, lanes), BF16),
+            pltpu.VMEM((chips, 4, rows, lanes), BF16),
             pltpu.VMEM(spectrum.shape, BF16),
             pltpu.VMEM(spectrum.shape, F32),
         ],
-        compiler_params=pltpu.CompilerParams(vmem_limit_bytes=40 * 2**20),
+        cost_estimate=CHEAP,
+        compiler_params=pltpu.CompilerParams(vmem_limit_bytes=32 * 2**20),
         name="backward",
-    )(cos, sin, table, spectrum, *filters)
+    )(cos, sin, table, spectrum, *first)
 
 
 def gate_kernel(chips, skip_ref, keep_ref, arrived_ref, *refs):
-    signal_refs, out_refs = refs[:chips], refs[chips:]
+    signal_refs, gate_refs, out_refs = refs[:chips], refs[chips : 2 * chips], refs[2 * chips :]
     chip, _ = own_place()
     rows, lanes = keep_ref.shape[1:]
     step = rows // len(out_refs)
     skip = skip_ref[:, block_at(chip, lanes)]
     for offset in range(chips):
         block = chip ^ offset
-        for part, out_ref in enumerate(out_refs):
-            here = pl.ds(part * step, step)
+        for piece, out_ref in enumerate(out_refs):
+            here = pl.ds(piece * step, step)
             convolved = keep_ref[block, here, :] + arrived_ref[block, here, :].astype(F32)
-            signal = signal_refs[offset][0, here, :].astype(F32)
-            gate = signal_refs[offset][1, here, :].astype(F32)
+            signal = signal_refs[offset][4, here, :].astype(F32)
+            gate = gate_refs[offset][here, :].astype(F32)
             out_ref[block_at(block, step), :] = (gate * (convolved + skip * signal)).astype(BF16)
 
 
-def gate(skip, keep, arrived, signals, pieces):
+def gate(skip, keep, arrived, first, second, pieces):
     chips, rows, lanes = keep.shape
     return pl.pallas_call(
         functools.partial(gate_kernel, chips),
-        in_specs=[WHOLE] * (3 + chips),
+        in_specs=[WHOLE] * (3 + 2 * chips),
         out_specs=[WHOLE] * pieces,
         out_shape=[jax.ShapeDtypeStruct((chips * rows // pieces, lanes), BF16)] * pieces,
+        cost_estimate=CHEAP,
+        compiler_params=pltpu.CompilerParams(vmem_limit_bytes=6 * 2**20),
         name="gate",
-    )(skip, keep, arrived, *signals)
-
-
-def arrange_kernel(layers, *refs):
-    own_refs, other_refs, out_ref = refs[:layers], refs[layers : 2 * layers], refs[2 * layers]
-    device, layer = lax.axis_index("seq"), lax.axis_index("chan")
-    share = own_refs[0].shape[1]
-    for step in range(layers):
-        target = device % layers ^ layer ^ step
-        out_ref[target, :, block_at(device % 2, share)] = own_refs[step][...]
-        out_ref[target, :, block_at(1 - device % 2, share)] = other_refs[step ^ 1][...]
+    )(skip, keep, arrived, *first, *second)
+
+
+def collect_kernel(chips, *refs):
+    in_refs, out_ref = refs[:chips], refs[chips]
+    chip, _ = own_place()
+    layer = lax.axis_index("chan")
+    depth, share = out_ref.shape[1:]
+    half = depth // 2
+    start = in_refs[0].shape[0] - half
+    for offset in range(chips):
+        for part in range(2):
+            block = in_refs[offset][pl.ds(start, half), pl.ds(part * share, share)]
+            out_ref[chip ^ layer ^ offset, pl.ds(part * half, half), :] = block
+
+
+def collect(second, depth):
+    chips = len(second)
+    return pl.pallas_call(
+        functools.partial(collect_kernel, chips),
+        in_specs=[WHOLE] * chips,
+        out_specs=WHOLE,
+        out_shape=jax.ShapeDtypeStruct((chips, depth, second[0].shape[1] // 2), BF16),
+        cost_estimate=CHEAP,
+        compiler_params=pltpu.CompilerParams(vmem_limit_bytes=4 * 2**20),
+        name="collect_weights",
+    )(*second)
+
+
+def arrange_kernel(own_ref, other_ref, out_ref):
+    _, core = own_place()
+    share = own_ref.shape[2]
+    out_ref[:, :, block_at(core, share)] = own_ref[...]
+    out_ref[:, :, block_at(1 - core, share)] = other_ref[...]
 
 
 def arrange(own, other):
-    layers = len(own)
-    rows, share = own[0].shape
-    return pl.pallas_call(
-        functools.partial(arrange_kernel, layers),
-        in_specs=[WHOLE] * (2 * layers),
+    layers, rows, share = own.shape
+    return pl.pallas_call(
+        arrange_kernel,
+        in_specs=[WHOLE] * 2,
         out_specs=WHOLE,
         out_shape=jax.ShapeDtypeStruct((layers, rows, 2 * share), BF16),
-        compiler_params=pltpu.CompilerParams(vmem_limit_bytes=32 * 2**20),
+        cost_estimate=CHEAP,
+        compiler_params=pltpu.CompilerParams(vmem_limit_bytes=8 * 2**20),
         name="arrange_weights",
-    )(*own, *other)
+    )(own, other)
 
 
 def project_kernel(chips, weight_ref, *refs):
@@ -475,7 +536,8 @@
         out_specs=[WHOLE] * 3,
         out_shape=[block, block, jax.ShapeDtypeStruct((2, rows, columns), BF16)],
         scratch_shapes=[pltpu.VMEM((rows, depth), BF16)],
-        compiler_params=pltpu.CompilerParams(vmem_limit_bytes=32 * 2**20),
+        cost_estimate=CHEAP,
+        compiler_params=pltpu.CompilerParams(vmem_limit_bytes=8 * 2**20),
         name="project",
     )(weight, *gated)
 
@@ -487,10 +549,10 @@
     step = keep_refs[0].shape[0] // chips
     for offset in range(chips):
         here = block_at(chip ^ offset, step)
-        for part in range(pieces):
-            total = keep_refs[part][here, :].astype(F32) + first_refs[part][0, here, :].astype(F32)
-            total = total + second_refs[part][here, :].astype(F32)
-            out_refs[offset][pl.ds(part * step, step), :] = total.astype(BF16)
+        for piece in range(pieces):
+            total = keep_refs[piece][here, :].astype(F32) + first_refs[piece][0, here, :].astype(F32)
+            total = total + second_refs[piece][here, :].astype(F32)
+            out_refs[offset][pl.ds(piece * step, step), :] = total.astype(BF16)
 
 
 def finish(keep, first, second, chips):
@@ -501,6 +563,8 @@
         in_specs=[WHOLE] * (3 * pieces),
         out_specs=[WHOLE] * chips,
         out_shape=[jax.ShapeDtypeStruct((rows * pieces // chips, columns), BF16)] * chips,
+        cost_estimate=CHEAP,
+        compiler_params=pltpu.CompilerParams(vmem_limit_bytes=4 * 2**20),
         name="finish",
     )(*keep, *first, *second)
 
@@ -508,9 +572,11 @@
 def join_kernel(chips, *refs):
     in_refs, out_ref = refs[:chips], refs[chips]
     chip, _ = own_place()
-    columns = in_refs[0].shape[1]
-    for offset in range(chips):
-        out_ref[:, block_at(chip ^ offset, columns)] = in_refs[offset][...]
+    share = in_refs[0].shape[1] // 2
+    for offset in range(chips):
+        for part in range(2):
+            block = in_refs[offset][:, pl.ds(part * share, share)]
+            out_ref[:, block_at(part * chips + (chip ^ offset), share)] = block
 
 
 def join(blocks):
@@ -521,6 +587,8 @@
         in_specs=[WHOLE] * chips,
         out_specs=WHOLE,
         out_shape=jax.ShapeDtypeStruct((rows, chips * columns), BF16),
+        cost_estimate=CHEAP,
+        compiler_params=pltpu.CompilerParams(vmem_limit_bytes=2 * 2**20),
         name="join",
     )(*blocks)
 
@@ -535,41 +603,34 @@
     return [swapped(block, "seq", 2 * offset) for offset, block in enumerate(blocks)]
 
 
+def after(value, *others):
+    return lax.optimization_barrier((value, *others))[0]
+
+
 def shards_direct(values_in, gate_values, filter_spectrum, skip_gain, out_weight):
     parts = lax.axis_size("seq")
-    layers = lax.axis_size("chan")
     chips = parts // 2
-    pieces = 2
     rows, width = values_in.shape
-    device = lax.axis_index("seq")
     tables = small_tables(parts, rows)
 
-    signals = to_chips(pack_signals(values_in, gate_values, chips))
-    flat_filters = filter_spectrum.reshape(4, rows, width)
-    filters = to_chips([pack_filter(flat_filters, chips, offset) for offset in range(chips)])
-
-    share = out_weight.shape[1] // layers
-    own_weight = []
-    for step in range(layers):
-        sent = lax.dynamic_slice_in_dim(out_weight, (device // 2 ^ step) * share, share, 1)
-        pairs = [(source, source % 2 * layers + (source // 2 ^ step)) for source in range(parts)]
-        own_weight.append(lax.ppermute(sent, "seq", pairs))
-    weight = arrange(own_weight, [swapped(block, "seq", 1) for block in own_weight])
-
-    own = jnp.stack([block[0] for block in signals])
+    first = pack_signals(values_in, filter_spectrum.reshape(4, rows, width), chips, tuple(range(chips)))
+    second = pack_weights(after(gate_values, first[0]), out_weight, chips)
+    first = to_chips(first)
+    own = jnp.stack([after(block, second[0])[4] for block in first])
+    second = to_chips(second)
     spectrum = forward(own, swapped(own, "seq", 1), tables)
-    keep, send = backward(spectrum, filters, tables)
-    gated = gate(skip_gain[None, :], keep, swapped(send, "seq", 1), signals, pieces)
-
-    kept, firsts, seconds = [], [], []
+    keep, send = backward(spectrum, first, tables)
+    gated = gate(skip_gain[None, :], keep, swapped(send, "seq", 1), first, second, 2)
+    own_weight = collect([after(block, *gated) for block in second], out_weight.shape[0])
+    weight = arrange(own_weight, swapped(own_weight, "seq", 1))
+
+    kept, arrived, passed = [], [], []
     for piece in gated:
-        keep, passed, send = project(weight, to_chips([piece] * chips))
-        first = swapped(send, "chan", 1)
-        passed = (passed.astype(F32) + first[1].astype(F32)).astype(BF16)
+        keep, second_keep, send = project(weight, to_chips([piece] * chips))
         kept.append(keep)
-        firsts.append(first)
-        seconds.append(swapped(passed, "chan", 2))
-    return join(to_chips(finish(kept, firsts, seconds, chips)))
+        arrived.append(swapped(send, "chan", 1))
+        passed.append(swapped((second_keep.astype(F32) + arrived[-1][1].astype(F32)).astype(BF16), "chan", 2))
+    return join(to_chips(finish(kept, arrived, passed, chips)))
 
 
 def shards(values_in, gate_values, filter_spectrum, skip_gain, out_weight):

time: 95.6 us -> 89 us (0.931)
  waiting for transfers between devices: 35 us -> 53.8 us
  Pallas kernels: 20.5 us -> 10.2 us
  starting transfers between devices: 34.8 us -> 24.6 us
  local copies, waits for them, and re-layouts: 4.5 us -> 0.05 us
    ppermute x25 -> x22, waiting for transfers between devices: 34.8 us -> 53.8 us  [swapped(): lax.ppermute(value, axis, [(source, source ^ offset) for source in range(...]
    ppermute x4 -> x0, starting transfers between devices: 6.57 us -> none  [shards_direct(): own_weight.append(lax.ppermute(sent, 'seq', pairs))]
    pallas_call x6 -> x4, Pallas kernels: 9.66 us -> 4.14 us  [the longest x1 1.9 us: pack_signals(): pl.pallas_call(functools.partial(pack_signals_kernel, offsets), in_specs=...]
    ppermute x25 -> x22, starting transfers between devices: 28.2 us -> 24.6 us  [swapped(): lax.ppermute(value, axis, [(source, source ^ offset) for source in range(...]
    unnamed x46 -> x10, local copies, waits for them, and re-layouts: 3.47 us -> 0.02 us
    pallas_call x1, Pallas kernels: 2.14 us -> 0.16 us  [gate(): pl.pallas_call(functools.partial(gate_kernel, chips), in_specs=[WHOLE] *...]
    pallas_call x1, Pallas kernels: 1.96 us -> 0.1 us  [finish(): pl.pallas_call(functools.partial(finish_kernel, chips, pieces), in_specs=...]
    dynamic_slice x1 -> x0, local copies, waits for them, and re-layouts: 1 us -> none  [shards_direct(): lax.dynamic_slice_in_dim(out_weight, (device // 2 ^ step) * share, share, 1)]
  transfers between devices with their start and end apart: 29 -> 22, of which waited for: 12 -> 13; matrix products, arithmetic and copies ran while one was open for 1% -> 0% of each run, Pallas kernels for 15% -> 7%
where the time goes in v8:
time: 89 us; the launch traced here: 88.9 us
  waiting for transfers between devices  53.8 us (60%)
  starting transfers between devices  24.6 us (28%)
  Pallas kernels  10.2 us (11%)
    ppermute x22, waiting for transfers between devices, swapped(): lax.ppermute(value, axis, [(source, source ^ offset) for source in range(...  53.8 us
    ppermute x22, starting transfers between devices, swapped(): lax.ppermute(value, axis, [(source, source ^ offset) for source in range(...  24.6 us
    pallas_call x1, Pallas kernels, backward(): pl.pallas_call(functools.partial(backward_kernel, chips), in_specs=[WHOLE...  2.02 us
    pallas_call x1, Pallas kernels, pack_signals(): pl.pallas_call(functools.partial(pack_signals_kernel, offsets), in_specs=...  1.9 us
  transfers between devices with their start and end apart: 22, of which 13 were waited for; matrix products, arithmetic and copies ran while one was open for 0% of the time, Pallas kernels for 7%

profile of v8, /device:TPU:0, one launch (start us, length us, event | category | flops | bytes accessed | tf_op | source)
XLA Modules:
  0.0 88.9 jit_solution(17077720728449260965)
XLA Ops:
  0.0 1.9 %pack_signals.1 = (bf16[5,128,256]{2,1,0:T(8,128)(2,1)S(1)}, bf16[5,128,256]{2,1,0:T(8,128)(2,1)S(1)}, bf16[5,128,256]{2,1,0:T(8,128)(2,1)S(1)}, bf16[5,128,256]{2,1,0:T(8,128)(2,1)S(1)}) custom-call(f32[4,128,1024]{2,1,0:T(8,128)} %bitcast.13, bf16[128,1024]{1,0:T(8,128)(2,1)} %values_ref.1), custom_call_target="tpu_custom_call" | custom-call | tf_op jit(solution)/shard_map/pack_signals/pallas_call | solution.py:245
  1.9 4.0 %collective-permute-start.2 = (bf16[5,128,256]{2,1,0:T(8,128)(2,1)S(1)}, bf16[5,128,256]{2,1,0:T(8,128)(2,1)S(1)}, u32[]{:S(2)}, u32[]{:S(2)}) collective-permute-start(bf16[5,128,256]{2,1,0:T(8,128)(2,1)S(1)} %get-tuple-element.44), channel_id=1, source_target_pairs={{0,24},{4,28},{8,16},{12,20},{16,8},{20,12},{24,0},{28,4},{1,25},{... | collective-permute-start | bytes 983048 | tf_op jit(solution)/shard_map/ppermute | solution.py:599
  6.5 1.5 %pack_weights.1 = (bf16[640,256]{1,0:T(8,128)(2,1)S(1)}, bf16[640,256]{1,0:T(8,128)(2,1)S(1)}, bf16[640,256]{1,0:T(8,128)(2,1)S(1)}, bf16[640,256]{1,0:T(8,128)(2,1)S(1)}) custom-call(bf16[128,1024]{1,0:T(8,128)(2,1)} %gate_ref, bf16[1024,512]{1,0:T(8,128)(2,1)} %weight_ref.1), custom_call_target="tpu_custom_call" | custom-call | tf_op jit(solution)/shard_map/pack_weights/pallas_call | solution.py:285
  8.1 6.4 %collective-permute-done.2.refs_3_ = bf16[5,128,256]{2,1,0:T(8,128)(2,1)S(1)} collective-permute-done((bf16[5,128,256]{2,1,0:T(8,128)(2,1)S(1)}, bf16[5,128,256]{2,1,0:T(8,128)(2,1)S(1)}, u32[]{:S(2)}, u32[]{:S(2)}) %collective-permute-start.2) | collective-permute-done | bytes 327712 | tf_op jit(solution)/shard_map/ppermute | solution.py:599
  14.5 6.1 %collective-permute-done.1.refs_2_ = bf16[5,128,256]{2,1,0:T(8,128)(2,1)S(1)} collective-permute-done((bf16[5,128,256]{2,1,0:T(8,128)(2,1)S(1)}, bf16[5,128,256]{2,1,0:T(8,128)(2,1)S(1)}, u32[]{:S(2)}, u32[]{:S(2)}) %collective-permute-start.1) | collective-permute-done | bytes 327712 | tf_op jit(solution)/shard_map/ppermute | solution.py:599
  21.1 1.6 %collective-permute-start.5 = (bf16[640,256]{1,0:T(8,128)(2,1)S(1)}, bf16[640,256]{1,0:T(8,128)(2,1)S(1)}, u32[]{:S(2)}, u32[]{:S(2)}) collective-permute-start(bf16[640,256]{1,0:T(8,128)(2,1)S(1)} %get-tuple-element.48), channel_id=1, source_target_pairs={{0,8},{4,12},{8,0},{12,4},{16,24},{20,28},{24,16},{28,20},{1,9},{5... | collective-permute-start | bytes 983048 | tf_op jit(solution)/shard_map/ppermute | solution.py:599
  24.6 1.5 %forward.1.spectrum_ref = f32[256,2048]{1,0:T(8,128)S(1)} custom-call(f32[2,128,8]{2,1,0:T(8,128)S(1)} %copy-done.1, f32[2,128,8]{2,1,0:T(8,128)S(1)} %copy-done, bf16[256,256]{1,0:T(8,128)(2,1)S(1)} %copy-done.2, bf16[4,128,256]{2,1,0:T(8,128)(2,1)S(1)} %pad_maximum_fusion.own_ref, bf16[4,128,256]{2,1,0:T(8,128)(2,1)S(1)} %collective-permute-done.3.other_ref), custom_call_target="tpu_custom_call" | custom-call | tf_op jit(solution)/shard_map/forward/pallas_call | solution.py:347
  26.1 2.0 %backward.1 = (f32[4,128,256]{2,1,0:T(8,128)S(1)}, bf16[4,128,256]{2,1,0:T(8,128)(2,1)S(1)}) custom-call(f32[2,128,8]{2,1,0:T(8,128)S(1)} %copy-done.1, f32[2,128,8]{2,1,0:T(8,128)S(1)} %copy-done, bf16[256,256]{1,0:T(8,128)(2,1)S(1)} %copy-done.3, f32[256,2048]{1,0:T(8,128)S(1)} %forward.1.spectrum_ref, bf16[5,128,256]{2,1,0:T(8,128)(2,1)S(1)} %get-tuple-element.39.refs_0_, ...), custom_call_target="tpu_custom_call" | custom-call | tf_op jit(solution)/shard_map/backward/pallas_call | solution.py:421
  28.2 3.4 %collective-permute-done.5.refs_5_.refs_1_ = bf16[640,256]{1,0:T(8,128)(2,1)S(1)} collective-permute-done((bf16[640,256]{1,0:T(8,128)(2,1)S(1)}, bf16[640,256]{1,0:T(8,128)(2,1)S(1)}, u32[]{:S(2)}, u32[]{:S(2)}) %collective-permute-start.5) | collective-permute-done | bytes 327712 | tf_op jit(solution)/shard_map/ppermute | solution.py:599
  31.6 7.8 %collective-permute-done.6.refs_6_.refs_2_ = bf16[640,256]{1,0:T(8,128)(2,1)S(1)} collective-permute-done((bf16[640,256]{1,0:T(8,128)(2,1)S(1)}, bf16[640,256]{1,0:T(8,128)(2,1)S(1)}, u32[]{:S(2)}, u32[]{:S(2)}) %collective-permute-start.6) | collective-permute-done | bytes 327712 | tf_op jit(solution)/shard_map/ppermute | solution.py:599
  39.9 1.5 %collective-permute-start.14 = (bf16[256,256]{1,0:T(8,128)(2,1)S(1)}, bf16[256,256]{1,0:T(8,128)(2,1)S(1)}, u32[]{:S(2)}, u32[]{:S(2)}) collective-permute-start(bf16[256,256]{1,0:T(8,128)(2,1)S(1)} %get-tuple-element.52.refs_0_), channel_id=1, source_target_pairs={{0,24},{4,28},{8,16},{12,20},{16,8},{20,12},{24,0},{28,4},{1,25},{... | collective-permute-start | bytes 393224 | tf_op jit(solution)/shard_map/ppermute | solution.py:599
  41.9 1.5 %collective-permute-start.12 = (bf16[256,256]{1,0:T(8,128)(2,1)S(1)}, bf16[256,256]{1,0:T(8,128)(2,1)S(1)}, u32[]{:S(2)}, u32[]{:S(2)}) collective-permute-start(bf16[256,256]{1,0:T(8,128)(2,1)S(1)} %get-tuple-element.52.refs_0_), channel_id=1, source_target_pairs={{0,8},{4,12},{8,0},{12,4},{16,24},{20,28},{24,16},{28,20},{1,9},{5... | collective-permute-start | bytes 393224 | tf_op jit(solution)/shard_map/ppermute | solution.py:599
  44.0 3.2 %collective-permute-done.14.refs_3_ = bf16[256,256]{1,0:T(8,128)(2,1)S(1)} collective-permute-done((bf16[256,256]{1,0:T(8,128)(2,1)S(1)}, bf16[256,256]{1,0:T(8,128)(2,1)S(1)}, u32[]{:S(2)}, u32[]{:S(2)}) %collective-permute-start.14) | collective-permute-done | bytes 131104 | tf_op jit(solution)/shard_map/ppermute | solution.py:599
  47.2 2.3 %collective-permute-done.13.refs_2_ = bf16[256,256]{1,0:T(8,128)(2,1)S(1)} collective-permute-done((bf16[256,256]{1,0:T(8,128)(2,1)S(1)}, bf16[256,256]{1,0:T(8,128)(2,1)S(1)}, u32[]{:S(2)}, u32[]{:S(2)}) %collective-permute-start.13) | collective-permute-done | bytes 131104 | tf_op jit(solution)/shard_map/ppermute | solution.py:599
  50.3 1.6 %collective-permute-start.16 = (bf16[2,256,256]{2,1,0:T(8,128)(2,1)S(1)}, bf16[2,256,256]{2,1,0:T(8,128)(2,1)S(1)}, u32[]{:S(2)}, u32[]{:S(2)}) collective-permute-start(bf16[2,256,256]{2,1,0:T(8,128)(2,1)S(1)} %get-tuple-element.60), channel_id=1, source_target_pairs={{0,1},{1,0},{2,3},{3,2},{4,5},{5,4},{6,7},{7,6},{8,9},{9,8},{10,11... | collective-permute-start | bytes 786440 | tf_op jit(solution)/shard_map/ppermute | solution.py:599
  53.9 1.5 %collective-permute-start.9 = (bf16[256,256]{1,0:T(8,128)(2,1)S(1)}, bf16[256,256]{1,0:T(8,128)(2,1)S(1)}, u32[]{:S(2)}, u32[]{:S(2)}) collective-permute-start(bf16[256,256]{1,0:T(8,128)(2,1)S(1)} %get-tuple-element.51.refs_0_), channel_id=1, source_target_pairs={{0,8},{4,12},{8,0},{12,4},{16,24},{20,28},{24,16},{28,20},{1,9},{5... | collective-permute-start | bytes 393224 | tf_op jit(solution)/shard_map/ppermute | solution.py:599
  55.4 3.8 %collective-permute-done.11.refs_3_ = bf16[256,256]{1,0:T(8,128)(2,1)S(1)} collective-permute-done((bf16[256,256]{1,0:T(8,128)(2,1)S(1)}, bf16[256,256]{1,0:T(8,128)(2,1)S(1)}, u32[]{:S(2)}, u32[]{:S(2)}) %collective-permute-start.11) | collective-permute-done | bytes 131104 | tf_op jit(solution)/shard_map/ppermute | solution.py:599
  59.2 1.6 %collective-permute-done.10.refs_2_ = bf16[256,256]{1,0:T(8,128)(2,1)S(1)} collective-permute-done((bf16[256,256]{1,0:T(8,128)(2,1)S(1)}, bf16[256,256]{1,0:T(8,128)(2,1)S(1)}, u32[]{:S(2)}, u32[]{:S(2)}) %collective-permute-start.10) | collective-permute-done | bytes 131104 | tf_op jit(solution)/shard_map/ppermute | solution.py:599
  62.1 2.7 %collective-permute-start.18 = (bf16[256,256]{1,0:T(8,128)(2,1)S(1)}, bf16[256,256]{1,0:T(8,128)(2,1)S(1)}, u32[]{:S(2)}, u32[]{:S(2)}) collective-permute-start(bf16[256,256]{1,0:T(8,128)(2,1)S(1)} %fusion), channel_id=1, source_target_pairs={{0,2},{1,3},{2,0},{3,1},{4,6},{5,7},{6,4},{7,5},{8,10},{9,11},{10,... | collective-permute-start | bytes 393224 | tf_op jit(solution)/shard_map/ppermute | solution.py:599
  64.8 7.9 %collective-permute-done.15.refs_2_ = bf16[2,256,256]{2,1,0:T(8,128)(2,1)S(1)} collective-permute-done((bf16[2,256,256]{2,1,0:T(8,128)(2,1)S(1)}, bf16[2,256,256]{2,1,0:T(8,128)(2,1)S(1)}, u32[]{:S(2)}, u32[]{:S(2)}) %collective-permute-start.15) | collective-permute-done | bytes 262176 | tf_op jit(solution)/shard_map/ppermute | solution.py:599
  73.5 7.4 %collective-permute-done.17.refs_4_ = bf16[256,256]{1,0:T(8,128)(2,1)S(1)} collective-permute-done((bf16[256,256]{1,0:T(8,128)(2,1)S(1)}, bf16[256,256]{1,0:T(8,128)(2,1)S(1)}, u32[]{:S(2)}, u32[]{:S(2)}) %collective-permute-start.17) | collective-permute-done | bytes 131104 | tf_op jit(solution)/shard_map/ppermute | solution.py:599
  81.4 1.5 %collective-permute-start.20 = (bf16[128,256]{1,0:T(8,128)(2,1)S(1)}, bf16[128,256]{1,0:T(8,128)(2,1)S(1)}, u32[]{:S(2)}, u32[]{:S(2)}) collective-permute-start(bf16[128,256]{1,0:T(8,128)(2,1)S(1)} %get-tuple-element.65), channel_id=1, source_target_pairs={{0,16},{4,20},{8,24},{12,28},{16,0},{20,4},{24,8},{28,12},{1,17},{... | collective-permute-start | bytes 196616 | tf_op jit(solution)/shard_map/ppermute | solution.py:599
  82.9 1.6 %collective-permute-start.21 = (bf16[128,256]{1,0:T(8,128)(2,1)S(1)}, bf16[128,256]{1,0:T(8,128)(2,1)S(1)}, u32[]{:S(2)}, u32[]{:S(2)}) collective-permute-start(bf16[128,256]{1,0:T(8,128)(2,1)S(1)} %get-tuple-element.66), channel_id=1, source_target_pairs={{0,24},{4,28},{8,16},{12,20},{16,8},{20,12},{24,0},{28,4},{1,25},{... | collective-permute-start | bytes 196616 | tf_op jit(solution)/shard_map/ppermute | solution.py:599
  85.7 2.4 %collective-permute-done.21.refs_3_ = bf16[128,256]{1,0:T(8,128)(2,1)S(1)} collective-permute-done((bf16[128,256]{1,0:T(8,128)(2,1)S(1)}, bf16[128,256]{1,0:T(8,128)(2,1)S(1)}, u32[]{:S(2)}, u32[]{:S(2)}) %collective-permute-start.21) | collective-permute-done | bytes 65568 | tf_op jit(solution)/shard_map/ppermute | solution.py:599
  (48 shorter events, 12.2 us)
Async XLA Ops:
  0.0 24.6 %copy-start.1 = (f32[2,128,8]{2,1,0:T(8,128)S(1)}, f32[2,128,8]{2,1,0:T(8,128)}, u32[]{:S(2)}) copy-start(f32[2,128,8]{2,1,0:T(8,128)} %constant.8.clone.cos_ref) | copy-start | bytes 24580
  0.0 24.6 %copy-start.2 = (bf16[256,256]{1,0:T(8,128)(2,1)S(1)}, bf16[256,256]{1,0:T(8,128)(2,1)}, u32[]{:S(2)}) copy-start(bf16[256,256]{1,0:T(8,128)(2,1)} %constant.10.clone.table_ref) | copy-start | bytes 393220
  1.9 12.6 %collective-permute-start.2 = (bf16[5,128,256]{2,1,0:T(8,128)(2,1)S(1)}, bf16[5,128,256]{2,1,0:T(8,128)(2,1)S(1)}, u32[]{:S(2)}, u32[]{:S(2)}) collective-permute-start(bf16[5,128,256]{2,1,0:T(8,128)(2,1)S(1)} %get-tuple-element.44), channel_id=1, source_target_pairs={{0,24},{4,28},{8,16},{12,20},{16,8},{20,12},{24,0},{28,4},{1,25},{... | collective-permute-start | bytes 983048 | tf_op jit(solution)/shard_map/ppermute | solution.py:599
  5.9 14.7 %collective-permute-start.1 = (bf16[5,128,256]{2,1,0:T(8,128)(2,1)S(1)}, bf16[5,128,256]{2,1,0:T(8,128)(2,1)S(1)}, u32[]{:S(2)}, u32[]{:S(2)}) collective-permute-start(bf16[5,128,256]{2,1,0:T(8,128)(2,1)S(1)} %get-tuple-element.42), channel_id=1, source_target_pairs={{0,16},{4,20},{8,24},{12,28},{16,0},{20,4},{24,8},{28,12},{1,17},{... | collective-permute-start | bytes 983048 | tf_op jit(solution)/shard_map/ppermute | solution.py:599
  6.4 14.5 %collective-permute-start = (bf16[5,128,256]{2,1,0:T(8,128)(2,1)S(1)}, bf16[5,128,256]{2,1,0:T(8,128)(2,1)S(1)}, u32[]{:S(2)}, u32[]{:S(2)}) collective-permute-start(bf16[5,128,256]{2,1,0:T(8,128)(2,1)S(1)} %get-tuple-element.40), channel_id=1, source_target_pairs={{0,8},{4,12},{8,0},{12,4},{16,24},{20,28},{24,16},{28,20},{1,9},{5... | collective-permute-start | bytes 983048 | tf_op jit(solution)/shard_map/ppermute | solution.py:599
  21.0 3.6 %collective-permute-start.3 = (bf16[4,128,256]{2,1,0:T(8,128)(2,1)S(1)}, bf16[4,128,256]{2,1,0:T(8,128)(2,1)S(1)}, u32[]{:S(2)}, u32[]{:S(2)}) collective-permute-start(bf16[4,128,256]{2,1,0:T(8,128)(2,1)S(1)} %pad_maximum_fusion.own_ref), channel_id=1, source_target_pairs={{0,4},{4,0},{8,12},{12,8},{16,20},{20,16},{24,28},{28,24},{1,5},{5... | collective-permute-start | bytes 786440 | tf_op jit(solution)/shard_map/ppermute | solution.py:599
  21.1 10.6 %collective-permute-start.5 = (bf16[640,256]{1,0:T(8,128)(2,1)S(1)}, bf16[640,256]{1,0:T(8,128)(2,1)S(1)}, u32[]{:S(2)}, u32[]{:S(2)}) collective-permute-start(bf16[640,256]{1,0:T(8,128)(2,1)S(1)} %get-tuple-element.48), channel_id=1, source_target_pairs={{0,8},{4,12},{8,0},{12,4},{16,24},{20,28},{24,16},{28,20},{1,9},{5... | collective-permute-start | bytes 983048 | tf_op jit(solution)/shard_map/ppermute | solution.py:599
  22.6 16.8 %collective-permute-start.6 = (bf16[640,256]{1,0:T(8,128)(2,1)S(1)}, bf16[640,256]{1,0:T(8,128)(2,1)S(1)}, u32[]{:S(2)}, u32[]{:S(2)}) collective-permute-start(bf16[640,256]{1,0:T(8,128)(2,1)S(1)} %get-tuple-element.49), channel_id=1, source_target_pairs={{0,16},{4,20},{8,24},{12,28},{16,0},{20,4},{24,8},{28,12},{1,17},{... | collective-permute-start | bytes 983048 | tf_op jit(solution)/shard_map/ppermute | solution.py:599
  23.2 16.2 %collective-permute-start.7 = (bf16[640,256]{1,0:T(8,128)(2,1)S(1)}, bf16[640,256]{1,0:T(8,128)(2,1)S(1)}, u32[]{:S(2)}, u32[]{:S(2)}) collective-permute-start(bf16[640,256]{1,0:T(8,128)(2,1)S(1)} %get-tuple-element.50), channel_id=1, source_target_pairs={{0,24},{4,28},{8,16},{12,20},{16,8},{20,12},{24,0},{28,4},{1,25},{... | collective-permute-start | bytes 983048 | tf_op jit(solution)/shard_map/ppermute | solution.py:599
  28.2 11.3 %collective-permute-start.4 = (bf16[4,128,256]{2,1,0:T(8,128)(2,1)S(1)}, bf16[4,128,256]{2,1,0:T(8,128)(2,1)S(1)}, u32[]{:S(2)}, u32[]{:S(2)}) collective-permute-start(bf16[4,128,256]{2,1,0:T(8,128)(2,1)S(1)} %get-tuple-element.47), channel_id=1, source_target_pairs={{0,4},{4,0},{8,12},{12,8},{16,20},{20,16},{24,28},{28,24},{1,5},{5... | collective-permute-start | bytes 786440 | tf_op jit(solution)/shard_map/ppermute | solution.py:599
  39.8 3.6 %collective-permute-start.8 = (bf16[4,1024,128]{2,1,0:T(8,128)(2,1)S(1)}, bf16[4,1024,128]{2,1,0:T(8,128)(2,1)S(1)}, u32[]{:S(2)}, u32[]{:S(2)}) collective-permute-start(bf16[4,1024,128]{2,1,0:T(8,128)(2,1)S(1)} %collect_weights.1.own_ref), channel_id=1, source_target_pairs={{0,4},{4,0},{8,12},{12,8},{16,20},{20,16},{24,28},{28,24},{1,5},{5... | collective-permute-start | bytes 3145736 | tf_op jit(solution)/shard_map/ppermute | solution.py:599
  39.9 7.3 %collective-permute-start.14 = (bf16[256,256]{1,0:T(8,128)(2,1)S(1)}, bf16[256,256]{1,0:T(8,128)(2,1)S(1)}, u32[]{:S(2)}, u32[]{:S(2)}) collective-permute-start(bf16[256,256]{1,0:T(8,128)(2,1)S(1)} %get-tuple-element.52.refs_0_), channel_id=1, source_target_pairs={{0,24},{4,28},{8,16},{12,20},{16,8},{20,12},{24,0},{28,4},{1,25},{... | collective-permute-start | bytes 393224 | tf_op jit(solution)/shard_map/ppermute | solution.py:599
  41.3 8.2 %collective-permute-start.13 = (bf16[256,256]{1,0:T(8,128)(2,1)S(1)}, bf16[256,256]{1,0:T(8,128)(2,1)S(1)}, u32[]{:S(2)}, u32[]{:S(2)}) collective-permute-start(bf16[256,256]{1,0:T(8,128)(2,1)S(1)} %get-tuple-element.52.refs_0_), channel_id=1, source_target_pairs={{0,16},{4,20},{8,24},{12,28},{16,0},{20,4},{24,8},{28,12},{1,17},{... | collective-permute-start | bytes 393224 | tf_op jit(solution)/shard_map/ppermute | solution.py:599
  41.9 7.6 %collective-permute-start.12 = (bf16[256,256]{1,0:T(8,128)(2,1)S(1)}, bf16[256,256]{1,0:T(8,128)(2,1)S(1)}, u32[]{:S(2)}, u32[]{:S(2)}) collective-permute-start(bf16[256,256]{1,0:T(8,128)(2,1)S(1)} %get-tuple-element.52.refs_0_), channel_id=1, source_target_pairs={{0,8},{4,12},{8,0},{12,4},{16,24},{20,28},{24,16},{28,20},{1,9},{5... | collective-permute-start | bytes 393224 | tf_op jit(solution)/shard_map/ppermute | solution.py:599
  50.3 11.8 %collective-permute-start.16 = (bf16[2,256,256]{2,1,0:T(8,128)(2,1)S(1)}, bf16[2,256,256]{2,1,0:T(8,128)(2,1)S(1)}, u32[]{:S(2)}, u32[]{:S(2)}) collective-permute-start(bf16[2,256,256]{2,1,0:T(8,128)(2,1)S(1)} %get-tuple-element.60), channel_id=1, source_target_pairs={{0,1},{1,0},{2,3},{3,2},{4,5},{5,4},{6,7},{7,6},{8,9},{9,8},{10,11... | collective-permute-start | bytes 786440 | tf_op jit(solution)/shard_map/ppermute | solution.py:599
  51.9 7.3 %collective-permute-start.11 = (bf16[256,256]{1,0:T(8,128)(2,1)S(1)}, bf16[256,256]{1,0:T(8,128)(2,1)S(1)}, u32[]{:S(2)}, u32[]{:S(2)}) collective-permute-start(bf16[256,256]{1,0:T(8,128)(2,1)S(1)} %get-tuple-element.51.refs_0_), channel_id=1, source_target_pairs={{0,24},{4,28},{8,16},{12,20},{16,8},{20,12},{24,0},{28,4},{1,25},{... | collective-permute-start | bytes 393224 | tf_op jit(solution)/shard_map/ppermute | solution.py:599
  53.3 7.5 %collective-permute-start.10 = (bf16[256,256]{1,0:T(8,128)(2,1)S(1)}, bf16[256,256]{1,0:T(8,128)(2,1)S(1)}, u32[]{:S(2)}, u32[]{:S(2)}) collective-permute-start(bf16[256,256]{1,0:T(8,128)(2,1)S(1)} %get-tuple-element.51.refs_0_), channel_id=1, source_target_pairs={{0,16},{4,20},{8,24},{12,28},{16,0},{20,4},{24,8},{28,12},{1,17},{... | collective-permute-start | bytes 393224 | tf_op jit(solution)/shard_map/ppermute | solution.py:599
  53.9 6.9 %collective-permute-start.9 = (bf16[256,256]{1,0:T(8,128)(2,1)S(1)}, bf16[256,256]{1,0:T(8,128)(2,1)S(1)}, u32[]{:S(2)}, u32[]{:S(2)}) collective-permute-start(bf16[256,256]{1,0:T(8,128)(2,1)S(1)} %get-tuple-element.51.refs_0_), channel_id=1, source_target_pairs={{0,8},{4,12},{8,0},{12,4},{16,24},{20,28},{24,16},{28,20},{1,9},{5... | collective-permute-start | bytes 393224 | tf_op jit(solution)/shard_map/ppermute | solution.py:599
  61.6 11.1 %collective-permute-start.15 = (bf16[2,256,256]{2,1,0:T(8,128)(2,1)S(1)}, bf16[2,256,256]{2,1,0:T(8,128)(2,1)S(1)}, u32[]{:S(2)}, u32[]{:S(2)}) collective-permute-start(bf16[2,256,256]{2,1,0:T(8,128)(2,1)S(1)} %get-tuple-element.59), channel_id=1, source_target_pairs={{0,1},{1,0},{2,3},{3,2},{4,5},{5,4},{6,7},{7,6},{8,9},{9,8},{10,11... | collective-permute-start | bytes 786440 | tf_op jit(solution)/shard_map/ppermute | solution.py:599
  62.1 11.4 %collective-permute-start.18 = (bf16[256,256]{1,0:T(8,128)(2,1)S(1)}, bf16[256,256]{1,0:T(8,128)(2,1)S(1)}, u32[]{:S(2)}, u32[]{:S(2)}) collective-permute-start(bf16[256,256]{1,0:T(8,128)(2,1)S(1)} %fusion), channel_id=1, source_target_pairs={{0,2},{1,3},{2,0},{3,1},{4,6},{5,7},{6,4},{7,5},{8,10},{9,11},{10,... | collective-permute-start | bytes 393224 | tf_op jit(solution)/shard_map/ppermute | solution.py:599
  72.7 8.2 %collective-permute-start.17 = (bf16[256,256]{1,0:T(8,128)(2,1)S(1)}, bf16[256,256]{1,0:T(8,128)(2,1)S(1)}, u32[]{:S(2)}, u32[]{:S(2)}) collective-permute-start(bf16[256,256]{1,0:T(8,128)(2,1)S(1)} %fusion.1), channel_id=1, source_target_pairs={{0,2},{1,3},{2,0},{3,1},{4,6},{5,7},{6,4},{7,5},{8,10},{9,11},{10,... | collective-permute-start | bytes 393224 | tf_op jit(solution)/shard_map/ppermute | solution.py:599
  81.0 4.7 %collective-permute-start.19 = (bf16[128,256]{1,0:T(8,128)(2,1)S(1)}, bf16[128,256]{1,0:T(8,128)(2,1)S(1)}, u32[]{:S(2)}, u32[]{:S(2)}) collective-permute-start(bf16[128,256]{1,0:T(8,128)(2,1)S(1)} %get-tuple-element.64), channel_id=1, source_target_pairs={{0,8},{4,12},{8,0},{12,4},{16,24},{20,28},{24,16},{28,20},{1,9},{5... | collective-permute-start | bytes 196616 | tf_op jit(solution)/shard_map/ppermute | solution.py:599
  81.4 4.3 %collective-permute-start.20 = (bf16[128,256]{1,0:T(8,128)(2,1)S(1)}, bf16[128,256]{1,0:T(8,128)(2,1)S(1)}, u32[]{:S(2)}, u32[]{:S(2)}) collective-permute-start(bf16[128,256]{1,0:T(8,128)(2,1)S(1)} %get-tuple-element.65), channel_id=1, source_target_pairs={{0,16},{4,20},{8,24},{12,28},{16,0},{20,4},{24,8},{28,12},{1,17},{... | collective-permute-start | bytes 196616 | tf_op jit(solution)/shard_map/ppermute | solution.py:599
  82.9 5.2 %collective-permute-start.21 = (bf16[128,256]{1,0:T(8,128)(2,1)S(1)}, bf16[128,256]{1,0:T(8,128)(2,1)S(1)}, u32[]{:S(2)}, u32[]{:S(2)}) collective-permute-start(bf16[128,256]{1,0:T(8,128)(2,1)S(1)} %get-tuple-element.66), channel_id=1, source_target_pairs={{0,24},{4,28},{8,16},{12,20},{16,8},{20,12},{24,0},{28,4},{1,25},{... | collective-permute-start | bytes 196616 | tf_op jit(solution)/shard_map/ppermute | solution.py:599
  (3 other events, 56.0 us)

commit v9 on v8

--- a/solution.py
+++ b/solution.py
@@ -257,41 +257,31 @@
     )(*(pltpu.with_memory_space_constraint(array, pltpu.HBM) for array in (filters, values_in)))
 
 
-def pack_weights_kernel(chips, gate_ref, weight_ref, *refs):
+def pack_gates_kernel(chips, gate_ref, *refs):
     out_refs, arrived = refs[:chips], refs[chips]
     chip, _ = own_place()
-    rows = gate_ref.shape[0]
-    depth, held = weight_ref.shape
-    half, share = depth // 2, held // chips
     copies = []
-    for offset in range(chips):
-        out_ref, target = out_refs[offset], chip ^ offset
-        gates = gate_ref.at[:, block_at(target, out_ref.shape[1])]
-        copies.append(pltpu.make_async_copy(gates, out_ref.at[pl.ds(0, rows)], arrived.at[offset, 2]))
-        for part in range(2):
-            source = weight_ref.at[pl.ds(part * half, half), block_at(target, share)]
-            sink = out_ref.at[pl.ds(rows, half), pl.ds(part * share, share)]
-            copies.append(pltpu.make_async_copy(source, sink, arrived.at[offset, part]))
+    for offset, out_ref in enumerate(out_refs):
+        gates = gate_ref.at[:, block_at(chip ^ offset, out_ref.shape[1])]
+        copies.append(pltpu.make_async_copy(gates, out_ref, arrived.at[offset]))
     for copy in copies:
         copy.start()
     for copy in copies:
         copy.wait()
 
 
-def pack_weights(gate_values, weight, chips):
+def pack_gates(gate_values, chips):
     rows, width = gate_values.shape
-    depth, held = weight.shape
-    shape = (rows + depth // 2, 2 * held // chips)
-    return pl.pallas_call(
-        functools.partial(pack_weights_kernel, chips),
-        in_specs=[pl.BlockSpec(memory_space=pltpu.HBM)] * 2,
+    return pl.pallas_call(
+        functools.partial(pack_gates_kernel, chips),
+        in_specs=[pl.BlockSpec(memory_space=pltpu.HBM)],
         out_specs=[WHOLE] * chips,
-        out_shape=[jax.ShapeDtypeStruct(shape, BF16)] * chips,
-        scratch_shapes=[pltpu.SemaphoreType.DMA((chips, 3))],
+        out_shape=[jax.ShapeDtypeStruct((rows, width // chips), BF16)] * chips,
+        scratch_shapes=[pltpu.SemaphoreType.DMA((chips,))],
         cost_estimate=CHEAP,
-        compiler_params=pltpu.CompilerParams(vmem_limit_bytes=8 * 2**20),
-        name="pack_weights",
-    )(*(pltpu.with_memory_space_constraint(array, pltpu.HBM) for array in (gate_values, weight)))
+        compiler_params=pltpu.CompilerParams(vmem_limit_bytes=4 * 2**20),
+        name="pack_gates",
+    )(pltpu.with_memory_space_constraint(gate_values, pltpu.HBM))
 
 
 def forward_kernel(chips, cos_ref, sin_ref, table_ref, own_ref, other_ref, out_ref, signal_ref, waves_ref):
@@ -435,162 +425,61 @@
 
 
 def gate_kernel(chips, skip_ref, keep_ref, arrived_ref, *refs):
-    signal_refs, gate_refs, out_refs = refs[:chips], refs[chips : 2 * chips], refs[2 * chips :]
+    signal_refs, gate_refs, out_ref = refs[:chips], refs[chips : 2 * chips], refs[2 * chips]
     chip, _ = own_place()
     rows, lanes = keep_ref.shape[1:]
-    step = rows // len(out_refs)
     skip = skip_ref[:, block_at(chip, lanes)]
     for offset in range(chips):
         block = chip ^ offset
-        for piece, out_ref in enumerate(out_refs):
-            here = pl.ds(piece * step, step)
-            convolved = keep_ref[block, here, :] + arrived_ref[block, here, :].astype(F32)
-            signal = signal_refs[offset][4, here, :].astype(F32)
-            gate = gate_refs[offset][here, :].astype(F32)
-            out_ref[block_at(block, step), :] = (gate * (convolved + skip * signal)).astype(BF16)
-
-
-def gate(skip, keep, arrived, first, second, pieces):
+        convolved = keep_ref[block] + arrived_ref[block].astype(F32)
+        signal = signal_refs[offset][4].astype(F32)
+        gate = gate_refs[offset][...].astype(F32)
+        out_ref[block_at(block, rows), :] = (gate * (convolved + skip * signal)).astype(BF16)
+
+
+def gate(skip, keep, arrived, first, gates):
     chips, rows, lanes = keep.shape
     return pl.pallas_call(
         functools.partial(gate_kernel, chips),
         in_specs=[WHOLE] * (3 + 2 * chips),
-        out_specs=[WHOLE] * pieces,
-        out_shape=[jax.ShapeDtypeStruct((chips * rows // pieces, lanes), BF16)] * pieces,
+        out_specs=WHOLE,
+        out_shape=jax.ShapeDtypeStruct((chips * rows, lanes), BF16),
         cost_estimate=CHEAP,
         compiler_params=pltpu.CompilerParams(vmem_limit_bytes=6 * 2**20),
         name="gate",
-    )(skip, keep, arrived, *first, *second)
-
-
-def collect_kernel(chips, *refs):
-    in_refs, out_ref = refs[:chips], refs[chips]
-    chip, _ = own_place()
+    )(skip, keep, arrived, *first, *gates)
+
+
+def project_kernel(chips, own_ref, other_ref, *refs):
+    gated_refs, out_refs, (joined_ref, weight_ref) = refs[:chips], refs[chips : 2 * chips], refs[2 * chips :]
+    chip, core = own_place()
     layer = lax.axis_index("chan")
-    depth, share = out_ref.shape[1:]
-    half = depth // 2
-    start = in_refs[0].shape[0] - half
-    for offset in range(chips):
-        for part in range(2):
-            block = in_refs[offset][pl.ds(start, half), pl.ds(part * share, share)]
-            out_ref[chip ^ layer ^ offset, pl.ds(part * half, half), :] = block
-
-
-def collect(second, depth):
-    chips = len(second)
-    return pl.pallas_call(
-        functools.partial(collect_kernel, chips),
-        in_specs=[WHOLE] * chips,
-        out_specs=WHOLE,
-        out_shape=jax.ShapeDtypeStruct((chips, depth, second[0].shape[1] // 2), BF16),
-        cost_estimate=CHEAP,
-        compiler_params=pltpu.CompilerParams(vmem_limit_bytes=4 * 2**20),
-        name="collect_weights",
-    )(*second)
-
-
-def arrange_kernel(own_ref, other_ref, out_ref):
-    _, core = own_place()
-    share = own_ref.shape[2]
-    out_ref[:, :, block_at(core, share)] = own_ref[...]
-    out_ref[:, :, block_at(1 - core, share)] = other_ref[...]
-
-
-def arrange(own, other):
-    layers, rows, share = own.shape
-    return pl.pallas_call(
-        arrange_kernel,
-        in_specs=[WHOLE] * 2,
-        out_specs=WHOLE,
-        out_shape=jax.ShapeDtypeStruct((layers, rows, 2 * share), BF16),
-        cost_estimate=CHEAP,
-        compiler_params=pltpu.CompilerParams(vmem_limit_bytes=8 * 2**20),
-        name="arrange_weights",
-    )(own, other)
-
-
-def project_kernel(chips, weight_ref, *refs):
-    gated_refs, (keep_ref, pass_ref, send_ref, joined_ref) = refs[:chips], refs[chips:]
-    chip, _ = own_place()
+    held = own_ref.shape[1]
     lanes = gated_refs[0].shape[1]
+    rows = out_refs[0].shape[0]
     for offset in range(chips):
         joined_ref[:, block_at(chip ^ offset, lanes)] = gated_refs[offset][...]
-
-    def partial_of(target):
-        return jnp.dot(joined_ref[...], weight_ref[target], preferred_element_type=F32).astype(BF16)
-
-    send_ref[0] = partial_of(1)
-    send_ref[1] = partial_of(3)
-    pass_ref[...] = partial_of(2)
-    keep_ref[...] = partial_of(0)
-
-
-def project(weight, gated):
+    weight_ref[:, block_at(core, held)] = own_ref[...]
+    weight_ref[:, block_at(1 - core, held)] = other_ref[...]
+    for step in range(chips):
+        gated = joined_ref[block_at(chip ^ layer ^ step, rows), :]
+        out_refs[step][...] = jnp.dot(gated, weight_ref[...], preferred_element_type=F32).astype(BF16)
+
+
+def project(own, other, gated):
     chips = len(gated)
-    _, depth, columns = weight.shape
-    rows = gated[0].shape[0]
-    block = jax.ShapeDtypeStruct((rows, columns), BF16)
+    depth, held = own.shape
+    rows = gated[0].shape[0] // chips
     return pl.pallas_call(
         functools.partial(project_kernel, chips),
-        in_specs=[WHOLE] * (1 + chips),
-        out_specs=[WHOLE] * 3,
-        out_shape=[block, block, jax.ShapeDtypeStruct((2, rows, columns), BF16)],
-        scratch_shapes=[pltpu.VMEM((rows, depth), BF16)],
+        in_specs=[WHOLE] * (2 + chips),
+        out_specs=[WHOLE] * chips,
+        out_shape=[jax.ShapeDtypeStruct((rows, 2 * held), BF16)] * chips,
+        scratch_shapes=[pltpu.VMEM((rows * chips, depth), BF16), pltpu.VMEM((depth, 2 * held), BF16)],
         cost_estimate=CHEAP,
-        compiler_params=pltpu.CompilerParams(vmem_limit_bytes=8 * 2**20),
+        compiler_params=pltpu.CompilerParams(vmem_limit_bytes=12 * 2**20),
         name="project",
-    )(weight, *gated)
-
-
-def finish_kernel(chips, pieces, *refs):
-    keep_refs, first_refs, second_refs = refs[:pieces], refs[pieces : 2 * pieces], refs[2 * pieces : 3 * pieces]
-    out_refs = refs[3 * pieces :]
-    chip, _ = own_place()
-    step = keep_refs[0].shape[0] // chips
-    for offset in range(chips):
-        here = block_at(chip ^ offset, step)
-        for piece in range(pieces):
-            total = keep_refs[piece][here, :].astype(F32) + first_refs[piece][0, here, :].astype(F32)
-            total = total + second_refs[piece][here, :].astype(F32)
-            out_refs[offset][pl.ds(piece * step, step), :] = total.astype(BF16)
-
-
-def finish(keep, first, second, chips):
-    pieces = len(keep)
-    rows, columns = keep[0].shape
-    return pl.pallas_call(
-        functools.partial(finish_kernel, chips, pieces),
-        in_specs=[WHOLE] * (3 * pieces),
-        out_specs=[WHOLE] * chips,
-        out_shape=[jax.ShapeDtypeStruct((rows * pieces // chips, columns), BF16)] * chips,
-        cost_estimate=CHEAP,
-        compiler_params=pltpu.CompilerParams(vmem_limit_bytes=4 * 2**20),
-        name="finish",
-    )(*keep, *first, *second)
-
-
-def join_kernel(chips, *refs):
-    in_refs, out_ref = refs[:chips], refs[chips]
-    chip, _ = own_place()
-    share = in_refs[0].shape[1] // 2
-    for offset in range(chips):
-        for part in range(2):
-            block = in_refs[offset][:, pl.ds(part * share, share)]
-            out_ref[:, block_at(part * chips + (chip ^ offset), share)] = block
-
-
-def join(blocks):
-    chips = len(blocks)
-    rows, columns = blocks[0].shape
-    return pl.pallas_call(
-        functools.partial(join_kernel, chips),
-        in_specs=[WHOLE] * chips,
-        out_specs=WHOLE,
-        out_shape=jax.ShapeDtypeStruct((rows, chips * columns), BF16),
-        cost_estimate=CHEAP,
-        compiler_params=pltpu.CompilerParams(vmem_limit_bytes=2 * 2**20),
-        name="join",
-    )(*blocks)
+    )(own, other, *gated)
 
 
 def swapped(value, axis, offset):
@@ -605,6 +494,20 @@
 
 def after(value, *others):
     return lax.optimization_barrier((value, *others))[0]
+
+
+def to_layers(partials):
+    chips = len(partials)
+    arrived = []
+    for step, partial in enumerate(partials):
+        pairs = []
+        for chip in range(chips):
+            for core in range(2):
+                for layer in range(chips):
+                    source = (2 * chip + core) * chips + layer
+                    pairs.append((source, (2 * (chip ^ layer ^ step) + core) * chips + chip))
+        arrived.append(lax.ppermute(partial, ("seq", "chan"), pairs))
+    return arrived
 
 
 def shards_direct(values_in, gate_values, filter_spectrum, skip_gain, out_weight):
@@ -614,23 +517,20 @@
     tables = small_tables(parts, rows)
 
     first = pack_signals(values_in, filter_spectrum.reshape(4, rows, width), chips, tuple(range(chips)))
-    second = pack_weights(after(gate_values, first[0]), out_weight, chips)
+    gates = pack_gates(after(gate_values, first[0]), chips)
     first = to_chips(first)
-    own = jnp.stack([after(block, second[0])[4] for block in first])
-    second = to_chips(second)
+    own = jnp.stack([after(block, gates[0])[4] for block in first])
+    gates = to_chips(gates)
     spectrum = forward(own, swapped(own, "seq", 1), tables)
     keep, send = backward(spectrum, first, tables)
-    gated = gate(skip_gain[None, :], keep, swapped(send, "seq", 1), first, second, 2)
-    own_weight = collect([after(block, *gated) for block in second], out_weight.shape[0])
-    weight = arrange(own_weight, swapped(own_weight, "seq", 1))
-
-    kept, arrived, passed = [], [], []
-    for piece in gated:
-        keep, second_keep, send = project(weight, to_chips([piece] * chips))
-        kept.append(keep)
-        arrived.append(swapped(send, "chan", 1))
-        passed.append(swapped((second_keep.astype(F32) + arrived[-1][1].astype(F32)).astype(BF16), "chan", 2))
-    return join(to_chips(finish(kept, arrived, passed, chips)))
+    gated = gate(skip_gain[None, :], keep, swapped(send, "seq", 1), first, gates)
+
+    partials = project(out_weight, swapped(out_weight, "seq", 1), to_chips([gated] * chips))
+    arrived = to_layers(partials)
+    total = arrived[0].astype(F32)
+    for partial in arrived[1:]:
+        total = total + partial.astype(F32)
+    return total.astype(BF16)
 
 
 def shards(values_in, gate_values, filter_spectrum, skip_gain, out_weight):

time: 89 us -> 120 us (1.35)
  the two profiles are of different devices: /device:TPU:0 before, /device:TPU:4 now
where the time goes in v9:
time: 120 us; the launch traced here: 119 us
  waiting for transfers between devices  83.5 us (70%)
  starting transfers between devices  26.3 us (22%)
  Pallas kernels  8.37 us (7%)
    ppermute x4, waiting for transfers between devices, to_layers(): arrived.append(lax.ppermute(partial, ('seq', 'chan'), pairs))  55.2 us
    ppermute x12, waiting for transfers between devices, swapped(): lax.ppermute(value, axis, [(source, source ^ offset) for source in range(...  28.3 us
    ppermute x4, starting transfers between devices, to_layers(): arrived.append(lax.ppermute(partial, ('seq', 'chan'), pairs))  15.4 us
    ppermute x12, starting transfers between devices, swapped(): lax.ppermute(value, axis, [(source, source ^ offset) for source in range(...  10.9 us
  transfers between devices with their start and end apart: 16, of which 10 were waited for; matrix products, arithmetic and copies ran while one was open for 0% of the time, Pallas kernels for 4%

profile of v9, /device:TPU:4, one launch (start us, length us, event | category | flops | bytes accessed | tf_op | source)
XLA Modules:
  0.0 119.3 jit_solution(3941043244430816855)
XLA Ops:
  0.0 2.0 %pack_signals.1 = (bf16[5,128,256]{2,1,0:T(8,128)(2,1)S(1)}, bf16[5,128,256]{2,1,0:T(8,128)(2,1)S(1)}, bf16[5,128,256]{2,1,0:T(8,128)(2,1)S(1)}, bf16[5,128,256]{2,1,0:T(8,128)(2,1)S(1)}) custom-call(f32[4,128,1024]{2,1,0:T(8,128)} %bitcast.3, bf16[128,1024]{1,0:T(8,128)(2,1)} %values_ref.1), custom_call_target="tpu_custom_call" | custom-call | tf_op jit(solution)/shard_map/pack_signals/pallas_call | solution.py:245
  2.0 1.6 %collective-permute-start.1 = (bf16[5,128,256]{2,1,0:T(8,128)(2,1)S(1)}, bf16[5,128,256]{2,1,0:T(8,128)(2,1)S(1)}, u32[]{:S(2)}, u32[]{:S(2)}) collective-permute-start(bf16[5,128,256]{2,1,0:T(8,128)(2,1)S(1)} %get-tuple-element.28), channel_id=1, source_target_pairs={{0,8},{4,12},{8,0},{12,4},{16,24},{20,28},{24,16},{28,20},{1,9},{5... | collective-permute-start | bytes 983048 | tf_op jit(solution)/shard_map/ppermute | solution.py:488
  4.1 1.5 %collective-permute-start.3 = (bf16[5,128,256]{2,1,0:T(8,128)(2,1)S(1)}, bf16[5,128,256]{2,1,0:T(8,128)(2,1)S(1)}, u32[]{:S(2)}, u32[]{:S(2)}) collective-permute-start(bf16[5,128,256]{2,1,0:T(8,128)(2,1)S(1)} %get-tuple-element.32), channel_id=1, source_target_pairs={{0,24},{4,28},{8,16},{12,20},{16,8},{20,12},{24,0},{28,4},{1,25},{... | collective-permute-start | bytes 983048 | tf_op jit(solution)/shard_map/ppermute | solution.py:488
  5.6 1.0 pack_gates.1
  6.6 6.1 %collective-permute-done.1.refs_1_ = bf16[5,128,256]{2,1,0:T(8,128)(2,1)S(1)} collective-permute-done((bf16[5,128,256]{2,1,0:T(8,128)(2,1)S(1)}, bf16[5,128,256]{2,1,0:T(8,128)(2,1)S(1)}, u32[]{:S(2)}, u32[]{:S(2)}) %collective-permute-start.1) | collective-permute-done | bytes 327712 | tf_op jit(solution)/shard_map/ppermute | solution.py:488
  12.7 7.1 %collective-permute-done.2.refs_2_ = bf16[5,128,256]{2,1,0:T(8,128)(2,1)S(1)} collective-permute-done((bf16[5,128,256]{2,1,0:T(8,128)(2,1)S(1)}, bf16[5,128,256]{2,1,0:T(8,128)(2,1)S(1)}, u32[]{:S(2)}, u32[]{:S(2)}) %collective-permute-start.2) | collective-permute-done | bytes 327712 | tf_op jit(solution)/shard_map/ppermute | solution.py:488
  19.9 1.5 %collective-permute-done.4.other_ref = bf16[4,128,256]{2,1,0:T(8,128)(2,1)S(1)} collective-permute-done((bf16[4,128,256]{2,1,0:T(8,128)(2,1)S(1)}, bf16[4,128,256]{2,1,0:T(8,128)(2,1)S(1)}, u32[]{:S(2)}, u32[]{:S(2)}) %collective-permute-start.4) | collective-permute-done | bytes 262176 | tf_op jit(solution)/shard_map/ppermute | solution.py:488
  21.4 1.5 %forward.1.spectrum_ref = f32[256,2048]{1,0:T(8,128)S(1)} custom-call(f32[2,128,8]{2,1,0:T(8,128)S(1)} %copy-done.1, f32[2,128,8]{2,1,0:T(8,128)S(1)} %copy-done.2, bf16[256,256]{1,0:T(8,128)(2,1)S(1)} %copy-done.3, bf16[4,128,256]{2,1,0:T(8,128)(2,1)S(1)} %pad_maximum_fusion.own_ref, bf16[4,128,256]{2,1,0:T(8,128)(2,1)S(1)} %collective-permute-done.4.other_ref), custom_call_target="tpu_custom_call" | custom-call | tf_op jit(solution)/shard_map/forward/pallas_call | solution.py:337
  22.9 2.0 %backward.1 = (f32[4,128,256]{2,1,0:T(8,128)S(1)}, bf16[4,128,256]{2,1,0:T(8,128)(2,1)S(1)}) custom-call(f32[2,128,8]{2,1,0:T(8,128)S(1)} %copy-done.1, f32[2,128,8]{2,1,0:T(8,128)S(1)} %copy-done.2, bf16[256,256]{1,0:T(8,128)(2,1)S(1)} %copy-done.4, f32[256,2048]{1,0:T(8,128)S(1)} %forward.1.spectrum_ref, ...), custom_call_target="tpu_custom_call" | custom-call | tf_op jit(solution)/shard_map/backward/pallas_call | solution.py:411
  25.7 1.2 collective-permute-start.7
  26.9 1.8 %collective-permute-start.8 = (bf16[128,256]{1,0:T(8,128)(2,1)S(1)}, bf16[128,256]{1,0:T(8,128)(2,1)S(1)}, u32[]{:S(2)}, u32[]{:S(2)}) collective-permute-start(bf16[128,256]{1,0:T(8,128)(2,1)S(1)} %get-tuple-element.38), channel_id=1, source_target_pairs={{0,24},{4,28},{8,16},{12,20},{16,8},{20,12},{24,0},{28,4},{1,25},{... | collective-permute-start | bytes 196616 | tf_op jit(solution)/shard_map/ppermute | solution.py:488
  30.0 2.1 %collective-permute-done.8.refs_7_ = bf16[128,256]{1,0:T(8,128)(2,1)S(1)} collective-permute-done((bf16[128,256]{1,0:T(8,128)(2,1)S(1)}, bf16[128,256]{1,0:T(8,128)(2,1)S(1)}, u32[]{:S(2)}, u32[]{:S(2)}) %collective-permute-start.8) | collective-permute-done | bytes 65568 | tf_op jit(solution)/shard_map/ppermute | solution.py:488
  32.2 0.9 collective-permute-start.10
  33.1 1.4 %collective-permute-start.11 = (bf16[512,256]{1,0:T(8,128)(2,1)S(1)}, bf16[512,256]{1,0:T(8,128)(2,1)S(1)}, u32[]{:S(2)}, u32[]{:S(2)}) collective-permute-start(bf16[512,256]{1,0:T(8,128)(2,1)S(1)} %gate.1.refs_0_), channel_id=1, source_target_pairs={{0,24},{4,28},{8,16},{12,20},{16,8},{20,12},{24,0},{28,4},{1,25},{... | collective-permute-start | bytes 786440 | tf_op jit(solution)/shard_map/ppermute | solution.py:488
  34.6 1.2 %collective-permute-start.9 = (bf16[512,256]{1,0:T(8,128)(2,1)S(1)}, bf16[512,256]{1,0:T(8,128)(2,1)S(1)}, u32[]{:S(2)}, u32[]{:S(2)}) collective-permute-start(bf16[512,256]{1,0:T(8,128)(2,1)S(1)} %gate.1.refs_0_), channel_id=1, source_target_pairs={{0,8},{4,12},{8,0},{12,4},{16,24},{20,28},{24,16},{28,20},{1,9},{5... | collective-permute-start | bytes 786440 | tf_op jit(solution)/shard_map/ppermute | solution.py:488
  35.8 9.0 %collective-permute-done.10.refs_2_ = bf16[512,256]{1,0:T(8,128)(2,1)S(1)} collective-permute-done((bf16[512,256]{1,0:T(8,128)(2,1)S(1)}, bf16[512,256]{1,0:T(8,128)(2,1)S(1)}, u32[]{:S(2)}, u32[]{:S(2)}) %collective-permute-start.10) | collective-permute-done | bytes 262176 | tf_op jit(solution)/shard_map/ppermute | solution.py:488
  44.8 1.2 %collective-permute-done.9.refs_1_ = bf16[512,256]{1,0:T(8,128)(2,1)S(1)} collective-permute-done((bf16[512,256]{1,0:T(8,128)(2,1)S(1)}, bf16[512,256]{1,0:T(8,128)(2,1)S(1)}, u32[]{:S(2)}, u32[]{:S(2)}) %collective-permute-start.9) | collective-permute-done | bytes 262176 | tf_op jit(solution)/shard_map/ppermute | solution.py:488
  46.0 1.8 %project.1 = (bf16[128,1024]{1,0:T(8,128)(2,1)S(1)}, bf16[128,1024]{1,0:T(8,128)(2,1)S(1)}, bf16[128,1024]{1,0:T(8,128)(2,1)S(1)}, bf16[128,1024]{1,0:T(8,128)(2,1)S(1)}) custom-call(bf16[1024,512]{1,0:T(8,128)(2,1)S(1)} %copy-done, bf16[1024,512]{1,0:T(8,128)(2,1)S(1)} %collective-permute-done.other_ref, bf16[512,256]{1,0:T(8,128)(2,1)S(1)} %gate.1.refs_0_, ...), custom_call_target="tpu_custom_call" | custom-call | tf_op jit(solution)/shard_map/project/pallas_call | solution.py:473
  47.8 4.5 %collective-permute-start.12 = (bf16[128,1024]{1,0:T(8,128)(2,1)S(1)}, bf16[128,1024]{1,0:T(8,128)(2,1)S(1)}, u32[]{:S(2)}, u32[]{:S(2)}) collective-permute-start(bf16[128,1024]{1,0:T(8,128)(2,1)S(1)} %get-tuple-element.39), channel_id=1, source_target_pairs={{0,0},{1,8},{2,16},{3,24},{4,4},{5,12},{6,20},{7,28},{8,9},{9,1},{... | collective-permute-start | bytes 786440 | tf_op jit(solution)/shard_map/ppermute | solution.py:509
  52.3 4.7 %collective-permute-start.13 = (bf16[128,1024]{1,0:T(8,128)(2,1)S(1)}, bf16[128,1024]{1,0:T(8,128)(2,1)S(1)}, u32[]{:S(2)}, u32[]{:S(2)}) collective-permute-start(bf16[128,1024]{1,0:T(8,128)(2,1)S(1)} %get-tuple-element.40), channel_id=1, source_target_pairs={{0,8},{1,0},{2,24},{3,16},{4,12},{5,4},{6,28},{7,20},{8,1},{9,9},{... | collective-permute-start | bytes 786440 | tf_op jit(solution)/shard_map/ppermute | solution.py:509
  57.0 4.3 %collective-permute-start.14 = (bf16[128,1024]{1,0:T(8,128)(2,1)S(1)}, bf16[128,1024]{1,0:T(8,128)(2,1)S(1)}, u32[]{:S(2)}, u32[]{:S(2)}) collective-permute-start(bf16[128,1024]{1,0:T(8,128)(2,1)S(1)} %get-tuple-element.41), channel_id=1, source_target_pairs={{0,16},{1,24},{2,0},{3,8},{4,20},{5,28},{6,4},{7,12},{8,25},{9,17}... | collective-permute-start | bytes 786440 | tf_op jit(solution)/shard_map/ppermute | solution.py:509
  61.3 1.9 %collective-permute-start.15 = (bf16[128,1024]{1,0:T(8,128)(2,1)S(1)}, bf16[128,1024]{1,0:T(8,128)(2,1)S(1)}, u32[]{:S(2)}, u32[]{:S(2)}) collective-permute-start(bf16[128,1024]{1,0:T(8,128)(2,1)S(1)} %get-tuple-element.42), channel_id=1, source_target_pairs={{0,24},{1,16},{2,8},{3,0},{4,28},{5,20},{6,12},{7,4},{8,17},{9,25}... | collective-permute-start | bytes 786440 | tf_op jit(solution)/shard_map/ppermute | solution.py:509
  63.2 18.0 %collective-permute-done.12 = bf16[128,1024]{1,0:T(8,128)(2,1)S(1)} collective-permute-done((bf16[128,1024]{1,0:T(8,128)(2,1)S(1)}, bf16[128,1024]{1,0:T(8,128)(2,1)S(1)}, u32[]{:S(2)}, u32[]{:S(2)}) %collective-permute-start.12) | collective-permute-done | bytes 262176 | tf_op jit(solution)/shard_map/ppermute | solution.py:509
  81.3 37.2 %collective-permute-done.15 = bf16[128,1024]{1,0:T(8,128)(2,1)S(1)} collective-permute-done((bf16[128,1024]{1,0:T(8,128)(2,1)S(1)}, bf16[128,1024]{1,0:T(8,128)(2,1)S(1)}, u32[]{:S(2)}, u32[]{:S(2)}) %collective-permute-start.15) | collective-permute-done | bytes 262176 | tf_op jit(solution)/shard_map/ppermute | solution.py:509
  (32 shorter events, 3.8 us)
Async XLA Ops:
  0.0 21.4 %copy-start.3 = (bf16[256,256]{1,0:T(8,128)(2,1)S(1)}, bf16[256,256]{1,0:T(8,128)(2,1)}, u32[]{:S(2)}) copy-start(bf16[256,256]{1,0:T(8,128)(2,1)} %constant.10.clone.table_ref) | copy-start | bytes 393220
  0.0 21.4 %copy-start.1 = (f32[2,128,8]{2,1,0:T(8,128)S(1)}, f32[2,128,8]{2,1,0:T(8,128)}, u32[]{:S(2)}) copy-start(f32[2,128,8]{2,1,0:T(8,128)} %constant.8.clone.cos_ref) | copy-start | bytes 24580
  0.0 21.4 %copy-start.2 = (f32[2,128,8]{2,1,0:T(8,128)S(1)}, f32[2,128,8]{2,1,0:T(8,128)}, u32[]{:S(2)}) copy-start(f32[2,128,8]{2,1,0:T(8,128)} %constant.9.clone.sin_ref) | copy-start | bytes 24580
  0.0 5.5 %copy-start = (bf16[1024,512]{1,0:T(8,128)(2,1)S(1)}, bf16[1024,512]{1,0:T(8,128)(2,1)}, u32[]{:S(2)}) copy-start(bf16[1024,512]{1,0:T(8,128)(2,1)} %own_ref.1) | copy-start | bytes 3145732
  2.0 10.7 %collective-permute-start.1 = (bf16[5,128,256]{2,1,0:T(8,128)(2,1)S(1)}, bf16[5,128,256]{2,1,0:T(8,128)(2,1)S(1)}, u32[]{:S(2)}, u32[]{:S(2)}) collective-permute-start(bf16[5,128,256]{2,1,0:T(8,128)(2,1)S(1)} %get-tuple-element.28), channel_id=1, source_target_pairs={{0,8},{4,12},{8,0},{12,4},{16,24},{20,28},{24,16},{28,20},{1,9},{5... | collective-permute-start | bytes 983048 | tf_op jit(solution)/shard_map/ppermute | solution.py:488
  3.6 16.2 %collective-permute-start.2 = (bf16[5,128,256]{2,1,0:T(8,128)(2,1)S(1)}, bf16[5,128,256]{2,1,0:T(8,128)(2,1)S(1)}, u32[]{:S(2)}, u32[]{:S(2)}) collective-permute-start(bf16[5,128,256]{2,1,0:T(8,128)(2,1)S(1)} %get-tuple-element.30), channel_id=1, source_target_pairs={{0,16},{4,20},{8,24},{12,28},{16,0},{20,4},{24,8},{28,12},{1,17},{... | collective-permute-start | bytes 983048 | tf_op jit(solution)/shard_map/ppermute | solution.py:488
  4.1 15.7 %collective-permute-start.3 = (bf16[5,128,256]{2,1,0:T(8,128)(2,1)S(1)}, bf16[5,128,256]{2,1,0:T(8,128)(2,1)S(1)}, u32[]{:S(2)}, u32[]{:S(2)}) collective-permute-start(bf16[5,128,256]{2,1,0:T(8,128)(2,1)S(1)} %get-tuple-element.32), channel_id=1, source_target_pairs={{0,24},{4,28},{8,16},{12,20},{16,8},{20,12},{24,0},{28,4},{1,25},{... | collective-permute-start | bytes 983048 | tf_op jit(solution)/shard_map/ppermute | solution.py:488
  5.6 30.2 %collective-permute-start = (bf16[1024,512]{1,0:T(8,128)(2,1)S(1)}, bf16[1024,512]{1,0:T(8,128)(2,1)S(1)}, u32[]{:S(2)}, u32[]{:S(2)}) collective-permute-start(bf16[1024,512]{1,0:T(8,128)(2,1)S(1)} %copy-done), channel_id=1, source_target_pairs={{0,4},{4,0},{8,12},{12,8},{16,20},{20,16},{24,28},{28,24},{1,5},{5... | collective-permute-start | bytes 3145736 | tf_op jit(solution)/shard_map/ppermute | solution.py:488
  6.5 16.4 %copy-start.4 = (bf16[256,256]{1,0:T(8,128)(2,1)S(1)}, bf16[256,256]{1,0:T(8,128)(2,1)}, u32[]{:S(2)}) copy-start(bf16[256,256]{1,0:T(8,128)(2,1)} %constant.11.clone.table_ref) | copy-start | bytes 393220
  19.8 1.6 %collective-permute-start.4 = (bf16[4,128,256]{2,1,0:T(8,128)(2,1)S(1)}, bf16[4,128,256]{2,1,0:T(8,128)(2,1)S(1)}, u32[]{:S(2)}, u32[]{:S(2)}) collective-permute-start(bf16[4,128,256]{2,1,0:T(8,128)(2,1)S(1)} %pad_maximum_fusion.own_ref), channel_id=1, source_target_pairs={{0,4},{4,0},{8,12},{12,8},{16,20},{20,16},{24,28},{28,24},{1,5},{5... | collective-permute-start | bytes 786440 | tf_op jit(solution)/shard_map/ppermute | solution.py:488
  22.9 9.1 %copy-start.5 = (f32[1024]{0:T(1024)S(1)}, f32[1024]{0:T(1024)}, u32[]{:S(2)}) copy-start(f32[1024]{0:T(1024)} %param.12) | copy-start | bytes 12292
  25.0 7.1 %collective-permute-start.5 = (bf16[4,128,256]{2,1,0:T(8,128)(2,1)S(1)}, bf16[4,128,256]{2,1,0:T(8,128)(2,1)S(1)}, u32[]{:S(2)}, u32[]{:S(2)}) collective-permute-start(bf16[4,128,256]{2,1,0:T(8,128)(2,1)S(1)} %get-tuple-element.35), channel_id=1, source_target_pairs={{0,4},{4,0},{8,12},{12,8},{16,20},{20,16},{24,28},{28,24},{1,5},{5... | collective-permute-start | bytes 786440 | tf_op jit(solution)/shard_map/ppermute | solution.py:488
  25.2 4.4 %collective-permute-start.6 = (bf16[128,256]{1,0:T(8,128)(2,1)S(1)}, bf16[128,256]{1,0:T(8,128)(2,1)S(1)}, u32[]{:S(2)}, u32[]{:S(2)}) collective-permute-start(bf16[128,256]{1,0:T(8,128)(2,1)S(1)} %get-tuple-element.36), channel_id=1, source_target_pairs={{0,8},{4,12},{8,0},{12,4},{16,24},{20,28},{24,16},{28,20},{1,9},{5... | collective-permute-start | bytes 196616 | tf_op jit(solution)/shard_map/ppermute | solution.py:488
  25.7 4.3 %collective-permute-start.7 = (bf16[128,256]{1,0:T(8,128)(2,1)S(1)}, bf16[128,256]{1,0:T(8,128)(2,1)S(1)}, u32[]{:S(2)}, u32[]{:S(2)}) collective-permute-start(bf16[128,256]{1,0:T(8,128)(2,1)S(1)} %get-tuple-element.37), channel_id=1, source_target_pairs={{0,16},{4,20},{8,24},{12,28},{16,0},{20,4},{24,8},{28,12},{1,17},{... | collective-permute-start | bytes 196616 | tf_op jit(solution)/shard_map/ppermute | solution.py:488
  26.9 5.2 %collective-permute-start.8 = (bf16[128,256]{1,0:T(8,128)(2,1)S(1)}, bf16[128,256]{1,0:T(8,128)(2,1)S(1)}, u32[]{:S(2)}, u32[]{:S(2)}) collective-permute-start(bf16[128,256]{1,0:T(8,128)(2,1)S(1)} %get-tuple-element.38), channel_id=1, source_target_pairs={{0,24},{4,28},{8,16},{12,20},{16,8},{20,12},{24,0},{28,4},{1,25},{... | collective-permute-start | bytes 196616 | tf_op jit(solution)/shard_map/ppermute | solution.py:488
  32.2 12.5 %collective-permute-start.10 = (bf16[512,256]{1,0:T(8,128)(2,1)S(1)}, bf16[512,256]{1,0:T(8,128)(2,1)S(1)}, u32[]{:S(2)}, u32[]{:S(2)}) collective-permute-start(bf16[512,256]{1,0:T(8,128)(2,1)S(1)} %gate.1.refs_0_), channel_id=1, source_target_pairs={{0,16},{4,20},{8,24},{12,28},{16,0},{20,4},{24,8},{28,12},{1,17},{... | collective-permute-start | bytes 786440 | tf_op jit(solution)/shard_map/ppermute | solution.py:488
  33.1 11.6 %collective-permute-start.11 = (bf16[512,256]{1,0:T(8,128)(2,1)S(1)}, bf16[512,256]{1,0:T(8,128)(2,1)S(1)}, u32[]{:S(2)}, u32[]{:S(2)}) collective-permute-start(bf16[512,256]{1,0:T(8,128)(2,1)S(1)} %gate.1.refs_0_), channel_id=1, source_target_pairs={{0,24},{4,28},{8,16},{12,20},{16,8},{20,12},{24,0},{28,4},{1,25},{... | collective-permute-start | bytes 786440 | tf_op jit(solution)/shard_map/ppermute | solution.py:488
  34.6 11.4 %collective-permute-start.9 = (bf16[512,256]{1,0:T(8,128)(2,1)S(1)}, bf16[512,256]{1,0:T(8,128)(2,1)S(1)}, u32[]{:S(2)}, u32[]{:S(2)}) collective-permute-start(bf16[512,256]{1,0:T(8,128)(2,1)S(1)} %gate.1.refs_0_), channel_id=1, source_target_pairs={{0,8},{4,12},{8,0},{12,4},{16,24},{20,28},{24,16},{28,20},{1,9},{5... | collective-permute-start | bytes 786440 | tf_op jit(solution)/shard_map/ppermute | solution.py:488
  47.8 33.5 %collective-permute-start.12 = (bf16[128,1024]{1,0:T(8,128)(2,1)S(1)}, bf16[128,1024]{1,0:T(8,128)(2,1)S(1)}, u32[]{:S(2)}, u32[]{:S(2)}) collective-permute-start(bf16[128,1024]{1,0:T(8,128)(2,1)S(1)} %get-tuple-element.39), channel_id=1, source_target_pairs={{0,0},{1,8},{2,16},{3,24},{4,4},{5,12},{6,20},{7,28},{8,9},{9,1},{... | collective-permute-start | bytes 786440 | tf_op jit(solution)/shard_map/ppermute | solution.py:509
  52.3 29.0 %collective-permute-start.13 = (bf16[128,1024]{1,0:T(8,128)(2,1)S(1)}, bf16[128,1024]{1,0:T(8,128)(2,1)S(1)}, u32[]{:S(2)}, u32[]{:S(2)}) collective-permute-start(bf16[128,1024]{1,0:T(8,128)(2,1)S(1)} %get-tuple-element.40), channel_id=1, source_target_pairs={{0,8},{1,0},{2,24},{3,16},{4,12},{5,4},{6,28},{7,20},{8,1},{9,9},{... | collective-permute-start | bytes 786440 | tf_op jit(solution)/shard_map/ppermute | solution.py:509
  57.0 24.3 %collective-permute-start.14 = (bf16[128,1024]{1,0:T(8,128)(2,1)S(1)}, bf16[128,1024]{1,0:T(8,128)(2,1)S(1)}, u32[]{:S(2)}, u32[]{:S(2)}) collective-permute-start(bf16[128,1024]{1,0:T(8,128)(2,1)S(1)} %get-tuple-element.41), channel_id=1, source_target_pairs={{0,16},{1,24},{2,0},{3,8},{4,20},{5,28},{6,4},{7,12},{8,25},{9,17}... | collective-permute-start | bytes 786440 | tf_op jit(solution)/shard_map/ppermute | solution.py:509
  61.3 57.1 %collective-permute-start.15 = (bf16[128,1024]{1,0:T(8,128)(2,1)S(1)}, bf16[128,1024]{1,0:T(8,128)(2,1)S(1)}, u32[]{:S(2)}, u32[]{:S(2)}) collective-permute-start(bf16[128,1024]{1,0:T(8,128)(2,1)S(1)} %get-tuple-element.42), channel_id=1, source_target_pairs={{0,24},{1,16},{2,8},{3,0},{4,28},{5,20},{6,12},{7,4},{8,17},{9,25}... | collective-permute-start | bytes 786440 | tf_op jit(solution)/shard_map/ppermute | solution.py:509

commit v10 on v9

--- a/solution.py
+++ b/solution.py
@@ -257,41 +257,62 @@
     )(*(pltpu.with_memory_space_constraint(array, pltpu.HBM) for array in (filters, values_in)))
 
 
-def pack_gates_kernel(chips, gate_ref, *refs):
+def pack_moved_kernel(chips, gate_ref, own_ref, other_ref, *refs):
     out_refs, arrived = refs[:chips], refs[chips]
-    chip, _ = own_place()
-    copies = []
-    for offset, out_ref in enumerate(out_refs):
-        gates = gate_ref.at[:, block_at(chip ^ offset, out_ref.shape[1])]
-        copies.append(pltpu.make_async_copy(gates, out_ref, arrived.at[offset]))
-    for copy in copies:
-        copy.start()
-    for copy in copies:
-        copy.wait()
-
-
-def pack_gates(gate_values, chips):
+    chip, core = own_place()
+    rows = gate_ref.shape[0]
+    depth, held = own_ref.shape
+    quarter, share = depth // 4, held // chips
+
+    def copies_from(weight_ref):
+        copies = []
+        for offset in range(chips):
+            out_ref, target = out_refs[offset], chip ^ offset
+            gates = gate_ref.at[:, block_at(target, out_ref.shape[1])]
+            copies.append(pltpu.make_async_copy(gates, out_ref.at[pl.ds(0, rows)], arrived.at[offset, 2]))
+            for part in range(2):
+                source = weight_ref.at[block_at(2 * core + part, quarter), block_at(target, share)]
+                sink = out_ref.at[pl.ds(rows, quarter), pl.ds(part * share, share)]
+                copies.append(pltpu.make_async_copy(source, sink, arrived.at[offset, part]))
+        for copy in copies:
+            copy.start()
+        for copy in copies:
+            copy.wait()
+
+    @pl.when(core == 0)
+    def _():
+        copies_from(own_ref)
+
+    @pl.when(core == 1)
+    def _():
+        copies_from(other_ref)
+
+
+def pack_moved(gate_values, own, other, chips):
     rows, width = gate_values.shape
-    return pl.pallas_call(
-        functools.partial(pack_gates_kernel, chips),
-        in_specs=[pl.BlockSpec(memory_space=pltpu.HBM)],
+    depth, held = own.shape
+    return pl.pallas_call(
+        functools.partial(pack_moved_kernel, chips),
+        in_specs=[pl.BlockSpec(memory_space=pltpu.HBM)] * 2 + [pl.BlockSpec(memory_space=pl.ANY)],
         out_specs=[WHOLE] * chips,
-        out_shape=[jax.ShapeDtypeStruct((rows, width // chips), BF16)] * chips,
-        scratch_shapes=[pltpu.SemaphoreType.DMA((chips,))],
-        cost_estimate=CHEAP,
-        compiler_params=pltpu.CompilerParams(vmem_limit_bytes=4 * 2**20),
-        name="pack_gates",
-    )(pltpu.with_memory_space_constraint(gate_values, pltpu.HBM))
-
-
-def forward_kernel(chips, cos_ref, sin_ref, table_ref, own_ref, other_ref, out_ref, signal_ref, waves_ref):
+        out_shape=[jax.ShapeDtypeStruct((rows + depth // 4, 2 * held // chips), BF16)] * chips,
+        scratch_shapes=[pltpu.SemaphoreType.DMA((chips, 3))],
+        cost_estimate=CHEAP,
+        compiler_params=pltpu.CompilerParams(vmem_limit_bytes=8 * 2**20),
+        name="pack_moved",
+    )(*(pltpu.with_memory_space_constraint(array, pltpu.HBM) for array in (gate_values, own)), other)
+
+
+def forward_kernel(chips, cos_ref, sin_ref, table_ref, *refs):
+    own_refs, other_refs, (out_ref, signal_ref, waves_ref) = refs[:2], refs[2:4], refs[4:]
     chip, core = own_place()
     parts = 2 * chips
-    rows, lanes = own_ref.shape[1:]
+    rows, lanes = own_refs[0].shape[1:]
     chunk, width = 16, 128
     for offset in range(chips):
-        signal_ref[2 * (chip ^ offset) + core] = own_ref[offset]
-        signal_ref[2 * (chip ^ offset) + 1 - core] = other_ref[offset]
+        part, place = divmod(offset, chips // 2)
+        signal_ref[2 * (chip ^ offset) + core] = own_refs[part][place]
+        signal_ref[2 * (chip ^ offset) + 1 - core] = other_refs[part][place]
     sign = (1 - 2 * core).astype(F32)
 
     def spread(index, carry):
@@ -331,23 +352,23 @@
 
 
 def forward(own, other, tables):
-    chips, rows, lanes = own.shape
+    chips, (_, rows, lanes) = 2 * own[0].shape[0], own[0].shape
     table, _, cos, sin = tables
     spectrum = (2 * rows, 2 * chips * lanes)
     return pl.pallas_call(
         functools.partial(forward_kernel, chips),
-        in_specs=[WHOLE] * 5,
+        in_specs=[WHOLE] * 7,
         out_specs=WHOLE,
         out_shape=jax.ShapeDtypeStruct(spectrum, F32),
         scratch_shapes=[pltpu.VMEM((2 * chips, rows, lanes), BF16), pltpu.VMEM(spectrum, BF16)],
         cost_estimate=CHEAP,
         compiler_params=pltpu.CompilerParams(vmem_limit_bytes=32 * 2**20),
         name="forward",
-    )(cos, sin, table, own, other)
+    )(cos, sin, table, *own, *other)
 
 
 def backward_kernel(chips, cos_ref, sin_ref, table_ref, spectrum_ref, *refs):
-    filter_refs, (keep_ref, send_ref, filter_ref, product_ref, back_ref) = refs[:chips], refs[chips:]
+    filter_refs, (keep_ref, *send_refs, filter_ref, product_ref, back_ref) = refs[:chips], refs[chips:]
     chip, core = own_place()
     parts = 2 * chips
     rows, lanes = keep_ref.shape[1:]
@@ -397,7 +418,8 @@
             for pair in range(chips):
                 low, high = totals[2 * pair], totals[2 * pair + 1] * sign
                 keep_ref[pair, here, lane] = jnp.where(upper, high, low)
-                send_ref[pair, here, lane] = jnp.where(upper, low, high).astype(BF16)
+                part, place = divmod(pair, chips // 2)
+                send_refs[part][place, here, lane] = jnp.where(upper, low, high).astype(BF16)
         return carry
 
     lax.fori_loop(0, rows // chunk, gather, 0)
@@ -407,12 +429,12 @@
     chips = len(first)
     _, rows, lanes = first[0].shape
     _, table, cos, sin = tables
-    kept = (chips, rows, lanes)
+    half = jax.ShapeDtypeStruct((chips // 2, rows, lanes), BF16)
     return pl.pallas_call(
         functools.partial(backward_kernel, chips),
         in_specs=[WHOLE] * (4 + chips),
-        out_specs=[WHOLE] * 2,
-        out_shape=[jax.ShapeDtypeStruct(kept, F32), jax.ShapeDtypeStruct(kept, BF16)],
+        out_specs=[WHOLE] * 3,
+        out_shape=[jax.ShapeDtypeStruct((chips, rows, lanes), F32), half, half],
         scratch_shapes=[
             pltpu.VMEM((chips, 4, rows, lanes), BF16),
             pltpu.VMEM(spectrum.shape, BF16),
@@ -424,16 +446,18 @@
     )(cos, sin, table, spectrum, *first)
 
 
-def gate_kernel(chips, skip_ref, keep_ref, arrived_ref, *refs):
-    signal_refs, gate_refs, out_ref = refs[:chips], refs[chips : 2 * chips], refs[2 * chips]
+def gate_kernel(chips, skip_ref, keep_ref, low_ref, high_ref, *refs):
+    signal_refs, gate_refs, (out_ref, arrived_ref) = refs[:chips], refs[chips : 2 * chips], refs[2 * chips :]
     chip, _ = own_place()
     rows, lanes = keep_ref.shape[1:]
     skip = skip_ref[:, block_at(chip, lanes)]
+    arrived_ref[pl.ds(0, chips // 2)] = low_ref[...]
+    arrived_ref[pl.ds(chips // 2, chips // 2)] = high_ref[...]
     for offset in range(chips):
         block = chip ^ offset
         convolved = keep_ref[block] + arrived_ref[block].astype(F32)
         signal = signal_refs[offset][4].astype(F32)
-        gate = gate_refs[offset][...].astype(F32)
+        gate = gate_refs[offset][pl.ds(0, rows), :].astype(F32)
         out_ref[block_at(block, rows), :] = (gate * (convolved + skip * signal)).astype(BF16)
 
 
@@ -441,45 +465,187 @@
     chips, rows, lanes = keep.shape
     return pl.pallas_call(
         functools.partial(gate_kernel, chips),
-        in_specs=[WHOLE] * (3 + 2 * chips),
+        in_specs=[WHOLE] * (4 + 2 * chips),
         out_specs=WHOLE,
         out_shape=jax.ShapeDtypeStruct((chips * rows, lanes), BF16),
+        scratch_shapes=[pltpu.VMEM((chips, rows, lanes), BF16)],
         cost_estimate=CHEAP,
         compiler_params=pltpu.CompilerParams(vmem_limit_bytes=6 * 2**20),
         name="gate",
-    )(skip, keep, arrived, *first, *gates)
-
-
-def project_kernel(chips, own_ref, other_ref, *refs):
-    gated_refs, out_refs, (joined_ref, weight_ref) = refs[:chips], refs[chips : 2 * chips], refs[2 * chips :]
-    chip, core = own_place()
+    )(skip, keep, *arrived, *first, *gates)
+
+
+def collect_kernel(chips, *refs):
+    in_refs, out_ref = refs[:chips], refs[chips]
+    chip, _ = own_place()
     layer = lax.axis_index("chan")
-    held = own_ref.shape[1]
+    quarter, share = out_ref.shape[0] // 2, out_ref.shape[1] // chips
+    start = in_refs[0].shape[0] - quarter
+    for offset in range(chips):
+        for part in range(2):
+            block = in_refs[offset][pl.ds(start, quarter), pl.ds(part * share, share)]
+            out_ref[pl.ds(part * quarter, quarter), block_at(chip ^ layer ^ offset, share)] = block
+
+
+def collect(moved, half):
+    chips = len(moved)
+    return pl.pallas_call(
+        functools.partial(collect_kernel, chips),
+        in_specs=[WHOLE] * chips,
+        out_specs=WHOLE,
+        out_shape=jax.ShapeDtypeStruct((half, chips * moved[0].shape[1] // 2), BF16),
+        cost_estimate=CHEAP,
+        compiler_params=pltpu.CompilerParams(vmem_limit_bytes=4 * 2**20),
+        name="collect_weights",
+    )(*moved)
+
+
+def join_channels(chips, gated_refs, joined_ref):
+    chip, _ = own_place()
     lanes = gated_refs[0].shape[1]
-    rows = out_refs[0].shape[0]
     for offset in range(chips):
         joined_ref[:, block_at(chip ^ offset, lanes)] = gated_refs[offset][...]
-    weight_ref[:, block_at(core, held)] = own_ref[...]
-    weight_ref[:, block_at(1 - core, held)] = other_ref[...]
-    for step in range(chips):
-        gated = joined_ref[block_at(chip ^ layer ^ step, rows), :]
-        out_refs[step][...] = jnp.dot(gated, weight_ref[...], preferred_element_type=F32).astype(BF16)
-
-
-def project(own, other, gated):
+
+
+def project_moved_kernel(chips, own_ref, other_ref, *refs):
+    gated_refs, (keep_ref, pass_ref, send_ref, joined_ref) = refs[:chips], refs[chips:]
+    _, core = own_place()
+    half = own_ref.shape[0]
+    share = keep_ref.shape[1]
+    join_channels(chips, gated_refs, joined_ref)
+    partial = jnp.dot(joined_ref[:, block_at(core, half)], own_ref[...], preferred_element_type=F32)
+    partial += jnp.dot(joined_ref[:, block_at(1 - core, half)], other_ref[...], preferred_element_type=F32)
+    partial = partial.astype(BF16)
+    keep_ref[...] = partial[:, :share]
+    send_ref[0] = partial[:, share : 2 * share]
+    pass_ref[...] = partial[:, 2 * share : 3 * share]
+    send_ref[1] = partial[:, 3 * share :]
+
+
+def project_moved(own, other, gated):
+    chips = len(gated)
+    half, columns = own.shape
+    rows = gated[0].shape[0]
+    block = jax.ShapeDtypeStruct((rows, columns // chips), BF16)
+    return pl.pallas_call(
+        functools.partial(project_moved_kernel, chips),
+        in_specs=[WHOLE] * (2 + chips),
+        out_specs=[WHOLE] * 3,
+        out_shape=[block, block, jax.ShapeDtypeStruct((2, rows, columns // chips), BF16)],
+        scratch_shapes=[pltpu.VMEM((rows, 2 * half), BF16)],
+        cost_estimate=CHEAP,
+        compiler_params=pltpu.CompilerParams(vmem_limit_bytes=8 * 2**20),
+        name="project_moved",
+    )(own, other, *gated)
+
+
+def project_still_kernel(chips, own_ref, other_ref, *refs):
+    gated_refs, out_refs, joined_ref = refs[:chips], refs[chips : 2 * chips], refs[2 * chips]
+    chip, core = own_place()
+    rows = out_refs[0].shape[0]
+    join_channels(chips, gated_refs, joined_ref)
+
+    def project_with(weight_ref):
+        for offset in range(chips):
+            gated = joined_ref[block_at(chip ^ offset, rows), :]
+            out_refs[offset][...] = jnp.dot(gated, weight_ref[...], preferred_element_type=F32).astype(BF16)
+
+    @pl.when(core == 0)
+    def _():
+        project_with(other_ref)
+
+    @pl.when(core == 1)
+    def _():
+        project_with(own_ref)
+
+
+def project_still(own, other, gated):
     chips = len(gated)
     depth, held = own.shape
     rows = gated[0].shape[0] // chips
     return pl.pallas_call(
-        functools.partial(project_kernel, chips),
+        functools.partial(project_still_kernel, chips),
         in_specs=[WHOLE] * (2 + chips),
         out_specs=[WHOLE] * chips,
-        out_shape=[jax.ShapeDtypeStruct((rows, 2 * held), BF16)] * chips,
-        scratch_shapes=[pltpu.VMEM((rows * chips, depth), BF16), pltpu.VMEM((depth, 2 * held), BF16)],
+        out_shape=[jax.ShapeDtypeStruct((rows, held), BF16)] * chips,
+        scratch_shapes=[pltpu.VMEM((rows * chips, depth), BF16)],
         cost_estimate=CHEAP,
         compiler_params=pltpu.CompilerParams(vmem_limit_bytes=12 * 2**20),
-        name="project",
+        name="project_still",
     )(own, other, *gated)
+
+
+def sort_kernel(chips, *refs):
+    in_refs, (keep_ref, pass_ref, send_ref, sorted_ref) = refs[:chips], refs[chips:]
+    chip, _ = own_place()
+    layer = lax.axis_index("chan")
+    for offset in range(chips):
+        sorted_ref[chip ^ layer ^ offset] = in_refs[offset][...]
+    keep_ref[...] = sorted_ref[0]
+    send_ref[0] = sorted_ref[1]
+    pass_ref[...] = sorted_ref[2]
+    send_ref[1] = sorted_ref[3]
+
+
+def sort_blocks(blocks):
+    chips = len(blocks)
+    block = jax.ShapeDtypeStruct(blocks[0].shape, BF16)
+    return pl.pallas_call(
+        functools.partial(sort_kernel, chips),
+        in_specs=[WHOLE] * chips,
+        out_specs=[WHOLE] * 3,
+        out_shape=[block, block, jax.ShapeDtypeStruct((2, *block.shape), BF16)],
+        scratch_shapes=[pltpu.VMEM((chips, *block.shape), BF16)],
+        cost_estimate=CHEAP,
+        compiler_params=pltpu.CompilerParams(vmem_limit_bytes=4 * 2**20),
+        name="sort_blocks",
+    )(*blocks)
+
+
+def finish_kernel(chips, keep_ref, first_ref, second_ref, *out_refs):
+    chip, _ = own_place()
+    rows = out_refs[0].shape[0]
+    for offset in range(chips):
+        here = block_at(chip ^ offset, rows)
+        total = keep_ref[here, :].astype(F32) + first_ref[0, here, :].astype(F32) + second_ref[here, :].astype(F32)
+        out_refs[offset][...] = total.astype(BF16)
+
+
+def finish(keep, first, second, chips):
+    rows, columns = keep.shape
+    return pl.pallas_call(
+        functools.partial(finish_kernel, chips),
+        in_specs=[WHOLE] * 3,
+        out_specs=[WHOLE] * chips,
+        out_shape=[jax.ShapeDtypeStruct((rows // chips, columns), BF16)] * chips,
+        cost_estimate=CHEAP,
+        compiler_params=pltpu.CompilerParams(vmem_limit_bytes=4 * 2**20),
+        name="finish",
+    )(keep, first, second)
+
+
+def join_kernel(chips, keep_ref, first_ref, second_ref, *refs):
+    in_refs, out_ref = refs[:chips], refs[chips]
+    chip, _ = own_place()
+    share = in_refs[0].shape[1]
+    for offset in range(chips):
+        out_ref[:, block_at(chip ^ offset, share)] = in_refs[offset][...]
+    total = keep_ref[...].astype(F32) + first_ref[0].astype(F32) + second_ref[...].astype(F32)
+    out_ref[:, pl.ds(chips * share, total.shape[1])] = total.astype(BF16)
+
+
+def join(keep, first, second, blocks):
+    chips = len(blocks)
+    rows, share = blocks[0].shape
+    return pl.pallas_call(
+        functools.partial(join_kernel, chips),
+        in_specs=[WHOLE] * (3 + chips),
+        out_specs=WHOLE,
+        out_shape=jax.ShapeDtypeStruct((rows, chips * share + keep.shape[1]), BF16),
+        cost_estimate=CHEAP,
+        compiler_params=pltpu.CompilerParams(vmem_limit_bytes=4 * 2**20),
+        name="join",
+    )(keep, first, second, *blocks)
 
 
 def swapped(value, axis, offset):
@@ -496,18 +662,10 @@
     return lax.optimization_barrier((value, *others))[0]
 
 
-def to_layers(partials):
-    chips = len(partials)
-    arrived = []
-    for step, partial in enumerate(partials):
-        pairs = []
-        for chip in range(chips):
-            for core in range(2):
-                for layer in range(chips):
-                    source = (2 * chip + core) * chips + layer
-                    pairs.append((source, (2 * (chip ^ layer ^ step) + core) * chips + chip))
-        arrived.append(lax.ppermute(partial, ("seq", "chan"), pairs))
-    return arrived
+def over_layers(passed, send):
+    first = swapped(send, "chan", 1)
+    passed = (passed.astype(F32) + first[1].astype(F32)).astype(BF16)
+    return first, swapped(passed, "chan", 2)
 
 
 def shards_direct(values_in, gate_values, filter_spectrum, skip_gain, out_weight):
@@ -517,20 +675,22 @@
     tables = small_tables(parts, rows)
 
     first = pack_signals(values_in, filter_spectrum.reshape(4, rows, width), chips, tuple(range(chips)))
-    gates = pack_gates(after(gate_values, first[0]), chips)
+    other_weight = swapped(out_weight, "seq", 1)
+    moved = pack_moved(after(gate_values, first[0]), out_weight, other_weight, chips)
     first = to_chips(first)
-    own = jnp.stack([after(block, gates[0])[4] for block in first])
-    gates = to_chips(gates)
-    spectrum = forward(own, swapped(own, "seq", 1), tables)
-    keep, send = backward(spectrum, first, tables)
-    gated = gate(skip_gain[None, :], keep, swapped(send, "seq", 1), first, gates)
-
-    partials = project(out_weight, swapped(out_weight, "seq", 1), to_chips([gated] * chips))
-    arrived = to_layers(partials)
-    total = arrived[0].astype(F32)
-    for partial in arrived[1:]:
-        total = total + partial.astype(F32)
-    return total.astype(BF16)
+    own = [after(block, moved[0])[4] for block in first]
+    own = [jnp.stack(own[: chips // 2]), jnp.stack(own[chips // 2 :])]
+    moved = to_chips(moved)
+    spectrum = forward(own, [swapped(half, "seq", 1) for half in own], tables)
+    keep, *send = backward(spectrum, first, tables)
+    gated = gate(skip_gain[None, :], keep, [swapped(half, "seq", 1) for half in send], first, moved)
+    own_moved = collect([after(block, gated) for block in moved], out_weight.shape[0] // 2)
+    gathered = to_chips([gated] * chips)
+
+    keep, passed, send = project_moved(own_moved, swapped(own_moved, "seq", 1), gathered)
+    blocks = to_chips(finish(keep, *over_layers(passed, send), chips))
+    keep, passed, send = sort_blocks(to_chips(project_still(out_weight, other_weight, gathered)))
+    return join(keep, *over_layers(passed, send), blocks)
 
 
 def shards(values_in, gate_values, filter_spectrum, skip_gain, out_weight):

time: 120 us -> 81.1 us (0.68)
  the two profiles are of different devices: /device:TPU:4 before, /device:TPU:0 now
where the time goes in v10:
time: 81.1 us; the launch traced here: 80.7 us
  waiting for transfers between devices  44.6 us (55%)
  starting transfers between devices  26.1 us (32%)
  Pallas kernels  9.53 us (12%)
    ppermute x25, waiting for transfers between devices, swapped(): lax.ppermute(value, axis, [(source, source ^ offset) for source in range(...  44.6 us
    ppermute x25, starting transfers between devices, swapped(): lax.ppermute(value, axis, [(source, source ^ offset) for source in range(...  26.1 us
    pallas_call x1, Pallas kernels, backward(): pl.pallas_call(functools.partial(backward_kernel, chips), in_specs=[WHOLE...  2.02 us
    pallas_call x1, Pallas kernels, pack_signals(): pl.pallas_call(functools.partial(pack_signals_kernel, offsets), in_specs=...  1.85 us
  transfers between devices with their start and end apart: 25, of which 12 were waited for; matrix products, arithmetic and copies ran while one was open for 0% of the time, Pallas kernels for 9%

profile of v10, /device:TPU:0, one launch (start us, length us, event | category | flops | bytes accessed | tf_op | source)
XLA Modules:
  0.0 80.7 jit_solution(7033242880629245108)
XLA Ops:
  0.5 1.9 %pack_signals.1 = (bf16[5,128,256]{2,1,0:T(8,128)(2,1)S(1)}, bf16[5,128,256]{2,1,0:T(8,128)(2,1)S(1)}, bf16[5,128,256]{2,1,0:T(8,128)(2,1)S(1)}, bf16[5,128,256]{2,1,0:T(8,128)(2,1)S(1)}) custom-call(f32[4,128,1024]{2,1,0:T(8,128)} %bitcast.13, bf16[128,1024]{1,0:T(8,128)(2,1)} %values_ref.1), custom_call_target="tpu_custom_call" | custom-call | tf_op jit(solution)/shard_map/pack_signals/pallas_call | solution.py:245
  2.4 3.5 %collective-permute-start.3 = (bf16[5,128,256]{2,1,0:T(8,128)(2,1)S(1)}, bf16[5,128,256]{2,1,0:T(8,128)(2,1)S(1)}, u32[]{:S(2)}, u32[]{:S(2)}) collective-permute-start(bf16[5,128,256]{2,1,0:T(8,128)(2,1)S(1)} %get-tuple-element.47), channel_id=1, source_target_pairs={{0,24},{4,28},{8,16},{12,20},{16,8},{20,12},{24,0},{28,4},{1,25},{... | collective-permute-start | bytes 983048 | tf_op jit(solution)/shard_map/ppermute | solution.py:654
  6.5 1.3 %pack_moved.1 = (bf16[384,256]{1,0:T(8,128)(2,1)S(1)}, bf16[384,256]{1,0:T(8,128)(2,1)S(1)}, bf16[384,256]{1,0:T(8,128)(2,1)S(1)}, bf16[384,256]{1,0:T(8,128)(2,1)S(1)}) custom-call(bf16[128,1024]{1,0:T(8,128)(2,1)} %gate_ref, bf16[1024,512]{1,0:T(8,128)(2,1)} %own_ref.3, bf16[1024,512]{1,0:T(8,128)(2,1)S(1)} %collective-permute-done.other_ref), custom_call_target="tpu_custom_call" | custom-call | tf_op jit(solution)/shard_map/pack_moved/pallas_call | solution.py:294
  7.8 6.7 %collective-permute-done.3.refs_3_ = bf16[5,128,256]{2,1,0:T(8,128)(2,1)S(1)} collective-permute-done((bf16[5,128,256]{2,1,0:T(8,128)(2,1)S(1)}, bf16[5,128,256]{2,1,0:T(8,128)(2,1)S(1)}, u32[]{:S(2)}, u32[]{:S(2)}) %collective-permute-start.3) | collective-permute-done | bytes 327712 | tf_op jit(solution)/shard_map/ppermute | solution.py:654
  14.5 6.8 %collective-permute-done.2.refs_2_ = bf16[5,128,256]{2,1,0:T(8,128)(2,1)S(1)} collective-permute-done((bf16[5,128,256]{2,1,0:T(8,128)(2,1)S(1)}, bf16[5,128,256]{2,1,0:T(8,128)(2,1)S(1)}, u32[]{:S(2)}, u32[]{:S(2)}) %collective-permute-start.2) | collective-permute-done | bytes 327712 | tf_op jit(solution)/shard_map/ppermute | solution.py:654
  22.3 1.5 %collective-permute-start.8 = (bf16[384,256]{1,0:T(8,128)(2,1)S(1)}, bf16[384,256]{1,0:T(8,128)(2,1)S(1)}, u32[]{:S(2)}, u32[]{:S(2)}) collective-permute-start(bf16[384,256]{1,0:T(8,128)(2,1)S(1)} %get-tuple-element.52), channel_id=1, source_target_pairs={{0,8},{4,12},{8,0},{12,4},{16,24},{20,28},{24,16},{28,20},{1,9},{5... | collective-permute-start | bytes 589832 | tf_op jit(solution)/shard_map/ppermute | solution.py:654
  24.4 1.4 %collective-permute-start.10 = (bf16[384,256]{1,0:T(8,128)(2,1)S(1)}, bf16[384,256]{1,0:T(8,128)(2,1)S(1)}, u32[]{:S(2)}, u32[]{:S(2)}) collective-permute-start(bf16[384,256]{1,0:T(8,128)(2,1)S(1)} %get-tuple-element.54), channel_id=1, source_target_pairs={{0,24},{4,28},{8,16},{12,20},{16,8},{20,12},{24,0},{28,4},{1,25},{... | collective-permute-start | bytes 589832 | tf_op jit(solution)/shard_map/ppermute | solution.py:654
  25.8 1.5 %forward.1.spectrum_ref = f32[256,2048]{1,0:T(8,128)S(1)} custom-call(f32[2,128,8]{2,1,0:T(8,128)S(1)} %copy-done.2, f32[2,128,8]{2,1,0:T(8,128)S(1)} %copy-done.1, bf16[256,256]{1,0:T(8,128)(2,1)S(1)} %copy-done.3, bf16[2,128,256]{2,1,0:T(8,128)(2,1)S(1)} %pad_maximum_fusion.refs_0_, bf16[2,128,256]{2,1,0:T(8,128)(2,1)S(1)} %pad_maximum_fusion.1.refs_1_, ...), custom_call_target="tpu_custom_call" | custom-call | tf_op jit(solution)/shard_map/forward/pallas_call | solution.py:358
  27.3 2.0 %backward.1 = (f32[4,128,256]{2,1,0:T(8,128)S(1)}, bf16[2,128,256]{2,1,0:T(8,128)(2,1)S(1)}, bf16[2,128,256]{2,1,0:T(8,128)(2,1)S(1)}) custom-call(f32[2,128,8]{2,1,0:T(8,128)S(1)} %copy-done.2, f32[2,128,8]{2,1,0:T(8,128)S(1)} %copy-done.1, bf16[256,256]{1,0:T(8,128)(2,1)S(1)} %copy-done.4, f32[256,2048]{1,0:T(8,128)S(1)} %forward.1.spectrum_ref, ...), custom_call_target="tpu_custom_call" | custom-call | tf_op jit(solution)/shard_map/backward/pallas_call | solution.py:433
  30.0 4.6 %collective-permute-done.9.refs_6_.refs_2_ = bf16[384,256]{1,0:T(8,128)(2,1)S(1)} collective-permute-done((bf16[384,256]{1,0:T(8,128)(2,1)S(1)}, bf16[384,256]{1,0:T(8,128)(2,1)S(1)}, u32[]{:S(2)}, u32[]{:S(2)}) %collective-permute-start.9) | collective-permute-done | bytes 196640 | tf_op jit(solution)/shard_map/ppermute | solution.py:654
  35.0 1.5 %collective-permute-start.13 = (bf16[512,256]{1,0:T(8,128)(2,1)S(1)}, bf16[512,256]{1,0:T(8,128)(2,1)S(1)}, u32[]{:S(2)}, u32[]{:S(2)}) collective-permute-start(bf16[512,256]{1,0:T(8,128)(2,1)S(1)} %gate.1.refs_0_), channel_id=1, source_target_pairs={{0,24},{4,28},{8,16},{12,20},{16,8},{20,12},{24,0},{28,4},{1,25},{... | collective-permute-start | bytes 786440 | tf_op jit(solution)/shard_map/ppermute | solution.py:654
  37.1 1.5 %collective-permute-start.11 = (bf16[512,256]{1,0:T(8,128)(2,1)S(1)}, bf16[512,256]{1,0:T(8,128)(2,1)S(1)}, u32[]{:S(2)}, u32[]{:S(2)}) collective-permute-start(bf16[512,256]{1,0:T(8,128)(2,1)S(1)} %gate.1.refs_0_), channel_id=1, source_target_pairs={{0,8},{4,12},{8,0},{12,4},{16,24},{20,28},{24,16},{28,20},{1,9},{5... | collective-permute-start | bytes 786440 | tf_op jit(solution)/shard_map/ppermute | solution.py:654
  38.6 6.6 %collective-permute-done.13.refs_3_ = bf16[512,256]{1,0:T(8,128)(2,1)S(1)} collective-permute-done((bf16[512,256]{1,0:T(8,128)(2,1)S(1)}, bf16[512,256]{1,0:T(8,128)(2,1)S(1)}, u32[]{:S(2)}, u32[]{:S(2)}) %collective-permute-start.13) | collective-permute-done | bytes 262176 | tf_op jit(solution)/shard_map/ppermute | solution.py:654
  45.1 5.1 %collective-permute-done.12.refs_2_ = bf16[512,256]{1,0:T(8,128)(2,1)S(1)} collective-permute-done((bf16[512,256]{1,0:T(8,128)(2,1)S(1)}, bf16[512,256]{1,0:T(8,128)(2,1)S(1)}, u32[]{:S(2)}, u32[]{:S(2)}) %collective-permute-start.12) | collective-permute-done | bytes 262176 | tf_op jit(solution)/shard_map/ppermute | solution.py:654
  51.1 1.6 %collective-permute-start.20 = (bf16[2,512,128]{2,1,0:T(8,128)(2,1)S(1)}, bf16[2,512,128]{2,1,0:T(8,128)(2,1)S(1)}, u32[]{:S(2)}, u32[]{:S(2)}) collective-permute-start(bf16[2,512,128]{2,1,0:T(8,128)(2,1)S(1)} %get-tuple-element.67), channel_id=1, source_target_pairs={{0,1},{1,0},{2,3},{3,2},{4,5},{5,4},{6,7},{7,6},{8,9},{9,8},{10,11... | collective-permute-start | bytes 786440 | tf_op jit(solution)/shard_map/ppermute | solution.py:654
  54.2 1.4 %collective-permute-start.15 = (bf16[128,512]{1,0:T(8,128)(2,1)S(1)}, bf16[128,512]{1,0:T(8,128)(2,1)S(1)}, u32[]{:S(2)}, u32[]{:S(2)}) collective-permute-start(bf16[128,512]{1,0:T(8,128)(2,1)S(1)} %get-tuple-element.57), channel_id=1, source_target_pairs={{0,16},{4,20},{8,24},{12,28},{16,0},{20,4},{24,8},{28,12},{1,17},{... | collective-permute-start | bytes 393224 | tf_op jit(solution)/shard_map/ppermute | solution.py:654
  55.6 1.5 %collective-permute-start.16 = (bf16[128,512]{1,0:T(8,128)(2,1)S(1)}, bf16[128,512]{1,0:T(8,128)(2,1)S(1)}, u32[]{:S(2)}, u32[]{:S(2)}) collective-permute-start(bf16[128,512]{1,0:T(8,128)(2,1)S(1)} %get-tuple-element.58), channel_id=1, source_target_pairs={{0,24},{4,28},{8,16},{12,20},{16,8},{20,12},{24,0},{28,4},{1,25},{... | collective-permute-start | bytes 393224 | tf_op jit(solution)/shard_map/ppermute | solution.py:654
  57.2 2.9 %collective-permute-done.14.refs_1_ = bf16[128,512]{1,0:T(8,128)(2,1)S(1)} collective-permute-done((bf16[128,512]{1,0:T(8,128)(2,1)S(1)}, bf16[128,512]{1,0:T(8,128)(2,1)S(1)}, u32[]{:S(2)}, u32[]{:S(2)}) %collective-permute-start.14) | collective-permute-done | bytes 131104 | tf_op jit(solution)/shard_map/ppermute | solution.py:654
  60.1 1.9 %collective-permute-done.15.refs_2_ = bf16[128,512]{1,0:T(8,128)(2,1)S(1)} collective-permute-done((bf16[128,512]{1,0:T(8,128)(2,1)S(1)}, bf16[128,512]{1,0:T(8,128)(2,1)S(1)}, u32[]{:S(2)}, u32[]{:S(2)}) %collective-permute-start.15) | collective-permute-done | bytes 131104 | tf_op jit(solution)/shard_map/ppermute | solution.py:654
  62.7 2.7 %collective-permute-start.21 = (bf16[512,128]{1,0:T(8,128)(2,1)S(1)}, bf16[512,128]{1,0:T(8,128)(2,1)S(1)}, u32[]{:S(2)}, u32[]{:S(2)}) collective-permute-start(bf16[512,128]{1,0:T(8,128)(2,1)S(1)} %fusion), channel_id=1, source_target_pairs={{0,2},{1,3},{2,0},{3,1},{4,6},{5,7},{6,4},{7,5},{8,10},{9,11},{10,... | collective-permute-start | bytes 393224 | tf_op jit(solution)/shard_map/ppermute | solution.py:654
  65.3 6.6 %collective-permute-done.17.first_ref = bf16[2,128,512]{2,1,0:T(8,128)(2,1)S(1)} collective-permute-done((bf16[2,128,512]{2,1,0:T(8,128)(2,1)S(1)}, bf16[2,128,512]{2,1,0:T(8,128)(2,1)S(1)}, u32[]{:S(2)}, u32[]{:S(2)}) %collective-permute-start.17) | collective-permute-done | bytes 262176 | tf_op jit(solution)/shard_map/ppermute | solution.py:654
  73.3 1.3 %collective-permute-start.22 = (bf16[128,128]{1,0:T(8,128)(2,1)S(1)}, bf16[128,128]{1,0:T(8,128)(2,1)S(1)}, u32[]{:S(2)}, u32[]{:S(2)}) collective-permute-start(bf16[128,128]{1,0:T(8,128)(2,1)S(1)} %get-tuple-element.70), channel_id=1, source_target_pairs={{0,8},{4,12},{8,0},{12,4},{16,24},{20,28},{24,16},{28,20},{1,9},{5... | collective-permute-start | bytes 98312 | tf_op jit(solution)/shard_map/ppermute | solution.py:654
  75.1 1.8 %collective-permute-start.24 = (bf16[128,128]{1,0:T(8,128)(2,1)S(1)}, bf16[128,128]{1,0:T(8,128)(2,1)S(1)}, u32[]{:S(2)}, u32[]{:S(2)}) collective-permute-start(bf16[128,128]{1,0:T(8,128)(2,1)S(1)} %get-tuple-element.72), channel_id=1, source_target_pairs={{0,24},{4,28},{8,16},{12,20},{16,8},{20,12},{24,0},{28,4},{1,25},{... | collective-permute-start | bytes 98312 | tf_op jit(solution)/shard_map/ppermute | solution.py:654
  76.9 2.7 %collective-permute-done.18.second_ref = bf16[128,512]{1,0:T(8,128)(2,1)S(1)} collective-permute-done((bf16[128,512]{1,0:T(8,128)(2,1)S(1)}, bf16[128,512]{1,0:T(8,128)(2,1)S(1)}, u32[]{:S(2)}, u32[]{:S(2)}) %collective-permute-start.18) | collective-permute-done | bytes 131104 | tf_op jit(solution)/shard_map/ppermute | solution.py:654
  (57 shorter events, 10.2 us)
Async XLA Ops:
  0.0 6.5 %collective-permute-start = (bf16[1024,512]{1,0:T(8,128)(2,1)}, bf16[1024,512]{1,0:T(8,128)(2,1)S(1)}, u32[]{:S(2)}, u32[]{:S(2)}) collective-permute-start(bf16[1024,512]{1,0:T(8,128)(2,1)} %own_ref.3), channel_id=1, source_target_pairs={{0,4},{4,0},{8,12},{12,8},{16,20},{20,16},{24,28},{28,24},{1,5},{5... | collective-permute-start | bytes 3145736 | tf_op jit(solution)/shard_map/ppermute | solution.py:654
  2.4 12.1 %collective-permute-start.3 = (bf16[5,128,256]{2,1,0:T(8,128)(2,1)S(1)}, bf16[5,128,256]{2,1,0:T(8,128)(2,1)S(1)}, u32[]{:S(2)}, u32[]{:S(2)}) collective-permute-start(bf16[5,128,256]{2,1,0:T(8,128)(2,1)S(1)} %get-tuple-element.47), channel_id=1, source_target_pairs={{0,24},{4,28},{8,16},{12,20},{16,8},{20,12},{24,0},{28,4},{1,25},{... | collective-permute-start | bytes 983048 | tf_op jit(solution)/shard_map/ppermute | solution.py:654
  5.9 15.4 %collective-permute-start.2 = (bf16[5,128,256]{2,1,0:T(8,128)(2,1)S(1)}, bf16[5,128,256]{2,1,0:T(8,128)(2,1)S(1)}, u32[]{:S(2)}, u32[]{:S(2)}) collective-permute-start(bf16[5,128,256]{2,1,0:T(8,128)(2,1)S(1)} %get-tuple-element.45), channel_id=1, source_target_pairs={{0,16},{4,20},{8,24},{12,28},{16,0},{20,4},{24,8},{28,12},{1,17},{... | collective-permute-start | bytes 983048 | tf_op jit(solution)/shard_map/ppermute | solution.py:654
  6.4 15.2 %collective-permute-start.1 = (bf16[5,128,256]{2,1,0:T(8,128)(2,1)S(1)}, bf16[5,128,256]{2,1,0:T(8,128)(2,1)S(1)}, u32[]{:S(2)}, u32[]{:S(2)}) collective-permute-start(bf16[5,128,256]{2,1,0:T(8,128)(2,1)S(1)} %get-tuple-element.43), channel_id=1, source_target_pairs={{0,8},{4,12},{8,0},{12,4},{16,24},{20,28},{24,16},{28,20},{1,9},{5... | collective-permute-start | bytes 983048 | tf_op jit(solution)/shard_map/ppermute | solution.py:654
  21.6 4.2 %collective-permute-start.5 = (bf16[2,128,256]{2,1,0:T(8,128)(2,1)S(1)}, bf16[2,128,256]{2,1,0:T(8,128)(2,1)S(1)}, u32[]{:S(2)}, u32[]{:S(2)}) collective-permute-start(bf16[2,128,256]{2,1,0:T(8,128)(2,1)S(1)} %pad_maximum_fusion.1.refs_1_), channel_id=1, source_target_pairs={{0,4},{4,0},{8,12},{12,8},{16,20},{20,16},{24,28},{28,24},{1,5},{5... | collective-permute-start | bytes 393224 | tf_op jit(solution)/shard_map/ppermute | solution.py:654
  22.3 7.8 %collective-permute-start.8 = (bf16[384,256]{1,0:T(8,128)(2,1)S(1)}, bf16[384,256]{1,0:T(8,128)(2,1)S(1)}, u32[]{:S(2)}, u32[]{:S(2)}) collective-permute-start(bf16[384,256]{1,0:T(8,128)(2,1)S(1)} %get-tuple-element.52), channel_id=1, source_target_pairs={{0,8},{4,12},{8,0},{12,4},{16,24},{20,28},{24,16},{28,20},{1,9},{5... | collective-permute-start | bytes 589832 | tf_op jit(solution)/shard_map/ppermute | solution.py:654
  23.8 10.8 %collective-permute-start.9 = (bf16[384,256]{1,0:T(8,128)(2,1)S(1)}, bf16[384,256]{1,0:T(8,128)(2,1)S(1)}, u32[]{:S(2)}, u32[]{:S(2)}) collective-permute-start(bf16[384,256]{1,0:T(8,128)(2,1)S(1)} %get-tuple-element.53), channel_id=1, source_target_pairs={{0,16},{4,20},{8,24},{12,28},{16,0},{20,4},{24,8},{28,12},{1,17},{... | collective-permute-start | bytes 589832 | tf_op jit(solution)/shard_map/ppermute | solution.py:654
  24.4 10.2 %collective-permute-start.10 = (bf16[384,256]{1,0:T(8,128)(2,1)S(1)}, bf16[384,256]{1,0:T(8,128)(2,1)S(1)}, u32[]{:S(2)}, u32[]{:S(2)}) collective-permute-start(bf16[384,256]{1,0:T(8,128)(2,1)S(1)} %get-tuple-element.54), channel_id=1, source_target_pairs={{0,24},{4,28},{8,16},{12,20},{16,8},{20,12},{24,0},{28,4},{1,25},{... | collective-permute-start | bytes 589832 | tf_op jit(solution)/shard_map/ppermute | solution.py:654
  29.3 5.3 %collective-permute-start.6 = (bf16[2,128,256]{2,1,0:T(8,128)(2,1)S(1)}, bf16[2,128,256]{2,1,0:T(8,128)(2,1)S(1)}, u32[]{:S(2)}, u32[]{:S(2)}) collective-permute-start(bf16[2,128,256]{2,1,0:T(8,128)(2,1)S(1)} %get-tuple-element.50), channel_id=1, source_target_pairs={{0,4},{4,0},{8,12},{12,8},{16,20},{20,16},{24,28},{28,24},{1,5},{5... | collective-permute-start | bytes 393224 | tf_op jit(solution)/shard_map/ppermute | solution.py:654
  29.4 5.2 %collective-permute-start.7 = (bf16[2,128,256]{2,1,0:T(8,128)(2,1)S(1)}, bf16[2,128,256]{2,1,0:T(8,128)(2,1)S(1)}, u32[]{:S(2)}, u32[]{:S(2)}) collective-permute-start(bf16[2,128,256]{2,1,0:T(8,128)(2,1)S(1)} %get-tuple-element.51), channel_id=1, source_target_pairs={{0,4},{4,0},{8,12},{12,8},{16,20},{20,16},{24,28},{28,24},{1,5},{5... | collective-permute-start | bytes 393224 | tf_op jit(solution)/shard_map/ppermute | solution.py:654
  34.9 15.3 %collective-permute-start.19 = (bf16[512,512]{1,0:T(8,128)(2,1)S(1)}, bf16[512,512]{1,0:T(8,128)(2,1)S(1)}, u32[]{:S(2)}, u32[]{:S(2)}) collective-permute-start(bf16[512,512]{1,0:T(8,128)(2,1)S(1)} %collect_weights.1.own_ref), channel_id=1, source_target_pairs={{0,4},{4,0},{8,12},{12,8},{16,20},{20,16},{24,28},{28,24},{1,5},{5... | collective-permute-start | bytes 1572872 | tf_op jit(solution)/shard_map/ppermute | solution.py:654
  35.0 10.1 %collective-permute-start.13 = (bf16[512,256]{1,0:T(8,128)(2,1)S(1)}, bf16[512,256]{1,0:T(8,128)(2,1)S(1)}, u32[]{:S(2)}, u32[]{:S(2)}) collective-permute-start(bf16[512,256]{1,0:T(8,128)(2,1)S(1)} %gate.1.refs_0_), channel_id=1, source_target_pairs={{0,24},{4,28},{8,16},{12,20},{16,8},{20,12},{24,0},{28,4},{1,25},{... | collective-permute-start | bytes 786440 | tf_op jit(solution)/shard_map/ppermute | solution.py:654
  36.5 13.8 %collective-permute-start.12 = (bf16[512,256]{1,0:T(8,128)(2,1)S(1)}, bf16[512,256]{1,0:T(8,128)(2,1)S(1)}, u32[]{:S(2)}, u32[]{:S(2)}) collective-permute-start(bf16[512,256]{1,0:T(8,128)(2,1)S(1)} %gate.1.refs_0_), channel_id=1, source_target_pairs={{0,16},{4,20},{8,24},{12,28},{16,0},{20,4},{24,8},{28,12},{1,17},{... | collective-permute-start | bytes 786440 | tf_op jit(solution)/shard_map/ppermute | solution.py:654
  37.1 13.2 %collective-permute-start.11 = (bf16[512,256]{1,0:T(8,128)(2,1)S(1)}, bf16[512,256]{1,0:T(8,128)(2,1)S(1)}, u32[]{:S(2)}, u32[]{:S(2)}) collective-permute-start(bf16[512,256]{1,0:T(8,128)(2,1)S(1)} %gate.1.refs_0_), channel_id=1, source_target_pairs={{0,8},{4,12},{8,0},{12,4},{16,24},{20,28},{24,16},{28,20},{1,9},{5... | collective-permute-start | bytes 786440 | tf_op jit(solution)/shard_map/ppermute | solution.py:654
  51.1 11.5 %collective-permute-start.20 = (bf16[2,512,128]{2,1,0:T(8,128)(2,1)S(1)}, bf16[2,512,128]{2,1,0:T(8,128)(2,1)S(1)}, u32[]{:S(2)}, u32[]{:S(2)}) collective-permute-start(bf16[2,512,128]{2,1,0:T(8,128)(2,1)S(1)} %get-tuple-element.67), channel_id=1, source_target_pairs={{0,1},{1,0},{2,3},{3,2},{4,5},{5,4},{6,7},{7,6},{8,9},{9,8},{10,11... | collective-permute-start | bytes 786440 | tf_op jit(solution)/shard_map/ppermute | solution.py:654
  53.6 6.5 %collective-permute-start.14 = (bf16[128,512]{1,0:T(8,128)(2,1)S(1)}, bf16[128,512]{1,0:T(8,128)(2,1)S(1)}, u32[]{:S(2)}, u32[]{:S(2)}) collective-permute-start(bf16[128,512]{1,0:T(8,128)(2,1)S(1)} %get-tuple-element.56), channel_id=1, source_target_pairs={{0,8},{4,12},{8,0},{12,4},{16,24},{20,28},{24,16},{28,20},{1,9},{5... | collective-permute-start | bytes 393224 | tf_op jit(solution)/shard_map/ppermute | solution.py:654
  54.2 7.8 %collective-permute-start.15 = (bf16[128,512]{1,0:T(8,128)(2,1)S(1)}, bf16[128,512]{1,0:T(8,128)(2,1)S(1)}, u32[]{:S(2)}, u32[]{:S(2)}) collective-permute-start(bf16[128,512]{1,0:T(8,128)(2,1)S(1)} %get-tuple-element.57), channel_id=1, source_target_pairs={{0,16},{4,20},{8,24},{12,28},{16,0},{20,4},{24,8},{28,12},{1,17},{... | collective-permute-start | bytes 393224 | tf_op jit(solution)/shard_map/ppermute | solution.py:654
  55.6 6.4 %collective-permute-start.16 = (bf16[128,512]{1,0:T(8,128)(2,1)S(1)}, bf16[128,512]{1,0:T(8,128)(2,1)S(1)}, u32[]{:S(2)}, u32[]{:S(2)}) collective-permute-start(bf16[128,512]{1,0:T(8,128)(2,1)S(1)} %get-tuple-element.58), channel_id=1, source_target_pairs={{0,24},{4,28},{8,16},{12,20},{16,8},{20,12},{24,0},{28,4},{1,25},{... | collective-permute-start | bytes 393224 | tf_op jit(solution)/shard_map/ppermute | solution.py:654
  62.1 9.9 %collective-permute-start.17 = (bf16[2,128,512]{2,1,0:T(8,128)(2,1)S(1)}, bf16[2,128,512]{2,1,0:T(8,128)(2,1)S(1)}, u32[]{:S(2)}, u32[]{:S(2)}) collective-permute-start(bf16[2,128,512]{2,1,0:T(8,128)(2,1)S(1)} %get-tuple-element.60), channel_id=1, source_target_pairs={{0,1},{1,0},{2,3},{3,2},{4,5},{5,4},{6,7},{7,6},{8,9},{9,8},{10,11... | collective-permute-start | bytes 786440 | tf_op jit(solution)/shard_map/ppermute | solution.py:654
  62.7 10.6 %collective-permute-start.21 = (bf16[512,128]{1,0:T(8,128)(2,1)S(1)}, bf16[512,128]{1,0:T(8,128)(2,1)S(1)}, u32[]{:S(2)}, u32[]{:S(2)}) collective-permute-start(bf16[512,128]{1,0:T(8,128)(2,1)S(1)} %fusion), channel_id=1, source_target_pairs={{0,2},{1,3},{2,0},{3,1},{4,6},{5,7},{6,4},{7,5},{8,10},{9,11},{10,... | collective-permute-start | bytes 393224 | tf_op jit(solution)/shard_map/ppermute | solution.py:654
  72.0 7.6 %collective-permute-start.18 = (bf16[128,512]{1,0:T(8,128)(2,1)S(1)}, bf16[128,512]{1,0:T(8,128)(2,1)S(1)}, u32[]{:S(2)}, u32[]{:S(2)}) collective-permute-start(bf16[128,512]{1,0:T(8,128)(2,1)S(1)} %fusion.1), channel_id=1, source_target_pairs={{0,2},{1,3},{2,0},{3,1},{4,6},{5,7},{6,4},{7,5},{8,10},{9,11},{10,... | collective-permute-start | bytes 393224 | tf_op jit(solution)/shard_map/ppermute | solution.py:654
  73.3 6.3 %collective-permute-start.22 = (bf16[128,128]{1,0:T(8,128)(2,1)S(1)}, bf16[128,128]{1,0:T(8,128)(2,1)S(1)}, u32[]{:S(2)}, u32[]{:S(2)}) collective-permute-start(bf16[128,128]{1,0:T(8,128)(2,1)S(1)} %get-tuple-element.70), channel_id=1, source_target_pairs={{0,8},{4,12},{8,0},{12,4},{16,24},{20,28},{24,16},{28,20},{1,9},{5... | collective-permute-start | bytes 98312 | tf_op jit(solution)/shard_map/ppermute | solution.py:654
  74.6 5.0 %collective-permute-start.23 = (bf16[128,128]{1,0:T(8,128)(2,1)S(1)}, bf16[128,128]{1,0:T(8,128)(2,1)S(1)}, u32[]{:S(2)}, u32[]{:S(2)}) collective-permute-start(bf16[128,128]{1,0:T(8,128)(2,1)S(1)} %get-tuple-element.71), channel_id=1, source_target_pairs={{0,16},{4,20},{8,24},{12,28},{16,0},{20,4},{24,8},{28,12},{1,17},{... | collective-permute-start | bytes 98312 | tf_op jit(solution)/shard_map/ppermute | solution.py:654
  75.1 4.8 %collective-permute-start.24 = (bf16[128,128]{1,0:T(8,128)(2,1)S(1)}, bf16[128,128]{1,0:T(8,128)(2,1)S(1)}, u32[]{:S(2)}, u32[]{:S(2)}) collective-permute-start(bf16[128,128]{1,0:T(8,128)(2,1)S(1)} %get-tuple-element.72), channel_id=1, source_target_pairs={{0,24},{4,28},{8,16},{12,20},{16,8},{20,12},{24,0},{28,4},{1,25},{... | collective-permute-start | bytes 98312 | tf_op jit(solution)/shard_map/ppermute | solution.py:654
  (7 other events, 119.2 us)

commit v11 on v10

--- a/solution.py
+++ b/solution.py
@@ -213,64 +213,67 @@
     return pl.ds(pl.multiple_of(index * size, size), size)
 
 
-def pack_signals_kernel(offsets, filter_ref, values_ref, *refs):
-    out_refs, (plane_ref, arrived) = refs[: len(offsets)], refs[len(offsets) :]
+def pack_signals_kernel(chips, values_ref, filter_ref, *refs):
+    out_refs, (plane_ref, arrived) = refs[:chips], refs[chips:]
     chip, _ = own_place()
-    planes = filter_ref.shape[0]
-    lanes = out_refs[0].shape[2]
+    planes, rows, _ = filter_ref.shape
+    lanes = out_refs[0].shape[1]
     copies, work = [], []
-    for place, offset in enumerate(offsets):
+    for offset in range(chips):
         here = block_at(chip ^ offset, lanes)
         for plane in range(planes):
             copies.append(
-                pltpu.make_async_copy(filter_ref.at[plane, :, here], plane_ref.at[place, plane], arrived.at[place, plane])
+                pltpu.make_async_copy(filter_ref.at[plane, :, here], plane_ref.at[offset, plane], arrived.at[offset, plane])
             )
-            work.append((place, plane))
-        copies.append(
-            pltpu.make_async_copy(values_ref.at[:, here], out_refs[place].at[planes], arrived.at[place, planes])
-        )
+            work.append((offset, plane))
+        values = out_refs[offset].at[pl.ds(planes * rows, rows)]
+        copies.append(pltpu.make_async_copy(values_ref.at[:, here], values, arrived.at[offset, planes]))
         work.append(None)
     for copy in copies:
         copy.start()
     for copy, task in zip(copies, work):
         copy.wait()
         if task:
-            place, plane = task
-            out_refs[place][plane] = plane_ref[place, plane].astype(BF16)
-
-
-def pack_signals(values_in, filters, chips, offsets):
+            offset, plane = task
+            out_refs[offset][pl.ds(plane * rows, rows), :] = plane_ref[offset, plane].astype(BF16)
+    used = (planes + 1) * rows
+    for out_ref in out_refs:
+        if out_ref.shape[0] > used:
+            out_ref[pl.ds(used, out_ref.shape[0] - used), :] = out_ref[pl.ds(0, out_ref.shape[0] - used), :]
+
+
+def pack_signals(values_in, filters, chips, spare):
     planes, rows, width = filters.shape
     lanes = width // chips
     return pl.pallas_call(
-        functools.partial(pack_signals_kernel, offsets),
+        functools.partial(pack_signals_kernel, chips),
         in_specs=[pl.BlockSpec(memory_space=pltpu.HBM)] * 2,
-        out_specs=[WHOLE] * len(offsets),
-        out_shape=[jax.ShapeDtypeStruct((planes + 1, rows, lanes), BF16)] * len(offsets),
+        out_specs=[WHOLE] * chips,
+        out_shape=[jax.ShapeDtypeStruct(((planes + 1) * rows + more, lanes), BF16) for more in spare],
         scratch_shapes=[
-            pltpu.VMEM((len(offsets), planes, rows, lanes), F32),
-            pltpu.SemaphoreType.DMA((len(offsets), planes + 1)),
+            pltpu.VMEM((chips, planes, rows, lanes), F32),
+            pltpu.SemaphoreType.DMA((chips, planes + 1)),
         ],
         cost_estimate=CHEAP,
         compiler_params=pltpu.CompilerParams(vmem_limit_bytes=8 * 2**20),
         name="pack_signals",
-    )(*(pltpu.with_memory_space_constraint(array, pltpu.HBM) for array in (filters, values_in)))
+    )(*(pltpu.with_memory_space_constraint(array, pltpu.HBM) for array in (values_in, filters)))
 
 
 def pack_moved_kernel(chips, gate_ref, own_ref, other_ref, *refs):
-    out_refs, arrived = refs[:chips], refs[chips]
+    out_refs, (mine_ref, arrived) = refs[:chips], refs[chips:]
     chip, core = own_place()
     rows = gate_ref.shape[0]
     depth, held = own_ref.shape
     quarter, share = depth // 4, held // chips
 
     def copies_from(weight_ref):
-        copies = []
+        copies = [pltpu.make_async_copy(weight_ref.at[:, block_at(chip, share)], mine_ref, arrived.at[0, 0])]
         for offset in range(chips):
             out_ref, target = out_refs[offset], chip ^ offset
             gates = gate_ref.at[:, block_at(target, out_ref.shape[1])]
             copies.append(pltpu.make_async_copy(gates, out_ref.at[pl.ds(0, rows)], arrived.at[offset, 2]))
-            for part in range(2):
+            for part in range(2 if offset else 0):
                 source = weight_ref.at[block_at(2 * core + part, quarter), block_at(target, share)]
                 sink = out_ref.at[pl.ds(rows, quarter), pl.ds(part * share, share)]
                 copies.append(pltpu.make_async_copy(source, sink, arrived.at[offset, part]))
@@ -291,16 +294,41 @@
 def pack_moved(gate_values, own, other, chips):
     rows, width = gate_values.shape
     depth, held = own.shape
+    share = held // chips
     return pl.pallas_call(
         functools.partial(pack_moved_kernel, chips),
         in_specs=[pl.BlockSpec(memory_space=pltpu.HBM)] * 2 + [pl.BlockSpec(memory_space=pl.ANY)],
-        out_specs=[WHOLE] * chips,
-        out_shape=[jax.ShapeDtypeStruct((rows + depth // 4, 2 * held // chips), BF16)] * chips,
+        out_specs=[WHOLE] * (chips + 1),
+        out_shape=[
+            *(jax.ShapeDtypeStruct((rows + (depth // 4 if offset else 0), 2 * share), BF16) for offset in range(chips)),
+            jax.ShapeDtypeStruct((depth, share), BF16),
+        ],
         scratch_shapes=[pltpu.SemaphoreType.DMA((chips, 3))],
         cost_estimate=CHEAP,
         compiler_params=pltpu.CompilerParams(vmem_limit_bytes=8 * 2**20),
         name="pack_moved",
     )(*(pltpu.with_memory_space_constraint(array, pltpu.HBM) for array in (gate_values, own)), other)
+
+
+def pick_values_kernel(chips, start, *refs):
+    in_refs, out_refs = refs[:chips], refs[chips:]
+    for offset in range(chips):
+        part, place = divmod(offset, chips // 2)
+        out_refs[part][place] = in_refs[offset][pl.ds(start, out_refs[part].shape[1]), :]
+
+
+def pick_values(first, rows, start):
+    chips = len(first)
+    half = jax.ShapeDtypeStruct((chips // 2, rows, first[0].shape[1]), BF16)
+    return pl.pallas_call(
+        functools.partial(pick_values_kernel, chips, start),
+        in_specs=[WHOLE] * chips,
+        out_specs=[WHOLE] * 2,
+        out_shape=[half, half],
+        cost_estimate=CHEAP,
+        compiler_params=pltpu.CompilerParams(vmem_limit_bytes=4 * 2**20),
+        name="pick_values",
+    )(*first)
 
 
 def forward_kernel(chips, cos_ref, sin_ref, table_ref, *refs):
@@ -375,7 +403,8 @@
     chip_bits = chips.bit_length() - 1
     chunk, width = 16, 128
     for offset in range(chips):
-        filter_ref[chip ^ offset] = filter_refs[offset][pl.ds(0, 4)]
+        for plane in range(filter_ref.shape[1]):
+            filter_ref[chip ^ offset, plane] = filter_refs[offset][pl.ds(plane * rows, rows), :]
 
     for residue in range(parts):
         source, odd = bit_reversed(residue // 2, chip_bits), residue % 2
@@ -427,7 +456,7 @@
 
 def backward(spectrum, first, tables):
     chips = len(first)
-    _, rows, lanes = first[0].shape
+    rows, lanes = spectrum.shape[0] // 2, first[0].shape[1]
     _, table, cos, sin = tables
     half = jax.ShapeDtypeStruct((chips // 2, rows, lanes), BF16)
     return pl.pallas_call(
@@ -447,7 +476,8 @@
 
 
 def gate_kernel(chips, skip_ref, keep_ref, low_ref, high_ref, *refs):
-    signal_refs, gate_refs, (out_ref, arrived_ref) = refs[:chips], refs[chips : 2 * chips], refs[2 * chips :]
+    signal_refs, gate_refs = refs[:chips], refs[chips : 2 * chips]
+    out_ref, longer_ref, arrived_ref = refs[2 * chips :]
     chip, _ = own_place()
     rows, lanes = keep_ref.shape[1:]
     skip = skip_ref[:, block_at(chip, lanes)]
@@ -456,18 +486,25 @@
     for offset in range(chips):
         block = chip ^ offset
         convolved = keep_ref[block] + arrived_ref[block].astype(F32)
-        signal = signal_refs[offset][4].astype(F32)
+        signal = signal_refs[offset][pl.ds(4 * rows, rows), :].astype(F32)
         gate = gate_refs[offset][pl.ds(0, rows), :].astype(F32)
-        out_ref[block_at(block, rows), :] = (gate * (convolved + skip * signal)).astype(BF16)
-
-
-def gate(skip, keep, arrived, first, gates):
+        gated = (gate * (convolved + skip * signal)).astype(BF16)
+        out_ref[block_at(block, rows), :] = gated
+        longer_ref[block_at(block, rows), :] = gated
+    end = chips * rows
+    longer_ref[pl.ds(end, longer_ref.shape[0] - end), :] = longer_ref[pl.ds(0, longer_ref.shape[0] - end), :]
+
+
+def gate(skip, keep, arrived, first, gates, spare):
     chips, rows, lanes = keep.shape
     return pl.pallas_call(
         functools.partial(gate_kernel, chips),
         in_specs=[WHOLE] * (4 + 2 * chips),
-        out_specs=WHOLE,
-        out_shape=jax.ShapeDtypeStruct((chips * rows, lanes), BF16),
+        out_specs=[WHOLE] * 2,
+        out_shape=[
+            jax.ShapeDtypeStruct((chips * rows, lanes), BF16),
+            jax.ShapeDtypeStruct((chips * rows + spare, lanes), BF16),
+        ],
         scratch_shapes=[pltpu.VMEM((chips, rows, lanes), BF16)],
         cost_estimate=CHEAP,
         compiler_params=pltpu.CompilerParams(vmem_limit_bytes=6 * 2**20),
@@ -475,68 +512,95 @@
     )(skip, keep, *arrived, *first, *gates)
 
 
-def collect_kernel(chips, *refs):
-    in_refs, out_ref = refs[:chips], refs[chips]
-    chip, _ = own_place()
-    layer = lax.axis_index("chan")
-    quarter, share = out_ref.shape[0] // 2, out_ref.shape[1] // chips
-    start = in_refs[0].shape[0] - quarter
-    for offset in range(chips):
-        for part in range(2):
-            block = in_refs[offset][pl.ds(start, quarter), pl.ds(part * share, share)]
-            out_ref[pl.ds(part * quarter, quarter), block_at(chip ^ layer ^ offset, share)] = block
+def piece_of(ref, half, part):
+    quarter, share = half // 2, ref.shape[1] // 2
+    return ref[pl.ds(ref.shape[0] - quarter, quarter), pl.ds(part * share, share)]
+
+
+def collect_kernel(in_refs, out_refs):
+    rows = out_refs[0].shape[0]
+    quarter = len(out_refs) * rows // (2 * len(in_refs))
+    for place in range(2 * len(in_refs)):
+        index, start = divmod(place * quarter, rows)
+        out_refs[index][pl.ds(start, quarter), :] = piece_of(in_refs[place // 2], 2 * quarter, place % 2)
 
 
 def collect(moved, half):
-    chips = len(moved)
-    return pl.pallas_call(
-        functools.partial(collect_kernel, chips),
-        in_specs=[WHOLE] * chips,
-        out_specs=WHOLE,
-        out_shape=jax.ShapeDtypeStruct((half, chips * moved[0].shape[1] // 2), BF16),
+    count = len(moved)
+    shape = (count * half // 2, moved[0].shape[1] // 2)
+    return pl.pallas_call(
+        lambda *refs: collect_kernel(refs[:count], refs[count:]),
+        in_specs=[WHOLE] * count,
+        out_specs=[WHOLE] * 2,
+        out_shape=[jax.ShapeDtypeStruct(shape, BF16)] * 2,
         cost_estimate=CHEAP,
         compiler_params=pltpu.CompilerParams(vmem_limit_bytes=4 * 2**20),
         name="collect_weights",
     )(*moved)
 
 
+def arrange_kernel(chips, mine_ref, *refs):
+    moved_refs, (*other_refs, out_ref) = refs[: chips - 1], refs[chips - 1 :]
+    chip, core = own_place()
+    layer = lax.axis_index("chan")
+    depth, share = mine_ref.shape
+    quarter = depth // 4
+    out_ref[:, block_at(chip ^ layer, share)] = mine_ref[...]
+    for place in range(2 * (chips - 1)):
+        offset, part = place // 2 + 1, place % 2
+        columns = block_at(chip ^ layer ^ offset, share)
+        index, start = divmod(place * quarter, other_refs[0].shape[0])
+        out_ref[block_at(2 * core + part, quarter), columns] = piece_of(moved_refs[offset - 1], 2 * quarter, part)
+        out_ref[block_at(2 * (1 - core) + part, quarter), columns] = other_refs[index][pl.ds(start, quarter), :]
+
+
+def arrange(mine, moved, others):
+    chips = len(moved) + 1
+    depth, share = mine.shape
+    return pl.pallas_call(
+        functools.partial(arrange_kernel, chips),
+        in_specs=[WHOLE] * (chips + len(others)),
+        out_specs=WHOLE,
+        out_shape=jax.ShapeDtypeStruct((depth, chips * share), BF16),
+        cost_estimate=CHEAP,
+        compiler_params=pltpu.CompilerParams(vmem_limit_bytes=8 * 2**20),
+        name="arrange_weights",
+    )(mine, *moved, *others)
+
+
 def join_channels(chips, gated_refs, joined_ref):
     chip, _ = own_place()
     lanes = gated_refs[0].shape[1]
     for offset in range(chips):
-        joined_ref[:, block_at(chip ^ offset, lanes)] = gated_refs[offset][...]
-
-
-def project_moved_kernel(chips, own_ref, other_ref, *refs):
+        joined_ref[:, block_at(chip ^ offset, lanes)] = gated_refs[offset][pl.ds(0, joined_ref.shape[0]), :]
+
+
+def project_moved_kernel(chips, weight_ref, *refs):
     gated_refs, (keep_ref, pass_ref, send_ref, joined_ref) = refs[:chips], refs[chips:]
-    _, core = own_place()
-    half = own_ref.shape[0]
     share = keep_ref.shape[1]
     join_channels(chips, gated_refs, joined_ref)
-    partial = jnp.dot(joined_ref[:, block_at(core, half)], own_ref[...], preferred_element_type=F32)
-    partial += jnp.dot(joined_ref[:, block_at(1 - core, half)], other_ref[...], preferred_element_type=F32)
-    partial = partial.astype(BF16)
+    partial = jnp.dot(joined_ref[...], weight_ref[...], preferred_element_type=F32).astype(BF16)
     keep_ref[...] = partial[:, :share]
     send_ref[0] = partial[:, share : 2 * share]
     pass_ref[...] = partial[:, 2 * share : 3 * share]
     send_ref[1] = partial[:, 3 * share :]
 
 
-def project_moved(own, other, gated):
+def project_moved(weight, gated):
     chips = len(gated)
-    half, columns = own.shape
+    depth, columns = weight.shape
     rows = gated[0].shape[0]
     block = jax.ShapeDtypeStruct((rows, columns // chips), BF16)
     return pl.pallas_call(
         functools.partial(project_moved_kernel, chips),
-        in_specs=[WHOLE] * (2 + chips),
+        in_specs=[WHOLE] * (1 + chips),
         out_specs=[WHOLE] * 3,
         out_shape=[block, block, jax.ShapeDtypeStruct((2, rows, columns // chips), BF16)],
-        scratch_shapes=[pltpu.VMEM((rows, 2 * half), BF16)],
+        scratch_shapes=[pltpu.VMEM((rows, depth), BF16)],
         cost_estimate=CHEAP,
         compiler_params=pltpu.CompilerParams(vmem_limit_bytes=8 * 2**20),
         name="project_moved",
-    )(own, other, *gated)
+    )(weight, *gated)
 
 
 def project_still_kernel(chips, own_ref, other_ref, *refs):
@@ -674,20 +738,19 @@
     rows, width = values_in.shape
     tables = small_tables(parts, rows)
 
-    first = pack_signals(values_in, filter_spectrum.reshape(4, rows, width), chips, tuple(range(chips)))
+    first = pack_signals(values_in, filter_spectrum.reshape(4, rows, width), chips, (0, 16, 16, 0))
     other_weight = swapped(out_weight, "seq", 1)
-    moved = pack_moved(after(gate_values, first[0]), out_weight, other_weight, chips)
+    *moved, mine = pack_moved(after(gate_values, first[0]), out_weight, other_weight, chips)
     first = to_chips(first)
-    own = [after(block, moved[0])[4] for block in first]
-    own = [jnp.stack(own[: chips // 2]), jnp.stack(own[chips // 2 :])]
+    own = pick_values([after(block, moved[0]) for block in first], rows, 4 * rows)
     moved = to_chips(moved)
-    spectrum = forward(own, [swapped(half, "seq", 1) for half in own], tables)
+    spectrum = forward(own, [swapped(part, "seq", 1) for part in own], tables)
     keep, *send = backward(spectrum, first, tables)
-    gated = gate(skip_gain[None, :], keep, [swapped(half, "seq", 1) for half in send], first, moved)
-    own_moved = collect([after(block, gated) for block in moved], out_weight.shape[0] // 2)
-    gathered = to_chips([gated] * chips)
-
-    keep, passed, send = project_moved(own_moved, swapped(own_moved, "seq", 1), gathered)
+    gated, longer = gate(skip_gain[None, :], keep, [swapped(part, "seq", 1) for part in send], first, moved, 16)
+    gathered = to_chips([gated, longer, longer, gated])
+
+    others = [swapped(part, "seq", 1) for part in collect([after(block, gated) for block in moved[1:]], out_weight.shape[0] // 2)]
+    keep, passed, send = project_moved(arrange(mine, moved[1:], others), gathered)
     blocks = to_chips(finish(keep, *over_layers(passed, send), chips))
     keep, passed, send = sort_blocks(to_chips(project_still(out_weight, other_weight, gathered)))
     return join(keep, *over_layers(passed, send), blocks)

time: 81.1 us -> 79.1 us (0.975)
  waiting for transfers between devices: 44.6 us -> 41.1 us
  starting transfers between devices: 26.1 us -> 27.8 us
    ppermute x25 -> x26, waiting for transfers between devices: 44.6 us -> 41.1 us  [swapped(): lax.ppermute(value, axis, [(source, source ^ offset) for source in range(...]
    ppermute x25 -> x26, starting transfers between devices: 26.1 us -> 27.8 us  [swapped(): lax.ppermute(value, axis, [(source, source ^ offset) for source in range(...]
    pallas_call x2 -> x4, Pallas kernels: 1.96 us -> 2.13 us  [the longest x1 1.86 us: pack_signals(): pl.pallas_call(functools.partial(pack_signals_kernel, chips), in_specs=[p...]
  transfers between devices with their start and end apart: 25 -> 26, of which waited for: 12 -> 13; matrix products, arithmetic and copies ran while one was open for 0% -> 0% of each run, Pallas kernels for 9% -> 10%
where the time goes in v11:
time: 79.1 us; the launch traced here: 78.9 us
  waiting for transfers between devices  41.1 us (52%)
  starting transfers between devices  27.8 us (35%)
  Pallas kernels  9.72 us (12%)
    ppermute x26, waiting for transfers between devices, swapped(): lax.ppermute(value, axis, [(source, source ^ offset) for source in range(...  41.1 us
    ppermute x26, starting transfers between devices, swapped(): lax.ppermute(value, axis, [(source, source ^ offset) for source in range(...  27.8 us
    pallas_call x1, Pallas kernels, backward(): pl.pallas_call(functools.partial(backward_kernel, chips), in_specs=[WHOLE...  2.02 us
    pallas_call x1, Pallas kernels, pack_signals(): pl.pallas_call(functools.partial(pack_signals_kernel, chips), in_specs=[p...  1.86 us
  transfers between devices with their start and end apart: 26, of which 13 were waited for; matrix products, arithmetic and copies ran while one was open for 0% of the time, Pallas kernels for 10%

profile of v11, /device:TPU:0, one launch (start us, length us, event | category | flops | bytes accessed | tf_op | source)
XLA Modules:
  0.0 78.9 jit_solution(14067779274823849820)
XLA Ops:
  0.5 1.9 %pack_signals.1 = (bf16[640,256]{1,0:T(8,128)(2,1)S(1)}, bf16[656,256]{1,0:T(8,128)(2,1)S(1)}, bf16[656,256]{1,0:T(8,128)(2,1)S(1)}, bf16[640,256]{1,0:T(8,128)(2,1)S(1)}) custom-call(bf16[128,1024]{1,0:T(8,128)(2,1)} %values_ref.1, f32[4,128,1024]{2,1,0:T(8,128)} %bitcast.13), custom_call_target="tpu_custom_call" | custom-call | tf_op jit(solution)/shard_map/pack_signals/pallas_call | solution.py:248
  2.4 2.6 %collective-permute-start.2 = (bf16[656,256]{1,0:T(8,128)(2,1)S(1)}, bf16[656,256]{1,0:T(8,128)(2,1)S(1)}, u32[]{:S(2)}, u32[]{:S(2)}) collective-permute-start(bf16[656,256]{1,0:T(8,128)(2,1)S(1)} %get-tuple-element.51), channel_id=1, source_target_pairs={{0,16},{4,20},{8,24},{12,28},{16,0},{20,4},{24,8},{28,12},{1,17},{... | collective-permute-start | bytes 1007624 | tf_op jit(solution)/shard_map/ppermute | solution.py:718
  4.9 1.5 %collective-permute-start.1 = (bf16[656,256]{1,0:T(8,128)(2,1)S(1)}, bf16[656,256]{1,0:T(8,128)(2,1)S(1)}, u32[]{:S(2)}, u32[]{:S(2)}) collective-permute-start(bf16[656,256]{1,0:T(8,128)(2,1)S(1)} %get-tuple-element.49), channel_id=1, source_target_pairs={{0,8},{4,12},{8,0},{12,4},{16,24},{20,28},{24,16},{28,20},{1,9},{5... | collective-permute-start | bytes 1007624 | tf_op jit(solution)/shard_map/ppermute | solution.py:718
  6.5 1.3 %pack_moved.1 = (bf16[128,256]{1,0:T(8,128)(2,1)S(1)}, bf16[384,256]{1,0:T(8,128)(2,1)S(1)}, bf16[384,256]{1,0:T(8,128)(2,1)S(1)}, bf16[384,256]{1,0:T(8,128)(2,1)S(1)}, bf16[1024,128]{1,0:T(8,128)(2,1)S(1)}) custom-call(bf16[128,1024]{1,0:T(8,128)(2,1)} %gate_ref, bf16[1024,512]{1,0:T(8,128)(2,1)} %own_ref.3, ...), custom_call_target="tpu_custom_call" | custom-call | tf_op jit(solution)/shard_map/pack_moved/pallas_call | solution.py:298
  7.8 14.0 %collective-permute-done.3.refs_3_ = bf16[640,256]{1,0:T(8,128)(2,1)S(1)} collective-permute-done((bf16[640,256]{1,0:T(8,128)(2,1)S(1)}, bf16[640,256]{1,0:T(8,128)(2,1)S(1)}, u32[]{:S(2)}, u32[]{:S(2)}) %collective-permute-start.3) | collective-permute-done | bytes 327712 | tf_op jit(solution)/shard_map/ppermute | solution.py:718
  22.4 1.6 %collective-permute-start.8 = (bf16[384,256]{1,0:T(8,128)(2,1)S(1)}, bf16[384,256]{1,0:T(8,128)(2,1)S(1)}, u32[]{:S(2)}, u32[]{:S(2)}) collective-permute-start(bf16[384,256]{1,0:T(8,128)(2,1)S(1)} %get-tuple-element.60), channel_id=1, source_target_pairs={{0,8},{4,12},{8,0},{12,4},{16,24},{20,28},{24,16},{28,20},{1,9},{5... | collective-permute-start | bytes 589832 | tf_op jit(solution)/shard_map/ppermute | solution.py:718
  24.0 1.5 %collective-permute-start.9 = (bf16[384,256]{1,0:T(8,128)(2,1)S(1)}, bf16[384,256]{1,0:T(8,128)(2,1)S(1)}, u32[]{:S(2)}, u32[]{:S(2)}) collective-permute-start(bf16[384,256]{1,0:T(8,128)(2,1)S(1)} %get-tuple-element.61), channel_id=1, source_target_pairs={{0,16},{4,20},{8,24},{12,28},{16,0},{20,4},{24,8},{28,12},{1,17},{... | collective-permute-start | bytes 589832 | tf_op jit(solution)/shard_map/ppermute | solution.py:718
  25.9 1.5 %forward.1.spectrum_ref = f32[256,2048]{1,0:T(8,128)S(1)} custom-call(f32[2,128,8]{2,1,0:T(8,128)S(1)} %copy-done.2, f32[2,128,8]{2,1,0:T(8,128)S(1)} %copy-done.1, bf16[256,256]{1,0:T(8,128)(2,1)S(1)} %copy-done.3, bf16[2,128,256]{2,1,0:T(8,128)(2,1)S(1)} %get-tuple-element.55.refs_0_, bf16[2,128,256]{2,1,0:T(8,128)(2,1)S(1)} %get-tuple-element.56.refs_1_, ...), custom_call_target="tpu_custom_call" | custom-call | tf_op jit(solution)/shard_map/forward/pallas_call | solution.py:386
  27.4 2.0 %backward.1 = (f32[4,128,256]{2,1,0:T(8,128)S(1)}, bf16[2,128,256]{2,1,0:T(8,128)(2,1)S(1)}, bf16[2,128,256]{2,1,0:T(8,128)(2,1)S(1)}) custom-call(f32[2,128,8]{2,1,0:T(8,128)S(1)} %copy-done.2, f32[2,128,8]{2,1,0:T(8,128)S(1)} %copy-done.1, bf16[256,256]{1,0:T(8,128)(2,1)S(1)} %copy-done.4, f32[256,2048]{1,0:T(8,128)S(1)} %forward.1.spectrum_ref, ...), custom_call_target="tpu_custom_call" | custom-call | tf_op jit(solution)/shard_map/backward/pallas_call | solution.py:462
  30.1 4.7 %collective-permute-done.9.refs_6_.refs_1_ = bf16[384,256]{1,0:T(8,128)(2,1)S(1)} collective-permute-done((bf16[384,256]{1,0:T(8,128)(2,1)S(1)}, bf16[384,256]{1,0:T(8,128)(2,1)S(1)}, u32[]{:S(2)}, u32[]{:S(2)}) %collective-permute-start.9) | collective-permute-done | bytes 196640 | tf_op jit(solution)/shard_map/ppermute | solution.py:718
  35.0 1.6 %collective-permute-start.12 = (bf16[528,256]{1,0:T(8,128)(2,1)S(1)}, bf16[528,256]{1,0:T(8,128)(2,1)S(1)}, u32[]{:S(2)}, u32[]{:S(2)}) collective-permute-start(bf16[528,256]{1,0:T(8,128)(2,1)S(1)} %get-tuple-element.64), channel_id=1, source_target_pairs={{0,16},{4,20},{8,24},{12,28},{16,0},{20,4},{24,8},{28,12},{1,17},{... | collective-permute-start | bytes 811016 | tf_op jit(solution)/shard_map/ppermute | solution.py:718
  37.2 1.4 %collective-permute-start.13 = (bf16[512,256]{1,0:T(8,128)(2,1)S(1)}, bf16[512,256]{1,0:T(8,128)(2,1)S(1)}, u32[]{:S(2)}, u32[]{:S(2)}) collective-permute-start(bf16[512,256]{1,0:T(8,128)(2,1)S(1)} %get-tuple-element.63.refs_0_), channel_id=1, source_target_pairs={{0,24},{4,28},{8,16},{12,20},{16,8},{20,12},{24,0},{28,4},{1,25},{... | collective-permute-start | bytes 786440 | tf_op jit(solution)/shard_map/ppermute | solution.py:718
  40.7 8.7 %collective-permute-done.13.refs_3_ = bf16[512,256]{1,0:T(8,128)(2,1)S(1)} collective-permute-done((bf16[512,256]{1,0:T(8,128)(2,1)S(1)}, bf16[512,256]{1,0:T(8,128)(2,1)S(1)}, u32[]{:S(2)}, u32[]{:S(2)}) %collective-permute-start.13) | collective-permute-done | bytes 262176 | tf_op jit(solution)/shard_map/ppermute | solution.py:718
  50.2 1.6 %collective-permute-start.21 = (bf16[2,512,128]{2,1,0:T(8,128)(2,1)S(1)}, bf16[2,512,128]{2,1,0:T(8,128)(2,1)S(1)}, u32[]{:S(2)}, u32[]{:S(2)}) collective-permute-start(bf16[2,512,128]{2,1,0:T(8,128)(2,1)S(1)} %get-tuple-element.79), channel_id=1, source_target_pairs={{0,1},{1,0},{2,3},{3,2},{4,5},{5,4},{6,7},{7,6},{8,9},{9,8},{10,11... | collective-permute-start | bytes 786440 | tf_op jit(solution)/shard_map/ppermute | solution.py:718
  52.7 1.5 %collective-permute-start.14 = (bf16[128,512]{1,0:T(8,128)(2,1)S(1)}, bf16[128,512]{1,0:T(8,128)(2,1)S(1)}, u32[]{:S(2)}, u32[]{:S(2)}) collective-permute-start(bf16[128,512]{1,0:T(8,128)(2,1)S(1)} %get-tuple-element.66), channel_id=1, source_target_pairs={{0,8},{4,12},{8,0},{12,4},{16,24},{20,28},{24,16},{28,20},{1,9},{5... | collective-permute-start | bytes 393224 | tf_op jit(solution)/shard_map/ppermute | solution.py:718
  54.8 1.5 %collective-permute-start.16 = (bf16[128,512]{1,0:T(8,128)(2,1)S(1)}, bf16[128,512]{1,0:T(8,128)(2,1)S(1)}, u32[]{:S(2)}, u32[]{:S(2)}) collective-permute-start(bf16[128,512]{1,0:T(8,128)(2,1)S(1)} %get-tuple-element.68), channel_id=1, source_target_pairs={{0,24},{4,28},{8,16},{12,20},{16,8},{20,12},{24,0},{28,4},{1,25},{... | collective-permute-start | bytes 393224 | tf_op jit(solution)/shard_map/ppermute | solution.py:718
  56.2 2.0 %collective-permute-done.14.refs_1_ = bf16[128,512]{1,0:T(8,128)(2,1)S(1)} collective-permute-done((bf16[128,512]{1,0:T(8,128)(2,1)S(1)}, bf16[128,512]{1,0:T(8,128)(2,1)S(1)}, u32[]{:S(2)}, u32[]{:S(2)}) %collective-permute-start.14) | collective-permute-done | bytes 131104 | tf_op jit(solution)/shard_map/ppermute | solution.py:718
  59.2 1.4 %collective-permute-done.16.refs_3_ = bf16[128,512]{1,0:T(8,128)(2,1)S(1)} collective-permute-done((bf16[128,512]{1,0:T(8,128)(2,1)S(1)}, bf16[128,512]{1,0:T(8,128)(2,1)S(1)}, u32[]{:S(2)}, u32[]{:S(2)}) %collective-permute-start.16) | collective-permute-done | bytes 131104 | tf_op jit(solution)/shard_map/ppermute | solution.py:718
  61.3 2.7 %collective-permute-start.22 = (bf16[512,128]{1,0:T(8,128)(2,1)S(1)}, bf16[512,128]{1,0:T(8,128)(2,1)S(1)}, u32[]{:S(2)}, u32[]{:S(2)}) collective-permute-start(bf16[512,128]{1,0:T(8,128)(2,1)S(1)} %fusion), channel_id=1, source_target_pairs={{0,2},{1,3},{2,0},{3,1},{4,6},{5,7},{6,4},{7,5},{8,10},{9,11},{10,... | collective-permute-start | bytes 393224 | tf_op jit(solution)/shard_map/ppermute | solution.py:718
  63.9 4.8 %collective-permute-done.17.first_ref = bf16[2,128,512]{2,1,0:T(8,128)(2,1)S(1)} collective-permute-done((bf16[2,128,512]{2,1,0:T(8,128)(2,1)S(1)}, bf16[2,128,512]{2,1,0:T(8,128)(2,1)S(1)}, u32[]{:S(2)}, u32[]{:S(2)}) %collective-permute-start.17) | collective-permute-done | bytes 262176 | tf_op jit(solution)/shard_map/ppermute | solution.py:718
  68.7 2.5 %collective-permute-start.18 = (bf16[128,512]{1,0:T(8,128)(2,1)S(1)}, bf16[128,512]{1,0:T(8,128)(2,1)S(1)}, u32[]{:S(2)}, u32[]{:S(2)}) collective-permute-start(bf16[128,512]{1,0:T(8,128)(2,1)S(1)} %fusion.1), channel_id=1, source_target_pairs={{0,2},{1,3},{2,0},{3,1},{4,6},{5,7},{6,4},{7,5},{8,10},{9,11},{10,... | collective-permute-start | bytes 393224 | tf_op jit(solution)/shard_map/ppermute | solution.py:718
  71.9 1.4 %collective-permute-start.24 = (bf16[128,128]{1,0:T(8,128)(2,1)S(1)}, bf16[128,128]{1,0:T(8,128)(2,1)S(1)}, u32[]{:S(2)}, u32[]{:S(2)}) collective-permute-start(bf16[128,128]{1,0:T(8,128)(2,1)S(1)} %get-tuple-element.83), channel_id=1, source_target_pairs={{0,16},{4,20},{8,24},{12,28},{16,0},{20,4},{24,8},{28,12},{1,17},{... | collective-permute-start | bytes 98312 | tf_op jit(solution)/shard_map/ppermute | solution.py:718
  73.3 1.5 %collective-permute-start.25 = (bf16[128,128]{1,0:T(8,128)(2,1)S(1)}, bf16[128,128]{1,0:T(8,128)(2,1)S(1)}, u32[]{:S(2)}, u32[]{:S(2)}) collective-permute-start(bf16[128,128]{1,0:T(8,128)(2,1)S(1)} %get-tuple-element.84), channel_id=1, source_target_pairs={{0,24},{4,28},{8,16},{12,20},{16,8},{20,12},{24,0},{28,4},{1,25},{... | collective-permute-start | bytes 98312 | tf_op jit(solution)/shard_map/ppermute | solution.py:718
  75.8 2.3 %collective-permute-done.25.refs_3_ = bf16[128,128]{1,0:T(8,128)(2,1)S(1)} collective-permute-done((bf16[128,128]{1,0:T(8,128)(2,1)S(1)}, bf16[128,128]{1,0:T(8,128)(2,1)S(1)}, u32[]{:S(2)}, u32[]{:S(2)}) %collective-permute-start.25) | collective-permute-done | bytes 32800 | tf_op jit(solution)/shard_map/ppermute | solution.py:718
  (55 shorter events, 11.2 us)
Async XLA Ops:
  0.0 6.5 %collective-permute-start = (bf16[1024,512]{1,0:T(8,128)(2,1)}, bf16[1024,512]{1,0:T(8,128)(2,1)S(1)}, u32[]{:S(2)}, u32[]{:S(2)}) collective-permute-start(bf16[1024,512]{1,0:T(8,128)(2,1)} %own_ref.3), channel_id=1, source_target_pairs={{0,4},{4,0},{8,12},{12,8},{16,20},{20,16},{24,28},{28,24},{1,5},{5... | collective-permute-start | bytes 3145736 | tf_op jit(solution)/shard_map/ppermute | solution.py:718
  2.4 19.4 %collective-permute-start.2 = (bf16[656,256]{1,0:T(8,128)(2,1)S(1)}, bf16[656,256]{1,0:T(8,128)(2,1)S(1)}, u32[]{:S(2)}, u32[]{:S(2)}) collective-permute-start(bf16[656,256]{1,0:T(8,128)(2,1)S(1)} %get-tuple-element.51), channel_id=1, source_target_pairs={{0,16},{4,20},{8,24},{12,28},{16,0},{20,4},{24,8},{28,12},{1,17},{... | collective-permute-start | bytes 1007624 | tf_op jit(solution)/shard_map/ppermute | solution.py:718
  4.9 16.8 %collective-permute-start.1 = (bf16[656,256]{1,0:T(8,128)(2,1)S(1)}, bf16[656,256]{1,0:T(8,128)(2,1)S(1)}, u32[]{:S(2)}, u32[]{:S(2)}) collective-permute-start(bf16[656,256]{1,0:T(8,128)(2,1)S(1)} %get-tuple-element.49), channel_id=1, source_target_pairs={{0,8},{4,12},{8,0},{12,4},{16,24},{20,28},{24,16},{28,20},{1,9},{5... | collective-permute-start | bytes 1007624 | tf_op jit(solution)/shard_map/ppermute | solution.py:718
  6.4 15.3 %collective-permute-start.3 = (bf16[640,256]{1,0:T(8,128)(2,1)S(1)}, bf16[640,256]{1,0:T(8,128)(2,1)S(1)}, u32[]{:S(2)}, u32[]{:S(2)}) collective-permute-start(bf16[640,256]{1,0:T(8,128)(2,1)S(1)} %get-tuple-element.53), channel_id=1, source_target_pairs={{0,24},{4,28},{8,16},{12,20},{16,8},{20,12},{24,0},{28,4},{1,25},{... | collective-permute-start | bytes 983048 | tf_op jit(solution)/shard_map/ppermute | solution.py:718
  21.8 4.1 %collective-permute-start.4 = (bf16[2,128,256]{2,1,0:T(8,128)(2,1)S(1)}, bf16[2,128,256]{2,1,0:T(8,128)(2,1)S(1)}, u32[]{:S(2)}, u32[]{:S(2)}) collective-permute-start(bf16[2,128,256]{2,1,0:T(8,128)(2,1)S(1)} %get-tuple-element.55.refs_0_), channel_id=1, source_target_pairs={{0,4},{4,0},{8,12},{12,8},{16,20},{20,16},{24,28},{28,24},{1,5},{5... | collective-permute-start | bytes 393224 | tf_op jit(solution)/shard_map/ppermute | solution.py:718
  21.9 4.0 %collective-permute-start.5 = (bf16[2,128,256]{2,1,0:T(8,128)(2,1)S(1)}, bf16[2,128,256]{2,1,0:T(8,128)(2,1)S(1)}, u32[]{:S(2)}, u32[]{:S(2)}) collective-permute-start(bf16[2,128,256]{2,1,0:T(8,128)(2,1)S(1)} %get-tuple-element.56.refs_1_), channel_id=1, source_target_pairs={{0,4},{4,0},{8,12},{12,8},{16,20},{20,16},{24,28},{28,24},{1,5},{5... | collective-permute-start | bytes 393224 | tf_op jit(solution)/shard_map/ppermute | solution.py:718
  22.4 7.8 %collective-permute-start.8 = (bf16[384,256]{1,0:T(8,128)(2,1)S(1)}, bf16[384,256]{1,0:T(8,128)(2,1)S(1)}, u32[]{:S(2)}, u32[]{:S(2)}) collective-permute-start(bf16[384,256]{1,0:T(8,128)(2,1)S(1)} %get-tuple-element.60), channel_id=1, source_target_pairs={{0,8},{4,12},{8,0},{12,4},{16,24},{20,28},{24,16},{28,20},{1,9},{5... | collective-permute-start | bytes 589832 | tf_op jit(solution)/shard_map/ppermute | solution.py:718
  24.0 10.8 %collective-permute-start.9 = (bf16[384,256]{1,0:T(8,128)(2,1)S(1)}, bf16[384,256]{1,0:T(8,128)(2,1)S(1)}, u32[]{:S(2)}, u32[]{:S(2)}) collective-permute-start(bf16[384,256]{1,0:T(8,128)(2,1)S(1)} %get-tuple-element.61), channel_id=1, source_target_pairs={{0,16},{4,20},{8,24},{12,28},{16,0},{20,4},{24,8},{28,12},{1,17},{... | collective-permute-start | bytes 589832 | tf_op jit(solution)/shard_map/ppermute | solution.py:718
  25.5 9.3 %collective-permute-start.10 = (bf16[384,256]{1,0:T(8,128)(2,1)S(1)}, bf16[384,256]{1,0:T(8,128)(2,1)S(1)}, u32[]{:S(2)}, u32[]{:S(2)}) collective-permute-start(bf16[384,256]{1,0:T(8,128)(2,1)S(1)} %get-tuple-element.62), channel_id=1, source_target_pairs={{0,24},{4,28},{8,16},{12,20},{16,8},{20,12},{24,0},{28,4},{1,25},{... | collective-permute-start | bytes 589832 | tf_op jit(solution)/shard_map/ppermute | solution.py:718
  29.4 5.4 %collective-permute-start.6 = (bf16[2,128,256]{2,1,0:T(8,128)(2,1)S(1)}, bf16[2,128,256]{2,1,0:T(8,128)(2,1)S(1)}, u32[]{:S(2)}, u32[]{:S(2)}) collective-permute-start(bf16[2,128,256]{2,1,0:T(8,128)(2,1)S(1)} %get-tuple-element.58), channel_id=1, source_target_pairs={{0,4},{4,0},{8,12},{12,8},{16,20},{20,16},{24,28},{28,24},{1,5},{5... | collective-permute-start | bytes 393224 | tf_op jit(solution)/shard_map/ppermute | solution.py:718
  29.5 5.3 %collective-permute-start.7 = (bf16[2,128,256]{2,1,0:T(8,128)(2,1)S(1)}, bf16[2,128,256]{2,1,0:T(8,128)(2,1)S(1)}, u32[]{:S(2)}, u32[]{:S(2)}) collective-permute-start(bf16[2,128,256]{2,1,0:T(8,128)(2,1)S(1)} %get-tuple-element.59), channel_id=1, source_target_pairs={{0,4},{4,0},{8,12},{12,8},{16,20},{20,16},{24,28},{28,24},{1,5},{5... | collective-permute-start | bytes 393224 | tf_op jit(solution)/shard_map/ppermute | solution.py:718
  35.0 14.3 %collective-permute-start.12 = (bf16[528,256]{1,0:T(8,128)(2,1)S(1)}, bf16[528,256]{1,0:T(8,128)(2,1)S(1)}, u32[]{:S(2)}, u32[]{:S(2)}) collective-permute-start(bf16[528,256]{1,0:T(8,128)(2,1)S(1)} %get-tuple-element.64), channel_id=1, source_target_pairs={{0,16},{4,20},{8,24},{12,28},{16,0},{20,4},{24,8},{28,12},{1,17},{... | collective-permute-start | bytes 811016 | tf_op jit(solution)/shard_map/ppermute | solution.py:718
  36.6 12.7 %collective-permute-start.11 = (bf16[528,256]{1,0:T(8,128)(2,1)S(1)}, bf16[528,256]{1,0:T(8,128)(2,1)S(1)}, u32[]{:S(2)}, u32[]{:S(2)}) collective-permute-start(bf16[528,256]{1,0:T(8,128)(2,1)S(1)} %get-tuple-element.64), channel_id=1, source_target_pairs={{0,8},{4,12},{8,0},{12,4},{16,24},{20,28},{24,16},{28,20},{1,9},{5... | collective-permute-start | bytes 811016 | tf_op jit(solution)/shard_map/ppermute | solution.py:718
  37.2 12.2 %collective-permute-start.13 = (bf16[512,256]{1,0:T(8,128)(2,1)S(1)}, bf16[512,256]{1,0:T(8,128)(2,1)S(1)}, u32[]{:S(2)}, u32[]{:S(2)}) collective-permute-start(bf16[512,256]{1,0:T(8,128)(2,1)S(1)} %get-tuple-element.63.refs_0_), channel_id=1, source_target_pairs={{0,24},{4,28},{8,16},{12,20},{16,8},{20,12},{24,0},{28,4},{1,25},{... | collective-permute-start | bytes 786440 | tf_op jit(solution)/shard_map/ppermute | solution.py:718
  50.2 11.1 %collective-permute-start.21 = (bf16[2,512,128]{2,1,0:T(8,128)(2,1)S(1)}, bf16[2,512,128]{2,1,0:T(8,128)(2,1)S(1)}, u32[]{:S(2)}, u32[]{:S(2)}) collective-permute-start(bf16[2,512,128]{2,1,0:T(8,128)(2,1)S(1)} %get-tuple-element.79), channel_id=1, source_target_pairs={{0,1},{1,0},{2,3},{3,2},{4,5},{5,4},{6,7},{7,6},{8,9},{9,8},{10,11... | collective-permute-start | bytes 786440 | tf_op jit(solution)/shard_map/ppermute | solution.py:718
  52.7 5.6 %collective-permute-start.14 = (bf16[128,512]{1,0:T(8,128)(2,1)S(1)}, bf16[128,512]{1,0:T(8,128)(2,1)S(1)}, u32[]{:S(2)}, u32[]{:S(2)}) collective-permute-start(bf16[128,512]{1,0:T(8,128)(2,1)S(1)} %get-tuple-element.66), channel_id=1, source_target_pairs={{0,8},{4,12},{8,0},{12,4},{16,24},{20,28},{24,16},{28,20},{1,9},{5... | collective-permute-start | bytes 393224 | tf_op jit(solution)/shard_map/ppermute | solution.py:718
  54.2 5.0 %collective-permute-start.15 = (bf16[128,512]{1,0:T(8,128)(2,1)S(1)}, bf16[128,512]{1,0:T(8,128)(2,1)S(1)}, u32[]{:S(2)}, u32[]{:S(2)}) collective-permute-start(bf16[128,512]{1,0:T(8,128)(2,1)S(1)} %get-tuple-element.67), channel_id=1, source_target_pairs={{0,16},{4,20},{8,24},{12,28},{16,0},{20,4},{24,8},{28,12},{1,17},{... | collective-permute-start | bytes 393224 | tf_op jit(solution)/shard_map/ppermute | solution.py:718
  54.8 5.9 %collective-permute-start.16 = (bf16[128,512]{1,0:T(8,128)(2,1)S(1)}, bf16[128,512]{1,0:T(8,128)(2,1)S(1)}, u32[]{:S(2)}, u32[]{:S(2)}) collective-permute-start(bf16[128,512]{1,0:T(8,128)(2,1)S(1)} %get-tuple-element.68), channel_id=1, source_target_pairs={{0,24},{4,28},{8,16},{12,20},{16,8},{20,12},{24,0},{28,4},{1,25},{... | collective-permute-start | bytes 393224 | tf_op jit(solution)/shard_map/ppermute | solution.py:718
  60.7 8.0 %collective-permute-start.17 = (bf16[2,128,512]{2,1,0:T(8,128)(2,1)S(1)}, bf16[2,128,512]{2,1,0:T(8,128)(2,1)S(1)}, u32[]{:S(2)}, u32[]{:S(2)}) collective-permute-start(bf16[2,128,512]{2,1,0:T(8,128)(2,1)S(1)} %get-tuple-element.70), channel_id=1, source_target_pairs={{0,1},{1,0},{2,3},{3,2},{4,5},{5,4},{6,7},{7,6},{8,9},{9,8},{10,11... | collective-permute-start | bytes 786440 | tf_op jit(solution)/shard_map/ppermute | solution.py:718
  61.3 10.0 %collective-permute-start.22 = (bf16[512,128]{1,0:T(8,128)(2,1)S(1)}, bf16[512,128]{1,0:T(8,128)(2,1)S(1)}, u32[]{:S(2)}, u32[]{:S(2)}) collective-permute-start(bf16[512,128]{1,0:T(8,128)(2,1)S(1)} %fusion), channel_id=1, source_target_pairs={{0,2},{1,3},{2,0},{3,1},{4,6},{5,7},{6,4},{7,5},{8,10},{9,11},{10,... | collective-permute-start | bytes 393224 | tf_op jit(solution)/shard_map/ppermute | solution.py:718
  68.7 9.4 %collective-permute-start.18 = (bf16[128,512]{1,0:T(8,128)(2,1)S(1)}, bf16[128,512]{1,0:T(8,128)(2,1)S(1)}, u32[]{:S(2)}, u32[]{:S(2)}) collective-permute-start(bf16[128,512]{1,0:T(8,128)(2,1)S(1)} %fusion.1), channel_id=1, source_target_pairs={{0,2},{1,3},{2,0},{3,1},{4,6},{5,7},{6,4},{7,5},{8,10},{9,11},{10,... | collective-permute-start | bytes 393224 | tf_op jit(solution)/shard_map/ppermute | solution.py:718
  71.3 4.0 %collective-permute-start.23 = (bf16[128,128]{1,0:T(8,128)(2,1)S(1)}, bf16[128,128]{1,0:T(8,128)(2,1)S(1)}, u32[]{:S(2)}, u32[]{:S(2)}) collective-permute-start(bf16[128,128]{1,0:T(8,128)(2,1)S(1)} %get-tuple-element.82), channel_id=1, source_target_pairs={{0,8},{4,12},{8,0},{12,4},{16,24},{20,28},{24,16},{28,20},{1,9},{5... | collective-permute-start | bytes 98312 | tf_op jit(solution)/shard_map/ppermute | solution.py:718
  71.9 3.9 %collective-permute-start.24 = (bf16[128,128]{1,0:T(8,128)(2,1)S(1)}, bf16[128,128]{1,0:T(8,128)(2,1)S(1)}, u32[]{:S(2)}, u32[]{:S(2)}) collective-permute-start(bf16[128,128]{1,0:T(8,128)(2,1)S(1)} %get-tuple-element.83), channel_id=1, source_target_pairs={{0,16},{4,20},{8,24},{12,28},{16,0},{20,4},{24,8},{28,12},{1,17},{... | collective-permute-start | bytes 98312 | tf_op jit(solution)/shard_map/ppermute | solution.py:718
  73.3 4.8 %collective-permute-start.25 = (bf16[128,128]{1,0:T(8,128)(2,1)S(1)}, bf16[128,128]{1,0:T(8,128)(2,1)S(1)}, u32[]{:S(2)}, u32[]{:S(2)}) collective-permute-start(bf16[128,128]{1,0:T(8,128)(2,1)S(1)} %get-tuple-element.84), channel_id=1, source_target_pairs={{0,24},{4,28},{8,16},{12,20},{16,8},{20,12},{24,0},{28,4},{1,25},{... | collective-permute-start | bytes 98312 | tf_op jit(solution)/shard_map/ppermute | solution.py:718
  (8 other events, 112.3 us)

commit v12 on v11

--- a/solution.py
+++ b/solution.py
@@ -213,46 +213,46 @@
     return pl.ds(pl.multiple_of(index * size, size), size)
 
 
-def pack_signals_kernel(chips, values_ref, filter_ref, *refs):
-    out_refs, (plane_ref, arrived) = refs[:chips], refs[chips:]
+def pack_signals_kernel(offsets, values_ref, filter_ref, *refs):
+    out_refs, (plane_ref, arrived) = refs[: len(offsets)], refs[len(offsets) :]
     chip, _ = own_place()
     planes, rows, _ = filter_ref.shape
     lanes = out_refs[0].shape[1]
     copies, work = [], []
-    for offset in range(chips):
+    for place, offset in enumerate(offsets):
         here = block_at(chip ^ offset, lanes)
         for plane in range(planes):
             copies.append(
-                pltpu.make_async_copy(filter_ref.at[plane, :, here], plane_ref.at[offset, plane], arrived.at[offset, plane])
+                pltpu.make_async_copy(filter_ref.at[plane, :, here], plane_ref.at[place, plane], arrived.at[place, plane])
             )
-            work.append((offset, plane))
-        values = out_refs[offset].at[pl.ds(planes * rows, rows)]
-        copies.append(pltpu.make_async_copy(values_ref.at[:, here], values, arrived.at[offset, planes]))
+            work.append((place, plane))
+        values = out_refs[place].at[pl.ds(planes * rows, rows)]
+        copies.append(pltpu.make_async_copy(values_ref.at[:, here], values, arrived.at[place, planes]))
         work.append(None)
     for copy in copies:
         copy.start()
     for copy, task in zip(copies, work):
         copy.wait()
         if task:
-            offset, plane = task
-            out_refs[offset][pl.ds(plane * rows, rows), :] = plane_ref[offset, plane].astype(BF16)
+            place, plane = task
+            out_refs[place][pl.ds(plane * rows, rows), :] = plane_ref[place, plane].astype(BF16)
     used = (planes + 1) * rows
     for out_ref in out_refs:
         if out_ref.shape[0] > used:
             out_ref[pl.ds(used, out_ref.shape[0] - used), :] = out_ref[pl.ds(0, out_ref.shape[0] - used), :]
 
 
-def pack_signals(values_in, filters, chips, spare):
+def pack_signals(values_in, filters, chips, offsets, spare):
     planes, rows, width = filters.shape
     lanes = width // chips
     return pl.pallas_call(
-        functools.partial(pack_signals_kernel, chips),
+        functools.partial(pack_signals_kernel, offsets),
         in_specs=[pl.BlockSpec(memory_space=pltpu.HBM)] * 2,
-        out_specs=[WHOLE] * chips,
-        out_shape=[jax.ShapeDtypeStruct(((planes + 1) * rows + more, lanes), BF16) for more in spare],
+        out_specs=[WHOLE] * len(offsets),
+        out_shape=[jax.ShapeDtypeStruct(((planes + 1) * rows + spare, lanes), BF16)] * len(offsets),
         scratch_shapes=[
-            pltpu.VMEM((chips, planes, rows, lanes), F32),
-            pltpu.SemaphoreType.DMA((chips, planes + 1)),
+            pltpu.VMEM((len(offsets), planes, rows, lanes), F32),
+            pltpu.SemaphoreType.DMA((len(offsets), planes + 1)),
         ],
         cost_estimate=CHEAP,
         compiler_params=pltpu.CompilerParams(vmem_limit_bytes=8 * 2**20),
@@ -576,14 +576,12 @@
 
 
 def project_moved_kernel(chips, weight_ref, *refs):
-    gated_refs, (keep_ref, pass_ref, send_ref, joined_ref) = refs[:chips], refs[chips:]
-    share = keep_ref.shape[1]
+    gated_refs, (*out_refs, joined_ref) = refs[:chips], refs[chips:]
+    share = out_refs[0].shape[1]
     join_channels(chips, gated_refs, joined_ref)
     partial = jnp.dot(joined_ref[...], weight_ref[...], preferred_element_type=F32).astype(BF16)
-    keep_ref[...] = partial[:, :share]
-    send_ref[0] = partial[:, share : 2 * share]
-    pass_ref[...] = partial[:, 2 * share : 3 * share]
-    send_ref[1] = partial[:, 3 * share :]
+    for target, out_ref in enumerate(out_refs):
+        out_ref[...] = partial[:, target * share : (target + 1) * share]
 
 
 def project_moved(weight, gated):
@@ -594,8 +592,8 @@
     return pl.pallas_call(
         functools.partial(project_moved_kernel, chips),
         in_specs=[WHOLE] * (1 + chips),
-        out_specs=[WHOLE] * 3,
-        out_shape=[block, block, jax.ShapeDtypeStruct((2, rows, columns // chips), BF16)],
+        out_specs=[WHOLE] * chips,
+        out_shape=[block] * chips,
         scratch_shapes=[pltpu.VMEM((rows, depth), BF16)],
         cost_estimate=CHEAP,
         compiler_params=pltpu.CompilerParams(vmem_limit_bytes=8 * 2**20),
@@ -612,7 +610,11 @@
     def project_with(weight_ref):
         for offset in range(chips):
             gated = joined_ref[block_at(chip ^ offset, rows), :]
-            out_refs[offset][...] = jnp.dot(gated, weight_ref[...], preferred_element_type=F32).astype(BF16)
+            partial = jnp.dot(gated, weight_ref[...], preferred_element_type=F32).astype(BF16)
+            out_refs[offset][pl.ds(0, rows), :] = partial
+            more = out_refs[offset].shape[0] - rows
+            if more:
+                out_refs[offset][pl.ds(rows, more), :] = partial[:more]
 
     @pl.when(core == 0)
     def _():
@@ -623,7 +625,7 @@
         project_with(own_ref)
 
 
-def project_still(own, other, gated):
+def project_still(own, other, gated, spare):
     chips = len(gated)
     depth, held = own.shape
     rows = gated[0].shape[0] // chips
@@ -631,7 +633,7 @@
         functools.partial(project_still_kernel, chips),
         in_specs=[WHOLE] * (2 + chips),
         out_specs=[WHOLE] * chips,
-        out_shape=[jax.ShapeDtypeStruct((rows, held), BF16)] * chips,
+        out_shape=[jax.ShapeDtypeStruct((rows + (spare if offset else 0), held), BF16) for offset in range(chips)],
         scratch_shapes=[pltpu.VMEM((rows * chips, depth), BF16)],
         cost_estimate=CHEAP,
         compiler_params=pltpu.CompilerParams(vmem_limit_bytes=12 * 2**20),
@@ -644,16 +646,16 @@
     chip, _ = own_place()
     layer = lax.axis_index("chan")
     for offset in range(chips):
-        sorted_ref[chip ^ layer ^ offset] = in_refs[offset][...]
+        sorted_ref[chip ^ layer ^ offset] = in_refs[offset][pl.ds(0, sorted_ref.shape[1]), :]
     keep_ref[...] = sorted_ref[0]
     send_ref[0] = sorted_ref[1]
     pass_ref[...] = sorted_ref[2]
     send_ref[1] = sorted_ref[3]
 
 
-def sort_blocks(blocks):
+def sort_blocks(blocks, rows):
     chips = len(blocks)
-    block = jax.ShapeDtypeStruct(blocks[0].shape, BF16)
+    block = jax.ShapeDtypeStruct((rows, blocks[0].shape[1]), BF16)
     return pl.pallas_call(
         functools.partial(sort_kernel, chips),
         in_specs=[WHOLE] * chips,
@@ -671,7 +673,7 @@
     rows = out_refs[0].shape[0]
     for offset in range(chips):
         here = block_at(chip ^ offset, rows)
-        total = keep_ref[here, :].astype(F32) + first_ref[0, here, :].astype(F32) + second_ref[here, :].astype(F32)
+        total = keep_ref[here, :].astype(F32) + first_ref[here, :].astype(F32) + second_ref[here, :].astype(F32)
         out_refs[offset][...] = total.astype(BF16)
 
 
@@ -726,10 +728,8 @@
     return lax.optimization_barrier((value, *others))[0]
 
 
-def over_layers(passed, send):
-    first = swapped(send, "chan", 1)
-    passed = (passed.astype(F32) + first[1].astype(F32)).astype(BF16)
-    return first, swapped(passed, "chan", 2)
+def added(left, right):
+    return (left.astype(F32) + right.astype(F32)).astype(BF16)
 
 
 def shards_direct(values_in, gate_values, filter_spectrum, skip_gain, out_weight):
@@ -738,7 +738,10 @@
     rows, width = values_in.shape
     tables = small_tables(parts, rows)
 
-    first = pack_signals(values_in, filter_spectrum.reshape(4, rows, width), chips, (0, 16, 16, 0))
+    flat_filters = filter_spectrum.reshape(4, rows, width)
+    near = pack_signals(values_in, flat_filters, chips, (1, 2), 16)
+    own, far = pack_signals(after(values_in, near[0]), flat_filters, chips, (0, 3), 0)
+    first = [own, *near, far]
     other_weight = swapped(out_weight, "seq", 1)
     *moved, mine = pack_moved(after(gate_values, first[0]), out_weight, other_weight, chips)
     first = to_chips(first)
@@ -749,11 +752,15 @@
     gated, longer = gate(skip_gain[None, :], keep, [swapped(part, "seq", 1) for part in send], first, moved, 16)
     gathered = to_chips([gated, longer, longer, gated])
 
+    still = project_still(out_weight, other_weight, gathered, 16)
     others = [swapped(part, "seq", 1) for part in collect([after(block, gated) for block in moved[1:]], out_weight.shape[0] // 2)]
-    keep, passed, send = project_moved(arrange(mine, moved[1:], others), gathered)
-    blocks = to_chips(finish(keep, *over_layers(passed, send), chips))
-    keep, passed, send = sort_blocks(to_chips(project_still(out_weight, other_weight, gathered)))
-    return join(keep, *over_layers(passed, send), blocks)
+    moved_weight = arrange(mine, moved[1:], others)
+    keep, near, passed, far = project_moved(moved_weight, [after(gated, still[0]), *gathered[1:]])
+    first, other = swapped(near, "chan", 1), swapped(far, "chan", 1)
+    blocks = to_chips(finish(keep, first, swapped(added(after(passed, first), other), "chan", 2), chips))
+    keep, passed, send = sort_blocks(to_chips(still), rows)
+    first = swapped(send, "chan", 1)
+    return join(keep, first, swapped(added(passed, first[1]), "chan", 2), blocks)
 
 
 def shards(values_in, gate_values, filter_spectrum, skip_gain, out_weight):

time: 79.1 us -> 83.2 us (1.052)
  waiting for transfers between devices: 41.1 us -> 42.9 us
  starting transfers between devices: 27.8 us -> 29 us
  Pallas kernels: 9.72 us -> 10.7 us
    ppermute x26 -> x27, waiting for transfers between devices: 41.1 us -> 42.9 us  [swapped(): lax.ppermute(value, axis, [(source, source ^ offset) for source in range(...]
    ppermute x26 -> x27, starting transfers between devices: 27.8 us -> 29 us  [swapped(): lax.ppermute(value, axis, [(source, source ^ offset) for source in range(...]
    pallas_call x1 -> x2, Pallas kernels: 1.86 us -> 2.81 us  [pack_signals(): pl.pallas_call(functools.partial(pack_signals_kernel, offsets), in_specs=...]
  transfers between devices with their start and end apart: 26 -> 27, of which waited for: 13 -> 12; matrix products, arithmetic and copies ran while one was open for 0% -> 0% of each run, Pallas kernels for 10% -> 12%
where the time goes in v12:
time: 83.2 us; the launch traced here: 83 us
  waiting for transfers between devices  42.9 us (52%)
  starting transfers between devices  29 us (35%)
  Pallas kernels  10.7 us (13%)
    ppermute x27, waiting for transfers between devices, swapped(): lax.ppermute(value, axis, [(source, source ^ offset) for source in range(...  42.9 us
    ppermute x27, starting transfers between devices, swapped(): lax.ppermute(value, axis, [(source, source ^ offset) for source in range(...  29 us
    pallas_call x2, Pallas kernels, pack_signals(): pl.pallas_call(functools.partial(pack_signals_kernel, offsets), in_specs=...  2.81 us
    pallas_call x1, Pallas kernels, backward(): pl.pallas_call(functools.partial(backward_kernel, chips), in_specs=[WHOLE...  2.02 us
  transfers between devices with their start and end apart: 27, of which 12 were waited for; matrix products, arithmetic and copies ran while one was open for 0% of the time, Pallas kernels for 12%

profile of v12, /device:TPU:0, one launch (start us, length us, event | category | flops | bytes accessed | tf_op | source)
XLA Modules:
  0.0 83.0 jit_solution(13597651926697937469)
XLA Ops:
  0.5 1.4 %pack_signals.2 = (bf16[656,256]{1,0:T(8,128)(2,1)S(1)}, bf16[656,256]{1,0:T(8,128)(2,1)S(1)}) custom-call(bf16[128,1024]{1,0:T(8,128)(2,1)} %values_ref.2, f32[4,128,1024]{2,1,0:T(8,128)} %bitcast.8), custom_call_target="tpu_custom_call" | custom-call | tf_op jit(solution)/shard_map/pack_signals/pallas_call | solution.py:248
  1.9 2.6 %collective-permute-start.2 = (bf16[656,256]{1,0:T(8,128)(2,1)S(1)}, bf16[656,256]{1,0:T(8,128)(2,1)S(1)}, u32[]{:S(2)}, u32[]{:S(2)}) collective-permute-start(bf16[656,256]{1,0:T(8,128)(2,1)S(1)} %get-tuple-element.56), channel_id=1, source_target_pairs={{0,16},{4,20},{8,24},{12,28},{16,0},{20,4},{24,8},{28,12},{1,17},{... | collective-permute-start | bytes 1007624 | tf_op jit(solution)/shard_map/ppermute | solution.py:720
  4.4 1.5 %collective-permute-start.1 = (bf16[656,256]{1,0:T(8,128)(2,1)S(1)}, bf16[656,256]{1,0:T(8,128)(2,1)S(1)}, u32[]{:S(2)}, u32[]{:S(2)}) collective-permute-start(bf16[656,256]{1,0:T(8,128)(2,1)S(1)} %get-tuple-element.49), channel_id=1, source_target_pairs={{0,8},{4,12},{8,0},{12,4},{16,24},{20,28},{24,16},{28,20},{1,9},{5... | collective-permute-start | bytes 1007624 | tf_op jit(solution)/shard_map/ppermute | solution.py:720
  8.8 12.5 %collective-permute-done.3.refs_3_ = bf16[640,256]{1,0:T(8,128)(2,1)S(1)} collective-permute-done((bf16[640,256]{1,0:T(8,128)(2,1)S(1)}, bf16[640,256]{1,0:T(8,128)(2,1)S(1)}, u32[]{:S(2)}, u32[]{:S(2)}) %collective-permute-start.3) | collective-permute-done | bytes 327712 | tf_op jit(solution)/shard_map/ppermute | solution.py:720
  21.9 1.6 %collective-permute-start.8 = (bf16[384,256]{1,0:T(8,128)(2,1)S(1)}, bf16[384,256]{1,0:T(8,128)(2,1)S(1)}, u32[]{:S(2)}, u32[]{:S(2)}) collective-permute-start(bf16[384,256]{1,0:T(8,128)(2,1)S(1)} %get-tuple-element.65), channel_id=1, source_target_pairs={{0,8},{4,12},{8,0},{12,4},{16,24},{20,28},{24,16},{28,20},{1,9},{5... | collective-permute-start | bytes 589832 | tf_op jit(solution)/shard_map/ppermute | solution.py:720
  23.5 1.5 %collective-permute-start.9 = (bf16[384,256]{1,0:T(8,128)(2,1)S(1)}, bf16[384,256]{1,0:T(8,128)(2,1)S(1)}, u32[]{:S(2)}, u32[]{:S(2)}) collective-permute-start(bf16[384,256]{1,0:T(8,128)(2,1)S(1)} %get-tuple-element.66), channel_id=1, source_target_pairs={{0,16},{4,20},{8,24},{12,28},{16,0},{20,4},{24,8},{28,12},{1,17},{... | collective-permute-start | bytes 589832 | tf_op jit(solution)/shard_map/ppermute | solution.py:720
  25.4 1.5 %forward.1.spectrum_ref = f32[256,2048]{1,0:T(8,128)S(1)} custom-call(f32[2,128,8]{2,1,0:T(8,128)S(1)} %copy-done.2, f32[2,128,8]{2,1,0:T(8,128)S(1)} %copy-done.1, bf16[256,256]{1,0:T(8,128)(2,1)S(1)} %copy-done.3, bf16[2,128,256]{2,1,0:T(8,128)(2,1)S(1)} %get-tuple-element.60.refs_0_, bf16[2,128,256]{2,1,0:T(8,128)(2,1)S(1)} %get-tuple-element.61.refs_1_, ...), custom_call_target="tpu_custom_call" | custom-call | tf_op jit(solution)/shard_map/forward/pallas_call | solution.py:386
  26.9 2.0 %backward.1 = (f32[4,128,256]{2,1,0:T(8,128)S(1)}, bf16[2,128,256]{2,1,0:T(8,128)(2,1)S(1)}, bf16[2,128,256]{2,1,0:T(8,128)(2,1)S(1)}) custom-call(f32[2,128,8]{2,1,0:T(8,128)S(1)} %copy-done.2, f32[2,128,8]{2,1,0:T(8,128)S(1)} %copy-done.1, bf16[256,256]{1,0:T(8,128)(2,1)S(1)} %copy-done.4, f32[256,2048]{1,0:T(8,128)S(1)} %forward.1.spectrum_ref, ...), custom_call_target="tpu_custom_call" | custom-call | tf_op jit(solution)/shard_map/backward/pallas_call | solution.py:462
  29.6 4.7 %collective-permute-done.9.refs_6_.refs_1_ = bf16[384,256]{1,0:T(8,128)(2,1)S(1)} collective-permute-done((bf16[384,256]{1,0:T(8,128)(2,1)S(1)}, bf16[384,256]{1,0:T(8,128)(2,1)S(1)}, u32[]{:S(2)}, u32[]{:S(2)}) %collective-permute-start.9) | collective-permute-done | bytes 196640 | tf_op jit(solution)/shard_map/ppermute | solution.py:720
  34.6 1.6 %collective-permute-start.12 = (bf16[528,256]{1,0:T(8,128)(2,1)S(1)}, bf16[528,256]{1,0:T(8,128)(2,1)S(1)}, u32[]{:S(2)}, u32[]{:S(2)}) collective-permute-start(bf16[528,256]{1,0:T(8,128)(2,1)S(1)} %get-tuple-element.69), channel_id=1, source_target_pairs={{0,16},{4,20},{8,24},{12,28},{16,0},{20,4},{24,8},{28,12},{1,17},{... | collective-permute-start | bytes 811016 | tf_op jit(solution)/shard_map/ppermute | solution.py:720
  36.7 1.4 %collective-permute-start.13 = (bf16[512,256]{1,0:T(8,128)(2,1)S(1)}, bf16[512,256]{1,0:T(8,128)(2,1)S(1)}, u32[]{:S(2)}, u32[]{:S(2)}) collective-permute-start(bf16[512,256]{1,0:T(8,128)(2,1)S(1)} %get-tuple-element.83.refs_0_), channel_id=1, source_target_pairs={{0,24},{4,28},{8,16},{12,20},{16,8},{20,12},{24,0},{28,4},{1,25},{... | collective-permute-start | bytes 786440 | tf_op jit(solution)/shard_map/ppermute | solution.py:720
  38.8 10.1 %collective-permute-done.13.refs_3_ = bf16[512,256]{1,0:T(8,128)(2,1)S(1)} collective-permute-done((bf16[512,256]{1,0:T(8,128)(2,1)S(1)}, bf16[512,256]{1,0:T(8,128)(2,1)S(1)}, u32[]{:S(2)}, u32[]{:S(2)}) %collective-permute-start.13) | collective-permute-done | bytes 262176 | tf_op jit(solution)/shard_map/ppermute | solution.py:720
  49.7 1.5 %collective-permute-start.14 = (bf16[144,512]{1,0:T(8,128)(2,1)S(1)}, bf16[144,512]{1,0:T(8,128)(2,1)S(1)}, u32[]{:S(2)}, u32[]{:S(2)}) collective-permute-start(bf16[144,512]{1,0:T(8,128)(2,1)S(1)} %get-tuple-element.71), channel_id=1, source_target_pairs={{0,8},{4,12},{8,0},{12,4},{16,24},{20,28},{24,16},{28,20},{1,9},{5... | collective-permute-start | bytes 442376 | tf_op jit(solution)/shard_map/ppermute | solution.py:720
  51.8 1.5 %collective-permute-start.16 = (bf16[144,512]{1,0:T(8,128)(2,1)S(1)}, bf16[144,512]{1,0:T(8,128)(2,1)S(1)}, u32[]{:S(2)}, u32[]{:S(2)}) collective-permute-start(bf16[144,512]{1,0:T(8,128)(2,1)S(1)} %get-tuple-element.73), channel_id=1, source_target_pairs={{0,24},{4,28},{8,16},{12,20},{16,8},{20,12},{24,0},{28,4},{1,25},{... | collective-permute-start | bytes 442376 | tf_op jit(solution)/shard_map/ppermute | solution.py:720
  54.3 1.6 %collective-permute-start.21 = (bf16[512,128]{1,0:T(8,128)(2,1)S(1)}, bf16[512,128]{1,0:T(8,128)(2,1)S(1)}, u32[]{:S(2)}, u32[]{:S(2)}) collective-permute-start(bf16[512,128]{1,0:T(8,128)(2,1)S(1)} %get-tuple-element.85), channel_id=1, source_target_pairs={{0,1},{1,0},{2,3},{3,2},{4,5},{5,4},{6,7},{7,6},{8,9},{9,8},{10,11... | collective-permute-start | bytes 393224 | tf_op jit(solution)/shard_map/ppermute | solution.py:720
  56.4 1.5 %collective-permute-done.15.refs_2_ = bf16[144,512]{1,0:T(8,128)(2,1)S(1)} collective-permute-done((bf16[144,512]{1,0:T(8,128)(2,1)S(1)}, bf16[144,512]{1,0:T(8,128)(2,1)S(1)}, u32[]{:S(2)}, u32[]{:S(2)}) %collective-permute-start.15) | collective-permute-done | bytes 147488 | tf_op jit(solution)/shard_map/ppermute | solution.py:720
  58.1 1.7 %collective-permute-start.17 = (bf16[2,128,512]{2,1,0:T(8,128)(2,1)S(1)}, bf16[2,128,512]{2,1,0:T(8,128)(2,1)S(1)}, u32[]{:S(2)}, u32[]{:S(2)}) collective-permute-start(bf16[2,128,512]{2,1,0:T(8,128)(2,1)S(1)} %get-tuple-element.75), channel_id=1, source_target_pairs={{0,1},{1,0},{2,3},{3,2},{4,5},{5,4},{6,7},{7,6},{8,9},{9,8},{10,11... | collective-permute-start | bytes 786440 | tf_op jit(solution)/shard_map/ppermute | solution.py:720
  59.7 2.4 %collective-permute-done.21.first_ref = bf16[512,128]{1,0:T(8,128)(2,1)S(1)} collective-permute-done((bf16[512,128]{1,0:T(8,128)(2,1)S(1)}, bf16[512,128]{1,0:T(8,128)(2,1)S(1)}, u32[]{:S(2)}, u32[]{:S(2)}) %collective-permute-start.21) | collective-permute-done | bytes 131104 | tf_op jit(solution)/shard_map/ppermute | solution.py:720
  62.2 2.5 %collective-permute-done.22 = bf16[512,128]{1,0:T(8,128)(2,1)S(1)} collective-permute-done((bf16[512,128]{1,0:T(8,128)(2,1)S(1)}, bf16[512,128]{1,0:T(8,128)(2,1)S(1)}, u32[]{:S(2)}, u32[]{:S(2)}) %collective-permute-start.22) | collective-permute-done | bytes 131104 | tf_op jit(solution)/shard_map/ppermute | solution.py:720
  64.7 1.6 %collective-permute-start.23 = (bf16[512,128]{1,0:T(8,128)(2,1)S(1)}, bf16[512,128]{1,0:T(8,128)(2,1)S(1)}, u32[]{:S(2)}, u32[]{:S(2)}) collective-permute-start(bf16[512,128]{1,0:T(8,128)(2,1)S(1)} %add_convert_fusion), channel_id=1, source_target_pairs={{0,2},{1,3},{2,0},{3,1},{4,6},{5,7},{6,4},{7,5},{8,10},{9,11},{10,... | collective-permute-start | bytes 393224 | tf_op jit(solution)/shard_map/ppermute | solution.py:720
  67.5 3.0 %collective-permute-start.18 = (bf16[128,512]{1,0:T(8,128)(2,1)S(1)}, bf16[128,512]{1,0:T(8,128)(2,1)S(1)}, u32[]{:S(2)}, u32[]{:S(2)}) collective-permute-start(bf16[128,512]{1,0:T(8,128)(2,1)S(1)} %fusion), channel_id=1, source_target_pairs={{0,2},{1,3},{2,0},{3,1},{4,6},{5,7},{6,4},{7,5},{8,10},{9,11},{10,... | collective-permute-start | bytes 393224 | tf_op jit(solution)/shard_map/ppermute | solution.py:720
  70.5 4.5 %collective-permute-done.23.second_ref = bf16[512,128]{1,0:T(8,128)(2,1)S(1)} collective-permute-done((bf16[512,128]{1,0:T(8,128)(2,1)S(1)}, bf16[512,128]{1,0:T(8,128)(2,1)S(1)}, u32[]{:S(2)}, u32[]{:S(2)}) %collective-permute-start.23) | collective-permute-done | bytes 131104 | tf_op jit(solution)/shard_map/ppermute | solution.py:720
  75.2 2.2 %collective-permute-start.25 = (bf16[128,128]{1,0:T(8,128)(2,1)S(1)}, bf16[128,128]{1,0:T(8,128)(2,1)S(1)}, u32[]{:S(2)}, u32[]{:S(2)}) collective-permute-start(bf16[128,128]{1,0:T(8,128)(2,1)S(1)} %get-tuple-element.91), channel_id=1, source_target_pairs={{0,16},{4,20},{8,24},{12,28},{16,0},{20,4},{24,8},{28,12},{1,17},{... | collective-permute-start | bytes 98312 | tf_op jit(solution)/shard_map/ppermute | solution.py:720
  79.3 2.9 %collective-permute-done.26.refs_3_ = bf16[128,128]{1,0:T(8,128)(2,1)S(1)} collective-permute-done((bf16[128,128]{1,0:T(8,128)(2,1)S(1)}, bf16[128,128]{1,0:T(8,128)(2,1)S(1)}, u32[]{:S(2)}, u32[]{:S(2)}) %collective-permute-start.26) | collective-permute-done | bytes 32800 | tf_op jit(solution)/shard_map/ppermute | solution.py:720
  (58 shorter events, 13.3 us)
Async XLA Ops:
  0.0 7.5 %collective-permute-start = (bf16[1024,512]{1,0:T(8,128)(2,1)}, bf16[1024,512]{1,0:T(8,128)(2,1)S(1)}, u32[]{:S(2)}, u32[]{:S(2)}) collective-permute-start(bf16[1024,512]{1,0:T(8,128)(2,1)} %own_ref.3), channel_id=1, source_target_pairs={{0,4},{4,0},{8,12},{12,8},{16,20},{20,16},{24,28},{28,24},{1,5},{5... | collective-permute-start | bytes 3145736 | tf_op jit(solution)/shard_map/ppermute | solution.py:720
  1.9 19.4 %collective-permute-start.2 = (bf16[656,256]{1,0:T(8,128)(2,1)S(1)}, bf16[656,256]{1,0:T(8,128)(2,1)S(1)}, u32[]{:S(2)}, u32[]{:S(2)}) collective-permute-start(bf16[656,256]{1,0:T(8,128)(2,1)S(1)} %get-tuple-element.56), channel_id=1, source_target_pairs={{0,16},{4,20},{8,24},{12,28},{16,0},{20,4},{24,8},{28,12},{1,17},{... | collective-permute-start | bytes 1007624 | tf_op jit(solution)/shard_map/ppermute | solution.py:720
  4.4 16.8 %collective-permute-start.1 = (bf16[656,256]{1,0:T(8,128)(2,1)S(1)}, bf16[656,256]{1,0:T(8,128)(2,1)S(1)}, u32[]{:S(2)}, u32[]{:S(2)}) collective-permute-start(bf16[656,256]{1,0:T(8,128)(2,1)S(1)} %get-tuple-element.49), channel_id=1, source_target_pairs={{0,8},{4,12},{8,0},{12,4},{16,24},{20,28},{24,16},{28,20},{1,9},{5... | collective-permute-start | bytes 1007624 | tf_op jit(solution)/shard_map/ppermute | solution.py:720
  7.4 13.9 %collective-permute-start.3 = (bf16[640,256]{1,0:T(8,128)(2,1)S(1)}, bf16[640,256]{1,0:T(8,128)(2,1)S(1)}, u32[]{:S(2)}, u32[]{:S(2)}) collective-permute-start(bf16[640,256]{1,0:T(8,128)(2,1)S(1)} %get-tuple-element.58), channel_id=1, source_target_pairs={{0,24},{4,28},{8,16},{12,20},{16,8},{20,12},{24,0},{28,4},{1,25},{... | collective-permute-start | bytes 983048 | tf_op jit(solution)/shard_map/ppermute | solution.py:720
  21.9 7.8 %collective-permute-start.8 = (bf16[384,256]{1,0:T(8,128)(2,1)S(1)}, bf16[384,256]{1,0:T(8,128)(2,1)S(1)}, u32[]{:S(2)}, u32[]{:S(2)}) collective-permute-start(bf16[384,256]{1,0:T(8,128)(2,1)S(1)} %get-tuple-element.65), channel_id=1, source_target_pairs={{0,8},{4,12},{8,0},{12,4},{16,24},{20,28},{24,16},{28,20},{1,9},{5... | collective-permute-start | bytes 589832 | tf_op jit(solution)/shard_map/ppermute | solution.py:720
  23.5 10.8 %collective-permute-start.9 = (bf16[384,256]{1,0:T(8,128)(2,1)S(1)}, bf16[384,256]{1,0:T(8,128)(2,1)S(1)}, u32[]{:S(2)}, u32[]{:S(2)}) collective-permute-start(bf16[384,256]{1,0:T(8,128)(2,1)S(1)} %get-tuple-element.66), channel_id=1, source_target_pairs={{0,16},{4,20},{8,24},{12,28},{16,0},{20,4},{24,8},{28,12},{1,17},{... | collective-permute-start | bytes 589832 | tf_op jit(solution)/shard_map/ppermute | solution.py:720
  25.1 9.3 %collective-permute-start.10 = (bf16[384,256]{1,0:T(8,128)(2,1)S(1)}, bf16[384,256]{1,0:T(8,128)(2,1)S(1)}, u32[]{:S(2)}, u32[]{:S(2)}) collective-permute-start(bf16[384,256]{1,0:T(8,128)(2,1)S(1)} %get-tuple-element.67), channel_id=1, source_target_pairs={{0,24},{4,28},{8,16},{12,20},{16,8},{20,12},{24,0},{28,4},{1,25},{... | collective-permute-start | bytes 589832 | tf_op jit(solution)/shard_map/ppermute | solution.py:720
  29.0 5.4 %collective-permute-start.6 = (bf16[2,128,256]{2,1,0:T(8,128)(2,1)S(1)}, bf16[2,128,256]{2,1,0:T(8,128)(2,1)S(1)}, u32[]{:S(2)}, u32[]{:S(2)}) collective-permute-start(bf16[2,128,256]{2,1,0:T(8,128)(2,1)S(1)} %get-tuple-element.63), channel_id=1, source_target_pairs={{0,4},{4,0},{8,12},{12,8},{16,20},{20,16},{24,28},{28,24},{1,5},{5... | collective-permute-start | bytes 393224 | tf_op jit(solution)/shard_map/ppermute | solution.py:720
  29.0 5.3 %collective-permute-start.7 = (bf16[2,128,256]{2,1,0:T(8,128)(2,1)S(1)}, bf16[2,128,256]{2,1,0:T(8,128)(2,1)S(1)}, u32[]{:S(2)}, u32[]{:S(2)}) collective-permute-start(bf16[2,128,256]{2,1,0:T(8,128)(2,1)S(1)} %get-tuple-element.64), channel_id=1, source_target_pairs={{0,4},{4,0},{8,12},{12,8},{16,20},{20,16},{24,28},{28,24},{1,5},{5... | collective-permute-start | bytes 393224 | tf_op jit(solution)/shard_map/ppermute | solution.py:720
  34.6 14.3 %collective-permute-start.12 = (bf16[528,256]{1,0:T(8,128)(2,1)S(1)}, bf16[528,256]{1,0:T(8,128)(2,1)S(1)}, u32[]{:S(2)}, u32[]{:S(2)}) collective-permute-start(bf16[528,256]{1,0:T(8,128)(2,1)S(1)} %get-tuple-element.69), channel_id=1, source_target_pairs={{0,16},{4,20},{8,24},{12,28},{16,0},{20,4},{24,8},{28,12},{1,17},{... | collective-permute-start | bytes 811016 | tf_op jit(solution)/shard_map/ppermute | solution.py:720
  36.1 12.7 %collective-permute-start.11 = (bf16[528,256]{1,0:T(8,128)(2,1)S(1)}, bf16[528,256]{1,0:T(8,128)(2,1)S(1)}, u32[]{:S(2)}, u32[]{:S(2)}) collective-permute-start(bf16[528,256]{1,0:T(8,128)(2,1)S(1)} %get-tuple-element.69), channel_id=1, source_target_pairs={{0,8},{4,12},{8,0},{12,4},{16,24},{20,28},{24,16},{28,20},{1,9},{5... | collective-permute-start | bytes 811016 | tf_op jit(solution)/shard_map/ppermute | solution.py:720
  36.7 12.2 %collective-permute-start.13 = (bf16[512,256]{1,0:T(8,128)(2,1)S(1)}, bf16[512,256]{1,0:T(8,128)(2,1)S(1)}, u32[]{:S(2)}, u32[]{:S(2)}) collective-permute-start(bf16[512,256]{1,0:T(8,128)(2,1)S(1)} %get-tuple-element.83.refs_0_), channel_id=1, source_target_pairs={{0,24},{4,28},{8,16},{12,20},{16,8},{20,12},{24,0},{28,4},{1,25},{... | collective-permute-start | bytes 786440 | tf_op jit(solution)/shard_map/ppermute | solution.py:720
  38.2 15.1 %collective-permute-start.19 = (bf16[768,128]{1,0:T(8,128)(2,1)S(1)}, bf16[768,128]{1,0:T(8,128)(2,1)S(1)}, u32[]{:S(2)}, u32[]{:S(2)}) collective-permute-start(bf16[768,128]{1,0:T(8,128)(2,1)S(1)} %get-tuple-element.81), channel_id=1, source_target_pairs={{0,4},{4,0},{8,12},{12,8},{16,20},{20,16},{24,28},{28,24},{1,5},{5... | collective-permute-start | bytes 589832 | tf_op jit(solution)/shard_map/ppermute | solution.py:720
  38.3 15.0 %collective-permute-start.20 = (bf16[768,128]{1,0:T(8,128)(2,1)S(1)}, bf16[768,128]{1,0:T(8,128)(2,1)S(1)}, u32[]{:S(2)}, u32[]{:S(2)}) collective-permute-start(bf16[768,128]{1,0:T(8,128)(2,1)S(1)} %get-tuple-element.82), channel_id=1, source_target_pairs={{0,4},{4,0},{8,12},{12,8},{16,20},{20,16},{24,28},{28,24},{1,5},{5... | collective-permute-start | bytes 589832 | tf_op jit(solution)/shard_map/ppermute | solution.py:720
  49.7 6.7 %collective-permute-start.14 = (bf16[144,512]{1,0:T(8,128)(2,1)S(1)}, bf16[144,512]{1,0:T(8,128)(2,1)S(1)}, u32[]{:S(2)}, u32[]{:S(2)}) collective-permute-start(bf16[144,512]{1,0:T(8,128)(2,1)S(1)} %get-tuple-element.71), channel_id=1, source_target_pairs={{0,8},{4,12},{8,0},{12,4},{16,24},{20,28},{24,16},{28,20},{1,9},{5... | collective-permute-start | bytes 442376 | tf_op jit(solution)/shard_map/ppermute | solution.py:720
  51.2 6.7 %collective-permute-start.15 = (bf16[144,512]{1,0:T(8,128)(2,1)S(1)}, bf16[144,512]{1,0:T(8,128)(2,1)S(1)}, u32[]{:S(2)}, u32[]{:S(2)}) collective-permute-start(bf16[144,512]{1,0:T(8,128)(2,1)S(1)} %get-tuple-element.72), channel_id=1, source_target_pairs={{0,16},{4,20},{8,24},{12,28},{16,0},{20,4},{24,8},{28,12},{1,17},{... | collective-permute-start | bytes 442376 | tf_op jit(solution)/shard_map/ppermute | solution.py:720
  51.8 6.2 %collective-permute-start.16 = (bf16[144,512]{1,0:T(8,128)(2,1)S(1)}, bf16[144,512]{1,0:T(8,128)(2,1)S(1)}, u32[]{:S(2)}, u32[]{:S(2)}) collective-permute-start(bf16[144,512]{1,0:T(8,128)(2,1)S(1)} %get-tuple-element.73), channel_id=1, source_target_pairs={{0,24},{4,28},{8,16},{12,20},{16,8},{20,12},{24,0},{28,4},{1,25},{... | collective-permute-start | bytes 442376 | tf_op jit(solution)/shard_map/ppermute | solution.py:720
  54.3 7.8 %collective-permute-start.21 = (bf16[512,128]{1,0:T(8,128)(2,1)S(1)}, bf16[512,128]{1,0:T(8,128)(2,1)S(1)}, u32[]{:S(2)}, u32[]{:S(2)}) collective-permute-start(bf16[512,128]{1,0:T(8,128)(2,1)S(1)} %get-tuple-element.85), channel_id=1, source_target_pairs={{0,1},{1,0},{2,3},{3,2},{4,5},{5,4},{6,7},{7,6},{8,9},{9,8},{10,11... | collective-permute-start | bytes 393224 | tf_op jit(solution)/shard_map/ppermute | solution.py:720
  56.0 8.7 %collective-permute-start.22 = (bf16[512,128]{1,0:T(8,128)(2,1)S(1)}, bf16[512,128]{1,0:T(8,128)(2,1)S(1)}, u32[]{:S(2)}, u32[]{:S(2)}) collective-permute-start(bf16[512,128]{1,0:T(8,128)(2,1)S(1)} %get-tuple-element.88), channel_id=1, source_target_pairs={{0,1},{1,0},{2,3},{3,2},{4,5},{5,4},{6,7},{7,6},{8,9},{9,8},{10,11... | collective-permute-start | bytes 393224 | tf_op jit(solution)/shard_map/ppermute | solution.py:720
  58.1 9.4 %collective-permute-start.17 = (bf16[2,128,512]{2,1,0:T(8,128)(2,1)S(1)}, bf16[2,128,512]{2,1,0:T(8,128)(2,1)S(1)}, u32[]{:S(2)}, u32[]{:S(2)}) collective-permute-start(bf16[2,128,512]{2,1,0:T(8,128)(2,1)S(1)} %get-tuple-element.75), channel_id=1, source_target_pairs={{0,1},{1,0},{2,3},{3,2},{4,5},{5,4},{6,7},{7,6},{8,9},{9,8},{10,11... | collective-permute-start | bytes 786440 | tf_op jit(solution)/shard_map/ppermute | solution.py:720
  64.7 10.4 %collective-permute-start.23 = (bf16[512,128]{1,0:T(8,128)(2,1)S(1)}, bf16[512,128]{1,0:T(8,128)(2,1)S(1)}, u32[]{:S(2)}, u32[]{:S(2)}) collective-permute-start(bf16[512,128]{1,0:T(8,128)(2,1)S(1)} %add_convert_fusion), channel_id=1, source_target_pairs={{0,2},{1,3},{2,0},{3,1},{4,6},{5,7},{6,4},{7,5},{8,10},{9,11},{10,... | collective-permute-start | bytes 393224 | tf_op jit(solution)/shard_map/ppermute | solution.py:720
  67.5 14.7 %collective-permute-start.18 = (bf16[128,512]{1,0:T(8,128)(2,1)S(1)}, bf16[128,512]{1,0:T(8,128)(2,1)S(1)}, u32[]{:S(2)}, u32[]{:S(2)}) collective-permute-start(bf16[128,512]{1,0:T(8,128)(2,1)S(1)} %fusion), channel_id=1, source_target_pairs={{0,2},{1,3},{2,0},{3,1},{4,6},{5,7},{6,4},{7,5},{8,10},{9,11},{10,... | collective-permute-start | bytes 393224 | tf_op jit(solution)/shard_map/ppermute | solution.py:720
  75.2 4.1 %collective-permute-start.25 = (bf16[128,128]{1,0:T(8,128)(2,1)S(1)}, bf16[128,128]{1,0:T(8,128)(2,1)S(1)}, u32[]{:S(2)}, u32[]{:S(2)}) collective-permute-start(bf16[128,128]{1,0:T(8,128)(2,1)S(1)} %get-tuple-element.91), channel_id=1, source_target_pairs={{0,16},{4,20},{8,24},{12,28},{16,0},{20,4},{24,8},{28,12},{1,17},{... | collective-permute-start | bytes 98312 | tf_op jit(solution)/shard_map/ppermute | solution.py:720
  77.4 4.8 %collective-permute-start.26 = (bf16[128,128]{1,0:T(8,128)(2,1)S(1)}, bf16[128,128]{1,0:T(8,128)(2,1)S(1)}, u32[]{:S(2)}, u32[]{:S(2)}) collective-permute-start(bf16[128,128]{1,0:T(8,128)(2,1)S(1)} %get-tuple-element.92), channel_id=1, source_target_pairs={{0,24},{4,28},{8,16},{12,20},{16,8},{20,12},{24,0},{28,4},{1,25},{... | collective-permute-start | bytes 98312 | tf_op jit(solution)/shard_map/ppermute | solution.py:720
  (9 other events, 111.6 us)

commit v13 on v11

--- a/solution.py
+++ b/solution.py
@@ -213,51 +213,74 @@
     return pl.ds(pl.multiple_of(index * size, size), size)
 
 
-def pack_signals_kernel(chips, values_ref, filter_ref, *refs):
-    out_refs, (plane_ref, arrived) = refs[:chips], refs[chips:]
+def pack_filters_kernel(offsets, filter_ref, *refs):
+    out_refs, (plane_ref, arrived) = refs[: len(offsets)], refs[len(offsets) :]
     chip, _ = own_place()
     planes, rows, _ = filter_ref.shape
     lanes = out_refs[0].shape[1]
-    copies, work = [], []
-    for offset in range(chips):
+    copies = []
+    for place, offset in enumerate(offsets):
         here = block_at(chip ^ offset, lanes)
         for plane in range(planes):
             copies.append(
-                pltpu.make_async_copy(filter_ref.at[plane, :, here], plane_ref.at[offset, plane], arrived.at[offset, plane])
+                pltpu.make_async_copy(filter_ref.at[plane, :, here], plane_ref.at[place, plane], arrived.at[place, plane])
             )
-            work.append((offset, plane))
-        values = out_refs[offset].at[pl.ds(planes * rows, rows)]
-        copies.append(pltpu.make_async_copy(values_ref.at[:, here], values, arrived.at[offset, planes]))
-        work.append(None)
     for copy in copies:
         copy.start()
-    for copy, task in zip(copies, work):
+    for index, copy in enumerate(copies):
         copy.wait()
-        if task:
-            offset, plane = task
-            out_refs[offset][pl.ds(plane * rows, rows), :] = plane_ref[offset, plane].astype(BF16)
-    used = (planes + 1) * rows
+        place, plane = divmod(index, planes)
+        out_refs[place][pl.ds(plane * rows, rows), :] = plane_ref[place, plane].astype(BF16)
+    used = planes * rows
     for out_ref in out_refs:
         if out_ref.shape[0] > used:
             out_ref[pl.ds(used, out_ref.shape[0] - used), :] = out_ref[pl.ds(0, out_ref.shape[0] - used), :]
 
 
-def pack_signals(values_in, filters, chips, spare):
+def pack_filters(filters, chips, offsets, spare):
     planes, rows, width = filters.shape
     lanes = width // chips
     return pl.pallas_call(
-        functools.partial(pack_signals_kernel, chips),
-        in_specs=[pl.BlockSpec(memory_space=pltpu.HBM)] * 2,
+        functools.partial(pack_filters_kernel, offsets),
+        in_specs=[pl.BlockSpec(memory_space=pltpu.HBM)],
+        out_specs=[WHOLE] * len(offsets),
+        out_shape=[jax.ShapeDtypeStruct((planes * rows + spare, lanes), BF16)] * len(offsets),
+        scratch_shapes=[
+            pltpu.VMEM((len(offsets), planes, rows, lanes), F32),
+            pltpu.SemaphoreType.DMA((len(offsets), planes)),
+        ],
+        cost_estimate=CHEAP,
+        compiler_params=pltpu.CompilerParams(vmem_limit_bytes=8 * 2**20),
+        name="pack_filters",
+    )(pltpu.with_memory_space_constraint(filters, pltpu.HBM))
+
+
+def pack_values_kernel(chips, values_ref, *refs):
+    out_refs, arrived = refs[:chips], refs[chips]
+    rows = values_ref.shape[0]
+    chip, _ = own_place()
+    copies = []
+    for offset, out_ref in enumerate(out_refs):
+        values = values_ref.at[:, block_at(chip ^ offset, out_ref.shape[1])]
+        copies.append(pltpu.make_async_copy(values, out_ref.at[pl.ds(0, rows)], arrived.at[offset]))
+    for copy in copies:
+        copy.start()
+    for copy in copies:
+        copy.wait()
+
+
+def pack_values(values_in, chips, spare):
+    rows, width = values_in.shape
+    return pl.pallas_call(
+        functools.partial(pack_values_kernel, chips),
+        in_specs=[pl.BlockSpec(memory_space=pltpu.HBM)],
         out_specs=[WHOLE] * chips,
-        out_shape=[jax.ShapeDtypeStruct(((planes + 1) * rows + more, lanes), BF16) for more in spare],
-        scratch_shapes=[
-            pltpu.VMEM((chips, planes, rows, lanes), F32),
-            pltpu.SemaphoreType.DMA((chips, planes + 1)),
-        ],
-        cost_estimate=CHEAP,
-        compiler_params=pltpu.CompilerParams(vmem_limit_bytes=8 * 2**20),
-        name="pack_signals",
-    )(*(pltpu.with_memory_space_constraint(array, pltpu.HBM) for array in (values_in, filters)))
+        out_shape=[jax.ShapeDtypeStruct((rows + spare, width // chips), BF16)] * chips,
+        scratch_shapes=[pltpu.SemaphoreType.DMA((chips,))],
+        cost_estimate=CHEAP,
+        compiler_params=pltpu.CompilerParams(vmem_limit_bytes=4 * 2**20),
+        name="pack_values",
+    )(pltpu.with_memory_space_constraint(values_in, pltpu.HBM))
 
 
 def pack_moved_kernel(chips, gate_ref, own_ref, other_ref, *refs):
@@ -310,25 +333,25 @@
     )(*(pltpu.with_memory_space_constraint(array, pltpu.HBM) for array in (gate_values, own)), other)
 
 
-def pick_values_kernel(chips, start, *refs):
+def stack_kernel(chips, *refs):
     in_refs, out_refs = refs[:chips], refs[chips:]
-    for offset in range(chips):
+    for offset, in_ref in enumerate(in_refs):
         part, place = divmod(offset, chips // 2)
-        out_refs[part][place] = in_refs[offset][pl.ds(start, out_refs[part].shape[1]), :]
-
-
-def pick_values(first, rows, start):
-    chips = len(first)
-    half = jax.ShapeDtypeStruct((chips // 2, rows, first[0].shape[1]), BF16)
-    return pl.pallas_call(
-        functools.partial(pick_values_kernel, chips, start),
+        out_refs[part][place] = in_ref[pl.ds(0, out_refs[part].shape[1]), :]
+
+
+def stack(blocks, rows):
+    chips = len(blocks)
+    half = jax.ShapeDtypeStruct((chips // 2, rows, blocks[0].shape[1]), BF16)
+    return pl.pallas_call(
+        functools.partial(stack_kernel, chips),
         in_specs=[WHOLE] * chips,
         out_specs=[WHOLE] * 2,
         out_shape=[half, half],
         cost_estimate=CHEAP,
         compiler_params=pltpu.CompilerParams(vmem_limit_bytes=4 * 2**20),
-        name="pick_values",
-    )(*first)
+        name="stack",
+    )(*blocks)
 
 
 def forward_kernel(chips, cos_ref, sin_ref, table_ref, *refs):
@@ -486,7 +509,7 @@
     for offset in range(chips):
         block = chip ^ offset
         convolved = keep_ref[block] + arrived_ref[block].astype(F32)
-        signal = signal_refs[offset][pl.ds(4 * rows, rows), :].astype(F32)
+        signal = signal_refs[offset][pl.ds(0, rows), :].astype(F32)
         gate = gate_refs[offset][pl.ds(0, rows), :].astype(F32)
         gated = (gate * (convolved + skip * signal)).astype(BF16)
         out_ref[block_at(block, rows), :] = gated
@@ -738,15 +761,18 @@
     rows, width = values_in.shape
     tables = small_tables(parts, rows)
 
-    first = pack_signals(values_in, filter_spectrum.reshape(4, rows, width), chips, (0, 16, 16, 0))
+    values = pack_values(values_in, chips, 0)
+    flat_filters = filter_spectrum.reshape(4, rows, width)
+    near = pack_filters(after(flat_filters, values[0]), chips, (1, 2), 0)
     other_weight = swapped(out_weight, "seq", 1)
-    *moved, mine = pack_moved(after(gate_values, first[0]), out_weight, other_weight, chips)
-    first = to_chips(first)
-    own = pick_values([after(block, moved[0]) for block in first], rows, 4 * rows)
-    moved = to_chips(moved)
+    *moved, mine = pack_moved(after(gate_values, near[0]), out_weight, other_weight, chips)
+    own, far = pack_filters(after(flat_filters, moved[0]), chips, (0, 3), 0)
+    values, filters = to_chips(values), to_chips([own, *near, far])
+    own = stack([after(block, far) for block in values], rows)
     spectrum = forward(own, [swapped(part, "seq", 1) for part in own], tables)
-    keep, *send = backward(spectrum, first, tables)
-    gated, longer = gate(skip_gain[None, :], keep, [swapped(part, "seq", 1) for part in send], first, moved, 16)
+    moved = to_chips([after(block, spectrum) for block in moved])
+    keep, *send = backward(spectrum, filters, tables)
+    gated, longer = gate(skip_gain[None, :], keep, [swapped(part, "seq", 1) for part in send], values, moved, 16)
     gathered = to_chips([gated, longer, longer, gated])
 
     others = [swapped(part, "seq", 1) for part in collect([after(block, gated) for block in moved[1:]], out_weight.shape[0] // 2)]

time: 79.1 us -> 76.3 us (0.965)
  waiting for transfers between devices: 41.1 us -> 33 us
  starting transfers between devices: 27.8 us -> 31.2 us
  Pallas kernels: 9.72 us -> 11.6 us
    ppermute x26 -> x29, waiting for transfers between devices: 41.1 us -> 33 us  [swapped(): lax.ppermute(value, axis, [(source, source ^ offset) for source in range(...]
    ppermute x26 -> x29, starting transfers between devices: 27.8 us -> 31.2 us  [swapped(): lax.ppermute(value, axis, [(source, source ^ offset) for source in range(...]
    pallas_call x2 -> x4, Pallas kernels: 1.87 us -> 3.73 us  [the longest x2 2.74 us: pack_filters(): pl.pallas_call(functools.partial(pack_filters_kernel, offsets), in_specs=...]
  transfers between devices with their start and end apart: 26 -> 29, of which waited for: 13 -> 16; matrix products, arithmetic and copies ran while one was open for 0% -> 0% of each run, Pallas kernels for 10% -> 13%
where the time goes in v13:
time: 76.3 us; the launch traced here: 76.1 us
  waiting for transfers between devices  33 us (43%)
  starting transfers between devices  31.2 us (41%)
  Pallas kernels  11.6 us (15%)
    ppermute x29, waiting for transfers between devices, swapped(): lax.ppermute(value, axis, [(source, source ^ offset) for source in range(...  33 us
    ppermute x29, starting transfers between devices, swapped(): lax.ppermute(value, axis, [(source, source ^ offset) for source in range(...  31.2 us
    pallas_call x2, Pallas kernels, pack_filters(): pl.pallas_call(functools.partial(pack_filters_kernel, offsets), in_specs=...  2.74 us
    pallas_call x1, Pallas kernels, backward(): pl.pallas_call(functools.partial(backward_kernel, chips), in_specs=[WHOLE...  2.01 us
  transfers between devices with their start and end apart: 29, of which 16 were waited for; matrix products, arithmetic and copies ran while one was open for 0% of the time, Pallas kernels for 13%

profile of v13, /device:TPU:0, one launch (start us, length us, event | category | flops | bytes accessed | tf_op | source)
XLA Modules:
  0.0 76.1 jit_solution(14146778500347280929)
XLA Ops:
  1.4 3.5 %collective-permute-start.3 = (bf16[128,256]{1,0:T(8,128)(2,1)S(1)}, bf16[128,256]{1,0:T(8,128)(2,1)S(1)}, u32[]{:S(2)}, u32[]{:S(2)}) collective-permute-start(bf16[128,256]{1,0:T(8,128)(2,1)S(1)} %get-tuple-element.67), channel_id=1, source_target_pairs={{0,24},{4,28},{8,16},{12,20},{16,8},{20,12},{24,0},{28,4},{1,25},{... | collective-permute-start | bytes 196616 | tf_op jit(solution)/shard_map/ppermute | solution.py:741
  4.9 1.4 %pack_filters.2 = (bf16[512,256]{1,0:T(8,128)(2,1)S(1)}, bf16[512,256]{1,0:T(8,128)(2,1)S(1)}) custom-call(f32[4,128,1024]{2,1,0:T(8,128)} %bitcast.13), custom_call_target="tpu_custom_call" | custom-call | tf_op jit(solution)/shard_map/pack_filters/pallas_call | solution.py:243
  6.9 1.5 %collective-permute-start.2 = (bf16[128,256]{1,0:T(8,128)(2,1)S(1)}, bf16[128,256]{1,0:T(8,128)(2,1)S(1)}, u32[]{:S(2)}, u32[]{:S(2)}) collective-permute-start(bf16[128,256]{1,0:T(8,128)(2,1)S(1)} %get-tuple-element.65), channel_id=1, source_target_pairs={{0,16},{4,20},{8,24},{12,28},{16,0},{20,4},{24,8},{28,12},{1,17},{... | collective-permute-start | bytes 196616 | tf_op jit(solution)/shard_map/ppermute | solution.py:741
  9.0 1.6 %collective-permute-start.6 = (bf16[512,256]{1,0:T(8,128)(2,1)S(1)}, bf16[512,256]{1,0:T(8,128)(2,1)S(1)}, u32[]{:S(2)}, u32[]{:S(2)}) collective-permute-start(bf16[512,256]{1,0:T(8,128)(2,1)S(1)} %get-tuple-element.57), channel_id=1, source_target_pairs={{0,8},{4,12},{8,0},{12,4},{16,24},{20,28},{24,16},{28,20},{1,9},{5... | collective-permute-start | bytes 786440 | tf_op jit(solution)/shard_map/ppermute | solution.py:741
  10.5 1.3 %pack_moved.1 = (bf16[128,256]{1,0:T(8,128)(2,1)S(1)}, bf16[384,256]{1,0:T(8,128)(2,1)S(1)}, bf16[384,256]{1,0:T(8,128)(2,1)S(1)}, bf16[384,256]{1,0:T(8,128)(2,1)S(1)}, bf16[1024,128]{1,0:T(8,128)(2,1)S(1)}) custom-call(bf16[128,1024]{1,0:T(8,128)(2,1)} %gate_ref, bf16[1024,512]{1,0:T(8,128)(2,1)} %own_ref.3, ...), custom_call_target="tpu_custom_call" | custom-call | tf_op jit(solution)/shard_map/pack_moved/pallas_call | solution.py:321
  11.8 1.4 %pack_filters.3 = (bf16[512,256]{1,0:T(8,128)(2,1)S(1)}, bf16[512,256]{1,0:T(8,128)(2,1)S(1)}) custom-call(f32[4,128,1024]{2,1,0:T(8,128)} %bitcast.14), custom_call_target="tpu_custom_call" | custom-call | tf_op jit(solution)/shard_map/pack_filters/pallas_call | solution.py:243
  13.3 2.9 %collective-permute-done.2.refs_2_ = bf16[128,256]{1,0:T(8,128)(2,1)S(1)} collective-permute-done((bf16[128,256]{1,0:T(8,128)(2,1)S(1)}, bf16[128,256]{1,0:T(8,128)(2,1)S(1)}, u32[]{:S(2)}, u32[]{:S(2)}) %collective-permute-start.2) | collective-permute-done | bytes 65568 | tf_op jit(solution)/shard_map/ppermute | solution.py:741
  17.9 1.5 %forward.1.spectrum_ref = f32[256,2048]{1,0:T(8,128)S(1)} custom-call(f32[2,128,8]{2,1,0:T(8,128)S(1)} %copy-done.2, f32[2,128,8]{2,1,0:T(8,128)S(1)} %copy-done.1, bf16[256,256]{1,0:T(8,128)(2,1)S(1)} %copy-done.4, bf16[2,128,256]{2,1,0:T(8,128)(2,1)S(1)} %get-tuple-element.69.refs_0_, bf16[2,128,256]{2,1,0:T(8,128)(2,1)S(1)} %get-tuple-element.70.refs_1_, ...), custom_call_target="tpu_custom_call" | custom-call | tf_op jit(solution)/shard_map/forward/pallas_call | solution.py:409
  21.1 1.8 %collective-permute-start.13 = (bf16[384,256]{1,0:T(8,128)(2,1)S(1)}, bf16[384,256]{1,0:T(8,128)(2,1)S(1)}, u32[]{:S(2)}, u32[]{:S(2)}) collective-permute-start(bf16[384,256]{1,0:T(8,128)(2,1)S(1)} %get-tuple-element.82), channel_id=1, source_target_pairs={{0,24},{4,28},{8,16},{12,20},{16,8},{20,12},{24,0},{28,4},{1,25},{... | collective-permute-start | bytes 589832 | tf_op jit(solution)/shard_map/ppermute | solution.py:741
  24.2 2.0 %backward.1 = (f32[4,128,256]{2,1,0:T(8,128)S(1)}, bf16[2,128,256]{2,1,0:T(8,128)(2,1)S(1)}, bf16[2,128,256]{2,1,0:T(8,128)(2,1)S(1)}) custom-call(f32[2,128,8]{2,1,0:T(8,128)S(1)} %copy-done.2, f32[2,128,8]{2,1,0:T(8,128)S(1)} %copy-done.1, bf16[256,256]{1,0:T(8,128)(2,1)S(1)} %copy-done.3, f32[256,2048]{1,0:T(8,128)S(1)} %forward.1.spectrum_ref, ...), custom_call_target="tpu_custom_call" | custom-call | tf_op jit(solution)/shard_map/backward/pallas_call | solution.py:485
  26.7 1.7 %collective-permute-done.11.refs_5_.refs_0_ = bf16[384,256]{1,0:T(8,128)(2,1)S(1)} collective-permute-done((bf16[384,256]{1,0:T(8,128)(2,1)S(1)}, bf16[384,256]{1,0:T(8,128)(2,1)S(1)}, u32[]{:S(2)}, u32[]{:S(2)}) %collective-permute-start.11) | collective-permute-done | bytes 196640 | tf_op jit(solution)/shard_map/ppermute | solution.py:741
  28.4 3.4 %collective-permute-done.12.refs_6_.refs_1_ = bf16[384,256]{1,0:T(8,128)(2,1)S(1)} collective-permute-done((bf16[384,256]{1,0:T(8,128)(2,1)S(1)}, bf16[384,256]{1,0:T(8,128)(2,1)S(1)}, u32[]{:S(2)}, u32[]{:S(2)}) %collective-permute-start.12) | collective-permute-done | bytes 196640 | tf_op jit(solution)/shard_map/ppermute | solution.py:741
  32.0 1.5 %collective-permute-start.15 = (bf16[528,256]{1,0:T(8,128)(2,1)S(1)}, bf16[528,256]{1,0:T(8,128)(2,1)S(1)}, u32[]{:S(2)}, u32[]{:S(2)}) collective-permute-start(bf16[528,256]{1,0:T(8,128)(2,1)S(1)} %get-tuple-element.84), channel_id=1, source_target_pairs={{0,16},{4,20},{8,24},{12,28},{16,0},{20,4},{24,8},{28,12},{1,17},{... | collective-permute-start | bytes 811016 | tf_op jit(solution)/shard_map/ppermute | solution.py:741
  37.6 8.8 %collective-permute-done.16.refs_3_ = bf16[512,256]{1,0:T(8,128)(2,1)S(1)} collective-permute-done((bf16[512,256]{1,0:T(8,128)(2,1)S(1)}, bf16[512,256]{1,0:T(8,128)(2,1)S(1)}, u32[]{:S(2)}, u32[]{:S(2)}) %collective-permute-start.16) | collective-permute-done | bytes 262176 | tf_op jit(solution)/shard_map/ppermute | solution.py:741
  47.2 1.6 %collective-permute-start.24 = (bf16[2,512,128]{2,1,0:T(8,128)(2,1)S(1)}, bf16[2,512,128]{2,1,0:T(8,128)(2,1)S(1)}, u32[]{:S(2)}, u32[]{:S(2)}) collective-permute-start(bf16[2,512,128]{2,1,0:T(8,128)(2,1)S(1)} %get-tuple-element.99), channel_id=1, source_target_pairs={{0,1},{1,0},{2,3},{3,2},{4,5},{5,4},{6,7},{7,6},{8,9},{9,8},{10,11... | collective-permute-start | bytes 786440 | tf_op jit(solution)/shard_map/ppermute | solution.py:741
  49.8 1.3 %collective-permute-start.17 = (bf16[128,512]{1,0:T(8,128)(2,1)S(1)}, bf16[128,512]{1,0:T(8,128)(2,1)S(1)}, u32[]{:S(2)}, u32[]{:S(2)}) collective-permute-start(bf16[128,512]{1,0:T(8,128)(2,1)S(1)} %get-tuple-element.86), channel_id=1, source_target_pairs={{0,8},{4,12},{8,0},{12,4},{16,24},{20,28},{24,16},{28,20},{1,9},{5... | collective-permute-start | bytes 393224 | tf_op jit(solution)/shard_map/ppermute | solution.py:741
  51.0 1.3 %collective-permute-start.18 = (bf16[128,512]{1,0:T(8,128)(2,1)S(1)}, bf16[128,512]{1,0:T(8,128)(2,1)S(1)}, u32[]{:S(2)}, u32[]{:S(2)}) collective-permute-start(bf16[128,512]{1,0:T(8,128)(2,1)S(1)} %get-tuple-element.87), channel_id=1, source_target_pairs={{0,16},{4,20},{8,24},{12,28},{16,0},{20,4},{24,8},{28,12},{1,17},{... | collective-permute-start | bytes 393224 | tf_op jit(solution)/shard_map/ppermute | solution.py:741
  53.3 1.7 %collective-permute-done.17.refs_1_ = bf16[128,512]{1,0:T(8,128)(2,1)S(1)} collective-permute-done((bf16[128,512]{1,0:T(8,128)(2,1)S(1)}, bf16[128,512]{1,0:T(8,128)(2,1)S(1)}, u32[]{:S(2)}, u32[]{:S(2)}) %collective-permute-start.17) | collective-permute-done | bytes 131104 | tf_op jit(solution)/shard_map/ppermute | solution.py:741
  56.0 2.2 %collective-permute-done.19.refs_3_ = bf16[128,512]{1,0:T(8,128)(2,1)S(1)} collective-permute-done((bf16[128,512]{1,0:T(8,128)(2,1)S(1)}, bf16[128,512]{1,0:T(8,128)(2,1)S(1)}, u32[]{:S(2)}, u32[]{:S(2)}) %collective-permute-start.19) | collective-permute-done | bytes 131104 | tf_op jit(solution)/shard_map/ppermute | solution.py:741
  58.9 2.7 %collective-permute-start.25 = (bf16[512,128]{1,0:T(8,128)(2,1)S(1)}, bf16[512,128]{1,0:T(8,128)(2,1)S(1)}, u32[]{:S(2)}, u32[]{:S(2)}) collective-permute-start(bf16[512,128]{1,0:T(8,128)(2,1)S(1)} %fusion), channel_id=1, source_target_pairs={{0,2},{1,3},{2,0},{3,1},{4,6},{5,7},{6,4},{7,5},{8,10},{9,11},{10,... | collective-permute-start | bytes 393224 | tf_op jit(solution)/shard_map/ppermute | solution.py:741
  61.5 5.0 %collective-permute-done.20.first_ref = bf16[2,128,512]{2,1,0:T(8,128)(2,1)S(1)} collective-permute-done((bf16[2,128,512]{2,1,0:T(8,128)(2,1)S(1)}, bf16[2,128,512]{2,1,0:T(8,128)(2,1)S(1)}, u32[]{:S(2)}, u32[]{:S(2)}) %collective-permute-start.20) | collective-permute-done | bytes 262176 | tf_op jit(solution)/shard_map/ppermute | solution.py:741
  66.6 2.2 %collective-permute-start.21 = (bf16[128,512]{1,0:T(8,128)(2,1)S(1)}, bf16[128,512]{1,0:T(8,128)(2,1)S(1)}, u32[]{:S(2)}, u32[]{:S(2)}) collective-permute-start(bf16[128,512]{1,0:T(8,128)(2,1)S(1)} %fusion.1), channel_id=1, source_target_pairs={{0,2},{1,3},{2,0},{3,1},{4,6},{5,7},{6,4},{7,5},{8,10},{9,11},{10,... | collective-permute-start | bytes 393224 | tf_op jit(solution)/shard_map/ppermute | solution.py:741
  70.5 1.9 %collective-permute-start.28 = (bf16[128,128]{1,0:T(8,128)(2,1)S(1)}, bf16[128,128]{1,0:T(8,128)(2,1)S(1)}, u32[]{:S(2)}, u32[]{:S(2)}) collective-permute-start(bf16[128,128]{1,0:T(8,128)(2,1)S(1)} %get-tuple-element.104), channel_id=1, source_target_pairs={{0,24},{4,28},{8,16},{12,20},{16,8},{20,12},{24,0},{28,4},{1,25},{... | collective-permute-start | bytes 98312 | tf_op jit(solution)/shard_map/ppermute | solution.py:741
  73.8 1.5 %collective-permute-done.28.refs_3_ = bf16[128,128]{1,0:T(8,128)(2,1)S(1)} collective-permute-done((bf16[128,128]{1,0:T(8,128)(2,1)S(1)}, bf16[128,128]{1,0:T(8,128)(2,1)S(1)}, u32[]{:S(2)}, u32[]{:S(2)}) %collective-permute-start.28) | collective-permute-done | bytes 32800 | tf_op jit(solution)/shard_map/ppermute | solution.py:741
  (63 shorter events, 20.4 us)
Async XLA Ops:
  0.0 8.9 %collective-permute-start = (bf16[1024,512]{1,0:T(8,128)(2,1)}, bf16[1024,512]{1,0:T(8,128)(2,1)S(1)}, u32[]{:S(2)}, u32[]{:S(2)}) collective-permute-start(bf16[1024,512]{1,0:T(8,128)(2,1)} %own_ref.3), channel_id=1, source_target_pairs={{0,4},{4,0},{8,12},{12,8},{16,20},{20,16},{24,28},{28,24},{1,5},{5... | collective-permute-start | bytes 3145736 | tf_op jit(solution)/shard_map/ppermute | solution.py:741
  1.4 11.8 %collective-permute-start.3 = (bf16[128,256]{1,0:T(8,128)(2,1)S(1)}, bf16[128,256]{1,0:T(8,128)(2,1)S(1)}, u32[]{:S(2)}, u32[]{:S(2)}) collective-permute-start(bf16[128,256]{1,0:T(8,128)(2,1)S(1)} %get-tuple-element.67), channel_id=1, source_target_pairs={{0,24},{4,28},{8,16},{12,20},{16,8},{20,12},{24,0},{28,4},{1,25},{... | collective-permute-start | bytes 196616 | tf_op jit(solution)/shard_map/ppermute | solution.py:741
  6.3 14.8 %collective-permute-start.7 = (bf16[512,256]{1,0:T(8,128)(2,1)S(1)}, bf16[512,256]{1,0:T(8,128)(2,1)S(1)}, u32[]{:S(2)}, u32[]{:S(2)}) collective-permute-start(bf16[512,256]{1,0:T(8,128)(2,1)S(1)} %get-tuple-element.72), channel_id=1, source_target_pairs={{0,16},{4,20},{8,24},{12,28},{16,0},{20,4},{24,8},{28,12},{1,17},{... | collective-permute-start | bytes 786440 | tf_op jit(solution)/shard_map/ppermute | solution.py:741
  6.9 9.3 %collective-permute-start.2 = (bf16[128,256]{1,0:T(8,128)(2,1)S(1)}, bf16[128,256]{1,0:T(8,128)(2,1)S(1)}, u32[]{:S(2)}, u32[]{:S(2)}) collective-permute-start(bf16[128,256]{1,0:T(8,128)(2,1)S(1)} %get-tuple-element.65), channel_id=1, source_target_pairs={{0,16},{4,20},{8,24},{12,28},{16,0},{20,4},{24,8},{28,12},{1,17},{... | collective-permute-start | bytes 196616 | tf_op jit(solution)/shard_map/ppermute | solution.py:741
  8.4 7.8 %collective-permute-start.1 = (bf16[128,256]{1,0:T(8,128)(2,1)S(1)}, bf16[128,256]{1,0:T(8,128)(2,1)S(1)}, u32[]{:S(2)}, u32[]{:S(2)}) collective-permute-start(bf16[128,256]{1,0:T(8,128)(2,1)S(1)} %get-tuple-element.63), channel_id=1, source_target_pairs={{0,8},{4,12},{8,0},{12,4},{16,24},{20,28},{24,16},{28,20},{1,9},{5... | collective-permute-start | bytes 196616 | tf_op jit(solution)/shard_map/ppermute | solution.py:741
  9.0 14.0 %collective-permute-start.6 = (bf16[512,256]{1,0:T(8,128)(2,1)S(1)}, bf16[512,256]{1,0:T(8,128)(2,1)S(1)}, u32[]{:S(2)}, u32[]{:S(2)}) collective-permute-start(bf16[512,256]{1,0:T(8,128)(2,1)S(1)} %get-tuple-element.57), channel_id=1, source_target_pairs={{0,8},{4,12},{8,0},{12,4},{16,24},{20,28},{24,16},{28,20},{1,9},{5... | collective-permute-start | bytes 786440 | tf_op jit(solution)/shard_map/ppermute | solution.py:741
  13.2 11.0 %collective-permute-start.8 = (bf16[512,256]{1,0:T(8,128)(2,1)S(1)}, bf16[512,256]{1,0:T(8,128)(2,1)S(1)}, u32[]{:S(2)}, u32[]{:S(2)}) collective-permute-start(bf16[512,256]{1,0:T(8,128)(2,1)S(1)} %get-tuple-element.61), channel_id=1, source_target_pairs={{0,24},{4,28},{8,16},{12,20},{16,8},{20,12},{24,0},{28,4},{1,25},{... | collective-permute-start | bytes 786440 | tf_op jit(solution)/shard_map/ppermute | solution.py:741
  19.4 9.1 %collective-permute-start.11 = (bf16[384,256]{1,0:T(8,128)(2,1)S(1)}, bf16[384,256]{1,0:T(8,128)(2,1)S(1)}, u32[]{:S(2)}, u32[]{:S(2)}) collective-permute-start(bf16[384,256]{1,0:T(8,128)(2,1)S(1)} %get-tuple-element.78), channel_id=1, source_target_pairs={{0,8},{4,12},{8,0},{12,4},{16,24},{20,28},{24,16},{28,20},{1,9},{5... | collective-permute-start | bytes 589832 | tf_op jit(solution)/shard_map/ppermute | solution.py:741
  20.0 11.8 %collective-permute-start.12 = (bf16[384,256]{1,0:T(8,128)(2,1)S(1)}, bf16[384,256]{1,0:T(8,128)(2,1)S(1)}, u32[]{:S(2)}, u32[]{:S(2)}) collective-permute-start(bf16[384,256]{1,0:T(8,128)(2,1)S(1)} %get-tuple-element.80), channel_id=1, source_target_pairs={{0,16},{4,20},{8,24},{12,28},{16,0},{20,4},{24,8},{28,12},{1,17},{... | collective-permute-start | bytes 589832 | tf_op jit(solution)/shard_map/ppermute | solution.py:741
  21.1 10.7 %collective-permute-start.13 = (bf16[384,256]{1,0:T(8,128)(2,1)S(1)}, bf16[384,256]{1,0:T(8,128)(2,1)S(1)}, u32[]{:S(2)}, u32[]{:S(2)}) collective-permute-start(bf16[384,256]{1,0:T(8,128)(2,1)S(1)} %get-tuple-element.82), channel_id=1, source_target_pairs={{0,24},{4,28},{8,16},{12,20},{16,8},{20,12},{24,0},{28,4},{1,25},{... | collective-permute-start | bytes 589832 | tf_op jit(solution)/shard_map/ppermute | solution.py:741
  26.2 5.6 %collective-permute-start.9 = (bf16[2,128,256]{2,1,0:T(8,128)(2,1)S(1)}, bf16[2,128,256]{2,1,0:T(8,128)(2,1)S(1)}, u32[]{:S(2)}, u32[]{:S(2)}) collective-permute-start(bf16[2,128,256]{2,1,0:T(8,128)(2,1)S(1)} %get-tuple-element.74), channel_id=1, source_target_pairs={{0,4},{4,0},{8,12},{12,8},{16,20},{20,16},{24,28},{28,24},{1,5},{5... | collective-permute-start | bytes 393224 | tf_op jit(solution)/shard_map/ppermute | solution.py:741
  26.3 5.6 %collective-permute-start.10 = (bf16[2,128,256]{2,1,0:T(8,128)(2,1)S(1)}, bf16[2,128,256]{2,1,0:T(8,128)(2,1)S(1)}, u32[]{:S(2)}, u32[]{:S(2)}) collective-permute-start(bf16[2,128,256]{2,1,0:T(8,128)(2,1)S(1)} %get-tuple-element.75), channel_id=1, source_target_pairs={{0,4},{4,0},{8,12},{12,8},{16,20},{20,16},{24,28},{28,24},{1,5},{5... | collective-permute-start | bytes 393224 | tf_op jit(solution)/shard_map/ppermute | solution.py:741
  32.0 14.4 %collective-permute-start.15 = (bf16[528,256]{1,0:T(8,128)(2,1)S(1)}, bf16[528,256]{1,0:T(8,128)(2,1)S(1)}, u32[]{:S(2)}, u32[]{:S(2)}) collective-permute-start(bf16[528,256]{1,0:T(8,128)(2,1)S(1)} %get-tuple-element.84), channel_id=1, source_target_pairs={{0,16},{4,20},{8,24},{12,28},{16,0},{20,4},{24,8},{28,12},{1,17},{... | collective-permute-start | bytes 811016 | tf_op jit(solution)/shard_map/ppermute | solution.py:741
  33.5 12.9 %collective-permute-start.14 = (bf16[528,256]{1,0:T(8,128)(2,1)S(1)}, bf16[528,256]{1,0:T(8,128)(2,1)S(1)}, u32[]{:S(2)}, u32[]{:S(2)}) collective-permute-start(bf16[528,256]{1,0:T(8,128)(2,1)S(1)} %get-tuple-element.84), channel_id=1, source_target_pairs={{0,8},{4,12},{8,0},{12,4},{16,24},{20,28},{24,16},{28,20},{1,9},{5... | collective-permute-start | bytes 811016 | tf_op jit(solution)/shard_map/ppermute | solution.py:741
  34.6 11.8 %collective-permute-start.16 = (bf16[512,256]{1,0:T(8,128)(2,1)S(1)}, bf16[512,256]{1,0:T(8,128)(2,1)S(1)}, u32[]{:S(2)}, u32[]{:S(2)}) collective-permute-start(bf16[512,256]{1,0:T(8,128)(2,1)S(1)} %get-tuple-element.83.refs_0_), channel_id=1, source_target_pairs={{0,24},{4,28},{8,16},{12,20},{16,8},{20,12},{24,0},{28,4},{1,25},{... | collective-permute-start | bytes 786440 | tf_op jit(solution)/shard_map/ppermute | solution.py:741
  47.2 11.6 %collective-permute-start.24 = (bf16[2,512,128]{2,1,0:T(8,128)(2,1)S(1)}, bf16[2,512,128]{2,1,0:T(8,128)(2,1)S(1)}, u32[]{:S(2)}, u32[]{:S(2)}) collective-permute-start(bf16[2,512,128]{2,1,0:T(8,128)(2,1)S(1)} %get-tuple-element.99), channel_id=1, source_target_pairs={{0,1},{1,0},{2,3},{3,2},{4,5},{5,4},{6,7},{7,6},{8,9},{9,8},{10,11... | collective-permute-start | bytes 786440 | tf_op jit(solution)/shard_map/ppermute | solution.py:741
  49.8 5.2 %collective-permute-start.17 = (bf16[128,512]{1,0:T(8,128)(2,1)S(1)}, bf16[128,512]{1,0:T(8,128)(2,1)S(1)}, u32[]{:S(2)}, u32[]{:S(2)}) collective-permute-start(bf16[128,512]{1,0:T(8,128)(2,1)S(1)} %get-tuple-element.86), channel_id=1, source_target_pairs={{0,8},{4,12},{8,0},{12,4},{16,24},{20,28},{24,16},{28,20},{1,9},{5... | collective-permute-start | bytes 393224 | tf_op jit(solution)/shard_map/ppermute | solution.py:741
  51.0 5.0 %collective-permute-start.18 = (bf16[128,512]{1,0:T(8,128)(2,1)S(1)}, bf16[128,512]{1,0:T(8,128)(2,1)S(1)}, u32[]{:S(2)}, u32[]{:S(2)}) collective-permute-start(bf16[128,512]{1,0:T(8,128)(2,1)S(1)} %get-tuple-element.87), channel_id=1, source_target_pairs={{0,16},{4,20},{8,24},{12,28},{16,0},{20,4},{24,8},{28,12},{1,17},{... | collective-permute-start | bytes 393224 | tf_op jit(solution)/shard_map/ppermute | solution.py:741
  52.4 5.9 %collective-permute-start.19 = (bf16[128,512]{1,0:T(8,128)(2,1)S(1)}, bf16[128,512]{1,0:T(8,128)(2,1)S(1)}, u32[]{:S(2)}, u32[]{:S(2)}) collective-permute-start(bf16[128,512]{1,0:T(8,128)(2,1)S(1)} %get-tuple-element.88), channel_id=1, source_target_pairs={{0,24},{4,28},{8,16},{12,20},{16,8},{20,12},{24,0},{28,4},{1,25},{... | collective-permute-start | bytes 393224 | tf_op jit(solution)/shard_map/ppermute | solution.py:741
  58.3 8.3 %collective-permute-start.20 = (bf16[2,128,512]{2,1,0:T(8,128)(2,1)S(1)}, bf16[2,128,512]{2,1,0:T(8,128)(2,1)S(1)}, u32[]{:S(2)}, u32[]{:S(2)}) collective-permute-start(bf16[2,128,512]{2,1,0:T(8,128)(2,1)S(1)} %get-tuple-element.90), channel_id=1, source_target_pairs={{0,1},{1,0},{2,3},{3,2},{4,5},{5,4},{6,7},{7,6},{8,9},{9,8},{10,11... | collective-permute-start | bytes 786440 | tf_op jit(solution)/shard_map/ppermute | solution.py:741
  58.9 9.9 %collective-permute-start.25 = (bf16[512,128]{1,0:T(8,128)(2,1)S(1)}, bf16[512,128]{1,0:T(8,128)(2,1)S(1)}, u32[]{:S(2)}, u32[]{:S(2)}) collective-permute-start(bf16[512,128]{1,0:T(8,128)(2,1)S(1)} %fusion), channel_id=1, source_target_pairs={{0,2},{1,3},{2,0},{3,1},{4,6},{5,7},{6,4},{7,5},{8,10},{9,11},{10,... | collective-permute-start | bytes 393224 | tf_op jit(solution)/shard_map/ppermute | solution.py:741
  66.6 8.7 %collective-permute-start.21 = (bf16[128,512]{1,0:T(8,128)(2,1)S(1)}, bf16[128,512]{1,0:T(8,128)(2,1)S(1)}, u32[]{:S(2)}, u32[]{:S(2)}) collective-permute-start(bf16[128,512]{1,0:T(8,128)(2,1)S(1)} %fusion.1), channel_id=1, source_target_pairs={{0,2},{1,3},{2,0},{3,1},{4,6},{5,7},{6,4},{7,5},{8,10},{9,11},{10,... | collective-permute-start | bytes 393224 | tf_op jit(solution)/shard_map/ppermute | solution.py:741
  68.9 4.0 %collective-permute-start.26 = (bf16[128,128]{1,0:T(8,128)(2,1)S(1)}, bf16[128,128]{1,0:T(8,128)(2,1)S(1)}, u32[]{:S(2)}, u32[]{:S(2)}) collective-permute-start(bf16[128,128]{1,0:T(8,128)(2,1)S(1)} %get-tuple-element.102), channel_id=1, source_target_pairs={{0,8},{4,12},{8,0},{12,4},{16,24},{20,28},{24,16},{28,20},{1,9},{5... | collective-permute-start | bytes 98312 | tf_op jit(solution)/shard_map/ppermute | solution.py:741
  70.5 4.8 %collective-permute-start.28 = (bf16[128,128]{1,0:T(8,128)(2,1)S(1)}, bf16[128,128]{1,0:T(8,128)(2,1)S(1)}, u32[]{:S(2)}, u32[]{:S(2)}) collective-permute-start(bf16[128,128]{1,0:T(8,128)(2,1)S(1)} %get-tuple-element.104), channel_id=1, source_target_pairs={{0,24},{4,28},{8,16},{12,20},{16,8},{20,12},{24,0},{28,4},{1,25},{... | collective-permute-start | bytes 98312 | tf_op jit(solution)/shard_map/ppermute | solution.py:741
  (11 other events, 71.7 us)

commit v14 on v13

--- a/solution.py
+++ b/solution.py
@@ -689,44 +689,69 @@
     )(*blocks)
 
 
-def finish_kernel(chips, keep_ref, first_ref, second_ref, *out_refs):
+def finish_kernel(keep_ref, first_ref, second_ref, own_ref, beside_ref, above_ref):
     chip, _ = own_place()
-    rows = out_refs[0].shape[0]
-    for offset in range(chips):
-        here = block_at(chip ^ offset, rows)
+    rows = own_ref.shape[0]
+
+    def block_of(target):
+        here = block_at(target, rows)
         total = keep_ref[here, :].astype(F32) + first_ref[0, here, :].astype(F32) + second_ref[here, :].astype(F32)
-        out_refs[offset][...] = total.astype(BF16)
-
-
-def finish(keep, first, second, chips):
-    rows, columns = keep.shape
-    return pl.pallas_call(
-        functools.partial(finish_kernel, chips),
+        return total.astype(BF16)
+
+    own_ref[...] = block_of(chip)
+    beside_ref[pl.ds(0, rows), :] = block_of(chip ^ 1)
+    beside_ref[pl.ds(rows, rows), :] = block_of(chip ^ 3)
+    more = beside_ref.shape[0] - 2 * rows
+    beside_ref[pl.ds(2 * rows, more), :] = beside_ref[pl.ds(0, more), :]
+    above_ref[...] = block_of(chip ^ 2)
+
+
+def finish(keep, first, second, rows, spare):
+    columns = keep.shape[1]
+    block = jax.ShapeDtypeStruct((rows, columns), BF16)
+    return pl.pallas_call(
+        finish_kernel,
         in_specs=[WHOLE] * 3,
-        out_specs=[WHOLE] * chips,
-        out_shape=[jax.ShapeDtypeStruct((rows // chips, columns), BF16)] * chips,
+        out_specs=[WHOLE] * 3,
+        out_shape=[block, jax.ShapeDtypeStruct((2 * rows + spare, columns), BF16), block],
         cost_estimate=CHEAP,
         compiler_params=pltpu.CompilerParams(vmem_limit_bytes=4 * 2**20),
         name="finish",
     )(keep, first, second)
 
 
-def join_kernel(chips, keep_ref, first_ref, second_ref, *refs):
-    in_refs, out_ref = refs[:chips], refs[chips]
+def relay_kernel(own_ref, arrived_ref, out_ref):
+    rows = own_ref.shape[0]
+    out_ref[pl.ds(0, rows), :] = own_ref[...]
+    out_ref[pl.ds(rows, out_ref.shape[0] - rows), :] = arrived_ref[pl.ds(rows, out_ref.shape[0] - rows), :]
+
+
+def relay(own, arrived):
+    return pl.pallas_call(
+        relay_kernel,
+        in_specs=[WHOLE] * 2,
+        out_specs=WHOLE,
+        out_shape=jax.ShapeDtypeStruct(arrived.shape, BF16),
+        cost_estimate=CHEAP,
+        compiler_params=pltpu.CompilerParams(vmem_limit_bytes=4 * 2**20),
+        name="relay",
+    )(own, arrived)
+
+
+def join_kernel(chips, keep_ref, first_ref, second_ref, own_ref, beside_ref, above_ref, out_ref):
     chip, _ = own_place()
-    share = in_refs[0].shape[1]
-    for offset in range(chips):
-        out_ref[:, block_at(chip ^ offset, share)] = in_refs[offset][...]
+    rows, share = own_ref.shape
+    for offset, (ref, part) in enumerate(((own_ref, 0), (beside_ref, 0), (above_ref, 0), (above_ref, 1))):
+        out_ref[:, block_at(chip ^ offset, share)] = ref[pl.ds(part * rows, rows), :]
     total = keep_ref[...].astype(F32) + first_ref[0].astype(F32) + second_ref[...].astype(F32)
     out_ref[:, pl.ds(chips * share, total.shape[1])] = total.astype(BF16)
 
 
-def join(keep, first, second, blocks):
-    chips = len(blocks)
+def join(keep, first, second, blocks, chips):
     rows, share = blocks[0].shape
     return pl.pallas_call(
         functools.partial(join_kernel, chips),
-        in_specs=[WHOLE] * (3 + chips),
+        in_specs=[WHOLE] * (3 + len(blocks)),
         out_specs=WHOLE,
         out_shape=jax.ShapeDtypeStruct((rows, chips * share + keep.shape[1]), BF16),
         cost_estimate=CHEAP,
@@ -743,6 +768,14 @@
 
 def to_chips(blocks):
     return [swapped(block, "seq", 2 * offset) for offset, block in enumerate(blocks)]
+
+
+def after(value, *others):
+    return lax.optimization_barrier((value, *others))[0]
+
+
+def added(left, right):
+    return (left.astype(F32) + right.astype(F32)).astype(BF16)
 
 
 def after(value, *others):
@@ -765,10 +798,10 @@
     flat_filters = filter_spectrum.reshape(4, rows, width)
     near = pack_filters(after(flat_filters, values[0]), chips, (1, 2), 0)
     other_weight = swapped(out_weight, "seq", 1)
-    *moved, mine = pack_moved(after(gate_values, near[0]), out_weight, other_weight, chips)
-    own, far = pack_filters(after(flat_filters, moved[0]), chips, (0, 3), 0)
+    own, far = pack_filters(after(flat_filters, near[0], other_weight), chips, (0, 3), 0)
+    *moved, mine = pack_moved(after(gate_values, far), out_weight, other_weight, chips)
     values, filters = to_chips(values), to_chips([own, *near, far])
-    own = stack([after(block, far) for block in values], rows)
+    own = stack([after(block, moved[0]) for block in values], rows)
     spectrum = forward(own, [swapped(part, "seq", 1) for part in own], tables)
     moved = to_chips([after(block, spectrum) for block in moved])
     keep, *send = backward(spectrum, filters, tables)
@@ -777,9 +810,14 @@
 
     others = [swapped(part, "seq", 1) for part in collect([after(block, gated) for block in moved[1:]], out_weight.shape[0] // 2)]
     keep, passed, send = project_moved(arrange(mine, moved[1:], others), gathered)
-    blocks = to_chips(finish(keep, *over_layers(passed, send), chips))
+    first = swapped(send, "chan", 1)
+    own, beside, above = finish(keep, first, swapped(added(passed, first[1]), "chan", 2), rows, 16)
+    beside = swapped(beside, "seq", 2)
+    above = swapped(relay(above, beside), "seq", 4)
     keep, passed, send = sort_blocks(to_chips(project_still(out_weight, other_weight, gathered)))
-    return join(keep, *over_layers(passed, send), blocks)
+    first = swapped(send, "chan", 1)
+    passed = added(after(passed, above), first[1])
+    return join(keep, first, swapped(passed, "chan", 2), (own, beside, above), chips)
 
 
 def shards(values_in, gate_values, filter_spectrum, skip_gain, out_weight):

time: 76.3 us -> 76.3 us (level)
    ppermute x29 -> x28, waiting for transfers between devices: 33 us -> 32.8 us  [swapped(): lax.ppermute(value, axis, [(source, source ^ offset) for source in range(...]
    ppermute x29 -> x28, starting transfers between devices: 31.2 us -> 31.3 us  [swapped(): lax.ppermute(value, axis, [(source, source ^ offset) for source in range(...]
  transfers between devices with their start and end apart: 29 -> 28, of which waited for: 16 -> 15; matrix products, arithmetic and copies ran while one was open for 0% -> 0% of each run, Pallas kernels for 13% -> 13%
where the time goes in v14:
time: 76.3 us; the launch traced here: 76 us
  waiting for transfers between devices  32.8 us (43%)
  starting transfers between devices  31.3 us (41%)
  Pallas kernels  11.6 us (15%)
    ppermute x28, waiting for transfers between devices, swapped(): lax.ppermute(value, axis, [(source, source ^ offset) for source in range(...  32.8 us
    ppermute x28, starting transfers between devices, swapped(): lax.ppermute(value, axis, [(source, source ^ offset) for source in range(...  31.3 us
    pallas_call x2, Pallas kernels, pack_filters(): pl.pallas_call(functools.partial(pack_filters_kernel, offsets), in_specs=...  2.73 us
    pallas_call x1, Pallas kernels, backward(): pl.pallas_call(functools.partial(backward_kernel, chips), in_specs=[WHOLE...  2.01 us
  transfers between devices with their start and end apart: 28, of which 15 were waited for; matrix products, arithmetic and copies ran while one was open for 0% of the time, Pallas kernels for 13%

profile of v14, /device:TPU:0, one launch (start us, length us, event | category | flops | bytes accessed | tf_op | source)
XLA Modules:
  0.0 76.0 jit_solution(2005354020095154947)
XLA Ops:
  1.4 3.5 %collective-permute-start.3 = (bf16[128,256]{1,0:T(8,128)(2,1)S(1)}, bf16[128,256]{1,0:T(8,128)(2,1)S(1)}, u32[]{:S(2)}, u32[]{:S(2)}) collective-permute-start(bf16[128,256]{1,0:T(8,128)(2,1)S(1)} %get-tuple-element.67), channel_id=1, source_target_pairs={{0,24},{4,28},{8,16},{12,20},{16,8},{20,12},{24,0},{28,4},{1,25},{... | collective-permute-start | bytes 196616 | tf_op jit(solution)/shard_map/ppermute | solution.py:766
  4.9 1.4 %pack_filters.2 = (bf16[512,256]{1,0:T(8,128)(2,1)S(1)}, bf16[512,256]{1,0:T(8,128)(2,1)S(1)}) custom-call(f32[4,128,1024]{2,1,0:T(8,128)} %bitcast.13), custom_call_target="tpu_custom_call" | custom-call | tf_op jit(solution)/shard_map/pack_filters/pallas_call | solution.py:243
  6.9 1.5 %collective-permute-start.2 = (bf16[128,256]{1,0:T(8,128)(2,1)S(1)}, bf16[128,256]{1,0:T(8,128)(2,1)S(1)}, u32[]{:S(2)}, u32[]{:S(2)}) collective-permute-start(bf16[128,256]{1,0:T(8,128)(2,1)S(1)} %get-tuple-element.65), channel_id=1, source_target_pairs={{0,16},{4,20},{8,24},{12,28},{16,0},{20,4},{24,8},{28,12},{1,17},{... | collective-permute-start | bytes 196616 | tf_op jit(solution)/shard_map/ppermute | solution.py:766
  9.0 1.6 %collective-permute-start.6 = (bf16[512,256]{1,0:T(8,128)(2,1)S(1)}, bf16[512,256]{1,0:T(8,128)(2,1)S(1)}, u32[]{:S(2)}, u32[]{:S(2)}) collective-permute-start(bf16[512,256]{1,0:T(8,128)(2,1)S(1)} %get-tuple-element.57), channel_id=1, source_target_pairs={{0,8},{4,12},{8,0},{12,4},{16,24},{20,28},{24,16},{28,20},{1,9},{5... | collective-permute-start | bytes 786440 | tf_op jit(solution)/shard_map/ppermute | solution.py:766
  10.5 1.4 %pack_filters.3 = (bf16[512,256]{1,0:T(8,128)(2,1)S(1)}, bf16[512,256]{1,0:T(8,128)(2,1)S(1)}) custom-call(f32[4,128,1024]{2,1,0:T(8,128)} %bitcast.14), custom_call_target="tpu_custom_call" | custom-call | tf_op jit(solution)/shard_map/pack_filters/pallas_call | solution.py:243
  13.3 2.9 %collective-permute-done.2.refs_2_ = bf16[128,256]{1,0:T(8,128)(2,1)S(1)} collective-permute-done((bf16[128,256]{1,0:T(8,128)(2,1)S(1)}, bf16[128,256]{1,0:T(8,128)(2,1)S(1)}, u32[]{:S(2)}, u32[]{:S(2)}) %collective-permute-start.2) | collective-permute-done | bytes 65568 | tf_op jit(solution)/shard_map/ppermute | solution.py:766
  17.9 1.5 %forward.1.spectrum_ref = f32[256,2048]{1,0:T(8,128)S(1)} custom-call(f32[2,128,8]{2,1,0:T(8,128)S(1)} %copy-done.2, f32[2,128,8]{2,1,0:T(8,128)S(1)} %copy-done.1, bf16[256,256]{1,0:T(8,128)(2,1)S(1)} %copy-done.4, bf16[2,128,256]{2,1,0:T(8,128)(2,1)S(1)} %get-tuple-element.69.refs_0_, bf16[2,128,256]{2,1,0:T(8,128)(2,1)S(1)} %get-tuple-element.70.refs_1_, ...), custom_call_target="tpu_custom_call" | custom-call | tf_op jit(solution)/shard_map/forward/pallas_call | solution.py:409
  21.1 1.8 %collective-permute-start.13 = (bf16[384,256]{1,0:T(8,128)(2,1)S(1)}, bf16[384,256]{1,0:T(8,128)(2,1)S(1)}, u32[]{:S(2)}, u32[]{:S(2)}) collective-permute-start(bf16[384,256]{1,0:T(8,128)(2,1)S(1)} %get-tuple-element.82), channel_id=1, source_target_pairs={{0,24},{4,28},{8,16},{12,20},{16,8},{20,12},{24,0},{28,4},{1,25},{... | collective-permute-start | bytes 589832 | tf_op jit(solution)/shard_map/ppermute | solution.py:766
  24.2 2.0 %backward.1 = (f32[4,128,256]{2,1,0:T(8,128)S(1)}, bf16[2,128,256]{2,1,0:T(8,128)(2,1)S(1)}, bf16[2,128,256]{2,1,0:T(8,128)(2,1)S(1)}) custom-call(f32[2,128,8]{2,1,0:T(8,128)S(1)} %copy-done.2, f32[2,128,8]{2,1,0:T(8,128)S(1)} %copy-done.1, bf16[256,256]{1,0:T(8,128)(2,1)S(1)} %copy-done.3, f32[256,2048]{1,0:T(8,128)S(1)} %forward.1.spectrum_ref, ...), custom_call_target="tpu_custom_call" | custom-call | tf_op jit(solution)/shard_map/backward/pallas_call | solution.py:485
  26.7 1.7 %collective-permute-done.11.refs_5_.refs_0_ = bf16[384,256]{1,0:T(8,128)(2,1)S(1)} collective-permute-done((bf16[384,256]{1,0:T(8,128)(2,1)S(1)}, bf16[384,256]{1,0:T(8,128)(2,1)S(1)}, u32[]{:S(2)}, u32[]{:S(2)}) %collective-permute-start.11) | collective-permute-done | bytes 196640 | tf_op jit(solution)/shard_map/ppermute | solution.py:766
  28.4 3.4 %collective-permute-done.12.refs_6_.refs_1_ = bf16[384,256]{1,0:T(8,128)(2,1)S(1)} collective-permute-done((bf16[384,256]{1,0:T(8,128)(2,1)S(1)}, bf16[384,256]{1,0:T(8,128)(2,1)S(1)}, u32[]{:S(2)}, u32[]{:S(2)}) %collective-permute-start.12) | collective-permute-done | bytes 196640 | tf_op jit(solution)/shard_map/ppermute | solution.py:766
  32.0 1.5 %collective-permute-start.15 = (bf16[528,256]{1,0:T(8,128)(2,1)S(1)}, bf16[528,256]{1,0:T(8,128)(2,1)S(1)}, u32[]{:S(2)}, u32[]{:S(2)}) collective-permute-start(bf16[528,256]{1,0:T(8,128)(2,1)S(1)} %get-tuple-element.84), channel_id=1, source_target_pairs={{0,16},{4,20},{8,24},{12,28},{16,0},{20,4},{24,8},{28,12},{1,17},{... | collective-permute-start | bytes 811016 | tf_op jit(solution)/shard_map/ppermute | solution.py:766
  37.6 8.8 %collective-permute-done.16.refs_3_ = bf16[512,256]{1,0:T(8,128)(2,1)S(1)} collective-permute-done((bf16[512,256]{1,0:T(8,128)(2,1)S(1)}, bf16[512,256]{1,0:T(8,128)(2,1)S(1)}, u32[]{:S(2)}, u32[]{:S(2)}) %collective-permute-start.16) | collective-permute-done | bytes 262176 | tf_op jit(solution)/shard_map/ppermute | solution.py:766
  47.2 1.6 %collective-permute-start.23 = (bf16[2,512,128]{2,1,0:T(8,128)(2,1)S(1)}, bf16[2,512,128]{2,1,0:T(8,128)(2,1)S(1)}, u32[]{:S(2)}, u32[]{:S(2)}) collective-permute-start(bf16[2,512,128]{2,1,0:T(8,128)(2,1)S(1)} %get-tuple-element.99), channel_id=1, source_target_pairs={{0,1},{1,0},{2,3},{3,2},{4,5},{5,4},{6,7},{7,6},{8,9},{9,8},{10,11... | collective-permute-start | bytes 786440 | tf_op jit(solution)/shard_map/ppermute | solution.py:766
  51.0 1.4 %collective-permute-start.18 = (bf16[128,512]{1,0:T(8,128)(2,1)S(1)}, bf16[128,512]{1,0:T(8,128)(2,1)S(1)}, u32[]{:S(2)}, u32[]{:S(2)}) collective-permute-start(bf16[128,512]{1,0:T(8,128)(2,1)S(1)} %get-tuple-element.87), channel_id=1, source_target_pairs={{0,16},{4,20},{8,24},{12,28},{16,0},{20,4},{24,8},{28,12},{1,17},{... | collective-permute-start | bytes 393224 | tf_op jit(solution)/shard_map/ppermute | solution.py:766
  53.7 3.2 %collective-permute-start.24 = (bf16[512,128]{1,0:T(8,128)(2,1)S(1)}, bf16[512,128]{1,0:T(8,128)(2,1)S(1)}, u32[]{:S(2)}, u32[]{:S(2)}) collective-permute-start(bf16[512,128]{1,0:T(8,128)(2,1)S(1)} %fusion.1), channel_id=1, source_target_pairs={{0,2},{1,3},{2,0},{3,1},{4,6},{5,7},{6,4},{7,5},{8,10},{9,11},{10,... | collective-permute-start | bytes 393224 | tf_op jit(solution)/shard_map/ppermute | solution.py:766
  56.9 1.3 %collective-permute-done.19.refs_3_ = bf16[128,512]{1,0:T(8,128)(2,1)S(1)} collective-permute-done((bf16[128,512]{1,0:T(8,128)(2,1)S(1)}, bf16[128,512]{1,0:T(8,128)(2,1)S(1)}, u32[]{:S(2)}, u32[]{:S(2)}) %collective-permute-start.19) | collective-permute-done | bytes 131104 | tf_op jit(solution)/shard_map/ppermute | solution.py:766
  58.9 1.7 %collective-permute-done.24.second_ref = bf16[512,128]{1,0:T(8,128)(2,1)S(1)} collective-permute-done((bf16[512,128]{1,0:T(8,128)(2,1)S(1)}, bf16[512,128]{1,0:T(8,128)(2,1)S(1)}, u32[]{:S(2)}, u32[]{:S(2)}) %collective-permute-start.24) | collective-permute-done | bytes 131104 | tf_op jit(solution)/shard_map/ppermute | solution.py:766
  60.6 1.5 %collective-permute-start.25 = (bf16[272,128]{1,0:T(8,128)(2,1)S(1)}, bf16[272,128]{1,0:T(8,128)(2,1)S(1)}, u32[]{:S(2)}, u32[]{:S(2)}) collective-permute-start(bf16[272,128]{1,0:T(8,128)(2,1)S(1)} %get-tuple-element.102), channel_id=1, source_target_pairs={{0,8},{4,12},{8,0},{12,4},{16,24},{20,28},{24,16},{28,20},{1,9},{5... | collective-permute-start | bytes 208904 | tf_op jit(solution)/shard_map/ppermute | solution.py:766
  62.0 2.9 %collective-permute-done.25.arrived_ref.beside_ref = bf16[272,128]{1,0:T(8,128)(2,1)S(1)} collective-permute-done((bf16[272,128]{1,0:T(8,128)(2,1)S(1)}, bf16[272,128]{1,0:T(8,128)(2,1)S(1)}, u32[]{:S(2)}, u32[]{:S(2)}) %collective-permute-start.25) | collective-permute-done | bytes 69664 | tf_op jit(solution)/shard_map/ppermute | solution.py:766
  64.9 1.4 %collective-permute-start.26 = (bf16[272,128]{1,0:T(8,128)(2,1)S(1)}, bf16[272,128]{1,0:T(8,128)(2,1)S(1)}, u32[]{:S(2)}, u32[]{:S(2)}) collective-permute-start(bf16[272,128]{1,0:T(8,128)(2,1)S(1)} %relay.1), channel_id=1, source_target_pairs={{0,16},{4,20},{8,24},{12,28},{16,0},{20,4},{24,8},{28,12},{1,17},{... | collective-permute-start | bytes 208904 | tf_op jit(solution)/shard_map/ppermute | solution.py:766
  66.3 2.9 %collective-permute-done.26.above_ref = bf16[272,128]{1,0:T(8,128)(2,1)S(1)} collective-permute-done((bf16[272,128]{1,0:T(8,128)(2,1)S(1)}, bf16[272,128]{1,0:T(8,128)(2,1)S(1)}, u32[]{:S(2)}, u32[]{:S(2)}) %collective-permute-start.26) | collective-permute-done | bytes 69664 | tf_op jit(solution)/shard_map/ppermute | solution.py:766
  69.3 2.5 %collective-permute-start.27 = (bf16[128,512]{1,0:T(8,128)(2,1)S(1)}, bf16[128,512]{1,0:T(8,128)(2,1)S(1)}, u32[]{:S(2)}, u32[]{:S(2)}) collective-permute-start(bf16[128,512]{1,0:T(8,128)(2,1)S(1)} %fusion), channel_id=1, source_target_pairs={{0,2},{1,3},{2,0},{3,1},{4,6},{5,7},{6,4},{7,5},{8,10},{9,11},{10,... | collective-permute-start | bytes 393224 | tf_op jit(solution)/shard_map/ppermute | solution.py:766
  71.8 3.5 %collective-permute-done.27.second_ref = bf16[128,512]{1,0:T(8,128)(2,1)S(1)} collective-permute-done((bf16[128,512]{1,0:T(8,128)(2,1)S(1)}, bf16[128,512]{1,0:T(8,128)(2,1)S(1)}, u32[]{:S(2)}, u32[]{:S(2)}) %collective-permute-start.27) | collective-permute-done | bytes 131104 | tf_op jit(solution)/shard_map/ppermute | solution.py:766
  (62 shorter events, 19.3 us)
Async XLA Ops:
  0.0 8.9 %collective-permute-start = (bf16[1024,512]{1,0:T(8,128)(2,1)}, bf16[1024,512]{1,0:T(8,128)(2,1)S(1)}, u32[]{:S(2)}, u32[]{:S(2)}) collective-permute-start(bf16[1024,512]{1,0:T(8,128)(2,1)} %own_ref.3), channel_id=1, source_target_pairs={{0,4},{4,0},{8,12},{12,8},{16,20},{20,16},{24,28},{28,24},{1,5},{5... | collective-permute-start | bytes 3145736 | tf_op jit(solution)/shard_map/ppermute | solution.py:766
  1.4 10.5 %collective-permute-start.3 = (bf16[128,256]{1,0:T(8,128)(2,1)S(1)}, bf16[128,256]{1,0:T(8,128)(2,1)S(1)}, u32[]{:S(2)}, u32[]{:S(2)}) collective-permute-start(bf16[128,256]{1,0:T(8,128)(2,1)S(1)} %get-tuple-element.67), channel_id=1, source_target_pairs={{0,24},{4,28},{8,16},{12,20},{16,8},{20,12},{24,0},{28,4},{1,25},{... | collective-permute-start | bytes 196616 | tf_op jit(solution)/shard_map/ppermute | solution.py:766
  6.3 14.8 %collective-permute-start.7 = (bf16[512,256]{1,0:T(8,128)(2,1)S(1)}, bf16[512,256]{1,0:T(8,128)(2,1)S(1)}, u32[]{:S(2)}, u32[]{:S(2)}) collective-permute-start(bf16[512,256]{1,0:T(8,128)(2,1)S(1)} %get-tuple-element.72), channel_id=1, source_target_pairs={{0,16},{4,20},{8,24},{12,28},{16,0},{20,4},{24,8},{28,12},{1,17},{... | collective-permute-start | bytes 786440 | tf_op jit(solution)/shard_map/ppermute | solution.py:766
  6.9 9.3 %collective-permute-start.2 = (bf16[128,256]{1,0:T(8,128)(2,1)S(1)}, bf16[128,256]{1,0:T(8,128)(2,1)S(1)}, u32[]{:S(2)}, u32[]{:S(2)}) collective-permute-start(bf16[128,256]{1,0:T(8,128)(2,1)S(1)} %get-tuple-element.65), channel_id=1, source_target_pairs={{0,16},{4,20},{8,24},{12,28},{16,0},{20,4},{24,8},{28,12},{1,17},{... | collective-permute-start | bytes 196616 | tf_op jit(solution)/shard_map/ppermute | solution.py:766
  8.4 7.8 %collective-permute-start.1 = (bf16[128,256]{1,0:T(8,128)(2,1)S(1)}, bf16[128,256]{1,0:T(8,128)(2,1)S(1)}, u32[]{:S(2)}, u32[]{:S(2)}) collective-permute-start(bf16[128,256]{1,0:T(8,128)(2,1)S(1)} %get-tuple-element.63), channel_id=1, source_target_pairs={{0,8},{4,12},{8,0},{12,4},{16,24},{20,28},{24,16},{28,20},{1,9},{5... | collective-permute-start | bytes 196616 | tf_op jit(solution)/shard_map/ppermute | solution.py:766
  9.0 14.0 %collective-permute-start.6 = (bf16[512,256]{1,0:T(8,128)(2,1)S(1)}, bf16[512,256]{1,0:T(8,128)(2,1)S(1)}, u32[]{:S(2)}, u32[]{:S(2)}) collective-permute-start(bf16[512,256]{1,0:T(8,128)(2,1)S(1)} %get-tuple-element.57), channel_id=1, source_target_pairs={{0,8},{4,12},{8,0},{12,4},{16,24},{20,28},{24,16},{28,20},{1,9},{5... | collective-permute-start | bytes 786440 | tf_op jit(solution)/shard_map/ppermute | solution.py:766
  11.9 12.3 %collective-permute-start.8 = (bf16[512,256]{1,0:T(8,128)(2,1)S(1)}, bf16[512,256]{1,0:T(8,128)(2,1)S(1)}, u32[]{:S(2)}, u32[]{:S(2)}) collective-permute-start(bf16[512,256]{1,0:T(8,128)(2,1)S(1)} %get-tuple-element.59), channel_id=1, source_target_pairs={{0,24},{4,28},{8,16},{12,20},{16,8},{20,12},{24,0},{28,4},{1,25},{... | collective-permute-start | bytes 786440 | tf_op jit(solution)/shard_map/ppermute | solution.py:766
  19.4 9.1 %collective-permute-start.11 = (bf16[384,256]{1,0:T(8,128)(2,1)S(1)}, bf16[384,256]{1,0:T(8,128)(2,1)S(1)}, u32[]{:S(2)}, u32[]{:S(2)}) collective-permute-start(bf16[384,256]{1,0:T(8,128)(2,1)S(1)} %get-tuple-element.78), channel_id=1, source_target_pairs={{0,8},{4,12},{8,0},{12,4},{16,24},{20,28},{24,16},{28,20},{1,9},{5... | collective-permute-start | bytes 589832 | tf_op jit(solution)/shard_map/ppermute | solution.py:766
  20.0 11.8 %collective-permute-start.12 = (bf16[384,256]{1,0:T(8,128)(2,1)S(1)}, bf16[384,256]{1,0:T(8,128)(2,1)S(1)}, u32[]{:S(2)}, u32[]{:S(2)}) collective-permute-start(bf16[384,256]{1,0:T(8,128)(2,1)S(1)} %get-tuple-element.80), channel_id=1, source_target_pairs={{0,16},{4,20},{8,24},{12,28},{16,0},{20,4},{24,8},{28,12},{1,17},{... | collective-permute-start | bytes 589832 | tf_op jit(solution)/shard_map/ppermute | solution.py:766
  21.1 10.7 %collective-permute-start.13 = (bf16[384,256]{1,0:T(8,128)(2,1)S(1)}, bf16[384,256]{1,0:T(8,128)(2,1)S(1)}, u32[]{:S(2)}, u32[]{:S(2)}) collective-permute-start(bf16[384,256]{1,0:T(8,128)(2,1)S(1)} %get-tuple-element.82), channel_id=1, source_target_pairs={{0,24},{4,28},{8,16},{12,20},{16,8},{20,12},{24,0},{28,4},{1,25},{... | collective-permute-start | bytes 589832 | tf_op jit(solution)/shard_map/ppermute | solution.py:766
  26.2 5.6 %collective-permute-start.9 = (bf16[2,128,256]{2,1,0:T(8,128)(2,1)S(1)}, bf16[2,128,256]{2,1,0:T(8,128)(2,1)S(1)}, u32[]{:S(2)}, u32[]{:S(2)}) collective-permute-start(bf16[2,128,256]{2,1,0:T(8,128)(2,1)S(1)} %get-tuple-element.74), channel_id=1, source_target_pairs={{0,4},{4,0},{8,12},{12,8},{16,20},{20,16},{24,28},{28,24},{1,5},{5... | collective-permute-start | bytes 393224 | tf_op jit(solution)/shard_map/ppermute | solution.py:766
  26.3 5.6 %collective-permute-start.10 = (bf16[2,128,256]{2,1,0:T(8,128)(2,1)S(1)}, bf16[2,128,256]{2,1,0:T(8,128)(2,1)S(1)}, u32[]{:S(2)}, u32[]{:S(2)}) collective-permute-start(bf16[2,128,256]{2,1,0:T(8,128)(2,1)S(1)} %get-tuple-element.75), channel_id=1, source_target_pairs={{0,4},{4,0},{8,12},{12,8},{16,20},{20,16},{24,28},{28,24},{1,5},{5... | collective-permute-start | bytes 393224 | tf_op jit(solution)/shard_map/ppermute | solution.py:766
  32.0 14.4 %collective-permute-start.15 = (bf16[528,256]{1,0:T(8,128)(2,1)S(1)}, bf16[528,256]{1,0:T(8,128)(2,1)S(1)}, u32[]{:S(2)}, u32[]{:S(2)}) collective-permute-start(bf16[528,256]{1,0:T(8,128)(2,1)S(1)} %get-tuple-element.84), channel_id=1, source_target_pairs={{0,16},{4,20},{8,24},{12,28},{16,0},{20,4},{24,8},{28,12},{1,17},{... | collective-permute-start | bytes 811016 | tf_op jit(solution)/shard_map/ppermute | solution.py:766
  33.5 12.9 %collective-permute-start.14 = (bf16[528,256]{1,0:T(8,128)(2,1)S(1)}, bf16[528,256]{1,0:T(8,128)(2,1)S(1)}, u32[]{:S(2)}, u32[]{:S(2)}) collective-permute-start(bf16[528,256]{1,0:T(8,128)(2,1)S(1)} %get-tuple-element.84), channel_id=1, source_target_pairs={{0,8},{4,12},{8,0},{12,4},{16,24},{20,28},{24,16},{28,20},{1,9},{5... | collective-permute-start | bytes 811016 | tf_op jit(solution)/shard_map/ppermute | solution.py:766
  34.6 11.8 %collective-permute-start.16 = (bf16[512,256]{1,0:T(8,128)(2,1)S(1)}, bf16[512,256]{1,0:T(8,128)(2,1)S(1)}, u32[]{:S(2)}, u32[]{:S(2)}) collective-permute-start(bf16[512,256]{1,0:T(8,128)(2,1)S(1)} %get-tuple-element.83.refs_0_), channel_id=1, source_target_pairs={{0,24},{4,28},{8,16},{12,20},{16,8},{20,12},{24,0},{28,4},{1,25},{... | collective-permute-start | bytes 786440 | tf_op jit(solution)/shard_map/ppermute | solution.py:766
  47.2 6.4 %collective-permute-start.23 = (bf16[2,512,128]{2,1,0:T(8,128)(2,1)S(1)}, bf16[2,512,128]{2,1,0:T(8,128)(2,1)S(1)}, u32[]{:S(2)}, u32[]{:S(2)}) collective-permute-start(bf16[2,512,128]{2,1,0:T(8,128)(2,1)S(1)} %get-tuple-element.99), channel_id=1, source_target_pairs={{0,1},{1,0},{2,3},{3,2},{4,5},{5,4},{6,7},{7,6},{8,9},{9,8},{10,11... | collective-permute-start | bytes 786440 | tf_op jit(solution)/shard_map/ppermute | solution.py:766
  49.8 7.2 %collective-permute-start.17 = (bf16[128,512]{1,0:T(8,128)(2,1)S(1)}, bf16[128,512]{1,0:T(8,128)(2,1)S(1)}, u32[]{:S(2)}, u32[]{:S(2)}) collective-permute-start(bf16[128,512]{1,0:T(8,128)(2,1)S(1)} %get-tuple-element.86), channel_id=1, source_target_pairs={{0,8},{4,12},{8,0},{12,4},{16,24},{20,28},{24,16},{28,20},{1,9},{5... | collective-permute-start | bytes 393224 | tf_op jit(solution)/shard_map/ppermute | solution.py:766
  51.0 5.9 %collective-permute-start.18 = (bf16[128,512]{1,0:T(8,128)(2,1)S(1)}, bf16[128,512]{1,0:T(8,128)(2,1)S(1)}, u32[]{:S(2)}, u32[]{:S(2)}) collective-permute-start(bf16[128,512]{1,0:T(8,128)(2,1)S(1)} %get-tuple-element.87), channel_id=1, source_target_pairs={{0,16},{4,20},{8,24},{12,28},{16,0},{20,4},{24,8},{28,12},{1,17},{... | collective-permute-start | bytes 393224 | tf_op jit(solution)/shard_map/ppermute | solution.py:766
  52.4 5.9 %collective-permute-start.19 = (bf16[128,512]{1,0:T(8,128)(2,1)S(1)}, bf16[128,512]{1,0:T(8,128)(2,1)S(1)}, u32[]{:S(2)}, u32[]{:S(2)}) collective-permute-start(bf16[128,512]{1,0:T(8,128)(2,1)S(1)} %get-tuple-element.88), channel_id=1, source_target_pairs={{0,24},{4,28},{8,16},{12,20},{16,8},{20,12},{24,0},{28,4},{1,25},{... | collective-permute-start | bytes 393224 | tf_op jit(solution)/shard_map/ppermute | solution.py:766
  53.7 6.8 %collective-permute-start.24 = (bf16[512,128]{1,0:T(8,128)(2,1)S(1)}, bf16[512,128]{1,0:T(8,128)(2,1)S(1)}, u32[]{:S(2)}, u32[]{:S(2)}) collective-permute-start(bf16[512,128]{1,0:T(8,128)(2,1)S(1)} %fusion.1), channel_id=1, source_target_pairs={{0,2},{1,3},{2,0},{3,1},{4,6},{5,7},{6,4},{7,5},{8,10},{9,11},{10,... | collective-permute-start | bytes 393224 | tf_op jit(solution)/shard_map/ppermute | solution.py:766
  58.3 10.9 %collective-permute-start.20 = (bf16[2,128,512]{2,1,0:T(8,128)(2,1)S(1)}, bf16[2,128,512]{2,1,0:T(8,128)(2,1)S(1)}, u32[]{:S(2)}, u32[]{:S(2)}) collective-permute-start(bf16[2,128,512]{2,1,0:T(8,128)(2,1)S(1)} %get-tuple-element.90), channel_id=1, source_target_pairs={{0,1},{1,0},{2,3},{3,2},{4,5},{5,4},{6,7},{7,6},{8,9},{9,8},{10,11... | collective-permute-start | bytes 786440 | tf_op jit(solution)/shard_map/ppermute | solution.py:766
  60.6 4.4 %collective-permute-start.25 = (bf16[272,128]{1,0:T(8,128)(2,1)S(1)}, bf16[272,128]{1,0:T(8,128)(2,1)S(1)}, u32[]{:S(2)}, u32[]{:S(2)}) collective-permute-start(bf16[272,128]{1,0:T(8,128)(2,1)S(1)} %get-tuple-element.102), channel_id=1, source_target_pairs={{0,8},{4,12},{8,0},{12,4},{16,24},{20,28},{24,16},{28,20},{1,9},{5... | collective-permute-start | bytes 208904 | tf_op jit(solution)/shard_map/ppermute | solution.py:766
  64.9 4.3 %collective-permute-start.26 = (bf16[272,128]{1,0:T(8,128)(2,1)S(1)}, bf16[272,128]{1,0:T(8,128)(2,1)S(1)}, u32[]{:S(2)}, u32[]{:S(2)}) collective-permute-start(bf16[272,128]{1,0:T(8,128)(2,1)S(1)} %relay.1), channel_id=1, source_target_pairs={{0,16},{4,20},{8,24},{12,28},{16,0},{20,4},{24,8},{28,12},{1,17},{... | collective-permute-start | bytes 208904 | tf_op jit(solution)/shard_map/ppermute | solution.py:766
  69.3 5.9 %collective-permute-start.27 = (bf16[128,512]{1,0:T(8,128)(2,1)S(1)}, bf16[128,512]{1,0:T(8,128)(2,1)S(1)}, u32[]{:S(2)}, u32[]{:S(2)}) collective-permute-start(bf16[128,512]{1,0:T(8,128)(2,1)S(1)} %fusion), channel_id=1, source_target_pairs={{0,2},{1,3},{2,0},{3,1},{4,6},{5,7},{6,4},{7,5},{8,10},{9,11},{10,... | collective-permute-start | bytes 393224 | tf_op jit(solution)/shard_map/ppermute | solution.py:766
  (10 other events, 67.6 us)

commit v15 on v14

--- a/solution.py
+++ b/solution.py
@@ -257,8 +257,8 @@
 
 def pack_values_kernel(chips, values_ref, *refs):
     out_refs, arrived = refs[:chips], refs[chips]
+    chip, _ = own_place()
     rows = values_ref.shape[0]
-    chip, _ = own_place()
     copies = []
     for offset, out_ref in enumerate(out_refs):
         values = values_ref.at[:, block_at(chip ^ offset, out_ref.shape[1])]
@@ -267,6 +267,10 @@
         copy.start()
     for copy in copies:
         copy.wait()
+    for out_ref in out_refs:
+        more = out_ref.shape[0] - rows
+        if more:
+            out_ref[pl.ds(rows, more), :] = out_ref[pl.ds(0, more), :]
 
 
 def pack_values(values_in, chips, spare):
@@ -275,7 +279,7 @@
         functools.partial(pack_values_kernel, chips),
         in_specs=[pl.BlockSpec(memory_space=pltpu.HBM)],
         out_specs=[WHOLE] * chips,
-        out_shape=[jax.ShapeDtypeStruct((rows + spare, width // chips), BF16)] * chips,
+        out_shape=[jax.ShapeDtypeStruct((rows + more, width // chips), BF16) for more in spare],
         scratch_shapes=[pltpu.SemaphoreType.DMA((chips,))],
         cost_estimate=CHEAP,
         compiler_params=pltpu.CompilerParams(vmem_limit_bytes=4 * 2**20),
@@ -335,7 +339,7 @@
 
 def stack_kernel(chips, *refs):
     in_refs, out_refs = refs[:chips], refs[chips:]
-    for offset, in_ref in enumerate(in_refs):
+    for offset, in_ref in enumerate(reversed(in_refs)):
         part, place = divmod(offset, chips // 2)
         out_refs[part][place] = in_ref[pl.ds(0, out_refs[part].shape[1]), :]
 
@@ -351,7 +355,7 @@
         cost_estimate=CHEAP,
         compiler_params=pltpu.CompilerParams(vmem_limit_bytes=4 * 2**20),
         name="stack",
-    )(*blocks)
+    )(*reversed(blocks))
 
 
 def forward_kernel(chips, cos_ref, sin_ref, table_ref, *refs):
@@ -794,7 +798,7 @@
     rows, width = values_in.shape
     tables = small_tables(parts, rows)
 
-    values = pack_values(values_in, chips, 0)
+    values = pack_values(values_in, chips, (0, 0, 0, 0))
     flat_filters = filter_spectrum.reshape(4, rows, width)
     near = pack_filters(after(flat_filters, values[0]), chips, (1, 2), 0)
     other_weight = swapped(out_weight, "seq", 1)
@@ -816,7 +820,7 @@
     above = swapped(relay(above, beside), "seq", 4)
     keep, passed, send = sort_blocks(to_chips(project_still(out_weight, other_weight, gathered)))
     first = swapped(send, "chan", 1)
-    passed = added(after(passed, above), first[1])
+    passed = added(passed, first[1])
     return join(keep, first, swapped(passed, "chan", 2), (own, beside, above), chips)
 
 

time: 76.3 us -> 76.6 us (level); the launches traced: 76 us -> 75.1 us
  waiting for transfers between devices: 32.8 us -> 31.8 us
    ppermute x28, waiting for transfers between devices: 32.8 us -> 31.8 us  [swapped(): lax.ppermute(value, axis, [(source, source ^ offset) for source in range(...]
  transfers between devices with their start and end apart: 28 -> 28, of which waited for: 15 -> 14; matrix products, arithmetic and copies ran while one was open for 0% -> 0% of each run, Pallas kernels for 13% -> 13%
where the time goes in v15:
time: 76.6 us; the launch traced here: 75.1 us
  waiting for transfers between devices  31.8 us (42%)
  starting transfers between devices  31.5 us (41%)
  Pallas kernels  11.6 us (15%)
    ppermute x28, waiting for transfers between devices, swapped(): lax.ppermute(value, axis, [(source, source ^ offset) for source in range(...  31.8 us
    ppermute x28, starting transfers between devices, swapped(): lax.ppermute(value, axis, [(source, source ^ offset) for source in range(...  31.5 us
    pallas_call x2, Pallas kernels, pack_filters(): pl.pallas_call(functools.partial(pack_filters_kernel, offsets), in_specs=...  2.73 us
    pallas_call x1, Pallas kernels, backward(): pl.pallas_call(functools.partial(backward_kernel, chips), in_specs=[WHOLE...  2.02 us
  transfers between devices with their start and end apart: 28, of which 14 were waited for; matrix products, arithmetic and copies ran while one was open for 0% of the time, Pallas kernels for 13%

profile of v15, /device:TPU:0, one launch (start us, length us, event | category | flops | bytes accessed | tf_op | source)
XLA Modules:
  0.0 75.1 jit_solution(5624999663004193288)
XLA Ops:
  1.4 2.6 %collective-permute-start.3 = (bf16[128,256]{1,0:T(8,128)(2,1)S(1)}, bf16[128,256]{1,0:T(8,128)(2,1)S(1)}, u32[]{:S(2)}, u32[]{:S(2)}) collective-permute-start(bf16[128,256]{1,0:T(8,128)(2,1)S(1)} %get-tuple-element.65), channel_id=1, source_target_pairs={{0,8},{4,12},{8,0},{12,4},{16,24},{20,28},{24,16},{28,20},{1,9},{5... | collective-permute-start | bytes 196616 | tf_op jit(solution)/shard_map/ppermute | solution.py:770
  4.0 1.4 %pack_filters.2 = (bf16[512,256]{1,0:T(8,128)(2,1)S(1)}, bf16[512,256]{1,0:T(8,128)(2,1)S(1)}) custom-call(f32[4,128,1024]{2,1,0:T(8,128)} %bitcast.13), custom_call_target="tpu_custom_call" | custom-call | tf_op jit(solution)/shard_map/pack_filters/pallas_call | solution.py:243
  5.4 1.6 %collective-permute-start.7 = (bf16[512,256]{1,0:T(8,128)(2,1)S(1)}, bf16[512,256]{1,0:T(8,128)(2,1)S(1)}, u32[]{:S(2)}, u32[]{:S(2)}) collective-permute-start(bf16[512,256]{1,0:T(8,128)(2,1)S(1)} %get-tuple-element.71), channel_id=1, source_target_pairs={{0,16},{4,20},{8,24},{12,28},{16,0},{20,4},{24,8},{28,12},{1,17},{... | collective-permute-start | bytes 786440 | tf_op jit(solution)/shard_map/ppermute | solution.py:770
  7.4 1.5 %collective-permute-start.1 = (bf16[128,256]{1,0:T(8,128)(2,1)S(1)}, bf16[128,256]{1,0:T(8,128)(2,1)S(1)}, u32[]{:S(2)}, u32[]{:S(2)}) collective-permute-start(bf16[128,256]{1,0:T(8,128)(2,1)S(1)} %get-tuple-element.54), channel_id=1, source_target_pairs={{0,24},{4,28},{8,16},{12,20},{16,8},{20,12},{24,0},{28,4},{1,25},{... | collective-permute-start | bytes 196616 | tf_op jit(solution)/shard_map/ppermute | solution.py:770
  9.0 1.6 %collective-permute-start.6 = (bf16[512,256]{1,0:T(8,128)(2,1)S(1)}, bf16[512,256]{1,0:T(8,128)(2,1)S(1)}, u32[]{:S(2)}, u32[]{:S(2)}) collective-permute-start(bf16[512,256]{1,0:T(8,128)(2,1)S(1)} %get-tuple-element.57), channel_id=1, source_target_pairs={{0,8},{4,12},{8,0},{12,4},{16,24},{20,28},{24,16},{28,20},{1,9},{5... | collective-permute-start | bytes 786440 | tf_op jit(solution)/shard_map/ppermute | solution.py:770
  10.5 1.4 %pack_filters.3 = (bf16[512,256]{1,0:T(8,128)(2,1)S(1)}, bf16[512,256]{1,0:T(8,128)(2,1)S(1)}) custom-call(f32[4,128,1024]{2,1,0:T(8,128)} %bitcast.14), custom_call_target="tpu_custom_call" | custom-call | tf_op jit(solution)/shard_map/pack_filters/pallas_call | solution.py:243
  13.3 3.7 %collective-permute-done.2.refs_1_.refs_2_ = bf16[128,256]{1,0:T(8,128)(2,1)S(1)} collective-permute-done((bf16[128,256]{1,0:T(8,128)(2,1)S(1)}, bf16[128,256]{1,0:T(8,128)(2,1)S(1)}, u32[]{:S(2)}, u32[]{:S(2)}) %collective-permute-start.2) | collective-permute-done | bytes 65568 | tf_op jit(solution)/shard_map/ppermute | solution.py:770
  18.7 1.5 %forward.1.spectrum_ref = f32[256,2048]{1,0:T(8,128)S(1)} custom-call(f32[2,128,8]{2,1,0:T(8,128)S(1)} %copy-done.2, f32[2,128,8]{2,1,0:T(8,128)S(1)} %copy-done.1, bf16[256,256]{1,0:T(8,128)(2,1)S(1)} %copy-done.4, bf16[2,128,256]{2,1,0:T(8,128)(2,1)S(1)} %get-tuple-element.68.refs_0_, bf16[2,128,256]{2,1,0:T(8,128)(2,1)S(1)} %get-tuple-element.69.refs_1_, ...), custom_call_target="tpu_custom_call" | custom-call | tf_op jit(solution)/shard_map/forward/pallas_call | solution.py:413
  20.3 1.7 %collective-permute-start.12 = (bf16[384,256]{1,0:T(8,128)(2,1)S(1)}, bf16[384,256]{1,0:T(8,128)(2,1)S(1)}, u32[]{:S(2)}, u32[]{:S(2)}) collective-permute-start(bf16[384,256]{1,0:T(8,128)(2,1)S(1)} %get-tuple-element.79), channel_id=1, source_target_pairs={{0,16},{4,20},{8,24},{12,28},{16,0},{20,4},{24,8},{28,12},{1,17},{... | collective-permute-start | bytes 589832 | tf_op jit(solution)/shard_map/ppermute | solution.py:770
  21.9 1.8 %collective-permute-start.13 = (bf16[384,256]{1,0:T(8,128)(2,1)S(1)}, bf16[384,256]{1,0:T(8,128)(2,1)S(1)}, u32[]{:S(2)}, u32[]{:S(2)}) collective-permute-start(bf16[384,256]{1,0:T(8,128)(2,1)S(1)} %get-tuple-element.81), channel_id=1, source_target_pairs={{0,24},{4,28},{8,16},{12,20},{16,8},{20,12},{24,0},{28,4},{1,25},{... | collective-permute-start | bytes 589832 | tf_op jit(solution)/shard_map/ppermute | solution.py:770
  23.7 2.0 %backward.1 = (f32[4,128,256]{2,1,0:T(8,128)S(1)}, bf16[2,128,256]{2,1,0:T(8,128)(2,1)S(1)}, bf16[2,128,256]{2,1,0:T(8,128)(2,1)S(1)}) custom-call(f32[2,128,8]{2,1,0:T(8,128)S(1)} %copy-done.2, f32[2,128,8]{2,1,0:T(8,128)S(1)} %copy-done.1, bf16[256,256]{1,0:T(8,128)(2,1)S(1)} %copy-done.3, f32[256,2048]{1,0:T(8,128)S(1)} %forward.1.spectrum_ref, ...), custom_call_target="tpu_custom_call" | custom-call | tf_op jit(solution)/shard_map/backward/pallas_call | solution.py:489
  26.3 1.6 %collective-permute-done.11.refs_5_.refs_0_ = bf16[384,256]{1,0:T(8,128)(2,1)S(1)} collective-permute-done((bf16[384,256]{1,0:T(8,128)(2,1)S(1)}, bf16[384,256]{1,0:T(8,128)(2,1)S(1)}, u32[]{:S(2)}, u32[]{:S(2)}) %collective-permute-start.11) | collective-permute-done | bytes 196640 | tf_op jit(solution)/shard_map/ppermute | solution.py:770
  28.0 4.6 %collective-permute-done.13.refs_7_.refs_2_ = bf16[384,256]{1,0:T(8,128)(2,1)S(1)} collective-permute-done((bf16[384,256]{1,0:T(8,128)(2,1)S(1)}, bf16[384,256]{1,0:T(8,128)(2,1)S(1)}, u32[]{:S(2)}, u32[]{:S(2)}) %collective-permute-start.13) | collective-permute-done | bytes 196640 | tf_op jit(solution)/shard_map/ppermute | solution.py:770
  33.5 1.8 %collective-permute-start.14 = (bf16[528,256]{1,0:T(8,128)(2,1)S(1)}, bf16[528,256]{1,0:T(8,128)(2,1)S(1)}, u32[]{:S(2)}, u32[]{:S(2)}) collective-permute-start(bf16[528,256]{1,0:T(8,128)(2,1)S(1)} %get-tuple-element.83), channel_id=1, source_target_pairs={{0,8},{4,12},{8,0},{12,4},{16,24},{20,28},{24,16},{28,20},{1,9},{5... | collective-permute-start | bytes 811016 | tf_op jit(solution)/shard_map/ppermute | solution.py:770
  38.4 9.2 %collective-permute-done.16.refs_3_ = bf16[512,256]{1,0:T(8,128)(2,1)S(1)} collective-permute-done((bf16[512,256]{1,0:T(8,128)(2,1)S(1)}, bf16[512,256]{1,0:T(8,128)(2,1)S(1)}, u32[]{:S(2)}, u32[]{:S(2)}) %collective-permute-start.16) | collective-permute-done | bytes 262176 | tf_op jit(solution)/shard_map/ppermute | solution.py:770
  48.4 1.6 %collective-permute-start.24 = (bf16[2,512,128]{2,1,0:T(8,128)(2,1)S(1)}, bf16[2,512,128]{2,1,0:T(8,128)(2,1)S(1)}, u32[]{:S(2)}, u32[]{:S(2)}) collective-permute-start(bf16[2,512,128]{2,1,0:T(8,128)(2,1)S(1)} %get-tuple-element.98), channel_id=1, source_target_pairs={{0,1},{1,0},{2,3},{3,2},{4,5},{5,4},{6,7},{7,6},{8,9},{9,8},{10,11... | collective-permute-start | bytes 786440 | tf_op jit(solution)/shard_map/ppermute | solution.py:770
  52.4 2.0 %collective-permute-start.19 = (bf16[128,512]{1,0:T(8,128)(2,1)S(1)}, bf16[128,512]{1,0:T(8,128)(2,1)S(1)}, u32[]{:S(2)}, u32[]{:S(2)}) collective-permute-start(bf16[128,512]{1,0:T(8,128)(2,1)S(1)} %get-tuple-element.87), channel_id=1, source_target_pairs={{0,24},{4,28},{8,16},{12,20},{16,8},{20,12},{24,0},{28,4},{1,25},{... | collective-permute-start | bytes 393224 | tf_op jit(solution)/shard_map/ppermute | solution.py:770
  54.4 1.5 %collective-permute-done.17.refs_1_ = bf16[128,512]{1,0:T(8,128)(2,1)S(1)} collective-permute-done((bf16[128,512]{1,0:T(8,128)(2,1)S(1)}, bf16[128,512]{1,0:T(8,128)(2,1)S(1)}, u32[]{:S(2)}, u32[]{:S(2)}) %collective-permute-start.17) | collective-permute-done | bytes 131104 | tf_op jit(solution)/shard_map/ppermute | solution.py:770
  56.4 1.9 %collective-permute-done.19.refs_3_ = bf16[128,512]{1,0:T(8,128)(2,1)S(1)} collective-permute-done((bf16[128,512]{1,0:T(8,128)(2,1)S(1)}, bf16[128,512]{1,0:T(8,128)(2,1)S(1)}, u32[]{:S(2)}, u32[]{:S(2)}) %collective-permute-start.19) | collective-permute-done | bytes 131104 | tf_op jit(solution)/shard_map/ppermute | solution.py:770
  58.9 2.7 %collective-permute-start.25 = (bf16[512,128]{1,0:T(8,128)(2,1)S(1)}, bf16[512,128]{1,0:T(8,128)(2,1)S(1)}, u32[]{:S(2)}, u32[]{:S(2)}) collective-permute-start(bf16[512,128]{1,0:T(8,128)(2,1)S(1)} %fusion), channel_id=1, source_target_pairs={{0,2},{1,3},{2,0},{3,1},{4,6},{5,7},{6,4},{7,5},{8,10},{9,11},{10,... | collective-permute-start | bytes 393224 | tf_op jit(solution)/shard_map/ppermute | solution.py:770
  61.6 3.5 %collective-permute-done.25.second_ref = bf16[512,128]{1,0:T(8,128)(2,1)S(1)} collective-permute-done((bf16[512,128]{1,0:T(8,128)(2,1)S(1)}, bf16[512,128]{1,0:T(8,128)(2,1)S(1)}, u32[]{:S(2)}, u32[]{:S(2)}) %collective-permute-start.25) | collective-permute-done | bytes 131104 | tf_op jit(solution)/shard_map/ppermute | solution.py:770
  65.1 2.5 %collective-permute-start.26 = (bf16[272,128]{1,0:T(8,128)(2,1)S(1)}, bf16[272,128]{1,0:T(8,128)(2,1)S(1)}, u32[]{:S(2)}, u32[]{:S(2)}) collective-permute-start(bf16[272,128]{1,0:T(8,128)(2,1)S(1)} %get-tuple-element.101), channel_id=1, source_target_pairs={{0,8},{4,12},{8,0},{12,4},{16,24},{20,28},{24,16},{28,20},{1,9},{5... | collective-permute-start | bytes 208904 | tf_op jit(solution)/shard_map/ppermute | solution.py:770
  67.7 2.3 %collective-permute-start.21 = (bf16[128,512]{1,0:T(8,128)(2,1)S(1)}, bf16[128,512]{1,0:T(8,128)(2,1)S(1)}, u32[]{:S(2)}, u32[]{:S(2)}) collective-permute-start(bf16[128,512]{1,0:T(8,128)(2,1)S(1)} %fusion.1), channel_id=1, source_target_pairs={{0,2},{1,3},{2,0},{3,1},{4,6},{5,7},{6,4},{7,5},{8,10},{9,11},{10,... | collective-permute-start | bytes 393224 | tf_op jit(solution)/shard_map/ppermute | solution.py:770
  71.2 2.4 %collective-permute-done.21.second_ref = bf16[128,512]{1,0:T(8,128)(2,1)S(1)} collective-permute-done((bf16[128,512]{1,0:T(8,128)(2,1)S(1)}, bf16[128,512]{1,0:T(8,128)(2,1)S(1)}, u32[]{:S(2)}, u32[]{:S(2)}) %collective-permute-start.21) | collective-permute-done | bytes 131104 | tf_op jit(solution)/shard_map/ppermute | solution.py:770
  (62 shorter events, 16.8 us)
Async XLA Ops:
  0.0 8.9 %collective-permute-start = (bf16[1024,512]{1,0:T(8,128)(2,1)}, bf16[1024,512]{1,0:T(8,128)(2,1)S(1)}, u32[]{:S(2)}, u32[]{:S(2)}) collective-permute-start(bf16[1024,512]{1,0:T(8,128)(2,1)} %own_ref.3), channel_id=1, source_target_pairs={{0,4},{4,0},{8,12},{12,8},{16,20},{20,16},{24,28},{28,24},{1,5},{5... | collective-permute-start | bytes 3145736 | tf_op jit(solution)/shard_map/ppermute | solution.py:770
  1.4 10.5 %collective-permute-start.3 = (bf16[128,256]{1,0:T(8,128)(2,1)S(1)}, bf16[128,256]{1,0:T(8,128)(2,1)S(1)}, u32[]{:S(2)}, u32[]{:S(2)}) collective-permute-start(bf16[128,256]{1,0:T(8,128)(2,1)S(1)} %get-tuple-element.65), channel_id=1, source_target_pairs={{0,8},{4,12},{8,0},{12,4},{16,24},{20,28},{24,16},{28,20},{1,9},{5... | collective-permute-start | bytes 196616 | tf_op jit(solution)/shard_map/ppermute | solution.py:770
  5.4 16.6 %collective-permute-start.7 = (bf16[512,256]{1,0:T(8,128)(2,1)S(1)}, bf16[512,256]{1,0:T(8,128)(2,1)S(1)}, u32[]{:S(2)}, u32[]{:S(2)}) collective-permute-start(bf16[512,256]{1,0:T(8,128)(2,1)S(1)} %get-tuple-element.71), channel_id=1, source_target_pairs={{0,16},{4,20},{8,24},{12,28},{16,0},{20,4},{24,8},{28,12},{1,17},{... | collective-permute-start | bytes 786440 | tf_op jit(solution)/shard_map/ppermute | solution.py:770
  6.9 10.1 %collective-permute-start.2 = (bf16[128,256]{1,0:T(8,128)(2,1)S(1)}, bf16[128,256]{1,0:T(8,128)(2,1)S(1)}, u32[]{:S(2)}, u32[]{:S(2)}) collective-permute-start(bf16[128,256]{1,0:T(8,128)(2,1)S(1)} %get-tuple-element.63), channel_id=1, source_target_pairs={{0,16},{4,20},{8,24},{12,28},{16,0},{20,4},{24,8},{28,12},{1,17},{... | collective-permute-start | bytes 196616 | tf_op jit(solution)/shard_map/ppermute | solution.py:770
  7.4 9.6 %collective-permute-start.1 = (bf16[128,256]{1,0:T(8,128)(2,1)S(1)}, bf16[128,256]{1,0:T(8,128)(2,1)S(1)}, u32[]{:S(2)}, u32[]{:S(2)}) collective-permute-start(bf16[128,256]{1,0:T(8,128)(2,1)S(1)} %get-tuple-element.54), channel_id=1, source_target_pairs={{0,24},{4,28},{8,16},{12,20},{16,8},{20,12},{24,0},{28,4},{1,25},{... | collective-permute-start | bytes 196616 | tf_op jit(solution)/shard_map/ppermute | solution.py:770
  9.0 14.8 %collective-permute-start.6 = (bf16[512,256]{1,0:T(8,128)(2,1)S(1)}, bf16[512,256]{1,0:T(8,128)(2,1)S(1)}, u32[]{:S(2)}, u32[]{:S(2)}) collective-permute-start(bf16[512,256]{1,0:T(8,128)(2,1)S(1)} %get-tuple-element.57), channel_id=1, source_target_pairs={{0,8},{4,12},{8,0},{12,4},{16,24},{20,28},{24,16},{28,20},{1,9},{5... | collective-permute-start | bytes 786440 | tf_op jit(solution)/shard_map/ppermute | solution.py:770
  11.9 11.8 %collective-permute-start.8 = (bf16[512,256]{1,0:T(8,128)(2,1)S(1)}, bf16[512,256]{1,0:T(8,128)(2,1)S(1)}, u32[]{:S(2)}, u32[]{:S(2)}) collective-permute-start(bf16[512,256]{1,0:T(8,128)(2,1)S(1)} %get-tuple-element.59), channel_id=1, source_target_pairs={{0,24},{4,28},{8,16},{12,20},{16,8},{20,12},{24,0},{28,4},{1,25},{... | collective-permute-start | bytes 786440 | tf_op jit(solution)/shard_map/ppermute | solution.py:770
  20.2 7.8 %collective-permute-start.11 = (bf16[384,256]{1,0:T(8,128)(2,1)S(1)}, bf16[384,256]{1,0:T(8,128)(2,1)S(1)}, u32[]{:S(2)}, u32[]{:S(2)}) collective-permute-start(bf16[384,256]{1,0:T(8,128)(2,1)S(1)} %get-tuple-element.77), channel_id=1, source_target_pairs={{0,8},{4,12},{8,0},{12,4},{16,24},{20,28},{24,16},{28,20},{1,9},{5... | collective-permute-start | bytes 589832 | tf_op jit(solution)/shard_map/ppermute | solution.py:770
  20.3 7.7 %collective-permute-start.12 = (bf16[384,256]{1,0:T(8,128)(2,1)S(1)}, bf16[384,256]{1,0:T(8,128)(2,1)S(1)}, u32[]{:S(2)}, u32[]{:S(2)}) collective-permute-start(bf16[384,256]{1,0:T(8,128)(2,1)S(1)} %get-tuple-element.79), channel_id=1, source_target_pairs={{0,16},{4,20},{8,24},{12,28},{16,0},{20,4},{24,8},{28,12},{1,17},{... | collective-permute-start | bytes 589832 | tf_op jit(solution)/shard_map/ppermute | solution.py:770
  21.9 10.6 %collective-permute-start.13 = (bf16[384,256]{1,0:T(8,128)(2,1)S(1)}, bf16[384,256]{1,0:T(8,128)(2,1)S(1)}, u32[]{:S(2)}, u32[]{:S(2)}) collective-permute-start(bf16[384,256]{1,0:T(8,128)(2,1)S(1)} %get-tuple-element.81), channel_id=1, source_target_pairs={{0,24},{4,28},{8,16},{12,20},{16,8},{20,12},{24,0},{28,4},{1,25},{... | collective-permute-start | bytes 589832 | tf_op jit(solution)/shard_map/ppermute | solution.py:770
  25.8 6.8 %collective-permute-start.9 = (bf16[2,128,256]{2,1,0:T(8,128)(2,1)S(1)}, bf16[2,128,256]{2,1,0:T(8,128)(2,1)S(1)}, u32[]{:S(2)}, u32[]{:S(2)}) collective-permute-start(bf16[2,128,256]{2,1,0:T(8,128)(2,1)S(1)} %get-tuple-element.73), channel_id=1, source_target_pairs={{0,4},{4,0},{8,12},{12,8},{16,20},{20,16},{24,28},{28,24},{1,5},{5... | collective-permute-start | bytes 393224 | tf_op jit(solution)/shard_map/ppermute | solution.py:770
  25.8 6.7 %collective-permute-start.10 = (bf16[2,128,256]{2,1,0:T(8,128)(2,1)S(1)}, bf16[2,128,256]{2,1,0:T(8,128)(2,1)S(1)}, u32[]{:S(2)}, u32[]{:S(2)}) collective-permute-start(bf16[2,128,256]{2,1,0:T(8,128)(2,1)S(1)} %get-tuple-element.74), channel_id=1, source_target_pairs={{0,4},{4,0},{8,12},{12,8},{16,20},{20,16},{24,28},{28,24},{1,5},{5... | collective-permute-start | bytes 393224 | tf_op jit(solution)/shard_map/ppermute | solution.py:770
  32.7 14.8 %collective-permute-start.15 = (bf16[528,256]{1,0:T(8,128)(2,1)S(1)}, bf16[528,256]{1,0:T(8,128)(2,1)S(1)}, u32[]{:S(2)}, u32[]{:S(2)}) collective-permute-start(bf16[528,256]{1,0:T(8,128)(2,1)S(1)} %get-tuple-element.83), channel_id=1, source_target_pairs={{0,16},{4,20},{8,24},{12,28},{16,0},{20,4},{24,8},{28,12},{1,17},{... | collective-permute-start | bytes 811016 | tf_op jit(solution)/shard_map/ppermute | solution.py:770
  33.5 14.0 %collective-permute-start.14 = (bf16[528,256]{1,0:T(8,128)(2,1)S(1)}, bf16[528,256]{1,0:T(8,128)(2,1)S(1)}, u32[]{:S(2)}, u32[]{:S(2)}) collective-permute-start(bf16[528,256]{1,0:T(8,128)(2,1)S(1)} %get-tuple-element.83), channel_id=1, source_target_pairs={{0,8},{4,12},{8,0},{12,4},{16,24},{20,28},{24,16},{28,20},{1,9},{5... | collective-permute-start | bytes 811016 | tf_op jit(solution)/shard_map/ppermute | solution.py:770
  35.3 12.2 %collective-permute-start.16 = (bf16[512,256]{1,0:T(8,128)(2,1)S(1)}, bf16[512,256]{1,0:T(8,128)(2,1)S(1)}, u32[]{:S(2)}, u32[]{:S(2)}) collective-permute-start(bf16[512,256]{1,0:T(8,128)(2,1)S(1)} %get-tuple-element.82.refs_0_), channel_id=1, source_target_pairs={{0,24},{4,28},{8,16},{12,20},{16,8},{20,12},{24,0},{28,4},{1,25},{... | collective-permute-start | bytes 786440 | tf_op jit(solution)/shard_map/ppermute | solution.py:770
  48.4 10.5 %collective-permute-start.24 = (bf16[2,512,128]{2,1,0:T(8,128)(2,1)S(1)}, bf16[2,512,128]{2,1,0:T(8,128)(2,1)S(1)}, u32[]{:S(2)}, u32[]{:S(2)}) collective-permute-start(bf16[2,512,128]{2,1,0:T(8,128)(2,1)S(1)} %get-tuple-element.98), channel_id=1, source_target_pairs={{0,1},{1,0},{2,3},{3,2},{4,5},{5,4},{6,7},{7,6},{8,9},{9,8},{10,11... | collective-permute-start | bytes 786440 | tf_op jit(solution)/shard_map/ppermute | solution.py:770
  50.9 5.0 %collective-permute-start.17 = (bf16[128,512]{1,0:T(8,128)(2,1)S(1)}, bf16[128,512]{1,0:T(8,128)(2,1)S(1)}, u32[]{:S(2)}, u32[]{:S(2)}) collective-permute-start(bf16[128,512]{1,0:T(8,128)(2,1)S(1)} %get-tuple-element.85), channel_id=1, source_target_pairs={{0,8},{4,12},{8,0},{12,4},{16,24},{20,28},{24,16},{28,20},{1,9},{5... | collective-permute-start | bytes 393224 | tf_op jit(solution)/shard_map/ppermute | solution.py:770
  51.4 5.0 %collective-permute-start.18 = (bf16[128,512]{1,0:T(8,128)(2,1)S(1)}, bf16[128,512]{1,0:T(8,128)(2,1)S(1)}, u32[]{:S(2)}, u32[]{:S(2)}) collective-permute-start(bf16[128,512]{1,0:T(8,128)(2,1)S(1)} %get-tuple-element.86), channel_id=1, source_target_pairs={{0,16},{4,20},{8,24},{12,28},{16,0},{20,4},{24,8},{28,12},{1,17},{... | collective-permute-start | bytes 393224 | tf_op jit(solution)/shard_map/ppermute | solution.py:770
  52.4 5.9 %collective-permute-start.19 = (bf16[128,512]{1,0:T(8,128)(2,1)S(1)}, bf16[128,512]{1,0:T(8,128)(2,1)S(1)}, u32[]{:S(2)}, u32[]{:S(2)}) collective-permute-start(bf16[128,512]{1,0:T(8,128)(2,1)S(1)} %get-tuple-element.87), channel_id=1, source_target_pairs={{0,24},{4,28},{8,16},{12,20},{16,8},{20,12},{24,0},{28,4},{1,25},{... | collective-permute-start | bytes 393224 | tf_op jit(solution)/shard_map/ppermute | solution.py:770
  58.4 9.2 %collective-permute-start.20 = (bf16[2,128,512]{2,1,0:T(8,128)(2,1)S(1)}, bf16[2,128,512]{2,1,0:T(8,128)(2,1)S(1)}, u32[]{:S(2)}, u32[]{:S(2)}) collective-permute-start(bf16[2,128,512]{2,1,0:T(8,128)(2,1)S(1)} %get-tuple-element.89), channel_id=1, source_target_pairs={{0,1},{1,0},{2,3},{3,2},{4,5},{5,4},{6,7},{7,6},{8,9},{9,8},{10,11... | collective-permute-start | bytes 786440 | tf_op jit(solution)/shard_map/ppermute | solution.py:770
  58.9 6.1 %collective-permute-start.25 = (bf16[512,128]{1,0:T(8,128)(2,1)S(1)}, bf16[512,128]{1,0:T(8,128)(2,1)S(1)}, u32[]{:S(2)}, u32[]{:S(2)}) collective-permute-start(bf16[512,128]{1,0:T(8,128)(2,1)S(1)} %fusion), channel_id=1, source_target_pairs={{0,2},{1,3},{2,0},{3,1},{4,6},{5,7},{6,4},{7,5},{8,10},{9,11},{10,... | collective-permute-start | bytes 393224 | tf_op jit(solution)/shard_map/ppermute | solution.py:770
  65.1 4.8 %collective-permute-start.26 = (bf16[272,128]{1,0:T(8,128)(2,1)S(1)}, bf16[272,128]{1,0:T(8,128)(2,1)S(1)}, u32[]{:S(2)}, u32[]{:S(2)}) collective-permute-start(bf16[272,128]{1,0:T(8,128)(2,1)S(1)} %get-tuple-element.101), channel_id=1, source_target_pairs={{0,8},{4,12},{8,0},{12,4},{16,24},{20,28},{24,16},{28,20},{1,9},{5... | collective-permute-start | bytes 208904 | tf_op jit(solution)/shard_map/ppermute | solution.py:770
  67.7 5.9 %collective-permute-start.21 = (bf16[128,512]{1,0:T(8,128)(2,1)S(1)}, bf16[128,512]{1,0:T(8,128)(2,1)S(1)}, u32[]{:S(2)}, u32[]{:S(2)}) collective-permute-start(bf16[128,512]{1,0:T(8,128)(2,1)S(1)} %fusion.1), channel_id=1, source_target_pairs={{0,2},{1,3},{2,0},{3,1},{4,6},{5,7},{6,4},{7,5},{8,10},{9,11},{10,... | collective-permute-start | bytes 393224 | tf_op jit(solution)/shard_map/ppermute | solution.py:770
  70.0 4.4 %collective-permute-start.27 = (bf16[272,128]{1,0:T(8,128)(2,1)S(1)}, bf16[272,128]{1,0:T(8,128)(2,1)S(1)}, u32[]{:S(2)}, u32[]{:S(2)}) collective-permute-start(bf16[272,128]{1,0:T(8,128)(2,1)S(1)} %relay.1), channel_id=1, source_target_pairs={{0,16},{4,20},{8,24},{12,28},{16,0},{20,4},{24,8},{28,12},{1,17},{... | collective-permute-start | bytes 208904 | tf_op jit(solution)/shard_map/ppermute | solution.py:770
  (10 other events, 70.0 us)

commit v16 on v15

--- a/solution.py
+++ b/solution.py
@@ -339,7 +339,7 @@
 
 def stack_kernel(chips, *refs):
     in_refs, out_refs = refs[:chips], refs[chips:]
-    for offset, in_ref in enumerate(reversed(in_refs)):
+    for offset, in_ref in enumerate(in_refs):
         part, place = divmod(offset, chips // 2)
         out_refs[part][place] = in_ref[pl.ds(0, out_refs[part].shape[1]), :]
 
@@ -355,7 +355,7 @@
         cost_estimate=CHEAP,
         compiler_params=pltpu.CompilerParams(vmem_limit_bytes=4 * 2**20),
         name="stack",
-    )(*reversed(blocks))
+    )(*blocks)
 
 
 def forward_kernel(chips, cos_ref, sin_ref, table_ref, *refs):

time: 76.6 us -> 77.3 us (level)
  the two profiles are of different devices: /device:TPU:0 before, /device:TPU:24 now
where the time goes in v16:
time: 77.3 us; the launch traced here: 77 us
  waiting for transfers between devices  41.4 us (54%)
  starting transfers between devices  23.8 us (31%)
  Pallas kernels  11.6 us (15%)
    ppermute x28, waiting for transfers between devices, swapped(): lax.ppermute(value, axis, [(source, source ^ offset) for source in range(...  41.4 us
    ppermute x28, starting transfers between devices, swapped(): lax.ppermute(value, axis, [(source, source ^ offset) for source in range(...  23.8 us
    pallas_call x2, Pallas kernels, pack_filters(): pl.pallas_call(functools.partial(pack_filters_kernel, offsets), in_specs=...  2.73 us
    pallas_call x1, Pallas kernels, backward(): pl.pallas_call(functools.partial(backward_kernel, chips), in_specs=[WHOLE...  2.01 us
  transfers between devices with their start and end apart: 28, of which 16 were waited for; matrix products, arithmetic and copies ran while one was open for 0% of the time, Pallas kernels for 13%

profile of v16, /device:TPU:24, one launch (start us, length us, event | category | flops | bytes accessed | tf_op | source)
XLA Modules:
  0.0 77.0 jit_solution(2203579811844304191)
XLA Ops:
  1.0 2.5 %collective-permute-start.3 = (bf16[128,256]{1,0:T(8,128)(2,1)S(1)}, bf16[128,256]{1,0:T(8,128)(2,1)S(1)}, u32[]{:S(2)}, u32[]{:S(2)}) collective-permute-start(bf16[128,256]{1,0:T(8,128)(2,1)S(1)} %get-tuple-element.66), channel_id=1, source_target_pairs={{0,24},{4,28},{8,16},{12,20},{16,8},{20,12},{24,0},{28,4},{1,25},{... | collective-permute-start | bytes 196616 | tf_op jit(solution)/shard_map/ppermute | solution.py:770
  3.5 1.4 %pack_filters.2 = (bf16[512,256]{1,0:T(8,128)(2,1)S(1)}, bf16[512,256]{1,0:T(8,128)(2,1)S(1)}) custom-call(f32[4,128,1024]{2,1,0:T(8,128)} %bitcast.13), custom_call_target="tpu_custom_call" | custom-call | tf_op jit(solution)/shard_map/pack_filters/pallas_call | solution.py:243
  5.4 1.5 %collective-permute-start.2 = (bf16[128,256]{1,0:T(8,128)(2,1)S(1)}, bf16[128,256]{1,0:T(8,128)(2,1)S(1)}, u32[]{:S(2)}, u32[]{:S(2)}) collective-permute-start(bf16[128,256]{1,0:T(8,128)(2,1)S(1)} %get-tuple-element.64), channel_id=1, source_target_pairs={{0,16},{4,20},{8,24},{12,28},{16,0},{20,4},{24,8},{28,12},{1,17},{... | collective-permute-start | bytes 196616 | tf_op jit(solution)/shard_map/ppermute | solution.py:770
  7.5 1.6 %collective-permute-start.6 = (bf16[512,256]{1,0:T(8,128)(2,1)S(1)}, bf16[512,256]{1,0:T(8,128)(2,1)S(1)}, u32[]{:S(2)}, u32[]{:S(2)}) collective-permute-start(bf16[512,256]{1,0:T(8,128)(2,1)S(1)} %get-tuple-element.56), channel_id=1, source_target_pairs={{0,8},{4,12},{8,0},{12,4},{16,24},{20,28},{24,16},{28,20},{1,9},{5... | collective-permute-start | bytes 786440 | tf_op jit(solution)/shard_map/ppermute | solution.py:770
  9.1 1.4 %pack_filters.3 = (bf16[512,256]{1,0:T(8,128)(2,1)S(1)}, bf16[512,256]{1,0:T(8,128)(2,1)S(1)}) custom-call(f32[4,128,1024]{2,1,0:T(8,128)} %bitcast.14), custom_call_target="tpu_custom_call" | custom-call | tf_op jit(solution)/shard_map/pack_filters/pallas_call | solution.py:243
  11.0 1.3 %pack_moved.1 = (bf16[128,256]{1,0:T(8,128)(2,1)S(1)}, bf16[384,256]{1,0:T(8,128)(2,1)S(1)}, bf16[384,256]{1,0:T(8,128)(2,1)S(1)}, bf16[384,256]{1,0:T(8,128)(2,1)S(1)}, bf16[1024,128]{1,0:T(8,128)(2,1)S(1)}) custom-call(bf16[128,1024]{1,0:T(8,128)(2,1)} %gate_ref, bf16[1024,512]{1,0:T(8,128)(2,1)} %own_ref.3, ...), custom_call_target="tpu_custom_call" | custom-call | tf_op jit(solution)/shard_map/pack_moved/pallas_call | solution.py:325
  12.3 2.5 %collective-permute-done.2.refs_2_ = bf16[128,256]{1,0:T(8,128)(2,1)S(1)} collective-permute-done((bf16[128,256]{1,0:T(8,128)(2,1)S(1)}, bf16[128,256]{1,0:T(8,128)(2,1)S(1)}, u32[]{:S(2)}, u32[]{:S(2)}) %collective-permute-start.2) | collective-permute-done | bytes 65568 | tf_op jit(solution)/shard_map/ppermute | solution.py:770
  16.4 1.5 %forward.1.spectrum_ref = f32[256,2048]{1,0:T(8,128)S(1)} custom-call(f32[2,128,8]{2,1,0:T(8,128)S(1)} %copy-done.2, f32[2,128,8]{2,1,0:T(8,128)S(1)} %copy-done.1, bf16[256,256]{1,0:T(8,128)(2,1)S(1)} %copy-done.4, bf16[2,128,256]{2,1,0:T(8,128)(2,1)S(1)} %get-tuple-element.68.refs_0_, bf16[2,128,256]{2,1,0:T(8,128)(2,1)S(1)} %get-tuple-element.69.refs_1_, ...), custom_call_target="tpu_custom_call" | custom-call | tf_op jit(solution)/shard_map/forward/pallas_call | solution.py:413
  19.7 1.8 %collective-permute-start.13 = (bf16[384,256]{1,0:T(8,128)(2,1)S(1)}, bf16[384,256]{1,0:T(8,128)(2,1)S(1)}, u32[]{:S(2)}, u32[]{:S(2)}) collective-permute-start(bf16[384,256]{1,0:T(8,128)(2,1)S(1)} %get-tuple-element.81), channel_id=1, source_target_pairs={{0,24},{4,28},{8,16},{12,20},{16,8},{20,12},{24,0},{28,4},{1,25},{... | collective-permute-start | bytes 589832 | tf_op jit(solution)/shard_map/ppermute | solution.py:770
  21.5 1.2 %collective-permute-done.8.refs_3_ = bf16[512,256]{1,0:T(8,128)(2,1)S(1)} collective-permute-done((bf16[512,256]{1,0:T(8,128)(2,1)S(1)}, bf16[512,256]{1,0:T(8,128)(2,1)S(1)}, u32[]{:S(2)}, u32[]{:S(2)}) %collective-permute-start.8) | collective-permute-done | bytes 262176 | tf_op jit(solution)/shard_map/ppermute | solution.py:770
  22.7 2.0 %backward.1 = (f32[4,128,256]{2,1,0:T(8,128)S(1)}, bf16[2,128,256]{2,1,0:T(8,128)(2,1)S(1)}, bf16[2,128,256]{2,1,0:T(8,128)(2,1)S(1)}) custom-call(f32[2,128,8]{2,1,0:T(8,128)S(1)} %copy-done.2, f32[2,128,8]{2,1,0:T(8,128)S(1)} %copy-done.1, bf16[256,256]{1,0:T(8,128)(2,1)S(1)} %copy-done.3, f32[256,2048]{1,0:T(8,128)S(1)} %forward.1.spectrum_ref, ...), custom_call_target="tpu_custom_call" | custom-call | tf_op jit(solution)/shard_map/backward/pallas_call | solution.py:489
  25.3 1.7 %collective-permute-done.11.refs_5_.refs_0_ = bf16[384,256]{1,0:T(8,128)(2,1)S(1)} collective-permute-done((bf16[384,256]{1,0:T(8,128)(2,1)S(1)}, bf16[384,256]{1,0:T(8,128)(2,1)S(1)}, u32[]{:S(2)}, u32[]{:S(2)}) %collective-permute-start.11) | collective-permute-done | bytes 196640 | tf_op jit(solution)/shard_map/ppermute | solution.py:770
  27.0 3.4 %collective-permute-done.12.refs_6_.refs_1_ = bf16[384,256]{1,0:T(8,128)(2,1)S(1)} collective-permute-done((bf16[384,256]{1,0:T(8,128)(2,1)S(1)}, bf16[384,256]{1,0:T(8,128)(2,1)S(1)}, u32[]{:S(2)}, u32[]{:S(2)}) %collective-permute-start.12) | collective-permute-done | bytes 196640 | tf_op jit(solution)/shard_map/ppermute | solution.py:770
  30.6 1.5 %collective-permute-start.15 = (bf16[528,256]{1,0:T(8,128)(2,1)S(1)}, bf16[528,256]{1,0:T(8,128)(2,1)S(1)}, u32[]{:S(2)}, u32[]{:S(2)}) collective-permute-start(bf16[528,256]{1,0:T(8,128)(2,1)S(1)} %get-tuple-element.83), channel_id=1, source_target_pairs={{0,16},{4,20},{8,24},{12,28},{16,0},{20,4},{24,8},{28,12},{1,17},{... | collective-permute-start | bytes 811016 | tf_op jit(solution)/shard_map/ppermute | solution.py:770
  36.2 8.8 %collective-permute-done.16.refs_3_ = bf16[512,256]{1,0:T(8,128)(2,1)S(1)} collective-permute-done((bf16[512,256]{1,0:T(8,128)(2,1)S(1)}, bf16[512,256]{1,0:T(8,128)(2,1)S(1)}, u32[]{:S(2)}, u32[]{:S(2)}) %collective-permute-start.16) | collective-permute-done | bytes 262176 | tf_op jit(solution)/shard_map/ppermute | solution.py:770
  47.2 1.3 %collective-permute-start.17 = (bf16[128,512]{1,0:T(8,128)(2,1)S(1)}, bf16[128,512]{1,0:T(8,128)(2,1)S(1)}, u32[]{:S(2)}, u32[]{:S(2)}) collective-permute-start(bf16[128,512]{1,0:T(8,128)(2,1)S(1)} %get-tuple-element.85), channel_id=1, source_target_pairs={{0,8},{4,12},{8,0},{12,4},{16,24},{20,28},{24,16},{28,20},{1,9},{5... | collective-permute-start | bytes 393224 | tf_op jit(solution)/shard_map/ppermute | solution.py:770
  48.5 1.4 %collective-permute-start.18 = (bf16[128,512]{1,0:T(8,128)(2,1)S(1)}, bf16[128,512]{1,0:T(8,128)(2,1)S(1)}, u32[]{:S(2)}, u32[]{:S(2)}) collective-permute-start(bf16[128,512]{1,0:T(8,128)(2,1)S(1)} %get-tuple-element.86), channel_id=1, source_target_pairs={{0,16},{4,20},{8,24},{12,28},{16,0},{20,4},{24,8},{28,12},{1,17},{... | collective-permute-start | bytes 393224 | tf_op jit(solution)/shard_map/ppermute | solution.py:770
  50.7 1.7 %collective-permute-done.17.refs_1_ = bf16[128,512]{1,0:T(8,128)(2,1)S(1)} collective-permute-done((bf16[128,512]{1,0:T(8,128)(2,1)S(1)}, bf16[128,512]{1,0:T(8,128)(2,1)S(1)}, u32[]{:S(2)}, u32[]{:S(2)}) %collective-permute-start.17) | collective-permute-done | bytes 131104 | tf_op jit(solution)/shard_map/ppermute | solution.py:770
  53.4 2.2 %collective-permute-done.19.refs_3_ = bf16[128,512]{1,0:T(8,128)(2,1)S(1)} collective-permute-done((bf16[128,512]{1,0:T(8,128)(2,1)S(1)}, bf16[128,512]{1,0:T(8,128)(2,1)S(1)}, u32[]{:S(2)}, u32[]{:S(2)}) %collective-permute-start.19) | collective-permute-done | bytes 131104 | tf_op jit(solution)/shard_map/ppermute | solution.py:770
  55.8 1.6 %collective-permute-start.20 = (bf16[2,128,512]{2,1,0:T(8,128)(2,1)S(1)}, bf16[2,128,512]{2,1,0:T(8,128)(2,1)S(1)}, u32[]{:S(2)}, u32[]{:S(2)}) collective-permute-start(bf16[2,128,512]{2,1,0:T(8,128)(2,1)S(1)} %get-tuple-element.89), channel_id=1, source_target_pairs={{0,1},{1,0},{2,3},{3,2},{4,5},{5,4},{6,7},{7,6},{8,9},{9,8},{10,11... | collective-permute-start | bytes 786440 | tf_op jit(solution)/shard_map/ppermute | solution.py:770
  57.9 9.6 %collective-permute-done.25.second_ref = bf16[512,128]{1,0:T(8,128)(2,1)S(1)} collective-permute-done((bf16[512,128]{1,0:T(8,128)(2,1)S(1)}, bf16[512,128]{1,0:T(8,128)(2,1)S(1)}, u32[]{:S(2)}, u32[]{:S(2)}) %collective-permute-start.25) | collective-permute-done | bytes 131104 | tf_op jit(solution)/shard_map/ppermute | solution.py:770
  68.7 3.2 %collective-permute-done.26.arrived_ref.beside_ref = bf16[272,128]{1,0:T(8,128)(2,1)S(1)} collective-permute-done((bf16[272,128]{1,0:T(8,128)(2,1)S(1)}, bf16[272,128]{1,0:T(8,128)(2,1)S(1)}, u32[]{:S(2)}, u32[]{:S(2)}) %collective-permute-start.26) | collective-permute-done | bytes 69664 | tf_op jit(solution)/shard_map/ppermute | solution.py:770
  72.5 2.1 %collective-permute-done.21.second_ref = bf16[128,512]{1,0:T(8,128)(2,1)S(1)} collective-permute-done((bf16[128,512]{1,0:T(8,128)(2,1)S(1)}, bf16[128,512]{1,0:T(8,128)(2,1)S(1)}, u32[]{:S(2)}, u32[]{:S(2)}) %collective-permute-start.21) | collective-permute-done | bytes 131104 | tf_op jit(solution)/shard_map/ppermute | solution.py:770
  74.5 1.7 %collective-permute-done.27.above_ref = bf16[272,128]{1,0:T(8,128)(2,1)S(1)} collective-permute-done((bf16[272,128]{1,0:T(8,128)(2,1)S(1)}, bf16[272,128]{1,0:T(8,128)(2,1)S(1)}, u32[]{:S(2)}, u32[]{:S(2)}) %collective-permute-start.27) | collective-permute-done | bytes 69664 | tf_op jit(solution)/shard_map/ppermute | solution.py:770
  (62 shorter events, 18.2 us)
Async XLA Ops:
  0.0 7.5 %collective-permute-start = (bf16[1024,512]{1,0:T(8,128)(2,1)}, bf16[1024,512]{1,0:T(8,128)(2,1)S(1)}, u32[]{:S(2)}, u32[]{:S(2)}) collective-permute-start(bf16[1024,512]{1,0:T(8,128)(2,1)} %own_ref.3), channel_id=1, source_target_pairs={{0,4},{4,0},{8,12},{12,8},{16,20},{20,16},{24,28},{28,24},{1,5},{5... | collective-permute-start | bytes 3145736 | tf_op jit(solution)/shard_map/ppermute | solution.py:770
  1.0 9.5 %collective-permute-start.3 = (bf16[128,256]{1,0:T(8,128)(2,1)S(1)}, bf16[128,256]{1,0:T(8,128)(2,1)S(1)}, u32[]{:S(2)}, u32[]{:S(2)}) collective-permute-start(bf16[128,256]{1,0:T(8,128)(2,1)S(1)} %get-tuple-element.66), channel_id=1, source_target_pairs={{0,24},{4,28},{8,16},{12,20},{16,8},{20,12},{24,0},{28,4},{1,25},{... | collective-permute-start | bytes 196616 | tf_op jit(solution)/shard_map/ppermute | solution.py:770
  4.9 14.8 %collective-permute-start.7 = (bf16[512,256]{1,0:T(8,128)(2,1)S(1)}, bf16[512,256]{1,0:T(8,128)(2,1)S(1)}, u32[]{:S(2)}, u32[]{:S(2)}) collective-permute-start(bf16[512,256]{1,0:T(8,128)(2,1)S(1)} %get-tuple-element.71), channel_id=1, source_target_pairs={{0,16},{4,20},{8,24},{12,28},{16,0},{20,4},{24,8},{28,12},{1,17},{... | collective-permute-start | bytes 786440 | tf_op jit(solution)/shard_map/ppermute | solution.py:770
  5.4 9.3 %collective-permute-start.2 = (bf16[128,256]{1,0:T(8,128)(2,1)S(1)}, bf16[128,256]{1,0:T(8,128)(2,1)S(1)}, u32[]{:S(2)}, u32[]{:S(2)}) collective-permute-start(bf16[128,256]{1,0:T(8,128)(2,1)S(1)} %get-tuple-element.64), channel_id=1, source_target_pairs={{0,16},{4,20},{8,24},{12,28},{16,0},{20,4},{24,8},{28,12},{1,17},{... | collective-permute-start | bytes 196616 | tf_op jit(solution)/shard_map/ppermute | solution.py:770
  7.0 7.8 %collective-permute-start.1 = (bf16[128,256]{1,0:T(8,128)(2,1)S(1)}, bf16[128,256]{1,0:T(8,128)(2,1)S(1)}, u32[]{:S(2)}, u32[]{:S(2)}) collective-permute-start(bf16[128,256]{1,0:T(8,128)(2,1)S(1)} %get-tuple-element.62), channel_id=1, source_target_pairs={{0,8},{4,12},{8,0},{12,4},{16,24},{20,28},{24,16},{28,20},{1,9},{5... | collective-permute-start | bytes 196616 | tf_op jit(solution)/shard_map/ppermute | solution.py:770
  7.5 14.0 %collective-permute-start.6 = (bf16[512,256]{1,0:T(8,128)(2,1)S(1)}, bf16[512,256]{1,0:T(8,128)(2,1)S(1)}, u32[]{:S(2)}, u32[]{:S(2)}) collective-permute-start(bf16[512,256]{1,0:T(8,128)(2,1)S(1)} %get-tuple-element.56), channel_id=1, source_target_pairs={{0,8},{4,12},{8,0},{12,4},{16,24},{20,28},{24,16},{28,20},{1,9},{5... | collective-permute-start | bytes 786440 | tf_op jit(solution)/shard_map/ppermute | solution.py:770
  10.4 12.3 %collective-permute-start.8 = (bf16[512,256]{1,0:T(8,128)(2,1)S(1)}, bf16[512,256]{1,0:T(8,128)(2,1)S(1)}, u32[]{:S(2)}, u32[]{:S(2)}) collective-permute-start(bf16[512,256]{1,0:T(8,128)(2,1)S(1)} %get-tuple-element.58), channel_id=1, source_target_pairs={{0,24},{4,28},{8,16},{12,20},{16,8},{20,12},{24,0},{28,4},{1,25},{... | collective-permute-start | bytes 786440 | tf_op jit(solution)/shard_map/ppermute | solution.py:770
  17.9 9.1 %collective-permute-start.11 = (bf16[384,256]{1,0:T(8,128)(2,1)S(1)}, bf16[384,256]{1,0:T(8,128)(2,1)S(1)}, u32[]{:S(2)}, u32[]{:S(2)}) collective-permute-start(bf16[384,256]{1,0:T(8,128)(2,1)S(1)} %get-tuple-element.77), channel_id=1, source_target_pairs={{0,8},{4,12},{8,0},{12,4},{16,24},{20,28},{24,16},{28,20},{1,9},{5... | collective-permute-start | bytes 589832 | tf_op jit(solution)/shard_map/ppermute | solution.py:770
  18.5 11.8 %collective-permute-start.12 = (bf16[384,256]{1,0:T(8,128)(2,1)S(1)}, bf16[384,256]{1,0:T(8,128)(2,1)S(1)}, u32[]{:S(2)}, u32[]{:S(2)}) collective-permute-start(bf16[384,256]{1,0:T(8,128)(2,1)S(1)} %get-tuple-element.79), channel_id=1, source_target_pairs={{0,16},{4,20},{8,24},{12,28},{16,0},{20,4},{24,8},{28,12},{1,17},{... | collective-permute-start | bytes 589832 | tf_op jit(solution)/shard_map/ppermute | solution.py:770
  19.7 10.7 %collective-permute-start.13 = (bf16[384,256]{1,0:T(8,128)(2,1)S(1)}, bf16[384,256]{1,0:T(8,128)(2,1)S(1)}, u32[]{:S(2)}, u32[]{:S(2)}) collective-permute-start(bf16[384,256]{1,0:T(8,128)(2,1)S(1)} %get-tuple-element.81), channel_id=1, source_target_pairs={{0,24},{4,28},{8,16},{12,20},{16,8},{20,12},{24,0},{28,4},{1,25},{... | collective-permute-start | bytes 589832 | tf_op jit(solution)/shard_map/ppermute | solution.py:770
  24.7 5.6 %collective-permute-start.9 = (bf16[2,128,256]{2,1,0:T(8,128)(2,1)S(1)}, bf16[2,128,256]{2,1,0:T(8,128)(2,1)S(1)}, u32[]{:S(2)}, u32[]{:S(2)}) collective-permute-start(bf16[2,128,256]{2,1,0:T(8,128)(2,1)S(1)} %get-tuple-element.73), channel_id=1, source_target_pairs={{0,4},{4,0},{8,12},{12,8},{16,20},{20,16},{24,28},{28,24},{1,5},{5... | collective-permute-start | bytes 393224 | tf_op jit(solution)/shard_map/ppermute | solution.py:770
  24.8 5.6 %collective-permute-start.10 = (bf16[2,128,256]{2,1,0:T(8,128)(2,1)S(1)}, bf16[2,128,256]{2,1,0:T(8,128)(2,1)S(1)}, u32[]{:S(2)}, u32[]{:S(2)}) collective-permute-start(bf16[2,128,256]{2,1,0:T(8,128)(2,1)S(1)} %get-tuple-element.74), channel_id=1, source_target_pairs={{0,4},{4,0},{8,12},{12,8},{16,20},{20,16},{24,28},{28,24},{1,5},{5... | collective-permute-start | bytes 393224 | tf_op jit(solution)/shard_map/ppermute | solution.py:770
  30.6 14.4 %collective-permute-start.15 = (bf16[528,256]{1,0:T(8,128)(2,1)S(1)}, bf16[528,256]{1,0:T(8,128)(2,1)S(1)}, u32[]{:S(2)}, u32[]{:S(2)}) collective-permute-start(bf16[528,256]{1,0:T(8,128)(2,1)S(1)} %get-tuple-element.83), channel_id=1, source_target_pairs={{0,16},{4,20},{8,24},{12,28},{16,0},{20,4},{24,8},{28,12},{1,17},{... | collective-permute-start | bytes 811016 | tf_op jit(solution)/shard_map/ppermute | solution.py:770
  32.0 12.9 %collective-permute-start.14 = (bf16[528,256]{1,0:T(8,128)(2,1)S(1)}, bf16[528,256]{1,0:T(8,128)(2,1)S(1)}, u32[]{:S(2)}, u32[]{:S(2)}) collective-permute-start(bf16[528,256]{1,0:T(8,128)(2,1)S(1)} %get-tuple-element.83), channel_id=1, source_target_pairs={{0,8},{4,12},{8,0},{12,4},{16,24},{20,28},{24,16},{28,20},{1,9},{5... | collective-permute-start | bytes 811016 | tf_op jit(solution)/shard_map/ppermute | solution.py:770
  33.1 11.8 %collective-permute-start.16 = (bf16[512,256]{1,0:T(8,128)(2,1)S(1)}, bf16[512,256]{1,0:T(8,128)(2,1)S(1)}, u32[]{:S(2)}, u32[]{:S(2)}) collective-permute-start(bf16[512,256]{1,0:T(8,128)(2,1)S(1)} %get-tuple-element.82.refs_0_), channel_id=1, source_target_pairs={{0,24},{4,28},{8,16},{12,20},{16,8},{20,12},{24,0},{28,4},{1,25},{... | collective-permute-start | bytes 786440 | tf_op jit(solution)/shard_map/ppermute | solution.py:770
  45.8 11.6 %collective-permute-start.24 = (bf16[2,512,128]{2,1,0:T(8,128)(2,1)S(1)}, bf16[2,512,128]{2,1,0:T(8,128)(2,1)S(1)}, u32[]{:S(2)}, u32[]{:S(2)}) collective-permute-start(bf16[2,512,128]{2,1,0:T(8,128)(2,1)S(1)} %get-tuple-element.98), channel_id=1, source_target_pairs={{0,1},{1,0},{2,3},{3,2},{4,5},{5,4},{6,7},{7,6},{8,9},{9,8},{10,11... | collective-permute-start | bytes 786440 | tf_op jit(solution)/shard_map/ppermute | solution.py:770
  47.2 5.2 %collective-permute-start.17 = (bf16[128,512]{1,0:T(8,128)(2,1)S(1)}, bf16[128,512]{1,0:T(8,128)(2,1)S(1)}, u32[]{:S(2)}, u32[]{:S(2)}) collective-permute-start(bf16[128,512]{1,0:T(8,128)(2,1)S(1)} %get-tuple-element.85), channel_id=1, source_target_pairs={{0,8},{4,12},{8,0},{12,4},{16,24},{20,28},{24,16},{28,20},{1,9},{5... | collective-permute-start | bytes 393224 | tf_op jit(solution)/shard_map/ppermute | solution.py:770
  48.5 5.0 %collective-permute-start.18 = (bf16[128,512]{1,0:T(8,128)(2,1)S(1)}, bf16[128,512]{1,0:T(8,128)(2,1)S(1)}, u32[]{:S(2)}, u32[]{:S(2)}) collective-permute-start(bf16[128,512]{1,0:T(8,128)(2,1)S(1)} %get-tuple-element.86), channel_id=1, source_target_pairs={{0,16},{4,20},{8,24},{12,28},{16,0},{20,4},{24,8},{28,12},{1,17},{... | collective-permute-start | bytes 393224 | tf_op jit(solution)/shard_map/ppermute | solution.py:770
  49.8 5.9 %collective-permute-start.19 = (bf16[128,512]{1,0:T(8,128)(2,1)S(1)}, bf16[128,512]{1,0:T(8,128)(2,1)S(1)}, u32[]{:S(2)}, u32[]{:S(2)}) collective-permute-start(bf16[128,512]{1,0:T(8,128)(2,1)S(1)} %get-tuple-element.87), channel_id=1, source_target_pairs={{0,24},{4,28},{8,16},{12,20},{16,8},{20,12},{24,0},{28,4},{1,25},{... | collective-permute-start | bytes 393224 | tf_op jit(solution)/shard_map/ppermute | solution.py:770
  55.8 12.8 %collective-permute-start.20 = (bf16[2,128,512]{2,1,0:T(8,128)(2,1)S(1)}, bf16[2,128,512]{2,1,0:T(8,128)(2,1)S(1)}, u32[]{:S(2)}, u32[]{:S(2)}) collective-permute-start(bf16[2,128,512]{2,1,0:T(8,128)(2,1)S(1)} %get-tuple-element.89), channel_id=1, source_target_pairs={{0,1},{1,0},{2,3},{3,2},{4,5},{5,4},{6,7},{7,6},{8,9},{9,8},{10,11... | collective-permute-start | bytes 786440 | tf_op jit(solution)/shard_map/ppermute | solution.py:770
  57.5 10.0 %collective-permute-start.25 = (bf16[512,128]{1,0:T(8,128)(2,1)S(1)}, bf16[512,128]{1,0:T(8,128)(2,1)S(1)}, u32[]{:S(2)}, u32[]{:S(2)}) collective-permute-start(bf16[512,128]{1,0:T(8,128)(2,1)S(1)} %fusion), channel_id=1, source_target_pairs={{0,2},{1,3},{2,0},{3,1},{4,6},{5,7},{6,4},{7,5},{8,10},{9,11},{10,... | collective-permute-start | bytes 393224 | tf_op jit(solution)/shard_map/ppermute | solution.py:770
  67.5 4.4 %collective-permute-start.26 = (bf16[272,128]{1,0:T(8,128)(2,1)S(1)}, bf16[272,128]{1,0:T(8,128)(2,1)S(1)}, u32[]{:S(2)}, u32[]{:S(2)}) collective-permute-start(bf16[272,128]{1,0:T(8,128)(2,1)S(1)} %get-tuple-element.101), channel_id=1, source_target_pairs={{0,8},{4,12},{8,0},{12,4},{16,24},{20,28},{24,16},{28,20},{1,9},{5... | collective-permute-start | bytes 208904 | tf_op jit(solution)/shard_map/ppermute | solution.py:770
  68.6 5.9 %collective-permute-start.21 = (bf16[128,512]{1,0:T(8,128)(2,1)S(1)}, bf16[128,512]{1,0:T(8,128)(2,1)S(1)}, u32[]{:S(2)}, u32[]{:S(2)}) collective-permute-start(bf16[128,512]{1,0:T(8,128)(2,1)S(1)} %fusion.1), channel_id=1, source_target_pairs={{0,2},{1,3},{2,0},{3,1},{4,6},{5,7},{6,4},{7,5},{8,10},{9,11},{10,... | collective-permute-start | bytes 393224 | tf_op jit(solution)/shard_map/ppermute | solution.py:770
  71.9 4.3 %collective-permute-start.27 = (bf16[272,128]{1,0:T(8,128)(2,1)S(1)}, bf16[272,128]{1,0:T(8,128)(2,1)S(1)}, u32[]{:S(2)}, u32[]{:S(2)}) collective-permute-start(bf16[272,128]{1,0:T(8,128)(2,1)S(1)} %relay.1), channel_id=1, source_target_pairs={{0,16},{4,20},{8,24},{12,28},{16,0},{20,4},{24,8},{28,12},{1,17},{... | collective-permute-start | bytes 208904 | tf_op jit(solution)/shard_map/ppermute | solution.py:770
  (10 other events, 66.1 us)

commit v17 on v13

--- a/solution.py
+++ b/solution.py
@@ -418,16 +418,16 @@
     )(cos, sin, table, *own, *other)
 
 
-def backward_kernel(chips, cos_ref, sin_ref, table_ref, spectrum_ref, *refs):
+def backward_kernel(chips, offsets, cos_ref, sin_ref, table_ref, spectrum_ref, *refs):
     filter_refs, (keep_ref, *send_refs, filter_ref, product_ref, back_ref) = refs[:chips], refs[chips:]
     chip, core = own_place()
     parts = 2 * chips
     rows, lanes = keep_ref.shape[1:]
     chip_bits = chips.bit_length() - 1
     chunk, width = 16, 128
-    for offset in range(chips):
+    for offset, ref in zip(offsets, filter_refs):
         for plane in range(filter_ref.shape[1]):
-            filter_ref[chip ^ offset, plane] = filter_refs[offset][pl.ds(plane * rows, rows), :]
+            filter_ref[chip ^ offset, plane] = ref[pl.ds(plane * rows, rows), :]
 
     for residue in range(parts):
         source, odd = bit_reversed(residue // 2, chip_bits), residue % 2
@@ -477,13 +477,14 @@
     lax.fori_loop(0, rows // chunk, gather, 0)
 
 
-def backward(spectrum, first, tables):
-    chips = len(first)
+def backward(spectrum, filters, offsets, tables):
+    chips = len(filters)
+    first = [filters[offset] for offset in offsets]
     rows, lanes = spectrum.shape[0] // 2, first[0].shape[1]
     _, table, cos, sin = tables
     half = jax.ShapeDtypeStruct((chips // 2, rows, lanes), BF16)
     return pl.pallas_call(
-        functools.partial(backward_kernel, chips),
+        functools.partial(backward_kernel, chips, offsets),
         in_specs=[WHOLE] * (4 + chips),
         out_specs=[WHOLE] * 3,
         out_shape=[jax.ShapeDtypeStruct((chips, rows, lanes), F32), half, half],
@@ -763,15 +764,17 @@
 
     values = pack_values(values_in, chips, 0)
     flat_filters = filter_spectrum.reshape(4, rows, width)
-    near = pack_filters(after(flat_filters, values[0]), chips, (1, 2), 0)
+    early = pack_filters(after(flat_filters, values[0]), chips, (3,), 0)
     other_weight = swapped(out_weight, "seq", 1)
-    *moved, mine = pack_moved(after(gate_values, near[0]), out_weight, other_weight, chips)
-    own, far = pack_filters(after(flat_filters, moved[0]), chips, (0, 3), 0)
-    values, filters = to_chips(values), to_chips([own, *near, far])
-    own = stack([after(block, far) for block in values], rows)
+    late = pack_filters(after(flat_filters, early[0], other_weight), chips, (1, 2), 0)
+    packed = dict(zip((3, 1, 2), (*early, *late)))
+    *moved, mine = pack_moved(after(gate_values, late[0]), out_weight, other_weight, chips)
+    (packed[0],) = pack_filters(after(flat_filters, moved[0]), chips, (0,), 0)
+    values, filters = to_chips(values), to_chips([packed[offset] for offset in range(chips)])
+    own = stack([after(block, packed[0]) for block in values], rows)
     spectrum = forward(own, [swapped(part, "seq", 1) for part in own], tables)
     moved = to_chips([after(block, spectrum) for block in moved])
-    keep, *send = backward(spectrum, filters, tables)
+    keep, *send = backward(spectrum, filters, (0, 1, 3, 2), tables)
     gated, longer = gate(skip_gain[None, :], keep, [swapped(part, "seq", 1) for part in send], values, moved, 16)
     gathered = to_chips([gated, longer, longer, gated])
 

time: 76.3 us -> 77.6 us (1.017)
  Pallas kernels: 11.6 us -> 12.5 us
    pallas_call x2 -> x3, Pallas kernels: 2.74 us -> 3.65 us  [pack_filters(): pl.pallas_call(functools.partial(pack_filters_kernel, offsets), in_specs=...]
  transfers between devices with their start and end apart: 29 -> 29, of which waited for: 16 -> 16; matrix products, arithmetic and copies ran while one was open for 0% -> 0% of each run, Pallas kernels for 13% -> 14%
where the time goes in v17:
time: 77.6 us; the launch traced here: 77.3 us
  waiting for transfers between devices  33.3 us (43%)
  starting transfers between devices  31.2 us (40%)
  Pallas kernels  12.5 us (16%)
    ppermute x29, waiting for transfers between devices, swapped(): lax.ppermute(value, axis, [(source, source ^ offset) for source in range(...  33.3 us
    ppermute x29, starting transfers between devices, swapped(): lax.ppermute(value, axis, [(source, source ^ offset) for source in range(...  31.2 us
    pallas_call x3, Pallas kernels, pack_filters(): pl.pallas_call(functools.partial(pack_filters_kernel, offsets), in_specs=...  3.65 us
    pallas_call x1, Pallas kernels, backward(): pl.pallas_call(functools.partial(backward_kernel, chips, offsets), in_spe...  2.02 us
  transfers between devices with their start and end apart: 29, of which 16 were waited for; matrix products, arithmetic and copies ran while one was open for 0% of the time, Pallas kernels for 14%

profile of v17, /device:TPU:0, one launch (start us, length us, event | category | flops | bytes accessed | tf_op | source)
XLA Modules:
  0.0 77.3 jit_solution(17632900647354972222)
XLA Ops:
  1.4 3.5 %collective-permute-start.3 = (bf16[128,256]{1,0:T(8,128)(2,1)S(1)}, bf16[128,256]{1,0:T(8,128)(2,1)S(1)}, u32[]{:S(2)}, u32[]{:S(2)}) collective-permute-start(bf16[128,256]{1,0:T(8,128)(2,1)S(1)} %get-tuple-element.66), channel_id=1, source_target_pairs={{0,24},{4,28},{8,16},{12,20},{16,8},{20,12},{24,0},{28,4},{1,25},{... | collective-permute-start | bytes 196616 | tf_op jit(solution)/shard_map/ppermute | solution.py:742
  6.2 2.0 %collective-permute-start.2 = (bf16[128,256]{1,0:T(8,128)(2,1)S(1)}, bf16[128,256]{1,0:T(8,128)(2,1)S(1)}, u32[]{:S(2)}, u32[]{:S(2)}) collective-permute-start(bf16[128,256]{1,0:T(8,128)(2,1)S(1)} %get-tuple-element.64), channel_id=1, source_target_pairs={{0,16},{4,20},{8,24},{12,28},{16,0},{20,4},{24,8},{28,12},{1,17},{... | collective-permute-start | bytes 196616 | tf_op jit(solution)/shard_map/ppermute | solution.py:742
  8.2 1.5 %collective-permute-start.1 = (bf16[128,256]{1,0:T(8,128)(2,1)S(1)}, bf16[128,256]{1,0:T(8,128)(2,1)S(1)}, u32[]{:S(2)}, u32[]{:S(2)}) collective-permute-start(bf16[128,256]{1,0:T(8,128)(2,1)S(1)} %get-tuple-element.62), channel_id=1, source_target_pairs={{0,8},{4,12},{8,0},{12,4},{16,24},{20,28},{24,16},{28,20},{1,9},{5... | collective-permute-start | bytes 196616 | tf_op jit(solution)/shard_map/ppermute | solution.py:742
  9.6 1.4 %pack_filters.4 = (bf16[512,256]{1,0:T(8,128)(2,1)S(1)}, bf16[512,256]{1,0:T(8,128)(2,1)S(1)}) custom-call(f32[4,128,1024]{2,1,0:T(8,128)} %bitcast.14), custom_call_target="tpu_custom_call" | custom-call | tf_op jit(solution)/shard_map/pack_filters/pallas_call | solution.py:243
  14.3 2.4 %collective-permute-done.2.refs_2_ = bf16[128,256]{1,0:T(8,128)(2,1)S(1)} collective-permute-done((bf16[128,256]{1,0:T(8,128)(2,1)S(1)}, bf16[128,256]{1,0:T(8,128)(2,1)S(1)}, u32[]{:S(2)}, u32[]{:S(2)}) %collective-permute-start.2) | collective-permute-done | bytes 65568 | tf_op jit(solution)/shard_map/ppermute | solution.py:742
  18.3 1.5 %forward.1.spectrum_ref = f32[256,2048]{1,0:T(8,128)S(1)} custom-call(f32[2,128,8]{2,1,0:T(8,128)S(1)} %copy-done.2, f32[2,128,8]{2,1,0:T(8,128)S(1)} %copy-done.1, bf16[256,256]{1,0:T(8,128)(2,1)S(1)} %copy-done.4, bf16[2,128,256]{2,1,0:T(8,128)(2,1)S(1)} %get-tuple-element.68.refs_0_, bf16[2,128,256]{2,1,0:T(8,128)(2,1)S(1)} %get-tuple-element.69.refs_1_, ...), custom_call_target="tpu_custom_call" | custom-call | tf_op jit(solution)/shard_map/forward/pallas_call | solution.py:409
  21.9 1.4 %collective-permute-start.13 = (bf16[384,256]{1,0:T(8,128)(2,1)S(1)}, bf16[384,256]{1,0:T(8,128)(2,1)S(1)}, u32[]{:S(2)}, u32[]{:S(2)}) collective-permute-start(bf16[384,256]{1,0:T(8,128)(2,1)S(1)} %get-tuple-element.80), channel_id=1, source_target_pairs={{0,24},{4,28},{8,16},{12,20},{16,8},{20,12},{24,0},{28,4},{1,25},{... | collective-permute-start | bytes 589832 | tf_op jit(solution)/shard_map/ppermute | solution.py:742
  23.4 2.0 %backward.1 = (f32[4,128,256]{2,1,0:T(8,128)S(1)}, bf16[2,128,256]{2,1,0:T(8,128)(2,1)S(1)}, bf16[2,128,256]{2,1,0:T(8,128)(2,1)S(1)}) custom-call(f32[2,128,8]{2,1,0:T(8,128)S(1)} %copy-done.2, f32[2,128,8]{2,1,0:T(8,128)S(1)} %copy-done.1, bf16[256,256]{1,0:T(8,128)(2,1)S(1)} %copy-done.3, f32[256,2048]{1,0:T(8,128)S(1)} %forward.1.spectrum_ref, ...), custom_call_target="tpu_custom_call" | custom-call | tf_op jit(solution)/shard_map/backward/pallas_call | solution.py:486
  26.0 1.6 %collective-permute-done.11.refs_5_.refs_0_ = bf16[384,256]{1,0:T(8,128)(2,1)S(1)} collective-permute-done((bf16[384,256]{1,0:T(8,128)(2,1)S(1)}, bf16[384,256]{1,0:T(8,128)(2,1)S(1)}, u32[]{:S(2)}, u32[]{:S(2)}) %collective-permute-start.11) | collective-permute-done | bytes 196640 | tf_op jit(solution)/shard_map/ppermute | solution.py:742
  27.6 2.9 %collective-permute-done.12.refs_6_.refs_1_ = bf16[384,256]{1,0:T(8,128)(2,1)S(1)} collective-permute-done((bf16[384,256]{1,0:T(8,128)(2,1)S(1)}, bf16[384,256]{1,0:T(8,128)(2,1)S(1)}, u32[]{:S(2)}, u32[]{:S(2)}) %collective-permute-start.12) | collective-permute-done | bytes 196640 | tf_op jit(solution)/shard_map/ppermute | solution.py:742
  30.5 1.6 %collective-permute-done.13.refs_7_.refs_2_ = bf16[384,256]{1,0:T(8,128)(2,1)S(1)} collective-permute-done((bf16[384,256]{1,0:T(8,128)(2,1)S(1)}, bf16[384,256]{1,0:T(8,128)(2,1)S(1)}, u32[]{:S(2)}, u32[]{:S(2)}) %collective-permute-start.13) | collective-permute-done | bytes 196640 | tf_op jit(solution)/shard_map/ppermute | solution.py:742
  33.3 1.5 %collective-permute-start.14 = (bf16[528,256]{1,0:T(8,128)(2,1)S(1)}, bf16[528,256]{1,0:T(8,128)(2,1)S(1)}, u32[]{:S(2)}, u32[]{:S(2)}) collective-permute-start(bf16[528,256]{1,0:T(8,128)(2,1)S(1)} %get-tuple-element.82), channel_id=1, source_target_pairs={{0,8},{4,12},{8,0},{12,4},{16,24},{20,28},{24,16},{28,20},{1,9},{5... | collective-permute-start | bytes 811016 | tf_op jit(solution)/shard_map/ppermute | solution.py:742
  38.0 9.2 %collective-permute-done.16.refs_3_ = bf16[512,256]{1,0:T(8,128)(2,1)S(1)} collective-permute-done((bf16[512,256]{1,0:T(8,128)(2,1)S(1)}, bf16[512,256]{1,0:T(8,128)(2,1)S(1)}, u32[]{:S(2)}, u32[]{:S(2)}) %collective-permute-start.16) | collective-permute-done | bytes 262176 | tf_op jit(solution)/shard_map/ppermute | solution.py:742
  48.0 1.6 %collective-permute-start.24 = (bf16[2,512,128]{2,1,0:T(8,128)(2,1)S(1)}, bf16[2,512,128]{2,1,0:T(8,128)(2,1)S(1)}, u32[]{:S(2)}, u32[]{:S(2)}) collective-permute-start(bf16[2,512,128]{2,1,0:T(8,128)(2,1)S(1)} %get-tuple-element.97), channel_id=1, source_target_pairs={{0,1},{1,0},{2,3},{3,2},{4,5},{5,4},{6,7},{7,6},{8,9},{9,8},{10,11... | collective-permute-start | bytes 786440 | tf_op jit(solution)/shard_map/ppermute | solution.py:742
  52.0 2.1 %collective-permute-start.19 = (bf16[128,512]{1,0:T(8,128)(2,1)S(1)}, bf16[128,512]{1,0:T(8,128)(2,1)S(1)}, u32[]{:S(2)}, u32[]{:S(2)}) collective-permute-start(bf16[128,512]{1,0:T(8,128)(2,1)S(1)} %get-tuple-element.86), channel_id=1, source_target_pairs={{0,24},{4,28},{8,16},{12,20},{16,8},{20,12},{24,0},{28,4},{1,25},{... | collective-permute-start | bytes 393224 | tf_op jit(solution)/shard_map/ppermute | solution.py:742
  54.1 1.5 %collective-permute-done.17.refs_1_ = bf16[128,512]{1,0:T(8,128)(2,1)S(1)} collective-permute-done((bf16[128,512]{1,0:T(8,128)(2,1)S(1)}, bf16[128,512]{1,0:T(8,128)(2,1)S(1)}, u32[]{:S(2)}, u32[]{:S(2)}) %collective-permute-start.17) | collective-permute-done | bytes 131104 | tf_op jit(solution)/shard_map/ppermute | solution.py:742
  56.1 1.7 %collective-permute-done.19.refs_3_ = bf16[128,512]{1,0:T(8,128)(2,1)S(1)} collective-permute-done((bf16[128,512]{1,0:T(8,128)(2,1)S(1)}, bf16[128,512]{1,0:T(8,128)(2,1)S(1)}, u32[]{:S(2)}, u32[]{:S(2)}) %collective-permute-start.19) | collective-permute-done | bytes 131104 | tf_op jit(solution)/shard_map/ppermute | solution.py:742
  58.5 2.7 %collective-permute-start.25 = (bf16[512,128]{1,0:T(8,128)(2,1)S(1)}, bf16[512,128]{1,0:T(8,128)(2,1)S(1)}, u32[]{:S(2)}, u32[]{:S(2)}) collective-permute-start(bf16[512,128]{1,0:T(8,128)(2,1)S(1)} %fusion), channel_id=1, source_target_pairs={{0,2},{1,3},{2,0},{3,1},{4,6},{5,7},{6,4},{7,5},{8,10},{9,11},{10,... | collective-permute-start | bytes 393224 | tf_op jit(solution)/shard_map/ppermute | solution.py:742
  61.2 5.1 %collective-permute-done.20.first_ref = bf16[2,128,512]{2,1,0:T(8,128)(2,1)S(1)} collective-permute-done((bf16[2,128,512]{2,1,0:T(8,128)(2,1)S(1)}, bf16[2,128,512]{2,1,0:T(8,128)(2,1)S(1)}, u32[]{:S(2)}, u32[]{:S(2)}) %collective-permute-start.20) | collective-permute-done | bytes 262176 | tf_op jit(solution)/shard_map/ppermute | solution.py:742
  66.2 2.2 %collective-permute-start.21 = (bf16[128,512]{1,0:T(8,128)(2,1)S(1)}, bf16[128,512]{1,0:T(8,128)(2,1)S(1)}, u32[]{:S(2)}, u32[]{:S(2)}) collective-permute-start(bf16[128,512]{1,0:T(8,128)(2,1)S(1)} %fusion.1), channel_id=1, source_target_pairs={{0,2},{1,3},{2,0},{3,1},{4,6},{5,7},{6,4},{7,5},{8,10},{9,11},{10,... | collective-permute-start | bytes 393224 | tf_op jit(solution)/shard_map/ppermute | solution.py:742
  68.5 1.4 %collective-permute-start.26 = (bf16[128,128]{1,0:T(8,128)(2,1)S(1)}, bf16[128,128]{1,0:T(8,128)(2,1)S(1)}, u32[]{:S(2)}, u32[]{:S(2)}) collective-permute-start(bf16[128,128]{1,0:T(8,128)(2,1)S(1)} %get-tuple-element.100), channel_id=1, source_target_pairs={{0,8},{4,12},{8,0},{12,4},{16,24},{20,28},{24,16},{28,20},{1,9},{5... | collective-permute-start | bytes 98312 | tf_op jit(solution)/shard_map/ppermute | solution.py:742
  69.9 1.8 %collective-permute-start.27 = (bf16[128,128]{1,0:T(8,128)(2,1)S(1)}, bf16[128,128]{1,0:T(8,128)(2,1)S(1)}, u32[]{:S(2)}, u32[]{:S(2)}) collective-permute-start(bf16[128,128]{1,0:T(8,128)(2,1)S(1)} %get-tuple-element.101), channel_id=1, source_target_pairs={{0,16},{4,20},{8,24},{12,28},{16,0},{20,4},{24,8},{28,12},{1,17},{... | collective-permute-start | bytes 98312 | tf_op jit(solution)/shard_map/ppermute | solution.py:742
  72.5 1.3 %collective-permute-done.27.refs_2_ = bf16[128,128]{1,0:T(8,128)(2,1)S(1)} collective-permute-done((bf16[128,128]{1,0:T(8,128)(2,1)S(1)}, bf16[128,128]{1,0:T(8,128)(2,1)S(1)}, u32[]{:S(2)}, u32[]{:S(2)}) %collective-permute-start.27) | collective-permute-done | bytes 32800 | tf_op jit(solution)/shard_map/ppermute | solution.py:742
  73.8 2.7 %collective-permute-done.28.refs_3_ = bf16[128,128]{1,0:T(8,128)(2,1)S(1)} collective-permute-done((bf16[128,128]{1,0:T(8,128)(2,1)S(1)}, bf16[128,128]{1,0:T(8,128)(2,1)S(1)}, u32[]{:S(2)}, u32[]{:S(2)}) %collective-permute-start.28) | collective-permute-done | bytes 32800 | tf_op jit(solution)/shard_map/ppermute | solution.py:742
  (64 shorter events, 20.6 us)
Async XLA Ops:
  0.0 9.6 %collective-permute-start = (bf16[1024,512]{1,0:T(8,128)(2,1)}, bf16[1024,512]{1,0:T(8,128)(2,1)S(1)}, u32[]{:S(2)}, u32[]{:S(2)}) collective-permute-start(bf16[1024,512]{1,0:T(8,128)(2,1)} %own_ref.3), channel_id=1, source_target_pairs={{0,4},{4,0},{8,12},{12,8},{16,20},{20,16},{24,28},{28,24},{1,5},{5... | collective-permute-start | bytes 3145736 | tf_op jit(solution)/shard_map/ppermute | solution.py:742
  1.4 10.2 %collective-permute-start.3 = (bf16[128,256]{1,0:T(8,128)(2,1)S(1)}, bf16[128,256]{1,0:T(8,128)(2,1)S(1)}, u32[]{:S(2)}, u32[]{:S(2)}) collective-permute-start(bf16[128,256]{1,0:T(8,128)(2,1)S(1)} %get-tuple-element.66), channel_id=1, source_target_pairs={{0,24},{4,28},{8,16},{12,20},{16,8},{20,12},{24,0},{28,4},{1,25},{... | collective-permute-start | bytes 196616 | tf_op jit(solution)/shard_map/ppermute | solution.py:742
  6.1 15.8 %collective-permute-start.7 = (bf16[512,256]{1,0:T(8,128)(2,1)S(1)}, bf16[512,256]{1,0:T(8,128)(2,1)S(1)}, u32[]{:S(2)}, u32[]{:S(2)}) collective-permute-start(bf16[512,256]{1,0:T(8,128)(2,1)S(1)} %pack_filters.3), channel_id=1, source_target_pairs={{0,24},{4,28},{8,16},{12,20},{16,8},{20,12},{24,0},{28,4},{1,25},{... | collective-permute-start | bytes 786440 | tf_op jit(solution)/shard_map/ppermute | solution.py:742
  6.2 10.5 %collective-permute-start.2 = (bf16[128,256]{1,0:T(8,128)(2,1)S(1)}, bf16[128,256]{1,0:T(8,128)(2,1)S(1)}, u32[]{:S(2)}, u32[]{:S(2)}) collective-permute-start(bf16[128,256]{1,0:T(8,128)(2,1)S(1)} %get-tuple-element.64), channel_id=1, source_target_pairs={{0,16},{4,20},{8,24},{12,28},{16,0},{20,4},{24,8},{28,12},{1,17},{... | collective-permute-start | bytes 196616 | tf_op jit(solution)/shard_map/ppermute | solution.py:742
  8.2 8.5 %collective-permute-start.1 = (bf16[128,256]{1,0:T(8,128)(2,1)S(1)}, bf16[128,256]{1,0:T(8,128)(2,1)S(1)}, u32[]{:S(2)}, u32[]{:S(2)}) collective-permute-start(bf16[128,256]{1,0:T(8,128)(2,1)S(1)} %get-tuple-element.62), channel_id=1, source_target_pairs={{0,8},{4,12},{8,0},{12,4},{16,24},{20,28},{24,16},{28,20},{1,9},{5... | collective-permute-start | bytes 196616 | tf_op jit(solution)/shard_map/ppermute | solution.py:742
  11.0 12.4 %collective-permute-start.8 = (bf16[512,256]{1,0:T(8,128)(2,1)S(1)}, bf16[512,256]{1,0:T(8,128)(2,1)S(1)}, u32[]{:S(2)}, u32[]{:S(2)}) collective-permute-start(bf16[512,256]{1,0:T(8,128)(2,1)S(1)} %get-tuple-element.70), channel_id=1, source_target_pairs={{0,16},{4,20},{8,24},{12,28},{16,0},{20,4},{24,8},{28,12},{1,17},{... | collective-permute-start | bytes 786440 | tf_op jit(solution)/shard_map/ppermute | solution.py:742
  11.6 11.8 %collective-permute-start.6 = (bf16[512,256]{1,0:T(8,128)(2,1)S(1)}, bf16[512,256]{1,0:T(8,128)(2,1)S(1)}, u32[]{:S(2)}, u32[]{:S(2)}) collective-permute-start(bf16[512,256]{1,0:T(8,128)(2,1)S(1)} %get-tuple-element.57), channel_id=1, source_target_pairs={{0,8},{4,12},{8,0},{12,4},{16,24},{20,28},{24,16},{28,20},{1,9},{5... | collective-permute-start | bytes 786440 | tf_op jit(solution)/shard_map/ppermute | solution.py:742
  19.8 7.8 %collective-permute-start.11 = (bf16[384,256]{1,0:T(8,128)(2,1)S(1)}, bf16[384,256]{1,0:T(8,128)(2,1)S(1)}, u32[]{:S(2)}, u32[]{:S(2)}) collective-permute-start(bf16[384,256]{1,0:T(8,128)(2,1)S(1)} %get-tuple-element.76), channel_id=1, source_target_pairs={{0,8},{4,12},{8,0},{12,4},{16,24},{20,28},{24,16},{28,20},{1,9},{5... | collective-permute-start | bytes 589832 | tf_op jit(solution)/shard_map/ppermute | solution.py:742
  20.7 9.8 %collective-permute-start.12 = (bf16[384,256]{1,0:T(8,128)(2,1)S(1)}, bf16[384,256]{1,0:T(8,128)(2,1)S(1)}, u32[]{:S(2)}, u32[]{:S(2)}) collective-permute-start(bf16[384,256]{1,0:T(8,128)(2,1)S(1)} %get-tuple-element.78), channel_id=1, source_target_pairs={{0,16},{4,20},{8,24},{12,28},{16,0},{20,4},{24,8},{28,12},{1,17},{... | collective-permute-start | bytes 589832 | tf_op jit(solution)/shard_map/ppermute | solution.py:742
  21.9 10.2 %collective-permute-start.13 = (bf16[384,256]{1,0:T(8,128)(2,1)S(1)}, bf16[384,256]{1,0:T(8,128)(2,1)S(1)}, u32[]{:S(2)}, u32[]{:S(2)}) collective-permute-start(bf16[384,256]{1,0:T(8,128)(2,1)S(1)} %get-tuple-element.80), channel_id=1, source_target_pairs={{0,24},{4,28},{8,16},{12,20},{16,8},{20,12},{24,0},{28,4},{1,25},{... | collective-permute-start | bytes 589832 | tf_op jit(solution)/shard_map/ppermute | solution.py:742
  25.4 6.8 %collective-permute-start.9 = (bf16[2,128,256]{2,1,0:T(8,128)(2,1)S(1)}, bf16[2,128,256]{2,1,0:T(8,128)(2,1)S(1)}, u32[]{:S(2)}, u32[]{:S(2)}) collective-permute-start(bf16[2,128,256]{2,1,0:T(8,128)(2,1)S(1)} %get-tuple-element.72), channel_id=1, source_target_pairs={{0,4},{4,0},{8,12},{12,8},{16,20},{20,16},{24,28},{28,24},{1,5},{5... | collective-permute-start | bytes 393224 | tf_op jit(solution)/shard_map/ppermute | solution.py:742
  25.5 6.7 %collective-permute-start.10 = (bf16[2,128,256]{2,1,0:T(8,128)(2,1)S(1)}, bf16[2,128,256]{2,1,0:T(8,128)(2,1)S(1)}, u32[]{:S(2)}, u32[]{:S(2)}) collective-permute-start(bf16[2,128,256]{2,1,0:T(8,128)(2,1)S(1)} %get-tuple-element.73), channel_id=1, source_target_pairs={{0,4},{4,0},{8,12},{12,8},{16,20},{20,16},{24,28},{28,24},{1,5},{5... | collective-permute-start | bytes 393224 | tf_op jit(solution)/shard_map/ppermute | solution.py:742
  32.4 14.8 %collective-permute-start.15 = (bf16[528,256]{1,0:T(8,128)(2,1)S(1)}, bf16[528,256]{1,0:T(8,128)(2,1)S(1)}, u32[]{:S(2)}, u32[]{:S(2)}) collective-permute-start(bf16[528,256]{1,0:T(8,128)(2,1)S(1)} %get-tuple-element.82), channel_id=1, source_target_pairs={{0,16},{4,20},{8,24},{12,28},{16,0},{20,4},{24,8},{28,12},{1,17},{... | collective-permute-start | bytes 811016 | tf_op jit(solution)/shard_map/ppermute | solution.py:742
  33.3 13.9 %collective-permute-start.14 = (bf16[528,256]{1,0:T(8,128)(2,1)S(1)}, bf16[528,256]{1,0:T(8,128)(2,1)S(1)}, u32[]{:S(2)}, u32[]{:S(2)}) collective-permute-start(bf16[528,256]{1,0:T(8,128)(2,1)S(1)} %get-tuple-element.82), channel_id=1, source_target_pairs={{0,8},{4,12},{8,0},{12,4},{16,24},{20,28},{24,16},{28,20},{1,9},{5... | collective-permute-start | bytes 811016 | tf_op jit(solution)/shard_map/ppermute | solution.py:742
  34.8 12.4 %collective-permute-start.16 = (bf16[512,256]{1,0:T(8,128)(2,1)S(1)}, bf16[512,256]{1,0:T(8,128)(2,1)S(1)}, u32[]{:S(2)}, u32[]{:S(2)}) collective-permute-start(bf16[512,256]{1,0:T(8,128)(2,1)S(1)} %get-tuple-element.81.refs_0_), channel_id=1, source_target_pairs={{0,24},{4,28},{8,16},{12,20},{16,8},{20,12},{24,0},{28,4},{1,25},{... | collective-permute-start | bytes 786440 | tf_op jit(solution)/shard_map/ppermute | solution.py:742
  48.0 10.5 %collective-permute-start.24 = (bf16[2,512,128]{2,1,0:T(8,128)(2,1)S(1)}, bf16[2,512,128]{2,1,0:T(8,128)(2,1)S(1)}, u32[]{:S(2)}, u32[]{:S(2)}) collective-permute-start(bf16[2,512,128]{2,1,0:T(8,128)(2,1)S(1)} %get-tuple-element.97), channel_id=1, source_target_pairs={{0,1},{1,0},{2,3},{3,2},{4,5},{5,4},{6,7},{7,6},{8,9},{9,8},{10,11... | collective-permute-start | bytes 786440 | tf_op jit(solution)/shard_map/ppermute | solution.py:742
  50.5 5.0 %collective-permute-start.17 = (bf16[128,512]{1,0:T(8,128)(2,1)S(1)}, bf16[128,512]{1,0:T(8,128)(2,1)S(1)}, u32[]{:S(2)}, u32[]{:S(2)}) collective-permute-start(bf16[128,512]{1,0:T(8,128)(2,1)S(1)} %get-tuple-element.84), channel_id=1, source_target_pairs={{0,8},{4,12},{8,0},{12,4},{16,24},{20,28},{24,16},{28,20},{1,9},{5... | collective-permute-start | bytes 393224 | tf_op jit(solution)/shard_map/ppermute | solution.py:742
  51.2 5.0 %collective-permute-start.18 = (bf16[128,512]{1,0:T(8,128)(2,1)S(1)}, bf16[128,512]{1,0:T(8,128)(2,1)S(1)}, u32[]{:S(2)}, u32[]{:S(2)}) collective-permute-start(bf16[128,512]{1,0:T(8,128)(2,1)S(1)} %get-tuple-element.85), channel_id=1, source_target_pairs={{0,16},{4,20},{8,24},{12,28},{16,0},{20,4},{24,8},{28,12},{1,17},{... | collective-permute-start | bytes 393224 | tf_op jit(solution)/shard_map/ppermute | solution.py:742
  52.0 5.9 %collective-permute-start.19 = (bf16[128,512]{1,0:T(8,128)(2,1)S(1)}, bf16[128,512]{1,0:T(8,128)(2,1)S(1)}, u32[]{:S(2)}, u32[]{:S(2)}) collective-permute-start(bf16[128,512]{1,0:T(8,128)(2,1)S(1)} %get-tuple-element.86), channel_id=1, source_target_pairs={{0,24},{4,28},{8,16},{12,20},{16,8},{20,12},{24,0},{28,4},{1,25},{... | collective-permute-start | bytes 393224 | tf_op jit(solution)/shard_map/ppermute | solution.py:742
  57.9 8.3 %collective-permute-start.20 = (bf16[2,128,512]{2,1,0:T(8,128)(2,1)S(1)}, bf16[2,128,512]{2,1,0:T(8,128)(2,1)S(1)}, u32[]{:S(2)}, u32[]{:S(2)}) collective-permute-start(bf16[2,128,512]{2,1,0:T(8,128)(2,1)S(1)} %get-tuple-element.88), channel_id=1, source_target_pairs={{0,1},{1,0},{2,3},{3,2},{4,5},{5,4},{6,7},{7,6},{8,9},{9,8},{10,11... | collective-permute-start | bytes 786440 | tf_op jit(solution)/shard_map/ppermute | solution.py:742
  58.5 10.0 %collective-permute-start.25 = (bf16[512,128]{1,0:T(8,128)(2,1)S(1)}, bf16[512,128]{1,0:T(8,128)(2,1)S(1)}, u32[]{:S(2)}, u32[]{:S(2)}) collective-permute-start(bf16[512,128]{1,0:T(8,128)(2,1)S(1)} %fusion), channel_id=1, source_target_pairs={{0,2},{1,3},{2,0},{3,1},{4,6},{5,7},{6,4},{7,5},{8,10},{9,11},{10,... | collective-permute-start | bytes 393224 | tf_op jit(solution)/shard_map/ppermute | solution.py:742
  66.2 10.3 %collective-permute-start.21 = (bf16[128,512]{1,0:T(8,128)(2,1)S(1)}, bf16[128,512]{1,0:T(8,128)(2,1)S(1)}, u32[]{:S(2)}, u32[]{:S(2)}) collective-permute-start(bf16[128,512]{1,0:T(8,128)(2,1)S(1)} %fusion.1), channel_id=1, source_target_pairs={{0,2},{1,3},{2,0},{3,1},{4,6},{5,7},{6,4},{7,5},{8,10},{9,11},{10,... | collective-permute-start | bytes 393224 | tf_op jit(solution)/shard_map/ppermute | solution.py:742
  68.5 4.0 %collective-permute-start.26 = (bf16[128,128]{1,0:T(8,128)(2,1)S(1)}, bf16[128,128]{1,0:T(8,128)(2,1)S(1)}, u32[]{:S(2)}, u32[]{:S(2)}) collective-permute-start(bf16[128,128]{1,0:T(8,128)(2,1)S(1)} %get-tuple-element.100), channel_id=1, source_target_pairs={{0,8},{4,12},{8,0},{12,4},{16,24},{20,28},{24,16},{28,20},{1,9},{5... | collective-permute-start | bytes 98312 | tf_op jit(solution)/shard_map/ppermute | solution.py:742
  71.7 4.8 %collective-permute-start.28 = (bf16[128,128]{1,0:T(8,128)(2,1)S(1)}, bf16[128,128]{1,0:T(8,128)(2,1)S(1)}, u32[]{:S(2)}, u32[]{:S(2)}) collective-permute-start(bf16[128,128]{1,0:T(8,128)(2,1)S(1)} %get-tuple-element.102), channel_id=1, source_target_pairs={{0,24},{4,28},{8,16},{12,20},{16,8},{20,12},{24,0},{28,4},{1,25},{... | collective-permute-start | bytes 98312 | tf_op jit(solution)/shard_map/ppermute | solution.py:742
  (11 other events, 63.6 us)

commit v18 on v13

--- a/solution.py
+++ b/solution.py
@@ -663,15 +663,13 @@
 
 
 def sort_kernel(chips, *refs):
-    in_refs, (keep_ref, pass_ref, send_ref, sorted_ref) = refs[:chips], refs[chips:]
+    in_refs, (*out_refs, sorted_ref) = refs[:chips], refs[chips:]
     chip, _ = own_place()
     layer = lax.axis_index("chan")
     for offset in range(chips):
         sorted_ref[chip ^ layer ^ offset] = in_refs[offset][...]
-    keep_ref[...] = sorted_ref[0]
-    send_ref[0] = sorted_ref[1]
-    pass_ref[...] = sorted_ref[2]
-    send_ref[1] = sorted_ref[3]
+    for target, out_ref in enumerate(out_refs):
+        out_ref[...] = sorted_ref[target]
 
 
 def sort_blocks(blocks):
@@ -680,13 +678,35 @@
     return pl.pallas_call(
         functools.partial(sort_kernel, chips),
         in_specs=[WHOLE] * chips,
-        out_specs=[WHOLE] * 3,
-        out_shape=[block, block, jax.ShapeDtypeStruct((2, *block.shape), BF16)],
+        out_specs=[WHOLE] * chips,
+        out_shape=[block] * chips,
         scratch_shapes=[pltpu.VMEM((chips, *block.shape), BF16)],
         cost_estimate=CHEAP,
         compiler_params=pltpu.CompilerParams(vmem_limit_bytes=4 * 2**20),
         name="sort_blocks",
     )(*blocks)
+
+
+def add_kernel(left_ref, right_ref, out_ref):
+    rows = left_ref.shape[0]
+    total = (left_ref[...].astype(F32) + right_ref[...].astype(F32)).astype(BF16)
+    out_ref[pl.ds(0, rows), :] = total
+    more = out_ref.shape[0] - rows
+    if more:
+        out_ref[pl.ds(rows, more), :] = total[:more]
+
+
+def add(left, right, spare):
+    rows, columns = left.shape
+    return pl.pallas_call(
+        add_kernel,
+        in_specs=[WHOLE] * 2,
+        out_specs=WHOLE,
+        out_shape=jax.ShapeDtypeStruct((rows + spare, columns), BF16),
+        cost_estimate=CHEAP,
+        compiler_params=pltpu.CompilerParams(vmem_limit_bytes=4 * 2**20),
+        name="add",
+    )(left, right)
 
 
 def finish_kernel(chips, keep_ref, first_ref, second_ref, *out_refs):
@@ -717,7 +737,8 @@
     share = in_refs[0].shape[1]
     for offset in range(chips):
         out_ref[:, block_at(chip ^ offset, share)] = in_refs[offset][...]
-    total = keep_ref[...].astype(F32) + first_ref[0].astype(F32) + second_ref[...].astype(F32)
+    total = keep_ref[...].astype(F32) + first_ref[...].astype(F32)
+    total = total + second_ref[pl.ds(0, total.shape[0]), :].astype(F32)
     out_ref[:, pl.ds(chips * share, total.shape[1])] = total.astype(BF16)
 
 
@@ -778,8 +799,9 @@
     others = [swapped(part, "seq", 1) for part in collect([after(block, gated) for block in moved[1:]], out_weight.shape[0] // 2)]
     keep, passed, send = project_moved(arrange(mine, moved[1:], others), gathered)
     blocks = to_chips(finish(keep, *over_layers(passed, send), chips))
-    keep, passed, send = sort_blocks(to_chips(project_still(out_weight, other_weight, gathered)))
-    return join(keep, *over_layers(passed, send), blocks)
+    keep, near, passed, far = sort_blocks(to_chips(project_still(out_weight, other_weight, gathered)))
+    second = swapped(add(passed, swapped(far, "chan", 1), 0), "chan", 2)
+    return join(keep, swapped(near, "chan", 1), second, blocks)
 
 
 def shards(values_in, gate_values, filter_spectrum, skip_gain, out_weight):

time: 76.3 us -> 76.2 us (level)
  waiting for transfers between devices: 33 us -> 30.2 us
  starting transfers between devices: 31.2 us -> 33.9 us
    ppermute x29 -> x30, waiting for transfers between devices: 33 us -> 30.2 us  [swapped(): lax.ppermute(value, axis, [(source, source ^ offset) for source in range(...]
    ppermute x29 -> x30, starting transfers between devices: 31.2 us -> 33.9 us  [swapped(): lax.ppermute(value, axis, [(source, source ^ offset) for source in range(...]
  transfers between devices with their start and end apart: 29 -> 30, of which waited for: 16 -> 17; matrix products, arithmetic and copies ran while one was open for 0% -> 0% of each run, Pallas kernels for 13% -> 13%
where the time goes in v18:
time: 76.2 us; the launch traced here: 76 us
  starting transfers between devices  33.9 us (44%)
  waiting for transfers between devices  30.2 us (40%)
  Pallas kernels  11.6 us (15%)
    ppermute x30, starting transfers between devices, swapped(): lax.ppermute(value, axis, [(source, source ^ offset) for source in range(...  33.9 us
    ppermute x30, waiting for transfers between devices, swapped(): lax.ppermute(value, axis, [(source, source ^ offset) for source in range(...  30.2 us
    pallas_call x2, Pallas kernels, pack_filters(): pl.pallas_call(functools.partial(pack_filters_kernel, offsets), in_specs=...  2.74 us
    pallas_call x1, Pallas kernels, backward(): pl.pallas_call(functools.partial(backward_kernel, chips), in_specs=[WHOLE...  2.01 us
  transfers between devices with their start and end apart: 30, of which 17 were waited for; matrix products, arithmetic and copies ran while one was open for 0% of the time, Pallas kernels for 13%

profile of v18, /device:TPU:0, one launch (start us, length us, event | category | flops | bytes accessed | tf_op | source)
XLA Modules:
  0.0 76.0 jit_solution(13245623795339262778)
XLA Ops:
  1.4 3.5 %collective-permute-start.3 = (bf16[128,256]{1,0:T(8,128)(2,1)S(1)}, bf16[128,256]{1,0:T(8,128)(2,1)S(1)}, u32[]{:S(2)}, u32[]{:S(2)}) collective-permute-start(bf16[128,256]{1,0:T(8,128)(2,1)S(1)} %get-tuple-element.68), channel_id=1, source_target_pairs={{0,24},{4,28},{8,16},{12,20},{16,8},{20,12},{24,0},{28,4},{1,25},{... | collective-permute-start | bytes 196616 | tf_op jit(solution)/shard_map/ppermute | solution.py:762
  4.9 1.4 %pack_filters.2 = (bf16[512,256]{1,0:T(8,128)(2,1)S(1)}, bf16[512,256]{1,0:T(8,128)(2,1)S(1)}) custom-call(f32[4,128,1024]{2,1,0:T(8,128)} %bitcast.8), custom_call_target="tpu_custom_call" | custom-call | tf_op jit(solution)/shard_map/pack_filters/pallas_call | solution.py:243
  6.9 1.5 %collective-permute-start.2 = (bf16[128,256]{1,0:T(8,128)(2,1)S(1)}, bf16[128,256]{1,0:T(8,128)(2,1)S(1)}, u32[]{:S(2)}, u32[]{:S(2)}) collective-permute-start(bf16[128,256]{1,0:T(8,128)(2,1)S(1)} %get-tuple-element.66), channel_id=1, source_target_pairs={{0,16},{4,20},{8,24},{12,28},{16,0},{20,4},{24,8},{28,12},{1,17},{... | collective-permute-start | bytes 196616 | tf_op jit(solution)/shard_map/ppermute | solution.py:762
  9.0 1.6 %collective-permute-start.6 = (bf16[512,256]{1,0:T(8,128)(2,1)S(1)}, bf16[512,256]{1,0:T(8,128)(2,1)S(1)}, u32[]{:S(2)}, u32[]{:S(2)}) collective-permute-start(bf16[512,256]{1,0:T(8,128)(2,1)S(1)} %get-tuple-element.58), channel_id=1, source_target_pairs={{0,8},{4,12},{8,0},{12,4},{16,24},{20,28},{24,16},{28,20},{1,9},{5... | collective-permute-start | bytes 786440 | tf_op jit(solution)/shard_map/ppermute | solution.py:762
  10.5 1.3 %pack_moved.1 = (bf16[128,256]{1,0:T(8,128)(2,1)S(1)}, bf16[384,256]{1,0:T(8,128)(2,1)S(1)}, bf16[384,256]{1,0:T(8,128)(2,1)S(1)}, bf16[384,256]{1,0:T(8,128)(2,1)S(1)}, bf16[1024,128]{1,0:T(8,128)(2,1)S(1)}) custom-call(bf16[128,1024]{1,0:T(8,128)(2,1)} %gate_ref, bf16[1024,512]{1,0:T(8,128)(2,1)} %own_ref.3, ...), custom_call_target="tpu_custom_call" | custom-call | tf_op jit(solution)/shard_map/pack_moved/pallas_call | solution.py:321
  11.8 1.4 %pack_filters.3 = (bf16[512,256]{1,0:T(8,128)(2,1)S(1)}, bf16[512,256]{1,0:T(8,128)(2,1)S(1)}) custom-call(f32[4,128,1024]{2,1,0:T(8,128)} %bitcast.9), custom_call_target="tpu_custom_call" | custom-call | tf_op jit(solution)/shard_map/pack_filters/pallas_call | solution.py:243
  13.3 2.9 %collective-permute-done.2.refs_2_ = bf16[128,256]{1,0:T(8,128)(2,1)S(1)} collective-permute-done((bf16[128,256]{1,0:T(8,128)(2,1)S(1)}, bf16[128,256]{1,0:T(8,128)(2,1)S(1)}, u32[]{:S(2)}, u32[]{:S(2)}) %collective-permute-start.2) | collective-permute-done | bytes 65568 | tf_op jit(solution)/shard_map/ppermute | solution.py:762
  17.9 1.5 %forward.1.spectrum_ref = f32[256,2048]{1,0:T(8,128)S(1)} custom-call(f32[2,128,8]{2,1,0:T(8,128)S(1)} %copy-done.2, f32[2,128,8]{2,1,0:T(8,128)S(1)} %copy-done.1, bf16[256,256]{1,0:T(8,128)(2,1)S(1)} %copy-done.4, bf16[2,128,256]{2,1,0:T(8,128)(2,1)S(1)} %get-tuple-element.70.refs_0_, bf16[2,128,256]{2,1,0:T(8,128)(2,1)S(1)} %get-tuple-element.71.refs_1_, ...), custom_call_target="tpu_custom_call" | custom-call | tf_op jit(solution)/shard_map/forward/pallas_call | solution.py:409
  21.1 1.8 %collective-permute-start.13 = (bf16[384,256]{1,0:T(8,128)(2,1)S(1)}, bf16[384,256]{1,0:T(8,128)(2,1)S(1)}, u32[]{:S(2)}, u32[]{:S(2)}) collective-permute-start(bf16[384,256]{1,0:T(8,128)(2,1)S(1)} %get-tuple-element.83), channel_id=1, source_target_pairs={{0,24},{4,28},{8,16},{12,20},{16,8},{20,12},{24,0},{28,4},{1,25},{... | collective-permute-start | bytes 589832 | tf_op jit(solution)/shard_map/ppermute | solution.py:762
  24.2 2.0 %backward.1 = (f32[4,128,256]{2,1,0:T(8,128)S(1)}, bf16[2,128,256]{2,1,0:T(8,128)(2,1)S(1)}, bf16[2,128,256]{2,1,0:T(8,128)(2,1)S(1)}) custom-call(f32[2,128,8]{2,1,0:T(8,128)S(1)} %copy-done.2, f32[2,128,8]{2,1,0:T(8,128)S(1)} %copy-done.1, bf16[256,256]{1,0:T(8,128)(2,1)S(1)} %copy-done.3, f32[256,2048]{1,0:T(8,128)S(1)} %forward.1.spectrum_ref, ...), custom_call_target="tpu_custom_call" | custom-call | tf_op jit(solution)/shard_map/backward/pallas_call | solution.py:485
  26.7 1.7 %collective-permute-done.11.refs_5_.refs_0_ = bf16[384,256]{1,0:T(8,128)(2,1)S(1)} collective-permute-done((bf16[384,256]{1,0:T(8,128)(2,1)S(1)}, bf16[384,256]{1,0:T(8,128)(2,1)S(1)}, u32[]{:S(2)}, u32[]{:S(2)}) %collective-permute-start.11) | collective-permute-done | bytes 196640 | tf_op jit(solution)/shard_map/ppermute | solution.py:762
  28.4 3.4 %collective-permute-done.12.refs_6_.refs_1_ = bf16[384,256]{1,0:T(8,128)(2,1)S(1)} collective-permute-done((bf16[384,256]{1,0:T(8,128)(2,1)S(1)}, bf16[384,256]{1,0:T(8,128)(2,1)S(1)}, u32[]{:S(2)}, u32[]{:S(2)}) %collective-permute-start.12) | collective-permute-done | bytes 196640 | tf_op jit(solution)/shard_map/ppermute | solution.py:762
  32.0 1.5 %collective-permute-start.15 = (bf16[528,256]{1,0:T(8,128)(2,1)S(1)}, bf16[528,256]{1,0:T(8,128)(2,1)S(1)}, u32[]{:S(2)}, u32[]{:S(2)}) collective-permute-start(bf16[528,256]{1,0:T(8,128)(2,1)S(1)} %get-tuple-element.85), channel_id=1, source_target_pairs={{0,16},{4,20},{8,24},{12,28},{16,0},{20,4},{24,8},{28,12},{1,17},{... | collective-permute-start | bytes 811016 | tf_op jit(solution)/shard_map/ppermute | solution.py:762
  37.6 8.8 %collective-permute-done.16.refs_3_ = bf16[512,256]{1,0:T(8,128)(2,1)S(1)} collective-permute-done((bf16[512,256]{1,0:T(8,128)(2,1)S(1)}, bf16[512,256]{1,0:T(8,128)(2,1)S(1)}, u32[]{:S(2)}, u32[]{:S(2)}) %collective-permute-start.16) | collective-permute-done | bytes 262176 | tf_op jit(solution)/shard_map/ppermute | solution.py:762
  47.2 1.6 %collective-permute-start.25 = (bf16[2,512,128]{2,1,0:T(8,128)(2,1)S(1)}, bf16[2,512,128]{2,1,0:T(8,128)(2,1)S(1)}, u32[]{:S(2)}, u32[]{:S(2)}) collective-permute-start(bf16[2,512,128]{2,1,0:T(8,128)(2,1)S(1)} %get-tuple-element.101), channel_id=1, source_target_pairs={{0,1},{1,0},{2,3},{3,2},{4,5},{5,4},{6,7},{7,6},{8,9},{9,8},{10,11... | collective-permute-start | bytes 786440 | tf_op jit(solution)/shard_map/ppermute | solution.py:762
  51.0 1.3 %collective-permute-start.18 = (bf16[128,512]{1,0:T(8,128)(2,1)S(1)}, bf16[128,512]{1,0:T(8,128)(2,1)S(1)}, u32[]{:S(2)}, u32[]{:S(2)}) collective-permute-start(bf16[128,512]{1,0:T(8,128)(2,1)S(1)} %get-tuple-element.88), channel_id=1, source_target_pairs={{0,16},{4,20},{8,24},{12,28},{16,0},{20,4},{24,8},{28,12},{1,17},{... | collective-permute-start | bytes 393224 | tf_op jit(solution)/shard_map/ppermute | solution.py:762
  53.3 1.7 %collective-permute-done.17.refs_1_ = bf16[128,512]{1,0:T(8,128)(2,1)S(1)} collective-permute-done((bf16[128,512]{1,0:T(8,128)(2,1)S(1)}, bf16[128,512]{1,0:T(8,128)(2,1)S(1)}, u32[]{:S(2)}, u32[]{:S(2)}) %collective-permute-start.17) | collective-permute-done | bytes 131104 | tf_op jit(solution)/shard_map/ppermute | solution.py:762
  56.0 2.2 %collective-permute-done.19.refs_3_ = bf16[128,512]{1,0:T(8,128)(2,1)S(1)} collective-permute-done((bf16[128,512]{1,0:T(8,128)(2,1)S(1)}, bf16[128,512]{1,0:T(8,128)(2,1)S(1)}, u32[]{:S(2)}, u32[]{:S(2)}) %collective-permute-start.19) | collective-permute-done | bytes 131104 | tf_op jit(solution)/shard_map/ppermute | solution.py:762
  58.9 2.7 %collective-permute-start.26 = (bf16[512,128]{1,0:T(8,128)(2,1)S(1)}, bf16[512,128]{1,0:T(8,128)(2,1)S(1)}, u32[]{:S(2)}, u32[]{:S(2)}) collective-permute-start(bf16[512,128]{1,0:T(8,128)(2,1)S(1)} %fusion), channel_id=1, source_target_pairs={{0,2},{1,3},{2,0},{3,1},{4,6},{5,7},{6,4},{7,5},{8,10},{9,11},{10,... | collective-permute-start | bytes 393224 | tf_op jit(solution)/shard_map/ppermute | solution.py:762
  61.5 1.6 %collective-permute-start.20 = (bf16[128,512]{1,0:T(8,128)(2,1)S(1)}, bf16[128,512]{1,0:T(8,128)(2,1)S(1)}, u32[]{:S(2)}, u32[]{:S(2)}) collective-permute-start(bf16[128,512]{1,0:T(8,128)(2,1)S(1)} %get-tuple-element.91), channel_id=1, source_target_pairs={{0,1},{1,0},{2,3},{3,2},{4,5},{5,4},{6,7},{7,6},{8,9},{9,8},{10,11... | collective-permute-start | bytes 393224 | tf_op jit(solution)/shard_map/ppermute | solution.py:762
  63.4 3.3 %collective-permute-start.22 = (bf16[128,512]{1,0:T(8,128)(2,1)S(1)}, bf16[128,512]{1,0:T(8,128)(2,1)S(1)}, u32[]{:S(2)}, u32[]{:S(2)}) collective-permute-start(bf16[128,512]{1,0:T(8,128)(2,1)S(1)} %add.8), channel_id=1, source_target_pairs={{0,2},{1,3},{2,0},{3,1},{4,6},{5,7},{6,4},{7,5},{8,10},{9,11},{10,... | collective-permute-start | bytes 393224 | tf_op jit(solution)/shard_map/ppermute | solution.py:762
  66.8 2.1 %collective-permute-done.26.second_ref = bf16[512,128]{1,0:T(8,128)(2,1)S(1)} collective-permute-done((bf16[512,128]{1,0:T(8,128)(2,1)S(1)}, bf16[512,128]{1,0:T(8,128)(2,1)S(1)}, u32[]{:S(2)}, u32[]{:S(2)}) %collective-permute-start.26) | collective-permute-done | bytes 131104 | tf_op jit(solution)/shard_map/ppermute | solution.py:762
  70.4 2.1 %collective-permute-start.29 = (bf16[128,128]{1,0:T(8,128)(2,1)S(1)}, bf16[128,128]{1,0:T(8,128)(2,1)S(1)}, u32[]{:S(2)}, u32[]{:S(2)}) collective-permute-start(bf16[128,128]{1,0:T(8,128)(2,1)S(1)} %get-tuple-element.106), channel_id=1, source_target_pairs={{0,24},{4,28},{8,16},{12,20},{16,8},{20,12},{24,0},{28,4},{1,25},{... | collective-permute-start | bytes 98312 | tf_op jit(solution)/shard_map/ppermute | solution.py:762
  73.8 1.4 %collective-permute-done.29.refs_3_ = bf16[128,128]{1,0:T(8,128)(2,1)S(1)} collective-permute-done((bf16[128,128]{1,0:T(8,128)(2,1)S(1)}, bf16[128,128]{1,0:T(8,128)(2,1)S(1)}, u32[]{:S(2)}, u32[]{:S(2)}) %collective-permute-start.29) | collective-permute-done | bytes 32800 | tf_op jit(solution)/shard_map/ppermute | solution.py:762
  (65 shorter events, 21.8 us)
Async XLA Ops:
  0.0 8.9 %collective-permute-start = (bf16[1024,512]{1,0:T(8,128)(2,1)}, bf16[1024,512]{1,0:T(8,128)(2,1)S(1)}, u32[]{:S(2)}, u32[]{:S(2)}) collective-permute-start(bf16[1024,512]{1,0:T(8,128)(2,1)} %own_ref.3), channel_id=1, source_target_pairs={{0,4},{4,0},{8,12},{12,8},{16,20},{20,16},{24,28},{28,24},{1,5},{5... | collective-permute-start | bytes 3145736 | tf_op jit(solution)/shard_map/ppermute | solution.py:762
  1.4 11.8 %collective-permute-start.3 = (bf16[128,256]{1,0:T(8,128)(2,1)S(1)}, bf16[128,256]{1,0:T(8,128)(2,1)S(1)}, u32[]{:S(2)}, u32[]{:S(2)}) collective-permute-start(bf16[128,256]{1,0:T(8,128)(2,1)S(1)} %get-tuple-element.68), channel_id=1, source_target_pairs={{0,24},{4,28},{8,16},{12,20},{16,8},{20,12},{24,0},{28,4},{1,25},{... | collective-permute-start | bytes 196616 | tf_op jit(solution)/shard_map/ppermute | solution.py:762
  6.3 14.8 %collective-permute-start.7 = (bf16[512,256]{1,0:T(8,128)(2,1)S(1)}, bf16[512,256]{1,0:T(8,128)(2,1)S(1)}, u32[]{:S(2)}, u32[]{:S(2)}) collective-permute-start(bf16[512,256]{1,0:T(8,128)(2,1)S(1)} %get-tuple-element.73), channel_id=1, source_target_pairs={{0,16},{4,20},{8,24},{12,28},{16,0},{20,4},{24,8},{28,12},{1,17},{... | collective-permute-start | bytes 786440 | tf_op jit(solution)/shard_map/ppermute | solution.py:762
  6.9 9.3 %collective-permute-start.2 = (bf16[128,256]{1,0:T(8,128)(2,1)S(1)}, bf16[128,256]{1,0:T(8,128)(2,1)S(1)}, u32[]{:S(2)}, u32[]{:S(2)}) collective-permute-start(bf16[128,256]{1,0:T(8,128)(2,1)S(1)} %get-tuple-element.66), channel_id=1, source_target_pairs={{0,16},{4,20},{8,24},{12,28},{16,0},{20,4},{24,8},{28,12},{1,17},{... | collective-permute-start | bytes 196616 | tf_op jit(solution)/shard_map/ppermute | solution.py:762
  8.4 7.8 %collective-permute-start.1 = (bf16[128,256]{1,0:T(8,128)(2,1)S(1)}, bf16[128,256]{1,0:T(8,128)(2,1)S(1)}, u32[]{:S(2)}, u32[]{:S(2)}) collective-permute-start(bf16[128,256]{1,0:T(8,128)(2,1)S(1)} %get-tuple-element.64), channel_id=1, source_target_pairs={{0,8},{4,12},{8,0},{12,4},{16,24},{20,28},{24,16},{28,20},{1,9},{5... | collective-permute-start | bytes 196616 | tf_op jit(solution)/shard_map/ppermute | solution.py:762
  9.0 14.0 %collective-permute-start.6 = (bf16[512,256]{1,0:T(8,128)(2,1)S(1)}, bf16[512,256]{1,0:T(8,128)(2,1)S(1)}, u32[]{:S(2)}, u32[]{:S(2)}) collective-permute-start(bf16[512,256]{1,0:T(8,128)(2,1)S(1)} %get-tuple-element.58), channel_id=1, source_target_pairs={{0,8},{4,12},{8,0},{12,4},{16,24},{20,28},{24,16},{28,20},{1,9},{5... | collective-permute-start | bytes 786440 | tf_op jit(solution)/shard_map/ppermute | solution.py:762
  13.2 11.0 %collective-permute-start.8 = (bf16[512,256]{1,0:T(8,128)(2,1)S(1)}, bf16[512,256]{1,0:T(8,128)(2,1)S(1)}, u32[]{:S(2)}, u32[]{:S(2)}) collective-permute-start(bf16[512,256]{1,0:T(8,128)(2,1)S(1)} %get-tuple-element.62), channel_id=1, source_target_pairs={{0,24},{4,28},{8,16},{12,20},{16,8},{20,12},{24,0},{28,4},{1,25},{... | collective-permute-start | bytes 786440 | tf_op jit(solution)/shard_map/ppermute | solution.py:762
  19.4 9.1 %collective-permute-start.11 = (bf16[384,256]{1,0:T(8,128)(2,1)S(1)}, bf16[384,256]{1,0:T(8,128)(2,1)S(1)}, u32[]{:S(2)}, u32[]{:S(2)}) collective-permute-start(bf16[384,256]{1,0:T(8,128)(2,1)S(1)} %get-tuple-element.79), channel_id=1, source_target_pairs={{0,8},{4,12},{8,0},{12,4},{16,24},{20,28},{24,16},{28,20},{1,9},{5... | collective-permute-start | bytes 589832 | tf_op jit(solution)/shard_map/ppermute | solution.py:762
  20.0 11.8 %collective-permute-start.12 = (bf16[384,256]{1,0:T(8,128)(2,1)S(1)}, bf16[384,256]{1,0:T(8,128)(2,1)S(1)}, u32[]{:S(2)}, u32[]{:S(2)}) collective-permute-start(bf16[384,256]{1,0:T(8,128)(2,1)S(1)} %get-tuple-element.81), channel_id=1, source_target_pairs={{0,16},{4,20},{8,24},{12,28},{16,0},{20,4},{24,8},{28,12},{1,17},{... | collective-permute-start | bytes 589832 | tf_op jit(solution)/shard_map/ppermute | solution.py:762
  21.1 10.7 %collective-permute-start.13 = (bf16[384,256]{1,0:T(8,128)(2,1)S(1)}, bf16[384,256]{1,0:T(8,128)(2,1)S(1)}, u32[]{:S(2)}, u32[]{:S(2)}) collective-permute-start(bf16[384,256]{1,0:T(8,128)(2,1)S(1)} %get-tuple-element.83), channel_id=1, source_target_pairs={{0,24},{4,28},{8,16},{12,20},{16,8},{20,12},{24,0},{28,4},{1,25},{... | collective-permute-start | bytes 589832 | tf_op jit(solution)/shard_map/ppermute | solution.py:762
  26.2 5.6 %collective-permute-start.9 = (bf16[2,128,256]{2,1,0:T(8,128)(2,1)S(1)}, bf16[2,128,256]{2,1,0:T(8,128)(2,1)S(1)}, u32[]{:S(2)}, u32[]{:S(2)}) collective-permute-start(bf16[2,128,256]{2,1,0:T(8,128)(2,1)S(1)} %get-tuple-element.75), channel_id=1, source_target_pairs={{0,4},{4,0},{8,12},{12,8},{16,20},{20,16},{24,28},{28,24},{1,5},{5... | collective-permute-start | bytes 393224 | tf_op jit(solution)/shard_map/ppermute | solution.py:762
  26.3 5.6 %collective-permute-start.10 = (bf16[2,128,256]{2,1,0:T(8,128)(2,1)S(1)}, bf16[2,128,256]{2,1,0:T(8,128)(2,1)S(1)}, u32[]{:S(2)}, u32[]{:S(2)}) collective-permute-start(bf16[2,128,256]{2,1,0:T(8,128)(2,1)S(1)} %get-tuple-element.76), channel_id=1, source_target_pairs={{0,4},{4,0},{8,12},{12,8},{16,20},{20,16},{24,28},{28,24},{1,5},{5... | collective-permute-start | bytes 393224 | tf_op jit(solution)/shard_map/ppermute | solution.py:762
  32.0 14.4 %collective-permute-start.15 = (bf16[528,256]{1,0:T(8,128)(2,1)S(1)}, bf16[528,256]{1,0:T(8,128)(2,1)S(1)}, u32[]{:S(2)}, u32[]{:S(2)}) collective-permute-start(bf16[528,256]{1,0:T(8,128)(2,1)S(1)} %get-tuple-element.85), channel_id=1, source_target_pairs={{0,16},{4,20},{8,24},{12,28},{16,0},{20,4},{24,8},{28,12},{1,17},{... | collective-permute-start | bytes 811016 | tf_op jit(solution)/shard_map/ppermute | solution.py:762
  33.5 12.9 %collective-permute-start.14 = (bf16[528,256]{1,0:T(8,128)(2,1)S(1)}, bf16[528,256]{1,0:T(8,128)(2,1)S(1)}, u32[]{:S(2)}, u32[]{:S(2)}) collective-permute-start(bf16[528,256]{1,0:T(8,128)(2,1)S(1)} %get-tuple-element.85), channel_id=1, source_target_pairs={{0,8},{4,12},{8,0},{12,4},{16,24},{20,28},{24,16},{28,20},{1,9},{5... | collective-permute-start | bytes 811016 | tf_op jit(solution)/shard_map/ppermute | solution.py:762
  34.6 11.8 %collective-permute-start.16 = (bf16[512,256]{1,0:T(8,128)(2,1)S(1)}, bf16[512,256]{1,0:T(8,128)(2,1)S(1)}, u32[]{:S(2)}, u32[]{:S(2)}) collective-permute-start(bf16[512,256]{1,0:T(8,128)(2,1)S(1)} %get-tuple-element.84.refs_0_), channel_id=1, source_target_pairs={{0,24},{4,28},{8,16},{12,20},{16,8},{20,12},{24,0},{28,4},{1,25},{... | collective-permute-start | bytes 786440 | tf_op jit(solution)/shard_map/ppermute | solution.py:762
  47.2 11.6 %collective-permute-start.25 = (bf16[2,512,128]{2,1,0:T(8,128)(2,1)S(1)}, bf16[2,512,128]{2,1,0:T(8,128)(2,1)S(1)}, u32[]{:S(2)}, u32[]{:S(2)}) collective-permute-start(bf16[2,512,128]{2,1,0:T(8,128)(2,1)S(1)} %get-tuple-element.101), channel_id=1, source_target_pairs={{0,1},{1,0},{2,3},{3,2},{4,5},{5,4},{6,7},{7,6},{8,9},{9,8},{10,11... | collective-permute-start | bytes 786440 | tf_op jit(solution)/shard_map/ppermute | solution.py:762
  49.8 5.2 %collective-permute-start.17 = (bf16[128,512]{1,0:T(8,128)(2,1)S(1)}, bf16[128,512]{1,0:T(8,128)(2,1)S(1)}, u32[]{:S(2)}, u32[]{:S(2)}) collective-permute-start(bf16[128,512]{1,0:T(8,128)(2,1)S(1)} %get-tuple-element.87), channel_id=1, source_target_pairs={{0,8},{4,12},{8,0},{12,4},{16,24},{20,28},{24,16},{28,20},{1,9},{5... | collective-permute-start | bytes 393224 | tf_op jit(solution)/shard_map/ppermute | solution.py:762
  51.0 5.0 %collective-permute-start.18 = (bf16[128,512]{1,0:T(8,128)(2,1)S(1)}, bf16[128,512]{1,0:T(8,128)(2,1)S(1)}, u32[]{:S(2)}, u32[]{:S(2)}) collective-permute-start(bf16[128,512]{1,0:T(8,128)(2,1)S(1)} %get-tuple-element.88), channel_id=1, source_target_pairs={{0,16},{4,20},{8,24},{12,28},{16,0},{20,4},{24,8},{28,12},{1,17},{... | collective-permute-start | bytes 393224 | tf_op jit(solution)/shard_map/ppermute | solution.py:762
  52.4 5.9 %collective-permute-start.19 = (bf16[128,512]{1,0:T(8,128)(2,1)S(1)}, bf16[128,512]{1,0:T(8,128)(2,1)S(1)}, u32[]{:S(2)}, u32[]{:S(2)}) collective-permute-start(bf16[128,512]{1,0:T(8,128)(2,1)S(1)} %get-tuple-element.89), channel_id=1, source_target_pairs={{0,24},{4,28},{8,16},{12,20},{16,8},{20,12},{24,0},{28,4},{1,25},{... | collective-permute-start | bytes 393224 | tf_op jit(solution)/shard_map/ppermute | solution.py:762
  58.3 5.0 %collective-permute-start.21 = (bf16[128,512]{1,0:T(8,128)(2,1)S(1)}, bf16[128,512]{1,0:T(8,128)(2,1)S(1)}, u32[]{:S(2)}, u32[]{:S(2)}) collective-permute-start(bf16[128,512]{1,0:T(8,128)(2,1)S(1)} %get-tuple-element.93), channel_id=1, source_target_pairs={{0,1},{1,0},{2,3},{3,2},{4,5},{5,4},{6,7},{7,6},{8,9},{9,8},{10,11... | collective-permute-start | bytes 393224 | tf_op jit(solution)/shard_map/ppermute | solution.py:762
  58.9 10.0 %collective-permute-start.26 = (bf16[512,128]{1,0:T(8,128)(2,1)S(1)}, bf16[512,128]{1,0:T(8,128)(2,1)S(1)}, u32[]{:S(2)}, u32[]{:S(2)}) collective-permute-start(bf16[512,128]{1,0:T(8,128)(2,1)S(1)} %fusion), channel_id=1, source_target_pairs={{0,2},{1,3},{2,0},{3,1},{4,6},{5,7},{6,4},{7,5},{8,10},{9,11},{10,... | collective-permute-start | bytes 393224 | tf_op jit(solution)/shard_map/ppermute | solution.py:762
  61.5 10.9 %collective-permute-start.20 = (bf16[128,512]{1,0:T(8,128)(2,1)S(1)}, bf16[128,512]{1,0:T(8,128)(2,1)S(1)}, u32[]{:S(2)}, u32[]{:S(2)}) collective-permute-start(bf16[128,512]{1,0:T(8,128)(2,1)S(1)} %get-tuple-element.91), channel_id=1, source_target_pairs={{0,1},{1,0},{2,3},{3,2},{4,5},{5,4},{6,7},{7,6},{8,9},{9,8},{10,11... | collective-permute-start | bytes 393224 | tf_op jit(solution)/shard_map/ppermute | solution.py:762
  63.4 9.1 %collective-permute-start.22 = (bf16[128,512]{1,0:T(8,128)(2,1)S(1)}, bf16[128,512]{1,0:T(8,128)(2,1)S(1)}, u32[]{:S(2)}, u32[]{:S(2)}) collective-permute-start(bf16[128,512]{1,0:T(8,128)(2,1)S(1)} %add.8), channel_id=1, source_target_pairs={{0,2},{1,3},{2,0},{3,1},{4,6},{5,7},{6,4},{7,5},{8,10},{9,11},{10,... | collective-permute-start | bytes 393224 | tf_op jit(solution)/shard_map/ppermute | solution.py:762
  70.4 4.8 %collective-permute-start.29 = (bf16[128,128]{1,0:T(8,128)(2,1)S(1)}, bf16[128,128]{1,0:T(8,128)(2,1)S(1)}, u32[]{:S(2)}, u32[]{:S(2)}) collective-permute-start(bf16[128,128]{1,0:T(8,128)(2,1)S(1)} %get-tuple-element.106), channel_id=1, source_target_pairs={{0,24},{4,28},{8,16},{12,20},{16,8},{20,12},{24,0},{28,4},{1,25},{... | collective-permute-start | bytes 98312 | tf_op jit(solution)/shard_map/ppermute | solution.py:762
  (12 other events, 75.7 us)

commit v19 on v18

--- a/solution.py
+++ b/solution.py
@@ -800,7 +800,7 @@
     keep, passed, send = project_moved(arrange(mine, moved[1:], others), gathered)
     blocks = to_chips(finish(keep, *over_layers(passed, send), chips))
     keep, near, passed, far = sort_blocks(to_chips(project_still(out_weight, other_weight, gathered)))
-    second = swapped(add(passed, swapped(far, "chan", 1), 0), "chan", 2)
+    second = swapped(add(after(passed, blocks[1]), swapped(far, "chan", 1), 0), "chan", 2)
     return join(keep, swapped(near, "chan", 1), second, blocks)
 
 

time: 76.2 us -> 74.8 us (0.982)
  waiting for transfers between devices: 30.2 us -> 27.8 us
  starting transfers between devices: 33.9 us -> 34.8 us
    ppermute x30, waiting for transfers between devices: 30.2 us -> 27.8 us  [swapped(): lax.ppermute(value, axis, [(source, source ^ offset) for source in range(...]
    ppermute x30, starting transfers between devices: 33.9 us -> 34.8 us  [swapped(): lax.ppermute(value, axis, [(source, source ^ offset) for source in range(...]
  transfers between devices with their start and end apart: 30 -> 30, of which waited for: 17 -> 16; matrix products, arithmetic and copies ran while one was open for 0% -> 0% of each run, Pallas kernels for 13% -> 13%
where the time goes in v19:
time: 74.8 us; the launch traced here: 74.5 us
  starting transfers between devices  34.8 us (47%)
  waiting for transfers between devices  27.8 us (37%)
  Pallas kernels  11.6 us (16%)
    ppermute x30, starting transfers between devices, swapped(): lax.ppermute(value, axis, [(source, source ^ offset) for source in range(...  34.8 us
    ppermute x30, waiting for transfers between devices, swapped(): lax.ppermute(value, axis, [(source, source ^ offset) for source in range(...  27.8 us
    pallas_call x2, Pallas kernels, pack_filters(): pl.pallas_call(functools.partial(pack_filters_kernel, offsets), in_specs=...  2.74 us
    pallas_call x1, Pallas kernels, backward(): pl.pallas_call(functools.partial(backward_kernel, chips), in_specs=[WHOLE...  2.01 us
  transfers between devices with their start and end apart: 30, of which 16 were waited for; matrix products, arithmetic and copies ran while one was open for 0% of the time, Pallas kernels for 13%

profile of v19, /device:TPU:0, one launch (start us, length us, event | category | flops | bytes accessed | tf_op | source)
XLA Modules:
  0.0 74.5 jit_solution(15438949655058521857)
XLA Ops:
  1.4 3.5 %collective-permute-start.3 = (bf16[128,256]{1,0:T(8,128)(2,1)S(1)}, bf16[128,256]{1,0:T(8,128)(2,1)S(1)}, u32[]{:S(2)}, u32[]{:S(2)}) collective-permute-start(bf16[128,256]{1,0:T(8,128)(2,1)S(1)} %get-tuple-element.69), channel_id=1, source_target_pairs={{0,24},{4,28},{8,16},{12,20},{16,8},{20,12},{24,0},{28,4},{1,25},{... | collective-permute-start | bytes 196616 | tf_op jit(solution)/shard_map/ppermute | solution.py:762
  4.9 1.4 %pack_filters.2 = (bf16[512,256]{1,0:T(8,128)(2,1)S(1)}, bf16[512,256]{1,0:T(8,128)(2,1)S(1)}) custom-call(f32[4,128,1024]{2,1,0:T(8,128)} %bitcast.8), custom_call_target="tpu_custom_call" | custom-call | tf_op jit(solution)/shard_map/pack_filters/pallas_call | solution.py:243
  6.9 1.5 %collective-permute-start.2 = (bf16[128,256]{1,0:T(8,128)(2,1)S(1)}, bf16[128,256]{1,0:T(8,128)(2,1)S(1)}, u32[]{:S(2)}, u32[]{:S(2)}) collective-permute-start(bf16[128,256]{1,0:T(8,128)(2,1)S(1)} %get-tuple-element.67), channel_id=1, source_target_pairs={{0,16},{4,20},{8,24},{12,28},{16,0},{20,4},{24,8},{28,12},{1,17},{... | collective-permute-start | bytes 196616 | tf_op jit(solution)/shard_map/ppermute | solution.py:762
  9.0 1.6 %collective-permute-start.6 = (bf16[512,256]{1,0:T(8,128)(2,1)S(1)}, bf16[512,256]{1,0:T(8,128)(2,1)S(1)}, u32[]{:S(2)}, u32[]{:S(2)}) collective-permute-start(bf16[512,256]{1,0:T(8,128)(2,1)S(1)} %get-tuple-element.59), channel_id=1, source_target_pairs={{0,8},{4,12},{8,0},{12,4},{16,24},{20,28},{24,16},{28,20},{1,9},{5... | collective-permute-start | bytes 786440 | tf_op jit(solution)/shard_map/ppermute | solution.py:762
  11.8 1.4 %pack_filters.3 = (bf16[512,256]{1,0:T(8,128)(2,1)S(1)}, bf16[512,256]{1,0:T(8,128)(2,1)S(1)}) custom-call(f32[4,128,1024]{2,1,0:T(8,128)} %bitcast.9), custom_call_target="tpu_custom_call" | custom-call | tf_op jit(solution)/shard_map/pack_filters/pallas_call | solution.py:243
  13.3 2.9 %collective-permute-done.2.refs_2_ = bf16[128,256]{1,0:T(8,128)(2,1)S(1)} collective-permute-done((bf16[128,256]{1,0:T(8,128)(2,1)S(1)}, bf16[128,256]{1,0:T(8,128)(2,1)S(1)}, u32[]{:S(2)}, u32[]{:S(2)}) %collective-permute-start.2) | collective-permute-done | bytes 65568 | tf_op jit(solution)/shard_map/ppermute | solution.py:762
  17.9 1.5 %forward.1.spectrum_ref = f32[256,2048]{1,0:T(8,128)S(1)} custom-call(f32[2,128,8]{2,1,0:T(8,128)S(1)} %copy-done.2, f32[2,128,8]{2,1,0:T(8,128)S(1)} %copy-done.1, bf16[256,256]{1,0:T(8,128)(2,1)S(1)} %copy-done.4, bf16[2,128,256]{2,1,0:T(8,128)(2,1)S(1)} %get-tuple-element.71.refs_0_, bf16[2,128,256]{2,1,0:T(8,128)(2,1)S(1)} %get-tuple-element.72.refs_1_, ...), custom_call_target="tpu_custom_call" | custom-call | tf_op jit(solution)/shard_map/forward/pallas_call | solution.py:409
  21.1 1.8 %collective-permute-start.13 = (bf16[384,256]{1,0:T(8,128)(2,1)S(1)}, bf16[384,256]{1,0:T(8,128)(2,1)S(1)}, u32[]{:S(2)}, u32[]{:S(2)}) collective-permute-start(bf16[384,256]{1,0:T(8,128)(2,1)S(1)} %get-tuple-element.84), channel_id=1, source_target_pairs={{0,24},{4,28},{8,16},{12,20},{16,8},{20,12},{24,0},{28,4},{1,25},{... | collective-permute-start | bytes 589832 | tf_op jit(solution)/shard_map/ppermute | solution.py:762
  24.2 2.0 %backward.1 = (f32[4,128,256]{2,1,0:T(8,128)S(1)}, bf16[2,128,256]{2,1,0:T(8,128)(2,1)S(1)}, bf16[2,128,256]{2,1,0:T(8,128)(2,1)S(1)}) custom-call(f32[2,128,8]{2,1,0:T(8,128)S(1)} %copy-done.2, f32[2,128,8]{2,1,0:T(8,128)S(1)} %copy-done.1, bf16[256,256]{1,0:T(8,128)(2,1)S(1)} %copy-done.3, f32[256,2048]{1,0:T(8,128)S(1)} %forward.1.spectrum_ref, ...), custom_call_target="tpu_custom_call" | custom-call | tf_op jit(solution)/shard_map/backward/pallas_call | solution.py:485
  26.7 1.7 %collective-permute-done.11.refs_5_.refs_0_ = bf16[384,256]{1,0:T(8,128)(2,1)S(1)} collective-permute-done((bf16[384,256]{1,0:T(8,128)(2,1)S(1)}, bf16[384,256]{1,0:T(8,128)(2,1)S(1)}, u32[]{:S(2)}, u32[]{:S(2)}) %collective-permute-start.11) | collective-permute-done | bytes 196640 | tf_op jit(solution)/shard_map/ppermute | solution.py:762
  28.4 3.4 %collective-permute-done.12.refs_6_.refs_1_ = bf16[384,256]{1,0:T(8,128)(2,1)S(1)} collective-permute-done((bf16[384,256]{1,0:T(8,128)(2,1)S(1)}, bf16[384,256]{1,0:T(8,128)(2,1)S(1)}, u32[]{:S(2)}, u32[]{:S(2)}) %collective-permute-start.12) | collective-permute-done | bytes 196640 | tf_op jit(solution)/shard_map/ppermute | solution.py:762
  32.0 1.5 %collective-permute-start.15 = (bf16[528,256]{1,0:T(8,128)(2,1)S(1)}, bf16[528,256]{1,0:T(8,128)(2,1)S(1)}, u32[]{:S(2)}, u32[]{:S(2)}) collective-permute-start(bf16[528,256]{1,0:T(8,128)(2,1)S(1)} %get-tuple-element.86), channel_id=1, source_target_pairs={{0,16},{4,20},{8,24},{12,28},{16,0},{20,4},{24,8},{28,12},{1,17},{... | collective-permute-start | bytes 811016 | tf_op jit(solution)/shard_map/ppermute | solution.py:762
  37.6 8.8 %collective-permute-done.16.refs_3_ = bf16[512,256]{1,0:T(8,128)(2,1)S(1)} collective-permute-done((bf16[512,256]{1,0:T(8,128)(2,1)S(1)}, bf16[512,256]{1,0:T(8,128)(2,1)S(1)}, u32[]{:S(2)}, u32[]{:S(2)}) %collective-permute-start.16) | collective-permute-done | bytes 262176 | tf_op jit(solution)/shard_map/ppermute | solution.py:762
  47.2 1.6 %collective-permute-start.23 = (bf16[2,512,128]{2,1,0:T(8,128)(2,1)S(1)}, bf16[2,512,128]{2,1,0:T(8,128)(2,1)S(1)}, u32[]{:S(2)}, u32[]{:S(2)}) collective-permute-start(bf16[2,512,128]{2,1,0:T(8,128)(2,1)S(1)} %get-tuple-element.101), channel_id=1, source_target_pairs={{0,1},{1,0},{2,3},{3,2},{4,5},{5,4},{6,7},{7,6},{8,9},{9,8},{10,11... | collective-permute-start | bytes 786440 | tf_op jit(solution)/shard_map/ppermute | solution.py:762
  51.0 1.3 %collective-permute-start.18 = (bf16[128,512]{1,0:T(8,128)(2,1)S(1)}, bf16[128,512]{1,0:T(8,128)(2,1)S(1)}, u32[]{:S(2)}, u32[]{:S(2)}) collective-permute-start(bf16[128,512]{1,0:T(8,128)(2,1)S(1)} %get-tuple-element.89), channel_id=1, source_target_pairs={{0,16},{4,20},{8,24},{12,28},{16,0},{20,4},{24,8},{28,12},{1,17},{... | collective-permute-start | bytes 393224 | tf_op jit(solution)/shard_map/ppermute | solution.py:762
  53.7 3.2 %collective-permute-start.24 = (bf16[512,128]{1,0:T(8,128)(2,1)S(1)}, bf16[512,128]{1,0:T(8,128)(2,1)S(1)}, u32[]{:S(2)}, u32[]{:S(2)}) collective-permute-start(bf16[512,128]{1,0:T(8,128)(2,1)S(1)} %fusion), channel_id=1, source_target_pairs={{0,2},{1,3},{2,0},{3,1},{4,6},{5,7},{6,4},{7,5},{8,10},{9,11},{10,... | collective-permute-start | bytes 393224 | tf_op jit(solution)/shard_map/ppermute | solution.py:762
  56.9 1.3 %collective-permute-done.19.refs_3_ = bf16[128,512]{1,0:T(8,128)(2,1)S(1)} collective-permute-done((bf16[128,512]{1,0:T(8,128)(2,1)S(1)}, bf16[128,512]{1,0:T(8,128)(2,1)S(1)}, u32[]{:S(2)}, u32[]{:S(2)}) %collective-permute-start.19) | collective-permute-done | bytes 131104 | tf_op jit(solution)/shard_map/ppermute | solution.py:762
  58.8 1.7 %collective-permute-done.24.second_ref = bf16[512,128]{1,0:T(8,128)(2,1)S(1)} collective-permute-done((bf16[512,128]{1,0:T(8,128)(2,1)S(1)}, bf16[512,128]{1,0:T(8,128)(2,1)S(1)}, u32[]{:S(2)}, u32[]{:S(2)}) %collective-permute-start.24) | collective-permute-done | bytes 131104 | tf_op jit(solution)/shard_map/ppermute | solution.py:762
  60.6 1.5 %collective-permute-start.25 = (bf16[128,128]{1,0:T(8,128)(2,1)S(1)}, bf16[128,128]{1,0:T(8,128)(2,1)S(1)}, u32[]{:S(2)}, u32[]{:S(2)}) collective-permute-start(bf16[128,128]{1,0:T(8,128)(2,1)S(1)} %get-tuple-element.103), channel_id=1, source_target_pairs={{0,8},{4,12},{8,0},{12,4},{16,24},{20,28},{24,16},{28,20},{1,9},{5... | collective-permute-start | bytes 98312 | tf_op jit(solution)/shard_map/ppermute | solution.py:762
  62.0 1.4 %collective-permute-start.20 = (bf16[128,512]{1,0:T(8,128)(2,1)S(1)}, bf16[128,512]{1,0:T(8,128)(2,1)S(1)}, u32[]{:S(2)}, u32[]{:S(2)}) collective-permute-start(bf16[128,512]{1,0:T(8,128)(2,1)S(1)} %get-tuple-element.92), channel_id=1, source_target_pairs={{0,1},{1,0},{2,3},{3,2},{4,5},{5,4},{6,7},{7,6},{8,9},{9,8},{10,11... | collective-permute-start | bytes 393224 | tf_op jit(solution)/shard_map/ppermute | solution.py:762
  65.0 2.7 %collective-permute-start.27 = (bf16[128,512]{1,0:T(8,128)(2,1)S(1)}, bf16[128,512]{1,0:T(8,128)(2,1)S(1)}, u32[]{:S(2)}, u32[]{:S(2)}) collective-permute-start(bf16[128,512]{1,0:T(8,128)(2,1)S(1)} %add.8), channel_id=1, source_target_pairs={{0,2},{1,3},{2,0},{3,1},{4,6},{5,7},{6,4},{7,5},{8,10},{9,11},{10,... | collective-permute-start | bytes 393224 | tf_op jit(solution)/shard_map/ppermute | solution.py:762
  67.6 1.3 %collective-permute-start.28 = (bf16[128,128]{1,0:T(8,128)(2,1)S(1)}, bf16[128,128]{1,0:T(8,128)(2,1)S(1)}, u32[]{:S(2)}, u32[]{:S(2)}) collective-permute-start(bf16[128,128]{1,0:T(8,128)(2,1)S(1)} %get-tuple-element.107), channel_id=1, source_target_pairs={{0,16},{4,20},{8,24},{12,28},{16,0},{20,4},{24,8},{28,12},{1,17},{... | collective-permute-start | bytes 98312 | tf_op jit(solution)/shard_map/ppermute | solution.py:762
  68.9 1.9 %collective-permute-start.29 = (bf16[128,128]{1,0:T(8,128)(2,1)S(1)}, bf16[128,128]{1,0:T(8,128)(2,1)S(1)}, u32[]{:S(2)}, u32[]{:S(2)}) collective-permute-start(bf16[128,128]{1,0:T(8,128)(2,1)S(1)} %get-tuple-element.108), channel_id=1, source_target_pairs={{0,24},{4,28},{8,16},{12,20},{16,8},{20,12},{24,0},{28,4},{1,25},{... | collective-permute-start | bytes 98312 | tf_op jit(solution)/shard_map/ppermute | solution.py:762
  71.5 2.2 %collective-permute-done.29.refs_3_ = bf16[128,128]{1,0:T(8,128)(2,1)S(1)} collective-permute-done((bf16[128,128]{1,0:T(8,128)(2,1)S(1)}, bf16[128,128]{1,0:T(8,128)(2,1)S(1)}, u32[]{:S(2)}, u32[]{:S(2)}) %collective-permute-start.29) | collective-permute-done | bytes 32800 | tf_op jit(solution)/shard_map/ppermute | solution.py:762
  (65 shorter events, 21.5 us)
Async XLA Ops:
  0.0 8.9 %collective-permute-start = (bf16[1024,512]{1,0:T(8,128)(2,1)}, bf16[1024,512]{1,0:T(8,128)(2,1)S(1)}, u32[]{:S(2)}, u32[]{:S(2)}) collective-permute-start(bf16[1024,512]{1,0:T(8,128)(2,1)} %own_ref.3), channel_id=1, source_target_pairs={{0,4},{4,0},{8,12},{12,8},{16,20},{20,16},{24,28},{28,24},{1,5},{5... | collective-permute-start | bytes 3145736 | tf_op jit(solution)/shard_map/ppermute | solution.py:762
  1.4 11.8 %collective-permute-start.3 = (bf16[128,256]{1,0:T(8,128)(2,1)S(1)}, bf16[128,256]{1,0:T(8,128)(2,1)S(1)}, u32[]{:S(2)}, u32[]{:S(2)}) collective-permute-start(bf16[128,256]{1,0:T(8,128)(2,1)S(1)} %get-tuple-element.69), channel_id=1, source_target_pairs={{0,24},{4,28},{8,16},{12,20},{16,8},{20,12},{24,0},{28,4},{1,25},{... | collective-permute-start | bytes 196616 | tf_op jit(solution)/shard_map/ppermute | solution.py:762
  6.3 14.8 %collective-permute-start.7 = (bf16[512,256]{1,0:T(8,128)(2,1)S(1)}, bf16[512,256]{1,0:T(8,128)(2,1)S(1)}, u32[]{:S(2)}, u32[]{:S(2)}) collective-permute-start(bf16[512,256]{1,0:T(8,128)(2,1)S(1)} %get-tuple-element.74), channel_id=1, source_target_pairs={{0,16},{4,20},{8,24},{12,28},{16,0},{20,4},{24,8},{28,12},{1,17},{... | collective-permute-start | bytes 786440 | tf_op jit(solution)/shard_map/ppermute | solution.py:762
  6.9 9.3 %collective-permute-start.2 = (bf16[128,256]{1,0:T(8,128)(2,1)S(1)}, bf16[128,256]{1,0:T(8,128)(2,1)S(1)}, u32[]{:S(2)}, u32[]{:S(2)}) collective-permute-start(bf16[128,256]{1,0:T(8,128)(2,1)S(1)} %get-tuple-element.67), channel_id=1, source_target_pairs={{0,16},{4,20},{8,24},{12,28},{16,0},{20,4},{24,8},{28,12},{1,17},{... | collective-permute-start | bytes 196616 | tf_op jit(solution)/shard_map/ppermute | solution.py:762
  8.4 7.8 %collective-permute-start.1 = (bf16[128,256]{1,0:T(8,128)(2,1)S(1)}, bf16[128,256]{1,0:T(8,128)(2,1)S(1)}, u32[]{:S(2)}, u32[]{:S(2)}) collective-permute-start(bf16[128,256]{1,0:T(8,128)(2,1)S(1)} %get-tuple-element.65), channel_id=1, source_target_pairs={{0,8},{4,12},{8,0},{12,4},{16,24},{20,28},{24,16},{28,20},{1,9},{5... | collective-permute-start | bytes 196616 | tf_op jit(solution)/shard_map/ppermute | solution.py:762
  9.0 14.0 %collective-permute-start.6 = (bf16[512,256]{1,0:T(8,128)(2,1)S(1)}, bf16[512,256]{1,0:T(8,128)(2,1)S(1)}, u32[]{:S(2)}, u32[]{:S(2)}) collective-permute-start(bf16[512,256]{1,0:T(8,128)(2,1)S(1)} %get-tuple-element.59), channel_id=1, source_target_pairs={{0,8},{4,12},{8,0},{12,4},{16,24},{20,28},{24,16},{28,20},{1,9},{5... | collective-permute-start | bytes 786440 | tf_op jit(solution)/shard_map/ppermute | solution.py:762
  13.2 11.0 %collective-permute-start.8 = (bf16[512,256]{1,0:T(8,128)(2,1)S(1)}, bf16[512,256]{1,0:T(8,128)(2,1)S(1)}, u32[]{:S(2)}, u32[]{:S(2)}) collective-permute-start(bf16[512,256]{1,0:T(8,128)(2,1)S(1)} %get-tuple-element.63), channel_id=1, source_target_pairs={{0,24},{4,28},{8,16},{12,20},{16,8},{20,12},{24,0},{28,4},{1,25},{... | collective-permute-start | bytes 786440 | tf_op jit(solution)/shard_map/ppermute | solution.py:762
  19.4 9.1 %collective-permute-start.11 = (bf16[384,256]{1,0:T(8,128)(2,1)S(1)}, bf16[384,256]{1,0:T(8,128)(2,1)S(1)}, u32[]{:S(2)}, u32[]{:S(2)}) collective-permute-start(bf16[384,256]{1,0:T(8,128)(2,1)S(1)} %get-tuple-element.80), channel_id=1, source_target_pairs={{0,8},{4,12},{8,0},{12,4},{16,24},{20,28},{24,16},{28,20},{1,9},{5... | collective-permute-start | bytes 589832 | tf_op jit(solution)/shard_map/ppermute | solution.py:762
  20.0 11.8 %collective-permute-start.12 = (bf16[384,256]{1,0:T(8,128)(2,1)S(1)}, bf16[384,256]{1,0:T(8,128)(2,1)S(1)}, u32[]{:S(2)}, u32[]{:S(2)}) collective-permute-start(bf16[384,256]{1,0:T(8,128)(2,1)S(1)} %get-tuple-element.82), channel_id=1, source_target_pairs={{0,16},{4,20},{8,24},{12,28},{16,0},{20,4},{24,8},{28,12},{1,17},{... | collective-permute-start | bytes 589832 | tf_op jit(solution)/shard_map/ppermute | solution.py:762
  21.1 10.7 %collective-permute-start.13 = (bf16[384,256]{1,0:T(8,128)(2,1)S(1)}, bf16[384,256]{1,0:T(8,128)(2,1)S(1)}, u32[]{:S(2)}, u32[]{:S(2)}) collective-permute-start(bf16[384,256]{1,0:T(8,128)(2,1)S(1)} %get-tuple-element.84), channel_id=1, source_target_pairs={{0,24},{4,28},{8,16},{12,20},{16,8},{20,12},{24,0},{28,4},{1,25},{... | collective-permute-start | bytes 589832 | tf_op jit(solution)/shard_map/ppermute | solution.py:762
  26.2 5.6 %collective-permute-start.9 = (bf16[2,128,256]{2,1,0:T(8,128)(2,1)S(1)}, bf16[2,128,256]{2,1,0:T(8,128)(2,1)S(1)}, u32[]{:S(2)}, u32[]{:S(2)}) collective-permute-start(bf16[2,128,256]{2,1,0:T(8,128)(2,1)S(1)} %get-tuple-element.76), channel_id=1, source_target_pairs={{0,4},{4,0},{8,12},{12,8},{16,20},{20,16},{24,28},{28,24},{1,5},{5... | collective-permute-start | bytes 393224 | tf_op jit(solution)/shard_map/ppermute | solution.py:762
  26.3 5.6 %collective-permute-start.10 = (bf16[2,128,256]{2,1,0:T(8,128)(2,1)S(1)}, bf16[2,128,256]{2,1,0:T(8,128)(2,1)S(1)}, u32[]{:S(2)}, u32[]{:S(2)}) collective-permute-start(bf16[2,128,256]{2,1,0:T(8,128)(2,1)S(1)} %get-tuple-element.77), channel_id=1, source_target_pairs={{0,4},{4,0},{8,12},{12,8},{16,20},{20,16},{24,28},{28,24},{1,5},{5... | collective-permute-start | bytes 393224 | tf_op jit(solution)/shard_map/ppermute | solution.py:762
  32.0 14.4 %collective-permute-start.15 = (bf16[528,256]{1,0:T(8,128)(2,1)S(1)}, bf16[528,256]{1,0:T(8,128)(2,1)S(1)}, u32[]{:S(2)}, u32[]{:S(2)}) collective-permute-start(bf16[528,256]{1,0:T(8,128)(2,1)S(1)} %get-tuple-element.86), channel_id=1, source_target_pairs={{0,16},{4,20},{8,24},{12,28},{16,0},{20,4},{24,8},{28,12},{1,17},{... | collective-permute-start | bytes 811016 | tf_op jit(solution)/shard_map/ppermute | solution.py:762
  33.5 12.9 %collective-permute-start.14 = (bf16[528,256]{1,0:T(8,128)(2,1)S(1)}, bf16[528,256]{1,0:T(8,128)(2,1)S(1)}, u32[]{:S(2)}, u32[]{:S(2)}) collective-permute-start(bf16[528,256]{1,0:T(8,128)(2,1)S(1)} %get-tuple-element.86), channel_id=1, source_target_pairs={{0,8},{4,12},{8,0},{12,4},{16,24},{20,28},{24,16},{28,20},{1,9},{5... | collective-permute-start | bytes 811016 | tf_op jit(solution)/shard_map/ppermute | solution.py:762
  34.6 11.8 %collective-permute-start.16 = (bf16[512,256]{1,0:T(8,128)(2,1)S(1)}, bf16[512,256]{1,0:T(8,128)(2,1)S(1)}, u32[]{:S(2)}, u32[]{:S(2)}) collective-permute-start(bf16[512,256]{1,0:T(8,128)(2,1)S(1)} %get-tuple-element.85.refs_0_), channel_id=1, source_target_pairs={{0,24},{4,28},{8,16},{12,20},{16,8},{20,12},{24,0},{28,4},{1,25},{... | collective-permute-start | bytes 786440 | tf_op jit(solution)/shard_map/ppermute | solution.py:762
  47.2 6.4 %collective-permute-start.23 = (bf16[2,512,128]{2,1,0:T(8,128)(2,1)S(1)}, bf16[2,512,128]{2,1,0:T(8,128)(2,1)S(1)}, u32[]{:S(2)}, u32[]{:S(2)}) collective-permute-start(bf16[2,512,128]{2,1,0:T(8,128)(2,1)S(1)} %get-tuple-element.101), channel_id=1, source_target_pairs={{0,1},{1,0},{2,3},{3,2},{4,5},{5,4},{6,7},{7,6},{8,9},{9,8},{10,11... | collective-permute-start | bytes 786440 | tf_op jit(solution)/shard_map/ppermute | solution.py:762
  49.8 7.2 %collective-permute-start.17 = (bf16[128,512]{1,0:T(8,128)(2,1)S(1)}, bf16[128,512]{1,0:T(8,128)(2,1)S(1)}, u32[]{:S(2)}, u32[]{:S(2)}) collective-permute-start(bf16[128,512]{1,0:T(8,128)(2,1)S(1)} %get-tuple-element.88), channel_id=1, source_target_pairs={{0,8},{4,12},{8,0},{12,4},{16,24},{20,28},{24,16},{28,20},{1,9},{5... | collective-permute-start | bytes 393224 | tf_op jit(solution)/shard_map/ppermute | solution.py:762
  51.0 5.9 %collective-permute-start.18 = (bf16[128,512]{1,0:T(8,128)(2,1)S(1)}, bf16[128,512]{1,0:T(8,128)(2,1)S(1)}, u32[]{:S(2)}, u32[]{:S(2)}) collective-permute-start(bf16[128,512]{1,0:T(8,128)(2,1)S(1)} %get-tuple-element.89), channel_id=1, source_target_pairs={{0,16},{4,20},{8,24},{12,28},{16,0},{20,4},{24,8},{28,12},{1,17},{... | collective-permute-start | bytes 393224 | tf_op jit(solution)/shard_map/ppermute | solution.py:762
  52.4 5.9 %collective-permute-start.19 = (bf16[128,512]{1,0:T(8,128)(2,1)S(1)}, bf16[128,512]{1,0:T(8,128)(2,1)S(1)}, u32[]{:S(2)}, u32[]{:S(2)}) collective-permute-start(bf16[128,512]{1,0:T(8,128)(2,1)S(1)} %get-tuple-element.90), channel_id=1, source_target_pairs={{0,24},{4,28},{8,16},{12,20},{16,8},{20,12},{24,0},{28,4},{1,25},{... | collective-permute-start | bytes 393224 | tf_op jit(solution)/shard_map/ppermute | solution.py:762
  53.7 6.8 %collective-permute-start.24 = (bf16[512,128]{1,0:T(8,128)(2,1)S(1)}, bf16[512,128]{1,0:T(8,128)(2,1)S(1)}, u32[]{:S(2)}, u32[]{:S(2)}) collective-permute-start(bf16[512,128]{1,0:T(8,128)(2,1)S(1)} %fusion), channel_id=1, source_target_pairs={{0,2},{1,3},{2,0},{3,1},{4,6},{5,7},{6,4},{7,5},{8,10},{9,11},{10,... | collective-permute-start | bytes 393224 | tf_op jit(solution)/shard_map/ppermute | solution.py:762
  58.3 6.6 %collective-permute-start.26 = (bf16[128,512]{1,0:T(8,128)(2,1)S(1)}, bf16[128,512]{1,0:T(8,128)(2,1)S(1)}, u32[]{:S(2)}, u32[]{:S(2)}) collective-permute-start(bf16[128,512]{1,0:T(8,128)(2,1)S(1)} %get-tuple-element.105), channel_id=1, source_target_pairs={{0,1},{1,0},{2,3},{3,2},{4,5},{5,4},{6,7},{7,6},{8,9},{9,8},{10,11... | collective-permute-start | bytes 393224 | tf_op jit(solution)/shard_map/ppermute | solution.py:762
  62.0 8.8 %collective-permute-start.20 = (bf16[128,512]{1,0:T(8,128)(2,1)S(1)}, bf16[128,512]{1,0:T(8,128)(2,1)S(1)}, u32[]{:S(2)}, u32[]{:S(2)}) collective-permute-start(bf16[128,512]{1,0:T(8,128)(2,1)S(1)} %get-tuple-element.92), channel_id=1, source_target_pairs={{0,1},{1,0},{2,3},{3,2},{4,5},{5,4},{6,7},{7,6},{8,9},{9,8},{10,11... | collective-permute-start | bytes 393224 | tf_op jit(solution)/shard_map/ppermute | solution.py:762
  65.0 8.8 %collective-permute-start.27 = (bf16[128,512]{1,0:T(8,128)(2,1)S(1)}, bf16[128,512]{1,0:T(8,128)(2,1)S(1)}, u32[]{:S(2)}, u32[]{:S(2)}) collective-permute-start(bf16[128,512]{1,0:T(8,128)(2,1)S(1)} %add.8), channel_id=1, source_target_pairs={{0,2},{1,3},{2,0},{3,1},{4,6},{5,7},{6,4},{7,5},{8,10},{9,11},{10,... | collective-permute-start | bytes 393224 | tf_op jit(solution)/shard_map/ppermute | solution.py:762
  68.9 4.8 %collective-permute-start.29 = (bf16[128,128]{1,0:T(8,128)(2,1)S(1)}, bf16[128,128]{1,0:T(8,128)(2,1)S(1)}, u32[]{:S(2)}, u32[]{:S(2)}) collective-permute-start(bf16[128,128]{1,0:T(8,128)(2,1)S(1)} %get-tuple-element.108), channel_id=1, source_target_pairs={{0,24},{4,28},{8,16},{12,20},{16,8},{20,12},{24,0},{28,4},{1,25},{... | collective-permute-start | bytes 98312 | tf_op jit(solution)/shard_map/ppermute | solution.py:762
  (12 other events, 75.7 us)

commit v20 on v19

--- a/solution.py
+++ b/solution.py
@@ -800,7 +800,7 @@
     keep, passed, send = project_moved(arrange(mine, moved[1:], others), gathered)
     blocks = to_chips(finish(keep, *over_layers(passed, send), chips))
     keep, near, passed, far = sort_blocks(to_chips(project_still(out_weight, other_weight, gathered)))
-    second = swapped(add(after(passed, blocks[1]), swapped(far, "chan", 1), 0), "chan", 2)
+    second = swapped(add(after(passed, *blocks[1:3]), swapped(far, "chan", 1), 16), "chan", 2)
     return join(keep, swapped(near, "chan", 1), second, blocks)
 
 

time: 74.8 us -> 76.4 us (1.021)
  waiting for transfers between devices: 27.8 us -> 29.3 us
    ppermute x30, waiting for transfers between devices: 27.8 us -> 29.3 us  [swapped(): lax.ppermute(value, axis, [(source, source ^ offset) for source in range(...]
where the time goes in v20:
time: 76.4 us; the launch traced here: 76.2 us
  starting transfers between devices  35 us (46%)
  waiting for transfers between devices  29.3 us (38%)
  Pallas kernels  11.6 us (15%)
    ppermute x30, starting transfers between devices, swapped(): lax.ppermute(value, axis, [(source, source ^ offset) for source in range(...  35 us
    ppermute x30, waiting for transfers between devices, swapped(): lax.ppermute(value, axis, [(source, source ^ offset) for source in range(...  29.3 us
    pallas_call x2, Pallas kernels, pack_filters(): pl.pallas_call(functools.partial(pack_filters_kernel, offsets), in_specs=...  2.74 us
    pallas_call x1, Pallas kernels, backward(): pl.pallas_call(functools.partial(backward_kernel, chips), in_specs=[WHOLE...  2.01 us
  transfers between devices with their start and end apart: 30, of which 16 were waited for; matrix products, arithmetic and copies ran while one was open for 0% of the time, Pallas kernels for 13%

profile of v20, /device:TPU:0, one launch (start us, length us, event | category | flops | bytes accessed | tf_op | source)
XLA Modules:
  0.0 76.2 jit_solution(17355181086424489779)
XLA Ops:
  1.4 3.5 %collective-permute-start.3 = (bf16[128,256]{1,0:T(8,128)(2,1)S(1)}, bf16[128,256]{1,0:T(8,128)(2,1)S(1)}, u32[]{:S(2)}, u32[]{:S(2)}) collective-permute-start(bf16[128,256]{1,0:T(8,128)(2,1)S(1)} %get-tuple-element.69), channel_id=1, source_target_pairs={{0,24},{4,28},{8,16},{12,20},{16,8},{20,12},{24,0},{28,4},{1,25},{... | collective-permute-start | bytes 196616 | tf_op jit(solution)/shard_map/ppermute | solution.py:762
  4.9 1.4 %pack_filters.2 = (bf16[512,256]{1,0:T(8,128)(2,1)S(1)}, bf16[512,256]{1,0:T(8,128)(2,1)S(1)}) custom-call(f32[4,128,1024]{2,1,0:T(8,128)} %bitcast.8), custom_call_target="tpu_custom_call" | custom-call | tf_op jit(solution)/shard_map/pack_filters/pallas_call | solution.py:243
  6.9 1.5 %collective-permute-start.2 = (bf16[128,256]{1,0:T(8,128)(2,1)S(1)}, bf16[128,256]{1,0:T(8,128)(2,1)S(1)}, u32[]{:S(2)}, u32[]{:S(2)}) collective-permute-start(bf16[128,256]{1,0:T(8,128)(2,1)S(1)} %get-tuple-element.67), channel_id=1, source_target_pairs={{0,16},{4,20},{8,24},{12,28},{16,0},{20,4},{24,8},{28,12},{1,17},{... | collective-permute-start | bytes 196616 | tf_op jit(solution)/shard_map/ppermute | solution.py:762
  9.0 1.6 %collective-permute-start.6 = (bf16[512,256]{1,0:T(8,128)(2,1)S(1)}, bf16[512,256]{1,0:T(8,128)(2,1)S(1)}, u32[]{:S(2)}, u32[]{:S(2)}) collective-permute-start(bf16[512,256]{1,0:T(8,128)(2,1)S(1)} %get-tuple-element.59), channel_id=1, source_target_pairs={{0,8},{4,12},{8,0},{12,4},{16,24},{20,28},{24,16},{28,20},{1,9},{5... | collective-permute-start | bytes 786440 | tf_op jit(solution)/shard_map/ppermute | solution.py:762
  11.8 1.4 %pack_filters.3 = (bf16[512,256]{1,0:T(8,128)(2,1)S(1)}, bf16[512,256]{1,0:T(8,128)(2,1)S(1)}) custom-call(f32[4,128,1024]{2,1,0:T(8,128)} %bitcast.9), custom_call_target="tpu_custom_call" | custom-call | tf_op jit(solution)/shard_map/pack_filters/pallas_call | solution.py:243
  13.3 2.9 %collective-permute-done.2.refs_2_ = bf16[128,256]{1,0:T(8,128)(2,1)S(1)} collective-permute-done((bf16[128,256]{1,0:T(8,128)(2,1)S(1)}, bf16[128,256]{1,0:T(8,128)(2,1)S(1)}, u32[]{:S(2)}, u32[]{:S(2)}) %collective-permute-start.2) | collective-permute-done | bytes 65568 | tf_op jit(solution)/shard_map/ppermute | solution.py:762
  17.9 1.5 %forward.1.spectrum_ref = f32[256,2048]{1,0:T(8,128)S(1)} custom-call(f32[2,128,8]{2,1,0:T(8,128)S(1)} %copy-done.2, f32[2,128,8]{2,1,0:T(8,128)S(1)} %copy-done.1, bf16[256,256]{1,0:T(8,128)(2,1)S(1)} %copy-done.4, bf16[2,128,256]{2,1,0:T(8,128)(2,1)S(1)} %get-tuple-element.71.refs_0_, bf16[2,128,256]{2,1,0:T(8,128)(2,1)S(1)} %get-tuple-element.72.refs_1_, ...), custom_call_target="tpu_custom_call" | custom-call | tf_op jit(solution)/shard_map/forward/pallas_call | solution.py:409
  21.1 1.8 %collective-permute-start.13 = (bf16[384,256]{1,0:T(8,128)(2,1)S(1)}, bf16[384,256]{1,0:T(8,128)(2,1)S(1)}, u32[]{:S(2)}, u32[]{:S(2)}) collective-permute-start(bf16[384,256]{1,0:T(8,128)(2,1)S(1)} %get-tuple-element.84), channel_id=1, source_target_pairs={{0,24},{4,28},{8,16},{12,20},{16,8},{20,12},{24,0},{28,4},{1,25},{... | collective-permute-start | bytes 589832 | tf_op jit(solution)/shard_map/ppermute | solution.py:762
  24.2 2.0 %backward.1 = (f32[4,128,256]{2,1,0:T(8,128)S(1)}, bf16[2,128,256]{2,1,0:T(8,128)(2,1)S(1)}, bf16[2,128,256]{2,1,0:T(8,128)(2,1)S(1)}) custom-call(f32[2,128,8]{2,1,0:T(8,128)S(1)} %copy-done.2, f32[2,128,8]{2,1,0:T(8,128)S(1)} %copy-done.1, bf16[256,256]{1,0:T(8,128)(2,1)S(1)} %copy-done.3, f32[256,2048]{1,0:T(8,128)S(1)} %forward.1.spectrum_ref, ...), custom_call_target="tpu_custom_call" | custom-call | tf_op jit(solution)/shard_map/backward/pallas_call | solution.py:485
  26.7 1.7 %collective-permute-done.11.refs_5_.refs_0_ = bf16[384,256]{1,0:T(8,128)(2,1)S(1)} collective-permute-done((bf16[384,256]{1,0:T(8,128)(2,1)S(1)}, bf16[384,256]{1,0:T(8,128)(2,1)S(1)}, u32[]{:S(2)}, u32[]{:S(2)}) %collective-permute-start.11) | collective-permute-done | bytes 196640 | tf_op jit(solution)/shard_map/ppermute | solution.py:762
  28.4 3.4 %collective-permute-done.12.refs_6_.refs_1_ = bf16[384,256]{1,0:T(8,128)(2,1)S(1)} collective-permute-done((bf16[384,256]{1,0:T(8,128)(2,1)S(1)}, bf16[384,256]{1,0:T(8,128)(2,1)S(1)}, u32[]{:S(2)}, u32[]{:S(2)}) %collective-permute-start.12) | collective-permute-done | bytes 196640 | tf_op jit(solution)/shard_map/ppermute | solution.py:762
  32.0 1.5 %collective-permute-start.15 = (bf16[528,256]{1,0:T(8,128)(2,1)S(1)}, bf16[528,256]{1,0:T(8,128)(2,1)S(1)}, u32[]{:S(2)}, u32[]{:S(2)}) collective-permute-start(bf16[528,256]{1,0:T(8,128)(2,1)S(1)} %get-tuple-element.86), channel_id=1, source_target_pairs={{0,16},{4,20},{8,24},{12,28},{16,0},{20,4},{24,8},{28,12},{1,17},{... | collective-permute-start | bytes 811016 | tf_op jit(solution)/shard_map/ppermute | solution.py:762
  37.6 8.8 %collective-permute-done.16.refs_3_ = bf16[512,256]{1,0:T(8,128)(2,1)S(1)} collective-permute-done((bf16[512,256]{1,0:T(8,128)(2,1)S(1)}, bf16[512,256]{1,0:T(8,128)(2,1)S(1)}, u32[]{:S(2)}, u32[]{:S(2)}) %collective-permute-start.16) | collective-permute-done | bytes 262176 | tf_op jit(solution)/shard_map/ppermute | solution.py:762
  47.2 1.6 %collective-permute-start.23 = (bf16[2,512,128]{2,1,0:T(8,128)(2,1)S(1)}, bf16[2,512,128]{2,1,0:T(8,128)(2,1)S(1)}, u32[]{:S(2)}, u32[]{:S(2)}) collective-permute-start(bf16[2,512,128]{2,1,0:T(8,128)(2,1)S(1)} %get-tuple-element.101), channel_id=1, source_target_pairs={{0,1},{1,0},{2,3},{3,2},{4,5},{5,4},{6,7},{7,6},{8,9},{9,8},{10,11... | collective-permute-start | bytes 786440 | tf_op jit(solution)/shard_map/ppermute | solution.py:762
  53.7 3.2 %collective-permute-start.24 = (bf16[512,128]{1,0:T(8,128)(2,1)S(1)}, bf16[512,128]{1,0:T(8,128)(2,1)S(1)}, u32[]{:S(2)}, u32[]{:S(2)}) collective-permute-start(bf16[512,128]{1,0:T(8,128)(2,1)S(1)} %fusion), channel_id=1, source_target_pairs={{0,2},{1,3},{2,0},{3,1},{4,6},{5,7},{6,4},{7,5},{8,10},{9,11},{10,... | collective-permute-start | bytes 393224 | tf_op jit(solution)/shard_map/ppermute | solution.py:762
  58.8 1.7 %collective-permute-done.24.second_ref = bf16[512,128]{1,0:T(8,128)(2,1)S(1)} collective-permute-done((bf16[512,128]{1,0:T(8,128)(2,1)S(1)}, bf16[512,128]{1,0:T(8,128)(2,1)S(1)}, u32[]{:S(2)}, u32[]{:S(2)}) %collective-permute-start.24) | collective-permute-done | bytes 131104 | tf_op jit(solution)/shard_map/ppermute | solution.py:762
  60.6 1.5 %collective-permute-start.25 = (bf16[128,128]{1,0:T(8,128)(2,1)S(1)}, bf16[128,128]{1,0:T(8,128)(2,1)S(1)}, u32[]{:S(2)}, u32[]{:S(2)}) collective-permute-start(bf16[128,128]{1,0:T(8,128)(2,1)S(1)} %get-tuple-element.103), channel_id=1, source_target_pairs={{0,8},{4,12},{8,0},{12,4},{16,24},{20,28},{24,16},{28,20},{1,9},{5... | collective-permute-start | bytes 98312 | tf_op jit(solution)/shard_map/ppermute | solution.py:762
  63.1 1.4 %collective-permute-done.25.refs_1_ = bf16[128,128]{1,0:T(8,128)(2,1)S(1)} collective-permute-done((bf16[128,128]{1,0:T(8,128)(2,1)S(1)}, bf16[128,128]{1,0:T(8,128)(2,1)S(1)}, u32[]{:S(2)}, u32[]{:S(2)}) %collective-permute-start.25) | collective-permute-done | bytes 32800 | tf_op jit(solution)/shard_map/ppermute | solution.py:762
  64.5 1.4 %collective-permute-done.26.refs_2_ = bf16[128,128]{1,0:T(8,128)(2,1)S(1)} collective-permute-done((bf16[128,128]{1,0:T(8,128)(2,1)S(1)}, bf16[128,128]{1,0:T(8,128)(2,1)S(1)}, u32[]{:S(2)}, u32[]{:S(2)}) %collective-permute-start.26) | collective-permute-done | bytes 32800 | tf_op jit(solution)/shard_map/ppermute | solution.py:762
  66.0 2.3 %collective-permute-start.28 = (bf16[144,512]{1,0:T(8,128)(2,1)S(1)}, bf16[144,512]{1,0:T(8,128)(2,1)S(1)}, u32[]{:S(2)}, u32[]{:S(2)}) collective-permute-start(bf16[144,512]{1,0:T(8,128)(2,1)S(1)} %add.8), channel_id=1, source_target_pairs={{0,2},{1,3},{2,0},{3,1},{4,6},{5,7},{6,4},{7,5},{8,10},{9,11},{10,... | collective-permute-start | bytes 442376 | tf_op jit(solution)/shard_map/ppermute | solution.py:762
  68.3 2.3 %collective-permute-start.20 = (bf16[128,512]{1,0:T(8,128)(2,1)S(1)}, bf16[128,512]{1,0:T(8,128)(2,1)S(1)}, u32[]{:S(2)}, u32[]{:S(2)}) collective-permute-start(bf16[128,512]{1,0:T(8,128)(2,1)S(1)} %get-tuple-element.92), channel_id=1, source_target_pairs={{0,1},{1,0},{2,3},{3,2},{4,5},{5,4},{6,7},{7,6},{8,9},{9,8},{10,11... | collective-permute-start | bytes 393224 | tf_op jit(solution)/shard_map/ppermute | solution.py:762
  70.6 1.8 %collective-permute-start.29 = (bf16[128,128]{1,0:T(8,128)(2,1)S(1)}, bf16[128,128]{1,0:T(8,128)(2,1)S(1)}, u32[]{:S(2)}, u32[]{:S(2)}) collective-permute-start(bf16[128,128]{1,0:T(8,128)(2,1)S(1)} %get-tuple-element.108), channel_id=1, source_target_pairs={{0,24},{4,28},{8,16},{12,20},{16,8},{20,12},{24,0},{28,4},{1,25},{... | collective-permute-start | bytes 98312 | tf_op jit(solution)/shard_map/ppermute | solution.py:762
  72.4 1.6 %collective-permute-done.20.first_ref = bf16[128,512]{1,0:T(8,128)(2,1)S(1)} collective-permute-done((bf16[128,512]{1,0:T(8,128)(2,1)S(1)}, bf16[128,512]{1,0:T(8,128)(2,1)S(1)}, u32[]{:S(2)}, u32[]{:S(2)}) %collective-permute-start.20) | collective-permute-done | bytes 131104 | tf_op jit(solution)/shard_map/ppermute | solution.py:762
  74.0 1.5 %collective-permute-done.29.refs_3_ = bf16[128,128]{1,0:T(8,128)(2,1)S(1)} collective-permute-done((bf16[128,128]{1,0:T(8,128)(2,1)S(1)}, bf16[128,128]{1,0:T(8,128)(2,1)S(1)}, u32[]{:S(2)}, u32[]{:S(2)}) %collective-permute-start.29) | collective-permute-done | bytes 32800 | tf_op jit(solution)/shard_map/ppermute | solution.py:762
  (65 shorter events, 23.0 us)
Async XLA Ops:
  0.0 8.9 %collective-permute-start = (bf16[1024,512]{1,0:T(8,128)(2,1)}, bf16[1024,512]{1,0:T(8,128)(2,1)S(1)}, u32[]{:S(2)}, u32[]{:S(2)}) collective-permute-start(bf16[1024,512]{1,0:T(8,128)(2,1)} %own_ref.3), channel_id=1, source_target_pairs={{0,4},{4,0},{8,12},{12,8},{16,20},{20,16},{24,28},{28,24},{1,5},{5... | collective-permute-start | bytes 3145736 | tf_op jit(solution)/shard_map/ppermute | solution.py:762
  1.4 11.8 %collective-permute-start.3 = (bf16[128,256]{1,0:T(8,128)(2,1)S(1)}, bf16[128,256]{1,0:T(8,128)(2,1)S(1)}, u32[]{:S(2)}, u32[]{:S(2)}) collective-permute-start(bf16[128,256]{1,0:T(8,128)(2,1)S(1)} %get-tuple-element.69), channel_id=1, source_target_pairs={{0,24},{4,28},{8,16},{12,20},{16,8},{20,12},{24,0},{28,4},{1,25},{... | collective-permute-start | bytes 196616 | tf_op jit(solution)/shard_map/ppermute | solution.py:762
  6.3 14.8 %collective-permute-start.7 = (bf16[512,256]{1,0:T(8,128)(2,1)S(1)}, bf16[512,256]{1,0:T(8,128)(2,1)S(1)}, u32[]{:S(2)}, u32[]{:S(2)}) collective-permute-start(bf16[512,256]{1,0:T(8,128)(2,1)S(1)} %get-tuple-element.74), channel_id=1, source_target_pairs={{0,16},{4,20},{8,24},{12,28},{16,0},{20,4},{24,8},{28,12},{1,17},{... | collective-permute-start | bytes 786440 | tf_op jit(solution)/shard_map/ppermute | solution.py:762
  6.9 9.3 %collective-permute-start.2 = (bf16[128,256]{1,0:T(8,128)(2,1)S(1)}, bf16[128,256]{1,0:T(8,128)(2,1)S(1)}, u32[]{:S(2)}, u32[]{:S(2)}) collective-permute-start(bf16[128,256]{1,0:T(8,128)(2,1)S(1)} %get-tuple-element.67), channel_id=1, source_target_pairs={{0,16},{4,20},{8,24},{12,28},{16,0},{20,4},{24,8},{28,12},{1,17},{... | collective-permute-start | bytes 196616 | tf_op jit(solution)/shard_map/ppermute | solution.py:762
  8.4 7.8 %collective-permute-start.1 = (bf16[128,256]{1,0:T(8,128)(2,1)S(1)}, bf16[128,256]{1,0:T(8,128)(2,1)S(1)}, u32[]{:S(2)}, u32[]{:S(2)}) collective-permute-start(bf16[128,256]{1,0:T(8,128)(2,1)S(1)} %get-tuple-element.65), channel_id=1, source_target_pairs={{0,8},{4,12},{8,0},{12,4},{16,24},{20,28},{24,16},{28,20},{1,9},{5... | collective-permute-start | bytes 196616 | tf_op jit(solution)/shard_map/ppermute | solution.py:762
  9.0 14.0 %collective-permute-start.6 = (bf16[512,256]{1,0:T(8,128)(2,1)S(1)}, bf16[512,256]{1,0:T(8,128)(2,1)S(1)}, u32[]{:S(2)}, u32[]{:S(2)}) collective-permute-start(bf16[512,256]{1,0:T(8,128)(2,1)S(1)} %get-tuple-element.59), channel_id=1, source_target_pairs={{0,8},{4,12},{8,0},{12,4},{16,24},{20,28},{24,16},{28,20},{1,9},{5... | collective-permute-start | bytes 786440 | tf_op jit(solution)/shard_map/ppermute | solution.py:762
  13.2 11.0 %collective-permute-start.8 = (bf16[512,256]{1,0:T(8,128)(2,1)S(1)}, bf16[512,256]{1,0:T(8,128)(2,1)S(1)}, u32[]{:S(2)}, u32[]{:S(2)}) collective-permute-start(bf16[512,256]{1,0:T(8,128)(2,1)S(1)} %get-tuple-element.63), channel_id=1, source_target_pairs={{0,24},{4,28},{8,16},{12,20},{16,8},{20,12},{24,0},{28,4},{1,25},{... | collective-permute-start | bytes 786440 | tf_op jit(solution)/shard_map/ppermute | solution.py:762
  19.4 9.1 %collective-permute-start.11 = (bf16[384,256]{1,0:T(8,128)(2,1)S(1)}, bf16[384,256]{1,0:T(8,128)(2,1)S(1)}, u32[]{:S(2)}, u32[]{:S(2)}) collective-permute-start(bf16[384,256]{1,0:T(8,128)(2,1)S(1)} %get-tuple-element.80), channel_id=1, source_target_pairs={{0,8},{4,12},{8,0},{12,4},{16,24},{20,28},{24,16},{28,20},{1,9},{5... | collective-permute-start | bytes 589832 | tf_op jit(solution)/shard_map/ppermute | solution.py:762
  20.0 11.8 %collective-permute-start.12 = (bf16[384,256]{1,0:T(8,128)(2,1)S(1)}, bf16[384,256]{1,0:T(8,128)(2,1)S(1)}, u32[]{:S(2)}, u32[]{:S(2)}) collective-permute-start(bf16[384,256]{1,0:T(8,128)(2,1)S(1)} %get-tuple-element.82), channel_id=1, source_target_pairs={{0,16},{4,20},{8,24},{12,28},{16,0},{20,4},{24,8},{28,12},{1,17},{... | collective-permute-start | bytes 589832 | tf_op jit(solution)/shard_map/ppermute | solution.py:762
  21.1 10.7 %collective-permute-start.13 = (bf16[384,256]{1,0:T(8,128)(2,1)S(1)}, bf16[384,256]{1,0:T(8,128)(2,1)S(1)}, u32[]{:S(2)}, u32[]{:S(2)}) collective-permute-start(bf16[384,256]{1,0:T(8,128)(2,1)S(1)} %get-tuple-element.84), channel_id=1, source_target_pairs={{0,24},{4,28},{8,16},{12,20},{16,8},{20,12},{24,0},{28,4},{1,25},{... | collective-permute-start | bytes 589832 | tf_op jit(solution)/shard_map/ppermute | solution.py:762
  26.2 5.6 %collective-permute-start.9 = (bf16[2,128,256]{2,1,0:T(8,128)(2,1)S(1)}, bf16[2,128,256]{2,1,0:T(8,128)(2,1)S(1)}, u32[]{:S(2)}, u32[]{:S(2)}) collective-permute-start(bf16[2,128,256]{2,1,0:T(8,128)(2,1)S(1)} %get-tuple-element.76), channel_id=1, source_target_pairs={{0,4},{4,0},{8,12},{12,8},{16,20},{20,16},{24,28},{28,24},{1,5},{5... | collective-permute-start | bytes 393224 | tf_op jit(solution)/shard_map/ppermute | solution.py:762
  26.3 5.6 %collective-permute-start.10 = (bf16[2,128,256]{2,1,0:T(8,128)(2,1)S(1)}, bf16[2,128,256]{2,1,0:T(8,128)(2,1)S(1)}, u32[]{:S(2)}, u32[]{:S(2)}) collective-permute-start(bf16[2,128,256]{2,1,0:T(8,128)(2,1)S(1)} %get-tuple-element.77), channel_id=1, source_target_pairs={{0,4},{4,0},{8,12},{12,8},{16,20},{20,16},{24,28},{28,24},{1,5},{5... | collective-permute-start | bytes 393224 | tf_op jit(solution)/shard_map/ppermute | solution.py:762
  32.0 14.4 %collective-permute-start.15 = (bf16[528,256]{1,0:T(8,128)(2,1)S(1)}, bf16[528,256]{1,0:T(8,128)(2,1)S(1)}, u32[]{:S(2)}, u32[]{:S(2)}) collective-permute-start(bf16[528,256]{1,0:T(8,128)(2,1)S(1)} %get-tuple-element.86), channel_id=1, source_target_pairs={{0,16},{4,20},{8,24},{12,28},{16,0},{20,4},{24,8},{28,12},{1,17},{... | collective-permute-start | bytes 811016 | tf_op jit(solution)/shard_map/ppermute | solution.py:762
  33.5 12.9 %collective-permute-start.14 = (bf16[528,256]{1,0:T(8,128)(2,1)S(1)}, bf16[528,256]{1,0:T(8,128)(2,1)S(1)}, u32[]{:S(2)}, u32[]{:S(2)}) collective-permute-start(bf16[528,256]{1,0:T(8,128)(2,1)S(1)} %get-tuple-element.86), channel_id=1, source_target_pairs={{0,8},{4,12},{8,0},{12,4},{16,24},{20,28},{24,16},{28,20},{1,9},{5... | collective-permute-start | bytes 811016 | tf_op jit(solution)/shard_map/ppermute | solution.py:762
  34.6 11.8 %collective-permute-start.16 = (bf16[512,256]{1,0:T(8,128)(2,1)S(1)}, bf16[512,256]{1,0:T(8,128)(2,1)S(1)}, u32[]{:S(2)}, u32[]{:S(2)}) collective-permute-start(bf16[512,256]{1,0:T(8,128)(2,1)S(1)} %get-tuple-element.85.refs_0_), channel_id=1, source_target_pairs={{0,24},{4,28},{8,16},{12,20},{16,8},{20,12},{24,0},{28,4},{1,25},{... | collective-permute-start | bytes 786440 | tf_op jit(solution)/shard_map/ppermute | solution.py:762
  47.2 6.4 %collective-permute-start.23 = (bf16[2,512,128]{2,1,0:T(8,128)(2,1)S(1)}, bf16[2,512,128]{2,1,0:T(8,128)(2,1)S(1)}, u32[]{:S(2)}, u32[]{:S(2)}) collective-permute-start(bf16[2,512,128]{2,1,0:T(8,128)(2,1)S(1)} %get-tuple-element.101), channel_id=1, source_target_pairs={{0,1},{1,0},{2,3},{3,2},{4,5},{5,4},{6,7},{7,6},{8,9},{9,8},{10,11... | collective-permute-start | bytes 786440 | tf_op jit(solution)/shard_map/ppermute | solution.py:762
  49.8 7.2 %collective-permute-start.17 = (bf16[128,512]{1,0:T(8,128)(2,1)S(1)}, bf16[128,512]{1,0:T(8,128)(2,1)S(1)}, u32[]{:S(2)}, u32[]{:S(2)}) collective-permute-start(bf16[128,512]{1,0:T(8,128)(2,1)S(1)} %get-tuple-element.88), channel_id=1, source_target_pairs={{0,8},{4,12},{8,0},{12,4},{16,24},{20,28},{24,16},{28,20},{1,9},{5... | collective-permute-start | bytes 393224 | tf_op jit(solution)/shard_map/ppermute | solution.py:762
  51.0 5.9 %collective-permute-start.18 = (bf16[128,512]{1,0:T(8,128)(2,1)S(1)}, bf16[128,512]{1,0:T(8,128)(2,1)S(1)}, u32[]{:S(2)}, u32[]{:S(2)}) collective-permute-start(bf16[128,512]{1,0:T(8,128)(2,1)S(1)} %get-tuple-element.89), channel_id=1, source_target_pairs={{0,16},{4,20},{8,24},{12,28},{16,0},{20,4},{24,8},{28,12},{1,17},{... | collective-permute-start | bytes 393224 | tf_op jit(solution)/shard_map/ppermute | solution.py:762
  52.4 5.9 %collective-permute-start.19 = (bf16[128,512]{1,0:T(8,128)(2,1)S(1)}, bf16[128,512]{1,0:T(8,128)(2,1)S(1)}, u32[]{:S(2)}, u32[]{:S(2)}) collective-permute-start(bf16[128,512]{1,0:T(8,128)(2,1)S(1)} %get-tuple-element.90), channel_id=1, source_target_pairs={{0,24},{4,28},{8,16},{12,20},{16,8},{20,12},{24,0},{28,4},{1,25},{... | collective-permute-start | bytes 393224 | tf_op jit(solution)/shard_map/ppermute | solution.py:762
  53.7 6.8 %collective-permute-start.24 = (bf16[512,128]{1,0:T(8,128)(2,1)S(1)}, bf16[512,128]{1,0:T(8,128)(2,1)S(1)}, u32[]{:S(2)}, u32[]{:S(2)}) collective-permute-start(bf16[512,128]{1,0:T(8,128)(2,1)S(1)} %fusion), channel_id=1, source_target_pairs={{0,2},{1,3},{2,0},{3,1},{4,6},{5,7},{6,4},{7,5},{8,10},{9,11},{10,... | collective-permute-start | bytes 393224 | tf_op jit(solution)/shard_map/ppermute | solution.py:762
  58.3 7.6 %collective-permute-start.27 = (bf16[128,512]{1,0:T(8,128)(2,1)S(1)}, bf16[128,512]{1,0:T(8,128)(2,1)S(1)}, u32[]{:S(2)}, u32[]{:S(2)}) collective-permute-start(bf16[128,512]{1,0:T(8,128)(2,1)S(1)} %get-tuple-element.106), channel_id=1, source_target_pairs={{0,1},{1,0},{2,3},{3,2},{4,5},{5,4},{6,7},{7,6},{8,9},{9,8},{10,11... | collective-permute-start | bytes 393224 | tf_op jit(solution)/shard_map/ppermute | solution.py:762
  66.0 9.4 %collective-permute-start.28 = (bf16[144,512]{1,0:T(8,128)(2,1)S(1)}, bf16[144,512]{1,0:T(8,128)(2,1)S(1)}, u32[]{:S(2)}, u32[]{:S(2)}) collective-permute-start(bf16[144,512]{1,0:T(8,128)(2,1)S(1)} %add.8), channel_id=1, source_target_pairs={{0,2},{1,3},{2,0},{3,1},{4,6},{5,7},{6,4},{7,5},{8,10},{9,11},{10,... | collective-permute-start | bytes 442376 | tf_op jit(solution)/shard_map/ppermute | solution.py:762
  68.3 5.7 %collective-permute-start.20 = (bf16[128,512]{1,0:T(8,128)(2,1)S(1)}, bf16[128,512]{1,0:T(8,128)(2,1)S(1)}, u32[]{:S(2)}, u32[]{:S(2)}) collective-permute-start(bf16[128,512]{1,0:T(8,128)(2,1)S(1)} %get-tuple-element.92), channel_id=1, source_target_pairs={{0,1},{1,0},{2,3},{3,2},{4,5},{5,4},{6,7},{7,6},{8,9},{9,8},{10,11... | collective-permute-start | bytes 393224 | tf_op jit(solution)/shard_map/ppermute | solution.py:762
  70.6 4.8 %collective-permute-start.29 = (bf16[128,128]{1,0:T(8,128)(2,1)S(1)}, bf16[128,128]{1,0:T(8,128)(2,1)S(1)}, u32[]{:S(2)}, u32[]{:S(2)}) collective-permute-start(bf16[128,128]{1,0:T(8,128)(2,1)S(1)} %get-tuple-element.108), channel_id=1, source_target_pairs={{0,24},{4,28},{8,16},{12,20},{16,8},{20,12},{24,0},{28,4},{1,25},{... | collective-permute-start | bytes 98312 | tf_op jit(solution)/shard_map/ppermute | solution.py:762
  (12 other events, 75.7 us)

commit v21 on v20

--- a/solution.py
+++ b/solution.py
@@ -800,7 +800,7 @@
     keep, passed, send = project_moved(arrange(mine, moved[1:], others), gathered)
     blocks = to_chips(finish(keep, *over_layers(passed, send), chips))
     keep, near, passed, far = sort_blocks(to_chips(project_still(out_weight, other_weight, gathered)))
-    second = swapped(add(after(passed, *blocks[1:3]), swapped(far, "chan", 1), 16), "chan", 2)
+    second = swapped(add(after(passed, blocks[3]), swapped(far, "chan", 1), 0), "chan", 2)
     return join(keep, swapped(near, "chan", 1), second, blocks)
 
 

time: 76.4 us -> 74.2 us (0.971)
  waiting for transfers between devices: 29.3 us -> 27 us
    ppermute x30, waiting for transfers between devices: 29.3 us -> 27 us  [swapped(): lax.ppermute(value, axis, [(source, source ^ offset) for source in range(...]
  transfers between devices with their start and end apart: 30 -> 30, of which waited for: 16 -> 15; matrix products, arithmetic and copies ran while one was open for 0% -> 0% of each run, Pallas kernels for 13% -> 13%
where the time goes in v21:
time: 74.2 us; the launch traced here: 73.9 us
  starting transfers between devices  35.1 us (47%)
  waiting for transfers between devices  27 us (36%)
  Pallas kernels  11.6 us (16%)
    ppermute x30, starting transfers between devices, swapped(): lax.ppermute(value, axis, [(source, source ^ offset) for source in range(...  35.1 us
    ppermute x30, waiting for transfers between devices, swapped(): lax.ppermute(value, axis, [(source, source ^ offset) for source in range(...  27 us
    pallas_call x2, Pallas kernels, pack_filters(): pl.pallas_call(functools.partial(pack_filters_kernel, offsets), in_specs=...  2.74 us
    pallas_call x1, Pallas kernels, backward(): pl.pallas_call(functools.partial(backward_kernel, chips), in_specs=[WHOLE...  2.01 us
  transfers between devices with their start and end apart: 30, of which 15 were waited for; matrix products, arithmetic and copies ran while one was open for 0% of the time, Pallas kernels for 13%

profile of v21, /device:TPU:0, one launch (start us, length us, event | category | flops | bytes accessed | tf_op | source)
XLA Modules:
  0.0 73.9 jit_solution(906859216225309336)
XLA Ops:
  1.4 3.5 %collective-permute-start.3 = (bf16[128,256]{1,0:T(8,128)(2,1)S(1)}, bf16[128,256]{1,0:T(8,128)(2,1)S(1)}, u32[]{:S(2)}, u32[]{:S(2)}) collective-permute-start(bf16[128,256]{1,0:T(8,128)(2,1)S(1)} %get-tuple-element.69), channel_id=1, source_target_pairs={{0,24},{4,28},{8,16},{12,20},{16,8},{20,12},{24,0},{28,4},{1,25},{... | collective-permute-start | bytes 196616 | tf_op jit(solution)/shard_map/ppermute | solution.py:762
  4.9 1.4 %pack_filters.2 = (bf16[512,256]{1,0:T(8,128)(2,1)S(1)}, bf16[512,256]{1,0:T(8,128)(2,1)S(1)}) custom-call(f32[4,128,1024]{2,1,0:T(8,128)} %bitcast.8), custom_call_target="tpu_custom_call" | custom-call | tf_op jit(solution)/shard_map/pack_filters/pallas_call | solution.py:243
  6.9 1.5 %collective-permute-start.2 = (bf16[128,256]{1,0:T(8,128)(2,1)S(1)}, bf16[128,256]{1,0:T(8,128)(2,1)S(1)}, u32[]{:S(2)}, u32[]{:S(2)}) collective-permute-start(bf16[128,256]{1,0:T(8,128)(2,1)S(1)} %get-tuple-element.67), channel_id=1, source_target_pairs={{0,16},{4,20},{8,24},{12,28},{16,0},{20,4},{24,8},{28,12},{1,17},{... | collective-permute-start | bytes 196616 | tf_op jit(solution)/shard_map/ppermute | solution.py:762
  9.0 1.6 %collective-permute-start.6 = (bf16[512,256]{1,0:T(8,128)(2,1)S(1)}, bf16[512,256]{1,0:T(8,128)(2,1)S(1)}, u32[]{:S(2)}, u32[]{:S(2)}) collective-permute-start(bf16[512,256]{1,0:T(8,128)(2,1)S(1)} %get-tuple-element.59), channel_id=1, source_target_pairs={{0,8},{4,12},{8,0},{12,4},{16,24},{20,28},{24,16},{28,20},{1,9},{5... | collective-permute-start | bytes 786440 | tf_op jit(solution)/shard_map/ppermute | solution.py:762
  10.5 1.3 %pack_moved.1 = (bf16[128,256]{1,0:T(8,128)(2,1)S(1)}, bf16[384,256]{1,0:T(8,128)(2,1)S(1)}, bf16[384,256]{1,0:T(8,128)(2,1)S(1)}, bf16[384,256]{1,0:T(8,128)(2,1)S(1)}, bf16[1024,128]{1,0:T(8,128)(2,1)S(1)}) custom-call(bf16[128,1024]{1,0:T(8,128)(2,1)} %gate_ref, bf16[1024,512]{1,0:T(8,128)(2,1)} %own_ref.3, ...), custom_call_target="tpu_custom_call" | custom-call | tf_op jit(solution)/shard_map/pack_moved/pallas_call | solution.py:321
  11.8 1.4 %pack_filters.3 = (bf16[512,256]{1,0:T(8,128)(2,1)S(1)}, bf16[512,256]{1,0:T(8,128)(2,1)S(1)}) custom-call(f32[4,128,1024]{2,1,0:T(8,128)} %bitcast.9), custom_call_target="tpu_custom_call" | custom-call | tf_op jit(solution)/shard_map/pack_filters/pallas_call | solution.py:243
  13.3 2.9 %collective-permute-done.2.refs_2_ = bf16[128,256]{1,0:T(8,128)(2,1)S(1)} collective-permute-done((bf16[128,256]{1,0:T(8,128)(2,1)S(1)}, bf16[128,256]{1,0:T(8,128)(2,1)S(1)}, u32[]{:S(2)}, u32[]{:S(2)}) %collective-permute-start.2) | collective-permute-done | bytes 65568 | tf_op jit(solution)/shard_map/ppermute | solution.py:762
  17.9 1.5 %forward.1.spectrum_ref = f32[256,2048]{1,0:T(8,128)S(1)} custom-call(f32[2,128,8]{2,1,0:T(8,128)S(1)} %copy-done.2, f32[2,128,8]{2,1,0:T(8,128)S(1)} %copy-done.1, bf16[256,256]{1,0:T(8,128)(2,1)S(1)} %copy-done.4, bf16[2,128,256]{2,1,0:T(8,128)(2,1)S(1)} %get-tuple-element.71.refs_0_, bf16[2,128,256]{2,1,0:T(8,128)(2,1)S(1)} %get-tuple-element.72.refs_1_, ...), custom_call_target="tpu_custom_call" | custom-call | tf_op jit(solution)/shard_map/forward/pallas_call | solution.py:409
  21.1 1.8 %collective-permute-start.13 = (bf16[384,256]{1,0:T(8,128)(2,1)S(1)}, bf16[384,256]{1,0:T(8,128)(2,1)S(1)}, u32[]{:S(2)}, u32[]{:S(2)}) collective-permute-start(bf16[384,256]{1,0:T(8,128)(2,1)S(1)} %get-tuple-element.84), channel_id=1, source_target_pairs={{0,24},{4,28},{8,16},{12,20},{16,8},{20,12},{24,0},{28,4},{1,25},{... | collective-permute-start | bytes 589832 | tf_op jit(solution)/shard_map/ppermute | solution.py:762
  24.2 2.0 %backward.1 = (f32[4,128,256]{2,1,0:T(8,128)S(1)}, bf16[2,128,256]{2,1,0:T(8,128)(2,1)S(1)}, bf16[2,128,256]{2,1,0:T(8,128)(2,1)S(1)}) custom-call(f32[2,128,8]{2,1,0:T(8,128)S(1)} %copy-done.2, f32[2,128,8]{2,1,0:T(8,128)S(1)} %copy-done.1, bf16[256,256]{1,0:T(8,128)(2,1)S(1)} %copy-done.3, f32[256,2048]{1,0:T(8,128)S(1)} %forward.1.spectrum_ref, ...), custom_call_target="tpu_custom_call" | custom-call | tf_op jit(solution)/shard_map/backward/pallas_call | solution.py:485
  26.7 1.7 %collective-permute-done.11.refs_5_.refs_0_ = bf16[384,256]{1,0:T(8,128)(2,1)S(1)} collective-permute-done((bf16[384,256]{1,0:T(8,128)(2,1)S(1)}, bf16[384,256]{1,0:T(8,128)(2,1)S(1)}, u32[]{:S(2)}, u32[]{:S(2)}) %collective-permute-start.11) | collective-permute-done | bytes 196640 | tf_op jit(solution)/shard_map/ppermute | solution.py:762
  28.4 3.4 %collective-permute-done.12.refs_6_.refs_1_ = bf16[384,256]{1,0:T(8,128)(2,1)S(1)} collective-permute-done((bf16[384,256]{1,0:T(8,128)(2,1)S(1)}, bf16[384,256]{1,0:T(8,128)(2,1)S(1)}, u32[]{:S(2)}, u32[]{:S(2)}) %collective-permute-start.12) | collective-permute-done | bytes 196640 | tf_op jit(solution)/shard_map/ppermute | solution.py:762
  32.0 1.5 %collective-permute-start.15 = (bf16[528,256]{1,0:T(8,128)(2,1)S(1)}, bf16[528,256]{1,0:T(8,128)(2,1)S(1)}, u32[]{:S(2)}, u32[]{:S(2)}) collective-permute-start(bf16[528,256]{1,0:T(8,128)(2,1)S(1)} %get-tuple-element.86), channel_id=1, source_target_pairs={{0,16},{4,20},{8,24},{12,28},{16,0},{20,4},{24,8},{28,12},{1,17},{... | collective-permute-start | bytes 811016 | tf_op jit(solution)/shard_map/ppermute | solution.py:762
  37.6 8.8 %collective-permute-done.16.refs_3_ = bf16[512,256]{1,0:T(8,128)(2,1)S(1)} collective-permute-done((bf16[512,256]{1,0:T(8,128)(2,1)S(1)}, bf16[512,256]{1,0:T(8,128)(2,1)S(1)}, u32[]{:S(2)}, u32[]{:S(2)}) %collective-permute-start.16) | collective-permute-done | bytes 262176 | tf_op jit(solution)/shard_map/ppermute | solution.py:762
  47.2 1.6 %collective-permute-start.23 = (bf16[2,512,128]{2,1,0:T(8,128)(2,1)S(1)}, bf16[2,512,128]{2,1,0:T(8,128)(2,1)S(1)}, u32[]{:S(2)}, u32[]{:S(2)}) collective-permute-start(bf16[2,512,128]{2,1,0:T(8,128)(2,1)S(1)} %get-tuple-element.101), channel_id=1, source_target_pairs={{0,1},{1,0},{2,3},{3,2},{4,5},{5,4},{6,7},{7,6},{8,9},{9,8},{10,11... | collective-permute-start | bytes 786440 | tf_op jit(solution)/shard_map/ppermute | solution.py:762
  51.0 1.3 %collective-permute-start.18 = (bf16[128,512]{1,0:T(8,128)(2,1)S(1)}, bf16[128,512]{1,0:T(8,128)(2,1)S(1)}, u32[]{:S(2)}, u32[]{:S(2)}) collective-permute-start(bf16[128,512]{1,0:T(8,128)(2,1)S(1)} %get-tuple-element.89), channel_id=1, source_target_pairs={{0,16},{4,20},{8,24},{12,28},{16,0},{20,4},{24,8},{28,12},{1,17},{... | collective-permute-start | bytes 393224 | tf_op jit(solution)/shard_map/ppermute | solution.py:762
  53.7 3.2 %collective-permute-start.24 = (bf16[512,128]{1,0:T(8,128)(2,1)S(1)}, bf16[512,128]{1,0:T(8,128)(2,1)S(1)}, u32[]{:S(2)}, u32[]{:S(2)}) collective-permute-start(bf16[512,128]{1,0:T(8,128)(2,1)S(1)} %fusion), channel_id=1, source_target_pairs={{0,2},{1,3},{2,0},{3,1},{4,6},{5,7},{6,4},{7,5},{8,10},{9,11},{10,... | collective-permute-start | bytes 393224 | tf_op jit(solution)/shard_map/ppermute | solution.py:762
  56.9 1.3 %collective-permute-done.19.refs_3_ = bf16[128,512]{1,0:T(8,128)(2,1)S(1)} collective-permute-done((bf16[128,512]{1,0:T(8,128)(2,1)S(1)}, bf16[128,512]{1,0:T(8,128)(2,1)S(1)}, u32[]{:S(2)}, u32[]{:S(2)}) %collective-permute-start.19) | collective-permute-done | bytes 131104 | tf_op jit(solution)/shard_map/ppermute | solution.py:762
  58.8 1.7 %collective-permute-done.24.second_ref = bf16[512,128]{1,0:T(8,128)(2,1)S(1)} collective-permute-done((bf16[512,128]{1,0:T(8,128)(2,1)S(1)}, bf16[512,128]{1,0:T(8,128)(2,1)S(1)}, u32[]{:S(2)}, u32[]{:S(2)}) %collective-permute-start.24) | collective-permute-done | bytes 131104 | tf_op jit(solution)/shard_map/ppermute | solution.py:762
  60.6 2.0 %collective-permute-start.25 = (bf16[128,128]{1,0:T(8,128)(2,1)S(1)}, bf16[128,128]{1,0:T(8,128)(2,1)S(1)}, u32[]{:S(2)}, u32[]{:S(2)}) collective-permute-start(bf16[128,128]{1,0:T(8,128)(2,1)S(1)} %get-tuple-element.103), channel_id=1, source_target_pairs={{0,24},{4,28},{8,16},{12,20},{16,8},{20,12},{24,0},{28,4},{1,25},{... | collective-permute-start | bytes 98312 | tf_op jit(solution)/shard_map/ppermute | solution.py:762
  62.6 1.4 %collective-permute-start.20 = (bf16[128,512]{1,0:T(8,128)(2,1)S(1)}, bf16[128,512]{1,0:T(8,128)(2,1)S(1)}, u32[]{:S(2)}, u32[]{:S(2)}) collective-permute-start(bf16[128,512]{1,0:T(8,128)(2,1)S(1)} %get-tuple-element.92), channel_id=1, source_target_pairs={{0,1},{1,0},{2,3},{3,2},{4,5},{5,4},{6,7},{7,6},{8,9},{9,8},{10,11... | collective-permute-start | bytes 393224 | tf_op jit(solution)/shard_map/ppermute | solution.py:762
  64.0 1.4 %collective-permute-done.25.refs_3_ = bf16[128,128]{1,0:T(8,128)(2,1)S(1)} collective-permute-done((bf16[128,128]{1,0:T(8,128)(2,1)S(1)}, bf16[128,128]{1,0:T(8,128)(2,1)S(1)}, u32[]{:S(2)}, u32[]{:S(2)}) %collective-permute-start.25) | collective-permute-done | bytes 32800 | tf_op jit(solution)/shard_map/ppermute | solution.py:762
  65.5 2.5 %collective-permute-start.27 = (bf16[128,512]{1,0:T(8,128)(2,1)S(1)}, bf16[128,512]{1,0:T(8,128)(2,1)S(1)}, u32[]{:S(2)}, u32[]{:S(2)}) collective-permute-start(bf16[128,512]{1,0:T(8,128)(2,1)S(1)} %add.8), channel_id=1, source_target_pairs={{0,2},{1,3},{2,0},{3,1},{4,6},{5,7},{6,4},{7,5},{8,10},{9,11},{10,... | collective-permute-start | bytes 393224 | tf_op jit(solution)/shard_map/ppermute | solution.py:762
  69.2 1.9 %collective-permute-start.29 = (bf16[128,128]{1,0:T(8,128)(2,1)S(1)}, bf16[128,128]{1,0:T(8,128)(2,1)S(1)}, u32[]{:S(2)}, u32[]{:S(2)}) collective-permute-start(bf16[128,128]{1,0:T(8,128)(2,1)S(1)} %get-tuple-element.108), channel_id=1, source_target_pairs={{0,16},{4,20},{8,24},{12,28},{16,0},{20,4},{24,8},{28,12},{1,17},{... | collective-permute-start | bytes 98312 | tf_op jit(solution)/shard_map/ppermute | solution.py:762
  (65 shorter events, 21.3 us)
Async XLA Ops:
  0.0 8.9 %collective-permute-start = (bf16[1024,512]{1,0:T(8,128)(2,1)}, bf16[1024,512]{1,0:T(8,128)(2,1)S(1)}, u32[]{:S(2)}, u32[]{:S(2)}) collective-permute-start(bf16[1024,512]{1,0:T(8,128)(2,1)} %own_ref.3), channel_id=1, source_target_pairs={{0,4},{4,0},{8,12},{12,8},{16,20},{20,16},{24,28},{28,24},{1,5},{5... | collective-permute-start | bytes 3145736 | tf_op jit(solution)/shard_map/ppermute | solution.py:762
  1.4 11.8 %collective-permute-start.3 = (bf16[128,256]{1,0:T(8,128)(2,1)S(1)}, bf16[128,256]{1,0:T(8,128)(2,1)S(1)}, u32[]{:S(2)}, u32[]{:S(2)}) collective-permute-start(bf16[128,256]{1,0:T(8,128)(2,1)S(1)} %get-tuple-element.69), channel_id=1, source_target_pairs={{0,24},{4,28},{8,16},{12,20},{16,8},{20,12},{24,0},{28,4},{1,25},{... | collective-permute-start | bytes 196616 | tf_op jit(solution)/shard_map/ppermute | solution.py:762
  6.3 14.8 %collective-permute-start.7 = (bf16[512,256]{1,0:T(8,128)(2,1)S(1)}, bf16[512,256]{1,0:T(8,128)(2,1)S(1)}, u32[]{:S(2)}, u32[]{:S(2)}) collective-permute-start(bf16[512,256]{1,0:T(8,128)(2,1)S(1)} %get-tuple-element.74), channel_id=1, source_target_pairs={{0,16},{4,20},{8,24},{12,28},{16,0},{20,4},{24,8},{28,12},{1,17},{... | collective-permute-start | bytes 786440 | tf_op jit(solution)/shard_map/ppermute | solution.py:762
  6.9 9.3 %collective-permute-start.2 = (bf16[128,256]{1,0:T(8,128)(2,1)S(1)}, bf16[128,256]{1,0:T(8,128)(2,1)S(1)}, u32[]{:S(2)}, u32[]{:S(2)}) collective-permute-start(bf16[128,256]{1,0:T(8,128)(2,1)S(1)} %get-tuple-element.67), channel_id=1, source_target_pairs={{0,16},{4,20},{8,24},{12,28},{16,0},{20,4},{24,8},{28,12},{1,17},{... | collective-permute-start | bytes 196616 | tf_op jit(solution)/shard_map/ppermute | solution.py:762
  8.4 7.8 %collective-permute-start.1 = (bf16[128,256]{1,0:T(8,128)(2,1)S(1)}, bf16[128,256]{1,0:T(8,128)(2,1)S(1)}, u32[]{:S(2)}, u32[]{:S(2)}) collective-permute-start(bf16[128,256]{1,0:T(8,128)(2,1)S(1)} %get-tuple-element.65), channel_id=1, source_target_pairs={{0,8},{4,12},{8,0},{12,4},{16,24},{20,28},{24,16},{28,20},{1,9},{5... | collective-permute-start | bytes 196616 | tf_op jit(solution)/shard_map/ppermute | solution.py:762
  9.0 14.0 %collective-permute-start.6 = (bf16[512,256]{1,0:T(8,128)(2,1)S(1)}, bf16[512,256]{1,0:T(8,128)(2,1)S(1)}, u32[]{:S(2)}, u32[]{:S(2)}) collective-permute-start(bf16[512,256]{1,0:T(8,128)(2,1)S(1)} %get-tuple-element.59), channel_id=1, source_target_pairs={{0,8},{4,12},{8,0},{12,4},{16,24},{20,28},{24,16},{28,20},{1,9},{5... | collective-permute-start | bytes 786440 | tf_op jit(solution)/shard_map/ppermute | solution.py:762
  13.2 11.0 %collective-permute-start.8 = (bf16[512,256]{1,0:T(8,128)(2,1)S(1)}, bf16[512,256]{1,0:T(8,128)(2,1)S(1)}, u32[]{:S(2)}, u32[]{:S(2)}) collective-permute-start(bf16[512,256]{1,0:T(8,128)(2,1)S(1)} %get-tuple-element.63), channel_id=1, source_target_pairs={{0,24},{4,28},{8,16},{12,20},{16,8},{20,12},{24,0},{28,4},{1,25},{... | collective-permute-start | bytes 786440 | tf_op jit(solution)/shard_map/ppermute | solution.py:762
  19.4 9.1 %collective-permute-start.11 = (bf16[384,256]{1,0:T(8,128)(2,1)S(1)}, bf16[384,256]{1,0:T(8,128)(2,1)S(1)}, u32[]{:S(2)}, u32[]{:S(2)}) collective-permute-start(bf16[384,256]{1,0:T(8,128)(2,1)S(1)} %get-tuple-element.80), channel_id=1, source_target_pairs={{0,8},{4,12},{8,0},{12,4},{16,24},{20,28},{24,16},{28,20},{1,9},{5... | collective-permute-start | bytes 589832 | tf_op jit(solution)/shard_map/ppermute | solution.py:762
  20.0 11.8 %collective-permute-start.12 = (bf16[384,256]{1,0:T(8,128)(2,1)S(1)}, bf16[384,256]{1,0:T(8,128)(2,1)S(1)}, u32[]{:S(2)}, u32[]{:S(2)}) collective-permute-start(bf16[384,256]{1,0:T(8,128)(2,1)S(1)} %get-tuple-element.82), channel_id=1, source_target_pairs={{0,16},{4,20},{8,24},{12,28},{16,0},{20,4},{24,8},{28,12},{1,17},{... | collective-permute-start | bytes 589832 | tf_op jit(solution)/shard_map/ppermute | solution.py:762
  21.1 10.7 %collective-permute-start.13 = (bf16[384,256]{1,0:T(8,128)(2,1)S(1)}, bf16[384,256]{1,0:T(8,128)(2,1)S(1)}, u32[]{:S(2)}, u32[]{:S(2)}) collective-permute-start(bf16[384,256]{1,0:T(8,128)(2,1)S(1)} %get-tuple-element.84), channel_id=1, source_target_pairs={{0,24},{4,28},{8,16},{12,20},{16,8},{20,12},{24,0},{28,4},{1,25},{... | collective-permute-start | bytes 589832 | tf_op jit(solution)/shard_map/ppermute | solution.py:762
  26.2 5.6 %collective-permute-start.9 = (bf16[2,128,256]{2,1,0:T(8,128)(2,1)S(1)}, bf16[2,128,256]{2,1,0:T(8,128)(2,1)S(1)}, u32[]{:S(2)}, u32[]{:S(2)}) collective-permute-start(bf16[2,128,256]{2,1,0:T(8,128)(2,1)S(1)} %get-tuple-element.76), channel_id=1, source_target_pairs={{0,4},{4,0},{8,12},{12,8},{16,20},{20,16},{24,28},{28,24},{1,5},{5... | collective-permute-start | bytes 393224 | tf_op jit(solution)/shard_map/ppermute | solution.py:762
  26.3 5.6 %collective-permute-start.10 = (bf16[2,128,256]{2,1,0:T(8,128)(2,1)S(1)}, bf16[2,128,256]{2,1,0:T(8,128)(2,1)S(1)}, u32[]{:S(2)}, u32[]{:S(2)}) collective-permute-start(bf16[2,128,256]{2,1,0:T(8,128)(2,1)S(1)} %get-tuple-element.77), channel_id=1, source_target_pairs={{0,4},{4,0},{8,12},{12,8},{16,20},{20,16},{24,28},{28,24},{1,5},{5... | collective-permute-start | bytes 393224 | tf_op jit(solution)/shard_map/ppermute | solution.py:762
  32.0 14.4 %collective-permute-start.15 = (bf16[528,256]{1,0:T(8,128)(2,1)S(1)}, bf16[528,256]{1,0:T(8,128)(2,1)S(1)}, u32[]{:S(2)}, u32[]{:S(2)}) collective-permute-start(bf16[528,256]{1,0:T(8,128)(2,1)S(1)} %get-tuple-element.86), channel_id=1, source_target_pairs={{0,16},{4,20},{8,24},{12,28},{16,0},{20,4},{24,8},{28,12},{1,17},{... | collective-permute-start | bytes 811016 | tf_op jit(solution)/shard_map/ppermute | solution.py:762
  33.5 12.9 %collective-permute-start.14 = (bf16[528,256]{1,0:T(8,128)(2,1)S(1)}, bf16[528,256]{1,0:T(8,128)(2,1)S(1)}, u32[]{:S(2)}, u32[]{:S(2)}) collective-permute-start(bf16[528,256]{1,0:T(8,128)(2,1)S(1)} %get-tuple-element.86), channel_id=1, source_target_pairs={{0,8},{4,12},{8,0},{12,4},{16,24},{20,28},{24,16},{28,20},{1,9},{5... | collective-permute-start | bytes 811016 | tf_op jit(solution)/shard_map/ppermute | solution.py:762
  34.6 11.8 %collective-permute-start.16 = (bf16[512,256]{1,0:T(8,128)(2,1)S(1)}, bf16[512,256]{1,0:T(8,128)(2,1)S(1)}, u32[]{:S(2)}, u32[]{:S(2)}) collective-permute-start(bf16[512,256]{1,0:T(8,128)(2,1)S(1)} %get-tuple-element.85.refs_0_), channel_id=1, source_target_pairs={{0,24},{4,28},{8,16},{12,20},{16,8},{20,12},{24,0},{28,4},{1,25},{... | collective-permute-start | bytes 786440 | tf_op jit(solution)/shard_map/ppermute | solution.py:762
  47.2 6.4 %collective-permute-start.23 = (bf16[2,512,128]{2,1,0:T(8,128)(2,1)S(1)}, bf16[2,512,128]{2,1,0:T(8,128)(2,1)S(1)}, u32[]{:S(2)}, u32[]{:S(2)}) collective-permute-start(bf16[2,512,128]{2,1,0:T(8,128)(2,1)S(1)} %get-tuple-element.101), channel_id=1, source_target_pairs={{0,1},{1,0},{2,3},{3,2},{4,5},{5,4},{6,7},{7,6},{8,9},{9,8},{10,11... | collective-permute-start | bytes 786440 | tf_op jit(solution)/shard_map/ppermute | solution.py:762
  49.8 7.2 %collective-permute-start.17 = (bf16[128,512]{1,0:T(8,128)(2,1)S(1)}, bf16[128,512]{1,0:T(8,128)(2,1)S(1)}, u32[]{:S(2)}, u32[]{:S(2)}) collective-permute-start(bf16[128,512]{1,0:T(8,128)(2,1)S(1)} %get-tuple-element.88), channel_id=1, source_target_pairs={{0,8},{4,12},{8,0},{12,4},{16,24},{20,28},{24,16},{28,20},{1,9},{5... | collective-permute-start | bytes 393224 | tf_op jit(solution)/shard_map/ppermute | solution.py:762
  51.0 5.9 %collective-permute-start.18 = (bf16[128,512]{1,0:T(8,128)(2,1)S(1)}, bf16[128,512]{1,0:T(8,128)(2,1)S(1)}, u32[]{:S(2)}, u32[]{:S(2)}) collective-permute-start(bf16[128,512]{1,0:T(8,128)(2,1)S(1)} %get-tuple-element.89), channel_id=1, source_target_pairs={{0,16},{4,20},{8,24},{12,28},{16,0},{20,4},{24,8},{28,12},{1,17},{... | collective-permute-start | bytes 393224 | tf_op jit(solution)/shard_map/ppermute | solution.py:762
  52.4 5.9 %collective-permute-start.19 = (bf16[128,512]{1,0:T(8,128)(2,1)S(1)}, bf16[128,512]{1,0:T(8,128)(2,1)S(1)}, u32[]{:S(2)}, u32[]{:S(2)}) collective-permute-start(bf16[128,512]{1,0:T(8,128)(2,1)S(1)} %get-tuple-element.90), channel_id=1, source_target_pairs={{0,24},{4,28},{8,16},{12,20},{16,8},{20,12},{24,0},{28,4},{1,25},{... | collective-permute-start | bytes 393224 | tf_op jit(solution)/shard_map/ppermute | solution.py:762
  53.7 6.8 %collective-permute-start.24 = (bf16[512,128]{1,0:T(8,128)(2,1)S(1)}, bf16[512,128]{1,0:T(8,128)(2,1)S(1)}, u32[]{:S(2)}, u32[]{:S(2)}) collective-permute-start(bf16[512,128]{1,0:T(8,128)(2,1)S(1)} %fusion), channel_id=1, source_target_pairs={{0,2},{1,3},{2,0},{3,1},{4,6},{5,7},{6,4},{7,5},{8,10},{9,11},{10,... | collective-permute-start | bytes 393224 | tf_op jit(solution)/shard_map/ppermute | solution.py:762
  58.3 7.1 %collective-permute-start.26 = (bf16[128,512]{1,0:T(8,128)(2,1)S(1)}, bf16[128,512]{1,0:T(8,128)(2,1)S(1)}, u32[]{:S(2)}, u32[]{:S(2)}) collective-permute-start(bf16[128,512]{1,0:T(8,128)(2,1)S(1)} %get-tuple-element.105), channel_id=1, source_target_pairs={{0,1},{1,0},{2,3},{3,2},{4,5},{5,4},{6,7},{7,6},{8,9},{9,8},{10,11... | collective-permute-start | bytes 393224 | tf_op jit(solution)/shard_map/ppermute | solution.py:762
  60.6 4.9 %collective-permute-start.25 = (bf16[128,128]{1,0:T(8,128)(2,1)S(1)}, bf16[128,128]{1,0:T(8,128)(2,1)S(1)}, u32[]{:S(2)}, u32[]{:S(2)}) collective-permute-start(bf16[128,128]{1,0:T(8,128)(2,1)S(1)} %get-tuple-element.103), channel_id=1, source_target_pairs={{0,24},{4,28},{8,16},{12,20},{16,8},{20,12},{24,0},{28,4},{1,25},{... | collective-permute-start | bytes 98312 | tf_op jit(solution)/shard_map/ppermute | solution.py:762
  62.6 8.5 %collective-permute-start.20 = (bf16[128,512]{1,0:T(8,128)(2,1)S(1)}, bf16[128,512]{1,0:T(8,128)(2,1)S(1)}, u32[]{:S(2)}, u32[]{:S(2)}) collective-permute-start(bf16[128,512]{1,0:T(8,128)(2,1)S(1)} %get-tuple-element.92), channel_id=1, source_target_pairs={{0,1},{1,0},{2,3},{3,2},{4,5},{5,4},{6,7},{7,6},{8,9},{9,8},{10,11... | collective-permute-start | bytes 393224 | tf_op jit(solution)/shard_map/ppermute | solution.py:762
  65.5 7.7 %collective-permute-start.27 = (bf16[128,512]{1,0:T(8,128)(2,1)S(1)}, bf16[128,512]{1,0:T(8,128)(2,1)S(1)}, u32[]{:S(2)}, u32[]{:S(2)}) collective-permute-start(bf16[128,512]{1,0:T(8,128)(2,1)S(1)} %add.8), channel_id=1, source_target_pairs={{0,2},{1,3},{2,0},{3,1},{4,6},{5,7},{6,4},{7,5},{8,10},{9,11},{10,... | collective-permute-start | bytes 393224 | tf_op jit(solution)/shard_map/ppermute | solution.py:762
  (12 other events, 75.6 us)

commit v22 on v21

--- a/solution.py
+++ b/solution.py
@@ -800,7 +800,7 @@
     keep, passed, send = project_moved(arrange(mine, moved[1:], others), gathered)
     blocks = to_chips(finish(keep, *over_layers(passed, send), chips))
     keep, near, passed, far = sort_blocks(to_chips(project_still(out_weight, other_weight, gathered)))
-    second = swapped(add(after(passed, blocks[3]), swapped(far, "chan", 1), 0), "chan", 2)
+    second = swapped(add(after(passed, blocks[3], blocks[1]), swapped(far, "chan", 1), 0), "chan", 2)
     return join(keep, swapped(near, "chan", 1), second, blocks)
 
 

time: 74.2 us -> 73.9 us (level)
  starting transfers between devices: 35.1 us -> 33.8 us
  waiting for transfers between devices: 27 us -> 28.1 us
    ppermute x30, starting transfers between devices: 35.1 us -> 33.8 us  [swapped(): lax.ppermute(value, axis, [(source, source ^ offset) for source in range(...]
    ppermute x30, waiting for transfers between devices: 27 us -> 28.1 us  [swapped(): lax.ppermute(value, axis, [(source, source ^ offset) for source in range(...]
where the time goes in v22:
time: 73.9 us; the launch traced here: 73.7 us
  starting transfers between devices  33.8 us (46%)
  waiting for transfers between devices  28.1 us (38%)
  Pallas kernels  11.6 us (16%)
    ppermute x30, starting transfers between devices, swapped(): lax.ppermute(value, axis, [(source, source ^ offset) for source in range(...  33.8 us
    ppermute x30, waiting for transfers between devices, swapped(): lax.ppermute(value, axis, [(source, source ^ offset) for source in range(...  28.1 us
    pallas_call x2, Pallas kernels, pack_filters(): pl.pallas_call(functools.partial(pack_filters_kernel, offsets), in_specs=...  2.74 us
    pallas_call x1, Pallas kernels, backward(): pl.pallas_call(functools.partial(backward_kernel, chips), in_specs=[WHOLE...  2.01 us
    pallas_call x1, Pallas kernels, forward(): pl.pallas_call(functools.partial(forward_kernel, chips), in_specs=[WHOLE]...  1.48 us
  transfers between devices with their start and end apart: 30, of which 15 were waited for; matrix products, arithmetic and copies ran while one was open for 0% of the time, Pallas kernels for 13%

profile of v22, /device:TPU:0, one launch (start us, length us, event | category | flops | bytes accessed | tf_op | source)
XLA Modules:
  0.0 73.7 jit_solution(17053236954905886145)
XLA Ops:
  1.4 3.5 %collective-permute-start.3 = (bf16[128,256]{1,0:T(8,128)(2,1)S(1)}, bf16[128,256]{1,0:T(8,128)(2,1)S(1)}, u32[]{:S(2)}, u32[]{:S(2)}) collective-permute-start(bf16[128,256]{1,0:T(8,128)(2,1)S(1)} %get-tuple-element.69), channel_id=1, source_target_pairs={{0,24},{4,28},{8,16},{12,20},{16,8},{20,12},{24,0},{28,4},{1,25},{... | collective-permute-start | bytes 196616 | tf_op jit(solution)/shard_map/ppermute | solution.py:762
  4.9 1.4 %pack_filters.2 = (bf16[512,256]{1,0:T(8,128)(2,1)S(1)}, bf16[512,256]{1,0:T(8,128)(2,1)S(1)}) custom-call(f32[4,128,1024]{2,1,0:T(8,128)} %bitcast.8), custom_call_target="tpu_custom_call" | custom-call | tf_op jit(solution)/shard_map/pack_filters/pallas_call | solution.py:243
  6.9 1.5 %collective-permute-start.2 = (bf16[128,256]{1,0:T(8,128)(2,1)S(1)}, bf16[128,256]{1,0:T(8,128)(2,1)S(1)}, u32[]{:S(2)}, u32[]{:S(2)}) collective-permute-start(bf16[128,256]{1,0:T(8,128)(2,1)S(1)} %get-tuple-element.67), channel_id=1, source_target_pairs={{0,16},{4,20},{8,24},{12,28},{16,0},{20,4},{24,8},{28,12},{1,17},{... | collective-permute-start | bytes 196616 | tf_op jit(solution)/shard_map/ppermute | solution.py:762
  9.0 1.6 %collective-permute-start.6 = (bf16[512,256]{1,0:T(8,128)(2,1)S(1)}, bf16[512,256]{1,0:T(8,128)(2,1)S(1)}, u32[]{:S(2)}, u32[]{:S(2)}) collective-permute-start(bf16[512,256]{1,0:T(8,128)(2,1)S(1)} %get-tuple-element.59), channel_id=1, source_target_pairs={{0,8},{4,12},{8,0},{12,4},{16,24},{20,28},{24,16},{28,20},{1,9},{5... | collective-permute-start | bytes 786440 | tf_op jit(solution)/shard_map/ppermute | solution.py:762
  10.5 1.3 %pack_moved.1 = (bf16[128,256]{1,0:T(8,128)(2,1)S(1)}, bf16[384,256]{1,0:T(8,128)(2,1)S(1)}, bf16[384,256]{1,0:T(8,128)(2,1)S(1)}, bf16[384,256]{1,0:T(8,128)(2,1)S(1)}, bf16[1024,128]{1,0:T(8,128)(2,1)S(1)}) custom-call(bf16[128,1024]{1,0:T(8,128)(2,1)} %gate_ref, bf16[1024,512]{1,0:T(8,128)(2,1)} %own_ref.3, ...), custom_call_target="tpu_custom_call" | custom-call | tf_op jit(solution)/shard_map/pack_moved/pallas_call | solution.py:321
  11.8 1.4 %pack_filters.3 = (bf16[512,256]{1,0:T(8,128)(2,1)S(1)}, bf16[512,256]{1,0:T(8,128)(2,1)S(1)}) custom-call(f32[4,128,1024]{2,1,0:T(8,128)} %bitcast.9), custom_call_target="tpu_custom_call" | custom-call | tf_op jit(solution)/shard_map/pack_filters/pallas_call | solution.py:243
  13.3 2.9 %collective-permute-done.2.refs_2_ = bf16[128,256]{1,0:T(8,128)(2,1)S(1)} collective-permute-done((bf16[128,256]{1,0:T(8,128)(2,1)S(1)}, bf16[128,256]{1,0:T(8,128)(2,1)S(1)}, u32[]{:S(2)}, u32[]{:S(2)}) %collective-permute-start.2) | collective-permute-done | bytes 65568 | tf_op jit(solution)/shard_map/ppermute | solution.py:762
  17.9 1.5 %forward.1.spectrum_ref = f32[256,2048]{1,0:T(8,128)S(1)} custom-call(f32[2,128,8]{2,1,0:T(8,128)S(1)} %copy-done.2, f32[2,128,8]{2,1,0:T(8,128)S(1)} %copy-done.1, bf16[256,256]{1,0:T(8,128)(2,1)S(1)} %copy-done.4, bf16[2,128,256]{2,1,0:T(8,128)(2,1)S(1)} %get-tuple-element.71.refs_0_, bf16[2,128,256]{2,1,0:T(8,128)(2,1)S(1)} %get-tuple-element.72.refs_1_, ...), custom_call_target="tpu_custom_call" | custom-call | tf_op jit(solution)/shard_map/forward/pallas_call | solution.py:409
  21.1 1.8 %collective-permute-start.13 = (bf16[384,256]{1,0:T(8,128)(2,1)S(1)}, bf16[384,256]{1,0:T(8,128)(2,1)S(1)}, u32[]{:S(2)}, u32[]{:S(2)}) collective-permute-start(bf16[384,256]{1,0:T(8,128)(2,1)S(1)} %get-tuple-element.84), channel_id=1, source_target_pairs={{0,24},{4,28},{8,16},{12,20},{16,8},{20,12},{24,0},{28,4},{1,25},{... | collective-permute-start | bytes 589832 | tf_op jit(solution)/shard_map/ppermute | solution.py:762
  24.2 2.0 %backward.1 = (f32[4,128,256]{2,1,0:T(8,128)S(1)}, bf16[2,128,256]{2,1,0:T(8,128)(2,1)S(1)}, bf16[2,128,256]{2,1,0:T(8,128)(2,1)S(1)}) custom-call(f32[2,128,8]{2,1,0:T(8,128)S(1)} %copy-done.2, f32[2,128,8]{2,1,0:T(8,128)S(1)} %copy-done.1, bf16[256,256]{1,0:T(8,128)(2,1)S(1)} %copy-done.3, f32[256,2048]{1,0:T(8,128)S(1)} %forward.1.spectrum_ref, ...), custom_call_target="tpu_custom_call" | custom-call | tf_op jit(solution)/shard_map/backward/pallas_call | solution.py:485
  26.7 1.7 %collective-permute-done.11.refs_5_.refs_0_ = bf16[384,256]{1,0:T(8,128)(2,1)S(1)} collective-permute-done((bf16[384,256]{1,0:T(8,128)(2,1)S(1)}, bf16[384,256]{1,0:T(8,128)(2,1)S(1)}, u32[]{:S(2)}, u32[]{:S(2)}) %collective-permute-start.11) | collective-permute-done | bytes 196640 | tf_op jit(solution)/shard_map/ppermute | solution.py:762
  28.4 3.4 %collective-permute-done.12.refs_6_.refs_1_ = bf16[384,256]{1,0:T(8,128)(2,1)S(1)} collective-permute-done((bf16[384,256]{1,0:T(8,128)(2,1)S(1)}, bf16[384,256]{1,0:T(8,128)(2,1)S(1)}, u32[]{:S(2)}, u32[]{:S(2)}) %collective-permute-start.12) | collective-permute-done | bytes 196640 | tf_op jit(solution)/shard_map/ppermute | solution.py:762
  32.0 1.5 %collective-permute-start.15 = (bf16[528,256]{1,0:T(8,128)(2,1)S(1)}, bf16[528,256]{1,0:T(8,128)(2,1)S(1)}, u32[]{:S(2)}, u32[]{:S(2)}) collective-permute-start(bf16[528,256]{1,0:T(8,128)(2,1)S(1)} %get-tuple-element.86), channel_id=1, source_target_pairs={{0,16},{4,20},{8,24},{12,28},{16,0},{20,4},{24,8},{28,12},{1,17},{... | collective-permute-start | bytes 811016 | tf_op jit(solution)/shard_map/ppermute | solution.py:762
  37.6 8.8 %collective-permute-done.16.refs_3_ = bf16[512,256]{1,0:T(8,128)(2,1)S(1)} collective-permute-done((bf16[512,256]{1,0:T(8,128)(2,1)S(1)}, bf16[512,256]{1,0:T(8,128)(2,1)S(1)}, u32[]{:S(2)}, u32[]{:S(2)}) %collective-permute-start.16) | collective-permute-done | bytes 262176 | tf_op jit(solution)/shard_map/ppermute | solution.py:762
  47.2 1.6 %collective-permute-start.23 = (bf16[2,512,128]{2,1,0:T(8,128)(2,1)S(1)}, bf16[2,512,128]{2,1,0:T(8,128)(2,1)S(1)}, u32[]{:S(2)}, u32[]{:S(2)}) collective-permute-start(bf16[2,512,128]{2,1,0:T(8,128)(2,1)S(1)} %get-tuple-element.101), channel_id=1, source_target_pairs={{0,1},{1,0},{2,3},{3,2},{4,5},{5,4},{6,7},{7,6},{8,9},{9,8},{10,11... | collective-permute-start | bytes 786440 | tf_op jit(solution)/shard_map/ppermute | solution.py:762
  49.8 1.3 %collective-permute-start.17 = (bf16[128,512]{1,0:T(8,128)(2,1)S(1)}, bf16[128,512]{1,0:T(8,128)(2,1)S(1)}, u32[]{:S(2)}, u32[]{:S(2)}) collective-permute-start(bf16[128,512]{1,0:T(8,128)(2,1)S(1)} %get-tuple-element.88), channel_id=1, source_target_pairs={{0,8},{4,12},{8,0},{12,4},{16,24},{20,28},{24,16},{28,20},{1,9},{5... | collective-permute-start | bytes 393224 | tf_op jit(solution)/shard_map/ppermute | solution.py:762
  51.0 1.3 %collective-permute-start.18 = (bf16[128,512]{1,0:T(8,128)(2,1)S(1)}, bf16[128,512]{1,0:T(8,128)(2,1)S(1)}, u32[]{:S(2)}, u32[]{:S(2)}) collective-permute-start(bf16[128,512]{1,0:T(8,128)(2,1)S(1)} %get-tuple-element.89), channel_id=1, source_target_pairs={{0,16},{4,20},{8,24},{12,28},{16,0},{20,4},{24,8},{28,12},{1,17},{... | collective-permute-start | bytes 393224 | tf_op jit(solution)/shard_map/ppermute | solution.py:762
  53.7 3.2 %collective-permute-start.24 = (bf16[512,128]{1,0:T(8,128)(2,1)S(1)}, bf16[512,128]{1,0:T(8,128)(2,1)S(1)}, u32[]{:S(2)}, u32[]{:S(2)}) collective-permute-start(bf16[512,128]{1,0:T(8,128)(2,1)S(1)} %fusion), channel_id=1, source_target_pairs={{0,2},{1,3},{2,0},{3,1},{4,6},{5,7},{6,4},{7,5},{8,10},{9,11},{10,... | collective-permute-start | bytes 393224 | tf_op jit(solution)/shard_map/ppermute | solution.py:762
  56.9 1.3 %collective-permute-done.19.refs_3_ = bf16[128,512]{1,0:T(8,128)(2,1)S(1)} collective-permute-done((bf16[128,512]{1,0:T(8,128)(2,1)S(1)}, bf16[128,512]{1,0:T(8,128)(2,1)S(1)}, u32[]{:S(2)}, u32[]{:S(2)}) %collective-permute-start.19) | collective-permute-done | bytes 131104 | tf_op jit(solution)/shard_map/ppermute | solution.py:762
  58.8 1.7 %collective-permute-done.24.second_ref = bf16[512,128]{1,0:T(8,128)(2,1)S(1)} collective-permute-done((bf16[512,128]{1,0:T(8,128)(2,1)S(1)}, bf16[512,128]{1,0:T(8,128)(2,1)S(1)}, u32[]{:S(2)}, u32[]{:S(2)}) %collective-permute-start.24) | collective-permute-done | bytes 131104 | tf_op jit(solution)/shard_map/ppermute | solution.py:762
  60.6 2.0 %collective-permute-start.25 = (bf16[128,128]{1,0:T(8,128)(2,1)S(1)}, bf16[128,128]{1,0:T(8,128)(2,1)S(1)}, u32[]{:S(2)}, u32[]{:S(2)}) collective-permute-start(bf16[128,128]{1,0:T(8,128)(2,1)S(1)} %get-tuple-element.103), channel_id=1, source_target_pairs={{0,24},{4,28},{8,16},{12,20},{16,8},{20,12},{24,0},{28,4},{1,25},{... | collective-permute-start | bytes 98312 | tf_op jit(solution)/shard_map/ppermute | solution.py:762
  63.5 1.6 %collective-permute-start.20 = (bf16[128,512]{1,0:T(8,128)(2,1)S(1)}, bf16[128,512]{1,0:T(8,128)(2,1)S(1)}, u32[]{:S(2)}, u32[]{:S(2)}) collective-permute-start(bf16[128,512]{1,0:T(8,128)(2,1)S(1)} %get-tuple-element.92), channel_id=1, source_target_pairs={{0,1},{1,0},{2,3},{3,2},{4,5},{5,4},{6,7},{7,6},{8,9},{9,8},{10,11... | collective-permute-start | bytes 393224 | tf_op jit(solution)/shard_map/ppermute | solution.py:762
  66.5 2.5 %collective-permute-start.28 = (bf16[128,512]{1,0:T(8,128)(2,1)S(1)}, bf16[128,512]{1,0:T(8,128)(2,1)S(1)}, u32[]{:S(2)}, u32[]{:S(2)}) collective-permute-start(bf16[128,512]{1,0:T(8,128)(2,1)S(1)} %add.8), channel_id=1, source_target_pairs={{0,2},{1,3},{2,0},{3,1},{4,6},{5,7},{6,4},{7,5},{8,10},{9,11},{10,... | collective-permute-start | bytes 393224 | tf_op jit(solution)/shard_map/ppermute | solution.py:762
  69.8 3.1 %collective-permute-done.29.refs_2_ = bf16[128,128]{1,0:T(8,128)(2,1)S(1)} collective-permute-done((bf16[128,128]{1,0:T(8,128)(2,1)S(1)}, bf16[128,128]{1,0:T(8,128)(2,1)S(1)}, u32[]{:S(2)}, u32[]{:S(2)}) %collective-permute-start.29) | collective-permute-done | bytes 32800 | tf_op jit(solution)/shard_map/ppermute | solution.py:762
  (65 shorter events, 19.9 us)
Async XLA Ops:
  0.0 8.9 %collective-permute-start = (bf16[1024,512]{1,0:T(8,128)(2,1)}, bf16[1024,512]{1,0:T(8,128)(2,1)S(1)}, u32[]{:S(2)}, u32[]{:S(2)}) collective-permute-start(bf16[1024,512]{1,0:T(8,128)(2,1)} %own_ref.3), channel_id=1, source_target_pairs={{0,4},{4,0},{8,12},{12,8},{16,20},{20,16},{24,28},{28,24},{1,5},{5... | collective-permute-start | bytes 3145736 | tf_op jit(solution)/shard_map/ppermute | solution.py:762
  1.4 11.8 %collective-permute-start.3 = (bf16[128,256]{1,0:T(8,128)(2,1)S(1)}, bf16[128,256]{1,0:T(8,128)(2,1)S(1)}, u32[]{:S(2)}, u32[]{:S(2)}) collective-permute-start(bf16[128,256]{1,0:T(8,128)(2,1)S(1)} %get-tuple-element.69), channel_id=1, source_target_pairs={{0,24},{4,28},{8,16},{12,20},{16,8},{20,12},{24,0},{28,4},{1,25},{... | collective-permute-start | bytes 196616 | tf_op jit(solution)/shard_map/ppermute | solution.py:762
  6.3 14.8 %collective-permute-start.7 = (bf16[512,256]{1,0:T(8,128)(2,1)S(1)}, bf16[512,256]{1,0:T(8,128)(2,1)S(1)}, u32[]{:S(2)}, u32[]{:S(2)}) collective-permute-start(bf16[512,256]{1,0:T(8,128)(2,1)S(1)} %get-tuple-element.74), channel_id=1, source_target_pairs={{0,16},{4,20},{8,24},{12,28},{16,0},{20,4},{24,8},{28,12},{1,17},{... | collective-permute-start | bytes 786440 | tf_op jit(solution)/shard_map/ppermute | solution.py:762
  6.9 9.3 %collective-permute-start.2 = (bf16[128,256]{1,0:T(8,128)(2,1)S(1)}, bf16[128,256]{1,0:T(8,128)(2,1)S(1)}, u32[]{:S(2)}, u32[]{:S(2)}) collective-permute-start(bf16[128,256]{1,0:T(8,128)(2,1)S(1)} %get-tuple-element.67), channel_id=1, source_target_pairs={{0,16},{4,20},{8,24},{12,28},{16,0},{20,4},{24,8},{28,12},{1,17},{... | collective-permute-start | bytes 196616 | tf_op jit(solution)/shard_map/ppermute | solution.py:762
  8.4 7.8 %collective-permute-start.1 = (bf16[128,256]{1,0:T(8,128)(2,1)S(1)}, bf16[128,256]{1,0:T(8,128)(2,1)S(1)}, u32[]{:S(2)}, u32[]{:S(2)}) collective-permute-start(bf16[128,256]{1,0:T(8,128)(2,1)S(1)} %get-tuple-element.65), channel_id=1, source_target_pairs={{0,8},{4,12},{8,0},{12,4},{16,24},{20,28},{24,16},{28,20},{1,9},{5... | collective-permute-start | bytes 196616 | tf_op jit(solution)/shard_map/ppermute | solution.py:762
  9.0 14.0 %collective-permute-start.6 = (bf16[512,256]{1,0:T(8,128)(2,1)S(1)}, bf16[512,256]{1,0:T(8,128)(2,1)S(1)}, u32[]{:S(2)}, u32[]{:S(2)}) collective-permute-start(bf16[512,256]{1,0:T(8,128)(2,1)S(1)} %get-tuple-element.59), channel_id=1, source_target_pairs={{0,8},{4,12},{8,0},{12,4},{16,24},{20,28},{24,16},{28,20},{1,9},{5... | collective-permute-start | bytes 786440 | tf_op jit(solution)/shard_map/ppermute | solution.py:762
  13.2 11.0 %collective-permute-start.8 = (bf16[512,256]{1,0:T(8,128)(2,1)S(1)}, bf16[512,256]{1,0:T(8,128)(2,1)S(1)}, u32[]{:S(2)}, u32[]{:S(2)}) collective-permute-start(bf16[512,256]{1,0:T(8,128)(2,1)S(1)} %get-tuple-element.63), channel_id=1, source_target_pairs={{0,24},{4,28},{8,16},{12,20},{16,8},{20,12},{24,0},{28,4},{1,25},{... | collective-permute-start | bytes 786440 | tf_op jit(solution)/shard_map/ppermute | solution.py:762
  19.4 9.1 %collective-permute-start.11 = (bf16[384,256]{1,0:T(8,128)(2,1)S(1)}, bf16[384,256]{1,0:T(8,128)(2,1)S(1)}, u32[]{:S(2)}, u32[]{:S(2)}) collective-permute-start(bf16[384,256]{1,0:T(8,128)(2,1)S(1)} %get-tuple-element.80), channel_id=1, source_target_pairs={{0,8},{4,12},{8,0},{12,4},{16,24},{20,28},{24,16},{28,20},{1,9},{5... | collective-permute-start | bytes 589832 | tf_op jit(solution)/shard_map/ppermute | solution.py:762
  20.0 11.8 %collective-permute-start.12 = (bf16[384,256]{1,0:T(8,128)(2,1)S(1)}, bf16[384,256]{1,0:T(8,128)(2,1)S(1)}, u32[]{:S(2)}, u32[]{:S(2)}) collective-permute-start(bf16[384,256]{1,0:T(8,128)(2,1)S(1)} %get-tuple-element.82), channel_id=1, source_target_pairs={{0,16},{4,20},{8,24},{12,28},{16,0},{20,4},{24,8},{28,12},{1,17},{... | collective-permute-start | bytes 589832 | tf_op jit(solution)/shard_map/ppermute | solution.py:762
  21.1 10.7 %collective-permute-start.13 = (bf16[384,256]{1,0:T(8,128)(2,1)S(1)}, bf16[384,256]{1,0:T(8,128)(2,1)S(1)}, u32[]{:S(2)}, u32[]{:S(2)}) collective-permute-start(bf16[384,256]{1,0:T(8,128)(2,1)S(1)} %get-tuple-element.84), channel_id=1, source_target_pairs={{0,24},{4,28},{8,16},{12,20},{16,8},{20,12},{24,0},{28,4},{1,25},{... | collective-permute-start | bytes 589832 | tf_op jit(solution)/shard_map/ppermute | solution.py:762
  26.2 5.6 %collective-permute-start.9 = (bf16[2,128,256]{2,1,0:T(8,128)(2,1)S(1)}, bf16[2,128,256]{2,1,0:T(8,128)(2,1)S(1)}, u32[]{:S(2)}, u32[]{:S(2)}) collective-permute-start(bf16[2,128,256]{2,1,0:T(8,128)(2,1)S(1)} %get-tuple-element.76), channel_id=1, source_target_pairs={{0,4},{4,0},{8,12},{12,8},{16,20},{20,16},{24,28},{28,24},{1,5},{5... | collective-permute-start | bytes 393224 | tf_op jit(solution)/shard_map/ppermute | solution.py:762
  26.3 5.6 %collective-permute-start.10 = (bf16[2,128,256]{2,1,0:T(8,128)(2,1)S(1)}, bf16[2,128,256]{2,1,0:T(8,128)(2,1)S(1)}, u32[]{:S(2)}, u32[]{:S(2)}) collective-permute-start(bf16[2,128,256]{2,1,0:T(8,128)(2,1)S(1)} %get-tuple-element.77), channel_id=1, source_target_pairs={{0,4},{4,0},{8,12},{12,8},{16,20},{20,16},{24,28},{28,24},{1,5},{5... | collective-permute-start | bytes 393224 | tf_op jit(solution)/shard_map/ppermute | solution.py:762
  32.0 14.4 %collective-permute-start.15 = (bf16[528,256]{1,0:T(8,128)(2,1)S(1)}, bf16[528,256]{1,0:T(8,128)(2,1)S(1)}, u32[]{:S(2)}, u32[]{:S(2)}) collective-permute-start(bf16[528,256]{1,0:T(8,128)(2,1)S(1)} %get-tuple-element.86), channel_id=1, source_target_pairs={{0,16},{4,20},{8,24},{12,28},{16,0},{20,4},{24,8},{28,12},{1,17},{... | collective-permute-start | bytes 811016 | tf_op jit(solution)/shard_map/ppermute | solution.py:762
  33.5 12.9 %collective-permute-start.14 = (bf16[528,256]{1,0:T(8,128)(2,1)S(1)}, bf16[528,256]{1,0:T(8,128)(2,1)S(1)}, u32[]{:S(2)}, u32[]{:S(2)}) collective-permute-start(bf16[528,256]{1,0:T(8,128)(2,1)S(1)} %get-tuple-element.86), channel_id=1, source_target_pairs={{0,8},{4,12},{8,0},{12,4},{16,24},{20,28},{24,16},{28,20},{1,9},{5... | collective-permute-start | bytes 811016 | tf_op jit(solution)/shard_map/ppermute | solution.py:762
  34.6 11.8 %collective-permute-start.16 = (bf16[512,256]{1,0:T(8,128)(2,1)S(1)}, bf16[512,256]{1,0:T(8,128)(2,1)S(1)}, u32[]{:S(2)}, u32[]{:S(2)}) collective-permute-start(bf16[512,256]{1,0:T(8,128)(2,1)S(1)} %get-tuple-element.85.refs_0_), channel_id=1, source_target_pairs={{0,24},{4,28},{8,16},{12,20},{16,8},{20,12},{24,0},{28,4},{1,25},{... | collective-permute-start | bytes 786440 | tf_op jit(solution)/shard_map/ppermute | solution.py:762
  47.2 6.4 %collective-permute-start.23 = (bf16[2,512,128]{2,1,0:T(8,128)(2,1)S(1)}, bf16[2,512,128]{2,1,0:T(8,128)(2,1)S(1)}, u32[]{:S(2)}, u32[]{:S(2)}) collective-permute-start(bf16[2,512,128]{2,1,0:T(8,128)(2,1)S(1)} %get-tuple-element.101), channel_id=1, source_target_pairs={{0,1},{1,0},{2,3},{3,2},{4,5},{5,4},{6,7},{7,6},{8,9},{9,8},{10,11... | collective-permute-start | bytes 786440 | tf_op jit(solution)/shard_map/ppermute | solution.py:762
  49.8 7.2 %collective-permute-start.17 = (bf16[128,512]{1,0:T(8,128)(2,1)S(1)}, bf16[128,512]{1,0:T(8,128)(2,1)S(1)}, u32[]{:S(2)}, u32[]{:S(2)}) collective-permute-start(bf16[128,512]{1,0:T(8,128)(2,1)S(1)} %get-tuple-element.88), channel_id=1, source_target_pairs={{0,8},{4,12},{8,0},{12,4},{16,24},{20,28},{24,16},{28,20},{1,9},{5... | collective-permute-start | bytes 393224 | tf_op jit(solution)/shard_map/ppermute | solution.py:762
  51.0 5.9 %collective-permute-start.18 = (bf16[128,512]{1,0:T(8,128)(2,1)S(1)}, bf16[128,512]{1,0:T(8,128)(2,1)S(1)}, u32[]{:S(2)}, u32[]{:S(2)}) collective-permute-start(bf16[128,512]{1,0:T(8,128)(2,1)S(1)} %get-tuple-element.89), channel_id=1, source_target_pairs={{0,16},{4,20},{8,24},{12,28},{16,0},{20,4},{24,8},{28,12},{1,17},{... | collective-permute-start | bytes 393224 | tf_op jit(solution)/shard_map/ppermute | solution.py:762
  52.4 5.9 %collective-permute-start.19 = (bf16[128,512]{1,0:T(8,128)(2,1)S(1)}, bf16[128,512]{1,0:T(8,128)(2,1)S(1)}, u32[]{:S(2)}, u32[]{:S(2)}) collective-permute-start(bf16[128,512]{1,0:T(8,128)(2,1)S(1)} %get-tuple-element.90), channel_id=1, source_target_pairs={{0,24},{4,28},{8,16},{12,20},{16,8},{20,12},{24,0},{28,4},{1,25},{... | collective-permute-start | bytes 393224 | tf_op jit(solution)/shard_map/ppermute | solution.py:762
  53.7 6.8 %collective-permute-start.24 = (bf16[512,128]{1,0:T(8,128)(2,1)S(1)}, bf16[512,128]{1,0:T(8,128)(2,1)S(1)}, u32[]{:S(2)}, u32[]{:S(2)}) collective-permute-start(bf16[512,128]{1,0:T(8,128)(2,1)S(1)} %fusion), channel_id=1, source_target_pairs={{0,2},{1,3},{2,0},{3,1},{4,6},{5,7},{6,4},{7,5},{8,10},{9,11},{10,... | collective-permute-start | bytes 393224 | tf_op jit(solution)/shard_map/ppermute | solution.py:762
  58.3 8.2 %collective-permute-start.27 = (bf16[128,512]{1,0:T(8,128)(2,1)S(1)}, bf16[128,512]{1,0:T(8,128)(2,1)S(1)}, u32[]{:S(2)}, u32[]{:S(2)}) collective-permute-start(bf16[128,512]{1,0:T(8,128)(2,1)S(1)} %get-tuple-element.106), channel_id=1, source_target_pairs={{0,1},{1,0},{2,3},{3,2},{4,5},{5,4},{6,7},{7,6},{8,9},{9,8},{10,11... | collective-permute-start | bytes 393224 | tf_op jit(solution)/shard_map/ppermute | solution.py:762
  60.6 4.9 %collective-permute-start.25 = (bf16[128,128]{1,0:T(8,128)(2,1)S(1)}, bf16[128,128]{1,0:T(8,128)(2,1)S(1)}, u32[]{:S(2)}, u32[]{:S(2)}) collective-permute-start(bf16[128,128]{1,0:T(8,128)(2,1)S(1)} %get-tuple-element.103), channel_id=1, source_target_pairs={{0,24},{4,28},{8,16},{12,20},{16,8},{20,12},{24,0},{28,4},{1,25},{... | collective-permute-start | bytes 98312 | tf_op jit(solution)/shard_map/ppermute | solution.py:762
  63.5 6.3 %collective-permute-start.20 = (bf16[128,512]{1,0:T(8,128)(2,1)S(1)}, bf16[128,512]{1,0:T(8,128)(2,1)S(1)}, u32[]{:S(2)}, u32[]{:S(2)}) collective-permute-start(bf16[128,512]{1,0:T(8,128)(2,1)S(1)} %get-tuple-element.92), channel_id=1, source_target_pairs={{0,1},{1,0},{2,3},{3,2},{4,5},{5,4},{6,7},{7,6},{8,9},{9,8},{10,11... | collective-permute-start | bytes 393224 | tf_op jit(solution)/shard_map/ppermute | solution.py:762
  66.5 6.4 %collective-permute-start.28 = (bf16[128,512]{1,0:T(8,128)(2,1)S(1)}, bf16[128,512]{1,0:T(8,128)(2,1)S(1)}, u32[]{:S(2)}, u32[]{:S(2)}) collective-permute-start(bf16[128,512]{1,0:T(8,128)(2,1)S(1)} %add.8), channel_id=1, source_target_pairs={{0,2},{1,3},{2,0},{3,1},{4,6},{5,7},{6,4},{7,5},{8,10},{9,11},{10,... | collective-permute-start | bytes 393224 | tf_op jit(solution)/shard_map/ppermute | solution.py:762
  (12 other events, 75.6 us)

commit v23 on v22

--- a/solution.py
+++ b/solution.py
@@ -498,7 +498,7 @@
     )(cos, sin, table, spectrum, *first)
 
 
-def gate_kernel(chips, skip_ref, keep_ref, low_ref, high_ref, *refs):
+def gate_kernel(chips, offsets, skip_ref, keep_ref, low_ref, high_ref, *refs):
     signal_refs, gate_refs = refs[:chips], refs[chips : 2 * chips]
     out_ref, longer_ref, arrived_ref = refs[2 * chips :]
     chip, _ = own_place()
@@ -510,7 +510,7 @@
         block = chip ^ offset
         convolved = keep_ref[block] + arrived_ref[block].astype(F32)
         signal = signal_refs[offset][pl.ds(0, rows), :].astype(F32)
-        gate = gate_refs[offset][pl.ds(0, rows), :].astype(F32)
+        gate = gate_refs[offsets.index(offset)][pl.ds(0, rows), :].astype(F32)
         gated = (gate * (convolved + skip * signal)).astype(BF16)
         out_ref[block_at(block, rows), :] = gated
         longer_ref[block_at(block, rows), :] = gated
@@ -518,10 +518,10 @@
     longer_ref[pl.ds(end, longer_ref.shape[0] - end), :] = longer_ref[pl.ds(0, longer_ref.shape[0] - end), :]
 
 
-def gate(skip, keep, arrived, first, gates, spare):
+def gate(skip, keep, arrived, first, gates, offsets, spare):
     chips, rows, lanes = keep.shape
     return pl.pallas_call(
-        functools.partial(gate_kernel, chips),
+        functools.partial(gate_kernel, chips, offsets),
         in_specs=[WHOLE] * (4 + 2 * chips),
         out_specs=[WHOLE] * 2,
         out_shape=[
@@ -532,7 +532,7 @@
         cost_estimate=CHEAP,
         compiler_params=pltpu.CompilerParams(vmem_limit_bytes=6 * 2**20),
         name="gate",
-    )(skip, keep, *arrived, *first, *gates)
+    )(skip, keep, *arrived, *first, *(gates[offset] for offset in offsets))
 
 
 def piece_of(ref, half, part):
@@ -793,7 +793,7 @@
     spectrum = forward(own, [swapped(part, "seq", 1) for part in own], tables)
     moved = to_chips([after(block, spectrum) for block in moved])
     keep, *send = backward(spectrum, filters, tables)
-    gated, longer = gate(skip_gain[None, :], keep, [swapped(part, "seq", 1) for part in send], values, moved, 16)
+    gated, longer = gate(skip_gain[None, :], keep, [swapped(part, "seq", 1) for part in send], values, moved, (0, 3, 1, 2), 16)
     gathered = to_chips([gated, longer, longer, gated])
 
     others = [swapped(part, "seq", 1) for part in collect([after(block, gated) for block in moved[1:]], out_weight.shape[0] // 2)]

time: 73.9 us -> 74.9 us (1.014)
  waiting for transfers between devices: 28.1 us -> 30 us
  starting transfers between devices: 33.8 us -> 32.8 us
    ppermute x30, waiting for transfers between devices: 28.1 us -> 30 us  [swapped(): lax.ppermute(value, axis, [(source, source ^ offset) for source in range(...]
    ppermute x30, starting transfers between devices: 33.8 us -> 32.8 us  [swapped(): lax.ppermute(value, axis, [(source, source ^ offset) for source in range(...]
where the time goes in v23:
time: 74.9 us; the launch traced here: 74.7 us
  starting transfers between devices  32.8 us (44%)
  waiting for transfers between devices  30 us (40%)
  Pallas kernels  11.6 us (15%)
    ppermute x30, starting transfers between devices, swapped(): lax.ppermute(value, axis, [(source, source ^ offset) for source in range(...  32.8 us
    ppermute x30, waiting for transfers between devices, swapped(): lax.ppermute(value, axis, [(source, source ^ offset) for source in range(...  30 us
    pallas_call x2, Pallas kernels, pack_filters(): pl.pallas_call(functools.partial(pack_filters_kernel, offsets), in_specs=...  2.74 us
    pallas_call x1, Pallas kernels, backward(): pl.pallas_call(functools.partial(backward_kernel, chips), in_specs=[WHOLE...  2.01 us
  transfers between devices with their start and end apart: 30, of which 15 were waited for; matrix products, arithmetic and copies ran while one was open for 0% of the time, Pallas kernels for 13%

profile of v23, /device:TPU:0, one launch (start us, length us, event | category | flops | bytes accessed | tf_op | source)
XLA Modules:
  0.0 74.7 jit_solution(18027369928894936029)
XLA Ops:
  1.4 3.5 %collective-permute-start.3 = (bf16[128,256]{1,0:T(8,128)(2,1)S(1)}, bf16[128,256]{1,0:T(8,128)(2,1)S(1)}, u32[]{:S(2)}, u32[]{:S(2)}) collective-permute-start(bf16[128,256]{1,0:T(8,128)(2,1)S(1)} %get-tuple-element.69), channel_id=1, source_target_pairs={{0,24},{4,28},{8,16},{12,20},{16,8},{20,12},{24,0},{28,4},{1,25},{... | collective-permute-start | bytes 196616 | tf_op jit(solution)/shard_map/ppermute | solution.py:762
  4.9 1.4 %pack_filters.2 = (bf16[512,256]{1,0:T(8,128)(2,1)S(1)}, bf16[512,256]{1,0:T(8,128)(2,1)S(1)}) custom-call(f32[4,128,1024]{2,1,0:T(8,128)} %bitcast.8), custom_call_target="tpu_custom_call" | custom-call | tf_op jit(solution)/shard_map/pack_filters/pallas_call | solution.py:243
  6.9 1.5 %collective-permute-start.2 = (bf16[128,256]{1,0:T(8,128)(2,1)S(1)}, bf16[128,256]{1,0:T(8,128)(2,1)S(1)}, u32[]{:S(2)}, u32[]{:S(2)}) collective-permute-start(bf16[128,256]{1,0:T(8,128)(2,1)S(1)} %get-tuple-element.67), channel_id=1, source_target_pairs={{0,16},{4,20},{8,24},{12,28},{16,0},{20,4},{24,8},{28,12},{1,17},{... | collective-permute-start | bytes 196616 | tf_op jit(solution)/shard_map/ppermute | solution.py:762
  9.0 1.6 %collective-permute-start.6 = (bf16[512,256]{1,0:T(8,128)(2,1)S(1)}, bf16[512,256]{1,0:T(8,128)(2,1)S(1)}, u32[]{:S(2)}, u32[]{:S(2)}) collective-permute-start(bf16[512,256]{1,0:T(8,128)(2,1)S(1)} %get-tuple-element.59), channel_id=1, source_target_pairs={{0,8},{4,12},{8,0},{12,4},{16,24},{20,28},{24,16},{28,20},{1,9},{5... | collective-permute-start | bytes 786440 | tf_op jit(solution)/shard_map/ppermute | solution.py:762
  10.5 1.3 %pack_moved.1 = (bf16[128,256]{1,0:T(8,128)(2,1)S(1)}, bf16[384,256]{1,0:T(8,128)(2,1)S(1)}, bf16[384,256]{1,0:T(8,128)(2,1)S(1)}, bf16[384,256]{1,0:T(8,128)(2,1)S(1)}, bf16[1024,128]{1,0:T(8,128)(2,1)S(1)}) custom-call(bf16[128,1024]{1,0:T(8,128)(2,1)} %gate_ref, bf16[1024,512]{1,0:T(8,128)(2,1)} %own_ref.3, ...), custom_call_target="tpu_custom_call" | custom-call | tf_op jit(solution)/shard_map/pack_moved/pallas_call | solution.py:321
  11.8 1.4 %pack_filters.3 = (bf16[512,256]{1,0:T(8,128)(2,1)S(1)}, bf16[512,256]{1,0:T(8,128)(2,1)S(1)}) custom-call(f32[4,128,1024]{2,1,0:T(8,128)} %bitcast.9), custom_call_target="tpu_custom_call" | custom-call | tf_op jit(solution)/shard_map/pack_filters/pallas_call | solution.py:243
  13.3 2.9 %collective-permute-done.2.refs_2_ = bf16[128,256]{1,0:T(8,128)(2,1)S(1)} collective-permute-done((bf16[128,256]{1,0:T(8,128)(2,1)S(1)}, bf16[128,256]{1,0:T(8,128)(2,1)S(1)}, u32[]{:S(2)}, u32[]{:S(2)}) %collective-permute-start.2) | collective-permute-done | bytes 65568 | tf_op jit(solution)/shard_map/ppermute | solution.py:762
  17.9 1.5 %forward.1.spectrum_ref = f32[256,2048]{1,0:T(8,128)S(1)} custom-call(f32[2,128,8]{2,1,0:T(8,128)S(1)} %copy-done.2, f32[2,128,8]{2,1,0:T(8,128)S(1)} %copy-done.1, bf16[256,256]{1,0:T(8,128)(2,1)S(1)} %copy-done.4, bf16[2,128,256]{2,1,0:T(8,128)(2,1)S(1)} %get-tuple-element.71.refs_0_, bf16[2,128,256]{2,1,0:T(8,128)(2,1)S(1)} %get-tuple-element.72.refs_1_, ...), custom_call_target="tpu_custom_call" | custom-call | tf_op jit(solution)/shard_map/forward/pallas_call | solution.py:409
  19.4 1.2 %collective-permute-start.11 = (bf16[384,256]{1,0:T(8,128)(2,1)S(1)}, bf16[384,256]{1,0:T(8,128)(2,1)S(1)}, u32[]{:S(2)}, u32[]{:S(2)}) collective-permute-start(bf16[384,256]{1,0:T(8,128)(2,1)S(1)} %get-tuple-element.80), channel_id=1, source_target_pairs={{0,24},{4,28},{8,16},{12,20},{16,8},{20,12},{24,0},{28,4},{1,25},{... | collective-permute-start | bytes 589832 | tf_op jit(solution)/shard_map/ppermute | solution.py:762
  21.4 1.5 %collective-permute-start.13 = (bf16[384,256]{1,0:T(8,128)(2,1)S(1)}, bf16[384,256]{1,0:T(8,128)(2,1)S(1)}, u32[]{:S(2)}, u32[]{:S(2)}) collective-permute-start(bf16[384,256]{1,0:T(8,128)(2,1)S(1)} %get-tuple-element.84), channel_id=1, source_target_pairs={{0,16},{4,20},{8,24},{12,28},{16,0},{20,4},{24,8},{28,12},{1,17},{... | collective-permute-start | bytes 589832 | tf_op jit(solution)/shard_map/ppermute | solution.py:762
  23.3 2.0 %backward.1 = (f32[4,128,256]{2,1,0:T(8,128)S(1)}, bf16[2,128,256]{2,1,0:T(8,128)(2,1)S(1)}, bf16[2,128,256]{2,1,0:T(8,128)(2,1)S(1)}) custom-call(f32[2,128,8]{2,1,0:T(8,128)S(1)} %copy-done.2, f32[2,128,8]{2,1,0:T(8,128)S(1)} %copy-done.1, bf16[256,256]{1,0:T(8,128)(2,1)S(1)} %copy-done.3, f32[256,2048]{1,0:T(8,128)S(1)} %forward.1.spectrum_ref, ...), custom_call_target="tpu_custom_call" | custom-call | tf_op jit(solution)/shard_map/backward/pallas_call | solution.py:485
  25.8 2.2 %collective-permute-done.11.refs_5_.refs_2_ = bf16[384,256]{1,0:T(8,128)(2,1)S(1)} collective-permute-done((bf16[384,256]{1,0:T(8,128)(2,1)S(1)}, bf16[384,256]{1,0:T(8,128)(2,1)S(1)}, u32[]{:S(2)}, u32[]{:S(2)}) %collective-permute-start.11) | collective-permute-done | bytes 196640 | tf_op jit(solution)/shard_map/ppermute | solution.py:762
  28.1 3.7 %collective-permute-done.12.refs_6_.refs_0_ = bf16[384,256]{1,0:T(8,128)(2,1)S(1)} collective-permute-done((bf16[384,256]{1,0:T(8,128)(2,1)S(1)}, bf16[384,256]{1,0:T(8,128)(2,1)S(1)}, u32[]{:S(2)}, u32[]{:S(2)}) %collective-permute-start.12) | collective-permute-done | bytes 196640 | tf_op jit(solution)/shard_map/ppermute | solution.py:762
  32.0 1.5 %collective-permute-start.15 = (bf16[528,256]{1,0:T(8,128)(2,1)S(1)}, bf16[528,256]{1,0:T(8,128)(2,1)S(1)}, u32[]{:S(2)}, u32[]{:S(2)}) collective-permute-start(bf16[528,256]{1,0:T(8,128)(2,1)S(1)} %get-tuple-element.86), channel_id=1, source_target_pairs={{0,16},{4,20},{8,24},{12,28},{16,0},{20,4},{24,8},{28,12},{1,17},{... | collective-permute-start | bytes 811016 | tf_op jit(solution)/shard_map/ppermute | solution.py:762
  37.6 9.5 %collective-permute-done.16.refs_3_ = bf16[512,256]{1,0:T(8,128)(2,1)S(1)} collective-permute-done((bf16[512,256]{1,0:T(8,128)(2,1)S(1)}, bf16[512,256]{1,0:T(8,128)(2,1)S(1)}, u32[]{:S(2)}, u32[]{:S(2)}) %collective-permute-start.16) | collective-permute-done | bytes 262176 | tf_op jit(solution)/shard_map/ppermute | solution.py:762
  48.0 1.6 %collective-permute-start.23 = (bf16[2,512,128]{2,1,0:T(8,128)(2,1)S(1)}, bf16[2,512,128]{2,1,0:T(8,128)(2,1)S(1)}, u32[]{:S(2)}, u32[]{:S(2)}) collective-permute-start(bf16[2,512,128]{2,1,0:T(8,128)(2,1)S(1)} %get-tuple-element.101), channel_id=1, source_target_pairs={{0,1},{1,0},{2,3},{3,2},{4,5},{5,4},{6,7},{7,6},{8,9},{9,8},{10,11... | collective-permute-start | bytes 786440 | tf_op jit(solution)/shard_map/ppermute | solution.py:762
  51.7 1.5 %collective-permute-start.18 = (bf16[128,512]{1,0:T(8,128)(2,1)S(1)}, bf16[128,512]{1,0:T(8,128)(2,1)S(1)}, u32[]{:S(2)}, u32[]{:S(2)}) collective-permute-start(bf16[128,512]{1,0:T(8,128)(2,1)S(1)} %get-tuple-element.89), channel_id=1, source_target_pairs={{0,16},{4,20},{8,24},{12,28},{16,0},{20,4},{24,8},{28,12},{1,17},{... | collective-permute-start | bytes 393224 | tf_op jit(solution)/shard_map/ppermute | solution.py:762
  55.0 2.7 %collective-permute-start.24 = (bf16[512,128]{1,0:T(8,128)(2,1)S(1)}, bf16[512,128]{1,0:T(8,128)(2,1)S(1)}, u32[]{:S(2)}, u32[]{:S(2)}) collective-permute-start(bf16[512,128]{1,0:T(8,128)(2,1)S(1)} %fusion), channel_id=1, source_target_pairs={{0,2},{1,3},{2,0},{3,1},{4,6},{5,7},{6,4},{7,5},{8,10},{9,11},{10,... | collective-permute-start | bytes 393224 | tf_op jit(solution)/shard_map/ppermute | solution.py:762
  57.7 1.4 %collective-permute-done.19.refs_3_ = bf16[128,512]{1,0:T(8,128)(2,1)S(1)} collective-permute-done((bf16[128,512]{1,0:T(8,128)(2,1)S(1)}, bf16[128,512]{1,0:T(8,128)(2,1)S(1)}, u32[]{:S(2)}, u32[]{:S(2)}) %collective-permute-start.19) | collective-permute-done | bytes 131104 | tf_op jit(solution)/shard_map/ppermute | solution.py:762
  59.7 2.7 %collective-permute-done.24.second_ref = bf16[512,128]{1,0:T(8,128)(2,1)S(1)} collective-permute-done((bf16[512,128]{1,0:T(8,128)(2,1)S(1)}, bf16[512,128]{1,0:T(8,128)(2,1)S(1)}, u32[]{:S(2)}, u32[]{:S(2)}) %collective-permute-start.24) | collective-permute-done | bytes 131104 | tf_op jit(solution)/shard_map/ppermute | solution.py:762
  62.4 1.3 %collective-permute-start.25 = (bf16[128,128]{1,0:T(8,128)(2,1)S(1)}, bf16[128,128]{1,0:T(8,128)(2,1)S(1)}, u32[]{:S(2)}, u32[]{:S(2)}) collective-permute-start(bf16[128,128]{1,0:T(8,128)(2,1)S(1)} %get-tuple-element.103), channel_id=1, source_target_pairs={{0,24},{4,28},{8,16},{12,20},{16,8},{20,12},{24,0},{28,4},{1,25},{... | collective-permute-start | bytes 98312 | tf_op jit(solution)/shard_map/ppermute | solution.py:762
  64.6 2.5 %collective-permute-start.20 = (bf16[128,512]{1,0:T(8,128)(2,1)S(1)}, bf16[128,512]{1,0:T(8,128)(2,1)S(1)}, u32[]{:S(2)}, u32[]{:S(2)}) collective-permute-start(bf16[128,512]{1,0:T(8,128)(2,1)S(1)} %get-tuple-element.92), channel_id=1, source_target_pairs={{0,1},{1,0},{2,3},{3,2},{4,5},{5,4},{6,7},{7,6},{8,9},{9,8},{10,11... | collective-permute-start | bytes 393224 | tf_op jit(solution)/shard_map/ppermute | solution.py:762
  67.7 2.3 %collective-permute-start.28 = (bf16[128,512]{1,0:T(8,128)(2,1)S(1)}, bf16[128,512]{1,0:T(8,128)(2,1)S(1)}, u32[]{:S(2)}, u32[]{:S(2)}) collective-permute-start(bf16[128,512]{1,0:T(8,128)(2,1)S(1)} %add.8), channel_id=1, source_target_pairs={{0,2},{1,3},{2,0},{3,1},{4,6},{5,7},{6,4},{7,5},{8,10},{9,11},{10,... | collective-permute-start | bytes 393224 | tf_op jit(solution)/shard_map/ppermute | solution.py:762
  70.4 3.5 %collective-permute-done.29.refs_2_ = bf16[128,128]{1,0:T(8,128)(2,1)S(1)} collective-permute-done((bf16[128,128]{1,0:T(8,128)(2,1)S(1)}, bf16[128,128]{1,0:T(8,128)(2,1)S(1)}, u32[]{:S(2)}, u32[]{:S(2)}) %collective-permute-start.29) | collective-permute-done | bytes 32800 | tf_op jit(solution)/shard_map/ppermute | solution.py:762
  (65 shorter events, 18.4 us)
Async XLA Ops:
  0.0 8.9 %collective-permute-start = (bf16[1024,512]{1,0:T(8,128)(2,1)}, bf16[1024,512]{1,0:T(8,128)(2,1)S(1)}, u32[]{:S(2)}, u32[]{:S(2)}) collective-permute-start(bf16[1024,512]{1,0:T(8,128)(2,1)} %own_ref.3), channel_id=1, source_target_pairs={{0,4},{4,0},{8,12},{12,8},{16,20},{20,16},{24,28},{28,24},{1,5},{5... | collective-permute-start | bytes 3145736 | tf_op jit(solution)/shard_map/ppermute | solution.py:762
  1.4 11.8 %collective-permute-start.3 = (bf16[128,256]{1,0:T(8,128)(2,1)S(1)}, bf16[128,256]{1,0:T(8,128)(2,1)S(1)}, u32[]{:S(2)}, u32[]{:S(2)}) collective-permute-start(bf16[128,256]{1,0:T(8,128)(2,1)S(1)} %get-tuple-element.69), channel_id=1, source_target_pairs={{0,24},{4,28},{8,16},{12,20},{16,8},{20,12},{24,0},{28,4},{1,25},{... | collective-permute-start | bytes 196616 | tf_op jit(solution)/shard_map/ppermute | solution.py:762
  6.3 15.1 %collective-permute-start.7 = (bf16[512,256]{1,0:T(8,128)(2,1)S(1)}, bf16[512,256]{1,0:T(8,128)(2,1)S(1)}, u32[]{:S(2)}, u32[]{:S(2)}) collective-permute-start(bf16[512,256]{1,0:T(8,128)(2,1)S(1)} %get-tuple-element.74), channel_id=1, source_target_pairs={{0,16},{4,20},{8,24},{12,28},{16,0},{20,4},{24,8},{28,12},{1,17},{... | collective-permute-start | bytes 786440 | tf_op jit(solution)/shard_map/ppermute | solution.py:762
  6.9 9.3 %collective-permute-start.2 = (bf16[128,256]{1,0:T(8,128)(2,1)S(1)}, bf16[128,256]{1,0:T(8,128)(2,1)S(1)}, u32[]{:S(2)}, u32[]{:S(2)}) collective-permute-start(bf16[128,256]{1,0:T(8,128)(2,1)S(1)} %get-tuple-element.67), channel_id=1, source_target_pairs={{0,16},{4,20},{8,24},{12,28},{16,0},{20,4},{24,8},{28,12},{1,17},{... | collective-permute-start | bytes 196616 | tf_op jit(solution)/shard_map/ppermute | solution.py:762
  8.4 7.8 %collective-permute-start.1 = (bf16[128,256]{1,0:T(8,128)(2,1)S(1)}, bf16[128,256]{1,0:T(8,128)(2,1)S(1)}, u32[]{:S(2)}, u32[]{:S(2)}) collective-permute-start(bf16[128,256]{1,0:T(8,128)(2,1)S(1)} %get-tuple-element.65), channel_id=1, source_target_pairs={{0,8},{4,12},{8,0},{12,4},{16,24},{20,28},{24,16},{28,20},{1,9},{5... | collective-permute-start | bytes 196616 | tf_op jit(solution)/shard_map/ppermute | solution.py:762
  9.0 14.0 %collective-permute-start.6 = (bf16[512,256]{1,0:T(8,128)(2,1)S(1)}, bf16[512,256]{1,0:T(8,128)(2,1)S(1)}, u32[]{:S(2)}, u32[]{:S(2)}) collective-permute-start(bf16[512,256]{1,0:T(8,128)(2,1)S(1)} %get-tuple-element.59), channel_id=1, source_target_pairs={{0,8},{4,12},{8,0},{12,4},{16,24},{20,28},{24,16},{28,20},{1,9},{5... | collective-permute-start | bytes 786440 | tf_op jit(solution)/shard_map/ppermute | solution.py:762
  13.2 10.1 %collective-permute-start.8 = (bf16[512,256]{1,0:T(8,128)(2,1)S(1)}, bf16[512,256]{1,0:T(8,128)(2,1)S(1)}, u32[]{:S(2)}, u32[]{:S(2)}) collective-permute-start(bf16[512,256]{1,0:T(8,128)(2,1)S(1)} %get-tuple-element.63), channel_id=1, source_target_pairs={{0,24},{4,28},{8,16},{12,20},{16,8},{20,12},{24,0},{28,4},{1,25},{... | collective-permute-start | bytes 786440 | tf_op jit(solution)/shard_map/ppermute | solution.py:762
  19.4 8.7 %collective-permute-start.11 = (bf16[384,256]{1,0:T(8,128)(2,1)S(1)}, bf16[384,256]{1,0:T(8,128)(2,1)S(1)}, u32[]{:S(2)}, u32[]{:S(2)}) collective-permute-start(bf16[384,256]{1,0:T(8,128)(2,1)S(1)} %get-tuple-element.80), channel_id=1, source_target_pairs={{0,24},{4,28},{8,16},{12,20},{16,8},{20,12},{24,0},{28,4},{1,25},{... | collective-permute-start | bytes 589832 | tf_op jit(solution)/shard_map/ppermute | solution.py:762
  20.6 11.2 %collective-permute-start.12 = (bf16[384,256]{1,0:T(8,128)(2,1)S(1)}, bf16[384,256]{1,0:T(8,128)(2,1)S(1)}, u32[]{:S(2)}, u32[]{:S(2)}) collective-permute-start(bf16[384,256]{1,0:T(8,128)(2,1)S(1)} %get-tuple-element.82), channel_id=1, source_target_pairs={{0,8},{4,12},{8,0},{12,4},{16,24},{20,28},{24,16},{28,20},{1,9},{5... | collective-permute-start | bytes 589832 | tf_op jit(solution)/shard_map/ppermute | solution.py:762
  21.4 10.4 %collective-permute-start.13 = (bf16[384,256]{1,0:T(8,128)(2,1)S(1)}, bf16[384,256]{1,0:T(8,128)(2,1)S(1)}, u32[]{:S(2)}, u32[]{:S(2)}) collective-permute-start(bf16[384,256]{1,0:T(8,128)(2,1)S(1)} %get-tuple-element.84), channel_id=1, source_target_pairs={{0,16},{4,20},{8,24},{12,28},{16,0},{20,4},{24,8},{28,12},{1,17},{... | collective-permute-start | bytes 589832 | tf_op jit(solution)/shard_map/ppermute | solution.py:762
  25.3 6.5 %collective-permute-start.9 = (bf16[2,128,256]{2,1,0:T(8,128)(2,1)S(1)}, bf16[2,128,256]{2,1,0:T(8,128)(2,1)S(1)}, u32[]{:S(2)}, u32[]{:S(2)}) collective-permute-start(bf16[2,128,256]{2,1,0:T(8,128)(2,1)S(1)} %get-tuple-element.76), channel_id=1, source_target_pairs={{0,4},{4,0},{8,12},{12,8},{16,20},{20,16},{24,28},{28,24},{1,5},{5... | collective-permute-start | bytes 393224 | tf_op jit(solution)/shard_map/ppermute | solution.py:762
  25.4 6.4 %collective-permute-start.10 = (bf16[2,128,256]{2,1,0:T(8,128)(2,1)S(1)}, bf16[2,128,256]{2,1,0:T(8,128)(2,1)S(1)}, u32[]{:S(2)}, u32[]{:S(2)}) collective-permute-start(bf16[2,128,256]{2,1,0:T(8,128)(2,1)S(1)} %get-tuple-element.77), channel_id=1, source_target_pairs={{0,4},{4,0},{8,12},{12,8},{16,20},{20,16},{24,28},{28,24},{1,5},{5... | collective-permute-start | bytes 393224 | tf_op jit(solution)/shard_map/ppermute | solution.py:762
  32.0 15.2 %collective-permute-start.15 = (bf16[528,256]{1,0:T(8,128)(2,1)S(1)}, bf16[528,256]{1,0:T(8,128)(2,1)S(1)}, u32[]{:S(2)}, u32[]{:S(2)}) collective-permute-start(bf16[528,256]{1,0:T(8,128)(2,1)S(1)} %get-tuple-element.86), channel_id=1, source_target_pairs={{0,16},{4,20},{8,24},{12,28},{16,0},{20,4},{24,8},{28,12},{1,17},{... | collective-permute-start | bytes 811016 | tf_op jit(solution)/shard_map/ppermute | solution.py:762
  33.5 13.7 %collective-permute-start.14 = (bf16[528,256]{1,0:T(8,128)(2,1)S(1)}, bf16[528,256]{1,0:T(8,128)(2,1)S(1)}, u32[]{:S(2)}, u32[]{:S(2)}) collective-permute-start(bf16[528,256]{1,0:T(8,128)(2,1)S(1)} %get-tuple-element.86), channel_id=1, source_target_pairs={{0,8},{4,12},{8,0},{12,4},{16,24},{20,28},{24,16},{28,20},{1,9},{5... | collective-permute-start | bytes 811016 | tf_op jit(solution)/shard_map/ppermute | solution.py:762
  34.6 12.6 %collective-permute-start.16 = (bf16[512,256]{1,0:T(8,128)(2,1)S(1)}, bf16[512,256]{1,0:T(8,128)(2,1)S(1)}, u32[]{:S(2)}, u32[]{:S(2)}) collective-permute-start(bf16[512,256]{1,0:T(8,128)(2,1)S(1)} %get-tuple-element.85.refs_0_), channel_id=1, source_target_pairs={{0,24},{4,28},{8,16},{12,20},{16,8},{20,12},{24,0},{28,4},{1,25},{... | collective-permute-start | bytes 786440 | tf_op jit(solution)/shard_map/ppermute | solution.py:762
  48.0 7.0 %collective-permute-start.23 = (bf16[2,512,128]{2,1,0:T(8,128)(2,1)S(1)}, bf16[2,512,128]{2,1,0:T(8,128)(2,1)S(1)}, u32[]{:S(2)}, u32[]{:S(2)}) collective-permute-start(bf16[2,512,128]{2,1,0:T(8,128)(2,1)S(1)} %get-tuple-element.101), channel_id=1, source_target_pairs={{0,1},{1,0},{2,3},{3,2},{4,5},{5,4},{6,7},{7,6},{8,9},{9,8},{10,11... | collective-permute-start | bytes 786440 | tf_op jit(solution)/shard_map/ppermute | solution.py:762
  50.5 7.2 %collective-permute-start.17 = (bf16[128,512]{1,0:T(8,128)(2,1)S(1)}, bf16[128,512]{1,0:T(8,128)(2,1)S(1)}, u32[]{:S(2)}, u32[]{:S(2)}) collective-permute-start(bf16[128,512]{1,0:T(8,128)(2,1)S(1)} %get-tuple-element.88), channel_id=1, source_target_pairs={{0,8},{4,12},{8,0},{12,4},{16,24},{20,28},{24,16},{28,20},{1,9},{5... | collective-permute-start | bytes 393224 | tf_op jit(solution)/shard_map/ppermute | solution.py:762
  51.7 6.0 %collective-permute-start.18 = (bf16[128,512]{1,0:T(8,128)(2,1)S(1)}, bf16[128,512]{1,0:T(8,128)(2,1)S(1)}, u32[]{:S(2)}, u32[]{:S(2)}) collective-permute-start(bf16[128,512]{1,0:T(8,128)(2,1)S(1)} %get-tuple-element.89), channel_id=1, source_target_pairs={{0,16},{4,20},{8,24},{12,28},{16,0},{20,4},{24,8},{28,12},{1,17},{... | collective-permute-start | bytes 393224 | tf_op jit(solution)/shard_map/ppermute | solution.py:762
  53.2 5.9 %collective-permute-start.19 = (bf16[128,512]{1,0:T(8,128)(2,1)S(1)}, bf16[128,512]{1,0:T(8,128)(2,1)S(1)}, u32[]{:S(2)}, u32[]{:S(2)}) collective-permute-start(bf16[128,512]{1,0:T(8,128)(2,1)S(1)} %get-tuple-element.90), channel_id=1, source_target_pairs={{0,24},{4,28},{8,16},{12,20},{16,8},{20,12},{24,0},{28,4},{1,25},{... | collective-permute-start | bytes 393224 | tf_op jit(solution)/shard_map/ppermute | solution.py:762
  55.0 7.3 %collective-permute-start.24 = (bf16[512,128]{1,0:T(8,128)(2,1)S(1)}, bf16[512,128]{1,0:T(8,128)(2,1)S(1)}, u32[]{:S(2)}, u32[]{:S(2)}) collective-permute-start(bf16[512,128]{1,0:T(8,128)(2,1)S(1)} %fusion), channel_id=1, source_target_pairs={{0,2},{1,3},{2,0},{3,1},{4,6},{5,7},{6,4},{7,5},{8,10},{9,11},{10,... | collective-permute-start | bytes 393224 | tf_op jit(solution)/shard_map/ppermute | solution.py:762
  59.2 8.5 %collective-permute-start.27 = (bf16[128,512]{1,0:T(8,128)(2,1)S(1)}, bf16[128,512]{1,0:T(8,128)(2,1)S(1)}, u32[]{:S(2)}, u32[]{:S(2)}) collective-permute-start(bf16[128,512]{1,0:T(8,128)(2,1)S(1)} %get-tuple-element.106), channel_id=1, source_target_pairs={{0,1},{1,0},{2,3},{3,2},{4,5},{5,4},{6,7},{7,6},{8,9},{9,8},{10,11... | collective-permute-start | bytes 393224 | tf_op jit(solution)/shard_map/ppermute | solution.py:762
  62.4 4.9 %collective-permute-start.25 = (bf16[128,128]{1,0:T(8,128)(2,1)S(1)}, bf16[128,128]{1,0:T(8,128)(2,1)S(1)}, u32[]{:S(2)}, u32[]{:S(2)}) collective-permute-start(bf16[128,128]{1,0:T(8,128)(2,1)S(1)} %get-tuple-element.103), channel_id=1, source_target_pairs={{0,24},{4,28},{8,16},{12,20},{16,8},{20,12},{24,0},{28,4},{1,25},{... | collective-permute-start | bytes 98312 | tf_op jit(solution)/shard_map/ppermute | solution.py:762
  64.6 5.8 %collective-permute-start.20 = (bf16[128,512]{1,0:T(8,128)(2,1)S(1)}, bf16[128,512]{1,0:T(8,128)(2,1)S(1)}, u32[]{:S(2)}, u32[]{:S(2)}) collective-permute-start(bf16[128,512]{1,0:T(8,128)(2,1)S(1)} %get-tuple-element.92), channel_id=1, source_target_pairs={{0,1},{1,0},{2,3},{3,2},{4,5},{5,4},{6,7},{7,6},{8,9},{9,8},{10,11... | collective-permute-start | bytes 393224 | tf_op jit(solution)/shard_map/ppermute | solution.py:762
  67.7 6.2 %collective-permute-start.28 = (bf16[128,512]{1,0:T(8,128)(2,1)S(1)}, bf16[128,512]{1,0:T(8,128)(2,1)S(1)}, u32[]{:S(2)}, u32[]{:S(2)}) collective-permute-start(bf16[128,512]{1,0:T(8,128)(2,1)S(1)} %add.8), channel_id=1, source_target_pairs={{0,2},{1,3},{2,0},{3,1},{4,6},{5,7},{6,4},{7,5},{8,10},{9,11},{10,... | collective-permute-start | bytes 393224 | tf_op jit(solution)/shard_map/ppermute | solution.py:762
  (12 other events, 75.5 us)

commit v24 on v22

--- a/solution.py
+++ b/solution.py
@@ -562,16 +562,20 @@
     )(*moved)
 
 
+def slot(target):
+    return (1 - target % 2) * 2 + target // 2
+
+
 def arrange_kernel(chips, mine_ref, *refs):
     moved_refs, (*other_refs, out_ref) = refs[: chips - 1], refs[chips - 1 :]
     chip, core = own_place()
     layer = lax.axis_index("chan")
     depth, share = mine_ref.shape
     quarter = depth // 4
-    out_ref[:, block_at(chip ^ layer, share)] = mine_ref[...]
+    out_ref[:, block_at(slot(chip ^ layer), share)] = mine_ref[...]
     for place in range(2 * (chips - 1)):
         offset, part = place // 2 + 1, place % 2
-        columns = block_at(chip ^ layer ^ offset, share)
+        columns = block_at(slot(chip ^ layer ^ offset), share)
         index, start = divmod(place * quarter, other_refs[0].shape[0])
         out_ref[block_at(2 * core + part, quarter), columns] = piece_of(moved_refs[offset - 1], 2 * quarter, part)
         out_ref[block_at(2 * (1 - core) + part, quarter), columns] = other_refs[index][pl.ds(start, quarter), :]
@@ -591,46 +595,61 @@
     )(mine, *moved, *others)
 
 
-def join_channels(chips, gated_refs, joined_ref):
+def project_sent_kernel(chips, weight_ref, *refs):
+    gated_refs, (send_ref, joined_ref) = refs[:chips], refs[chips:]
     chip, _ = own_place()
     lanes = gated_refs[0].shape[1]
+    share = send_ref.shape[2]
     for offset in range(chips):
         joined_ref[:, block_at(chip ^ offset, lanes)] = gated_refs[offset][pl.ds(0, joined_ref.shape[0]), :]
-
-
-def project_moved_kernel(chips, weight_ref, *refs):
-    gated_refs, (keep_ref, pass_ref, send_ref, joined_ref) = refs[:chips], refs[chips:]
-    share = keep_ref.shape[1]
-    join_channels(chips, gated_refs, joined_ref)
-    partial = jnp.dot(joined_ref[...], weight_ref[...], preferred_element_type=F32).astype(BF16)
-    keep_ref[...] = partial[:, :share]
-    send_ref[0] = partial[:, share : 2 * share]
-    pass_ref[...] = partial[:, 2 * share : 3 * share]
-    send_ref[1] = partial[:, 3 * share :]
-
-
-def project_moved(weight, gated):
+    weight = weight_ref[:, pl.ds(0, 2 * share)]
+    partial = jnp.dot(joined_ref[...], weight, preferred_element_type=F32).astype(BF16)
+    send_ref[0] = partial[:, :share]
+    send_ref[1] = partial[:, share:]
+
+
+def project_sent(weight, gated):
     chips = len(gated)
     depth, columns = weight.shape
     rows = gated[0].shape[0]
-    block = jax.ShapeDtypeStruct((rows, columns // chips), BF16)
-    return pl.pallas_call(
-        functools.partial(project_moved_kernel, chips),
+    return pl.pallas_call(
+        functools.partial(project_sent_kernel, chips),
         in_specs=[WHOLE] * (1 + chips),
-        out_specs=[WHOLE] * 3,
-        out_shape=[block, block, jax.ShapeDtypeStruct((2, rows, columns // chips), BF16)],
-        scratch_shapes=[pltpu.VMEM((rows, depth), BF16)],
+        out_specs=[WHOLE] * 2,
+        out_shape=[
+            jax.ShapeDtypeStruct((2, rows, columns // chips), BF16),
+            jax.ShapeDtypeStruct((rows, depth), BF16),
+        ],
         cost_estimate=CHEAP,
         compiler_params=pltpu.CompilerParams(vmem_limit_bytes=8 * 2**20),
-        name="project_moved",
+        name="project_sent",
     )(weight, *gated)
 
 
-def project_still_kernel(chips, own_ref, other_ref, *refs):
-    gated_refs, out_refs, joined_ref = refs[:chips], refs[chips : 2 * chips], refs[2 * chips]
+def project_kept_kernel(weight_ref, joined_ref, keep_ref, pass_ref):
+    share = keep_ref.shape[1]
+    weight = weight_ref[:, pl.ds(2 * share, 2 * share)]
+    partial = jnp.dot(joined_ref[...], weight, preferred_element_type=F32).astype(BF16)
+    keep_ref[...] = partial[:, :share]
+    pass_ref[...] = partial[:, share:]
+
+
+def project_kept(weight, joined):
+    block = jax.ShapeDtypeStruct((joined.shape[0], weight.shape[1] // 4), BF16)
+    return pl.pallas_call(
+        project_kept_kernel,
+        in_specs=[WHOLE] * 2,
+        out_specs=[WHOLE] * 2,
+        out_shape=[block, block],
+        cost_estimate=CHEAP,
+        compiler_params=pltpu.CompilerParams(vmem_limit_bytes=8 * 2**20),
+        name="project_kept",
+    )(weight, joined)
+
+
+def project_still_kernel(chips, own_ref, other_ref, joined_ref, *out_refs):
     chip, core = own_place()
     rows = out_refs[0].shape[0]
-    join_channels(chips, gated_refs, joined_ref)
 
     def project_with(weight_ref):
         for offset in range(chips):
@@ -646,20 +665,18 @@
         project_with(own_ref)
 
 
-def project_still(own, other, gated):
-    chips = len(gated)
-    depth, held = own.shape
-    rows = gated[0].shape[0] // chips
+def project_still(own, other, joined, chips):
+    held = own.shape[1]
+    rows = joined.shape[0] // chips
     return pl.pallas_call(
         functools.partial(project_still_kernel, chips),
-        in_specs=[WHOLE] * (2 + chips),
+        in_specs=[WHOLE] * 3,
         out_specs=[WHOLE] * chips,
         out_shape=[jax.ShapeDtypeStruct((rows, held), BF16)] * chips,
-        scratch_shapes=[pltpu.VMEM((rows * chips, depth), BF16)],
         cost_estimate=CHEAP,
         compiler_params=pltpu.CompilerParams(vmem_limit_bytes=12 * 2**20),
         name="project_still",
-    )(own, other, *gated)
+    )(own, other, joined)
 
 
 def sort_kernel(chips, *refs):
@@ -764,6 +781,10 @@
 
 def to_chips(blocks):
     return [swapped(block, "seq", 2 * offset) for offset, block in enumerate(blocks)]
+
+
+def after(value, *others):
+    return lax.optimization_barrier((value, *others))[0]
 
 
 def after(value, *others):
@@ -797,9 +818,13 @@
     gathered = to_chips([gated, longer, longer, gated])
 
     others = [swapped(part, "seq", 1) for part in collect([after(block, gated) for block in moved[1:]], out_weight.shape[0] // 2)]
-    keep, passed, send = project_moved(arrange(mine, moved[1:], others), gathered)
-    blocks = to_chips(finish(keep, *over_layers(passed, send), chips))
-    keep, near, passed, far = sort_blocks(to_chips(project_still(out_weight, other_weight, gathered)))
+    moved_weight = arrange(mine, moved[1:], others)
+    send, joined = project_sent(moved_weight, gathered)
+    first = swapped(send, "chan", 1)
+    keep, passed = project_kept(moved_weight, after(joined, first))
+    passed = (passed.astype(F32) + first[1].astype(F32)).astype(BF16)
+    blocks = to_chips(finish(keep, first, swapped(passed, "chan", 2), chips))
+    keep, near, passed, far = sort_blocks(to_chips(project_still(out_weight, other_weight, joined, chips)))
     second = swapped(add(after(passed, blocks[3], blocks[1]), swapped(far, "chan", 1), 0), "chan", 2)
     return join(keep, swapped(near, "chan", 1), second, blocks)
 

time: 73.9 us -> 75.8 us (1.026)
  waiting for transfers between devices: 28.1 us -> 31.2 us
  starting transfers between devices: 33.8 us -> 32.4 us
    ppermute x30, waiting for transfers between devices: 28.1 us -> 31.2 us  [swapped(): lax.ppermute(value, axis, [(source, source ^ offset) for source in range(...]
    ppermute x30, starting transfers between devices: 33.8 us -> 32.4 us  [swapped(): lax.ppermute(value, axis, [(source, source ^ offset) for source in range(...]
  transfers between devices with their start and end apart: 30 -> 30, of which waited for: 15 -> 17; matrix products, arithmetic and copies ran while one was open for 0% -> 0% of each run, Pallas kernels for 13% -> 13%
where the time goes in v24:
time: 75.8 us; the launch traced here: 75.5 us
  starting transfers between devices  32.4 us (43%)
  waiting for transfers between devices  31.2 us (41%)
  Pallas kernels  11.6 us (15%)
    ppermute x30, starting transfers between devices, swapped(): lax.ppermute(value, axis, [(source, source ^ offset) for source in range(...  32.4 us
    ppermute x30, waiting for transfers between devices, swapped(): lax.ppermute(value, axis, [(source, source ^ offset) for source in range(...  31.2 us
    pallas_call x2, Pallas kernels, pack_filters(): pl.pallas_call(functools.partial(pack_filters_kernel, offsets), in_specs=...  2.74 us
    pallas_call x1, Pallas kernels, backward(): pl.pallas_call(functools.partial(backward_kernel, chips), in_specs=[WHOLE...  2.01 us
  transfers between devices with their start and end apart: 30, of which 17 were waited for; matrix products, arithmetic and copies ran while one was open for 0% of the time, Pallas kernels for 13%

profile of v24, /device:TPU:0, one launch (start us, length us, event | category | flops | bytes accessed | tf_op | source)
XLA Modules:
  0.0 75.5 jit_solution(16651461139343745009)
XLA Ops:
  1.4 3.5 %collective-permute-start.3 = (bf16[128,256]{1,0:T(8,128)(2,1)S(1)}, bf16[128,256]{1,0:T(8,128)(2,1)S(1)}, u32[]{:S(2)}, u32[]{:S(2)}) collective-permute-start(bf16[128,256]{1,0:T(8,128)(2,1)S(1)} %get-tuple-element.73), channel_id=1, source_target_pairs={{0,24},{4,28},{8,16},{12,20},{16,8},{20,12},{24,0},{28,4},{1,25},{... | collective-permute-start | bytes 196616 | tf_op jit(solution)/shard_map/ppermute | solution.py:779
  4.9 1.4 %pack_filters.2 = (bf16[512,256]{1,0:T(8,128)(2,1)S(1)}, bf16[512,256]{1,0:T(8,128)(2,1)S(1)}) custom-call(f32[4,128,1024]{2,1,0:T(8,128)} %bitcast.8), custom_call_target="tpu_custom_call" | custom-call | tf_op jit(solution)/shard_map/pack_filters/pallas_call | solution.py:243
  6.9 1.5 %collective-permute-start.2 = (bf16[128,256]{1,0:T(8,128)(2,1)S(1)}, bf16[128,256]{1,0:T(8,128)(2,1)S(1)}, u32[]{:S(2)}, u32[]{:S(2)}) collective-permute-start(bf16[128,256]{1,0:T(8,128)(2,1)S(1)} %get-tuple-element.71), channel_id=1, source_target_pairs={{0,16},{4,20},{8,24},{12,28},{16,0},{20,4},{24,8},{28,12},{1,17},{... | collective-permute-start | bytes 196616 | tf_op jit(solution)/shard_map/ppermute | solution.py:779
  9.0 1.6 %collective-permute-start.9 = (bf16[512,256]{1,0:T(8,128)(2,1)S(1)}, bf16[512,256]{1,0:T(8,128)(2,1)S(1)}, u32[]{:S(2)}, u32[]{:S(2)}) collective-permute-start(bf16[512,256]{1,0:T(8,128)(2,1)S(1)} %get-tuple-element.61), channel_id=1, source_target_pairs={{0,8},{4,12},{8,0},{12,4},{16,24},{20,28},{24,16},{28,20},{1,9},{5... | collective-permute-start | bytes 786440 | tf_op jit(solution)/shard_map/ppermute | solution.py:779
  10.5 1.3 %pack_moved.1 = (bf16[128,256]{1,0:T(8,128)(2,1)S(1)}, bf16[384,256]{1,0:T(8,128)(2,1)S(1)}, bf16[384,256]{1,0:T(8,128)(2,1)S(1)}, bf16[384,256]{1,0:T(8,128)(2,1)S(1)}, bf16[1024,128]{1,0:T(8,128)(2,1)S(1)}) custom-call(bf16[128,1024]{1,0:T(8,128)(2,1)} %gate_ref, bf16[1024,512]{1,0:T(8,128)(2,1)} %own_ref.3, ...), custom_call_target="tpu_custom_call" | custom-call | tf_op jit(solution)/shard_map/pack_moved/pallas_call | solution.py:321
  11.8 1.4 %pack_filters.3 = (bf16[512,256]{1,0:T(8,128)(2,1)S(1)}, bf16[512,256]{1,0:T(8,128)(2,1)S(1)}) custom-call(f32[4,128,1024]{2,1,0:T(8,128)} %bitcast.9), custom_call_target="tpu_custom_call" | custom-call | tf_op jit(solution)/shard_map/pack_filters/pallas_call | solution.py:243
  13.3 2.9 %collective-permute-done.2.refs_2_ = bf16[128,256]{1,0:T(8,128)(2,1)S(1)} collective-permute-done((bf16[128,256]{1,0:T(8,128)(2,1)S(1)}, bf16[128,256]{1,0:T(8,128)(2,1)S(1)}, u32[]{:S(2)}, u32[]{:S(2)}) %collective-permute-start.2) | collective-permute-done | bytes 65568 | tf_op jit(solution)/shard_map/ppermute | solution.py:779
  17.9 1.5 %forward.1.spectrum_ref = f32[256,2048]{1,0:T(8,128)S(1)} custom-call(f32[2,128,8]{2,1,0:T(8,128)S(1)} %copy-done.2, f32[2,128,8]{2,1,0:T(8,128)S(1)} %copy-done.1, bf16[256,256]{1,0:T(8,128)(2,1)S(1)} %copy-done.4, bf16[2,128,256]{2,1,0:T(8,128)(2,1)S(1)} %get-tuple-element.75.refs_0_, bf16[2,128,256]{2,1,0:T(8,128)(2,1)S(1)} %get-tuple-element.76.refs_1_, ...), custom_call_target="tpu_custom_call" | custom-call | tf_op jit(solution)/shard_map/forward/pallas_call | solution.py:409
  21.1 1.8 %collective-permute-start.8 = (bf16[384,256]{1,0:T(8,128)(2,1)S(1)}, bf16[384,256]{1,0:T(8,128)(2,1)S(1)}, u32[]{:S(2)}, u32[]{:S(2)}) collective-permute-start(bf16[384,256]{1,0:T(8,128)(2,1)S(1)} %get-tuple-element.81), channel_id=1, source_target_pairs={{0,24},{4,28},{8,16},{12,20},{16,8},{20,12},{24,0},{28,4},{1,25},{... | collective-permute-start | bytes 589832 | tf_op jit(solution)/shard_map/ppermute | solution.py:779
  24.2 2.0 %backward.1 = (f32[4,128,256]{2,1,0:T(8,128)S(1)}, bf16[2,128,256]{2,1,0:T(8,128)(2,1)S(1)}, bf16[2,128,256]{2,1,0:T(8,128)(2,1)S(1)}) custom-call(f32[2,128,8]{2,1,0:T(8,128)S(1)} %copy-done.2, f32[2,128,8]{2,1,0:T(8,128)S(1)} %copy-done.1, bf16[256,256]{1,0:T(8,128)(2,1)S(1)} %copy-done.3, f32[256,2048]{1,0:T(8,128)S(1)} %forward.1.spectrum_ref, ...), custom_call_target="tpu_custom_call" | custom-call | tf_op jit(solution)/shard_map/backward/pallas_call | solution.py:485
  26.7 1.7 %collective-permute-done.6.refs_5_.refs_0_ = bf16[384,256]{1,0:T(8,128)(2,1)S(1)} collective-permute-done((bf16[384,256]{1,0:T(8,128)(2,1)S(1)}, bf16[384,256]{1,0:T(8,128)(2,1)S(1)}, u32[]{:S(2)}, u32[]{:S(2)}) %collective-permute-start.6) | collective-permute-done | bytes 196640 | tf_op jit(solution)/shard_map/ppermute | solution.py:779
  28.4 3.4 %collective-permute-done.7.refs_6_.refs_1_ = bf16[384,256]{1,0:T(8,128)(2,1)S(1)} collective-permute-done((bf16[384,256]{1,0:T(8,128)(2,1)S(1)}, bf16[384,256]{1,0:T(8,128)(2,1)S(1)}, u32[]{:S(2)}, u32[]{:S(2)}) %collective-permute-start.7) | collective-permute-done | bytes 196640 | tf_op jit(solution)/shard_map/ppermute | solution.py:779
  32.0 1.5 %collective-permute-start.17 = (bf16[528,256]{1,0:T(8,128)(2,1)S(1)}, bf16[528,256]{1,0:T(8,128)(2,1)S(1)}, u32[]{:S(2)}, u32[]{:S(2)}) collective-permute-start(bf16[528,256]{1,0:T(8,128)(2,1)S(1)} %get-tuple-element.94), channel_id=1, source_target_pairs={{0,16},{4,20},{8,24},{12,28},{16,0},{20,4},{24,8},{28,12},{1,17},{... | collective-permute-start | bytes 811016 | tf_op jit(solution)/shard_map/ppermute | solution.py:779
  37.6 8.7 %collective-permute-done.18.refs_3_ = bf16[512,256]{1,0:T(8,128)(2,1)S(1)} collective-permute-done((bf16[512,256]{1,0:T(8,128)(2,1)S(1)}, bf16[512,256]{1,0:T(8,128)(2,1)S(1)}, u32[]{:S(2)}, u32[]{:S(2)}) %collective-permute-start.18) | collective-permute-done | bytes 262176 | tf_op jit(solution)/shard_map/ppermute | solution.py:779
  47.0 1.6 %collective-permute-start.23 = (bf16[2,512,128]{2,1,0:T(8,128)(2,1)S(1)}, bf16[2,512,128]{2,1,0:T(8,128)(2,1)S(1)}, u32[]{:S(2)}, u32[]{:S(2)}) collective-permute-start(bf16[2,512,128]{2,1,0:T(8,128)(2,1)S(1)} %get-tuple-element.103), channel_id=1, source_target_pairs={{0,1},{1,0},{2,3},{3,2},{4,5},{5,4},{6,7},{7,6},{8,9},{9,8},{10,11... | collective-permute-start | bytes 786440 | tf_op jit(solution)/shard_map/ppermute | solution.py:779
  49.3 1.3 %collective-permute-start.19 = (bf16[128,512]{1,0:T(8,128)(2,1)S(1)}, bf16[128,512]{1,0:T(8,128)(2,1)S(1)}, u32[]{:S(2)}, u32[]{:S(2)}) collective-permute-start(bf16[128,512]{1,0:T(8,128)(2,1)S(1)} %get-tuple-element.97), channel_id=1, source_target_pairs={{0,8},{4,12},{8,0},{12,4},{16,24},{20,28},{24,16},{28,20},{1,9},{5... | collective-permute-start | bytes 393224 | tf_op jit(solution)/shard_map/ppermute | solution.py:779
  50.6 1.3 %collective-permute-start.20 = (bf16[128,512]{1,0:T(8,128)(2,1)S(1)}, bf16[128,512]{1,0:T(8,128)(2,1)S(1)}, u32[]{:S(2)}, u32[]{:S(2)}) collective-permute-start(bf16[128,512]{1,0:T(8,128)(2,1)S(1)} %get-tuple-element.98), channel_id=1, source_target_pairs={{0,16},{4,20},{8,24},{12,28},{16,0},{20,4},{24,8},{28,12},{1,17},{... | collective-permute-start | bytes 393224 | tf_op jit(solution)/shard_map/ppermute | solution.py:779
  53.9 2.8 %collective-permute-start.24 = (bf16[512,128]{1,0:T(8,128)(2,1)S(1)}, bf16[512,128]{1,0:T(8,128)(2,1)S(1)}, u32[]{:S(2)}, u32[]{:S(2)}) collective-permute-start(bf16[512,128]{1,0:T(8,128)(2,1)S(1)} %fusion), channel_id=1, source_target_pairs={{0,2},{1,3},{2,0},{3,1},{4,6},{5,7},{6,4},{7,5},{8,10},{9,11},{10,... | collective-permute-start | bytes 393224 | tf_op jit(solution)/shard_map/ppermute | solution.py:779
  58.4 1.8 %collective-permute-done.24.second_ref = bf16[512,128]{1,0:T(8,128)(2,1)S(1)} collective-permute-done((bf16[512,128]{1,0:T(8,128)(2,1)S(1)}, bf16[512,128]{1,0:T(8,128)(2,1)S(1)}, u32[]{:S(2)}, u32[]{:S(2)}) %collective-permute-start.24) | collective-permute-done | bytes 131104 | tf_op jit(solution)/shard_map/ppermute | solution.py:779
  60.3 3.2 %collective-permute-start.25 = (bf16[128,128]{1,0:T(8,128)(2,1)S(1)}, bf16[128,128]{1,0:T(8,128)(2,1)S(1)}, u32[]{:S(2)}, u32[]{:S(2)}) collective-permute-start(bf16[128,128]{1,0:T(8,128)(2,1)S(1)} %get-tuple-element.107), channel_id=1, source_target_pairs={{0,24},{4,28},{8,16},{12,20},{16,8},{20,12},{24,0},{28,4},{1,25},{... | collective-permute-start | bytes 98312 | tf_op jit(solution)/shard_map/ppermute | solution.py:779
  65.3 2.0 %collective-permute-done.26.refs_1_ = bf16[128,128]{1,0:T(8,128)(2,1)S(1)} collective-permute-done((bf16[128,128]{1,0:T(8,128)(2,1)S(1)}, bf16[128,128]{1,0:T(8,128)(2,1)S(1)}, u32[]{:S(2)}, u32[]{:S(2)}) %collective-permute-start.26) | collective-permute-done | bytes 32800 | tf_op jit(solution)/shard_map/ppermute | solution.py:779
  67.4 1.3 %collective-permute-start.28 = (bf16[128,512]{1,0:T(8,128)(2,1)S(1)}, bf16[128,512]{1,0:T(8,128)(2,1)S(1)}, u32[]{:S(2)}, u32[]{:S(2)}) collective-permute-start(bf16[128,512]{1,0:T(8,128)(2,1)S(1)} %add.8), channel_id=1, source_target_pairs={{0,2},{1,3},{2,0},{3,1},{4,6},{5,7},{6,4},{7,5},{8,10},{9,11},{10,... | collective-permute-start | bytes 393224 | tf_op jit(solution)/shard_map/ppermute | solution.py:779
  69.7 2.9 %collective-permute-done.29.refs_2_ = bf16[128,128]{1,0:T(8,128)(2,1)S(1)} collective-permute-done((bf16[128,128]{1,0:T(8,128)(2,1)S(1)}, bf16[128,128]{1,0:T(8,128)(2,1)S(1)}, u32[]{:S(2)}, u32[]{:S(2)}) %collective-permute-start.29) | collective-permute-done | bytes 32800 | tf_op jit(solution)/shard_map/ppermute | solution.py:779
  72.6 2.1 %collective-permute-done.28.second_ref = bf16[128,512]{1,0:T(8,128)(2,1)S(1)} collective-permute-done((bf16[128,512]{1,0:T(8,128)(2,1)S(1)}, bf16[128,512]{1,0:T(8,128)(2,1)S(1)}, u32[]{:S(2)}, u32[]{:S(2)}) %collective-permute-start.28) | collective-permute-done | bytes 131104 | tf_op jit(solution)/shard_map/ppermute | solution.py:779
  (66 shorter events, 20.9 us)
Async XLA Ops:
  0.0 8.9 %collective-permute-start = (bf16[1024,512]{1,0:T(8,128)(2,1)}, bf16[1024,512]{1,0:T(8,128)(2,1)S(1)}, u32[]{:S(2)}, u32[]{:S(2)}) collective-permute-start(bf16[1024,512]{1,0:T(8,128)(2,1)} %own_ref.3), channel_id=1, source_target_pairs={{0,4},{4,0},{8,12},{12,8},{16,20},{20,16},{24,28},{28,24},{1,5},{5... | collective-permute-start | bytes 3145736 | tf_op jit(solution)/shard_map/ppermute | solution.py:779
  1.4 11.8 %collective-permute-start.3 = (bf16[128,256]{1,0:T(8,128)(2,1)S(1)}, bf16[128,256]{1,0:T(8,128)(2,1)S(1)}, u32[]{:S(2)}, u32[]{:S(2)}) collective-permute-start(bf16[128,256]{1,0:T(8,128)(2,1)S(1)} %get-tuple-element.73), channel_id=1, source_target_pairs={{0,24},{4,28},{8,16},{12,20},{16,8},{20,12},{24,0},{28,4},{1,25},{... | collective-permute-start | bytes 196616 | tf_op jit(solution)/shard_map/ppermute | solution.py:779
  6.3 14.8 %collective-permute-start.10 = (bf16[512,256]{1,0:T(8,128)(2,1)S(1)}, bf16[512,256]{1,0:T(8,128)(2,1)S(1)}, u32[]{:S(2)}, u32[]{:S(2)}) collective-permute-start(bf16[512,256]{1,0:T(8,128)(2,1)S(1)} %get-tuple-element.83), channel_id=1, source_target_pairs={{0,16},{4,20},{8,24},{12,28},{16,0},{20,4},{24,8},{28,12},{1,17},{... | collective-permute-start | bytes 786440 | tf_op jit(solution)/shard_map/ppermute | solution.py:779
  6.9 9.3 %collective-permute-start.2 = (bf16[128,256]{1,0:T(8,128)(2,1)S(1)}, bf16[128,256]{1,0:T(8,128)(2,1)S(1)}, u32[]{:S(2)}, u32[]{:S(2)}) collective-permute-start(bf16[128,256]{1,0:T(8,128)(2,1)S(1)} %get-tuple-element.71), channel_id=1, source_target_pairs={{0,16},{4,20},{8,24},{12,28},{16,0},{20,4},{24,8},{28,12},{1,17},{... | collective-permute-start | bytes 196616 | tf_op jit(solution)/shard_map/ppermute | solution.py:779
  8.4 7.8 %collective-permute-start.1 = (bf16[128,256]{1,0:T(8,128)(2,1)S(1)}, bf16[128,256]{1,0:T(8,128)(2,1)S(1)}, u32[]{:S(2)}, u32[]{:S(2)}) collective-permute-start(bf16[128,256]{1,0:T(8,128)(2,1)S(1)} %get-tuple-element.69), channel_id=1, source_target_pairs={{0,8},{4,12},{8,0},{12,4},{16,24},{20,28},{24,16},{28,20},{1,9},{5... | collective-permute-start | bytes 196616 | tf_op jit(solution)/shard_map/ppermute | solution.py:779
  9.0 14.0 %collective-permute-start.9 = (bf16[512,256]{1,0:T(8,128)(2,1)S(1)}, bf16[512,256]{1,0:T(8,128)(2,1)S(1)}, u32[]{:S(2)}, u32[]{:S(2)}) collective-permute-start(bf16[512,256]{1,0:T(8,128)(2,1)S(1)} %get-tuple-element.61), channel_id=1, source_target_pairs={{0,8},{4,12},{8,0},{12,4},{16,24},{20,28},{24,16},{28,20},{1,9},{5... | collective-permute-start | bytes 786440 | tf_op jit(solution)/shard_map/ppermute | solution.py:779
  13.2 11.0 %collective-permute-start.11 = (bf16[512,256]{1,0:T(8,128)(2,1)S(1)}, bf16[512,256]{1,0:T(8,128)(2,1)S(1)}, u32[]{:S(2)}, u32[]{:S(2)}) collective-permute-start(bf16[512,256]{1,0:T(8,128)(2,1)S(1)} %get-tuple-element.67), channel_id=1, source_target_pairs={{0,24},{4,28},{8,16},{12,20},{16,8},{20,12},{24,0},{28,4},{1,25},{... | collective-permute-start | bytes 786440 | tf_op jit(solution)/shard_map/ppermute | solution.py:779
  19.4 9.1 %collective-permute-start.6 = (bf16[384,256]{1,0:T(8,128)(2,1)S(1)}, bf16[384,256]{1,0:T(8,128)(2,1)S(1)}, u32[]{:S(2)}, u32[]{:S(2)}) collective-permute-start(bf16[384,256]{1,0:T(8,128)(2,1)S(1)} %get-tuple-element.77), channel_id=1, source_target_pairs={{0,8},{4,12},{8,0},{12,4},{16,24},{20,28},{24,16},{28,20},{1,9},{5... | collective-permute-start | bytes 589832 | tf_op jit(solution)/shard_map/ppermute | solution.py:779
  20.0 11.8 %collective-permute-start.7 = (bf16[384,256]{1,0:T(8,128)(2,1)S(1)}, bf16[384,256]{1,0:T(8,128)(2,1)S(1)}, u32[]{:S(2)}, u32[]{:S(2)}) collective-permute-start(bf16[384,256]{1,0:T(8,128)(2,1)S(1)} %get-tuple-element.79), channel_id=1, source_target_pairs={{0,16},{4,20},{8,24},{12,28},{16,0},{20,4},{24,8},{28,12},{1,17},{... | collective-permute-start | bytes 589832 | tf_op jit(solution)/shard_map/ppermute | solution.py:779
  21.1 10.7 %collective-permute-start.8 = (bf16[384,256]{1,0:T(8,128)(2,1)S(1)}, bf16[384,256]{1,0:T(8,128)(2,1)S(1)}, u32[]{:S(2)}, u32[]{:S(2)}) collective-permute-start(bf16[384,256]{1,0:T(8,128)(2,1)S(1)} %get-tuple-element.81), channel_id=1, source_target_pairs={{0,24},{4,28},{8,16},{12,20},{16,8},{20,12},{24,0},{28,4},{1,25},{... | collective-permute-start | bytes 589832 | tf_op jit(solution)/shard_map/ppermute | solution.py:779
  26.2 5.6 %collective-permute-start.12 = (bf16[2,128,256]{2,1,0:T(8,128)(2,1)S(1)}, bf16[2,128,256]{2,1,0:T(8,128)(2,1)S(1)}, u32[]{:S(2)}, u32[]{:S(2)}) collective-permute-start(bf16[2,128,256]{2,1,0:T(8,128)(2,1)S(1)} %get-tuple-element.85), channel_id=1, source_target_pairs={{0,4},{4,0},{8,12},{12,8},{16,20},{20,16},{24,28},{28,24},{1,5},{5... | collective-permute-start | bytes 393224 | tf_op jit(solution)/shard_map/ppermute | solution.py:779
  26.3 5.6 %collective-permute-start.13 = (bf16[2,128,256]{2,1,0:T(8,128)(2,1)S(1)}, bf16[2,128,256]{2,1,0:T(8,128)(2,1)S(1)}, u32[]{:S(2)}, u32[]{:S(2)}) collective-permute-start(bf16[2,128,256]{2,1,0:T(8,128)(2,1)S(1)} %get-tuple-element.86), channel_id=1, source_target_pairs={{0,4},{4,0},{8,12},{12,8},{16,20},{20,16},{24,28},{28,24},{1,5},{5... | collective-permute-start | bytes 393224 | tf_op jit(solution)/shard_map/ppermute | solution.py:779
  32.0 14.4 %collective-permute-start.17 = (bf16[528,256]{1,0:T(8,128)(2,1)S(1)}, bf16[528,256]{1,0:T(8,128)(2,1)S(1)}, u32[]{:S(2)}, u32[]{:S(2)}) collective-permute-start(bf16[528,256]{1,0:T(8,128)(2,1)S(1)} %get-tuple-element.94), channel_id=1, source_target_pairs={{0,16},{4,20},{8,24},{12,28},{16,0},{20,4},{24,8},{28,12},{1,17},{... | collective-permute-start | bytes 811016 | tf_op jit(solution)/shard_map/ppermute | solution.py:779
  33.5 12.9 %collective-permute-start.16 = (bf16[528,256]{1,0:T(8,128)(2,1)S(1)}, bf16[528,256]{1,0:T(8,128)(2,1)S(1)}, u32[]{:S(2)}, u32[]{:S(2)}) collective-permute-start(bf16[528,256]{1,0:T(8,128)(2,1)S(1)} %get-tuple-element.94), channel_id=1, source_target_pairs={{0,8},{4,12},{8,0},{12,4},{16,24},{20,28},{24,16},{28,20},{1,9},{5... | collective-permute-start | bytes 811016 | tf_op jit(solution)/shard_map/ppermute | solution.py:779
  34.6 11.8 %collective-permute-start.18 = (bf16[512,256]{1,0:T(8,128)(2,1)S(1)}, bf16[512,256]{1,0:T(8,128)(2,1)S(1)}, u32[]{:S(2)}, u32[]{:S(2)}) collective-permute-start(bf16[512,256]{1,0:T(8,128)(2,1)S(1)} %get-tuple-element.88.refs_0_), channel_id=1, source_target_pairs={{0,24},{4,28},{8,16},{12,20},{16,8},{20,12},{24,0},{28,4},{1,25},{... | collective-permute-start | bytes 786440 | tf_op jit(solution)/shard_map/ppermute | solution.py:779
  47.0 6.4 %collective-permute-start.23 = (bf16[2,512,128]{2,1,0:T(8,128)(2,1)S(1)}, bf16[2,512,128]{2,1,0:T(8,128)(2,1)S(1)}, u32[]{:S(2)}, u32[]{:S(2)}) collective-permute-start(bf16[2,512,128]{2,1,0:T(8,128)(2,1)S(1)} %get-tuple-element.103), channel_id=1, source_target_pairs={{0,1},{1,0},{2,3},{3,2},{4,5},{5,4},{6,7},{7,6},{8,9},{9,8},{10,11... | collective-permute-start | bytes 786440 | tf_op jit(solution)/shard_map/ppermute | solution.py:779
  49.3 7.3 %collective-permute-start.19 = (bf16[128,512]{1,0:T(8,128)(2,1)S(1)}, bf16[128,512]{1,0:T(8,128)(2,1)S(1)}, u32[]{:S(2)}, u32[]{:S(2)}) collective-permute-start(bf16[128,512]{1,0:T(8,128)(2,1)S(1)} %get-tuple-element.97), channel_id=1, source_target_pairs={{0,8},{4,12},{8,0},{12,4},{16,24},{20,28},{24,16},{28,20},{1,9},{5... | collective-permute-start | bytes 393224 | tf_op jit(solution)/shard_map/ppermute | solution.py:779
  50.6 6.1 %collective-permute-start.20 = (bf16[128,512]{1,0:T(8,128)(2,1)S(1)}, bf16[128,512]{1,0:T(8,128)(2,1)S(1)}, u32[]{:S(2)}, u32[]{:S(2)}) collective-permute-start(bf16[128,512]{1,0:T(8,128)(2,1)S(1)} %get-tuple-element.98), channel_id=1, source_target_pairs={{0,16},{4,20},{8,24},{12,28},{16,0},{20,4},{24,8},{28,12},{1,17},{... | collective-permute-start | bytes 393224 | tf_op jit(solution)/shard_map/ppermute | solution.py:779
  52.0 5.9 %collective-permute-start.21 = (bf16[128,512]{1,0:T(8,128)(2,1)S(1)}, bf16[128,512]{1,0:T(8,128)(2,1)S(1)}, u32[]{:S(2)}, u32[]{:S(2)}) collective-permute-start(bf16[128,512]{1,0:T(8,128)(2,1)S(1)} %get-tuple-element.99), channel_id=1, source_target_pairs={{0,24},{4,28},{8,16},{12,20},{16,8},{20,12},{24,0},{28,4},{1,25},{... | collective-permute-start | bytes 393224 | tf_op jit(solution)/shard_map/ppermute | solution.py:779
  53.9 6.3 %collective-permute-start.24 = (bf16[512,128]{1,0:T(8,128)(2,1)S(1)}, bf16[512,128]{1,0:T(8,128)(2,1)S(1)}, u32[]{:S(2)}, u32[]{:S(2)}) collective-permute-start(bf16[512,128]{1,0:T(8,128)(2,1)S(1)} %fusion), channel_id=1, source_target_pairs={{0,2},{1,3},{2,0},{3,1},{4,6},{5,7},{6,4},{7,5},{8,10},{9,11},{10,... | collective-permute-start | bytes 393224 | tf_op jit(solution)/shard_map/ppermute | solution.py:779
  57.9 9.4 %collective-permute-start.27 = (bf16[128,512]{1,0:T(8,128)(2,1)S(1)}, bf16[128,512]{1,0:T(8,128)(2,1)S(1)}, u32[]{:S(2)}, u32[]{:S(2)}) collective-permute-start(bf16[128,512]{1,0:T(8,128)(2,1)S(1)} %get-tuple-element.110), channel_id=1, source_target_pairs={{0,1},{1,0},{2,3},{3,2},{4,5},{5,4},{6,7},{7,6},{8,9},{9,8},{10,11... | collective-permute-start | bytes 393224 | tf_op jit(solution)/shard_map/ppermute | solution.py:779
  60.3 5.0 %collective-permute-start.25 = (bf16[128,128]{1,0:T(8,128)(2,1)S(1)}, bf16[128,128]{1,0:T(8,128)(2,1)S(1)}, u32[]{:S(2)}, u32[]{:S(2)}) collective-permute-start(bf16[128,128]{1,0:T(8,128)(2,1)S(1)} %get-tuple-element.107), channel_id=1, source_target_pairs={{0,24},{4,28},{8,16},{12,20},{16,8},{20,12},{24,0},{28,4},{1,25},{... | collective-permute-start | bytes 98312 | tf_op jit(solution)/shard_map/ppermute | solution.py:779
  64.4 5.3 %collective-permute-start.22 = (bf16[128,512]{1,0:T(8,128)(2,1)S(1)}, bf16[128,512]{1,0:T(8,128)(2,1)S(1)}, u32[]{:S(2)}, u32[]{:S(2)}) collective-permute-start(bf16[128,512]{1,0:T(8,128)(2,1)S(1)} %get-tuple-element.101), channel_id=1, source_target_pairs={{0,1},{1,0},{2,3},{3,2},{4,5},{5,4},{6,7},{7,6},{8,9},{9,8},{10,11... | collective-permute-start | bytes 393224 | tf_op jit(solution)/shard_map/ppermute | solution.py:779
  67.4 7.3 %collective-permute-start.28 = (bf16[128,512]{1,0:T(8,128)(2,1)S(1)}, bf16[128,512]{1,0:T(8,128)(2,1)S(1)}, u32[]{:S(2)}, u32[]{:S(2)}) collective-permute-start(bf16[128,512]{1,0:T(8,128)(2,1)S(1)} %add.8), channel_id=1, source_target_pairs={{0,2},{1,3},{2,0},{3,1},{4,6},{5,7},{6,4},{7,5},{8,10},{9,11},{10,... | collective-permute-start | bytes 393224 | tf_op jit(solution)/shard_map/ppermute | solution.py:779
  (12 other events, 75.3 us)

commit v25 on v22

--- a/solution.py
+++ b/solution.py
@@ -800,7 +800,7 @@
     keep, passed, send = project_moved(arrange(mine, moved[1:], others), gathered)
     blocks = to_chips(finish(keep, *over_layers(passed, send), chips))
     keep, near, passed, far = sort_blocks(to_chips(project_still(out_weight, other_weight, gathered)))
-    second = swapped(add(after(passed, blocks[3], blocks[1]), swapped(far, "chan", 1), 0), "chan", 2)
+    second = swapped(add(after(passed, blocks[3], blocks[2]), swapped(far, "chan", 1), 0), "chan", 2)
     return join(keep, swapped(near, "chan", 1), second, blocks)
 
 

time: 73.9 us -> 73.9 us (level)
  no operation moved by 1% of the time
where the time goes in v25:
time: 73.9 us; the launch traced here: 73.7 us
  starting transfers between devices  33.8 us (46%)
  waiting for transfers between devices  28 us (38%)
  Pallas kernels  11.6 us (16%)
    ppermute x30, starting transfers between devices, swapped(): lax.ppermute(value, axis, [(source, source ^ offset) for source in range(...  33.8 us
    ppermute x30, waiting for transfers between devices, swapped(): lax.ppermute(value, axis, [(source, source ^ offset) for source in range(...  28 us
    pallas_call x2, Pallas kernels, pack_filters(): pl.pallas_call(functools.partial(pack_filters_kernel, offsets), in_specs=...  2.74 us
    pallas_call x1, Pallas kernels, backward(): pl.pallas_call(functools.partial(backward_kernel, chips), in_specs=[WHOLE...  2.01 us
    pallas_call x1, Pallas kernels, forward(): pl.pallas_call(functools.partial(forward_kernel, chips), in_specs=[WHOLE]...  1.48 us
  transfers between devices with their start and end apart: 30, of which 15 were waited for; matrix products, arithmetic and copies ran while one was open for 0% of the time, Pallas kernels for 13%

profile of v25, /device:TPU:0, one launch (start us, length us, event | category | flops | bytes accessed | tf_op | source)
XLA Modules:
  0.0 73.7 jit_solution(5129805973576246643)
XLA Ops:
  1.4 3.5 %collective-permute-start.3 = (bf16[128,256]{1,0:T(8,128)(2,1)S(1)}, bf16[128,256]{1,0:T(8,128)(2,1)S(1)}, u32[]{:S(2)}, u32[]{:S(2)}) collective-permute-start(bf16[128,256]{1,0:T(8,128)(2,1)S(1)} %get-tuple-element.69), channel_id=1, source_target_pairs={{0,24},{4,28},{8,16},{12,20},{16,8},{20,12},{24,0},{28,4},{1,25},{... | collective-permute-start | bytes 196616 | tf_op jit(solution)/shard_map/ppermute | solution.py:762
  4.9 1.4 %pack_filters.2 = (bf16[512,256]{1,0:T(8,128)(2,1)S(1)}, bf16[512,256]{1,0:T(8,128)(2,1)S(1)}) custom-call(f32[4,128,1024]{2,1,0:T(8,128)} %bitcast.8), custom_call_target="tpu_custom_call" | custom-call | tf_op jit(solution)/shard_map/pack_filters/pallas_call | solution.py:243
  6.9 1.5 %collective-permute-start.2 = (bf16[128,256]{1,0:T(8,128)(2,1)S(1)}, bf16[128,256]{1,0:T(8,128)(2,1)S(1)}, u32[]{:S(2)}, u32[]{:S(2)}) collective-permute-start(bf16[128,256]{1,0:T(8,128)(2,1)S(1)} %get-tuple-element.67), channel_id=1, source_target_pairs={{0,16},{4,20},{8,24},{12,28},{16,0},{20,4},{24,8},{28,12},{1,17},{... | collective-permute-start | bytes 196616 | tf_op jit(solution)/shard_map/ppermute | solution.py:762
  9.0 1.6 %collective-permute-start.6 = (bf16[512,256]{1,0:T(8,128)(2,1)S(1)}, bf16[512,256]{1,0:T(8,128)(2,1)S(1)}, u32[]{:S(2)}, u32[]{:S(2)}) collective-permute-start(bf16[512,256]{1,0:T(8,128)(2,1)S(1)} %get-tuple-element.59), channel_id=1, source_target_pairs={{0,8},{4,12},{8,0},{12,4},{16,24},{20,28},{24,16},{28,20},{1,9},{5... | collective-permute-start | bytes 786440 | tf_op jit(solution)/shard_map/ppermute | solution.py:762
  10.5 1.3 %pack_moved.1 = (bf16[128,256]{1,0:T(8,128)(2,1)S(1)}, bf16[384,256]{1,0:T(8,128)(2,1)S(1)}, bf16[384,256]{1,0:T(8,128)(2,1)S(1)}, bf16[384,256]{1,0:T(8,128)(2,1)S(1)}, bf16[1024,128]{1,0:T(8,128)(2,1)S(1)}) custom-call(bf16[128,1024]{1,0:T(8,128)(2,1)} %gate_ref, bf16[1024,512]{1,0:T(8,128)(2,1)} %own_ref.3, ...), custom_call_target="tpu_custom_call" | custom-call | tf_op jit(solution)/shard_map/pack_moved/pallas_call | solution.py:321
  11.8 1.4 %pack_filters.3 = (bf16[512,256]{1,0:T(8,128)(2,1)S(1)}, bf16[512,256]{1,0:T(8,128)(2,1)S(1)}) custom-call(f32[4,128,1024]{2,1,0:T(8,128)} %bitcast.9), custom_call_target="tpu_custom_call" | custom-call | tf_op jit(solution)/shard_map/pack_filters/pallas_call | solution.py:243
  13.3 2.9 %collective-permute-done.2.refs_2_ = bf16[128,256]{1,0:T(8,128)(2,1)S(1)} collective-permute-done((bf16[128,256]{1,0:T(8,128)(2,1)S(1)}, bf16[128,256]{1,0:T(8,128)(2,1)S(1)}, u32[]{:S(2)}, u32[]{:S(2)}) %collective-permute-start.2) | collective-permute-done | bytes 65568 | tf_op jit(solution)/shard_map/ppermute | solution.py:762
  17.9 1.5 %forward.1.spectrum_ref = f32[256,2048]{1,0:T(8,128)S(1)} custom-call(f32[2,128,8]{2,1,0:T(8,128)S(1)} %copy-done.2, f32[2,128,8]{2,1,0:T(8,128)S(1)} %copy-done.1, bf16[256,256]{1,0:T(8,128)(2,1)S(1)} %copy-done.4, bf16[2,128,256]{2,1,0:T(8,128)(2,1)S(1)} %get-tuple-element.71.refs_0_, bf16[2,128,256]{2,1,0:T(8,128)(2,1)S(1)} %get-tuple-element.72.refs_1_, ...), custom_call_target="tpu_custom_call" | custom-call | tf_op jit(solution)/shard_map/forward/pallas_call | solution.py:409
  21.1 1.8 %collective-permute-start.13 = (bf16[384,256]{1,0:T(8,128)(2,1)S(1)}, bf16[384,256]{1,0:T(8,128)(2,1)S(1)}, u32[]{:S(2)}, u32[]{:S(2)}) collective-permute-start(bf16[384,256]{1,0:T(8,128)(2,1)S(1)} %get-tuple-element.84), channel_id=1, source_target_pairs={{0,24},{4,28},{8,16},{12,20},{16,8},{20,12},{24,0},{28,4},{1,25},{... | collective-permute-start | bytes 589832 | tf_op jit(solution)/shard_map/ppermute | solution.py:762
  24.2 2.0 %backward.1 = (f32[4,128,256]{2,1,0:T(8,128)S(1)}, bf16[2,128,256]{2,1,0:T(8,128)(2,1)S(1)}, bf16[2,128,256]{2,1,0:T(8,128)(2,1)S(1)}) custom-call(f32[2,128,8]{2,1,0:T(8,128)S(1)} %copy-done.2, f32[2,128,8]{2,1,0:T(8,128)S(1)} %copy-done.1, bf16[256,256]{1,0:T(8,128)(2,1)S(1)} %copy-done.3, f32[256,2048]{1,0:T(8,128)S(1)} %forward.1.spectrum_ref, ...), custom_call_target="tpu_custom_call" | custom-call | tf_op jit(solution)/shard_map/backward/pallas_call | solution.py:485
  26.7 1.7 %collective-permute-done.11.refs_5_.refs_0_ = bf16[384,256]{1,0:T(8,128)(2,1)S(1)} collective-permute-done((bf16[384,256]{1,0:T(8,128)(2,1)S(1)}, bf16[384,256]{1,0:T(8,128)(2,1)S(1)}, u32[]{:S(2)}, u32[]{:S(2)}) %collective-permute-start.11) | collective-permute-done | bytes 196640 | tf_op jit(solution)/shard_map/ppermute | solution.py:762
  28.4 3.4 %collective-permute-done.12.refs_6_.refs_1_ = bf16[384,256]{1,0:T(8,128)(2,1)S(1)} collective-permute-done((bf16[384,256]{1,0:T(8,128)(2,1)S(1)}, bf16[384,256]{1,0:T(8,128)(2,1)S(1)}, u32[]{:S(2)}, u32[]{:S(2)}) %collective-permute-start.12) | collective-permute-done | bytes 196640 | tf_op jit(solution)/shard_map/ppermute | solution.py:762
  32.0 1.5 %collective-permute-start.15 = (bf16[528,256]{1,0:T(8,128)(2,1)S(1)}, bf16[528,256]{1,0:T(8,128)(2,1)S(1)}, u32[]{:S(2)}, u32[]{:S(2)}) collective-permute-start(bf16[528,256]{1,0:T(8,128)(2,1)S(1)} %get-tuple-element.86), channel_id=1, source_target_pairs={{0,16},{4,20},{8,24},{12,28},{16,0},{20,4},{24,8},{28,12},{1,17},{... | collective-permute-start | bytes 811016 | tf_op jit(solution)/shard_map/ppermute | solution.py:762
  37.6 8.8 %collective-permute-done.16.refs_3_ = bf16[512,256]{1,0:T(8,128)(2,1)S(1)} collective-permute-done((bf16[512,256]{1,0:T(8,128)(2,1)S(1)}, bf16[512,256]{1,0:T(8,128)(2,1)S(1)}, u32[]{:S(2)}, u32[]{:S(2)}) %collective-permute-start.16) | collective-permute-done | bytes 262176 | tf_op jit(solution)/shard_map/ppermute | solution.py:762
  47.2 1.6 %collective-permute-start.23 = (bf16[2,512,128]{2,1,0:T(8,128)(2,1)S(1)}, bf16[2,512,128]{2,1,0:T(8,128)(2,1)S(1)}, u32[]{:S(2)}, u32[]{:S(2)}) collective-permute-start(bf16[2,512,128]{2,1,0:T(8,128)(2,1)S(1)} %get-tuple-element.101), channel_id=1, source_target_pairs={{0,1},{1,0},{2,3},{3,2},{4,5},{5,4},{6,7},{7,6},{8,9},{9,8},{10,11... | collective-permute-start | bytes 786440 | tf_op jit(solution)/shard_map/ppermute | solution.py:762
  49.8 1.3 %collective-permute-start.17 = (bf16[128,512]{1,0:T(8,128)(2,1)S(1)}, bf16[128,512]{1,0:T(8,128)(2,1)S(1)}, u32[]{:S(2)}, u32[]{:S(2)}) collective-permute-start(bf16[128,512]{1,0:T(8,128)(2,1)S(1)} %get-tuple-element.88), channel_id=1, source_target_pairs={{0,8},{4,12},{8,0},{12,4},{16,24},{20,28},{24,16},{28,20},{1,9},{5... | collective-permute-start | bytes 393224 | tf_op jit(solution)/shard_map/ppermute | solution.py:762
  51.0 1.3 %collective-permute-start.18 = (bf16[128,512]{1,0:T(8,128)(2,1)S(1)}, bf16[128,512]{1,0:T(8,128)(2,1)S(1)}, u32[]{:S(2)}, u32[]{:S(2)}) collective-permute-start(bf16[128,512]{1,0:T(8,128)(2,1)S(1)} %get-tuple-element.89), channel_id=1, source_target_pairs={{0,16},{4,20},{8,24},{12,28},{16,0},{20,4},{24,8},{28,12},{1,17},{... | collective-permute-start | bytes 393224 | tf_op jit(solution)/shard_map/ppermute | solution.py:762
  53.7 3.2 %collective-permute-start.24 = (bf16[512,128]{1,0:T(8,128)(2,1)S(1)}, bf16[512,128]{1,0:T(8,128)(2,1)S(1)}, u32[]{:S(2)}, u32[]{:S(2)}) collective-permute-start(bf16[512,128]{1,0:T(8,128)(2,1)S(1)} %fusion), channel_id=1, source_target_pairs={{0,2},{1,3},{2,0},{3,1},{4,6},{5,7},{6,4},{7,5},{8,10},{9,11},{10,... | collective-permute-start | bytes 393224 | tf_op jit(solution)/shard_map/ppermute | solution.py:762
  56.9 1.3 %collective-permute-done.19.refs_3_ = bf16[128,512]{1,0:T(8,128)(2,1)S(1)} collective-permute-done((bf16[128,512]{1,0:T(8,128)(2,1)S(1)}, bf16[128,512]{1,0:T(8,128)(2,1)S(1)}, u32[]{:S(2)}, u32[]{:S(2)}) %collective-permute-start.19) | collective-permute-done | bytes 131104 | tf_op jit(solution)/shard_map/ppermute | solution.py:762
  58.8 1.7 %collective-permute-done.24.second_ref = bf16[512,128]{1,0:T(8,128)(2,1)S(1)} collective-permute-done((bf16[512,128]{1,0:T(8,128)(2,1)S(1)}, bf16[512,128]{1,0:T(8,128)(2,1)S(1)}, u32[]{:S(2)}, u32[]{:S(2)}) %collective-permute-start.24) | collective-permute-done | bytes 131104 | tf_op jit(solution)/shard_map/ppermute | solution.py:762
  60.6 2.0 %collective-permute-start.25 = (bf16[128,128]{1,0:T(8,128)(2,1)S(1)}, bf16[128,128]{1,0:T(8,128)(2,1)S(1)}, u32[]{:S(2)}, u32[]{:S(2)}) collective-permute-start(bf16[128,128]{1,0:T(8,128)(2,1)S(1)} %get-tuple-element.103), channel_id=1, source_target_pairs={{0,24},{4,28},{8,16},{12,20},{16,8},{20,12},{24,0},{28,4},{1,25},{... | collective-permute-start | bytes 98312 | tf_op jit(solution)/shard_map/ppermute | solution.py:762
  63.5 1.4 %collective-permute-start.20 = (bf16[128,512]{1,0:T(8,128)(2,1)S(1)}, bf16[128,512]{1,0:T(8,128)(2,1)S(1)}, u32[]{:S(2)}, u32[]{:S(2)}) collective-permute-start(bf16[128,512]{1,0:T(8,128)(2,1)S(1)} %get-tuple-element.92), channel_id=1, source_target_pairs={{0,1},{1,0},{2,3},{3,2},{4,5},{5,4},{6,7},{7,6},{8,9},{9,8},{10,11... | collective-permute-start | bytes 393224 | tf_op jit(solution)/shard_map/ppermute | solution.py:762
  66.5 2.5 %collective-permute-start.28 = (bf16[128,512]{1,0:T(8,128)(2,1)S(1)}, bf16[128,512]{1,0:T(8,128)(2,1)S(1)}, u32[]{:S(2)}, u32[]{:S(2)}) collective-permute-start(bf16[128,512]{1,0:T(8,128)(2,1)S(1)} %add.8), channel_id=1, source_target_pairs={{0,2},{1,3},{2,0},{3,1},{4,6},{5,7},{6,4},{7,5},{8,10},{9,11},{10,... | collective-permute-start | bytes 393224 | tf_op jit(solution)/shard_map/ppermute | solution.py:762
  69.9 3.0 %collective-permute-done.29.refs_1_ = bf16[128,128]{1,0:T(8,128)(2,1)S(1)} collective-permute-done((bf16[128,128]{1,0:T(8,128)(2,1)S(1)}, bf16[128,128]{1,0:T(8,128)(2,1)S(1)}, u32[]{:S(2)}, u32[]{:S(2)}) %collective-permute-start.29) | collective-permute-done | bytes 32800 | tf_op jit(solution)/shard_map/ppermute | solution.py:762
  (65 shorter events, 20.1 us)
Async XLA Ops:
  0.0 8.9 %collective-permute-start = (bf16[1024,512]{1,0:T(8,128)(2,1)}, bf16[1024,512]{1,0:T(8,128)(2,1)S(1)}, u32[]{:S(2)}, u32[]{:S(2)}) collective-permute-start(bf16[1024,512]{1,0:T(8,128)(2,1)} %own_ref.3), channel_id=1, source_target_pairs={{0,4},{4,0},{8,12},{12,8},{16,20},{20,16},{24,28},{28,24},{1,5},{5... | collective-permute-start | bytes 3145736 | tf_op jit(solution)/shard_map/ppermute | solution.py:762
  1.4 11.8 %collective-permute-start.3 = (bf16[128,256]{1,0:T(8,128)(2,1)S(1)}, bf16[128,256]{1,0:T(8,128)(2,1)S(1)}, u32[]{:S(2)}, u32[]{:S(2)}) collective-permute-start(bf16[128,256]{1,0:T(8,128)(2,1)S(1)} %get-tuple-element.69), channel_id=1, source_target_pairs={{0,24},{4,28},{8,16},{12,20},{16,8},{20,12},{24,0},{28,4},{1,25},{... | collective-permute-start | bytes 196616 | tf_op jit(solution)/shard_map/ppermute | solution.py:762
  6.3 14.8 %collective-permute-start.7 = (bf16[512,256]{1,0:T(8,128)(2,1)S(1)}, bf16[512,256]{1,0:T(8,128)(2,1)S(1)}, u32[]{:S(2)}, u32[]{:S(2)}) collective-permute-start(bf16[512,256]{1,0:T(8,128)(2,1)S(1)} %get-tuple-element.74), channel_id=1, source_target_pairs={{0,16},{4,20},{8,24},{12,28},{16,0},{20,4},{24,8},{28,12},{1,17},{... | collective-permute-start | bytes 786440 | tf_op jit(solution)/shard_map/ppermute | solution.py:762
  6.9 9.3 %collective-permute-start.2 = (bf16[128,256]{1,0:T(8,128)(2,1)S(1)}, bf16[128,256]{1,0:T(8,128)(2,1)S(1)}, u32[]{:S(2)}, u32[]{:S(2)}) collective-permute-start(bf16[128,256]{1,0:T(8,128)(2,1)S(1)} %get-tuple-element.67), channel_id=1, source_target_pairs={{0,16},{4,20},{8,24},{12,28},{16,0},{20,4},{24,8},{28,12},{1,17},{... | collective-permute-start | bytes 196616 | tf_op jit(solution)/shard_map/ppermute | solution.py:762
  8.4 7.8 %collective-permute-start.1 = (bf16[128,256]{1,0:T(8,128)(2,1)S(1)}, bf16[128,256]{1,0:T(8,128)(2,1)S(1)}, u32[]{:S(2)}, u32[]{:S(2)}) collective-permute-start(bf16[128,256]{1,0:T(8,128)(2,1)S(1)} %get-tuple-element.65), channel_id=1, source_target_pairs={{0,8},{4,12},{8,0},{12,4},{16,24},{20,28},{24,16},{28,20},{1,9},{5... | collective-permute-start | bytes 196616 | tf_op jit(solution)/shard_map/ppermute | solution.py:762
  9.0 14.0 %collective-permute-start.6 = (bf16[512,256]{1,0:T(8,128)(2,1)S(1)}, bf16[512,256]{1,0:T(8,128)(2,1)S(1)}, u32[]{:S(2)}, u32[]{:S(2)}) collective-permute-start(bf16[512,256]{1,0:T(8,128)(2,1)S(1)} %get-tuple-element.59), channel_id=1, source_target_pairs={{0,8},{4,12},{8,0},{12,4},{16,24},{20,28},{24,16},{28,20},{1,9},{5... | collective-permute-start | bytes 786440 | tf_op jit(solution)/shard_map/ppermute | solution.py:762
  13.2 11.0 %collective-permute-start.8 = (bf16[512,256]{1,0:T(8,128)(2,1)S(1)}, bf16[512,256]{1,0:T(8,128)(2,1)S(1)}, u32[]{:S(2)}, u32[]{:S(2)}) collective-permute-start(bf16[512,256]{1,0:T(8,128)(2,1)S(1)} %get-tuple-element.63), channel_id=1, source_target_pairs={{0,24},{4,28},{8,16},{12,20},{16,8},{20,12},{24,0},{28,4},{1,25},{... | collective-permute-start | bytes 786440 | tf_op jit(solution)/shard_map/ppermute | solution.py:762
  19.4 9.1 %collective-permute-start.11 = (bf16[384,256]{1,0:T(8,128)(2,1)S(1)}, bf16[384,256]{1,0:T(8,128)(2,1)S(1)}, u32[]{:S(2)}, u32[]{:S(2)}) collective-permute-start(bf16[384,256]{1,0:T(8,128)(2,1)S(1)} %get-tuple-element.80), channel_id=1, source_target_pairs={{0,8},{4,12},{8,0},{12,4},{16,24},{20,28},{24,16},{28,20},{1,9},{5... | collective-permute-start | bytes 589832 | tf_op jit(solution)/shard_map/ppermute | solution.py:762
  20.0 11.8 %collective-permute-start.12 = (bf16[384,256]{1,0:T(8,128)(2,1)S(1)}, bf16[384,256]{1,0:T(8,128)(2,1)S(1)}, u32[]{:S(2)}, u32[]{:S(2)}) collective-permute-start(bf16[384,256]{1,0:T(8,128)(2,1)S(1)} %get-tuple-element.82), channel_id=1, source_target_pairs={{0,16},{4,20},{8,24},{12,28},{16,0},{20,4},{24,8},{28,12},{1,17},{... | collective-permute-start | bytes 589832 | tf_op jit(solution)/shard_map/ppermute | solution.py:762
  21.1 10.7 %collective-permute-start.13 = (bf16[384,256]{1,0:T(8,128)(2,1)S(1)}, bf16[384,256]{1,0:T(8,128)(2,1)S(1)}, u32[]{:S(2)}, u32[]{:S(2)}) collective-permute-start(bf16[384,256]{1,0:T(8,128)(2,1)S(1)} %get-tuple-element.84), channel_id=1, source_target_pairs={{0,24},{4,28},{8,16},{12,20},{16,8},{20,12},{24,0},{28,4},{1,25},{... | collective-permute-start | bytes 589832 | tf_op jit(solution)/shard_map/ppermute | solution.py:762
  26.2 5.6 %collective-permute-start.9 = (bf16[2,128,256]{2,1,0:T(8,128)(2,1)S(1)}, bf16[2,128,256]{2,1,0:T(8,128)(2,1)S(1)}, u32[]{:S(2)}, u32[]{:S(2)}) collective-permute-start(bf16[2,128,256]{2,1,0:T(8,128)(2,1)S(1)} %get-tuple-element.76), channel_id=1, source_target_pairs={{0,4},{4,0},{8,12},{12,8},{16,20},{20,16},{24,28},{28,24},{1,5},{5... | collective-permute-start | bytes 393224 | tf_op jit(solution)/shard_map/ppermute | solution.py:762
  26.3 5.6 %collective-permute-start.10 = (bf16[2,128,256]{2,1,0:T(8,128)(2,1)S(1)}, bf16[2,128,256]{2,1,0:T(8,128)(2,1)S(1)}, u32[]{:S(2)}, u32[]{:S(2)}) collective-permute-start(bf16[2,128,256]{2,1,0:T(8,128)(2,1)S(1)} %get-tuple-element.77), channel_id=1, source_target_pairs={{0,4},{4,0},{8,12},{12,8},{16,20},{20,16},{24,28},{28,24},{1,5},{5... | collective-permute-start | bytes 393224 | tf_op jit(solution)/shard_map/ppermute | solution.py:762
  32.0 14.4 %collective-permute-start.15 = (bf16[528,256]{1,0:T(8,128)(2,1)S(1)}, bf16[528,256]{1,0:T(8,128)(2,1)S(1)}, u32[]{:S(2)}, u32[]{:S(2)}) collective-permute-start(bf16[528,256]{1,0:T(8,128)(2,1)S(1)} %get-tuple-element.86), channel_id=1, source_target_pairs={{0,16},{4,20},{8,24},{12,28},{16,0},{20,4},{24,8},{28,12},{1,17},{... | collective-permute-start | bytes 811016 | tf_op jit(solution)/shard_map/ppermute | solution.py:762
  33.5 12.9 %collective-permute-start.14 = (bf16[528,256]{1,0:T(8,128)(2,1)S(1)}, bf16[528,256]{1,0:T(8,128)(2,1)S(1)}, u32[]{:S(2)}, u32[]{:S(2)}) collective-permute-start(bf16[528,256]{1,0:T(8,128)(2,1)S(1)} %get-tuple-element.86), channel_id=1, source_target_pairs={{0,8},{4,12},{8,0},{12,4},{16,24},{20,28},{24,16},{28,20},{1,9},{5... | collective-permute-start | bytes 811016 | tf_op jit(solution)/shard_map/ppermute | solution.py:762
  34.6 11.8 %collective-permute-start.16 = (bf16[512,256]{1,0:T(8,128)(2,1)S(1)}, bf16[512,256]{1,0:T(8,128)(2,1)S(1)}, u32[]{:S(2)}, u32[]{:S(2)}) collective-permute-start(bf16[512,256]{1,0:T(8,128)(2,1)S(1)} %get-tuple-element.85.refs_0_), channel_id=1, source_target_pairs={{0,24},{4,28},{8,16},{12,20},{16,8},{20,12},{24,0},{28,4},{1,25},{... | collective-permute-start | bytes 786440 | tf_op jit(solution)/shard_map/ppermute | solution.py:762
  47.2 6.4 %collective-permute-start.23 = (bf16[2,512,128]{2,1,0:T(8,128)(2,1)S(1)}, bf16[2,512,128]{2,1,0:T(8,128)(2,1)S(1)}, u32[]{:S(2)}, u32[]{:S(2)}) collective-permute-start(bf16[2,512,128]{2,1,0:T(8,128)(2,1)S(1)} %get-tuple-element.101), channel_id=1, source_target_pairs={{0,1},{1,0},{2,3},{3,2},{4,5},{5,4},{6,7},{7,6},{8,9},{9,8},{10,11... | collective-permute-start | bytes 786440 | tf_op jit(solution)/shard_map/ppermute | solution.py:762
  49.8 7.2 %collective-permute-start.17 = (bf16[128,512]{1,0:T(8,128)(2,1)S(1)}, bf16[128,512]{1,0:T(8,128)(2,1)S(1)}, u32[]{:S(2)}, u32[]{:S(2)}) collective-permute-start(bf16[128,512]{1,0:T(8,128)(2,1)S(1)} %get-tuple-element.88), channel_id=1, source_target_pairs={{0,8},{4,12},{8,0},{12,4},{16,24},{20,28},{24,16},{28,20},{1,9},{5... | collective-permute-start | bytes 393224 | tf_op jit(solution)/shard_map/ppermute | solution.py:762
  51.0 5.9 %collective-permute-start.18 = (bf16[128,512]{1,0:T(8,128)(2,1)S(1)}, bf16[128,512]{1,0:T(8,128)(2,1)S(1)}, u32[]{:S(2)}, u32[]{:S(2)}) collective-permute-start(bf16[128,512]{1,0:T(8,128)(2,1)S(1)} %get-tuple-element.89), channel_id=1, source_target_pairs={{0,16},{4,20},{8,24},{12,28},{16,0},{20,4},{24,8},{28,12},{1,17},{... | collective-permute-start | bytes 393224 | tf_op jit(solution)/shard_map/ppermute | solution.py:762
  52.4 5.9 %collective-permute-start.19 = (bf16[128,512]{1,0:T(8,128)(2,1)S(1)}, bf16[128,512]{1,0:T(8,128)(2,1)S(1)}, u32[]{:S(2)}, u32[]{:S(2)}) collective-permute-start(bf16[128,512]{1,0:T(8,128)(2,1)S(1)} %get-tuple-element.90), channel_id=1, source_target_pairs={{0,24},{4,28},{8,16},{12,20},{16,8},{20,12},{24,0},{28,4},{1,25},{... | collective-permute-start | bytes 393224 | tf_op jit(solution)/shard_map/ppermute | solution.py:762
  53.7 6.8 %collective-permute-start.24 = (bf16[512,128]{1,0:T(8,128)(2,1)S(1)}, bf16[512,128]{1,0:T(8,128)(2,1)S(1)}, u32[]{:S(2)}, u32[]{:S(2)}) collective-permute-start(bf16[512,128]{1,0:T(8,128)(2,1)S(1)} %fusion), channel_id=1, source_target_pairs={{0,2},{1,3},{2,0},{3,1},{4,6},{5,7},{6,4},{7,5},{8,10},{9,11},{10,... | collective-permute-start | bytes 393224 | tf_op jit(solution)/shard_map/ppermute | solution.py:762
  58.3 8.2 %collective-permute-start.27 = (bf16[128,512]{1,0:T(8,128)(2,1)S(1)}, bf16[128,512]{1,0:T(8,128)(2,1)S(1)}, u32[]{:S(2)}, u32[]{:S(2)}) collective-permute-start(bf16[128,512]{1,0:T(8,128)(2,1)S(1)} %get-tuple-element.106), channel_id=1, source_target_pairs={{0,1},{1,0},{2,3},{3,2},{4,5},{5,4},{6,7},{7,6},{8,9},{9,8},{10,11... | collective-permute-start | bytes 393224 | tf_op jit(solution)/shard_map/ppermute | solution.py:762
  60.6 4.9 %collective-permute-start.25 = (bf16[128,128]{1,0:T(8,128)(2,1)S(1)}, bf16[128,128]{1,0:T(8,128)(2,1)S(1)}, u32[]{:S(2)}, u32[]{:S(2)}) collective-permute-start(bf16[128,128]{1,0:T(8,128)(2,1)S(1)} %get-tuple-element.103), channel_id=1, source_target_pairs={{0,24},{4,28},{8,16},{12,20},{16,8},{20,12},{24,0},{28,4},{1,25},{... | collective-permute-start | bytes 98312 | tf_op jit(solution)/shard_map/ppermute | solution.py:762
  63.5 6.4 %collective-permute-start.20 = (bf16[128,512]{1,0:T(8,128)(2,1)S(1)}, bf16[128,512]{1,0:T(8,128)(2,1)S(1)}, u32[]{:S(2)}, u32[]{:S(2)}) collective-permute-start(bf16[128,512]{1,0:T(8,128)(2,1)S(1)} %get-tuple-element.92), channel_id=1, source_target_pairs={{0,1},{1,0},{2,3},{3,2},{4,5},{5,4},{6,7},{7,6},{8,9},{9,8},{10,11... | collective-permute-start | bytes 393224 | tf_op jit(solution)/shard_map/ppermute | solution.py:762
  66.5 6.4 %collective-permute-start.28 = (bf16[128,512]{1,0:T(8,128)(2,1)S(1)}, bf16[128,512]{1,0:T(8,128)(2,1)S(1)}, u32[]{:S(2)}, u32[]{:S(2)}) collective-permute-start(bf16[128,512]{1,0:T(8,128)(2,1)S(1)} %add.8), channel_id=1, source_target_pairs={{0,2},{1,3},{2,0},{3,1},{4,6},{5,7},{6,4},{7,5},{8,10},{9,11},{10,... | collective-permute-start | bytes 393224 | tf_op jit(solution)/shard_map/ppermute | solution.py:762
  (12 other events, 75.6 us)
